TPU v7x, 32 devices: a whole 2x2x4 slice. The times are simulated.
32 devices in a mesh: group: 2 (over x), row: 16 (over z, y, core).
Axes of the slice: x: 2, y: 2, z: 4, core: 2. Of those that a mesh axis runs over, the one named last changes fastest.
Arguments:
- features: bfloat16 [32, 65536], P(None, ('group', 'row')), parts along dimension 1
- right_side: float32 [8, 65536], P(None, ('group', 'row')), parts along dimension 1
- variance: float32 [65536], P(('group', 'row')), parts along dimension 0, may hold values from 0.5 to 2
- hilbert_order: int32 [32, 2048], P(('group', 'row')), parts along dimension 0, may hold values from 0 to 2047, each once within a row
- tile_list: int32 [32, 5, 2], P(('group', 'row')), parts along dimension 0, may hold values from -1 to 15, as said below
Outputs:
- solution: float32 [8, 65536], P(None, ('group', 'row')), parts along dimension 1
- residual: float32 [8, 65536], P(None, ('group', 'row')), parts along dimension 1
There are 2 independent parts, one for each index of `group`. A program takes and returns all parts, laid end to end along the dimension named above; each array names one. Nothing has to cross between parts.
Inputs may be any that keep to these rules, and one draw needn't show every extreme that they name: `tile_list`: row s lists the blocks coupled to block s above it: valid entries (s, b) with b > s first, in rising b, then (-1, -1). The blocks fall into disjoint groups of at most 6 blocks; two blocks are coupled exactly when they share a group. Some block lists 5 entries. `hilbert_order`: each row is a permutation.
All inputs are finite; a program needn't handle non-finite values.
Results may differ from a plain program's by a relative error of at most 0.0072.
Values may be sent and summed in bfloat16 or wider, within the bound.
No kernel may reach another device: no remote copies, remote signals or barrier semaphores. Data moves between devices by JAX's collectives and lax.ppermute only.
A program may use at most 128 MiB of HBM per device.

v0:
```python
import jax
import jax.numpy as jnp
from jax import lax
from jax.sharding import PartitionSpec as P

ITERS = 2


def wendland(left_feat, left_norm, right_feat, right_norm):
    gram = lax.dot_general(
        left_feat, right_feat, (((0,), (0,)), ((), ())), preferred_element_type=jnp.float32
    )
    dist_sq = jnp.maximum(left_norm[:, None] + right_norm[None, :] - 2.0 * gram, 0.0)
    radius = jnp.sqrt(dist_sq)
    remain = jnp.maximum(1.0 - radius, 0.0)
    power_two = remain * remain
    power_four = power_two * power_two
    power_eight = power_four * power_four
    power_sixteen = power_eight * power_eight
    return (power_sixteen * power_two * remain * (19.0 * radius + 1.0)).astype(jnp.bfloat16)


def tile_terms(left_feat, left_norm, right_feat, right_norm, left_vec, right_vec, with_back):
    rows_all = left_feat.shape[1]
    width = min(128, rows_all)
    own_term = jnp.zeros((right_vec.shape[0], rows_all), jnp.float32)
    back_term = jnp.zeros((right_vec.shape[0], right_feat.shape[1]), jnp.float32)

    def sub_step(sub_index, state_pair):
        own_acc, back_acc = state_pair
        begin = sub_index * width
        feat_rows = lax.dynamic_slice_in_dim(left_feat, begin, width, 1)
        norm_rows = lax.dynamic_slice_in_dim(left_norm, begin, width, 0)
        kernel = wendland(feat_rows, norm_rows, right_feat, right_norm)
        part_own = lax.dot_general(
            right_vec, kernel, (((1,), (1,)), ((), ())), preferred_element_type=jnp.float32
        )
        own_acc = lax.dynamic_update_slice_in_dim(own_acc, part_own, begin, 1)
        if with_back:
            vec_rows = lax.dynamic_slice_in_dim(left_vec, begin, width, 1)
            back_acc = back_acc + jnp.dot(vec_rows, kernel, preferred_element_type=jnp.float32)
        return (own_acc, back_acc)

    return lax.fori_loop(0, rows_all // width, sub_step, (own_term, back_term))


def add_block(accum, block_id, width, term):
    start_col = block_id * width
    old_part = lax.dynamic_slice_in_dim(accum, start_col, width, 1)
    return lax.dynamic_update_slice_in_dim(accum, old_part + term, start_col, 1)


def local(features, right_side, variance, hilbert_order, tile_list):
    width = features.shape[1]
    perm_local = hilbert_order[0]
    ordered = jnp.take(features, perm_local, axis=1)
    rhs_ordered = jnp.take(right_side, perm_local, axis=1)
    var_ordered = jnp.take(variance, perm_local, axis=0)
    norm_own = jnp.sum(jnp.square(ordered.astype(jnp.float32)), axis=0)
    every_feat = lax.all_gather(ordered, "row", axis=1, tiled=True)
    every_norm = jnp.sum(jnp.square(every_feat.astype(jnp.float32)), axis=0)
    my_pairs = tile_list[0]
    sol_ord = jnp.zeros_like(rhs_ordered)
    res_ord = rhs_ordered
    direction = rhs_ordered
    norm_now = lax.psum(jnp.sum(res_ord * res_ord, axis=1), "row")
    for iteration in range(ITERS):
        rounded = direction.astype(jnp.bfloat16)
        every_dir = lax.all_gather(rounded, "row", axis=1, tiled=True)
        own_rows, unused_back = tile_terms(
            ordered, norm_own, ordered, norm_own, rounded, rounded, False
        )
        others = jnp.zeros((direction.shape[0], every_dir.shape[1]), jnp.float32)
        state_pair = (own_rows, others)
        for slot_index in range(my_pairs.shape[0]):
            row_block = my_pairs[slot_index, 0]
            col_block = my_pairs[slot_index, 1]

            def pair_work(state_in):
                own_in, others_in = state_in
                row_feat = lax.dynamic_slice_in_dim(every_feat, row_block * width, width, 1)
                row_norm = lax.dynamic_slice_in_dim(every_norm, row_block * width, width, 0)
                row_vec = lax.dynamic_slice_in_dim(every_dir, row_block * width, width, 1)
                col_feat = lax.dynamic_slice_in_dim(every_feat, col_block * width, width, 1)
                col_norm = lax.dynamic_slice_in_dim(every_norm, col_block * width, width, 0)
                col_vec = lax.dynamic_slice_in_dim(every_dir, col_block * width, width, 1)
                row_term, col_term = tile_terms(
                    row_feat, row_norm, col_feat, col_norm, row_vec, col_vec, True
                )
                others_out = add_block(others_in, col_block, width, col_term)
                return (own_in + row_term, others_out)

            state_pair = lax.cond(row_block >= 0, pair_work, lambda state_in: state_in, state_pair)
        own_rows, others = state_pair
        arrived = lax.psum_scatter(others, "row", scatter_dimension=1, tiled=True)
        image = var_ordered[None, :] * direction + own_rows + arrived
        curve_sum = lax.psum(jnp.sum(direction * image, axis=1), "row")
        step_size = norm_now / curve_sum
        sol_ord = sol_ord + step_size[:, None] * direction
        res_ord = res_ord - step_size[:, None] * image
        norm_next = norm_now
        if iteration + 1 < ITERS:
            norm_next = lax.psum(jnp.sum(res_ord * res_ord, axis=1), "row")
        if iteration + 1 < ITERS:
            direction = res_ord + (norm_next / norm_now)[:, None] * direction
            norm_now = norm_next
    return (sol_ord, res_ord)


def solution(mesh):
    in_specs = (
        P(None, ("group", "row")),
        P(None, ("group", "row")),
        P(("group", "row")),
        P(("group", "row"), None),
        P(("group", "row"), None, None),
    )
    out_specs = (P(None, ("group", "row")), P(None, ("group", "row")))
    return jax.shard_map(local, mesh=mesh, in_specs=in_specs, out_specs=out_specs, check_vma=False)
```

profile of v0, /device:TPU:0, one launch (start us, length us, event | category | flops | bytes accessed | tf_op | source)
XLA Modules:
  0.0 686.5 jit_solution(11077723319729190476)
XLA Ops:
  28.3 26.6 %all_gather.10 = bf16[8,32768]{1,0:T(8,128)(2,1)S(1)} all-gather(bf16[8,2048]{1,0:T(8,128)(2,1)S(1)} %bitcast_convert_fusion), channel_id=1, replica_groups=mesh['group'=2,'row'=16] {'row'}, dimensions={1}, use_global_device_ids=true | all-gather | bytes 557056 | tf_op jit(solution)/shard_map/all_gather | solution.py:69
  73.9 23.9 %all-gather.2.cloned.1.call-done = bf16[32,32768]{0,1:T(8,128)(2,1)} async-done(((bf16[32,2048]{0,1:T(8,128)(2,1)}), bf16[32,32768]{0,1:T(8,128)(2,1)}) %all-gather.2.cloned.1.call-update) | async-done | bytes 2097168 | tf_op jit(solution)/shard_map/all_gather | solution.py:60
  104.6 33.6 %conditional.10 = (f32[8,2048]{1,0:T(8,128)S(1)}, f32[8,32768]{1,0:T(8,128)}) conditional(s32[]{:T(128)} %convert_element_type.120, f32[8,2048]{1,0:T(8,128)S(1)} %get-tuple-element.1998, (s32[]{:T(128)}, bf16[32,32768]{0,1:T(8,128)(2,1)}, f32[32768]{0:T(1024)S(1)}, s32[]{:T(128)}, bf16[8,32768]{1,0:T(8,128)(2,1)S(1)}, ...), branch_computations={%region_6.7_spmd, %region_7.10_spmd} | conditional | flops 29409292 | bytes 8216517 | solution.py:93
  112.8 23.7 %while.182 = (s32[]{:T(128)}, f32[8,2048]{1,0:T(8,128)S(1)}, f32[8,2048]{1,0:T(8,128)S(1)}, f32[2048]{0:T(1024)S(1)}, f32[2048]{0:T(1024)S(1)}, /*index=5*/bf16[...) while((s32[]{:T(128)}, f32[8,2048]{1,0:T(8,128)S(1)}, ...), condition=%wide.region_9.9_spmd.clone, body=%wide.region_8.8_spmd.clone.sunk | while | flops 29392900 | bytes 1892037 | solution.py:44
  138.2 33.4 %conditional.11 = ((f32[8,2048]{1,0:T(8,128)S(1)}, f32[8,32768]{1,0:T(8,128)})) conditional(s32[]{:T(128)} %convert_element_type.119, (f32[8,2048]{1,0:T(8,128)S(1)}, f32[8,32768]{1,0:T(8,128)}) %conditional.10, (s32[]{:T(128)}, bf16[32,32768]{0,1:T(8,128)(2,1)}, f32[32768]{0:T(1024)S(1)}, s32[]{:T(128)}, bf16[8,32768]{1,0:T(8,128)(2,1)S(1)}, ...), branch_computations={%region_10.11_spmd, %region_11.14_spmd} | conditional | flops 29425676 | bytes 7233481 | solution.py:93
  146.4 23.7 %while.183 = (s32[]{:T(128)}, f32[8,2048]{1,0:T(8,128)S(1)}, f32[8,2048]{1,0:T(8,128)S(1)}, f32[2048]{0:T(1024)S(1)}, f32[2048]{0:T(1024)S(1)}, /*index=5*/bf16[...) while((s32[]{:T(128)}, f32[8,2048]{1,0:T(8,128)S(1)}, ...), condition=%wide.region_13.13_spmd.clone, body=%wide.region_12.12_spmd.clone.sunk | while | flops 29392900 | bytes 1892037 | solution.py:44
  171.6 33.5 %conditional.12 = ((f32[8,2048]{1,0:T(8,128)S(1)}, f32[8,32768]{1,0:T(8,128)})) conditional(s32[]{:T(128)} %convert_element_type.118, (f32[8,2048]{1,0:T(8,128)S(1)}, f32[8,32768]{1,0:T(8,128)}) %get-tuple-element.3934, (s32[]{:T(128)}, bf16[32,32768]{0,1:T(8,128)(2,1)}, f32[32768]{0:T(1024)S(1)}, s32[]{:T(128)}, bf16[8,32768]{1,0:T(8,128)(2,1)S(1)}, ...), branch_computations={%region_14.15_spmd, %region_15.18_spmd} | conditional | flops 29425676 | bytes 7233481 | solution.py:93
  179.9 23.7 %while.184 = (s32[]{:T(128)}, f32[8,2048]{1,0:T(8,128)S(1)}, f32[8,2048]{1,0:T(8,128)S(1)}, f32[2048]{0:T(1024)S(1)}, f32[2048]{0:T(1024)S(1)}, /*index=5*/bf16[...) while((s32[]{:T(128)}, f32[8,2048]{1,0:T(8,128)S(1)}, ...), condition=%wide.region_17.17_spmd.clone, body=%wide.region_16.16_spmd.clone.sunk | while | flops 29392900 | bytes 1892037 | solution.py:44
  205.1 33.4 %conditional.13 = ((f32[8,2048]{1,0:T(8,128)S(1)}, f32[8,32768]{1,0:T(8,128)})) conditional(s32[]{:T(128)} %convert_element_type.117, (f32[8,2048]{1,0:T(8,128)S(1)}, f32[8,32768]{1,0:T(8,128)}) %get-tuple-element.3935, (s32[]{:T(128)}, bf16[32,32768]{0,1:T(8,128)(2,1)}, f32[32768]{0:T(1024)S(1)}, s32[]{:T(128)}, bf16[8,32768]{1,0:T(8,128)(2,1)S(1)}, ...), branch_computations={%region_18.19_spmd, %region_19.22_spmd} | conditional | flops 29425676 | bytes 7233481 | solution.py:93
  238.5 33.8 %conditional.14 = ((f32[8,2048]{1,0:T(8,128)S(1)}, f32[8,32768]{1,0:T(8,128)})) conditional(s32[]{:T(128)} %convert_element_type.116, (f32[8,2048]{1,0:T(8,128)S(1)}, f32[8,32768]{1,0:T(8,128)}) %get-tuple-element.3936, (s32[]{:T(128)}, bf16[32,32768]{0,1:T(8,128)(2,1)}, f32[32768]{0:T(1024)S(1)}, s32[]{:T(128)}, bf16[8,32768]{1,0:T(8,128)(2,1)S(1)}, ...), branch_computations={%region_22.23_spmd, %region_23.26_spmd} | conditional | flops 29425676 | bytes 7233481 | solution.py:93
  247.1 23.7 %while.186 = (s32[]{:T(128)}, f32[8,2048]{1,0:T(8,128)S(1)}, f32[8,2048]{1,0:T(8,128)S(1)}, f32[2048]{0:T(1024)S(1)}, f32[2048]{0:T(1024)S(1)}, /*index=5*/bf16[...) while((s32[]{:T(128)}, f32[8,2048]{1,0:T(8,128)S(1)}, ...), condition=%wide.region_25.25_spmd.clone, body=%wide.region_24.24_spmd.clone.sunk | while | flops 29392900 | bytes 1892037 | solution.py:44
  284.2 42.9 %reduce-scatter.3.cloned.1.call-done = f32[8,2048]{1,0:T(8,128)} async-done(((f32[8,32768]{1,0:T(8,128)}), f32[8,2048]{1,0:T(8,128)}) %reduce-scatter.3.cloned.1.call-update) | async-done | bytes 65552 | tf_op jit(solution)/shard_map/reduce_scatter | solution.py:95
  328.1 29.6 %all-reduce = (f32[8]{0:T(128)S(1)}, f32[8]{0:T(128)S(1)}) all-reduce(f32[8]{0:T(128)S(1)} %get-tuple-element.2559, f32[8]{0:T(128)S(1)} %get-tuple-element.2558), channel_id=1, replica_groups=mesh['group'=2,'row'=16] {'row'}, use_global_device_ids=true, to_apply=%region_1.2 | all-reduce | flops 16 | bytes 128 | tf_op jit(solution)/shard_map/psum | solution.py:66
  358.7 29.5 %psum.30 = f32[8]{0:T(128)S(1)} all-reduce(f32[8]{0:T(128)S(1)} %get-tuple-element.2762), channel_id=1, replica_groups=mesh['group'=2,'row'=16] {'row'}, use_global_device_ids=true, to_apply=%region_30.31 | all-reduce | flops 8 | bytes 64 | tf_op jit(solution)/shard_map/psum | solution.py:103
  425.4 33.6 %conditional.15 = (f32[8,2048]{1,0:T(8,128)S(1)}, f32[8,32768]{1,0:T(8,128)}) conditional(s32[]{:T(128)} %convert_element_type.120, f32[8,2048]{1,0:T(8,128)S(1)} %get-tuple-element.2009, (s32[]{:T(128)}, bf16[32,32768]{0,1:T(8,128)(2,1)}, f32[32768]{0:T(1024)S(1)}, s32[]{:T(128)}, bf16[8,32768]{1,0:T(8,128)(2,1)S(1)}, ...), branch_computations={%region_33.34_spmd, %region_34.37_spmd} | conditional | flops 29409292 | bytes 8216517 | solution.py:93
  459.0 33.4 %conditional.16 = ((f32[8,2048]{1,0:T(8,128)S(1)}, f32[8,32768]{1,0:T(8,128)})) conditional(s32[]{:T(128)} %convert_element_type.119, (f32[8,2048]{1,0:T(8,128)S(1)}, f32[8,32768]{1,0:T(8,128)}) %conditional.15, (s32[]{:T(128)}, bf16[32,32768]{0,1:T(8,128)(2,1)}, f32[32768]{0:T(1024)S(1)}, s32[]{:T(128)}, bf16[8,32768]{1,0:T(8,128)(2,1)S(1)}, ...), branch_computations={%region_37.38_spmd, %region_38.41_spmd} | conditional | flops 29425676 | bytes 7233481 | solution.py:93
  492.4 33.5 %conditional.17 = ((f32[8,2048]{1,0:T(8,128)S(1)}, f32[8,32768]{1,0:T(8,128)})) conditional(s32[]{:T(128)} %convert_element_type.118, (f32[8,2048]{1,0:T(8,128)S(1)}, f32[8,32768]{1,0:T(8,128)}) %get-tuple-element.3938, (s32[]{:T(128)}, bf16[32,32768]{0,1:T(8,128)(2,1)}, f32[32768]{0:T(1024)S(1)}, s32[]{:T(128)}, bf16[8,32768]{1,0:T(8,128)(2,1)S(1)}, ...), branch_computations={%region_41.42_spmd, %region_42.45_spmd} | conditional | flops 29425676 | bytes 7233481 | solution.py:93
  500.6 23.7 %while.189 = (s32[]{:T(128)}, f32[8,2048]{1,0:T(8,128)S(1)}, f32[8,2048]{1,0:T(8,128)S(1)}, f32[2048]{0:T(1024)S(1)}, f32[2048]{0:T(1024)S(1)}, /*index=5*/bf16[...) while((s32[]{:T(128)}, f32[8,2048]{1,0:T(8,128)S(1)}, ...), condition=%wide.region_44.44_spmd.clone, body=%wide.region_43.43_spmd.clone.sunk | while | flops 29392900 | bytes 1892037 | solution.py:44
  525.9 33.4 %conditional.18 = ((f32[8,2048]{1,0:T(8,128)S(1)}, f32[8,32768]{1,0:T(8,128)})) conditional(s32[]{:T(128)} %convert_element_type.117, (f32[8,2048]{1,0:T(8,128)S(1)}, f32[8,32768]{1,0:T(8,128)}) %get-tuple-element.3939, (s32[]{:T(128)}, bf16[32,32768]{0,1:T(8,128)(2,1)}, f32[32768]{0:T(1024)S(1)}, s32[]{:T(128)}, bf16[8,32768]{1,0:T(8,128)(2,1)S(1)}, ...), branch_computations={%region_45.46_spmd, %region_46.49_spmd} | conditional | flops 29425676 | bytes 7233481 | solution.py:93
  534.1 23.7 %while.190 = (s32[]{:T(128)}, f32[8,2048]{1,0:T(8,128)S(1)}, f32[8,2048]{1,0:T(8,128)S(1)}, f32[2048]{0:T(1024)S(1)}, f32[2048]{0:T(1024)S(1)}, /*index=5*/bf16[...) while((s32[]{:T(128)}, f32[8,2048]{1,0:T(8,128)S(1)}, ...), condition=%wide.region_48.48_spmd.clone, body=%wide.region_47.47_spmd.clone.sunk | while | flops 29392900 | bytes 1892037 | solution.py:44
  559.3 33.6 %conditional.19 = ((f32[8,2048]{1,0:T(8,128)S(1)}, f32[8,32768]{1,0:T(8,128)})) conditional(s32[]{:T(128)} %convert_element_type.116, (f32[8,2048]{1,0:T(8,128)S(1)}, f32[8,32768]{1,0:T(8,128)}) %get-tuple-element.3940, (s32[]{:T(128)}, bf16[32,32768]{0,1:T(8,128)(2,1)}, f32[32768]{0:T(1024)S(1)}, s32[]{:T(128)}, bf16[8,32768]{1,0:T(8,128)(2,1)S(1)}, ...), branch_computations={%region_49.50_spmd, %region_50.53_spmd} | conditional | flops 29425676 | bytes 7233481 | solution.py:93
  567.7 23.7 %while.191 = (s32[]{:T(128)}, f32[8,2048]{1,0:T(8,128)S(1)}, f32[8,2048]{1,0:T(8,128)S(1)}, f32[2048]{0:T(1024)S(1)}, f32[2048]{0:T(1024)S(1)}, /*index=5*/bf16[...) while((s32[]{:T(128)}, f32[8,2048]{1,0:T(8,128)S(1)}, ...), condition=%wide.region_52.52_spmd.clone, body=%wide.region_51.51_spmd.clone.sunk | while | flops 29392900 | bytes 1892037 | solution.py:44
  592.9 54.9 %reduce-scatter.5.cloned.1.call-done = f32[8,2048]{1,0:T(8,128)} async-done(((f32[8,32768]{1,0:T(8,128)}), f32[8,2048]{1,0:T(8,128)}) %reduce-scatter.5.cloned.1.call-update) | async-done | bytes 65552 | tf_op jit(solution)/shard_map/reduce_scatter | solution.py:95
  648.8 29.6 %psum.31 = f32[8]{0:T(128)S(1)} all-reduce(f32[8]{0:T(128)S(1)} %multiply_reduce_fusion.2), channel_id=1, replica_groups=mesh['group'=2,'row'=16] {'row'}, use_global_device_ids=true, to_apply=%region_55.56 | all-reduce | flops 8 | bytes 64 | tf_op jit(solution)/shard_map/psum | solution.py:97
  (835 shorter events, 525.6 us)
Async XLA Ops:
  7.2 265.2 %copy-start = (f32[2048]{0:T(1024)S(1)}, f32[2048]{0:T(1024)}, u32[]{:S(2)}) copy-start(f32[2048]{0:T(1024)} %param.51) | copy-start | bytes 24580
  7.2 11.3 %copy-start.4 = (f32[8,2048]{1,0:T(8,128)S(1)}, f32[8,2048]{1,0:T(8,128)}, u32[]{:S(2)}) copy-start(f32[8,2048]{1,0:T(8,128)} %param.50) | copy-start | bytes 196612
  7.2 90.6 %all-gather.2.cloned.1.call-start = ((), (), s32[]{:S(2)}) async-start(), calls=%async_computation.2 | async-start | bytes 8912896 | tf_op jit(solution)/shard_map/all_gather | solution.py:60
  17.2 7.4 %copy-start.5 = (s32[1,5,2]{1,2,0:T(2,128)S(1)}, s32[1,5,2]{1,2,0:T(2,128)}, u32[]{:S(2)}) copy-start(s32[1,5,2]{1,2,0:T(2,128)} %param.53) | copy-start | bytes 124
  17.2 309.9 %reduce-scatter.3.cloned.1.call-start = ((), (), s32[]{:S(2)}) async-start(), calls=%async_computation.3 | async-start | bytes 1114112 | tf_op jit(solution)/shard_map/reduce_scatter | solution.py:95
  73.2 0.7 copy-start.1
  272.3 375.4 %reduce-scatter.5.cloned.1.call-start = ((), (), s32[]{:S(2)}) async-start(), calls=%async_computation.4 | async-start | bytes 1114112 | tf_op jit(solution)/shard_map/reduce_scatter | solution.py:95
  272.4 11.8 %copy-start.3 = (s32[1,2048]{1,0:T(1,128)S(1)}, s32[1,2048]{1,0:T(1,128)}, u32[]{:S(2)}) copy-start(s32[1,2048]{1,0:T(1,128)} %param.52) | copy-start | bytes 24580
  272.4 134.6 %copy-start.2 = (bf16[32,2048]{1,0:T(8,128)(2,1)S(1)}, bf16[32,2048]{1,0:T(8,128)(2,1)}, u32[]{:S(2)}) copy-start(bf16[32,2048]{1,0:T(8,128)(2,1)} %copy-done.1) | copy-start | bytes 393220
Sparse Core Ops, SparseCore 0:
  17.3 80.3 all-gather.1
  272.4 54.6 reduce-scatter.2
  593.0 54.6 reduce-scatter.4
where the time goes:
time: 689 us; the launch traced here: 686 us
  matrix products  258 us (37%)
  blocking collectives  134 us (19%)
  waiting for transfers between devices  122 us (18%)
  local copies, waits for them, and re-layouts  115 us (17%)
  other arithmetic  26.2 us (4%)
  between operations  16.9 us (2%)
  loops' own time  14.9 us (2%)
    dot_general x160, matrix products, wendland(): lax.dot_general(left_feat, right_feat, (((0,), (0,)), ((), ())), preferre...  156 us
    reduce_scatter x2, waiting for transfers between devices, local(): arrived = lax.psum_scatter(others, 'row', scatter_dimension=1, tiled=True)  97.7 us
    dot_general x192, matrix products, sub_step(): lax.dot_general(right_vec, kernel, (((1,), (1,)), ((), ())), preferred_el...  73 us
    another operation x24, local copies, waits for them, and re-layouts  71 us
    all_gather x2, blocking collectives, local(): every_dir = lax.all_gather(rounded, 'row', axis=1, tiled=True)  45.3 us
    psum x1, blocking collectives, local(): norm_now = lax.psum(jnp.sum(res_ord * res_ord, axis=1), 'row')  29.6 us
    psum x1, blocking collectives, local(): curve_sum = lax.psum(jnp.sum(direction * image, axis=1), 'row')  29.6 us
    psum x1, blocking collectives, local(): norm_next = lax.psum(jnp.sum(res_ord * res_ord, axis=1), 'row')  29.5 us
  transfers between devices with their start and end apart: 3, of which 3 were waited for; matrix products, arithmetic and copies ran while one was open for 6% of the time, Pallas kernels for 0%

commit v1 on v0

v1 whole, which is shorter than its diff:
```python
import jax
import jax.numpy as jnp
import numpy as np
from jax import lax
from jax.experimental import pallas as pl
from jax.experimental.pallas import tpu as pltpu
from jax.sharding import PartitionSpec as P

SHRINK = 0.95
SCALE = 20.0 * (20.0 / 19.0) ** 19
DIAGONAL = float(1.0 - SCALE * float(np.float32(1.0 / SCALE).astype(jnp.bfloat16)))
KDIM = 128
CHUNK = 256
ROWS = 512


def split_three(value):
    high = value.astype(jnp.bfloat16).astype(jnp.float32)
    rest = value - high
    middle = rest.astype(jnp.bfloat16).astype(jnp.float32)
    return high, middle, rest - middle


def norm_rows(norm, first):
    high, middle, low = split_three(norm)
    row = lax.broadcasted_iota(jnp.int32, (32, norm.shape[1]), 0)
    out = jnp.where(row < 6, 1.0, 0.0)
    out = jnp.where(row == first, high, out)
    out = jnp.where(row == first + 1, middle, out)
    return jnp.where(row == first + 2, low, out).astype(jnp.bfloat16)


def own_factor(feat):
    wide = feat.astype(jnp.float32)
    norm = jnp.sum(wide * wide, axis=0, keepdims=True) * (SHRINK * SHRINK)
    pieces = split_three(wide * (-2.0 * SHRINK * SHRINK))
    return jnp.concatenate(
        [piece.astype(jnp.bfloat16) for piece in pieces] + [norm_rows(norm, 0)], axis=0
    )


def other_factor(feat):
    wide = feat.astype(jnp.float32)
    norm = jnp.sum(wide * wide, axis=0, keepdims=True) * (SHRINK * SHRINK)
    whole = jnp.concatenate([feat, feat, feat, norm_rows(norm, 3)], axis=0)
    return jnp.transpose(whole)


def psi_tile(dist):
    dist = jnp.maximum(dist, 1e-30)
    radius = dist * lax.rsqrt(dist)
    u = jnp.maximum(SHRINK - radius, 0.0)
    two = u * u
    four = two * two
    eight = four * four
    sixteen = eight * eight
    return (sixteen * two * (u - two)).astype(jnp.bfloat16)


def tile_rows(left_ref, right_ref, vec_ref, begin, tile_ref, sum_ref):
    width = right_ref.shape[1]

    def step(index, carry):
        at = pl.multiple_of(index * CHUNK, CHUNK)
        left = left_ref[pl.ds(pl.multiple_of(begin + at, CHUNK), CHUNK), :]
        vec = vec_ref[:, pl.ds(pl.multiple_of(begin + at, CHUNK), CHUNK)]
        for col in range(0, width, CHUNK):
            parts = []
            for half in range(0, CHUNK, 128):
                dist = jnp.dot(
                    left[half : half + 128],
                    right_ref[:, col : col + CHUNK],
                    preferred_element_type=jnp.float32,
                )
                part = psi_tile(dist)
                tile_ref[pl.ds(at + half, 128), col : col + CHUNK] = part
                parts.append(part)
            sum_ref[:, col : col + CHUNK] += jnp.dot(
                vec, jnp.concatenate(parts, axis=0), preferred_element_type=jnp.float32
            )
        return carry

    lax.fori_loop(0, ROWS // CHUNK, step, 0)


def own_kernel(pay_ref, tile_ref, sum_ref, left_ref, right_ref, vec_ref):
    step = pl.program_id(0)

    @pl.when(step == 0)
    def _():
        pay = pay_ref[...]
        left_ref[...] = other_factor(pay[:32])
        right_ref[...] = own_factor(pay[:32])
        vec_ref[...] = pay[32:40]
        sum_ref[...] = jnp.zeros_like(sum_ref)

    tile_rows(left_ref, right_ref, vec_ref, step * ROWS, tile_ref, sum_ref)


def pair_kernel(
    slots_ref, own_ref, pay_ref, first_ref, tile_ref, sum_ref, left_ref, right_ref, vec_ref
):
    slot, step = pl.program_id(0), pl.program_id(1)

    @pl.when((slot == 0) & (step == 0))
    def _():
        right_ref[...] = own_factor(own_ref[...][:32])
        sum_ref[...] = first_ref[...]

    @pl.when(slot < slots_ref[0])
    def _():
        @pl.when(step == 0)
        def _():
            pay = pay_ref[0]
            left_ref[...] = other_factor(pay[:32])
            vec_ref[...] = pay[32:40]

        tile_rows(left_ref, right_ref, vec_ref, step * ROWS, tile_ref.at[0], sum_ref)


def again_kernel(slots_ref, tile_ref, vec_ref, first_ref, sum_ref):
    slot, step = pl.program_id(0), pl.program_id(1)

    @pl.when((slot == 0) & (step == 0))
    def _():
        sum_ref[...] = first_ref[...]

    @pl.when(slot < slots_ref[0])
    def _():
        at = pl.multiple_of(step * ROWS, ROWS)
        sum_ref[...] += jnp.dot(
            vec_ref[0, :, pl.ds(at, ROWS)], tile_ref[0], preferred_element_type=jnp.float32
        )


def own_again_kernel(tile_ref, vec_ref, sum_ref):
    step = pl.program_id(0)

    @pl.when(step == 0)
    def _():
        sum_ref[...] = jnp.zeros_like(sum_ref)

    at = pl.multiple_of(step * ROWS, ROWS)
    sum_ref[...] += jnp.dot(
        vec_ref[:, pl.ds(at, ROWS)], tile_ref[...], preferred_element_type=jnp.float32
    )


def order_kernel(rows_ref, perm_ref, out_ref):
    rows = rows_ref[...]
    count, width = rows.shape
    pieces = jnp.concatenate([piece for piece in split_three(rows)], axis=0).astype(jnp.bfloat16)
    perm = perm_ref[...]
    for col in range(0, width, CHUNK):
        total = jnp.zeros((3 * count, CHUNK), jnp.float32)
        for at in range(0, width, CHUNK):
            index = lax.broadcasted_iota(jnp.int32, (CHUNK, CHUNK), 0) + at
            pick = jnp.where(index == perm[:, col : col + CHUNK], 1.0, 0.0).astype(jnp.bfloat16)
            total += jnp.dot(pieces[:, at : at + CHUNK], pick, preferred_element_type=jnp.float32)
        out_ref[:, col : col + CHUNK] = (
            total[:count] + total[count : 2 * count] + total[2 * count :]
        )


def swap(value, mask, count):
    return lax.ppermute(value, "row", [(i, i ^ mask) for i in range(count)])


def halves(count):
    mask = count // 2
    while mask:
        yield mask
        mask //= 2


def tree_sum(value, count):
    for mask in halves(count):
        value = value + swap(value, mask, count)
    return value


def tree_gather(value, count):
    blocks, masks = value[None], [0]
    for mask in halves(count):
        blocks = jnp.concatenate([blocks, swap(blocks, mask, count)], axis=0)
        masks = masks + [other ^ mask for other in masks]
    return blocks, masks


def partners(tile_list, count):
    most = tile_list.shape[1]
    me = lax.axis_index("row")
    lists, masks = tree_gather(tile_list[0, :, 1], count)
    number = me ^ jnp.asarray(masks, jnp.int32)
    lower = jnp.any(lists == me, axis=1)
    upper = jnp.any(tile_list[0, :, 1][None, :] == number[:, None], axis=1)
    valid = lower | upper
    before = jnp.sum((valid[None, :] & (number[None, :] < number[:, None])).astype(jnp.int32), axis=1)
    total = jnp.sum(valid.astype(jnp.int32))
    place = jnp.minimum(jnp.arange(most), jnp.maximum(total - 1, 0))
    hit = valid[None, :] & (before[None, :] == place[:, None])
    picked = jnp.sum(jnp.where(hit, number[None, :], 0), axis=1)
    return jnp.concatenate([total[None], picked]).astype(jnp.int32)


def local(features, right_side, variance, hilbert_order, tile_list):
    width = features.shape[1]
    count = lax.axis_size("row")
    most = tile_list.shape[1]
    steps = width // ROWS
    f32 = jnp.float32
    shape = jax.ShapeDtypeStruct
    params = pltpu.CompilerParams(vmem_limit_bytes=40 * 1024 * 1024)

    payload = jnp.concatenate([features, right_side.astype(jnp.bfloat16)], axis=0)
    slots = partners(tile_list, count)
    every = lax.all_gather(payload, "row", axis=0)
    scratch = [
        pltpu.VMEM((width, KDIM), jnp.bfloat16),
        pltpu.VMEM((KDIM, width), jnp.bfloat16),
        pltpu.VMEM((8, width), jnp.bfloat16),
    ]
    own_tile, own_sum = pl.pallas_call(
        own_kernel,
        grid=(steps,),
        in_specs=[pl.BlockSpec(payload.shape, lambda i: (0, 0))],
        out_specs=[
            pl.BlockSpec((ROWS, width), lambda i: (i, 0)),
            pl.BlockSpec((8, width), lambda i: (0, 0)),
        ],
        out_shape=[shape((width, width), jnp.bfloat16), shape((8, width), f32)],
        scratch_shapes=scratch,
        compiler_params=params,
        cost_estimate=pl.CostEstimate(
            flops=30 * width * width, bytes_accessed=2 * width * width, transcendentals=width * width
        ),
        name="own_tile",
    )(payload)

    def tile_at(k, i, s):
        live = k < s[0]
        return (jnp.minimum(k, jnp.maximum(s[0] - 1, 0)), jnp.where(live, i, steps - 1), 0)

    pair_tiles, pair_sum = pl.pallas_call(
        pair_kernel,
        grid_spec=pltpu.PrefetchScalarGridSpec(
            num_scalar_prefetch=1,
            grid=(most, steps),
            in_specs=[
                pl.BlockSpec(payload.shape, lambda k, i, s: (0, 0)),
                pl.BlockSpec((1,) + payload.shape, lambda k, i, s: (s[1 + k], 0, 0)),
                pl.BlockSpec((8, width), lambda k, i, s: (0, 0)),
            ],
            out_specs=[
                pl.BlockSpec((1, ROWS, width), tile_at),
                pl.BlockSpec((8, width), lambda k, i, s: (0, 0)),
            ],
            scratch_shapes=scratch,
        ),
        out_shape=[shape((most, width, width), jnp.bfloat16), shape((8, width), f32)],
        compiler_params=params,
        name="pair_tiles",
    )(slots, payload, every, own_sum)

    first = (variance + DIAGONAL)[None, :] * right_side + SCALE * pair_sum
    rounded = first.astype(jnp.bfloat16)
    every_first = lax.all_gather(rounded, "row", axis=0)

    sums = jnp.stack([jnp.sum(right_side * right_side, axis=1), jnp.sum(right_side * first, axis=1)])
    sums = tree_sum(sums, count)
    step_one = sums[0] / sums[1]
    res_one = right_side - step_one[:, None] * first
    norm_one = tree_sum(jnp.sum(res_one * res_one, axis=1), count)
    ratio = norm_one / sums[0]

    own_again = pl.pallas_call(
        own_again_kernel,
        grid=(steps,),
        in_specs=[
            pl.BlockSpec((ROWS, width), lambda i: (i, 0)),
            pl.BlockSpec((8, width), lambda i: (0, 0)),
        ],
        out_specs=pl.BlockSpec((8, width), lambda i: (0, 0)),
        out_shape=shape((8, width), f32),
        compiler_params=params,
        name="own_again",
    )(own_tile, rounded)
    pair_again = pl.pallas_call(
        again_kernel,
        grid_spec=pltpu.PrefetchScalarGridSpec(
            num_scalar_prefetch=1,
            grid=(most, steps),
            in_specs=[
                pl.BlockSpec((1, ROWS, width), tile_at),
                pl.BlockSpec((1, 8, width), lambda k, i, s: (s[1 + k], 0, 0)),
                pl.BlockSpec((8, width), lambda k, i, s: (0, 0)),
            ],
            out_specs=pl.BlockSpec((8, width), lambda k, i, s: (0, 0)),
        ),
        out_shape=shape((8, width), f32),
        compiler_params=params,
        name="pair_again",
    )(slots, pair_tiles, every_first, own_again)
    second = (variance + DIAGONAL)[None, :] * first + SCALE * pair_again

    direction = res_one + ratio[:, None] * right_side
    image = (1.0 + ratio)[:, None] * first - step_one[:, None] * second
    curve = tree_sum(jnp.sum(direction * image, axis=1), count)
    step_two = norm_one / curve

    rows = jnp.concatenate([step_one[:, None] * right_side, direction, res_one, image], axis=0)
    ordered = pl.pallas_call(
        order_kernel,
        out_shape=shape(rows.shape, f32),
        compiler_params=params,
        name="curve_order",
    )(rows, hilbert_order)
    solved = ordered[:8] + step_two[:, None] * ordered[8:16]
    residual = ordered[16:24] - step_two[:, None] * ordered[24:32]
    return (solved, residual)


def solution(mesh):
    in_specs = (
        P(None, ("group", "row")),
        P(None, ("group", "row")),
        P(("group", "row")),
        P(("group", "row"), None),
        P(("group", "row"), None, None),
    )
    out_specs = (P(None, ("group", "row")), P(None, ("group", "row")))
    return jax.shard_map(local, mesh=mesh, in_specs=in_specs, out_specs=out_specs, check_vma=False)
```

time: 689 us -> 232 us (0.34)
  matrix products: 258 us -> 0 us
  Pallas kernels: 0 us -> 125 us
  blocking collectives: 134 us -> 18.9 us
  local copies, waits for them, and re-layouts: 115 us -> 10.9 us
  waiting for transfers between devices: 122 us -> 41.2 us
  other arithmetic: 26.2 us -> 7.16 us
  loops' own time: 14.9 us -> 0 us
  starting transfers between devices: 0.12 us -> 12.9 us
    dot_general x512 -> x0, matrix products: 258 us -> none  [the longest x160 156 us: wendland(): lax.dot_general(left_feat, right_feat, (((0,), (0,)), ((), ())), preferre...]
    pallas_call x0 -> x5, Pallas kernels: none -> 125 us  [the longest x1 83.3 us: local(): pl.pallas_call(pair_kernel, grid_spec=pltpu.PrefetchScalarGridSpec(num_sc...]
    reduce_scatter x2 -> x0, waiting for transfers between devices: 97.7 us -> none  [local(): arrived = lax.psum_scatter(others, 'row', scatter_dimension=1, tiled=True)]
    psum x3 -> x0, blocking collectives: 88.6 us -> none  [the longest x1 29.6 us: local(): norm_now = lax.psum(jnp.sum(res_ord * res_ord, axis=1), 'row')]
    another operation x24 -> x0, local copies, waits for them, and re-layouts: 71 us -> none
    ppermute x0 -> x16, waiting for transfers between devices: none -> 31.1 us  [swap(): return lax.ppermute(value, 'row', [(i, i ^ mask) for i in range(count)])]
    all_gather x2 -> x1, blocking collectives: 45.3 us -> 18.9 us  [local(): every_first = lax.all_gather(rounded, 'row', axis=0)]
    gather x4 -> x0, local copies, waits for them, and re-layouts: 23.7 us -> none  [the longest x1 11.8 us: local(): var_ordered = jnp.take(variance, perm_local, axis=0)]
  transfers between devices with their start and end apart: 3 -> 17, of which waited for: 3 -> 14; matrix products, arithmetic and copies ran while one was open for 6% -> 2% of each run, Pallas kernels for 0% -> 17%
where the time goes in v1:
time: 232 us; the launch traced here: 231 us
  Pallas kernels  125 us (54%)
  waiting for transfers between devices  41.2 us (18%)
  blocking collectives  18.9 us (8%)
  between operations  14.8 us (6%)
  starting transfers between devices  12.9 us (6%)
  local copies, waits for them, and re-layouts  10.9 us (5%)
  other arithmetic  7.16 us (3%)
    pallas_call x1, Pallas kernels, local(): pl.pallas_call(pair_kernel, grid_spec=pltpu.PrefetchScalarGridSpec(num_sc...  83.3 us
    ppermute x16, waiting for transfers between devices, swap(): return lax.ppermute(value, 'row', [(i, i ^ mask) for i in range(count)])  31.1 us
    pallas_call x1, Pallas kernels, local(): pl.pallas_call(again_kernel, grid_spec=pltpu.PrefetchScalarGridSpec(num_s...  22.4 us
    all_gather x1, blocking collectives, local(): every_first = lax.all_gather(rounded, 'row', axis=0)  18.9 us
    pallas_call x1, Pallas kernels, local(): pl.pallas_call(own_kernel, grid=(steps,), in_specs=[pl.BlockSpec(payload....  16.3 us
    ppermute x16, starting transfers between devices, swap(): return lax.ppermute(value, 'row', [(i, i ^ mask) for i in range(count)])  12.8 us
    unnamed x14, local copies, waits for them, and re-layouts  10.2 us
    all_gather x1, waiting for transfers between devices, local(): every = lax.all_gather(payload, 'row', axis=0)  10 us
  transfers between devices with their start and end apart: 17, of which 14 were waited for; matrix products, arithmetic and copies ran while one was open for 2% of the time, Pallas kernels for 17%

profile of v1, /device:TPU:0, one launch (start us, length us, event | category | flops | bytes accessed | tf_op | source)
XLA Modules:
  0.0 230.8 jit_solution(8769592003094775133)
XLA Ops:
  8.1 1.6 pad_maximum_fusion.1.pay_ref.own_ref
  10.4 4.0 %collective-permute-start = (s32[1,5]{1,0:T(1,128)S(1)}, s32[1,5]{1,0:T(1,128)S(1)}, u32[]{:S(2)}, u32[]{:S(2)}) collective-permute-start(s32[1,5]{1,0:T(1,128)S(1)} %get-tuple-element.27), channel_id=1, source_target_pairs={{0,8},{1,9},{2,10},{3,11},{4,12},{5,13},{6,14},{7,15},{8,0},{9,1},... | collective-permute-start | bytes 68 | tf_op jit(solution)/shard_map/ppermute | solution.py:166
  15.9 2.0 collective-permute-start.1
  17.9 1.7 collective-permute-done.1
  19.6 1.9 collective-permute-start.2
  21.6 1.6 collective-permute-done.2
  24.2 16.3 %own_tile.1 = (bf16[2048,2048]{1,0:T(8,128)(2,1)S(1)}, f32[8,2048]{1,0:T(8,128)S(1)}) custom-call(bf16[40,2048]{1,0:T(8,128)(2,1)S(1)} %copy-done.3), custom_call_target="tpu_custom_call" | custom-call | flops 125829120 | bytes 8388608 | tf_op jit(solution)/shard_map/own_tile/pallas_call | solution.py:223
  40.5 3.2 %copy-done = bf16[2048,2048]{1,0:T(8,128)(2,1)} copy-done((bf16[2048,2048]{1,0:T(8,128)(2,1)}, bf16[2048,2048]{1,0:T(8,128)(2,1)S(1)}, u32[]{:S(2)}) %copy-start) | copy-done | bytes 8388632
  46.3 10.0 %all-gather.4.cloned.1.call-done = bf16[640,2048]{1,0:T(8,128)(2,1)} async-done(((bf16[40,2048]{1,0:T(8,128)(2,1)}), bf16[640,2048]{1,0:T(8,128)(2,1)}) %all-gather.4.cloned.1.call-update) | async-done | bytes 2621456 | tf_op jit(solution)/shard_map/all_gather | solution.py:217
  56.3 1.7 copy-done.2
  59.0 83.3 %pair_tiles.1 = (bf16[5,2048,2048]{2,1,0:T(8,128)(2,1)}, f32[8,2048]{1,0:T(8,128)S(1)}) custom-call(s32[6]{0:T(128)S(1)} %pad_add_fusion.3.slots_ref, bf16[40,2048]{1,0:T(8,128)(2,1)S(1)} %copy-done.4, bf16[16,40,2048]{2,1,0:T(8,128)(2,1)S(1)} %bitcast.15, f32[8,2048]{1,0:T(8,128)S(1)} %get-tuple-element.6.first_ref), custom_call_target="tpu_custom_call" | custom-call | tf_op jit(solution)/shard_map/pair_tiles/pallas_call | solution.py:244
  142.4 1.5 collective-permute-start.4
  144.0 3.0 %collective-permute-done.4 = f32[2,8]{1,0:T(2,128)S(1)} collective-permute-done((f32[2,8]{1,0:T(2,128)S(1)}, f32[2,8]{1,0:T(2,128)S(1)}, u32[]{:S(2)}, u32[]{:S(2)}) %collective-permute-start.4) | collective-permute-done | bytes 96 | tf_op jit(solution)/shard_map/ppermute | solution.py:166
  147.0 3.6 %collective-permute-done.5 = f32[2,8]{1,0:T(2,128)S(1)} collective-permute-done((f32[2,8]{1,0:T(2,128)S(1)}, f32[2,8]{1,0:T(2,128)S(1)}, u32[]{:S(2)}, u32[]{:S(2)}) %collective-permute-start.5) | collective-permute-done | bytes 96 | tf_op jit(solution)/shard_map/ppermute | solution.py:166
  150.7 3.6 %collective-permute-done.6 = f32[2,8]{1,0:T(2,128)S(1)} collective-permute-done((f32[2,8]{1,0:T(2,128)S(1)}, f32[2,8]{1,0:T(2,128)S(1)}, u32[]{:S(2)}, u32[]{:S(2)}) %collective-permute-start.6) | collective-permute-done | bytes 96 | tf_op jit(solution)/shard_map/ppermute | solution.py:166
  155.6 18.9 %all-gather.1 = bf16[128,2048]{1,0:T(8,128)(2,1)S(1)} all-gather(bf16[8,2048]{1,0:T(8,128)(2,1)S(1)} %get-tuple-element.24.vec_ref), channel_id=3, replica_groups=mesh['group'=2,'row'=16] {'row'}, dimensions={0}, use_global_device_ids=true | all-gather | bytes 557056 | tf_op jit(solution)/shard_map/all_gather | solution.py:267
  174.5 3.4 %copy-done.1 = bf16[2048,2048]{1,0:T(8,128)(2,1)S(1)} copy-done((bf16[2048,2048]{1,0:T(8,128)(2,1)S(1)}, bf16[2048,2048]{1,0:T(8,128)(2,1)}, u32[]{:S(2)}) %copy-start.1) | copy-done | bytes 8388632
  177.9 1.6 own_again.1.first_ref
  179.5 22.4 %pair_again.1 = f32[8,2048]{1,0:T(8,128)S(1)} custom-call(s32[6]{0:T(128)S(1)} %pad_add_fusion.3.slots_ref, bf16[5,2048,2048]{2,1,0:T(8,128)(2,1)} %get-tuple-element.8.tile_ref, bf16[16,8,2048]{2,1,0:T(8,128)(2,1)S(1)} %bitcast.16, f32[8,2048]{1,0:T(8,128)S(1)} %own_again.1.first_ref), custom_call_target="tpu_custom_call" | custom-call | tf_op jit(solution)/shard_map/pair_again/pallas_call | solution.py:288
  202.0 3.5 %collective-permute-done.9 = f32[8]{0:T(128)S(1)} collective-permute-done((f32[8]{0:T(128)S(1)}, f32[8]{0:T(128)S(1)}, u32[]{:S(2)}, u32[]{:S(2)}) %collective-permute-start.9) | collective-permute-done | bytes 64 | tf_op jit(solution)/shard_map/ppermute | solution.py:166
  205.6 3.5 %collective-permute-done.10 = f32[8]{0:T(128)S(1)} collective-permute-done((f32[8]{0:T(128)S(1)}, f32[8]{0:T(128)S(1)}, u32[]{:S(2)}, u32[]{:S(2)}) %collective-permute-start.10) | collective-permute-done | bytes 64 | tf_op jit(solution)/shard_map/ppermute | solution.py:166
  210.4 3.0 %collective-permute-start.12 = (f32[8]{0:T(128)S(1)}, f32[8]{0:T(128)S(1)}, u32[]{:S(2)}, u32[]{:S(2)}) collective-permute-start(f32[8]{0:T(128)S(1)} %get-tuple-element.12), channel_id=1, source_target_pairs={{0,8},{1,9},{2,10},{3,11},{4,12},{5,13},{6,14},{7,15},{8,0},{9,1},... | collective-permute-start | bytes 104 | tf_op jit(solution)/shard_map/ppermute | solution.py:166
  215.0 3.5 %collective-permute-done.13 = f32[8]{0:T(128)S(1)} collective-permute-done((f32[8]{0:T(128)S(1)}, f32[8]{0:T(128)S(1)}, u32[]{:S(2)}, u32[]{:S(2)}) %collective-permute-start.13) | collective-permute-done | bytes 64 | tf_op jit(solution)/shard_map/ppermute | solution.py:166
  218.5 3.5 %collective-permute-done.14 = f32[8]{0:T(128)S(1)} collective-permute-done((f32[8]{0:T(128)S(1)}, f32[8]{0:T(128)S(1)}, u32[]{:S(2)}, u32[]{:S(2)}) %collective-permute-start.14) | collective-permute-done | bytes 64 | tf_op jit(solution)/shard_map/ppermute | solution.py:166
  (66 shorter events, 13.6 us)
Async XLA Ops:
  7.2 135.1 %copy-start.6 = (f32[8,2048]{1,0:T(8,128)S(1)}, f32[8,2048]{1,0:T(8,128)}, u32[]{:S(2)}) copy-start(f32[8,2048]{1,0:T(8,128)} %param.7) | copy-start | bytes 196612
  7.2 49.1 %all-gather.4.cloned.1.call-start = ((), (), s32[]{:S(2)}) async-start(), calls=%async_computation | async-start | bytes 2785280 | tf_op jit(solution)/shard_map/all_gather | solution.py:217
  10.4 5.6 %collective-permute-start = (s32[1,5]{1,0:T(1,128)S(1)}, s32[1,5]{1,0:T(1,128)S(1)}, u32[]{:S(2)}, u32[]{:S(2)}) collective-permute-start(s32[1,5]{1,0:T(1,128)S(1)} %get-tuple-element.27), channel_id=1, source_target_pairs={{0,8},{1,9},{2,10},{3,11},{4,12},{5,13},{6,14},{7,15},{8,0},{9,1},... | collective-permute-start | bytes 68 | tf_op jit(solution)/shard_map/ppermute | solution.py:166
  15.9 3.6 %collective-permute-start.1 = (s32[2,5]{1,0:T(2,128)S(1)}, s32[2,5]{1,0:T(2,128)S(1)}, u32[]{:S(2)}, u32[]{:S(2)}) collective-permute-start(s32[2,5]{1,0:T(2,128)S(1)} %pad_add_fusion.2), channel_id=1, source_target_pairs={{0,4},{1,5},{2,6},{3,7},{4,0},{5,1},{6,2},{7,3},{8,12},{9,13},{10,... | collective-permute-start | bytes 128 | tf_op jit(solution)/shard_map/ppermute | solution.py:166
  19.6 3.7 %collective-permute-start.2 = (s32[4,5]{1,0:T(4,128)S(1)}, s32[4,5]{1,0:T(4,128)S(1)}, u32[]{:S(2)}, u32[]{:S(2)}) collective-permute-start(s32[4,5]{1,0:T(4,128)S(1)} %pad_add_fusion.1), channel_id=1, source_target_pairs={{0,2},{1,3},{2,0},{3,1},{4,6},{5,7},{6,4},{7,5},{8,10},{9,11},{10,... | collective-permute-start | bytes 248 | tf_op jit(solution)/shard_map/ppermute | solution.py:166
  23.2 20.5 %collective-permute-start.3 = (s32[8,5]{1,0:T(8,128)S(1)}, s32[8,5]{1,0:T(8,128)S(1)}, u32[]{:S(2)}, u32[]{:S(2)}) collective-permute-start(s32[8,5]{1,0:T(8,128)S(1)} %pad_add_fusion), channel_id=1, source_target_pairs={{0,1},{1,0},{2,3},{3,2},{4,5},{5,4},{6,7},{7,6},{8,9},{9,8},{10,11... | collective-permute-start | bytes 488 | tf_op jit(solution)/shard_map/ppermute | solution.py:166
  23.3 0.9 copy-start.3
  40.5 3.2 %copy-start = (bf16[2048,2048]{1,0:T(8,128)(2,1)}, bf16[2048,2048]{1,0:T(8,128)(2,1)S(1)}, u32[]{:S(2)}) copy-start(bf16[2048,2048]{1,0:T(8,128)(2,1)S(1)} %get-tuple-element.9.tile_ref) | copy-start | bytes 25165828
  56.3 1.7 copy-start.2
  58.0 0.9 copy-start.4
  142.4 4.5 %collective-permute-start.4 = (f32[2,8]{1,0:T(2,128)S(1)}, f32[2,8]{1,0:T(2,128)S(1)}, u32[]{:S(2)}, u32[]{:S(2)}) collective-permute-start(f32[2,8]{1,0:T(2,128)S(1)} %pad_maximum_fusion.2), channel_id=1, source_target_pairs={{0,8},{1,9},{2,10},{3,11},{4,12},{5,13},{6,14},{7,15},{8,0},{9,1},... | collective-permute-start | bytes 200 | tf_op jit(solution)/shard_map/ppermute | solution.py:166
  147.0 3.6 %collective-permute-start.5 = (f32[2,8]{1,0:T(2,128)S(1)}, f32[2,8]{1,0:T(2,128)S(1)}, u32[]{:S(2)}, u32[]{:S(2)}) collective-permute-start(f32[2,8]{1,0:T(2,128)S(1)} %fusion.2), channel_id=1, source_target_pairs={{0,4},{1,5},{2,6},{3,7},{4,0},{5,1},{6,2},{7,3},{8,12},{9,13},{10,... | collective-permute-start | bytes 200 | tf_op jit(solution)/shard_map/ppermute | solution.py:166
  150.6 3.6 %collective-permute-start.6 = (f32[2,8]{1,0:T(2,128)S(1)}, f32[2,8]{1,0:T(2,128)S(1)}, u32[]{:S(2)}, u32[]{:S(2)}) collective-permute-start(f32[2,8]{1,0:T(2,128)S(1)} %fusion.4), channel_id=1, source_target_pairs={{0,2},{1,3},{2,0},{3,1},{4,6},{5,7},{6,4},{7,5},{8,10},{9,11},{10,... | collective-permute-start | bytes 200 | tf_op jit(solution)/shard_map/ppermute | solution.py:166
  154.2 1.1 collective-permute-start.7
  174.5 3.4 %copy-start.1 = (bf16[2048,2048]{1,0:T(8,128)(2,1)S(1)}, bf16[2048,2048]{1,0:T(8,128)(2,1)}, u32[]{:S(2)}) copy-start(bf16[2048,2048]{1,0:T(8,128)(2,1)} %copy-done) | copy-start | bytes 25165828
  179.4 22.5 %collective-permute-start.8 = (f32[8]{0:T(128)S(1)}, f32[8]{0:T(128)S(1)}, u32[]{:S(2)}, u32[]{:S(2)}) collective-permute-start(f32[8]{0:T(128)S(1)} %get-tuple-element.18), channel_id=1, source_target_pairs={{0,8},{1,9},{2,10},{3,11},{4,12},{5,13},{6,14},{7,15},{8,0},{9,1},... | collective-permute-start | bytes 104 | tf_op jit(solution)/shard_map/ppermute | solution.py:166
  179.5 33.9 %copy-start.5 = (s32[1,2048]{1,0:T(1,128)S(1)}, s32[1,2048]{1,0:T(1,128)}, u32[]{:S(2)}) copy-start(s32[1,2048]{1,0:T(1,128)} %perm_ref.1) | copy-start | bytes 24580
  202.0 3.6 %collective-permute-start.9 = (f32[8]{0:T(128)S(1)}, f32[8]{0:T(128)S(1)}, u32[]{:S(2)}, u32[]{:S(2)}) collective-permute-start(f32[8]{0:T(128)S(1)} %add.62), channel_id=1, source_target_pairs={{0,4},{1,5},{2,6},{3,7},{4,0},{5,1},{6,2},{7,3},{8,12},{9,13},{10,... | collective-permute-start | bytes 104 | tf_op jit(solution)/shard_map/ppermute | solution.py:166
  205.6 3.5 %collective-permute-start.10 = (f32[8]{0:T(128)S(1)}, f32[8]{0:T(128)S(1)}, u32[]{:S(2)}, u32[]{:S(2)}) collective-permute-start(f32[8]{0:T(128)S(1)} %add.63), channel_id=1, source_target_pairs={{0,2},{1,3},{2,0},{3,1},{4,6},{5,7},{6,4},{7,5},{8,10},{9,11},{10,... | collective-permute-start | bytes 104 | tf_op jit(solution)/shard_map/ppermute | solution.py:166
  209.1 1.1 collective-permute-start.11
  210.4 4.5 %collective-permute-start.12 = (f32[8]{0:T(128)S(1)}, f32[8]{0:T(128)S(1)}, u32[]{:S(2)}, u32[]{:S(2)}) collective-permute-start(f32[8]{0:T(128)S(1)} %get-tuple-element.12), channel_id=1, source_target_pairs={{0,8},{1,9},{2,10},{3,11},{4,12},{5,13},{6,14},{7,15},{8,0},{9,1},... | collective-permute-start | bytes 104 | tf_op jit(solution)/shard_map/ppermute | solution.py:166
  214.9 3.6 %collective-permute-start.13 = (f32[8]{0:T(128)S(1)}, f32[8]{0:T(128)S(1)}, u32[]{:S(2)}, u32[]{:S(2)}) collective-permute-start(f32[8]{0:T(128)S(1)} %add.69), channel_id=1, source_target_pairs={{0,4},{1,5},{2,6},{3,7},{4,0},{5,1},{6,2},{7,3},{8,12},{9,13},{10,... | collective-permute-start | bytes 104 | tf_op jit(solution)/shard_map/ppermute | solution.py:166
  218.5 3.5 %collective-permute-start.14 = (f32[8]{0:T(128)S(1)}, f32[8]{0:T(128)S(1)}, u32[]{:S(2)}, u32[]{:S(2)}) collective-permute-start(f32[8]{0:T(128)S(1)} %add.70), channel_id=1, source_target_pairs={{0,2},{1,3},{2,0},{3,1},{4,6},{5,7},{6,4},{7,5},{8,10},{9,11},{10,... | collective-permute-start | bytes 104 | tf_op jit(solution)/shard_map/ppermute | solution.py:166
  222.1 1.1 collective-permute-start.15
Sparse Core Ops, SparseCore 0:
  10.3 45.9 all-gather.3

commit v2 on v1

v2 whole, which is shorter than its diff:
```python
import jax
import jax.numpy as jnp
import numpy as np
from jax import lax
from jax.experimental import pallas as pl
from jax.experimental.pallas import tpu as pltpu
from jax.sharding import PartitionSpec as P

SHRINK = 0.95
SCALE = 20.0 * (20.0 / 19.0) ** 19
DIAGONAL = float(1.0 - SCALE * float(np.float32(1.0 / SCALE).astype(jnp.bfloat16)))
KDIM = 128
COLS = 512
ROWS = 512
TAIL = 128
BF16 = jnp.bfloat16
F32 = jnp.float32
CONTRACT_LANES = (((1,), (1,)), ((), ()))


def split_three(value):
    high = value.astype(BF16).astype(F32)
    rest = value - high
    middle = rest.astype(BF16).astype(F32)
    return high, middle, rest - middle


def norm_rows(norm, first):
    high, middle, low = split_three(norm)
    row = lax.broadcasted_iota(jnp.int32, (32, norm.shape[1]), 0)
    out = jnp.where(row < 6, 1.0, 0.0)
    out = jnp.where(row == first, high, out)
    out = jnp.where(row == first + 1, middle, out)
    return jnp.where(row == first + 2, low, out).astype(BF16)


def own_factor(feat):
    wide = feat.astype(F32)
    norm = jnp.sum(wide * wide, axis=0, keepdims=True) * (SHRINK * SHRINK)
    pieces = split_three(wide * (-2.0 * SHRINK * SHRINK))
    whole = jnp.concatenate([piece.astype(BF16) for piece in pieces] + [norm_rows(norm, 0)], axis=0)
    return jnp.transpose(whole)


def other_factor(feat):
    wide = feat.astype(F32)
    norm = jnp.sum(wide * wide, axis=0, keepdims=True) * (SHRINK * SHRINK)
    return jnp.concatenate([feat, feat, feat, norm_rows(norm, 3)], axis=0)


def psi_tile(dist):
    dist = jnp.maximum(dist, 1e-30)
    radius = dist * lax.rsqrt(dist)
    u = jnp.maximum(SHRINK - radius, 0.0)
    two = u * u
    four = two * two
    eight = four * four
    sixteen = eight * eight
    return (sixteen * two * (u - two)).astype(BF16)


def tile_columns(left_ref, right_ref, vec_ref, begin, tile_ref, sum_ref):
    at = pl.multiple_of(begin, COLS)
    right = right_ref[:, pl.ds(at, COLS)]
    vec = vec_ref[:, pl.ds(at, COLS)]

    def step(index, carry):
        rows = pl.multiple_of(index * ROWS, ROWS)
        dist = jnp.dot(left_ref[pl.ds(rows, ROWS), :], right, preferred_element_type=F32)
        parts = []
        for sub in range(0, ROWS, 64):
            part = psi_tile(dist[sub : sub + 64])
            tile_ref[pl.ds(rows + sub, 64), :] = part
            parts.append(part)
        sum_ref[pl.ds(rows, ROWS), :] += lax.dot_general(
            jnp.concatenate(parts, axis=0), vec, CONTRACT_LANES, preferred_element_type=F32
        )
        return carry

    lax.fori_loop(0, left_ref.shape[0] // ROWS, step, 0)


def own_kernel(pay_ref, tile_ref, sum_ref, left_ref, right_ref, vec_ref):
    step = pl.program_id(0)

    @pl.when(step == 0)
    def _():
        pay = pay_ref[...]
        left_ref[...] = own_factor(pay[:32])
        right_ref[...] = other_factor(pay[:32])
        vec_ref[...] = pay[32:40]
        sum_ref[...] = jnp.zeros_like(sum_ref)

    tile_columns(left_ref, right_ref, vec_ref, step * COLS, tile_ref, sum_ref)


def pair_kernel(
    slots_ref, own_ref, pay_ref, first_ref, rhs_ref, var_ref,
    tile_ref, image_ref, send_ref,
    left_ref, right_ref, vec_ref, sum_ref,
):
    slot, step = pl.program_id(0), pl.program_id(1)

    @pl.when((slot == 0) & (step == 0))
    def _():
        left_ref[...] = own_factor(own_ref[...][:32])
        sum_ref[...] = first_ref[...]

    @pl.when(slot < slots_ref[0])
    def _():
        @pl.when(step == 0)
        def _():
            pay = pay_ref[0]
            right_ref[...] = other_factor(pay[:32])
            vec_ref[...] = pay[32:40]

        tile_columns(left_ref, right_ref, vec_ref, step * COLS, tile_ref.at[0], sum_ref)

    @pl.when((slot == pl.num_programs(0) - 1) & (step == pl.num_programs(1) - 1))
    def _():
        rhs = rhs_ref[...]
        width = rhs.shape[1]
        image = (var_ref[...] + DIAGONAL) * rhs + SCALE * jnp.transpose(sum_ref[...])
        image_ref[...] = image
        send_ref[:, :width] = image.astype(BF16)
        pieces = split_three(jnp.sum(rhs * rhs, axis=1, keepdims=True))
        pieces += split_three(jnp.sum(rhs * image, axis=1, keepdims=True))
        lane = lax.broadcasted_iota(jnp.int32, (rhs.shape[0], TAIL), 1)
        tail = jnp.zeros((rhs.shape[0], TAIL), F32)
        for place, piece in enumerate(pieces):
            tail = jnp.where(lane == place, piece, tail)
        send_ref[:, width:] = tail.astype(BF16)


def own_again_kernel(tile_ref, vec_ref, sum_ref):
    width = tile_ref.shape[1]
    sum_ref[...] = lax.dot_general(
        tile_ref[...], vec_ref[:, :width], CONTRACT_LANES, preferred_element_type=F32
    )


def again_kernel(
    slots_ref, tile_ref, vec_ref, tails_ref, first_ref, rhs_ref, var_ref, image_ref,
    rows_ref, dots_ref, step_ref,
    sum_ref,
):
    slot, step = pl.program_id(0), pl.program_id(1)
    width = rhs_ref.shape[1]

    @pl.when((slot == 0) & (step == 0))
    def _():
        sum_ref[...] = first_ref[...]

    @pl.when(slot < slots_ref[0])
    def _():
        at = pl.multiple_of(step * ROWS, ROWS)
        sum_ref[pl.ds(at, ROWS), :] += lax.dot_general(
            tile_ref[0], vec_ref[0, :, :width], CONTRACT_LANES, preferred_element_type=F32
        )

    @pl.when((slot == pl.num_programs(0) - 1) & (step == pl.num_programs(1) - 1))
    def _():
        rhs = rhs_ref[...]
        image = image_ref[...]
        total = jnp.sum(tails_ref[...].astype(F32), axis=0)
        norm = total[:, 0:1] + total[:, 1:2] + total[:, 2:3]
        curve = total[:, 3:4] + total[:, 4:5] + total[:, 5:6]
        length = norm / curve
        second = (var_ref[...] + DIAGONAL) * image + SCALE * jnp.transpose(sum_ref[...])
        res = rhs - length * image
        res_image = image - length * second
        rows_ref[0:8] = rhs
        rows_ref[8:16] = res
        rows_ref[16:24] = image
        rows_ref[24:32] = res_image
        lane = lax.broadcasted_iota(jnp.int32, (rhs.shape[0], TAIL), 1)
        dots = jnp.zeros((rhs.shape[0], TAIL), F32)
        for place, product in enumerate((res * res, res * res_image, res * image, rhs * res_image)):
            dots = jnp.where(lane == place, jnp.sum(product, axis=1, keepdims=True), dots)
        dots_ref[...] = dots
        step_ref[...] = jnp.where(lane == 0, norm, jnp.where(lane == 1, curve, 0.0))


def order_kernel(rows_ref, perm_ref, out_ref):
    rows = rows_ref[...]
    count, width = rows.shape
    pieces = jnp.concatenate([piece for piece in split_three(rows)], axis=0).astype(BF16)
    perm = perm_ref[...]
    chunk = 256
    for col in range(0, width, chunk):
        total = jnp.zeros((3 * count, chunk), F32)
        for at in range(0, width, chunk):
            index = lax.broadcasted_iota(jnp.int32, (chunk, chunk), 0) + at
            pick = jnp.where(index == perm[:, col : col + chunk], 1.0, 0.0).astype(BF16)
            total += jnp.dot(pieces[:, at : at + chunk], pick, preferred_element_type=F32)
        out_ref[:, col : col + chunk] = total[:count] + total[count : 2 * count] + total[2 * count :]


def swap(value, mask, count):
    return lax.ppermute(value, "row", [(i, i ^ mask) for i in range(count)])


def levels(count, sizes):
    bits = count.bit_length() - 1
    out = []
    sizes = list(sizes)
    while bits:
        take = min(sizes.pop(0) if sizes else 1, bits)
        bits -= take
        out.append([mask << bits for mask in range(1, 1 << take)])
    return out


def tree_sum(value, count):
    for masks in levels(count, [2, 2, 2]):
        others = [swap(value, mask, count) for mask in masks]
        if len(masks) == 3:
            value = (value + others[0]) + (others[1] + others[2])
        else:
            value = value + others[0]
    return value


def tree_gather(value, count):
    blocks, places = value[None], [0]
    for masks in levels(count, [2] if count <= 16 else [2, 2]):
        blocks = jnp.concatenate([blocks] + [swap(blocks, mask, count) for mask in masks], axis=0)
        places = places + [place ^ mask for mask in masks for place in places]
    return blocks, places


def partners(tile_list, count):
    most = tile_list.shape[1]
    me = lax.axis_index("row")
    lists, places = tree_gather(tile_list[0, :, 1], count)
    number = me ^ jnp.asarray(places, jnp.int32)
    lower = jnp.any(lists == me, axis=1)
    upper = jnp.any(tile_list[0, :, 1][None, :] == number[:, None], axis=1)
    valid = lower | upper
    before = jnp.sum((valid[None, :] & (number[None, :] < number[:, None])).astype(jnp.int32), axis=1)
    total = jnp.sum(valid.astype(jnp.int32))
    place = jnp.minimum(jnp.arange(most), jnp.maximum(total - 1, 0))
    hit = valid[None, :] & (before[None, :] == place[:, None])
    picked = jnp.sum(jnp.where(hit, number[None, :], 0), axis=1)
    where = jnp.sum(jnp.where(hit, jnp.arange(count)[None, :], 0), axis=1)
    return jnp.concatenate([total[None], picked, where]).astype(jnp.int32)


def local(features, right_side, variance, hilbert_order, tile_list):
    width = features.shape[1]
    rhs_count = right_side.shape[0]
    count = lax.axis_size("row")
    most = tile_list.shape[1]
    steps = width // COLS
    row_steps = width // ROWS
    shape = jax.ShapeDtypeStruct
    params = pltpu.CompilerParams(vmem_limit_bytes=40 * 1024 * 1024)
    var_row = variance[None, :]

    payload = jnp.concatenate([features, right_side.astype(BF16)], axis=0)
    slots = partners(tile_list, count)
    every = lax.all_gather(payload, "row", axis=0)
    scratch = [
        pltpu.VMEM((width, KDIM), BF16),
        pltpu.VMEM((KDIM, width), BF16),
        pltpu.VMEM((rhs_count, width), BF16),
    ]
    sum_shape = (width, rhs_count)
    whole = lambda *ignored: (0, 0)
    own_tile, own_sum = pl.pallas_call(
        own_kernel,
        grid=(steps,),
        in_specs=[pl.BlockSpec(payload.shape, whole)],
        out_specs=[
            pl.BlockSpec((width, COLS), lambda i: (0, i)),
            pl.BlockSpec(sum_shape, whole),
        ],
        out_shape=[shape((width, width), BF16), shape(sum_shape, F32)],
        scratch_shapes=scratch,
        compiler_params=params,
        name="own_tile",
    )(payload)

    def tile_out(k, i, s):
        live = k < s[0]
        return (jnp.minimum(k, jnp.maximum(s[0] - 1, 0)), 0, jnp.where(live, i, steps - 1))

    def tile_in(k, i, s):
        live = k < s[0]
        return (jnp.minimum(k, jnp.maximum(s[0] - 1, 0)), jnp.where(live, i, row_steps - 1), 0)

    row_spec = pl.BlockSpec(right_side.shape, whole)
    var_spec = pl.BlockSpec(var_row.shape, whole)
    sum_spec = pl.BlockSpec(sum_shape, whole)
    send_shape = (rhs_count, width + TAIL)
    pair_tiles, image, send = pl.pallas_call(
        pair_kernel,
        grid_spec=pltpu.PrefetchScalarGridSpec(
            num_scalar_prefetch=1,
            grid=(most, steps),
            in_specs=[
                pl.BlockSpec(payload.shape, whole),
                pl.BlockSpec((1,) + payload.shape, lambda k, i, s: (s[1 + k], 0, 0)),
                sum_spec,
                row_spec,
                var_spec,
            ],
            out_specs=[
                pl.BlockSpec((1, width, COLS), tile_out),
                row_spec,
                pl.BlockSpec(send_shape, whole),
            ],
            scratch_shapes=scratch + [pltpu.VMEM(sum_shape, F32)],
        ),
        out_shape=[
            shape((most, width, width), BF16),
            shape(right_side.shape, F32),
            shape(send_shape, BF16),
        ],
        compiler_params=params,
        name="pair_tiles",
    )(slots, payload, every, own_sum, right_side, var_row)

    every_send, _ = tree_gather(send, count)
    own_again = pl.pallas_call(
        own_again_kernel,
        grid=(row_steps,),
        in_specs=[
            pl.BlockSpec((ROWS, width), lambda i: (i, 0)),
            pl.BlockSpec(send_shape, whole),
        ],
        out_specs=pl.BlockSpec((ROWS, rhs_count), lambda i: (i, 0)),
        out_shape=shape(sum_shape, F32),
        compiler_params=params,
        name="own_again",
    )(own_tile, send)
    dots_spec = pl.BlockSpec((rhs_count, TAIL), whole)
    rows, dots, steps_one = pl.pallas_call(
        again_kernel,
        grid_spec=pltpu.PrefetchScalarGridSpec(
            num_scalar_prefetch=1,
            grid=(most, row_steps),
            in_specs=[
                pl.BlockSpec((1, ROWS, width), tile_in),
                pl.BlockSpec((1,) + send_shape, lambda k, i, s: (s[1 + most + k], 0, 0)),
                pl.BlockSpec((count, rhs_count, TAIL), lambda k, i, s: (0, 0, width // TAIL)),
                sum_spec,
                row_spec,
                var_spec,
                row_spec,
            ],
            out_specs=[
                pl.BlockSpec((4 * rhs_count, width), whole),
                dots_spec,
                dots_spec,
            ],
            scratch_shapes=[pltpu.VMEM(sum_shape, F32)],
        ),
        out_shape=[
            shape((4 * rhs_count, width), F32),
            shape((rhs_count, TAIL), F32),
            shape((rhs_count, TAIL), F32),
        ],
        compiler_params=params,
        name="pair_again",
    )(slots, pair_tiles, every_send, every_send, own_again, right_side, var_row, image)

    dots = tree_sum(dots, count)
    ordered = pl.pallas_call(
        order_kernel,
        out_shape=shape(rows.shape, F32),
        compiler_params=params,
        name="curve_order",
    )(rows, hilbert_order)
    norm, curve = steps_one[:, 0:1], steps_one[:, 1:2]
    length = norm / curve
    norm_next = dots[:, 0:1]
    ratio = norm_next / norm
    curve_next = dots[:, 1:2] + ratio * (dots[:, 2:3] + dots[:, 3:4]) + ratio * ratio * curve
    length_next = norm_next / curve_next
    rhs_o, res_o, image_o, res_image_o = [ordered[at : at + 8] for at in range(0, 32, 8)]
    solved = length * rhs_o + length_next * (res_o + ratio * rhs_o)
    residual = res_o - length_next * (res_image_o + ratio * image_o)
    return (solved, residual)


def solution(mesh):
    in_specs = (
        P(None, ("group", "row")),
        P(None, ("group", "row")),
        P(("group", "row")),
        P(("group", "row"), None),
        P(("group", "row"), None, None),
    )
    out_specs = (P(None, ("group", "row")), P(None, ("group", "row")))
    return jax.shard_map(local, mesh=mesh, in_specs=in_specs, out_specs=out_specs, check_vma=False)
```

time: 232 us -> 189 us (0.81)
  Pallas kernels: 125 us -> 24.9 us
  starting transfers between devices: 12.9 us -> 98.4 us
  blocking collectives: 18.9 us -> 0 us
  waiting for transfers between devices: 41.2 us -> 30.8 us
    ppermute x16, starting transfers between devices: 12.8 us -> 98.4 us  [swap(): return lax.ppermute(value, 'row', [(i, i ^ mask) for i in range(count)])]
    pallas_call x1, Pallas kernels: 83.3 us -> 3.57 us  [local(): pl.pallas_call(pair_kernel, grid_spec=pltpu.PrefetchScalarGridSpec(num_sc...]
    all_gather x1 -> x0, blocking collectives: 18.9 us -> none  [local(): every_first = lax.all_gather(rounded, 'row', axis=0)]
    pallas_call x1, Pallas kernels: 22.4 us -> 3.74 us  [local(): pl.pallas_call(again_kernel, grid_spec=pltpu.PrefetchScalarGridSpec(num_s...]
    ppermute x16, waiting for transfers between devices: 31.1 us -> 18.2 us  [swap(): return lax.ppermute(value, 'row', [(i, i ^ mask) for i in range(count)])]
    pallas_call x1, Pallas kernels: 16.3 us -> 13.4 us  [local(): pl.pallas_call(own_kernel, grid=(steps,), in_specs=[pl.BlockSpec(payload....]
    all_gather x1, waiting for transfers between devices: 10 us -> 12.6 us  [local(): every = lax.all_gather(payload, 'row', axis=0)]
    unnamed x14 -> x24, local copies, waits for them, and re-layouts: 10.2 us -> 11.7 us
  transfers between devices with their start and end apart: 17 -> 17, of which waited for: 14 -> 11; matrix products, arithmetic and copies ran while one was open for 2% -> 2% of each run, Pallas kernels for 17% -> 9%
where the time goes in v2:
time: 189 us; the launch traced here: 188 us
  starting transfers between devices  98.4 us (52%)
  waiting for transfers between devices  30.8 us (16%)
  Pallas kernels  24.9 us (13%)
  between operations  14.9 us (8%)
  local copies, waits for them, and re-layouts  12.5 us (7%)
  other arithmetic  6.05 us (3%)
    ppermute x16, starting transfers between devices, swap(): return lax.ppermute(value, 'row', [(i, i ^ mask) for i in range(count)])  98.4 us
    ppermute x16, waiting for transfers between devices, swap(): return lax.ppermute(value, 'row', [(i, i ^ mask) for i in range(count)])  18.2 us
    pallas_call x1, Pallas kernels, local(): pl.pallas_call(own_kernel, grid=(steps,), in_specs=[pl.BlockSpec(payload....  13.4 us
    all_gather x1, waiting for transfers between devices, local(): every = lax.all_gather(payload, 'row', axis=0)  12.6 us
    unnamed x24, local copies, waits for them, and re-layouts  11.7 us
  transfers between devices with their start and end apart: 17, of which 11 were waited for; matrix products, arithmetic and copies ran while one was open for 2% of the time, Pallas kernels for 9%

profile of v2, /device:TPU:0, one launch (start us, length us, event | category | flops | bytes accessed | tf_op | source)
XLA Modules:
  0.0 187.5 jit_solution(6022540258756811903)
XLA Ops:
  8.1 1.6 pad_maximum_fusion.pay_ref.own_ref
  10.4 5.0 %collective-permute-start.2 = (s32[1,5]{1,0:T(1,128)S(1)}, s32[1,5]{1,0:T(1,128)S(1)}, u32[]{:S(2)}, u32[]{:S(2)}) collective-permute-start(s32[1,5]{1,0:T(1,128)S(1)} %get-tuple-element.38), channel_id=1, source_target_pairs={{0,12},{1,13},{2,14},{3,15},{4,8},{5,9},{6,10},{7,11},{8,4},{9,5},... | collective-permute-start | bytes 68 | tf_op jit(solution)/shard_map/ppermute | solution.py:200
  16.0 0.9 collective-permute-done.2
  16.9 2.9 %collective-permute-done.1 = s32[1,5]{1,0:T(1,128)S(1)} collective-permute-done((s32[1,5]{1,0:T(1,128)S(1)}, s32[1,5]{1,0:T(1,128)S(1)}, u32[]{:S(2)}, u32[]{:S(2)}) %collective-permute-start.1) | collective-permute-done | bytes 52 | tf_op jit(solution)/shard_map/ppermute | solution.py:200
  19.9 1.6 collective-permute-start.3
  22.1 1.4 collective-permute-done.3
  23.7 0.9 copy-done.2
  24.6 13.4 %own_tile.1 = (bf16[2048,2048]{1,0:T(8,128)(2,1)S(1)}, f32[2048,8]{1,0:T(8,128)S(1)}) custom-call(bf16[40,2048]{1,0:T(8,128)(2,1)S(1)} %copy-done.2), custom_call_target="tpu_custom_call" | custom-call | tf_op jit(solution)/shard_map/own_tile/pallas_call | solution.py:270
  38.0 3.2 %copy-done = bf16[2048,2048]{1,0:T(8,128)(2,1)} copy-done((bf16[2048,2048]{1,0:T(8,128)(2,1)}, bf16[2048,2048]{1,0:T(8,128)(2,1)S(1)}, u32[]{:S(2)}) %copy-start) | copy-done | bytes 8388632
  43.7 12.6 %all-gather.3.cloned.1.call-done = bf16[640,2048]{1,0:T(8,128)(2,1)} async-done(((bf16[40,2048]{1,0:T(8,128)(2,1)}), bf16[640,2048]{1,0:T(8,128)(2,1)}) %all-gather.3.cloned.1.call-update) | async-done | bytes 2621456 | tf_op jit(solution)/shard_map/all_gather | solution.py:262
  56.3 0.9 copy-done.3
  57.2 1.7 copy-done.4
  60.5 3.6 %pair_tiles.1 = (bf16[5,2048,2048]{2,1,0:T(8,128)(2,1)}, f32[8,2048]{1,0:T(8,128)S(1)}, bf16[8,2176]{1,0:T(8,128)(2,1)S(1)}) custom-call(s32[11]{0:T(128)S(1)} %pad_add_fusion.1.slots_ref, bf16[40,2048]{1,0:T(8,128)(2,1)S(1)} %copy-done.3, bf16[16,40,2048]{2,1,0:T(8,128)(2,1)S(1)} %bitcast.10, f32[2048,8]{1,0:T(8,128)S(1)} %get-tuple-element.10.first_ref, ...), custom_call_target="tpu_custom_call" | custom-call | tf_op jit(solution)/shard_map/pair_tiles/pallas_call | solution.py:296
  64.1 63.4 %collective-permute-start.7 = (bf16[1,8,2176]{2,1,0:T(8,128)(2,1)S(1)}, bf16[1,8,2176]{2,1,0:T(8,128)(2,1)S(1)}, u32[]{:S(2)}, u32[]{:S(2)}) collective-permute-start(bf16[1,8,2176]{2,1,0:T(8,128)(2,1)S(1)} %bitcast.11), channel_id=1, source_target_pairs={{0,12},{1,13},{2,14},{3,15},{4,8},{5,9},{6,10},{7,11},{8,4},{9,5},... | collective-permute-start | bytes 104456 | tf_op jit(solution)/shard_map/ppermute | solution.py:200
  128.2 1.1 collective-permute-done.7
  129.3 3.0 %collective-permute-done.6 = bf16[1,8,2176]{2,1,0:T(8,128)(2,1)S(1)} collective-permute-done((bf16[1,8,2176]{2,1,0:T(8,128)(2,1)S(1)}, bf16[1,8,2176]{2,1,0:T(8,128)(2,1)S(1)}, u32[]{:S(2)}, u32[]{:S(2)}) %collective-permute-start.6) | collective-permute-done | bytes 34848 | tf_op jit(solution)/shard_map/ppermute | solution.py:200
  132.8 4.9 %collective-permute-done.8 = bf16[4,8,2176]{2,1,0:T(8,128)(2,1)S(1)} collective-permute-done((bf16[4,8,2176]{2,1,0:T(8,128)(2,1)S(1)}, bf16[4,8,2176]{2,1,0:T(8,128)(2,1)S(1)}, u32[]{:S(2)}, u32[]{:S(2)}) %collective-permute-start.8) | collective-permute-done | bytes 139296 | tf_op jit(solution)/shard_map/ppermute | solution.py:200
  137.8 3.4 %copy-done.1 = bf16[2048,2048]{1,0:T(8,128)(2,1)S(1)} copy-done((bf16[2048,2048]{1,0:T(8,128)(2,1)S(1)}, bf16[2048,2048]{1,0:T(8,128)(2,1)}, u32[]{:S(2)}) %copy-start.1) | copy-done | bytes 8388632
  141.2 2.8 %own_again.1.first_ref = f32[2048,8]{1,0:T(8,128)S(1)} custom-call(bf16[2048,2048]{1,0:T(8,128)(2,1)S(1)} %copy-done.1, bf16[8,2176]{1,0:T(8,128)(2,1)S(1)} %get-tuple-element.12.vec_ref), custom_call_target="tpu_custom_call" | custom-call | tf_op jit(solution)/shard_map/own_again/pallas_call | solution.py:325
  144.0 3.7 %pair_again.1 = (f32[32,2048]{1,0:T(8,128)S(1)}, f32[8,128]{1,0:T(8,128)S(1)}, f32[8,128]{1,0:T(8,128)S(1)}) custom-call(s32[11]{0:T(128)S(1)} %pad_add_fusion.1.slots_ref, bf16[5,2048,2048]{2,1,0:T(8,128)(2,1)} %get-tuple-element.11.tile_ref, bf16[16,8,2176]{2,1,0:T(8,128)(2,1)S(1)} %constant_dynamic-update-slice_fusion.5.vec_ref.tails_ref, ...), custom_call_target="tpu_custom_call" | custom-call | tf_op jit(solution)/shard_map/pair_again/pallas_call | solution.py:338
  147.8 23.7 %collective-permute-start.12 = (f32[8,128]{1,0:T(8,128)S(1)}, f32[8,128]{1,0:T(8,128)S(1)}, u32[]{:S(2)}, u32[]{:S(2)}) collective-permute-start(f32[8,128]{1,0:T(8,128)S(1)} %get-tuple-element.17), channel_id=1, source_target_pairs={{0,12},{1,13},{2,14},{3,15},{4,8},{5,9},{6,10},{7,11},{8,4},{9,5},... | collective-permute-start | bytes 12296 | tf_op jit(solution)/shard_map/ppermute | solution.py:200
  173.0 2.9 %collective-permute-done.11 = f32[8,128]{1,0:T(8,128)S(1)} collective-permute-done((f32[8,128]{1,0:T(8,128)S(1)}, f32[8,128]{1,0:T(8,128)S(1)}, u32[]{:S(2)}, u32[]{:S(2)}) %collective-permute-start.11) | collective-permute-done | bytes 4128 | tf_op jit(solution)/shard_map/ppermute | solution.py:200
  176.0 1.1 collective-permute-start.14
  177.9 1.5 curve_order.1
  (61 shorter events, 11.5 us)
Async XLA Ops:
  7.2 136.8 %copy-start.6 = (f32[8,2048]{1,0:T(8,128)S(1)}, f32[8,2048]{1,0:T(8,128)}, u32[]{:S(2)}) copy-start(f32[8,2048]{1,0:T(8,128)} %rhs_ref.3) | copy-start | bytes 196612
  7.2 136.8 %copy-start.8 = (f32[2048]{0:T(1024)S(1)}, f32[2048]{0:T(1024)}, u32[]{:S(2)}) copy-start(f32[2048]{0:T(1024)} %param.8) | copy-start | bytes 24580
  7.2 49.1 %all-gather.3.cloned.1.call-start = ((), (), s32[]{:S(2)}) async-start(), calls=%async_computation | async-start | bytes 2785280 | tf_op jit(solution)/shard_map/all_gather | solution.py:262
  10.4 6.6 %collective-permute-start.2 = (s32[1,5]{1,0:T(1,128)S(1)}, s32[1,5]{1,0:T(1,128)S(1)}, u32[]{:S(2)}, u32[]{:S(2)}) collective-permute-start(s32[1,5]{1,0:T(1,128)S(1)} %get-tuple-element.38), channel_id=1, source_target_pairs={{0,12},{1,13},{2,14},{3,15},{4,8},{5,9},{6,10},{7,11},{8,4},{9,5},... | collective-permute-start | bytes 68 | tf_op jit(solution)/shard_map/ppermute | solution.py:200
  15.4 4.4 %collective-permute-start.1 = (s32[1,5]{1,0:T(1,128)S(1)}, s32[1,5]{1,0:T(1,128)S(1)}, u32[]{:S(2)}, u32[]{:S(2)}) collective-permute-start(s32[1,5]{1,0:T(1,128)S(1)} %get-tuple-element.38), channel_id=1, source_target_pairs={{0,8},{1,9},{2,10},{3,11},{4,12},{5,13},{6,14},{7,15},{8,0},{9,1},... | collective-permute-start | bytes 68 | tf_op jit(solution)/shard_map/ppermute | solution.py:200
  15.4 4.4 %collective-permute-start = (s32[1,5]{1,0:T(1,128)S(1)}, s32[1,5]{1,0:T(1,128)S(1)}, u32[]{:S(2)}, u32[]{:S(2)}) collective-permute-start(s32[1,5]{1,0:T(1,128)S(1)} %get-tuple-element.38), channel_id=1, source_target_pairs={{0,4},{1,5},{2,6},{3,7},{4,0},{5,1},{6,2},{7,3},{8,12},{9,13},{10,... | collective-permute-start | bytes 68 | tf_op jit(solution)/shard_map/ppermute | solution.py:200
  19.9 3.7 %collective-permute-start.3 = (s32[4,5]{1,0:T(4,128)S(1)}, s32[4,5]{1,0:T(4,128)S(1)}, u32[]{:S(2)}, u32[]{:S(2)}) collective-permute-start(s32[4,5]{1,0:T(4,128)S(1)} %pad_add_fusion), channel_id=1, source_target_pairs={{0,2},{1,3},{2,0},{3,1},{4,6},{5,7},{6,4},{7,5},{8,10},{9,11},{10,... | collective-permute-start | bytes 248 | tf_op jit(solution)/shard_map/ppermute | solution.py:200
  23.6 17.7 %collective-permute-start.4 = (s32[8,5]{1,0:T(8,128)S(1)}, s32[8,5]{1,0:T(8,128)S(1)}, u32[]{:S(2)}, u32[]{:S(2)}) collective-permute-start(s32[8,5]{1,0:T(8,128)S(1)} %concatenate.29), channel_id=1, source_target_pairs={{0,1},{1,0},{2,3},{3,2},{4,5},{5,4},{6,7},{7,6},{8,9},{9,8},{10,11... | collective-permute-start | bytes 488 | tf_op jit(solution)/shard_map/ppermute | solution.py:200
  23.7 0.9 copy-start.2
  38.0 3.2 %copy-start = (bf16[2048,2048]{1,0:T(8,128)(2,1)}, bf16[2048,2048]{1,0:T(8,128)(2,1)S(1)}, u32[]{:S(2)}) copy-start(bf16[2048,2048]{1,0:T(8,128)(2,1)S(1)} %get-tuple-element.13.tile_ref) | copy-start | bytes 25165828
  57.2 1.7 copy-start.4
  64.1 65.3 %collective-permute-start.7 = (bf16[1,8,2176]{2,1,0:T(8,128)(2,1)S(1)}, bf16[1,8,2176]{2,1,0:T(8,128)(2,1)S(1)}, u32[]{:S(2)}, u32[]{:S(2)}) collective-permute-start(bf16[1,8,2176]{2,1,0:T(8,128)(2,1)S(1)} %bitcast.11), channel_id=1, source_target_pairs={{0,12},{1,13},{2,14},{3,15},{4,8},{5,9},{6,10},{7,11},{8,4},{9,5},... | collective-permute-start | bytes 104456 | tf_op jit(solution)/shard_map/ppermute | solution.py:200
  127.4 4.9 %collective-permute-start.6 = (bf16[1,8,2176]{2,1,0:T(8,128)(2,1)S(1)}, bf16[1,8,2176]{2,1,0:T(8,128)(2,1)S(1)}, u32[]{:S(2)}, u32[]{:S(2)}) collective-permute-start(bf16[1,8,2176]{2,1,0:T(8,128)(2,1)S(1)} %bitcast.12), channel_id=1, source_target_pairs={{0,8},{1,9},{2,10},{3,11},{4,12},{5,13},{6,14},{7,15},{8,0},{9,1},... | collective-permute-start | bytes 104456 | tf_op jit(solution)/shard_map/ppermute | solution.py:200
  128.2 4.3 %collective-permute-start.5 = (bf16[1,8,2176]{2,1,0:T(8,128)(2,1)S(1)}, bf16[1,8,2176]{2,1,0:T(8,128)(2,1)S(1)}, u32[]{:S(2)}, u32[]{:S(2)}) collective-permute-start(bf16[1,8,2176]{2,1,0:T(8,128)(2,1)S(1)} %bitcast.13), channel_id=1, source_target_pairs={{0,4},{1,5},{2,6},{3,7},{4,0},{5,1},{6,2},{7,3},{8,12},{9,13},{10,... | collective-permute-start | bytes 104456 | tf_op jit(solution)/shard_map/ppermute | solution.py:200
  132.6 5.1 %collective-permute-start.8 = (bf16[4,8,2176]{2,1,0:T(8,128)(2,1)S(1)}, bf16[4,8,2176]{2,1,0:T(8,128)(2,1)S(1)}, u32[]{:S(2)}, u32[]{:S(2)}) collective-permute-start(bf16[4,8,2176]{2,1,0:T(8,128)(2,1)S(1)} %pad_maximum_fusion.1), channel_id=1, source_target_pairs={{0,2},{1,3},{2,0},{3,1},{4,6},{5,7},{6,4},{7,5},{8,10},{9,11},{10,... | collective-permute-start | bytes 417800 | tf_op jit(solution)/shard_map/ppermute | solution.py:200
  137.7 6.2 %collective-permute-start.9 = (bf16[8,8,2176]{2,1,0:T(8,128)(2,1)S(1)}, bf16[8,8,2176]{2,1,0:T(8,128)(2,1)S(1)}, u32[]{:S(2)}, u32[]{:S(2)}) collective-permute-start(bf16[8,8,2176]{2,1,0:T(8,128)(2,1)S(1)} %get-tuple-element.27), channel_id=1, source_target_pairs={{0,1},{1,0},{2,3},{3,2},{4,5},{5,4},{6,7},{7,6},{8,9},{9,8},{10,11... | collective-permute-start | bytes 835592 | tf_op jit(solution)/shard_map/ppermute | solution.py:200
  137.8 3.4 %copy-start.1 = (bf16[2048,2048]{1,0:T(8,128)(2,1)S(1)}, bf16[2048,2048]{1,0:T(8,128)(2,1)}, u32[]{:S(2)}) copy-start(bf16[2048,2048]{1,0:T(8,128)(2,1)} %copy-done) | copy-start | bytes 25165828
  144.0 33.9 %copy-start.9 = (s32[1,2048]{1,0:T(1,128)S(1)}, s32[1,2048]{1,0:T(1,128)}, u32[]{:S(2)}) copy-start(s32[1,2048]{1,0:T(1,128)} %perm_ref.1) | copy-start | bytes 24580
  147.8 25.3 %collective-permute-start.12 = (f32[8,128]{1,0:T(8,128)S(1)}, f32[8,128]{1,0:T(8,128)S(1)}, u32[]{:S(2)}, u32[]{:S(2)}) collective-permute-start(f32[8,128]{1,0:T(8,128)S(1)} %get-tuple-element.17), channel_id=1, source_target_pairs={{0,12},{1,13},{2,14},{3,15},{4,8},{5,9},{6,10},{7,11},{8,4},{9,5},... | collective-permute-start | bytes 12296 | tf_op jit(solution)/shard_map/ppermute | solution.py:200
  171.4 4.5 %collective-permute-start.11 = (f32[8,128]{1,0:T(8,128)S(1)}, f32[8,128]{1,0:T(8,128)S(1)}, u32[]{:S(2)}, u32[]{:S(2)}) collective-permute-start(f32[8,128]{1,0:T(8,128)S(1)} %get-tuple-element.17), channel_id=1, source_target_pairs={{0,8},{1,9},{2,10},{3,11},{4,12},{5,13},{6,14},{7,15},{8,0},{9,1},... | collective-permute-start | bytes 12296 | tf_op jit(solution)/shard_map/ppermute | solution.py:200
  172.0 3.9 %collective-permute-start.10 = (f32[8,128]{1,0:T(8,128)S(1)}, f32[8,128]{1,0:T(8,128)S(1)}, u32[]{:S(2)}, u32[]{:S(2)}) collective-permute-start(f32[8,128]{1,0:T(8,128)S(1)} %get-tuple-element.17), channel_id=1, source_target_pairs={{0,4},{1,5},{2,6},{3,7},{4,0},{5,1},{6,2},{7,3},{8,12},{9,13},{10,... | collective-permute-start | bytes 12296 | tf_op jit(solution)/shard_map/ppermute | solution.py:200
  175.9 3.4 %collective-permute-start.15 = (f32[8,128]{1,0:T(8,128)S(1)}, f32[8,128]{1,0:T(8,128)S(1)}, u32[]{:S(2)}, u32[]{:S(2)}) collective-permute-start(f32[8,128]{1,0:T(8,128)S(1)} %add_add_fusion.1), channel_id=1, source_target_pairs={{0,3},{1,2},{2,1},{3,0},{4,7},{5,6},{6,5},{7,4},{8,11},{9,10},{10,... | collective-permute-start | bytes 12296 | tf_op jit(solution)/shard_map/ppermute | solution.py:200
  176.0 3.7 %collective-permute-start.14 = (f32[8,128]{1,0:T(8,128)S(1)}, f32[8,128]{1,0:T(8,128)S(1)}, u32[]{:S(2)}, u32[]{:S(2)}) collective-permute-start(f32[8,128]{1,0:T(8,128)S(1)} %add_add_fusion.1), channel_id=1, source_target_pairs={{0,2},{1,3},{2,0},{3,1},{4,6},{5,7},{6,4},{7,5},{8,10},{9,11},{10,... | collective-permute-start | bytes 12296 | tf_op jit(solution)/shard_map/ppermute | solution.py:200
  177.1 2.6 %collective-permute-start.13 = (f32[8,128]{1,0:T(8,128)S(1)}, f32[8,128]{1,0:T(8,128)S(1)}, u32[]{:S(2)}, u32[]{:S(2)}) collective-permute-start(f32[8,128]{1,0:T(8,128)S(1)} %add_add_fusion.1), channel_id=1, source_target_pairs={{0,1},{1,0},{2,3},{3,2},{4,5},{5,4},{6,7},{7,6},{8,9},{9,8},{10,11... | collective-permute-start | bytes 12296 | tf_op jit(solution)/shard_map/ppermute | solution.py:200
  (3 other events, 2.5 us)
Sparse Core Ops, SparseCore 0:
  10.3 45.9 all-gather.2

commit v3 on v2

--- a/solution.py
+++ b/solution.py
@@ -10,12 +10,12 @@
 SCALE = 20.0 * (20.0 / 19.0) ** 19
 DIAGONAL = float(1.0 - SCALE * float(np.float32(1.0 / SCALE).astype(jnp.bfloat16)))
 KDIM = 128
-COLS = 512
 ROWS = 512
+UNIT = 256
+SUB = 64
 TAIL = 128
 BF16 = jnp.bfloat16
 F32 = jnp.float32
-CONTRACT_LANES = (((1,), (1,)), ((), ()))
 
 
 def split_three(value):
@@ -38,14 +38,13 @@
     wide = feat.astype(F32)
     norm = jnp.sum(wide * wide, axis=0, keepdims=True) * (SHRINK * SHRINK)
     pieces = split_three(wide * (-2.0 * SHRINK * SHRINK))
-    whole = jnp.concatenate([piece.astype(BF16) for piece in pieces] + [norm_rows(norm, 0)], axis=0)
-    return jnp.transpose(whole)
+    return jnp.concatenate([piece.astype(BF16) for piece in pieces] + [norm_rows(norm, 0)], axis=0)
 
 
 def other_factor(feat):
     wide = feat.astype(F32)
     norm = jnp.sum(wide * wide, axis=0, keepdims=True) * (SHRINK * SHRINK)
-    return jnp.concatenate([feat, feat, feat, norm_rows(norm, 3)], axis=0)
+    return jnp.transpose(jnp.concatenate([feat, feat, feat, norm_rows(norm, 3)], axis=0))
 
 
 def psi_tile(dist):
@@ -59,51 +58,73 @@
     return (sixteen * two * (u - two)).astype(BF16)
 
 
-def tile_columns(left_ref, right_ref, vec_ref, begin, tile_ref, sum_ref):
-    at = pl.multiple_of(begin, COLS)
-    right = right_ref[:, pl.ds(at, COLS)]
-    vec = vec_ref[:, pl.ds(at, COLS)]
+def tile_rows(left_ref, right_ref, vec_ref, begin, tile_ref, sum_ref, dist_refs):
+    width = right_ref.shape[1]
+    units = width // UNIT
+
+    def gram(row, unit, dist_ref):
+        col = unit * UNIT
+        dist_ref[...] = jnp.dot(
+            left_ref[pl.ds(pl.multiple_of(row, UNIT), UNIT), :],
+            right_ref[:, col : col + UNIT],
+            preferred_element_type=F32,
+        )
+
+    def product(vec, at, unit):
+        col = unit * UNIT
+        sum_ref[:, col : col + UNIT] += jnp.dot(
+            vec, tile_ref[pl.ds(at, UNIT), col : col + UNIT], preferred_element_type=F32
+        )
+
+    gram(begin, 0, dist_refs[0])
 
     def step(index, carry):
-        rows = pl.multiple_of(index * ROWS, ROWS)
-        dist = jnp.dot(left_ref[pl.ds(rows, ROWS), :], right, preferred_element_type=F32)
-        parts = []
-        for sub in range(0, ROWS, 64):
-            part = psi_tile(dist[sub : sub + 64])
-            tile_ref[pl.ds(rows + sub, 64), :] = part
-            parts.append(part)
-        sum_ref[pl.ds(rows, ROWS), :] += lax.dot_general(
-            jnp.concatenate(parts, axis=0), vec, CONTRACT_LANES, preferred_element_type=F32
-        )
+        at = pl.multiple_of(index * UNIT, UNIT)
+        row = begin + at
+        following = begin + jnp.minimum(at + UNIT, ROWS - UNIT)
+        vec = vec_ref[:, pl.ds(pl.multiple_of(row, UNIT), UNIT)]
+        for unit in range(units):
+            if unit + 1 < units:
+                gram(row, unit + 1, dist_refs[(unit + 1) % 2])
+            else:
+                gram(following, 0, dist_refs[(unit + 1) % 2])
+            col = unit * UNIT
+            for sub in range(0, UNIT, SUB):
+                tile_ref[pl.ds(at + sub, SUB), col : col + UNIT] = psi_tile(
+                    dist_refs[unit % 2][sub : sub + SUB, :]
+                )
+            if unit:
+                product(vec, at, unit - 1)
+        product(vec, at, units - 1)
         return carry
 
-    lax.fori_loop(0, left_ref.shape[0] // ROWS, step, 0)
-
-
-def own_kernel(pay_ref, tile_ref, sum_ref, left_ref, right_ref, vec_ref):
+    lax.fori_loop(0, ROWS // UNIT, step, 0)
+
+
+def own_kernel(pay_ref, tile_ref, sum_ref, left_ref, right_ref, vec_ref, *dist_refs):
     step = pl.program_id(0)
 
     @pl.when(step == 0)
     def _():
         pay = pay_ref[...]
-        left_ref[...] = own_factor(pay[:32])
-        right_ref[...] = other_factor(pay[:32])
+        left_ref[...] = other_factor(pay[:32])
+        right_ref[...] = own_factor(pay[:32])
         vec_ref[...] = pay[32:40]
         sum_ref[...] = jnp.zeros_like(sum_ref)
 
-    tile_columns(left_ref, right_ref, vec_ref, step * COLS, tile_ref, sum_ref)
+    tile_rows(left_ref, right_ref, vec_ref, step * ROWS, tile_ref, sum_ref, dist_refs)
 
 
 def pair_kernel(
     slots_ref, own_ref, pay_ref, first_ref, rhs_ref, var_ref,
     tile_ref, image_ref, send_ref,
-    left_ref, right_ref, vec_ref, sum_ref,
+    left_ref, right_ref, vec_ref, dist_zero_ref, dist_one_ref, sum_ref,
 ):
     slot, step = pl.program_id(0), pl.program_id(1)
 
     @pl.when((slot == 0) & (step == 0))
     def _():
-        left_ref[...] = own_factor(own_ref[...][:32])
+        right_ref[...] = own_factor(own_ref[...][:32])
         sum_ref[...] = first_ref[...]
 
     @pl.when(slot < slots_ref[0])
@@ -111,16 +132,19 @@
         @pl.when(step == 0)
         def _():
             pay = pay_ref[0]
-            right_ref[...] = other_factor(pay[:32])
+            left_ref[...] = other_factor(pay[:32])
             vec_ref[...] = pay[32:40]
 
-        tile_columns(left_ref, right_ref, vec_ref, step * COLS, tile_ref.at[0], sum_ref)
+        tile_rows(
+            left_ref, right_ref, vec_ref, step * ROWS, tile_ref.at[0], sum_ref,
+            (dist_zero_ref, dist_one_ref),
+        )
 
     @pl.when((slot == pl.num_programs(0) - 1) & (step == pl.num_programs(1) - 1))
     def _():
         rhs = rhs_ref[...]
         width = rhs.shape[1]
-        image = (var_ref[...] + DIAGONAL) * rhs + SCALE * jnp.transpose(sum_ref[...])
+        image = (var_ref[...] + DIAGONAL) * rhs + SCALE * sum_ref[...]
         image_ref[...] = image
         send_ref[:, :width] = image.astype(BF16)
         pieces = split_three(jnp.sum(rhs * rhs, axis=1, keepdims=True))
@@ -133,9 +157,15 @@
 
 
 def own_again_kernel(tile_ref, vec_ref, sum_ref):
-    width = tile_ref.shape[1]
-    sum_ref[...] = lax.dot_general(
-        tile_ref[...], vec_ref[:, :width], CONTRACT_LANES, preferred_element_type=F32
+    step = pl.program_id(0)
+
+    @pl.when(step == 0)
+    def _():
+        sum_ref[...] = jnp.zeros_like(sum_ref)
+
+    at = pl.multiple_of(step * ROWS, ROWS)
+    sum_ref[...] += jnp.dot(
+        vec_ref[:, pl.ds(at, ROWS)], tile_ref[...], preferred_element_type=F32
     )
 
 
@@ -145,7 +175,6 @@
     sum_ref,
 ):
     slot, step = pl.program_id(0), pl.program_id(1)
-    width = rhs_ref.shape[1]
 
     @pl.when((slot == 0) & (step == 0))
     def _():
@@ -154,8 +183,8 @@
     @pl.when(slot < slots_ref[0])
     def _():
         at = pl.multiple_of(step * ROWS, ROWS)
-        sum_ref[pl.ds(at, ROWS), :] += lax.dot_general(
-            tile_ref[0], vec_ref[0, :, :width], CONTRACT_LANES, preferred_element_type=F32
+        sum_ref[...] += jnp.dot(
+            vec_ref[0, :, pl.ds(at, ROWS)], tile_ref[0], preferred_element_type=F32
         )
 
     @pl.when((slot == pl.num_programs(0) - 1) & (step == pl.num_programs(1) - 1))
@@ -166,7 +195,7 @@
         norm = total[:, 0:1] + total[:, 1:2] + total[:, 2:3]
         curve = total[:, 3:4] + total[:, 4:5] + total[:, 5:6]
         length = norm / curve
-        second = (var_ref[...] + DIAGONAL) * image + SCALE * jnp.transpose(sum_ref[...])
+        second = (var_ref[...] + DIAGONAL) * image + SCALE * sum_ref[...]
         res = rhs - length * image
         res_image = image - length * second
         rows_ref[0:8] = rhs
@@ -251,10 +280,9 @@
     rhs_count = right_side.shape[0]
     count = lax.axis_size("row")
     most = tile_list.shape[1]
-    steps = width // COLS
-    row_steps = width // ROWS
+    steps = width // ROWS
     shape = jax.ShapeDtypeStruct
-    params = pltpu.CompilerParams(vmem_limit_bytes=40 * 1024 * 1024)
+    params = pltpu.CompilerParams(vmem_limit_bytes=24 * 1024 * 1024)
     var_row = variance[None, :]
 
     payload = jnp.concatenate([features, right_side.astype(BF16)], axis=0)
@@ -264,34 +292,27 @@
         pltpu.VMEM((width, KDIM), BF16),
         pltpu.VMEM((KDIM, width), BF16),
         pltpu.VMEM((rhs_count, width), BF16),
+        pltpu.VMEM((UNIT, UNIT), F32),
+        pltpu.VMEM((UNIT, UNIT), F32),
     ]
-    sum_shape = (width, rhs_count)
     whole = lambda *ignored: (0, 0)
+    row_spec = pl.BlockSpec(right_side.shape, whole)
+    var_spec = pl.BlockSpec(var_row.shape, whole)
     own_tile, own_sum = pl.pallas_call(
         own_kernel,
         grid=(steps,),
         in_specs=[pl.BlockSpec(payload.shape, whole)],
-        out_specs=[
-            pl.BlockSpec((width, COLS), lambda i: (0, i)),
-            pl.BlockSpec(sum_shape, whole),
-        ],
-        out_shape=[shape((width, width), BF16), shape(sum_shape, F32)],
+        out_specs=[pl.BlockSpec((ROWS, width), lambda i: (i, 0)), row_spec],
+        out_shape=[shape((width, width), BF16), shape(right_side.shape, F32)],
         scratch_shapes=scratch,
         compiler_params=params,
         name="own_tile",
     )(payload)
 
-    def tile_out(k, i, s):
+    def tile_at(k, i, s):
         live = k < s[0]
-        return (jnp.minimum(k, jnp.maximum(s[0] - 1, 0)), 0, jnp.where(live, i, steps - 1))
-
-    def tile_in(k, i, s):
-        live = k < s[0]
-        return (jnp.minimum(k, jnp.maximum(s[0] - 1, 0)), jnp.where(live, i, row_steps - 1), 0)
-
-    row_spec = pl.BlockSpec(right_side.shape, whole)
-    var_spec = pl.BlockSpec(var_row.shape, whole)
-    sum_spec = pl.BlockSpec(sum_shape, whole)
+        return (jnp.minimum(k, jnp.maximum(s[0] - 1, 0)), jnp.where(live, i, steps - 1), 0)
+
     send_shape = (rhs_count, width + TAIL)
     pair_tiles, image, send = pl.pallas_call(
         pair_kernel,
@@ -301,16 +322,16 @@
             in_specs=[
                 pl.BlockSpec(payload.shape, whole),
                 pl.BlockSpec((1,) + payload.shape, lambda k, i, s: (s[1 + k], 0, 0)),
-                sum_spec,
+                row_spec,
                 row_spec,
                 var_spec,
             ],
             out_specs=[
-                pl.BlockSpec((1, width, COLS), tile_out),
+                pl.BlockSpec((1, ROWS, width), tile_at),
                 row_spec,
                 pl.BlockSpec(send_shape, whole),
             ],
-            scratch_shapes=scratch + [pltpu.VMEM(sum_shape, F32)],
+            scratch_shapes=scratch + [pltpu.VMEM(right_side.shape, F32)],
         ),
         out_shape=[
             shape((most, width, width), BF16),
@@ -324,13 +345,13 @@
     every_send, _ = tree_gather(send, count)
     own_again = pl.pallas_call(
         own_again_kernel,
-        grid=(row_steps,),
+        grid=(steps,),
         in_specs=[
             pl.BlockSpec((ROWS, width), lambda i: (i, 0)),
             pl.BlockSpec(send_shape, whole),
         ],
-        out_specs=pl.BlockSpec((ROWS, rhs_count), lambda i: (i, 0)),
-        out_shape=shape(sum_shape, F32),
+        out_specs=row_spec,
+        out_shape=shape(right_side.shape, F32),
         compiler_params=params,
         name="own_again",
     )(own_tile, send)
@@ -339,12 +360,12 @@
         again_kernel,
         grid_spec=pltpu.PrefetchScalarGridSpec(
             num_scalar_prefetch=1,
-            grid=(most, row_steps),
+            grid=(most, steps),
             in_specs=[
-                pl.BlockSpec((1, ROWS, width), tile_in),
+                pl.BlockSpec((1, ROWS, width), tile_at),
                 pl.BlockSpec((1,) + send_shape, lambda k, i, s: (s[1 + most + k], 0, 0)),
                 pl.BlockSpec((count, rhs_count, TAIL), lambda k, i, s: (0, 0, width // TAIL)),
-                sum_spec,
+                row_spec,
                 row_spec,
                 var_spec,
                 row_spec,
@@ -354,7 +375,7 @@
                 dots_spec,
                 dots_spec,
             ],
-            scratch_shapes=[pltpu.VMEM(sum_shape, F32)],
+            scratch_shapes=[pltpu.VMEM(right_side.shape, F32)],
         ),
         out_shape=[
             shape((4 * rhs_count, width), F32),

time: 189 us -> 190 us (level)
  Pallas kernels: 24.9 us -> 57.6 us
  starting transfers between devices: 98.4 us -> 68.1 us
    ppermute x16, starting transfers between devices: 98.4 us -> 68.1 us  [swap(): return lax.ppermute(value, 'row', [(i, i ^ mask) for i in range(count)])]
    pallas_call x1, Pallas kernels: 3.57 us -> 30.3 us  [local(): pl.pallas_call(pair_kernel, grid_spec=pltpu.PrefetchScalarGridSpec(num_sc...]
    pallas_call x1, Pallas kernels: 3.74 us -> 10.6 us  [local(): pl.pallas_call(again_kernel, grid_spec=pltpu.PrefetchScalarGridSpec(num_s...]
  transfers between devices with their start and end apart: 17 -> 17, of which waited for: 11 -> 10; matrix products, arithmetic and copies ran while one was open for 2% -> 2% of each run, Pallas kernels for 9% -> 9%
where the time goes in v3:
time: 190 us; the launch traced here: 189 us
  starting transfers between devices  68.1 us (36%)
  Pallas kernels  57.6 us (30%)
  waiting for transfers between devices  29.4 us (15%)
  between operations  14.8 us (8%)
  local copies, waits for them, and re-layouts  12.5 us (7%)
  other arithmetic  6.05 us (3%)
    ppermute x16, starting transfers between devices, swap(): return lax.ppermute(value, 'row', [(i, i ^ mask) for i in range(count)])  68.1 us
    pallas_call x1, Pallas kernels, local(): pl.pallas_call(pair_kernel, grid_spec=pltpu.PrefetchScalarGridSpec(num_sc...  30.3 us
    ppermute x16, waiting for transfers between devices, swap(): return lax.ppermute(value, 'row', [(i, i ^ mask) for i in range(count)])  17.2 us
    pallas_call x1, Pallas kernels, local(): pl.pallas_call(own_kernel, grid=(steps,), in_specs=[pl.BlockSpec(payload....  13.7 us
    all_gather x1, waiting for transfers between devices, local(): every = lax.all_gather(payload, 'row', axis=0)  12.2 us
    unnamed x24, local copies, waits for them, and re-layouts  11.7 us
    pallas_call x1, Pallas kernels, local(): pl.pallas_call(again_kernel, grid_spec=pltpu.PrefetchScalarGridSpec(num_s...  10.6 us
  transfers between devices with their start and end apart: 17, of which 10 were waited for; matrix products, arithmetic and copies ran while one was open for 2% of the time, Pallas kernels for 9%

profile of v3, /device:TPU:0, one launch (start us, length us, event | category | flops | bytes accessed | tf_op | source)
XLA Modules:
  0.0 188.6 jit_solution(6506827172577651473)
XLA Ops:
  8.1 1.6 pad_maximum_fusion.pay_ref.own_ref
  10.4 5.0 %collective-permute-start.2 = (s32[1,5]{1,0:T(1,128)S(1)}, s32[1,5]{1,0:T(1,128)S(1)}, u32[]{:S(2)}, u32[]{:S(2)}) collective-permute-start(s32[1,5]{1,0:T(1,128)S(1)} %get-tuple-element.38), channel_id=1, source_target_pairs={{0,12},{1,13},{2,14},{3,15},{4,8},{5,9},{6,10},{7,11},{8,4},{9,5},... | collective-permute-start | bytes 68 | tf_op jit(solution)/shard_map/ppermute | solution.py:229
  16.9 2.9 %collective-permute-done.1 = s32[1,5]{1,0:T(1,128)S(1)} collective-permute-done((s32[1,5]{1,0:T(1,128)S(1)}, s32[1,5]{1,0:T(1,128)S(1)}, u32[]{:S(2)}, u32[]{:S(2)}) %collective-permute-start.1) | collective-permute-done | bytes 52 | tf_op jit(solution)/shard_map/ppermute | solution.py:229
  19.9 1.6 collective-permute-start.3
  22.1 1.4 collective-permute-done.3
  24.6 13.7 %own_tile.1 = (bf16[2048,2048]{1,0:T(8,128)(2,1)S(1)}, f32[8,2048]{1,0:T(8,128)S(1)}) custom-call(bf16[40,2048]{1,0:T(8,128)(2,1)S(1)} %copy-done.2), custom_call_target="tpu_custom_call" | custom-call | tf_op jit(solution)/shard_map/own_tile/pallas_call | solution.py:301
  38.3 3.2 %copy-done = bf16[2048,2048]{1,0:T(8,128)(2,1)} copy-done((bf16[2048,2048]{1,0:T(8,128)(2,1)}, bf16[2048,2048]{1,0:T(8,128)(2,1)S(1)}, u32[]{:S(2)}) %copy-start) | copy-done | bytes 8388632
  44.1 12.2 %all-gather.3.cloned.1.call-done = bf16[640,2048]{1,0:T(8,128)(2,1)} async-done(((bf16[40,2048]{1,0:T(8,128)(2,1)}), bf16[640,2048]{1,0:T(8,128)(2,1)}) %all-gather.3.cloned.1.call-update) | async-done | bytes 2621456 | tf_op jit(solution)/shard_map/all_gather | solution.py:290
  57.2 1.7 copy-done.4
  60.4 30.3 %pair_tiles.1 = (bf16[5,2048,2048]{2,1,0:T(8,128)(2,1)}, f32[8,2048]{1,0:T(8,128)S(1)}, bf16[8,2176]{1,0:T(8,128)(2,1)S(1)}) custom-call(s32[11]{0:T(128)S(1)} %pad_add_fusion.1.slots_ref, bf16[40,2048]{1,0:T(8,128)(2,1)S(1)} %copy-done.3, bf16[16,40,2048]{2,1,0:T(8,128)(2,1)S(1)} %bitcast.10, f32[8,2048]{1,0:T(8,128)S(1)} %get-tuple-element.10.first_ref, ...), custom_call_target="tpu_custom_call" | custom-call | tf_op jit(solution)/shard_map/pair_tiles/pallas_call | solution.py:317
  90.8 30.0 %collective-permute-start.6 = (bf16[1,8,2176]{2,1,0:T(8,128)(2,1)S(1)}, bf16[1,8,2176]{2,1,0:T(8,128)(2,1)S(1)}, u32[]{:S(2)}, u32[]{:S(2)}) collective-permute-start(bf16[1,8,2176]{2,1,0:T(8,128)(2,1)S(1)} %bitcast.12), channel_id=1, source_target_pairs={{0,8},{1,9},{2,10},{3,11},{4,12},{5,13},{6,14},{7,15},{8,0},{9,1},... | collective-permute-start | bytes 104456 | tf_op jit(solution)/shard_map/ppermute | solution.py:229
  120.7 2.3 %collective-permute-done.6 = bf16[1,8,2176]{2,1,0:T(8,128)(2,1)S(1)} collective-permute-done((bf16[1,8,2176]{2,1,0:T(8,128)(2,1)S(1)}, bf16[1,8,2176]{2,1,0:T(8,128)(2,1)S(1)}, u32[]{:S(2)}, u32[]{:S(2)}) %collective-permute-start.6) | collective-permute-done | bytes 34848 | tf_op jit(solution)/shard_map/ppermute | solution.py:229
  123.0 1.7 collective-permute-done.5
  124.7 14.3 %collective-permute-start.8 = (bf16[4,8,2176]{2,1,0:T(8,128)(2,1)S(1)}, bf16[4,8,2176]{2,1,0:T(8,128)(2,1)S(1)}, u32[]{:S(2)}, u32[]{:S(2)}) collective-permute-start(bf16[4,8,2176]{2,1,0:T(8,128)(2,1)S(1)} %pad_maximum_fusion.1), channel_id=1, source_target_pairs={{0,2},{1,3},{2,0},{3,1},{4,6},{5,7},{6,4},{7,5},{8,10},{9,11},{10,... | collective-permute-start | bytes 417800 | tf_op jit(solution)/shard_map/ppermute | solution.py:229
  139.0 4.0 %collective-permute-done.8 = bf16[4,8,2176]{2,1,0:T(8,128)(2,1)S(1)} collective-permute-done((bf16[4,8,2176]{2,1,0:T(8,128)(2,1)S(1)}, bf16[4,8,2176]{2,1,0:T(8,128)(2,1)S(1)}, u32[]{:S(2)}, u32[]{:S(2)}) %collective-permute-start.8) | collective-permute-done | bytes 139296 | tf_op jit(solution)/shard_map/ppermute | solution.py:229
  143.1 3.4 %copy-done.1 = bf16[2048,2048]{1,0:T(8,128)(2,1)S(1)} copy-done((bf16[2048,2048]{1,0:T(8,128)(2,1)S(1)}, bf16[2048,2048]{1,0:T(8,128)(2,1)}, u32[]{:S(2)}) %copy-start.1) | copy-done | bytes 8388632
  146.4 1.6 own_again.1.first_ref
  148.1 10.6 %pair_again.1 = (f32[32,2048]{1,0:T(8,128)S(1)}, f32[8,128]{1,0:T(8,128)S(1)}, f32[8,128]{1,0:T(8,128)S(1)}) custom-call(s32[11]{0:T(128)S(1)} %pad_add_fusion.1.slots_ref, bf16[5,2048,2048]{2,1,0:T(8,128)(2,1)} %get-tuple-element.11.tile_ref, bf16[16,8,2176]{2,1,0:T(8,128)(2,1)S(1)} %constant_dynamic-update-slice_fusion.5.vec_ref.tails_ref, ...), custom_call_target="tpu_custom_call" | custom-call | tf_op jit(solution)/shard_map/pair_again/pallas_call | solution.py:359
  158.7 10.8 %collective-permute-start.11 = (f32[8,128]{1,0:T(8,128)S(1)}, f32[8,128]{1,0:T(8,128)S(1)}, u32[]{:S(2)}, u32[]{:S(2)}) collective-permute-start(f32[8,128]{1,0:T(8,128)S(1)} %get-tuple-element.17), channel_id=1, source_target_pairs={{0,8},{1,9},{2,10},{3,11},{4,12},{5,13},{6,14},{7,15},{8,0},{9,1},... | collective-permute-start | bytes 12296 | tf_op jit(solution)/shard_map/ppermute | solution.py:229
  169.5 1.6 collective-permute-done.11
  171.1 2.0 %collective-permute-done.10 = f32[8,128]{1,0:T(8,128)S(1)} collective-permute-done((f32[8,128]{1,0:T(8,128)S(1)}, f32[8,128]{1,0:T(8,128)S(1)}, u32[]{:S(2)}, u32[]{:S(2)}) %collective-permute-start.10) | collective-permute-done | bytes 4128 | tf_op jit(solution)/shard_map/ppermute | solution.py:229
  173.1 4.0 %collective-permute-start.15 = (f32[8,128]{1,0:T(8,128)S(1)}, f32[8,128]{1,0:T(8,128)S(1)}, u32[]{:S(2)}, u32[]{:S(2)}) collective-permute-start(f32[8,128]{1,0:T(8,128)S(1)} %add_add_fusion.1), channel_id=1, source_target_pairs={{0,3},{1,2},{2,1},{3,0},{4,7},{5,6},{6,5},{7,4},{8,11},{9,10},{10,... | collective-permute-start | bytes 12296 | tf_op jit(solution)/shard_map/ppermute | solution.py:229
  177.1 1.6 collective-permute-start.14
  178.8 1.5 curve_order.1
  (61 shorter events, 11.0 us)
Async XLA Ops:
  7.2 140.9 %copy-start.6 = (f32[8,2048]{1,0:T(8,128)S(1)}, f32[8,2048]{1,0:T(8,128)}, u32[]{:S(2)}) copy-start(f32[8,2048]{1,0:T(8,128)} %rhs_ref.3) | copy-start | bytes 196612
  7.2 140.9 %copy-start.8 = (f32[2048]{0:T(1024)S(1)}, f32[2048]{0:T(1024)}, u32[]{:S(2)}) copy-start(f32[2048]{0:T(1024)} %param.8) | copy-start | bytes 24580
  7.2 49.0 %all-gather.3.cloned.1.call-start = ((), (), s32[]{:S(2)}) async-start(), calls=%async_computation | async-start | bytes 2785280 | tf_op jit(solution)/shard_map/all_gather | solution.py:290
  10.4 6.6 %collective-permute-start.2 = (s32[1,5]{1,0:T(1,128)S(1)}, s32[1,5]{1,0:T(1,128)S(1)}, u32[]{:S(2)}, u32[]{:S(2)}) collective-permute-start(s32[1,5]{1,0:T(1,128)S(1)} %get-tuple-element.38), channel_id=1, source_target_pairs={{0,12},{1,13},{2,14},{3,15},{4,8},{5,9},{6,10},{7,11},{8,4},{9,5},... | collective-permute-start | bytes 68 | tf_op jit(solution)/shard_map/ppermute | solution.py:229
  15.4 4.4 %collective-permute-start.1 = (s32[1,5]{1,0:T(1,128)S(1)}, s32[1,5]{1,0:T(1,128)S(1)}, u32[]{:S(2)}, u32[]{:S(2)}) collective-permute-start(s32[1,5]{1,0:T(1,128)S(1)} %get-tuple-element.38), channel_id=1, source_target_pairs={{0,8},{1,9},{2,10},{3,11},{4,12},{5,13},{6,14},{7,15},{8,0},{9,1},... | collective-permute-start | bytes 68 | tf_op jit(solution)/shard_map/ppermute | solution.py:229
  15.4 4.4 %collective-permute-start = (s32[1,5]{1,0:T(1,128)S(1)}, s32[1,5]{1,0:T(1,128)S(1)}, u32[]{:S(2)}, u32[]{:S(2)}) collective-permute-start(s32[1,5]{1,0:T(1,128)S(1)} %get-tuple-element.38), channel_id=1, source_target_pairs={{0,4},{1,5},{2,6},{3,7},{4,0},{5,1},{6,2},{7,3},{8,12},{9,13},{10,... | collective-permute-start | bytes 68 | tf_op jit(solution)/shard_map/ppermute | solution.py:229
  19.9 3.7 %collective-permute-start.3 = (s32[4,5]{1,0:T(4,128)S(1)}, s32[4,5]{1,0:T(4,128)S(1)}, u32[]{:S(2)}, u32[]{:S(2)}) collective-permute-start(s32[4,5]{1,0:T(4,128)S(1)} %pad_add_fusion), channel_id=1, source_target_pairs={{0,2},{1,3},{2,0},{3,1},{4,6},{5,7},{6,4},{7,5},{8,10},{9,11},{10,... | collective-permute-start | bytes 248 | tf_op jit(solution)/shard_map/ppermute | solution.py:229
  23.6 18.0 %collective-permute-start.4 = (s32[8,5]{1,0:T(8,128)S(1)}, s32[8,5]{1,0:T(8,128)S(1)}, u32[]{:S(2)}, u32[]{:S(2)}) collective-permute-start(s32[8,5]{1,0:T(8,128)S(1)} %concatenate.29), channel_id=1, source_target_pairs={{0,1},{1,0},{2,3},{3,2},{4,5},{5,4},{6,7},{7,6},{8,9},{9,8},{10,11... | collective-permute-start | bytes 488 | tf_op jit(solution)/shard_map/ppermute | solution.py:229
  23.7 0.9 copy-start.2
  38.3 3.2 %copy-start = (bf16[2048,2048]{1,0:T(8,128)(2,1)}, bf16[2048,2048]{1,0:T(8,128)(2,1)S(1)}, u32[]{:S(2)}) copy-start(bf16[2048,2048]{1,0:T(8,128)(2,1)S(1)} %get-tuple-element.13.tile_ref) | copy-start | bytes 25165828
  57.2 1.7 copy-start.4
  90.8 30.0 %collective-permute-start.7 = (bf16[1,8,2176]{2,1,0:T(8,128)(2,1)S(1)}, bf16[1,8,2176]{2,1,0:T(8,128)(2,1)S(1)}, u32[]{:S(2)}, u32[]{:S(2)}) collective-permute-start(bf16[1,8,2176]{2,1,0:T(8,128)(2,1)S(1)} %bitcast.11), channel_id=1, source_target_pairs={{0,12},{1,13},{2,14},{3,15},{4,8},{5,9},{6,10},{7,11},{8,4},{9,5},... | collective-permute-start | bytes 104456 | tf_op jit(solution)/shard_map/ppermute | solution.py:229
  90.8 32.2 %collective-permute-start.6 = (bf16[1,8,2176]{2,1,0:T(8,128)(2,1)S(1)}, bf16[1,8,2176]{2,1,0:T(8,128)(2,1)S(1)}, u32[]{:S(2)}, u32[]{:S(2)}) collective-permute-start(bf16[1,8,2176]{2,1,0:T(8,128)(2,1)S(1)} %bitcast.12), channel_id=1, source_target_pairs={{0,8},{1,9},{2,10},{3,11},{4,12},{5,13},{6,14},{7,15},{8,0},{9,1},... | collective-permute-start | bytes 104456 | tf_op jit(solution)/shard_map/ppermute | solution.py:229
  120.7 3.9 %collective-permute-start.5 = (bf16[1,8,2176]{2,1,0:T(8,128)(2,1)S(1)}, bf16[1,8,2176]{2,1,0:T(8,128)(2,1)S(1)}, u32[]{:S(2)}, u32[]{:S(2)}) collective-permute-start(bf16[1,8,2176]{2,1,0:T(8,128)(2,1)S(1)} %bitcast.13), channel_id=1, source_target_pairs={{0,4},{1,5},{2,6},{3,7},{4,0},{5,1},{6,2},{7,3},{8,12},{9,13},{10,... | collective-permute-start | bytes 104456 | tf_op jit(solution)/shard_map/ppermute | solution.py:229
  124.7 18.3 %collective-permute-start.8 = (bf16[4,8,2176]{2,1,0:T(8,128)(2,1)S(1)}, bf16[4,8,2176]{2,1,0:T(8,128)(2,1)S(1)}, u32[]{:S(2)}, u32[]{:S(2)}) collective-permute-start(bf16[4,8,2176]{2,1,0:T(8,128)(2,1)S(1)} %pad_maximum_fusion.1), channel_id=1, source_target_pairs={{0,2},{1,3},{2,0},{3,1},{4,6},{5,7},{6,4},{7,5},{8,10},{9,11},{10,... | collective-permute-start | bytes 417800 | tf_op jit(solution)/shard_map/ppermute | solution.py:229
  143.0 5.0 %collective-permute-start.9 = (bf16[8,8,2176]{2,1,0:T(8,128)(2,1)S(1)}, bf16[8,8,2176]{2,1,0:T(8,128)(2,1)S(1)}, u32[]{:S(2)}, u32[]{:S(2)}) collective-permute-start(bf16[8,8,2176]{2,1,0:T(8,128)(2,1)S(1)} %get-tuple-element.27), channel_id=1, source_target_pairs={{0,1},{1,0},{2,3},{3,2},{4,5},{5,4},{6,7},{7,6},{8,9},{9,8},{10,11... | collective-permute-start | bytes 835592 | tf_op jit(solution)/shard_map/ppermute | solution.py:229
  143.1 3.4 %copy-start.1 = (bf16[2048,2048]{1,0:T(8,128)(2,1)S(1)}, bf16[2048,2048]{1,0:T(8,128)(2,1)}, u32[]{:S(2)}) copy-start(bf16[2048,2048]{1,0:T(8,128)(2,1)} %copy-done) | copy-start | bytes 25165828
  148.1 30.7 %copy-start.9 = (s32[1,2048]{1,0:T(1,128)S(1)}, s32[1,2048]{1,0:T(1,128)}, u32[]{:S(2)}) copy-start(s32[1,2048]{1,0:T(1,128)} %perm_ref.1) | copy-start | bytes 24580
  158.6 10.8 %collective-permute-start.12 = (f32[8,128]{1,0:T(8,128)S(1)}, f32[8,128]{1,0:T(8,128)S(1)}, u32[]{:S(2)}, u32[]{:S(2)}) collective-permute-start(f32[8,128]{1,0:T(8,128)S(1)} %get-tuple-element.17), channel_id=1, source_target_pairs={{0,12},{1,13},{2,14},{3,15},{4,8},{5,9},{6,10},{7,11},{8,4},{9,5},... | collective-permute-start | bytes 12296 | tf_op jit(solution)/shard_map/ppermute | solution.py:229
  158.7 12.4 %collective-permute-start.11 = (f32[8,128]{1,0:T(8,128)S(1)}, f32[8,128]{1,0:T(8,128)S(1)}, u32[]{:S(2)}, u32[]{:S(2)}) collective-permute-start(f32[8,128]{1,0:T(8,128)S(1)} %get-tuple-element.17), channel_id=1, source_target_pairs={{0,8},{1,9},{2,10},{3,11},{4,12},{5,13},{6,14},{7,15},{8,0},{9,1},... | collective-permute-start | bytes 12296 | tf_op jit(solution)/shard_map/ppermute | solution.py:229
  169.5 3.6 %collective-permute-start.10 = (f32[8,128]{1,0:T(8,128)S(1)}, f32[8,128]{1,0:T(8,128)S(1)}, u32[]{:S(2)}, u32[]{:S(2)}) collective-permute-start(f32[8,128]{1,0:T(8,128)S(1)} %get-tuple-element.17), channel_id=1, source_target_pairs={{0,4},{1,5},{2,6},{3,7},{4,0},{5,1},{6,2},{7,3},{8,12},{9,13},{10,... | collective-permute-start | bytes 12296 | tf_op jit(solution)/shard_map/ppermute | solution.py:229
  173.1 7.2 %collective-permute-start.15 = (f32[8,128]{1,0:T(8,128)S(1)}, f32[8,128]{1,0:T(8,128)S(1)}, u32[]{:S(2)}, u32[]{:S(2)}) collective-permute-start(f32[8,128]{1,0:T(8,128)S(1)} %add_add_fusion.1), channel_id=1, source_target_pairs={{0,3},{1,2},{2,1},{3,0},{4,7},{5,6},{6,5},{7,4},{8,11},{9,10},{10,... | collective-permute-start | bytes 12296 | tf_op jit(solution)/shard_map/ppermute | solution.py:229
  177.1 3.6 %collective-permute-start.14 = (f32[8,128]{1,0:T(8,128)S(1)}, f32[8,128]{1,0:T(8,128)S(1)}, u32[]{:S(2)}, u32[]{:S(2)}) collective-permute-start(f32[8,128]{1,0:T(8,128)S(1)} %add_add_fusion.1), channel_id=1, source_target_pairs={{0,2},{1,3},{2,0},{3,1},{4,6},{5,7},{6,4},{7,5},{8,10},{9,11},{10,... | collective-permute-start | bytes 12296 | tf_op jit(solution)/shard_map/ppermute | solution.py:229
  178.7 2.0 %collective-permute-start.13 = (f32[8,128]{1,0:T(8,128)S(1)}, f32[8,128]{1,0:T(8,128)S(1)}, u32[]{:S(2)}, u32[]{:S(2)}) collective-permute-start(f32[8,128]{1,0:T(8,128)S(1)} %add_add_fusion.1), channel_id=1, source_target_pairs={{0,1},{1,0},{2,3},{3,2},{4,5},{5,4},{6,7},{7,6},{8,9},{9,8},{10,11... | collective-permute-start | bytes 12296 | tf_op jit(solution)/shard_map/ppermute | solution.py:229
  (3 other events, 2.5 us)
Sparse Core Ops, SparseCore 0:
  10.3 45.8 all-gather.2

commit v4 on v3

--- a/solution.py
+++ b/solution.py
@@ -7,12 +7,15 @@
 from jax.sharding import PartitionSpec as P
 
 SHRINK = 0.95
+GRAM = SHRINK * SHRINK / 4.0
 SCALE = 20.0 * (20.0 / 19.0) ** 19
 DIAGONAL = float(1.0 - SCALE * float(np.float32(1.0 / SCALE).astype(jnp.bfloat16)))
 KDIM = 128
 ROWS = 512
 UNIT = 256
 SUB = 64
+FRONT = 3
+HELD = 4
 TAIL = 128
 BF16 = jnp.bfloat16
 F32 = jnp.float32
@@ -36,21 +39,22 @@
 
 def own_factor(feat):
     wide = feat.astype(F32)
-    norm = jnp.sum(wide * wide, axis=0, keepdims=True) * (SHRINK * SHRINK)
-    pieces = split_three(wide * (-2.0 * SHRINK * SHRINK))
+    norm = jnp.sum(wide * wide, axis=0, keepdims=True) * GRAM
+    pieces = split_three(wide * (-2.0 * GRAM))
     return jnp.concatenate([piece.astype(BF16) for piece in pieces] + [norm_rows(norm, 0)], axis=0)
 
 
 def other_factor(feat):
     wide = feat.astype(F32)
-    norm = jnp.sum(wide * wide, axis=0, keepdims=True) * (SHRINK * SHRINK)
+    norm = jnp.sum(wide * wide, axis=0, keepdims=True) * GRAM
     return jnp.transpose(jnp.concatenate([feat, feat, feat, norm_rows(norm, 3)], axis=0))
 
 
-def psi_tile(dist):
-    dist = jnp.maximum(dist, 1e-30)
-    radius = dist * lax.rsqrt(dist)
-    u = jnp.maximum(SHRINK - radius, 0.0)
+def psi_tile(quarter):
+    quarter = jnp.maximum(quarter, 1e-30)
+    start = lax.rsqrt(quarter.astype(BF16)).astype(F32)
+    w = quarter * start
+    u = jnp.maximum(SHRINK + w * (w * start - 3.0), 0.0)
     two = u * u
     four = two * two
     eight = four * four
@@ -101,44 +105,73 @@
     lax.fori_loop(0, ROWS // UNIT, step, 0)
 
 
+def unpack(pay):
+    half = pay.shape[1]
+    return jnp.concatenate([pay[:32], pay[32:64]], axis=1), jnp.concatenate([pay[64:72], pay[72:80]], axis=1)
+
+
 def own_kernel(pay_ref, tile_ref, sum_ref, left_ref, right_ref, vec_ref, *dist_refs):
     step = pl.program_id(0)
 
     @pl.when(step == 0)
     def _():
-        pay = pay_ref[...]
-        left_ref[...] = other_factor(pay[:32])
-        right_ref[...] = own_factor(pay[:32])
-        vec_ref[...] = pay[32:40]
+        feat, vec = unpack(pay_ref[...])
+        left_ref[...] = other_factor(feat)
+        right_ref[...] = own_factor(feat)
+        vec_ref[...] = vec
         sum_ref[...] = jnp.zeros_like(sum_ref)
 
     tile_rows(left_ref, right_ref, vec_ref, step * ROWS, tile_ref, sum_ref, dist_refs)
 
 
-def pair_kernel(
-    slots_ref, own_ref, pay_ref, first_ref, rhs_ref, var_ref,
-    tile_ref, image_ref, send_ref,
-    left_ref, right_ref, vec_ref, dist_zero_ref, dist_one_ref, sum_ref,
-):
+def pair_kernel(slots_ref, own_ref, first_ref, rhs_ref, var_ref, *refs):
+    block_refs = refs[:-11]
+    front_ref, back_ref, image_ref, send_ref = refs[-11:-7]
+    left_ref, right_ref, vec_ref, dist_zero_ref, dist_one_ref, pay_ref, sem_ref = refs[-7:]
     slot, step = pl.program_id(0), pl.program_id(1)
+    sum_ref = image_ref
+
+    def fetch(which):
+        place = slots_ref[1 + which]
+        for at, block_ref in enumerate(block_refs):
+            @pl.when(place == at)
+            def _():
+                pltpu.make_async_copy(
+                    block_ref, pay_ref.at[which % 2], sem_ref.at[which % 2]
+                ).start()
 
     @pl.when((slot == 0) & (step == 0))
     def _():
-        right_ref[...] = own_factor(own_ref[...][:32])
+        right_ref[...] = own_factor(unpack(own_ref[...])[0])
         sum_ref[...] = first_ref[...]
+
+        @pl.when(slots_ref[0] > 0)
+        def _():
+            fetch(0)
 
     @pl.when(slot < slots_ref[0])
     def _():
         @pl.when(step == 0)
         def _():
-            pay = pay_ref[0]
-            left_ref[...] = other_factor(pay[:32])
-            vec_ref[...] = pay[32:40]
-
-        tile_rows(
-            left_ref, right_ref, vec_ref, step * ROWS, tile_ref.at[0], sum_ref,
-            (dist_zero_ref, dist_one_ref),
-        )
+            pltpu.make_async_copy(
+                block_refs[0], pay_ref.at[slot % 2], sem_ref.at[slot % 2]
+            ).wait()
+
+            @pl.when(slot + 1 < slots_ref[0])
+            def _():
+                fetch(slot + 1)
+
+            feat, vec = unpack(pay_ref[slot % 2])
+            left_ref[...] = other_factor(feat)
+            vec_ref[...] = vec
+
+        for tile_ref, here in ((front_ref, slot < FRONT), (back_ref, slot >= FRONT)):
+            @pl.when(here)
+            def _():
+                tile_rows(
+                    left_ref, right_ref, vec_ref, step * ROWS, tile_ref.at[0], sum_ref,
+                    (dist_zero_ref, dist_one_ref),
+                )
 
     @pl.when((slot == pl.num_programs(0) - 1) & (step == pl.num_programs(1) - 1))
     def _():
@@ -170,22 +203,51 @@
 
 
 def again_kernel(
-    slots_ref, tile_ref, vec_ref, tails_ref, first_ref, rhs_ref, var_ref, image_ref,
+    slots_ref, front_ref, back_ref, vec_ref, tails_ref, first_ref, rhs_ref, var_ref, image_ref,
     rows_ref, dots_ref, step_ref,
-    sum_ref,
+    sum_ref, held_ref, sem_ref,
 ):
     slot, step = pl.program_id(0), pl.program_id(1)
+    width = rhs_ref.shape[1]
+
+    steps = width // ROWS
+    parts = (slots_ref[0] - FRONT) * steps
+
+    def fetch(part):
+        at = pl.ds(pl.multiple_of((part % steps) * ROWS, ROWS), ROWS)
+        return pltpu.make_async_copy(
+            back_ref.at[part // steps, at], held_ref.at[part % HELD], sem_ref.at[part % HELD]
+        )
 
     @pl.when((slot == 0) & (step == 0))
     def _():
         sum_ref[...] = first_ref[...]
+        for part in range(HELD):
+            @pl.when(part < parts)
+            def _():
+                fetch(part).start()
 
     @pl.when(slot < slots_ref[0])
     def _():
         at = pl.multiple_of(step * ROWS, ROWS)
-        sum_ref[...] += jnp.dot(
-            vec_ref[0, :, pl.ds(at, ROWS)], tile_ref[0], preferred_element_type=F32
-        )
+
+        @pl.when(slot < FRONT)
+        def _():
+            sum_ref[...] += jnp.dot(
+                vec_ref[0, :, pl.ds(at, ROWS)], front_ref[0], preferred_element_type=F32
+            )
+
+        @pl.when(slot >= FRONT)
+        def _():
+            part = (slot - FRONT) * steps + step
+            fetch(part).wait()
+            sum_ref[...] += jnp.dot(
+                vec_ref[0, :, pl.ds(at, ROWS)], held_ref[part % HELD], preferred_element_type=F32
+            )
+
+            @pl.when(part + HELD < parts)
+            def _():
+                fetch(part + HELD).start()
 
     @pl.when((slot == pl.num_programs(0) - 1) & (step == pl.num_programs(1) - 1))
     def _():
@@ -250,29 +312,46 @@
     return value
 
 
+def gather_levels(count):
+    return levels(count, [2] if count <= 16 else [2, 2])
+
+
+def gather_places(count):
+    places = [0]
+    for masks in gather_levels(count):
+        places = places + [place ^ mask for mask in masks for place in places]
+    return places
+
+
 def tree_gather(value, count):
-    blocks, places = value[None], [0]
-    for masks in levels(count, [2] if count <= 16 else [2, 2]):
+    blocks = value[None]
+    for masks in gather_levels(count):
         blocks = jnp.concatenate([blocks] + [swap(blocks, mask, count) for mask in masks], axis=0)
-        places = places + [place ^ mask for mask in masks for place in places]
-    return blocks, places
+    return blocks
+
+
+def pass_on(value, count):
+    blocks = [value]
+    for masks in gather_levels(count):
+        blocks = blocks + [swap(block, mask, count) for mask in masks for block in blocks]
+    return blocks
 
 
 def partners(tile_list, count):
     most = tile_list.shape[1]
     me = lax.axis_index("row")
-    lists, places = tree_gather(tile_list[0, :, 1], count)
-    number = me ^ jnp.asarray(places, jnp.int32)
+    lists = tree_gather(tile_list[0, :, 1], count)
+    number = me ^ jnp.asarray(gather_places(count), jnp.int32)
     lower = jnp.any(lists == me, axis=1)
     upper = jnp.any(tile_list[0, :, 1][None, :] == number[:, None], axis=1)
     valid = lower | upper
-    before = jnp.sum((valid[None, :] & (number[None, :] < number[:, None])).astype(jnp.int32), axis=1)
+    earlier = np.tri(count, k=-1, dtype=bool)
+    before = jnp.sum((valid[None, :] & earlier).astype(jnp.int32), axis=1)
     total = jnp.sum(valid.astype(jnp.int32))
-    place = jnp.minimum(jnp.arange(most), jnp.maximum(total - 1, 0))
-    hit = valid[None, :] & (before[None, :] == place[:, None])
-    picked = jnp.sum(jnp.where(hit, number[None, :], 0), axis=1)
+    slot = jnp.minimum(jnp.arange(most), jnp.maximum(total - 1, 0))
+    hit = valid[None, :] & (before[None, :] == slot[:, None])
     where = jnp.sum(jnp.where(hit, jnp.arange(count)[None, :], 0), axis=1)
-    return jnp.concatenate([total[None], picked, where]).astype(jnp.int32)
+    return jnp.concatenate([total[None], where]).astype(jnp.int32)
 
 
 def local(features, right_side, variance, hilbert_order, tile_list):
@@ -282,12 +361,16 @@
     most = tile_list.shape[1]
     steps = width // ROWS
     shape = jax.ShapeDtypeStruct
-    params = pltpu.CompilerParams(vmem_limit_bytes=24 * 1024 * 1024)
+    params = pltpu.CompilerParams(vmem_limit_bytes=10 * 1024 * 1024)
     var_row = variance[None, :]
 
-    payload = jnp.concatenate([features, right_side.astype(BF16)], axis=0)
+    rounded = right_side.astype(BF16)
+    half = width // 2
+    payload = jnp.concatenate(
+        [features[:, :half], features[:, half:], rounded[:, :half], rounded[:, half:]], axis=0
+    )
+    every = pass_on(payload, count)
     slots = partners(tile_list, count)
-    every = lax.all_gather(payload, "row", axis=0)
     scratch = [
         pltpu.VMEM((width, KDIM), BF16),
         pltpu.VMEM((KDIM, width), BF16),
@@ -303,46 +386,53 @@
         grid=(steps,),
         in_specs=[pl.BlockSpec(payload.shape, whole)],
         out_specs=[pl.BlockSpec((ROWS, width), lambda i: (i, 0)), row_spec],
-        out_shape=[shape((width, width), BF16), shape(right_side.shape, F32)],
+        out_shape=[pltpu.HBM((width, width), BF16), shape(right_side.shape, F32)],
         scratch_shapes=scratch,
         compiler_params=params,
         name="own_tile",
     )(payload)
 
-    def tile_at(k, i, s):
-        live = k < s[0]
-        return (jnp.minimum(k, jnp.maximum(s[0] - 1, 0)), jnp.where(live, i, steps - 1), 0)
-
+    def front_at(k, i, s):
+        return (jnp.minimum(k, FRONT - 1), jnp.where(k < FRONT, i, steps - 1), 0)
+
+    def back_at(k, i, s):
+        return (jnp.maximum(k - FRONT, 0), jnp.where(k < FRONT, 0, i), 0)
+
+    tile_specs = [pl.BlockSpec((1, ROWS, width), front_at), pl.BlockSpec((1, ROWS, width), back_at)]
     send_shape = (rhs_count, width + TAIL)
-    pair_tiles, image, send = pl.pallas_call(
+    front_tiles, back_tiles, image, send = pl.pallas_call(
         pair_kernel,
         grid_spec=pltpu.PrefetchScalarGridSpec(
             num_scalar_prefetch=1,
             grid=(most, steps),
             in_specs=[
                 pl.BlockSpec(payload.shape, whole),
-                pl.BlockSpec((1,) + payload.shape, lambda k, i, s: (s[1 + k], 0, 0)),
                 row_spec,
                 row_spec,
                 var_spec,
-            ],
-            out_specs=[
-                pl.BlockSpec((1, ROWS, width), tile_at),
+            ]
+            + [pl.BlockSpec(memory_space=pl.ANY)] * count,
+            out_specs=tile_specs
+            + [
                 row_spec,
                 pl.BlockSpec(send_shape, whole),
             ],
-            scratch_shapes=scratch + [pltpu.VMEM(right_side.shape, F32)],
+            scratch_shapes=scratch
+            + [pltpu.VMEM((2,) + payload.shape, BF16), pltpu.SemaphoreType.DMA((2,))],
         ),
         out_shape=[
-            shape((most, width, width), BF16),
+            pltpu.VMEM((FRONT, width, width), BF16),
+            pltpu.HBM((most - FRONT, width, width), BF16),
             shape(right_side.shape, F32),
             shape(send_shape, BF16),
         ],
         compiler_params=params,
         name="pair_tiles",
-    )(slots, payload, every, own_sum, right_side, var_row)
-
-    every_send, _ = tree_gather(send, count)
+    )(slots, payload, own_sum, right_side, var_row, *every)
+    front_tiles = pltpu.with_memory_space_constraint(front_tiles, pltpu.VMEM)
+    back_tiles = pltpu.with_memory_space_constraint(back_tiles, pltpu.HBM)
+
+    every_send = tree_gather(send, count)
     own_again = pl.pallas_call(
         own_again_kernel,
         grid=(steps,),
@@ -354,7 +444,7 @@
         out_shape=shape(right_side.shape, F32),
         compiler_params=params,
         name="own_again",
-    )(own_tile, send)
+    )(pltpu.with_memory_space_constraint(own_tile, pltpu.HBM), send)
     dots_spec = pl.BlockSpec((rhs_count, TAIL), whole)
     rows, dots, steps_one = pl.pallas_call(
         again_kernel,
@@ -362,8 +452,9 @@
             num_scalar_prefetch=1,
             grid=(most, steps),
             in_specs=[
-                pl.BlockSpec((1, ROWS, width), tile_at),
-                pl.BlockSpec((1,) + send_shape, lambda k, i, s: (s[1 + most + k], 0, 0)),
+                tile_specs[0],
+                pl.BlockSpec(memory_space=pl.ANY),
+                pl.BlockSpec((1,) + send_shape, lambda k, i, s: (s[1 + k], 0, 0)),
                 pl.BlockSpec((count, rhs_count, TAIL), lambda k, i, s: (0, 0, width // TAIL)),
                 row_spec,
                 row_spec,
@@ -375,7 +466,11 @@
                 dots_spec,
                 dots_spec,
             ],
-            scratch_shapes=[pltpu.VMEM(right_side.shape, F32)],
+            scratch_shapes=[
+                pltpu.VMEM(right_side.shape, F32),
+                pltpu.VMEM((HELD, ROWS, width), BF16),
+                pltpu.SemaphoreType.DMA((HELD,)),
+            ],
         ),
         out_shape=[
             shape((4 * rhs_count, width), F32),
@@ -384,7 +479,7 @@
         ],
         compiler_params=params,
         name="pair_again",
-    )(slots, pair_tiles, every_send, every_send, own_again, right_side, var_row, image)
+    )(slots, front_tiles, back_tiles, every_send, every_send, own_again, right_side, var_row, image)
 
     dots = tree_sum(dots, count)
     ordered = pl.pallas_call(

time: 190 us -> 178 us (0.937)
  Pallas kernels: 57.6 us -> 117 us
  starting transfers between devices: 68.1 us -> 29.1 us
  between operations: 14.8 us -> 1.47 us
  waiting for transfers between devices: 29.4 us -> 20.4 us
  local copies, waits for them, and re-layouts: 12.5 us -> 4.78 us
    pallas_call x1, Pallas kernels: 30.3 us -> 83.5 us  [local(): pl.pallas_call(pair_kernel, grid_spec=pltpu.PrefetchScalarGridSpec(num_sc...]
    ppermute x16 -> x31, starting transfers between devices: 68.1 us -> 29.1 us  [swap(): return lax.ppermute(value, 'row', [(i, i ^ mask) for i in range(count)])]
    all_gather x1 -> x0, waiting for transfers between devices: 12.2 us -> none  [local(): every = lax.all_gather(payload, 'row', axis=0)]
    unnamed x24 -> x14, local copies, waits for them, and re-layouts: 11.7 us -> 3.11 us
    pallas_call x1, Pallas kernels: 13.7 us -> 17 us  [local(): pl.pallas_call(own_kernel, grid=(steps,), in_specs=[pl.BlockSpec(payload....]
    pallas_call x1, Pallas kernels: 1.56 us -> 4.74 us  [local(): pl.pallas_call(own_again_kernel, grid=(steps,), in_specs=[pl.BlockSpec((R...]
    ppermute x16 -> x31, waiting for transfers between devices: 17.2 us -> 20.4 us  [swap(): return lax.ppermute(value, 'row', [(i, i ^ mask) for i in range(count)])]
  transfers between devices with their start and end apart: 17 -> 31, of which waited for: 10 -> 13; matrix products, arithmetic and copies ran while one was open for 2% -> 3% of each run, Pallas kernels for 9% -> 13%
where the time goes in v4:
time: 178 us
  Pallas kernels  117 us (66%)
  starting transfers between devices  29.1 us (16%)
  waiting for transfers between devices  20.4 us (11%)
  other arithmetic  5.09 us (3%)
  local copies, waits for them, and re-layouts  4.78 us (3%)
    pallas_call x1, Pallas kernels, local(): pl.pallas_call(pair_kernel, grid_spec=pltpu.PrefetchScalarGridSpec(num_sc...  83.5 us
    ppermute x31, starting transfers between devices, swap(): return lax.ppermute(value, 'row', [(i, i ^ mask) for i in range(count)])  29.1 us
    ppermute x31, waiting for transfers between devices, swap(): return lax.ppermute(value, 'row', [(i, i ^ mask) for i in range(count)])  20.4 us
    pallas_call x1, Pallas kernels, local(): pl.pallas_call(own_kernel, grid=(steps,), in_specs=[pl.BlockSpec(payload....  17 us
    pallas_call x1, Pallas kernels, local(): pl.pallas_call(again_kernel, grid_spec=pltpu.PrefetchScalarGridSpec(num_s...  10 us
    pallas_call x1, Pallas kernels, local(): pl.pallas_call(own_again_kernel, grid=(steps,), in_specs=[pl.BlockSpec((R...  4.74 us
  transfers between devices with their start and end apart: 31, of which 13 were waited for; matrix products, arithmetic and copies ran while one was open for 3% of the time, Pallas kernels for 13%

profile of v4, /device:TPU:0, one launch (start us, length us, event | category | flops | bytes accessed | tf_op | source)
XLA Modules:
  0.0 177.5 jit_solution(2855085809473760096)
XLA Ops:
  1.3 5.0 %collective-permute-start.2 = (s32[1,5]{1,0:T(1,128)S(1)}, s32[1,5]{1,0:T(1,128)S(1)}, u32[]{:S(2)}, u32[]{:S(2)}) collective-permute-start(s32[1,5]{1,0:T(1,128)S(1)} %get-tuple-element.42), channel_id=1, source_target_pairs={{0,12},{1,13},{2,14},{3,15},{4,8},{5,9},{6,10},{7,11},{8,4},{9,5},... | collective-permute-start | bytes 68 | tf_op jit(solution)/shard_map/ppermute | solution.py:291
  7.8 0.9 fusion.4
  8.8 1.8 %collective-permute-start.8 = (bf16[80,1024]{1,0:T(8,128)(2,1)S(1)}, bf16[80,1024]{1,0:T(8,128)(2,1)S(1)}, u32[]{:S(2)}, u32[]{:S(2)}) collective-permute-start(bf16[80,1024]{1,0:T(8,128)(2,1)S(1)} %pad_maximum_fusion.pay_ref.own_ref.refs_0_), channel_id=1, source_target_pairs={{0,2},{1,3},{2,0},{3,1},{4,6},{5,7},{6,4},{7,5},{8,10},{9,11},{10,... | collective-permute-start | bytes 491528 | tf_op jit(solution)/shard_map/ppermute | solution.py:291
  10.6 3.6 %collective-permute-start.7 = (bf16[80,1024]{1,0:T(8,128)(2,1)S(1)}, bf16[80,1024]{1,0:T(8,128)(2,1)S(1)}, u32[]{:S(2)}, u32[]{:S(2)}) collective-permute-start(bf16[80,1024]{1,0:T(8,128)(2,1)S(1)} %pad_maximum_fusion.pay_ref.own_ref.refs_0_), channel_id=1, source_target_pairs={{0,12},{1,13},{2,14},{3,15},{4,8},{5,9},{6,10},{7,11},{8,4},{9,5},... | collective-permute-start | bytes 491528 | tf_op jit(solution)/shard_map/ppermute | solution.py:291
  15.4 2.4 %collective-permute-done.3 = s32[4,5]{1,0:T(4,128)S(1)} collective-permute-done((s32[4,5]{1,0:T(4,128)S(1)}, s32[4,5]{1,0:T(4,128)S(1)}, u32[]{:S(2)}, u32[]{:S(2)}) %collective-permute-start.3) | collective-permute-done | bytes 112 | tf_op jit(solution)/shard_map/ppermute | solution.py:291
  18.0 17.0 %own_tile.1 = (bf16[2048,2048]{1,0:T(8,128)(2,1)}, f32[8,2048]{1,0:T(8,128)S(1)}) custom-call(bf16[80,1024]{1,0:T(8,128)(2,1)S(1)} %pad_maximum_fusion.pay_ref.own_ref.refs_0_), custom_call_target="tpu_custom_call" | custom-call | tf_op jit(solution)/shard_map/own_tile/pallas_call | solution.py:384
  37.9 1.7 collective-permute-start.10
  39.6 2.0 %collective-permute-done.5.refs_1_ = bf16[80,1024]{1,0:T(8,128)(2,1)S(1)} collective-permute-done((bf16[80,1024]{1,0:T(8,128)(2,1)S(1)}, bf16[80,1024]{1,0:T(8,128)(2,1)S(1)}, u32[]{:S(2)}, u32[]{:S(2)}) %collective-permute-start.5) | collective-permute-done | bytes 163872 | tf_op jit(solution)/shard_map/ppermute | solution.py:291
  43.5 1.0 collective-permute-done.11.refs_7_
  44.5 3.5 %collective-permute-done.10.refs_6_ = bf16[80,1024]{1,0:T(8,128)(2,1)S(1)} collective-permute-done((bf16[80,1024]{1,0:T(8,128)(2,1)S(1)}, bf16[80,1024]{1,0:T(8,128)(2,1)S(1)}, u32[]{:S(2)}, u32[]{:S(2)}) %collective-permute-start.10) | collective-permute-done | bytes 163872 | tf_op jit(solution)/shard_map/ppermute | solution.py:291
  48.0 2.9 %collective-permute-done.9.refs_5_ = bf16[80,1024]{1,0:T(8,128)(2,1)S(1)} collective-permute-done((bf16[80,1024]{1,0:T(8,128)(2,1)S(1)}, bf16[80,1024]{1,0:T(8,128)(2,1)S(1)}, u32[]{:S(2)}, u32[]{:S(2)}) %collective-permute-start.9) | collective-permute-done | bytes 163872 | tf_op jit(solution)/shard_map/ppermute | solution.py:291
  53.8 83.5 %pair_tiles.1 = (bf16[3,2048,2048]{2,1,0:T(8,128)(2,1)S(1)}, bf16[2,2048,2048]{2,1,0:T(8,128)(2,1)}, f32[8,2048]{1,0:T(8,128)S(1)}, bf16[8,2176]{1,0:T(8,128)(2,1)S(1)}) custom-call(s32[6]{0:T(128)S(1)} %pad_add_fusion.1.slots_ref, bf16[80,1024]{1,0:T(8,128)(2,1)S(1)} %pad_maximum_fusion.pay_ref.own_ref.refs_0_, f32[8,2048]{1,0:T(8,128)S(1)} %get-tuple-element.11.first_ref, ...), custom_call_target="tpu_custom_call" | custom-call | tf_op jit(solution)/shard_map/pair_tiles/pallas_call | solution.py:403
  137.5 2.3 %collective-permute-start.21 = (bf16[1,8,2176]{2,1,0:T(8,128)(2,1)S(1)}, bf16[1,8,2176]{2,1,0:T(8,128)(2,1)S(1)}, u32[]{:S(2)}, u32[]{:S(2)}) collective-permute-start(bf16[1,8,2176]{2,1,0:T(8,128)(2,1)S(1)} %bitcast.10), channel_id=1, source_target_pairs={{0,8},{1,9},{2,10},{3,11},{4,12},{5,13},{6,14},{7,15},{8,0},{9,1},... | collective-permute-start | bytes 104456 | tf_op jit(solution)/shard_map/ppermute | solution.py:291
  139.8 2.1 %collective-permute-start.20 = (bf16[1,8,2176]{2,1,0:T(8,128)(2,1)S(1)}, bf16[1,8,2176]{2,1,0:T(8,128)(2,1)S(1)}, u32[]{:S(2)}, u32[]{:S(2)}) collective-permute-start(bf16[1,8,2176]{2,1,0:T(8,128)(2,1)S(1)} %bitcast.11), channel_id=1, source_target_pairs={{0,4},{1,5},{2,6},{3,7},{4,0},{5,1},{6,2},{7,3},{8,12},{9,13},{10,... | collective-permute-start | bytes 104456 | tf_op jit(solution)/shard_map/ppermute | solution.py:291
  141.9 1.5 collective-permute-done.22
  144.2 2.3 %collective-permute-start.23 = (bf16[4,8,2176]{2,1,0:T(8,128)(2,1)S(1)}, bf16[4,8,2176]{2,1,0:T(8,128)(2,1)S(1)}, u32[]{:S(2)}, u32[]{:S(2)}) collective-permute-start(bf16[4,8,2176]{2,1,0:T(8,128)(2,1)S(1)} %pad_maximum_fusion.1), channel_id=1, source_target_pairs={{0,2},{1,3},{2,0},{3,1},{4,6},{5,7},{6,4},{7,5},{8,10},{9,11},{10,... | collective-permute-start | bytes 417800 | tf_op jit(solution)/shard_map/ppermute | solution.py:291
  146.6 3.8 %collective-permute-done.23 = bf16[4,8,2176]{2,1,0:T(8,128)(2,1)S(1)} collective-permute-done((bf16[4,8,2176]{2,1,0:T(8,128)(2,1)S(1)}, bf16[4,8,2176]{2,1,0:T(8,128)(2,1)S(1)}, u32[]{:S(2)}, u32[]{:S(2)}) %collective-permute-start.23) | collective-permute-done | bytes 139296 | tf_op jit(solution)/shard_map/ppermute | solution.py:291
  150.5 4.7 %own_again.1.first_ref = f32[8,2048]{1,0:T(8,128)S(1)} custom-call(bf16[2048,2048]{1,0:T(8,128)(2,1)} %get-tuple-element.15.tile_ref, bf16[8,2176]{1,0:T(8,128)(2,1)S(1)} %get-tuple-element.14.vec_ref), custom_call_target="tpu_custom_call" | custom-call | tf_op jit(solution)/shard_map/own_again/pallas_call | solution.py:436
  156.8 10.0 %pair_again.1 = (f32[32,2048]{1,0:T(8,128)S(1)}, f32[8,128]{1,0:T(8,128)S(1)}, f32[8,128]{1,0:T(8,128)S(1)}) custom-call(s32[6]{0:T(128)S(1)} %pad_add_fusion.1.slots_ref, bf16[3,2048,2048]{2,1,0:T(8,128)(2,1)S(1)} %get-tuple-element.12.front_ref, bf16[2,2048,2048]{2,1,0:T(8,128)(2,1)} %get-tuple-element.13.back_ref, ...), custom_call_target="tpu_custom_call" | custom-call | tf_op jit(solution)/shard_map/pair_again/pallas_call | solution.py:449
  166.9 1.8 %collective-permute-start.26 = (f32[8,128]{1,0:T(8,128)S(1)}, f32[8,128]{1,0:T(8,128)S(1)}, u32[]{:S(2)}, u32[]{:S(2)}) collective-permute-start(f32[8,128]{1,0:T(8,128)S(1)} %get-tuple-element.19), channel_id=1, source_target_pairs={{0,8},{1,9},{2,10},{3,11},{4,12},{5,13},{6,14},{7,15},{8,0},{9,1},... | collective-permute-start | bytes 12296 | tf_op jit(solution)/shard_map/ppermute | solution.py:291
  168.7 2.6 %collective-permute-start.25 = (f32[8,128]{1,0:T(8,128)S(1)}, f32[8,128]{1,0:T(8,128)S(1)}, u32[]{:S(2)}, u32[]{:S(2)}) collective-permute-start(f32[8,128]{1,0:T(8,128)S(1)} %get-tuple-element.19), channel_id=1, source_target_pairs={{0,4},{1,5},{2,6},{3,7},{4,0},{5,1},{6,2},{7,3},{8,12},{9,13},{10,... | collective-permute-start | bytes 12296 | tf_op jit(solution)/shard_map/ppermute | solution.py:291
  171.3 1.0 collective-permute-done.27
  172.9 1.8 collective-permute-start.29
  174.7 1.5 curve_order.1
  (80 shorter events, 15.3 us)
Async XLA Ops:
  1.3 9.3 %collective-permute-start.2 = (s32[1,5]{1,0:T(1,128)S(1)}, s32[1,5]{1,0:T(1,128)S(1)}, u32[]{:S(2)}, u32[]{:S(2)}) collective-permute-start(s32[1,5]{1,0:T(1,128)S(1)} %get-tuple-element.42), channel_id=1, source_target_pairs={{0,12},{1,13},{2,14},{3,15},{4,8},{5,9},{6,10},{7,11},{8,4},{9,5},... | collective-permute-start | bytes 68 | tf_op jit(solution)/shard_map/ppermute | solution.py:291
  6.4 7.8 %collective-permute-start.1 = (s32[1,5]{1,0:T(1,128)S(1)}, s32[1,5]{1,0:T(1,128)S(1)}, u32[]{:S(2)}, u32[]{:S(2)}) collective-permute-start(s32[1,5]{1,0:T(1,128)S(1)} %get-tuple-element.42), channel_id=1, source_target_pairs={{0,8},{1,9},{2,10},{3,11},{4,12},{5,13},{6,14},{7,15},{8,0},{9,1},... | collective-permute-start | bytes 68 | tf_op jit(solution)/shard_map/ppermute | solution.py:291
  6.4 7.8 %collective-permute-start = (s32[1,5]{1,0:T(1,128)S(1)}, s32[1,5]{1,0:T(1,128)S(1)}, u32[]{:S(2)}, u32[]{:S(2)}) collective-permute-start(s32[1,5]{1,0:T(1,128)S(1)} %get-tuple-element.42), channel_id=1, source_target_pairs={{0,4},{1,5},{2,6},{3,7},{4,0},{5,1},{6,2},{7,3},{8,12},{9,13},{10,... | collective-permute-start | bytes 68 | tf_op jit(solution)/shard_map/ppermute | solution.py:291
  8.7 28.8 %collective-permute-start.12 = (bf16[80,1024]{1,0:T(8,128)(2,1)S(1)}, bf16[80,1024]{1,0:T(8,128)(2,1)S(1)}, u32[]{:S(2)}, u32[]{:S(2)}) collective-permute-start(bf16[80,1024]{1,0:T(8,128)(2,1)S(1)} %pad_maximum_fusion.pay_ref.own_ref.refs_0_), channel_id=1, source_target_pairs={{0,1},{1,0},{2,3},{3,2},{4,5},{5,4},{6,7},{7,6},{8,9},{9,8},{10,11... | collective-permute-start | bytes 491528 | tf_op jit(solution)/shard_map/ppermute | solution.py:291
  8.8 29.1 %collective-permute-start.8 = (bf16[80,1024]{1,0:T(8,128)(2,1)S(1)}, bf16[80,1024]{1,0:T(8,128)(2,1)S(1)}, u32[]{:S(2)}, u32[]{:S(2)}) collective-permute-start(bf16[80,1024]{1,0:T(8,128)(2,1)S(1)} %pad_maximum_fusion.pay_ref.own_ref.refs_0_), channel_id=1, source_target_pairs={{0,2},{1,3},{2,0},{3,1},{4,6},{5,7},{6,4},{7,5},{8,10},{9,11},{10,... | collective-permute-start | bytes 491528 | tf_op jit(solution)/shard_map/ppermute | solution.py:291
  10.6 26.6 %collective-permute-start.7 = (bf16[80,1024]{1,0:T(8,128)(2,1)S(1)}, bf16[80,1024]{1,0:T(8,128)(2,1)S(1)}, u32[]{:S(2)}, u32[]{:S(2)}) collective-permute-start(bf16[80,1024]{1,0:T(8,128)(2,1)S(1)} %pad_maximum_fusion.pay_ref.own_ref.refs_0_), channel_id=1, source_target_pairs={{0,12},{1,13},{2,14},{3,15},{4,8},{5,9},{6,10},{7,11},{8,4},{9,5},... | collective-permute-start | bytes 491528 | tf_op jit(solution)/shard_map/ppermute | solution.py:291
  14.2 23.7 %collective-permute-start.6 = (bf16[80,1024]{1,0:T(8,128)(2,1)S(1)}, bf16[80,1024]{1,0:T(8,128)(2,1)S(1)}, u32[]{:S(2)}, u32[]{:S(2)}) collective-permute-start(bf16[80,1024]{1,0:T(8,128)(2,1)S(1)} %pad_maximum_fusion.pay_ref.own_ref.refs_0_), channel_id=1, source_target_pairs={{0,8},{1,9},{2,10},{3,11},{4,12},{5,13},{6,14},{7,15},{8,0},{9,1},... | collective-permute-start | bytes 491528 | tf_op jit(solution)/shard_map/ppermute | solution.py:291
  17.9 17.1 %collective-permute-start.4 = (s32[8,5]{1,0:T(8,128)S(1)}, s32[8,5]{1,0:T(8,128)S(1)}, u32[]{:S(2)}, u32[]{:S(2)}) collective-permute-start(s32[8,5]{1,0:T(8,128)S(1)} %concatenate.29), channel_id=1, source_target_pairs={{0,1},{1,0},{2,3},{3,2},{4,5},{5,4},{6,7},{7,6},{8,9},{9,8},{10,11... | collective-permute-start | bytes 488 | tf_op jit(solution)/shard_map/ppermute | solution.py:291
  35.0 6.6 %collective-permute-start.5 = (bf16[80,1024]{1,0:T(8,128)(2,1)S(1)}, bf16[80,1024]{1,0:T(8,128)(2,1)S(1)}, u32[]{:S(2)}, u32[]{:S(2)}) collective-permute-start(bf16[80,1024]{1,0:T(8,128)(2,1)S(1)} %pad_maximum_fusion.pay_ref.own_ref.refs_0_), channel_id=1, source_target_pairs={{0,4},{1,5},{2,6},{3,7},{4,0},{5,1},{6,2},{7,3},{8,12},{9,13},{10,... | collective-permute-start | bytes 491528 | tf_op jit(solution)/shard_map/ppermute | solution.py:291
  37.2 5.8 %collective-permute-start.15 = (bf16[80,1024]{1,0:T(8,128)(2,1)S(1)}, bf16[80,1024]{1,0:T(8,128)(2,1)S(1)}, u32[]{:S(2)}, u32[]{:S(2)}) collective-permute-start(bf16[80,1024]{1,0:T(8,128)(2,1)S(1)} %collective-permute-done.7.refs_3_), channel_id=1, source_target_pairs={{0,1},{1,0},{2,3},{3,2},{4,5},{5,4},{6,7},{7,6},{8,9},{9,8},{10,11... | collective-permute-start | bytes 491528 | tf_op jit(solution)/shard_map/ppermute | solution.py:291
  37.5 7.0 %collective-permute-start.11 = (bf16[80,1024]{1,0:T(8,128)(2,1)S(1)}, bf16[80,1024]{1,0:T(8,128)(2,1)S(1)}, u32[]{:S(2)}, u32[]{:S(2)}) collective-permute-start(bf16[80,1024]{1,0:T(8,128)(2,1)S(1)} %collective-permute-done.7.refs_3_), channel_id=1, source_target_pairs={{0,2},{1,3},{2,0},{3,1},{4,6},{5,7},{6,4},{7,5},{8,10},{9,11},{10,... | collective-permute-start | bytes 491528 | tf_op jit(solution)/shard_map/ppermute | solution.py:291
  37.9 5.0 %collective-permute-start.16 = (bf16[80,1024]{1,0:T(8,128)(2,1)S(1)}, bf16[80,1024]{1,0:T(8,128)(2,1)S(1)}, u32[]{:S(2)}, u32[]{:S(2)}) collective-permute-start(bf16[80,1024]{1,0:T(8,128)(2,1)S(1)} %collective-permute-done.8.refs_4_), channel_id=1, source_target_pairs={{0,1},{1,0},{2,3},{3,2},{4,5},{5,4},{6,7},{7,6},{8,9},{9,8},{10,11... | collective-permute-start | bytes 491528 | tf_op jit(solution)/shard_map/ppermute | solution.py:291
  37.9 10.1 %collective-permute-start.10 = (bf16[80,1024]{1,0:T(8,128)(2,1)S(1)}, bf16[80,1024]{1,0:T(8,128)(2,1)S(1)}, u32[]{:S(2)}, u32[]{:S(2)}) collective-permute-start(bf16[80,1024]{1,0:T(8,128)(2,1)S(1)} %collective-permute-done.6.refs_2_), channel_id=1, source_target_pairs={{0,2},{1,3},{2,0},{3,1},{4,6},{5,7},{6,4},{7,5},{8,10},{9,11},{10,... | collective-permute-start | bytes 491528 | tf_op jit(solution)/shard_map/ppermute | solution.py:291
  41.6 9.3 %collective-permute-start.9 = (bf16[80,1024]{1,0:T(8,128)(2,1)S(1)}, bf16[80,1024]{1,0:T(8,128)(2,1)S(1)}, u32[]{:S(2)}, u32[]{:S(2)}) collective-permute-start(bf16[80,1024]{1,0:T(8,128)(2,1)S(1)} %collective-permute-done.5.refs_1_), channel_id=1, source_target_pairs={{0,2},{1,3},{2,0},{3,1},{4,6},{5,7},{6,4},{7,5},{8,10},{9,11},{10,... | collective-permute-start | bytes 491528 | tf_op jit(solution)/shard_map/ppermute | solution.py:291
  42.9 8.9 %collective-permute-start.14 = (bf16[80,1024]{1,0:T(8,128)(2,1)S(1)}, bf16[80,1024]{1,0:T(8,128)(2,1)S(1)}, u32[]{:S(2)}, u32[]{:S(2)}) collective-permute-start(bf16[80,1024]{1,0:T(8,128)(2,1)S(1)} %collective-permute-done.6.refs_2_), channel_id=1, source_target_pairs={{0,1},{1,0},{2,3},{3,2},{4,5},{5,4},{6,7},{7,6},{8,9},{9,8},{10,11... | collective-permute-start | bytes 491528 | tf_op jit(solution)/shard_map/ppermute | solution.py:291
  43.0 8.8 %collective-permute-start.13 = (bf16[80,1024]{1,0:T(8,128)(2,1)S(1)}, bf16[80,1024]{1,0:T(8,128)(2,1)S(1)}, u32[]{:S(2)}, u32[]{:S(2)}) collective-permute-start(bf16[80,1024]{1,0:T(8,128)(2,1)S(1)} %collective-permute-done.5.refs_1_), channel_id=1, source_target_pairs={{0,1},{1,0},{2,3},{3,2},{4,5},{5,4},{6,7},{7,6},{8,9},{9,8},{10,11... | collective-permute-start | bytes 491528 | tf_op jit(solution)/shard_map/ppermute | solution.py:291
  44.5 7.3 %collective-permute-start.19 = (bf16[80,1024]{1,0:T(8,128)(2,1)S(1)}, bf16[80,1024]{1,0:T(8,128)(2,1)S(1)}, u32[]{:S(2)}, u32[]{:S(2)}) collective-permute-start(bf16[80,1024]{1,0:T(8,128)(2,1)S(1)} %collective-permute-done.11.refs_7_), channel_id=1, source_target_pairs={{0,1},{1,0},{2,3},{3,2},{4,5},{5,4},{6,7},{7,6},{8,9},{9,8},{10,11... | collective-permute-start | bytes 491528 | tf_op jit(solution)/shard_map/ppermute | solution.py:291
  137.4 5.9 %collective-permute-start.22 = (bf16[1,8,2176]{2,1,0:T(8,128)(2,1)S(1)}, bf16[1,8,2176]{2,1,0:T(8,128)(2,1)S(1)}, u32[]{:S(2)}, u32[]{:S(2)}) collective-permute-start(bf16[1,8,2176]{2,1,0:T(8,128)(2,1)S(1)} %bitcast.9), channel_id=1, source_target_pairs={{0,12},{1,13},{2,14},{3,15},{4,8},{5,9},{6,10},{7,11},{8,4},{9,5},... | collective-permute-start | bytes 104456 | tf_op jit(solution)/shard_map/ppermute | solution.py:291
  137.5 6.0 %collective-permute-start.21 = (bf16[1,8,2176]{2,1,0:T(8,128)(2,1)S(1)}, bf16[1,8,2176]{2,1,0:T(8,128)(2,1)S(1)}, u32[]{:S(2)}, u32[]{:S(2)}) collective-permute-start(bf16[1,8,2176]{2,1,0:T(8,128)(2,1)S(1)} %bitcast.10), channel_id=1, source_target_pairs={{0,8},{1,9},{2,10},{3,11},{4,12},{5,13},{6,14},{7,15},{8,0},{9,1},... | collective-permute-start | bytes 104456 | tf_op jit(solution)/shard_map/ppermute | solution.py:291
  139.8 4.4 %collective-permute-start.20 = (bf16[1,8,2176]{2,1,0:T(8,128)(2,1)S(1)}, bf16[1,8,2176]{2,1,0:T(8,128)(2,1)S(1)}, u32[]{:S(2)}, u32[]{:S(2)}) collective-permute-start(bf16[1,8,2176]{2,1,0:T(8,128)(2,1)S(1)} %bitcast.11), channel_id=1, source_target_pairs={{0,4},{1,5},{2,6},{3,7},{4,0},{5,1},{6,2},{7,3},{8,12},{9,13},{10,... | collective-permute-start | bytes 104456 | tf_op jit(solution)/shard_map/ppermute | solution.py:291
  144.2 6.2 %collective-permute-start.23 = (bf16[4,8,2176]{2,1,0:T(8,128)(2,1)S(1)}, bf16[4,8,2176]{2,1,0:T(8,128)(2,1)S(1)}, u32[]{:S(2)}, u32[]{:S(2)}) collective-permute-start(bf16[4,8,2176]{2,1,0:T(8,128)(2,1)S(1)} %pad_maximum_fusion.1), channel_id=1, source_target_pairs={{0,2},{1,3},{2,0},{3,1},{4,6},{5,7},{6,4},{7,5},{8,10},{9,11},{10,... | collective-permute-start | bytes 417800 | tf_op jit(solution)/shard_map/ppermute | solution.py:291
  150.4 4.8 %collective-permute-start.24 = (bf16[8,8,2176]{2,1,0:T(8,128)(2,1)S(1)}, bf16[8,8,2176]{2,1,0:T(8,128)(2,1)S(1)}, u32[]{:S(2)}, u32[]{:S(2)}) collective-permute-start(bf16[8,8,2176]{2,1,0:T(8,128)(2,1)S(1)} %get-tuple-element.27), channel_id=1, source_target_pairs={{0,1},{1,0},{2,3},{3,2},{4,5},{5,4},{6,7},{7,6},{8,9},{9,8},{10,11... | collective-permute-start | bytes 835592 | tf_op jit(solution)/shard_map/ppermute | solution.py:291
  166.8 5.5 %collective-permute-start.27 = (f32[8,128]{1,0:T(8,128)S(1)}, f32[8,128]{1,0:T(8,128)S(1)}, u32[]{:S(2)}, u32[]{:S(2)}) collective-permute-start(f32[8,128]{1,0:T(8,128)S(1)} %get-tuple-element.19), channel_id=1, source_target_pairs={{0,12},{1,13},{2,14},{3,15},{4,8},{5,9},{6,10},{7,11},{8,4},{9,5},... | collective-permute-start | bytes 12296 | tf_op jit(solution)/shard_map/ppermute | solution.py:291
  166.9 5.4 %collective-permute-start.26 = (f32[8,128]{1,0:T(8,128)S(1)}, f32[8,128]{1,0:T(8,128)S(1)}, u32[]{:S(2)}, u32[]{:S(2)}) collective-permute-start(f32[8,128]{1,0:T(8,128)S(1)} %get-tuple-element.19), channel_id=1, source_target_pairs={{0,8},{1,9},{2,10},{3,11},{4,12},{5,13},{6,14},{7,15},{8,0},{9,1},... | collective-permute-start | bytes 12296 | tf_op jit(solution)/shard_map/ppermute | solution.py:291
  (12 other events, 42.9 us)

commit v5 on v4

--- a/solution.py
+++ b/solution.py
@@ -1,3 +1,5 @@
+import functools
+
 import jax
 import jax.numpy as jnp
 import numpy as np
@@ -7,13 +9,13 @@
 from jax.sharding import PartitionSpec as P
 
 SHRINK = 0.95
-GRAM = SHRINK * SHRINK / 4.0
+GRAM = SHRINK * SHRINK
 SCALE = 20.0 * (20.0 / 19.0) ** 19
 DIAGONAL = float(1.0 - SCALE * float(np.float32(1.0 / SCALE).astype(jnp.bfloat16)))
 KDIM = 128
 ROWS = 512
+PARTS = 4
 UNIT = 256
-SUB = 64
 FRONT = 3
 HELD = 4
 TAIL = 128
@@ -50,11 +52,10 @@
     return jnp.transpose(jnp.concatenate([feat, feat, feat, norm_rows(norm, 3)], axis=0))
 
 
-def psi_tile(quarter):
-    quarter = jnp.maximum(quarter, 1e-30)
-    start = lax.rsqrt(quarter.astype(BF16)).astype(F32)
-    w = quarter * start
-    u = jnp.maximum(SHRINK + w * (w * start - 3.0), 0.0)
+def psi_chain(dist):
+    dist = jnp.maximum(dist, 1e-30)
+    radius = dist * lax.rsqrt(dist)
+    u = jnp.maximum(SHRINK - radius, 0.0)
     two = u * u
     four = two * two
     eight = four * four
@@ -62,7 +63,14 @@
     return (sixteen * two * (u - two)).astype(BF16)
 
 
-def tile_rows(left_ref, right_ref, vec_ref, begin, tile_ref, sum_ref, dist_refs):
+def psi_power(dist):
+    dist = jnp.maximum(dist, 1e-30)
+    radius = dist * lax.rsqrt(dist)
+    u = jnp.maximum(SHRINK - radius, 1e-30)
+    return (jnp.exp2(19.0 * lax.log2(u)) * (1.0 - u)).astype(BF16)
+
+
+def tile_rows(left_ref, right_ref, vec_ref, begin, tile_ref, sum_ref, dist_refs, psi, rows_at_once):
     width = right_ref.shape[1]
     units = width // UNIT
 
@@ -93,9 +101,9 @@
             else:
                 gram(following, 0, dist_refs[(unit + 1) % 2])
             col = unit * UNIT
-            for sub in range(0, UNIT, SUB):
-                tile_ref[pl.ds(at + sub, SUB), col : col + UNIT] = psi_tile(
-                    dist_refs[unit % 2][sub : sub + SUB, :]
+            for sub in range(0, UNIT, rows_at_once):
+                tile_ref[pl.ds(at + sub, rows_at_once), col : col + UNIT] = psi(
+                    dist_refs[unit % 2][sub : sub + rows_at_once, :]
                 )
             if unit:
                 product(vec, at, unit - 1)
@@ -110,24 +118,25 @@
     return jnp.concatenate([pay[:32], pay[32:64]], axis=1), jnp.concatenate([pay[64:72], pay[72:80]], axis=1)
 
 
-def own_kernel(pay_ref, tile_ref, sum_ref, left_ref, right_ref, vec_ref, *dist_refs):
-    step = pl.program_id(0)
-
-    @pl.when(step == 0)
-    def _():
-        feat, vec = unpack(pay_ref[...])
-        left_ref[...] = other_factor(feat)
-        right_ref[...] = own_factor(feat)
-        vec_ref[...] = vec
-        sum_ref[...] = jnp.zeros_like(sum_ref)
-
-    tile_rows(left_ref, right_ref, vec_ref, step * ROWS, tile_ref, sum_ref, dist_refs)
-
-
-def pair_kernel(slots_ref, own_ref, first_ref, rhs_ref, var_ref, *refs):
-    block_refs = refs[:-11]
-    front_ref, back_ref, image_ref, send_ref = refs[-11:-7]
-    left_ref, right_ref, vec_ref, dist_zero_ref, dist_one_ref, pay_ref, sem_ref = refs[-7:]
+def own_kernel(part, pay_ref, right_in_ref, arrived_ref, tile_ref, sum_ref, left_ref, vec_ref, *dist_refs):
+    feat, vec = unpack(pay_ref[...])
+    begin = part * ROWS
+    left_ref[...] = other_factor(feat[:, begin : begin + ROWS])
+    vec_ref[...] = vec[:, begin : begin + ROWS]
+    sum_ref[...] = jnp.zeros_like(sum_ref)
+    tile_rows(left_ref, right_in_ref, vec_ref, 0, tile_ref, sum_ref, dist_refs, psi_chain, 16)
+
+
+def factor_kernel(pay_ref, list_ref, right_ref, list_out_ref):
+    right_ref[...] = own_factor(unpack(pay_ref[...])[0])
+    list_out_ref[...] = list_ref[...]
+
+
+def pair_kernel(slots_ref, right_ref, rhs_ref, var_ref, *refs):
+    first_refs = refs[:PARTS]
+    block_refs = refs[PARTS:-10]
+    front_ref, back_ref, image_ref, send_ref = refs[-10:-6]
+    left_ref, vec_ref, dist_zero_ref, dist_one_ref, pay_ref, sem_ref = refs[-6:]
     slot, step = pl.program_id(0), pl.program_id(1)
     sum_ref = image_ref
 
@@ -142,8 +151,7 @@
 
     @pl.when((slot == 0) & (step == 0))
     def _():
-        right_ref[...] = own_factor(unpack(own_ref[...])[0])
-        sum_ref[...] = first_ref[...]
+        sum_ref[...] = functools.reduce(jnp.add, [first_ref[...] for first_ref in first_refs])
 
         @pl.when(slots_ref[0] > 0)
         def _():
@@ -170,7 +178,7 @@
             def _():
                 tile_rows(
                     left_ref, right_ref, vec_ref, step * ROWS, tile_ref.at[0], sum_ref,
-                    (dist_zero_ref, dist_one_ref),
+                    (dist_zero_ref, dist_one_ref), psi_power, 64,
                 )
 
     @pl.when((slot == pl.num_programs(0) - 1) & (step == pl.num_programs(1) - 1))
@@ -189,17 +197,20 @@
         send_ref[:, width:] = tail.astype(BF16)
 
 
-def own_again_kernel(tile_ref, vec_ref, sum_ref):
+def own_again_kernel(*refs):
+    tile_refs, (vec_ref, sum_ref) = refs[:PARTS], refs[PARTS:]
     step = pl.program_id(0)
+    rows = tile_refs[0].shape[0]
 
     @pl.when(step == 0)
     def _():
         sum_ref[...] = jnp.zeros_like(sum_ref)
 
-    at = pl.multiple_of(step * ROWS, ROWS)
-    sum_ref[...] += jnp.dot(
-        vec_ref[:, pl.ds(at, ROWS)], tile_ref[...], preferred_element_type=F32
-    )
+    for part, tile_ref in enumerate(tile_refs):
+        at = pl.multiple_of(part * ROWS + step * rows, rows)
+        sum_ref[...] += jnp.dot(
+            vec_ref[:, pl.ds(at, rows)], tile_ref[...], preferred_element_type=F32
+        )
 
 
 def again_kernel(
@@ -337,13 +348,13 @@
     return blocks
 
 
-def partners(tile_list, count):
-    most = tile_list.shape[1]
+def partners(coupled, count):
+    most = coupled.shape[1]
     me = lax.axis_index("row")
-    lists = tree_gather(tile_list[0, :, 1], count)
+    lists = tree_gather(coupled[0], count)
     number = me ^ jnp.asarray(gather_places(count), jnp.int32)
     lower = jnp.any(lists == me, axis=1)
-    upper = jnp.any(tile_list[0, :, 1][None, :] == number[:, None], axis=1)
+    upper = jnp.any(coupled == number[:, None], axis=1)
     valid = lower | upper
     earlier = np.tri(count, k=-1, dtype=bool)
     before = jnp.sum((valid[None, :] & earlier).astype(jnp.int32), axis=1)
@@ -370,27 +381,38 @@
         [features[:, :half], features[:, half:], rounded[:, :half], rounded[:, half:]], axis=0
     )
     every = pass_on(payload, count)
-    slots = partners(tile_list, count)
-    scratch = [
-        pltpu.VMEM((width, KDIM), BF16),
-        pltpu.VMEM((KDIM, width), BF16),
-        pltpu.VMEM((rhs_count, width), BF16),
-        pltpu.VMEM((UNIT, UNIT), F32),
-        pltpu.VMEM((UNIT, UNIT), F32),
-    ]
+    dist_scratch = [pltpu.VMEM((UNIT, UNIT), F32)] * 2
     whole = lambda *ignored: (0, 0)
     row_spec = pl.BlockSpec(right_side.shape, whole)
     var_spec = pl.BlockSpec(var_row.shape, whole)
-    own_tile, own_sum = pl.pallas_call(
-        own_kernel,
-        grid=(steps,),
-        in_specs=[pl.BlockSpec(payload.shape, whole)],
-        out_specs=[pl.BlockSpec((ROWS, width), lambda i: (i, 0)), row_spec],
-        out_shape=[pltpu.HBM((width, width), BF16), shape(right_side.shape, F32)],
-        scratch_shapes=scratch,
+    right, coupled = pl.pallas_call(
+        factor_kernel,
+        out_shape=[shape((KDIM, width), BF16), shape((1, most), jnp.int32)],
         compiler_params=params,
-        name="own_tile",
-    )(payload)
+        name="own_factor",
+    )(payload, tile_list[:, :, 1])
+    slots = partners(coupled, count)
+    own_parts = [
+        pl.pallas_call(
+            functools.partial(own_kernel, part),
+            in_specs=[
+                pl.BlockSpec(payload.shape, lambda: (0, 0)),
+                pl.BlockSpec(right.shape, lambda: (0, 0)),
+                pl.BlockSpec(memory_space=pl.ANY),
+            ],
+            out_shape=[pltpu.HBM((ROWS, width), BF16), shape(right_side.shape, F32)],
+            scratch_shapes=[pltpu.VMEM((ROWS, KDIM), BF16), pltpu.VMEM((rhs_count, ROWS), BF16)]
+            + dist_scratch,
+            compiler_params=params,
+            cost_estimate=pl.CostEstimate(
+                flops=4_000_000_000, bytes_accessed=2 * ROWS * width, transcendentals=0
+            ),
+            name=f"own_tile_{part}",
+        )(payload, right, every[part])
+        for part in range(PARTS)
+    ]
+    own_tiles = [part[0] for part in own_parts]
+    own_sums = [part[1] for part in own_parts]
 
     def front_at(k, i, s):
         return (jnp.minimum(k, FRONT - 1), jnp.where(k < FRONT, i, steps - 1), 0)
@@ -406,18 +428,19 @@
             num_scalar_prefetch=1,
             grid=(most, steps),
             in_specs=[
-                pl.BlockSpec(payload.shape, whole),
-                row_spec,
+                pl.BlockSpec(right.shape, whole),
                 row_spec,
                 var_spec,
             ]
+            + [row_spec] * PARTS
             + [pl.BlockSpec(memory_space=pl.ANY)] * count,
             out_specs=tile_specs
             + [
                 row_spec,
                 pl.BlockSpec(send_shape, whole),
             ],
-            scratch_shapes=scratch
+            scratch_shapes=[pltpu.VMEM((width, KDIM), BF16), pltpu.VMEM((rhs_count, width), BF16)]
+            + dist_scratch
             + [pltpu.VMEM((2,) + payload.shape, BF16), pltpu.SemaphoreType.DMA((2,))],
         ),
         out_shape=[
@@ -428,23 +451,21 @@
         ],
         compiler_params=params,
         name="pair_tiles",
-    )(slots, payload, own_sum, right_side, var_row, *every)
+    )(slots, right, right_side, var_row, *own_sums, *every)
     front_tiles = pltpu.with_memory_space_constraint(front_tiles, pltpu.VMEM)
     back_tiles = pltpu.with_memory_space_constraint(back_tiles, pltpu.HBM)
 
     every_send = tree_gather(send, count)
     own_again = pl.pallas_call(
         own_again_kernel,
-        grid=(steps,),
-        in_specs=[
-            pl.BlockSpec((ROWS, width), lambda i: (i, 0)),
-            pl.BlockSpec(send_shape, whole),
-        ],
+        grid=(2,),
+        in_specs=[pl.BlockSpec((ROWS // 2, width), lambda i: (i, 0))] * PARTS
+        + [pl.BlockSpec(send_shape, whole)],
         out_specs=row_spec,
         out_shape=shape(right_side.shape, F32),
         compiler_params=params,
         name="own_again",
-    )(pltpu.with_memory_space_constraint(own_tile, pltpu.HBM), send)
+    )(*[pltpu.with_memory_space_constraint(tile, pltpu.HBM) for tile in own_tiles], send)
     dots_spec = pl.BlockSpec((rhs_count, TAIL), whole)
     rows, dots, steps_one = pl.pallas_call(
         again_kernel,

time: 178 us -> 167 us (0.938)
  Pallas kernels: 117 us -> 47.4 us
  starting transfers between devices: 29.1 us -> 85.2 us
  waiting for transfers between devices: 20.4 us -> 27 us
  local copies, waits for them, and re-layouts: 4.78 us -> 1.74 us
    pallas_call x1, Pallas kernels: 83.5 us -> 20.1 us  [local(): pl.pallas_call(pair_kernel, grid_spec=pltpu.PrefetchScalarGridSpec(num_sc...]
    ppermute x31, starting transfers between devices: 29.1 us -> 85.2 us  [swap(): return lax.ppermute(value, 'row', [(i, i ^ mask) for i in range(count)])]
    pallas_call x1, Pallas kernels: 10 us -> 3.29 us  [local(): pl.pallas_call(again_kernel, grid_spec=pltpu.PrefetchScalarGridSpec(num_s...]
    ppermute x31, waiting for transfers between devices: 20.4 us -> 27 us  [swap(): return lax.ppermute(value, 'row', [(i, i ^ mask) for i in range(count)])]
    unnamed x14, local copies, waits for them, and re-layouts: 3.11 us -> 0.07 us
    pallas_call x2 -> x6, Pallas kernels: 21.7 us -> 22.5 us  [the longest x4 18.3 us: local(): pl.pallas_call(functools.partial(own_kernel, part), in_specs=[pl.BlockSpe...]
  transfers between devices with their start and end apart: 31 -> 31, of which waited for: 13 -> 13; matrix products, arithmetic and copies ran while one was open for 3% -> 2% of each run, Pallas kernels for 13% -> 14%
where the time goes in v5:
time: 167 us
  starting transfers between devices  85.2 us (51%)
  Pallas kernels  47.4 us (28%)
  waiting for transfers between devices  27 us (16%)
  other arithmetic  3.76 us (2%)
  local copies, waits for them, and re-layouts  1.74 us (1%)
    ppermute x31, starting transfers between devices, swap(): return lax.ppermute(value, 'row', [(i, i ^ mask) for i in range(count)])  85.2 us
    ppermute x31, waiting for transfers between devices, swap(): return lax.ppermute(value, 'row', [(i, i ^ mask) for i in range(count)])  27 us
    pallas_call x1, Pallas kernels, local(): pl.pallas_call(pair_kernel, grid_spec=pltpu.PrefetchScalarGridSpec(num_sc...  20.1 us
    pallas_call x4, Pallas kernels, local(): pl.pallas_call(functools.partial(own_kernel, part), in_specs=[pl.BlockSpe...  18.3 us
    pallas_call x1, Pallas kernels, local(): pl.pallas_call(own_again_kernel, grid=(2,), in_specs=[pl.BlockSpec((ROWS...  4.06 us
  transfers between devices with their start and end apart: 31, of which 13 were waited for; matrix products, arithmetic and copies ran while one was open for 2% of the time, Pallas kernels for 14%

profile of v5, /device:TPU:0, one launch (start us, length us, event | category | flops | bytes accessed | tf_op | source)
XLA Modules:
  0.0 166.7 jit_solution(18203396843875032407)
XLA Ops:
  2.9 2.6 %collective-permute-start.8 = (bf16[80,1024]{1,0:T(8,128)(2,1)S(1)}, bf16[80,1024]{1,0:T(8,128)(2,1)S(1)}, u32[]{:S(2)}, u32[]{:S(2)}) collective-permute-start(bf16[80,1024]{1,0:T(8,128)(2,1)S(1)} %pad_maximum_fusion.pay_ref.arrived_ref.refs_4_), channel_id=1, source_target_pairs={{0,2},{1,3},{2,0},{3,1},{4,6},{5,7},{6,4},{7,5},{8,10},{9,11},{10,... | collective-permute-start | bytes 491528 | tf_op jit(solution)/shard_map/ppermute | solution.py:302
  5.5 3.6 %collective-permute-start.7 = (bf16[80,1024]{1,0:T(8,128)(2,1)S(1)}, bf16[80,1024]{1,0:T(8,128)(2,1)S(1)}, u32[]{:S(2)}, u32[]{:S(2)}) collective-permute-start(bf16[80,1024]{1,0:T(8,128)(2,1)S(1)} %pad_maximum_fusion.pay_ref.arrived_ref.refs_4_), channel_id=1, source_target_pairs={{0,12},{1,13},{2,14},{3,15},{4,8},{5,9},{6,10},{7,11},{8,4},{9,5},... | collective-permute-start | bytes 491528 | tf_op jit(solution)/shard_map/ppermute | solution.py:302
  9.9 2.0 %collective-permute-start.2 = (s32[1,5]{1,0:T(1,128)S(1)}, s32[1,5]{1,0:T(1,128)S(1)}, u32[]{:S(2)}, u32[]{:S(2)}) collective-permute-start(s32[1,5]{1,0:T(1,128)S(1)} %get-tuple-element.19), channel_id=1, source_target_pairs={{0,12},{1,13},{2,14},{3,15},{4,8},{5,9},{6,10},{7,11},{8,4},{9,5},... | collective-permute-start | bytes 68 | tf_op jit(solution)/shard_map/ppermute | solution.py:302
  11.9 4.6 %own_tile_0.1 = (bf16[512,2048]{1,0:T(8,128)(2,1)}, f32[8,2048]{1,0:T(8,128)S(1)}) custom-call(bf16[80,1024]{1,0:T(8,128)(2,1)S(1)} %pad_maximum_fusion.pay_ref.arrived_ref.refs_4_, bf16[128,2048]{1,0:T(8,128)(2,1)S(1)} %get-tuple-element.20.right_in_ref.right_ref, bf16[80,1024]{1,0:T(8,128)(2,1)S(1)} %pad_maximum_fusion.pay_ref.arrived_ref.refs_4_), custom_call_target="tpu_custom_call" | custom-call | flops 4000000000 | bytes 2097152 | tf_op jit(solution)/shard_map/own_tile_0/pallas_call | solution.py:396
  17.2 7.7 %collective-permute-start.1 = (s32[1,5]{1,0:T(1,128)S(1)}, s32[1,5]{1,0:T(1,128)S(1)}, u32[]{:S(2)}, u32[]{:S(2)}) collective-permute-start(s32[1,5]{1,0:T(1,128)S(1)} %get-tuple-element.19), channel_id=1, source_target_pairs={{0,8},{1,9},{2,10},{3,11},{4,12},{5,13},{6,14},{7,15},{8,0},{9,1},... | collective-permute-start | bytes 68 | tf_op jit(solution)/shard_map/ppermute | solution.py:302
  24.9 1.5 collective-permute-done.1
  26.4 1.9 %collective-permute-start = (s32[1,5]{1,0:T(1,128)S(1)}, s32[1,5]{1,0:T(1,128)S(1)}, u32[]{:S(2)}, u32[]{:S(2)}) collective-permute-start(s32[1,5]{1,0:T(1,128)S(1)} %get-tuple-element.19), channel_id=1, source_target_pairs={{0,4},{1,5},{2,6},{3,7},{4,0},{5,1},{6,2},{7,3},{8,12},{9,13},{10,... | collective-permute-start | bytes 68 | tf_op jit(solution)/shard_map/ppermute | solution.py:302
  28.3 1.6 collective-permute-done
  30.5 3.1 %collective-permute-done.3 = s32[4,5]{1,0:T(4,128)S(1)} collective-permute-done((s32[4,5]{1,0:T(4,128)S(1)}, s32[4,5]{1,0:T(4,128)S(1)}, u32[]{:S(2)}, u32[]{:S(2)}) %collective-permute-start.3) | collective-permute-done | bytes 112 | tf_op jit(solution)/shard_map/ppermute | solution.py:302
  34.9 1.9 %collective-permute-start.5 = (bf16[80,1024]{1,0:T(8,128)(2,1)S(1)}, bf16[80,1024]{1,0:T(8,128)(2,1)S(1)}, u32[]{:S(2)}, u32[]{:S(2)}) collective-permute-start(bf16[80,1024]{1,0:T(8,128)(2,1)S(1)} %pad_maximum_fusion.pay_ref.arrived_ref.refs_4_), channel_id=1, source_target_pairs={{0,4},{1,5},{2,6},{3,7},{4,0},{5,1},{6,2},{7,3},{8,12},{9,13},{10,... | collective-permute-start | bytes 491528 | tf_op jit(solution)/shard_map/ppermute | solution.py:302
  39.3 4.6 %own_tile_3.1 = (bf16[512,2048]{1,0:T(8,128)(2,1)}, f32[8,2048]{1,0:T(8,128)S(1)}) custom-call(bf16[80,1024]{1,0:T(8,128)(2,1)S(1)} %pad_maximum_fusion.pay_ref.arrived_ref.refs_4_, bf16[128,2048]{1,0:T(8,128)(2,1)S(1)} %get-tuple-element.20.right_in_ref.right_ref, bf16[80,1024]{1,0:T(8,128)(2,1)S(1)} %collective-permute-done.7.arrived_ref.refs_7_), custom_call_target="tpu_custom_call" | custom-call | flops 4000000000 | bytes 2097152 | tf_op jit(solution)/shard_map/own_tile_3/pallas_call | solution.py:396
  44.6 1.5 collective-permute-start.10
  46.7 4.6 %own_tile_2.1 = (bf16[512,2048]{1,0:T(8,128)(2,1)}, f32[8,2048]{1,0:T(8,128)S(1)}) custom-call(bf16[80,1024]{1,0:T(8,128)(2,1)S(1)} %pad_maximum_fusion.pay_ref.arrived_ref.refs_4_, bf16[128,2048]{1,0:T(8,128)(2,1)S(1)} %get-tuple-element.20.right_in_ref.right_ref, bf16[80,1024]{1,0:T(8,128)(2,1)S(1)} %collective-permute-done.6.arrived_ref.refs_6_), custom_call_target="tpu_custom_call" | custom-call | flops 4000000000 | bytes 2097152 | tf_op jit(solution)/shard_map/own_tile_2/pallas_call | solution.py:396
  51.9 2.6 %collective-permute-done.10.refs_10_ = bf16[80,1024]{1,0:T(8,128)(2,1)S(1)} collective-permute-done((bf16[80,1024]{1,0:T(8,128)(2,1)S(1)}, bf16[80,1024]{1,0:T(8,128)(2,1)S(1)}, u32[]{:S(2)}, u32[]{:S(2)}) %collective-permute-start.10) | collective-permute-done | bytes 163872 | tf_op jit(solution)/shard_map/ppermute | solution.py:302
  54.4 3.1 %collective-permute-done.9.refs_9_ = bf16[80,1024]{1,0:T(8,128)(2,1)S(1)} collective-permute-done((bf16[80,1024]{1,0:T(8,128)(2,1)S(1)}, bf16[80,1024]{1,0:T(8,128)(2,1)S(1)}, u32[]{:S(2)}, u32[]{:S(2)}) %collective-permute-start.9) | collective-permute-done | bytes 163872 | tf_op jit(solution)/shard_map/ppermute | solution.py:302
  57.5 4.5 %own_tile_1.1 = (bf16[512,2048]{1,0:T(8,128)(2,1)}, f32[8,2048]{1,0:T(8,128)S(1)}) custom-call(bf16[80,1024]{1,0:T(8,128)(2,1)S(1)} %pad_maximum_fusion.pay_ref.arrived_ref.refs_4_, bf16[128,2048]{1,0:T(8,128)(2,1)S(1)} %get-tuple-element.20.right_in_ref.right_ref, bf16[80,1024]{1,0:T(8,128)(2,1)S(1)} %collective-permute-done.5.arrived_ref.refs_5_), custom_call_target="tpu_custom_call" | custom-call | flops 4000000000 | bytes 2097152 | tf_op jit(solution)/shard_map/own_tile_1/pallas_call | solution.py:396
  62.1 20.1 %pair_tiles.1 = (bf16[3,2048,2048]{2,1,0:T(8,128)(2,1)S(1)}, bf16[2,2048,2048]{2,1,0:T(8,128)(2,1)}, f32[8,2048]{1,0:T(8,128)S(1)}, bf16[8,2176]{1,0:T(8,128)(2,1)S(1)}) custom-call(s32[6]{0:T(128)S(1)} %pad_add_fusion.1.slots_ref, bf16[128,2048]{1,0:T(8,128)(2,1)S(1)} %get-tuple-element.20.right_in_ref.right_ref, f32[8,2048]{1,0:T(8,128)S(1)} %copy-done, ...), custom_call_target="tpu_custom_call" | custom-call | tf_op jit(solution)/shard_map/pair_tiles/pallas_call | solution.py:425
  82.3 49.2 %collective-permute-start.22 = (bf16[1,8,2176]{2,1,0:T(8,128)(2,1)S(1)}, bf16[1,8,2176]{2,1,0:T(8,128)(2,1)S(1)}, u32[]{:S(2)}, u32[]{:S(2)}) collective-permute-start(bf16[1,8,2176]{2,1,0:T(8,128)(2,1)S(1)} %bitcast.8), channel_id=1, source_target_pairs={{0,12},{1,13},{2,14},{3,15},{4,8},{5,9},{6,10},{7,11},{8,4},{9,5},... | collective-permute-start | bytes 104456 | tf_op jit(solution)/shard_map/ppermute | solution.py:302
  133.4 2.9 %collective-permute-done.21 = bf16[1,8,2176]{2,1,0:T(8,128)(2,1)S(1)} collective-permute-done((bf16[1,8,2176]{2,1,0:T(8,128)(2,1)S(1)}, bf16[1,8,2176]{2,1,0:T(8,128)(2,1)S(1)}, u32[]{:S(2)}, u32[]{:S(2)}) %collective-permute-start.21) | collective-permute-done | bytes 34848 | tf_op jit(solution)/shard_map/ppermute | solution.py:302
  136.5 5.0 %collective-permute-done.23 = bf16[4,8,2176]{2,1,0:T(8,128)(2,1)S(1)} collective-permute-done((bf16[4,8,2176]{2,1,0:T(8,128)(2,1)S(1)}, bf16[4,8,2176]{2,1,0:T(8,128)(2,1)S(1)}, u32[]{:S(2)}, u32[]{:S(2)}) %collective-permute-start.23) | collective-permute-done | bytes 139296 | tf_op jit(solution)/shard_map/ppermute | solution.py:302
  141.6 4.1 %own_again.1.first_ref = f32[8,2048]{1,0:T(8,128)S(1)} custom-call(bf16[512,2048]{1,0:T(8,128)(2,1)} %get-tuple-element.28.refs_0_, bf16[512,2048]{1,0:T(8,128)(2,1)} %get-tuple-element.29.refs_1_, bf16[512,2048]{1,0:T(8,128)(2,1)} %get-tuple-element.30.refs_2_, bf16[512,2048]{1,0:T(8,128)(2,1)} %get-tuple-element.31.refs_3_, ...), custom_call_target="tpu_custom_call" | custom-call | tf_op jit(solution)/shard_map/own_again/pallas_call | solution.py:459
  145.7 3.3 %pair_again.1 = (f32[32,2048]{1,0:T(8,128)S(1)}, f32[8,128]{1,0:T(8,128)S(1)}, f32[8,128]{1,0:T(8,128)S(1)}) custom-call(s32[6]{0:T(128)S(1)} %pad_add_fusion.1.slots_ref, bf16[3,2048,2048]{2,1,0:T(8,128)(2,1)S(1)} %get-tuple-element.25.front_ref, bf16[2,2048,2048]{2,1,0:T(8,128)(2,1)} %get-tuple-element.26.back_ref, ...), custom_call_target="tpu_custom_call" | custom-call | tf_op jit(solution)/shard_map/pair_again/pallas_call | solution.py:470
  149.0 8.4 %collective-permute-start.27 = (f32[8,128]{1,0:T(8,128)S(1)}, f32[8,128]{1,0:T(8,128)S(1)}, u32[]{:S(2)}, u32[]{:S(2)}) collective-permute-start(f32[8,128]{1,0:T(8,128)S(1)} %get-tuple-element.35), channel_id=1, source_target_pairs={{0,12},{1,13},{2,14},{3,15},{4,8},{5,9},{6,10},{7,11},{8,4},{9,5},... | collective-permute-start | bytes 12296 | tf_op jit(solution)/shard_map/ppermute | solution.py:302
  159.0 2.9 %collective-permute-done.26 = f32[8,128]{1,0:T(8,128)S(1)} collective-permute-done((f32[8,128]{1,0:T(8,128)S(1)}, f32[8,128]{1,0:T(8,128)S(1)}, u32[]{:S(2)}, u32[]{:S(2)}) %collective-permute-start.26) | collective-permute-done | bytes 4128 | tf_op jit(solution)/shard_map/ppermute | solution.py:302
  (84 shorter events, 17.9 us)
Async XLA Ops:
  2.4 41.5 %collective-permute-start.12 = (bf16[80,1024]{1,0:T(8,128)(2,1)S(1)}, bf16[80,1024]{1,0:T(8,128)(2,1)S(1)}, u32[]{:S(2)}, u32[]{:S(2)}) collective-permute-start(bf16[80,1024]{1,0:T(8,128)(2,1)S(1)} %pad_maximum_fusion.pay_ref.arrived_ref.refs_4_), channel_id=1, source_target_pairs={{0,1},{1,0},{2,3},{3,2},{4,5},{5,4},{6,7},{7,6},{8,9},{9,8},{10,11... | collective-permute-start | bytes 491528 | tf_op jit(solution)/shard_map/ppermute | solution.py:302
  2.9 41.5 %collective-permute-start.8 = (bf16[80,1024]{1,0:T(8,128)(2,1)S(1)}, bf16[80,1024]{1,0:T(8,128)(2,1)S(1)}, u32[]{:S(2)}, u32[]{:S(2)}) collective-permute-start(bf16[80,1024]{1,0:T(8,128)(2,1)S(1)} %pad_maximum_fusion.pay_ref.arrived_ref.refs_4_), channel_id=1, source_target_pairs={{0,2},{1,3},{2,0},{3,1},{4,6},{5,7},{6,4},{7,5},{8,10},{9,11},{10,... | collective-permute-start | bytes 491528 | tf_op jit(solution)/shard_map/ppermute | solution.py:302
  5.5 33.7 %collective-permute-start.7 = (bf16[80,1024]{1,0:T(8,128)(2,1)S(1)}, bf16[80,1024]{1,0:T(8,128)(2,1)S(1)}, u32[]{:S(2)}, u32[]{:S(2)}) collective-permute-start(bf16[80,1024]{1,0:T(8,128)(2,1)S(1)} %pad_maximum_fusion.pay_ref.arrived_ref.refs_4_), channel_id=1, source_target_pairs={{0,12},{1,13},{2,14},{3,15},{4,8},{5,9},{6,10},{7,11},{8,4},{9,5},... | collective-permute-start | bytes 491528 | tf_op jit(solution)/shard_map/ppermute | solution.py:302
  9.1 35.5 %collective-permute-start.6 = (bf16[80,1024]{1,0:T(8,128)(2,1)S(1)}, bf16[80,1024]{1,0:T(8,128)(2,1)S(1)}, u32[]{:S(2)}, u32[]{:S(2)}) collective-permute-start(bf16[80,1024]{1,0:T(8,128)(2,1)S(1)} %pad_maximum_fusion.pay_ref.arrived_ref.refs_4_), channel_id=1, source_target_pairs={{0,8},{1,9},{2,10},{3,11},{4,12},{5,13},{6,14},{7,15},{8,0},{9,1},... | collective-permute-start | bytes 491528 | tf_op jit(solution)/shard_map/ppermute | solution.py:302
  9.9 7.3 %collective-permute-start.2 = (s32[1,5]{1,0:T(1,128)S(1)}, s32[1,5]{1,0:T(1,128)S(1)}, u32[]{:S(2)}, u32[]{:S(2)}) collective-permute-start(s32[1,5]{1,0:T(1,128)S(1)} %get-tuple-element.19), channel_id=1, source_target_pairs={{0,12},{1,13},{2,14},{3,15},{4,8},{5,9},{6,10},{7,11},{8,4},{9,5},... | collective-permute-start | bytes 68 | tf_op jit(solution)/shard_map/ppermute | solution.py:302
  17.2 9.2 %collective-permute-start.1 = (s32[1,5]{1,0:T(1,128)S(1)}, s32[1,5]{1,0:T(1,128)S(1)}, u32[]{:S(2)}, u32[]{:S(2)}) collective-permute-start(s32[1,5]{1,0:T(1,128)S(1)} %get-tuple-element.19), channel_id=1, source_target_pairs={{0,8},{1,9},{2,10},{3,11},{4,12},{5,13},{6,14},{7,15},{8,0},{9,1},... | collective-permute-start | bytes 68 | tf_op jit(solution)/shard_map/ppermute | solution.py:302
  34.9 11.3 %collective-permute-start.5 = (bf16[80,1024]{1,0:T(8,128)(2,1)S(1)}, bf16[80,1024]{1,0:T(8,128)(2,1)S(1)}, u32[]{:S(2)}, u32[]{:S(2)}) collective-permute-start(bf16[80,1024]{1,0:T(8,128)(2,1)S(1)} %pad_maximum_fusion.pay_ref.arrived_ref.refs_4_), channel_id=1, source_target_pairs={{0,4},{1,5},{2,6},{3,7},{4,0},{5,1},{6,2},{7,3},{8,12},{9,13},{10,... | collective-permute-start | bytes 491528 | tf_op jit(solution)/shard_map/ppermute | solution.py:302
  39.2 12.0 %collective-permute-start.15 = (bf16[80,1024]{1,0:T(8,128)(2,1)S(1)}, bf16[80,1024]{1,0:T(8,128)(2,1)S(1)}, u32[]{:S(2)}, u32[]{:S(2)}) collective-permute-start(bf16[80,1024]{1,0:T(8,128)(2,1)S(1)} %collective-permute-done.7.arrived_ref.refs_7_), channel_id=1, source_target_pairs={{0,1},{1,0},{2,3},{3,2},{4,5},{5,4},{6,7},{7,6},{8,9},{9,8},{10,11... | collective-permute-start | bytes 491528 | tf_op jit(solution)/shard_map/ppermute | solution.py:302
  43.9 7.9 %collective-permute-start.11 = (bf16[80,1024]{1,0:T(8,128)(2,1)S(1)}, bf16[80,1024]{1,0:T(8,128)(2,1)S(1)}, u32[]{:S(2)}, u32[]{:S(2)}) collective-permute-start(bf16[80,1024]{1,0:T(8,128)(2,1)S(1)} %collective-permute-done.7.arrived_ref.refs_7_), channel_id=1, source_target_pairs={{0,2},{1,3},{2,0},{3,1},{4,6},{5,7},{6,4},{7,5},{8,10},{9,11},{10,... | collective-permute-start | bytes 491528 | tf_op jit(solution)/shard_map/ppermute | solution.py:302
  44.4 6.8 %collective-permute-start.16 = (bf16[80,1024]{1,0:T(8,128)(2,1)S(1)}, bf16[80,1024]{1,0:T(8,128)(2,1)S(1)}, u32[]{:S(2)}, u32[]{:S(2)}) collective-permute-start(bf16[80,1024]{1,0:T(8,128)(2,1)S(1)} %collective-permute-done.8.refs_8_), channel_id=1, source_target_pairs={{0,1},{1,0},{2,3},{3,2},{4,5},{5,4},{6,7},{7,6},{8,9},{9,8},{10,11... | collective-permute-start | bytes 491528 | tf_op jit(solution)/shard_map/ppermute | solution.py:302
  44.6 9.8 %collective-permute-start.10 = (bf16[80,1024]{1,0:T(8,128)(2,1)S(1)}, bf16[80,1024]{1,0:T(8,128)(2,1)S(1)}, u32[]{:S(2)}, u32[]{:S(2)}) collective-permute-start(bf16[80,1024]{1,0:T(8,128)(2,1)S(1)} %collective-permute-done.6.arrived_ref.refs_6_), channel_id=1, source_target_pairs={{0,2},{1,3},{2,0},{3,1},{4,6},{5,7},{6,4},{7,5},{8,10},{9,11},{10,... | collective-permute-start | bytes 491528 | tf_op jit(solution)/shard_map/ppermute | solution.py:302
  46.2 11.4 %collective-permute-start.9 = (bf16[80,1024]{1,0:T(8,128)(2,1)S(1)}, bf16[80,1024]{1,0:T(8,128)(2,1)S(1)}, u32[]{:S(2)}, u32[]{:S(2)}) collective-permute-start(bf16[80,1024]{1,0:T(8,128)(2,1)S(1)} %collective-permute-done.5.arrived_ref.refs_5_), channel_id=1, source_target_pairs={{0,2},{1,3},{2,0},{3,1},{4,6},{5,7},{6,4},{7,5},{8,10},{9,11},{10,... | collective-permute-start | bytes 491528 | tf_op jit(solution)/shard_map/ppermute | solution.py:302
  51.3 10.8 %collective-permute-start.14 = (bf16[80,1024]{1,0:T(8,128)(2,1)S(1)}, bf16[80,1024]{1,0:T(8,128)(2,1)S(1)}, u32[]{:S(2)}, u32[]{:S(2)}) collective-permute-start(bf16[80,1024]{1,0:T(8,128)(2,1)S(1)} %collective-permute-done.6.arrived_ref.refs_6_), channel_id=1, source_target_pairs={{0,1},{1,0},{2,3},{3,2},{4,5},{5,4},{6,7},{7,6},{8,9},{9,8},{10,11... | collective-permute-start | bytes 491528 | tf_op jit(solution)/shard_map/ppermute | solution.py:302
  51.3 10.8 %collective-permute-start.13 = (bf16[80,1024]{1,0:T(8,128)(2,1)S(1)}, bf16[80,1024]{1,0:T(8,128)(2,1)S(1)}, u32[]{:S(2)}, u32[]{:S(2)}) collective-permute-start(bf16[80,1024]{1,0:T(8,128)(2,1)S(1)} %collective-permute-done.5.arrived_ref.refs_5_), channel_id=1, source_target_pairs={{0,1},{1,0},{2,3},{3,2},{4,5},{5,4},{6,7},{7,6},{8,9},{9,8},{10,11... | collective-permute-start | bytes 491528 | tf_op jit(solution)/shard_map/ppermute | solution.py:302
  51.8 10.3 %collective-permute-start.19 = (bf16[80,1024]{1,0:T(8,128)(2,1)S(1)}, bf16[80,1024]{1,0:T(8,128)(2,1)S(1)}, u32[]{:S(2)}, u32[]{:S(2)}) collective-permute-start(bf16[80,1024]{1,0:T(8,128)(2,1)S(1)} %collective-permute-done.11.refs_11_), channel_id=1, source_target_pairs={{0,1},{1,0},{2,3},{3,2},{4,5},{5,4},{6,7},{7,6},{8,9},{9,8},{10,11... | collective-permute-start | bytes 491528 | tf_op jit(solution)/shard_map/ppermute | solution.py:302
  54.4 7.7 %collective-permute-start.18 = (bf16[80,1024]{1,0:T(8,128)(2,1)S(1)}, bf16[80,1024]{1,0:T(8,128)(2,1)S(1)}, u32[]{:S(2)}, u32[]{:S(2)}) collective-permute-start(bf16[80,1024]{1,0:T(8,128)(2,1)S(1)} %collective-permute-done.10.refs_10_), channel_id=1, source_target_pairs={{0,1},{1,0},{2,3},{3,2},{4,5},{5,4},{6,7},{7,6},{8,9},{9,8},{10,11... | collective-permute-start | bytes 491528 | tf_op jit(solution)/shard_map/ppermute | solution.py:302
  57.5 4.6 %collective-permute-start.17 = (bf16[80,1024]{1,0:T(8,128)(2,1)S(1)}, bf16[80,1024]{1,0:T(8,128)(2,1)S(1)}, u32[]{:S(2)}, u32[]{:S(2)}) collective-permute-start(bf16[80,1024]{1,0:T(8,128)(2,1)S(1)} %collective-permute-done.9.refs_9_), channel_id=1, source_target_pairs={{0,1},{1,0},{2,3},{3,2},{4,5},{5,4},{6,7},{7,6},{8,9},{9,8},{10,11... | collective-permute-start | bytes 491528 | tf_op jit(solution)/shard_map/ppermute | solution.py:302
  82.3 51.2 %collective-permute-start.22 = (bf16[1,8,2176]{2,1,0:T(8,128)(2,1)S(1)}, bf16[1,8,2176]{2,1,0:T(8,128)(2,1)S(1)}, u32[]{:S(2)}, u32[]{:S(2)}) collective-permute-start(bf16[1,8,2176]{2,1,0:T(8,128)(2,1)S(1)} %bitcast.8), channel_id=1, source_target_pairs={{0,12},{1,13},{2,14},{3,15},{4,8},{5,9},{6,10},{7,11},{8,4},{9,5},... | collective-permute-start | bytes 104456 | tf_op jit(solution)/shard_map/ppermute | solution.py:302
  131.5 4.8 %collective-permute-start.21 = (bf16[1,8,2176]{2,1,0:T(8,128)(2,1)S(1)}, bf16[1,8,2176]{2,1,0:T(8,128)(2,1)S(1)}, u32[]{:S(2)}, u32[]{:S(2)}) collective-permute-start(bf16[1,8,2176]{2,1,0:T(8,128)(2,1)S(1)} %bitcast.9), channel_id=1, source_target_pairs={{0,8},{1,9},{2,10},{3,11},{4,12},{5,13},{6,14},{7,15},{8,0},{9,1},... | collective-permute-start | bytes 104456 | tf_op jit(solution)/shard_map/ppermute | solution.py:302
  131.5 4.8 %collective-permute-start.20 = (bf16[1,8,2176]{2,1,0:T(8,128)(2,1)S(1)}, bf16[1,8,2176]{2,1,0:T(8,128)(2,1)S(1)}, u32[]{:S(2)}, u32[]{:S(2)}) collective-permute-start(bf16[1,8,2176]{2,1,0:T(8,128)(2,1)S(1)} %bitcast.10), channel_id=1, source_target_pairs={{0,4},{1,5},{2,6},{3,7},{4,0},{5,1},{6,2},{7,3},{8,12},{9,13},{10,... | collective-permute-start | bytes 104456 | tf_op jit(solution)/shard_map/ppermute | solution.py:302
  136.4 5.1 %collective-permute-start.23 = (bf16[4,8,2176]{2,1,0:T(8,128)(2,1)S(1)}, bf16[4,8,2176]{2,1,0:T(8,128)(2,1)S(1)}, u32[]{:S(2)}, u32[]{:S(2)}) collective-permute-start(bf16[4,8,2176]{2,1,0:T(8,128)(2,1)S(1)} %pad_maximum_fusion.1), channel_id=1, source_target_pairs={{0,2},{1,3},{2,0},{3,1},{4,6},{5,7},{6,4},{7,5},{8,10},{9,11},{10,... | collective-permute-start | bytes 417800 | tf_op jit(solution)/shard_map/ppermute | solution.py:302
  141.5 4.1 %collective-permute-start.24 = (bf16[8,8,2176]{2,1,0:T(8,128)(2,1)S(1)}, bf16[8,8,2176]{2,1,0:T(8,128)(2,1)S(1)}, u32[]{:S(2)}, u32[]{:S(2)}) collective-permute-start(bf16[8,8,2176]{2,1,0:T(8,128)(2,1)S(1)} %get-tuple-element.43), channel_id=1, source_target_pairs={{0,1},{1,0},{2,3},{3,2},{4,5},{5,4},{6,7},{7,6},{8,9},{9,8},{10,11... | collective-permute-start | bytes 835592 | tf_op jit(solution)/shard_map/ppermute | solution.py:302
  149.0 10.0 %collective-permute-start.27 = (f32[8,128]{1,0:T(8,128)S(1)}, f32[8,128]{1,0:T(8,128)S(1)}, u32[]{:S(2)}, u32[]{:S(2)}) collective-permute-start(f32[8,128]{1,0:T(8,128)S(1)} %get-tuple-element.35), channel_id=1, source_target_pairs={{0,12},{1,13},{2,14},{3,15},{4,8},{5,9},{6,10},{7,11},{8,4},{9,5},... | collective-permute-start | bytes 12296 | tf_op jit(solution)/shard_map/ppermute | solution.py:302
  157.4 4.5 %collective-permute-start.26 = (f32[8,128]{1,0:T(8,128)S(1)}, f32[8,128]{1,0:T(8,128)S(1)}, u32[]{:S(2)}, u32[]{:S(2)}) collective-permute-start(f32[8,128]{1,0:T(8,128)S(1)} %get-tuple-element.35), channel_id=1, source_target_pairs={{0,8},{1,9},{2,10},{3,11},{4,12},{5,13},{6,14},{7,15},{8,0},{9,1},... | collective-permute-start | bytes 12296 | tf_op jit(solution)/shard_map/ppermute | solution.py:302
  (12 other events, 107.1 us)

commit v6 on v5

--- a/solution.py
+++ b/solution.py
@@ -15,7 +15,7 @@
 KDIM = 128
 ROWS = 512
 PARTS = 4
-UNIT = 256
+COLS = 512
 FRONT = 3
 HELD = 4
 TAIL = 128
@@ -52,17 +52,6 @@
     return jnp.transpose(jnp.concatenate([feat, feat, feat, norm_rows(norm, 3)], axis=0))
 
 
-def psi_chain(dist):
-    dist = jnp.maximum(dist, 1e-30)
-    radius = dist * lax.rsqrt(dist)
-    u = jnp.maximum(SHRINK - radius, 0.0)
-    two = u * u
-    four = two * two
-    eight = four * four
-    sixteen = eight * eight
-    return (sixteen * two * (u - two)).astype(BF16)
-
-
 def psi_power(dist):
     dist = jnp.maximum(dist, 1e-30)
     radius = dist * lax.rsqrt(dist)
@@ -70,47 +59,25 @@
     return (jnp.exp2(19.0 * lax.log2(u)) * (1.0 - u)).astype(BF16)
 
 
-def tile_rows(left_ref, right_ref, vec_ref, begin, tile_ref, sum_ref, dist_refs, psi, rows_at_once):
-    width = right_ref.shape[1]
-    units = width // UNIT
-
-    def gram(row, unit, dist_ref):
-        col = unit * UNIT
-        dist_ref[...] = jnp.dot(
-            left_ref[pl.ds(pl.multiple_of(row, UNIT), UNIT), :],
-            right_ref[:, col : col + UNIT],
-            preferred_element_type=F32,
+def tile_rows(left_ref, right_ref, vec_ref, begin, tile_ref, sum_ref, rows_at_once):
+    at = pl.multiple_of(begin, ROWS)
+    left = left_ref[pl.ds(at, ROWS), :]
+    vec = vec_ref[:, pl.ds(at, ROWS)]
+
+    def step(index, carry):
+        cols = pl.ds(pl.multiple_of(index * COLS, COLS), COLS)
+        dist = jnp.dot(left, right_ref[:, cols], preferred_element_type=F32)
+        parts = []
+        for sub in range(0, ROWS, rows_at_once):
+            part = psi_power(dist[sub : sub + rows_at_once])
+            tile_ref[sub : sub + rows_at_once, cols] = part
+            parts.append(part)
+        sum_ref[:, cols] += jnp.dot(
+            vec, jnp.concatenate(parts, axis=0), preferred_element_type=F32
         )
-
-    def product(vec, at, unit):
-        col = unit * UNIT
-        sum_ref[:, col : col + UNIT] += jnp.dot(
-            vec, tile_ref[pl.ds(at, UNIT), col : col + UNIT], preferred_element_type=F32
-        )
-
-    gram(begin, 0, dist_refs[0])
-
-    def step(index, carry):
-        at = pl.multiple_of(index * UNIT, UNIT)
-        row = begin + at
-        following = begin + jnp.minimum(at + UNIT, ROWS - UNIT)
-        vec = vec_ref[:, pl.ds(pl.multiple_of(row, UNIT), UNIT)]
-        for unit in range(units):
-            if unit + 1 < units:
-                gram(row, unit + 1, dist_refs[(unit + 1) % 2])
-            else:
-                gram(following, 0, dist_refs[(unit + 1) % 2])
-            col = unit * UNIT
-            for sub in range(0, UNIT, rows_at_once):
-                tile_ref[pl.ds(at + sub, rows_at_once), col : col + UNIT] = psi(
-                    dist_refs[unit % 2][sub : sub + rows_at_once, :]
-                )
-            if unit:
-                product(vec, at, unit - 1)
-        product(vec, at, units - 1)
         return carry
 
-    lax.fori_loop(0, ROWS // UNIT, step, 0)
+    lax.fori_loop(0, right_ref.shape[1] // COLS, step, 0)
 
 
 def unpack(pay):
@@ -118,25 +85,24 @@
     return jnp.concatenate([pay[:32], pay[32:64]], axis=1), jnp.concatenate([pay[64:72], pay[72:80]], axis=1)
 
 
-def own_kernel(part, pay_ref, right_in_ref, arrived_ref, tile_ref, sum_ref, left_ref, vec_ref, *dist_refs):
+def own_kernel(part, pay_ref, right_ref, arrived_ref, tile_ref, sum_ref, left_ref, vec_ref):
     feat, vec = unpack(pay_ref[...])
     begin = part * ROWS
     left_ref[...] = other_factor(feat[:, begin : begin + ROWS])
     vec_ref[...] = vec[:, begin : begin + ROWS]
     sum_ref[...] = jnp.zeros_like(sum_ref)
-    tile_rows(left_ref, right_in_ref, vec_ref, 0, tile_ref, sum_ref, dist_refs, psi_chain, 16)
-
-
-def factor_kernel(pay_ref, list_ref, right_ref, list_out_ref):
+    tile_rows(left_ref, right_ref, vec_ref, 0, tile_ref, sum_ref, 128)
+
+
+def factor_kernel(pay_ref, right_ref):
     right_ref[...] = own_factor(unpack(pay_ref[...])[0])
-    list_out_ref[...] = list_ref[...]
 
 
 def pair_kernel(slots_ref, right_ref, rhs_ref, var_ref, *refs):
     first_refs = refs[:PARTS]
-    block_refs = refs[PARTS:-10]
-    front_ref, back_ref, image_ref, send_ref = refs[-10:-6]
-    left_ref, vec_ref, dist_zero_ref, dist_one_ref, pay_ref, sem_ref = refs[-6:]
+    block_refs = refs[PARTS:-8]
+    front_ref, back_ref, image_ref, send_ref = refs[-8:-4]
+    left_ref, vec_ref, pay_ref, sem_ref = refs[-4:]
     slot, step = pl.program_id(0), pl.program_id(1)
     sum_ref = image_ref
 
@@ -177,8 +143,7 @@
             @pl.when(here)
             def _():
                 tile_rows(
-                    left_ref, right_ref, vec_ref, step * ROWS, tile_ref.at[0], sum_ref,
-                    (dist_zero_ref, dist_one_ref), psi_power, 64,
+                    left_ref, right_ref, vec_ref, step * ROWS, tile_ref.at[0], sum_ref, 64
                 )
 
     @pl.when((slot == pl.num_programs(0) - 1) & (step == pl.num_programs(1) - 1))
@@ -381,17 +346,16 @@
         [features[:, :half], features[:, half:], rounded[:, :half], rounded[:, half:]], axis=0
     )
     every = pass_on(payload, count)
-    dist_scratch = [pltpu.VMEM((UNIT, UNIT), F32)] * 2
     whole = lambda *ignored: (0, 0)
     row_spec = pl.BlockSpec(right_side.shape, whole)
     var_spec = pl.BlockSpec(var_row.shape, whole)
-    right, coupled = pl.pallas_call(
+    right = pl.pallas_call(
         factor_kernel,
-        out_shape=[shape((KDIM, width), BF16), shape((1, most), jnp.int32)],
+        out_shape=shape((KDIM, width), BF16),
         compiler_params=params,
         name="own_factor",
-    )(payload, tile_list[:, :, 1])
-    slots = partners(coupled, count)
+    )(payload)
+    slots = partners(tile_list[:, :, 1], count)
     own_parts = [
         pl.pallas_call(
             functools.partial(own_kernel, part),
@@ -401,14 +365,13 @@
                 pl.BlockSpec(memory_space=pl.ANY),
             ],
             out_shape=[pltpu.HBM((ROWS, width), BF16), shape(right_side.shape, F32)],
-            scratch_shapes=[pltpu.VMEM((ROWS, KDIM), BF16), pltpu.VMEM((rhs_count, ROWS), BF16)]
-            + dist_scratch,
+            scratch_shapes=[pltpu.VMEM((ROWS, KDIM), BF16), pltpu.VMEM((rhs_count, ROWS), BF16)],
             compiler_params=params,
             cost_estimate=pl.CostEstimate(
                 flops=4_000_000_000, bytes_accessed=2 * ROWS * width, transcendentals=0
             ),
             name=f"own_tile_{part}",
-        )(payload, right, every[part])
+        )(payload, right, every[part or PARTS])
         for part in range(PARTS)
     ]
     own_tiles = [part[0] for part in own_parts]
@@ -440,7 +403,6 @@
                 pl.BlockSpec(send_shape, whole),
             ],
             scratch_shapes=[pltpu.VMEM((width, KDIM), BF16), pltpu.VMEM((rhs_count, width), BF16)]
-            + dist_scratch
             + [pltpu.VMEM((2,) + payload.shape, BF16), pltpu.SemaphoreType.DMA((2,))],
         ),
         out_shape=[

time: 167 us -> 148 us (0.89)
  starting transfers between devices: 85.2 us -> 37.7 us
  Pallas kernels: 47.4 us -> 82.8 us
  waiting for transfers between devices: 27 us -> 18.6 us
    ppermute x31, starting transfers between devices: 85.2 us -> 37.7 us  [swap(): return lax.ppermute(value, 'row', [(i, i ^ mask) for i in range(count)])]
    pallas_call x1, Pallas kernels: 20.1 us -> 52.9 us  [local(): pl.pallas_call(pair_kernel, grid_spec=pltpu.PrefetchScalarGridSpec(num_sc...]
    ppermute x31, waiting for transfers between devices: 27 us -> 18.6 us  [swap(): return lax.ppermute(value, 'row', [(i, i ^ mask) for i in range(count)])]
    pallas_call x1, Pallas kernels: 3.29 us -> 7.36 us  [local(): pl.pallas_call(again_kernel, grid_spec=pltpu.PrefetchScalarGridSpec(num_s...]
  transfers between devices with their start and end apart: 31 -> 31, of which waited for: 13 -> 10; matrix products, arithmetic and copies ran while one was open for 2% -> 3% of each run, Pallas kernels for 14% -> 15%
where the time goes in v6:
time: 148 us; the launch traced here: 147 us
  Pallas kernels  82.8 us (56%)
  starting transfers between devices  37.7 us (25%)
  waiting for transfers between devices  18.6 us (13%)
  other arithmetic  5.1 us (3%)
  local copies, waits for them, and re-layouts  1.73 us (1%)
  between operations  1.49 us (1%)
    pallas_call x1, Pallas kernels, local(): pl.pallas_call(pair_kernel, grid_spec=pltpu.PrefetchScalarGridSpec(num_sc...  52.9 us
    ppermute x31, starting transfers between devices, swap(): return lax.ppermute(value, 'row', [(i, i ^ mask) for i in range(count)])  37.7 us
    ppermute x31, waiting for transfers between devices, swap(): return lax.ppermute(value, 'row', [(i, i ^ mask) for i in range(count)])  18.6 us
    pallas_call x4, Pallas kernels, local(): pl.pallas_call(functools.partial(own_kernel, part), in_specs=[pl.BlockSpe...  16.8 us
    pallas_call x1, Pallas kernels, local(): pl.pallas_call(again_kernel, grid_spec=pltpu.PrefetchScalarGridSpec(num_s...  7.36 us
    pallas_call x1, Pallas kernels, local(): pl.pallas_call(own_again_kernel, grid=(2,), in_specs=[pl.BlockSpec((ROWS...  4.06 us
  transfers between devices with their start and end apart: 31, of which 10 were waited for; matrix products, arithmetic and copies ran while one was open for 3% of the time, Pallas kernels for 15%

profile of v6, /device:TPU:0, one launch (start us, length us, event | category | flops | bytes accessed | tf_op | source)
XLA Modules:
  0.0 147.4 jit_solution(4661627523909957402)
XLA Ops:
  1.3 5.0 %collective-permute-start.2 = (s32[1,5]{1,0:T(1,128)S(1)}, s32[1,5]{1,0:T(1,128)S(1)}, u32[]{:S(2)}, u32[]{:S(2)}) collective-permute-start(s32[1,5]{1,0:T(1,128)S(1)} %get-tuple-element.54), channel_id=1, source_target_pairs={{0,12},{1,13},{2,14},{3,15},{4,8},{5,9},{6,10},{7,11},{8,4},{9,5},... | collective-permute-start | bytes 68 | tf_op jit(solution)/shard_map/ppermute | solution.py:267
  8.8 3.9 %collective-permute-start.8 = (bf16[80,1024]{1,0:T(8,128)(2,1)S(1)}, bf16[80,1024]{1,0:T(8,128)(2,1)S(1)}, u32[]{:S(2)}, u32[]{:S(2)}) collective-permute-start(bf16[80,1024]{1,0:T(8,128)(2,1)S(1)} %pad_maximum_fusion.pay_ref.refs_4_), channel_id=1, source_target_pairs={{0,12},{1,13},{2,14},{3,15},{4,8},{5,9},{6,10},{7,11},{8,4},{9,5},... | collective-permute-start | bytes 491528 | tf_op jit(solution)/shard_map/ppermute | solution.py:267
  13.3 1.7 %collective-permute-start.3 = (s32[4,5]{1,0:T(4,128)S(1)}, s32[4,5]{1,0:T(4,128)S(1)}, u32[]{:S(2)}, u32[]{:S(2)}) collective-permute-start(s32[4,5]{1,0:T(4,128)S(1)} %pad_add_fusion), channel_id=1, source_target_pairs={{0,2},{1,3},{2,0},{3,1},{4,6},{5,7},{6,4},{7,5},{8,10},{9,11},{10,... | collective-permute-start | bytes 248 | tf_op jit(solution)/shard_map/ppermute | solution.py:267
  15.7 1.3 collective-permute-done.3
  18.2 1.7 %collective-permute-start.5 = (bf16[80,1024]{1,0:T(8,128)(2,1)S(1)}, bf16[80,1024]{1,0:T(8,128)(2,1)S(1)}, u32[]{:S(2)}, u32[]{:S(2)}) collective-permute-start(bf16[80,1024]{1,0:T(8,128)(2,1)S(1)} %pad_maximum_fusion.pay_ref.refs_4_), channel_id=1, source_target_pairs={{0,2},{1,3},{2,0},{3,1},{4,6},{5,7},{6,4},{7,5},{8,10},{9,11},{10,... | collective-permute-start | bytes 491528 | tf_op jit(solution)/shard_map/ppermute | solution.py:267
  23.1 4.2 %own_tile_3.1 = (bf16[512,2048]{1,0:T(8,128)(2,1)}, f32[8,2048]{1,0:T(8,128)S(1)}) custom-call(bf16[80,1024]{1,0:T(8,128)(2,1)S(1)} %pad_maximum_fusion.pay_ref.refs_4_, bf16[128,2048]{1,0:T(8,128)(2,1)S(1)} %own_factor.1.right_ref, bf16[80,1024]{1,0:T(8,128)(2,1)S(1)} %collective-permute-done.8.arrived_ref.refs_7_), custom_call_target="tpu_custom_call" | custom-call | flops 4000000000 | bytes 2097152 | tf_op jit(solution)/shard_map/own_tile_3/pallas_call | solution.py:360
  27.3 1.0 collective-permute-start.11
  28.3 4.2 %own_tile_2.1 = (bf16[512,2048]{1,0:T(8,128)(2,1)}, f32[8,2048]{1,0:T(8,128)S(1)}) custom-call(bf16[80,1024]{1,0:T(8,128)(2,1)S(1)} %pad_maximum_fusion.pay_ref.refs_4_, bf16[128,2048]{1,0:T(8,128)(2,1)S(1)} %own_factor.1.right_ref, bf16[80,1024]{1,0:T(8,128)(2,1)S(1)} %collective-permute-done.7.arrived_ref.refs_6_), custom_call_target="tpu_custom_call" | custom-call | flops 4000000000 | bytes 2097152 | tf_op jit(solution)/shard_map/own_tile_2/pallas_call | solution.py:360
  32.5 1.2 collective-permute-start.10
  34.6 4.2 %own_tile_1.1 = (bf16[512,2048]{1,0:T(8,128)(2,1)}, f32[8,2048]{1,0:T(8,128)S(1)}) custom-call(bf16[80,1024]{1,0:T(8,128)(2,1)S(1)} %pad_maximum_fusion.pay_ref.refs_4_, bf16[128,2048]{1,0:T(8,128)(2,1)S(1)} %own_factor.1.right_ref, bf16[80,1024]{1,0:T(8,128)(2,1)S(1)} %collective-permute-done.6.arrived_ref.refs_5_), custom_call_target="tpu_custom_call" | custom-call | flops 4000000000 | bytes 2097152 | tf_op jit(solution)/shard_map/own_tile_1/pallas_call | solution.py:360
  39.8 2.8 %collective-permute-done.9.refs_9_ = bf16[80,1024]{1,0:T(8,128)(2,1)S(1)} collective-permute-done((bf16[80,1024]{1,0:T(8,128)(2,1)S(1)}, bf16[80,1024]{1,0:T(8,128)(2,1)S(1)}, u32[]{:S(2)}, u32[]{:S(2)}) %collective-permute-start.9) | collective-permute-done | bytes 163872 | tf_op jit(solution)/shard_map/ppermute | solution.py:267
  42.7 4.2 %own_tile_0.1 = (bf16[512,2048]{1,0:T(8,128)(2,1)}, f32[8,2048]{1,0:T(8,128)S(1)}) custom-call(bf16[80,1024]{1,0:T(8,128)(2,1)S(1)} %pad_maximum_fusion.pay_ref.refs_4_, bf16[128,2048]{1,0:T(8,128)(2,1)S(1)} %own_factor.1.right_ref, bf16[80,1024]{1,0:T(8,128)(2,1)S(1)} %collective-permute-done.5.arrived_ref.refs_8_), custom_call_target="tpu_custom_call" | custom-call | flops 4000000000 | bytes 2097152 | tf_op jit(solution)/shard_map/own_tile_0/pallas_call | solution.py:360
  46.9 52.9 %pair_tiles.1 = (bf16[3,2048,2048]{2,1,0:T(8,128)(2,1)S(1)}, bf16[2,2048,2048]{2,1,0:T(8,128)(2,1)}, f32[8,2048]{1,0:T(8,128)S(1)}, bf16[8,2176]{1,0:T(8,128)(2,1)S(1)}) custom-call(s32[6]{0:T(128)S(1)} %pad_add_fusion.1.slots_ref, bf16[128,2048]{1,0:T(8,128)(2,1)S(1)} %own_factor.1.right_ref, f32[8,2048]{1,0:T(8,128)S(1)} %copy-done, ...), custom_call_target="tpu_custom_call" | custom-call | tf_op jit(solution)/shard_map/pair_tiles/pallas_call | solution.py:388
  99.9 12.4 %collective-permute-start.22 = (bf16[1,8,2176]{2,1,0:T(8,128)(2,1)S(1)}, bf16[1,8,2176]{2,1,0:T(8,128)(2,1)S(1)}, u32[]{:S(2)}, u32[]{:S(2)}) collective-permute-start(bf16[1,8,2176]{2,1,0:T(8,128)(2,1)S(1)} %bitcast.9), channel_id=1, source_target_pairs={{0,12},{1,13},{2,14},{3,15},{4,8},{5,9},{6,10},{7,11},{8,4},{9,5},... | collective-permute-start | bytes 104456 | tf_op jit(solution)/shard_map/ppermute | solution.py:267
  112.9 1.5 %collective-permute-done.22 = bf16[1,8,2176]{2,1,0:T(8,128)(2,1)S(1)} collective-permute-done((bf16[1,8,2176]{2,1,0:T(8,128)(2,1)S(1)}, bf16[1,8,2176]{2,1,0:T(8,128)(2,1)S(1)}, u32[]{:S(2)}, u32[]{:S(2)}) %collective-permute-start.22) | collective-permute-done | bytes 34848 | tf_op jit(solution)/shard_map/ppermute | solution.py:267
  114.4 2.7 %collective-permute-done.21 = bf16[1,8,2176]{2,1,0:T(8,128)(2,1)S(1)} collective-permute-done((bf16[1,8,2176]{2,1,0:T(8,128)(2,1)S(1)}, bf16[1,8,2176]{2,1,0:T(8,128)(2,1)S(1)}, u32[]{:S(2)}, u32[]{:S(2)}) %collective-permute-start.21) | collective-permute-done | bytes 34848 | tf_op jit(solution)/shard_map/ppermute | solution.py:267
  117.3 5.0 %collective-permute-done.23 = bf16[4,8,2176]{2,1,0:T(8,128)(2,1)S(1)} collective-permute-done((bf16[4,8,2176]{2,1,0:T(8,128)(2,1)S(1)}, bf16[4,8,2176]{2,1,0:T(8,128)(2,1)S(1)}, u32[]{:S(2)}, u32[]{:S(2)}) %collective-permute-start.23) | collective-permute-done | bytes 139296 | tf_op jit(solution)/shard_map/ppermute | solution.py:267
  122.3 4.1 %own_again.1.first_ref = f32[8,2048]{1,0:T(8,128)S(1)} custom-call(bf16[512,2048]{1,0:T(8,128)(2,1)} %get-tuple-element.24.refs_0_, bf16[512,2048]{1,0:T(8,128)(2,1)} %get-tuple-element.25.refs_1_, bf16[512,2048]{1,0:T(8,128)(2,1)} %get-tuple-element.26.refs_2_, bf16[512,2048]{1,0:T(8,128)(2,1)} %get-tuple-element.27.refs_3_, ...), custom_call_target="tpu_custom_call" | custom-call | tf_op jit(solution)/shard_map/own_again/pallas_call | solution.py:421
  126.4 7.4 %pair_again.1 = (f32[32,2048]{1,0:T(8,128)S(1)}, f32[8,128]{1,0:T(8,128)S(1)}, f32[8,128]{1,0:T(8,128)S(1)}) custom-call(s32[6]{0:T(128)S(1)} %pad_add_fusion.1.slots_ref, bf16[3,2048,2048]{2,1,0:T(8,128)(2,1)S(1)} %get-tuple-element.21.front_ref, bf16[2,2048,2048]{2,1,0:T(8,128)(2,1)} %get-tuple-element.22.back_ref, ...), custom_call_target="tpu_custom_call" | custom-call | tf_op jit(solution)/shard_map/pair_again/pallas_call | solution.py:432
  133.8 4.4 %collective-permute-start.27 = (f32[8,128]{1,0:T(8,128)S(1)}, f32[8,128]{1,0:T(8,128)S(1)}, u32[]{:S(2)}, u32[]{:S(2)}) collective-permute-start(f32[8,128]{1,0:T(8,128)S(1)} %get-tuple-element.31), channel_id=1, source_target_pairs={{0,12},{1,13},{2,14},{3,15},{4,8},{5,9},{6,10},{7,11},{8,4},{9,5},... | collective-permute-start | bytes 12296 | tf_op jit(solution)/shard_map/ppermute | solution.py:267
  138.8 0.9 collective-permute-done.27
  139.8 2.9 %collective-permute-done.26 = f32[8,128]{1,0:T(8,128)S(1)} collective-permute-done((f32[8,128]{1,0:T(8,128)S(1)}, f32[8,128]{1,0:T(8,128)S(1)}, u32[]{:S(2)}, u32[]{:S(2)}) %collective-permute-start.26) | collective-permute-done | bytes 4128 | tf_op jit(solution)/shard_map/ppermute | solution.py:267
  143.3 1.3 collective-permute-start.28
  144.6 1.5 curve_order.1
  (80 shorter events, 13.6 us)
Async XLA Ops:
  1.3 11.3 %collective-permute-start.2 = (s32[1,5]{1,0:T(1,128)S(1)}, s32[1,5]{1,0:T(1,128)S(1)}, u32[]{:S(2)}, u32[]{:S(2)}) collective-permute-start(s32[1,5]{1,0:T(1,128)S(1)} %get-tuple-element.54), channel_id=1, source_target_pairs={{0,12},{1,13},{2,14},{3,15},{4,8},{5,9},{6,10},{7,11},{8,4},{9,5},... | collective-permute-start | bytes 68 | tf_op jit(solution)/shard_map/ppermute | solution.py:267
  6.4 6.3 %collective-permute-start.1 = (s32[1,5]{1,0:T(1,128)S(1)}, s32[1,5]{1,0:T(1,128)S(1)}, u32[]{:S(2)}, u32[]{:S(2)}) collective-permute-start(s32[1,5]{1,0:T(1,128)S(1)} %get-tuple-element.54), channel_id=1, source_target_pairs={{0,8},{1,9},{2,10},{3,11},{4,12},{5,13},{6,14},{7,15},{8,0},{9,1},... | collective-permute-start | bytes 68 | tf_op jit(solution)/shard_map/ppermute | solution.py:267
  6.4 6.9 %collective-permute-start = (s32[1,5]{1,0:T(1,128)S(1)}, s32[1,5]{1,0:T(1,128)S(1)}, u32[]{:S(2)}, u32[]{:S(2)}) collective-permute-start(s32[1,5]{1,0:T(1,128)S(1)} %get-tuple-element.54), channel_id=1, source_target_pairs={{0,4},{1,5},{2,6},{3,7},{4,0},{5,1},{6,2},{7,3},{8,12},{9,13},{10,... | collective-permute-start | bytes 68 | tf_op jit(solution)/shard_map/ppermute | solution.py:267
  8.7 23.9 %collective-permute-start.12 = (bf16[80,1024]{1,0:T(8,128)(2,1)S(1)}, bf16[80,1024]{1,0:T(8,128)(2,1)S(1)}, u32[]{:S(2)}, u32[]{:S(2)}) collective-permute-start(bf16[80,1024]{1,0:T(8,128)(2,1)S(1)} %pad_maximum_fusion.pay_ref.refs_4_), channel_id=1, source_target_pairs={{0,1},{1,0},{2,3},{3,2},{4,5},{5,4},{6,7},{7,6},{8,9},{9,8},{10,11... | collective-permute-start | bytes 491528 | tf_op jit(solution)/shard_map/ppermute | solution.py:267
  8.8 14.3 %collective-permute-start.8 = (bf16[80,1024]{1,0:T(8,128)(2,1)S(1)}, bf16[80,1024]{1,0:T(8,128)(2,1)S(1)}, u32[]{:S(2)}, u32[]{:S(2)}) collective-permute-start(bf16[80,1024]{1,0:T(8,128)(2,1)S(1)} %pad_maximum_fusion.pay_ref.refs_4_), channel_id=1, source_target_pairs={{0,12},{1,13},{2,14},{3,15},{4,8},{5,9},{6,10},{7,11},{8,4},{9,5},... | collective-permute-start | bytes 491528 | tf_op jit(solution)/shard_map/ppermute | solution.py:267
  12.7 14.7 %collective-permute-start.7 = (bf16[80,1024]{1,0:T(8,128)(2,1)S(1)}, bf16[80,1024]{1,0:T(8,128)(2,1)S(1)}, u32[]{:S(2)}, u32[]{:S(2)}) collective-permute-start(bf16[80,1024]{1,0:T(8,128)(2,1)S(1)} %pad_maximum_fusion.pay_ref.refs_4_), channel_id=1, source_target_pairs={{0,8},{1,9},{2,10},{3,11},{4,12},{5,13},{6,14},{7,15},{8,0},{9,1},... | collective-permute-start | bytes 491528 | tf_op jit(solution)/shard_map/ppermute | solution.py:267
  12.7 19.9 %collective-permute-start.6 = (bf16[80,1024]{1,0:T(8,128)(2,1)S(1)}, bf16[80,1024]{1,0:T(8,128)(2,1)S(1)}, u32[]{:S(2)}, u32[]{:S(2)}) collective-permute-start(bf16[80,1024]{1,0:T(8,128)(2,1)S(1)} %pad_maximum_fusion.pay_ref.refs_4_), channel_id=1, source_target_pairs={{0,4},{1,5},{2,6},{3,7},{4,0},{5,1},{6,2},{7,3},{8,12},{9,13},{10,... | collective-permute-start | bytes 491528 | tf_op jit(solution)/shard_map/ppermute | solution.py:267
  18.2 15.5 %collective-permute-start.5 = (bf16[80,1024]{1,0:T(8,128)(2,1)S(1)}, bf16[80,1024]{1,0:T(8,128)(2,1)S(1)}, u32[]{:S(2)}, u32[]{:S(2)}) collective-permute-start(bf16[80,1024]{1,0:T(8,128)(2,1)S(1)} %pad_maximum_fusion.pay_ref.refs_4_), channel_id=1, source_target_pairs={{0,2},{1,3},{2,0},{3,1},{4,6},{5,7},{6,4},{7,5},{8,10},{9,11},{10,... | collective-permute-start | bytes 491528 | tf_op jit(solution)/shard_map/ppermute | solution.py:267
  23.0 15.8 %collective-permute-start.15 = (bf16[80,1024]{1,0:T(8,128)(2,1)S(1)}, bf16[80,1024]{1,0:T(8,128)(2,1)S(1)}, u32[]{:S(2)}, u32[]{:S(2)}) collective-permute-start(bf16[80,1024]{1,0:T(8,128)(2,1)S(1)} %collective-permute-done.8.arrived_ref.refs_7_), channel_id=1, source_target_pairs={{0,1},{1,0},{2,3},{3,2},{4,5},{5,4},{6,7},{7,6},{8,9},{9,8},{10,11... | collective-permute-start | bytes 491528 | tf_op jit(solution)/shard_map/ppermute | solution.py:267
  27.3 11.5 %collective-permute-start.11 = (bf16[80,1024]{1,0:T(8,128)(2,1)S(1)}, bf16[80,1024]{1,0:T(8,128)(2,1)S(1)}, u32[]{:S(2)}, u32[]{:S(2)}) collective-permute-start(bf16[80,1024]{1,0:T(8,128)(2,1)S(1)} %collective-permute-done.8.arrived_ref.refs_7_), channel_id=1, source_target_pairs={{0,2},{1,3},{2,0},{3,1},{4,6},{5,7},{6,4},{7,5},{8,10},{9,11},{10,... | collective-permute-start | bytes 491528 | tf_op jit(solution)/shard_map/ppermute | solution.py:267
  32.5 6.8 %collective-permute-start.14 = (bf16[80,1024]{1,0:T(8,128)(2,1)S(1)}, bf16[80,1024]{1,0:T(8,128)(2,1)S(1)}, u32[]{:S(2)}, u32[]{:S(2)}) collective-permute-start(bf16[80,1024]{1,0:T(8,128)(2,1)S(1)} %collective-permute-done.7.arrived_ref.refs_6_), channel_id=1, source_target_pairs={{0,1},{1,0},{2,3},{3,2},{4,5},{5,4},{6,7},{7,6},{8,9},{9,8},{10,11... | collective-permute-start | bytes 491528 | tf_op jit(solution)/shard_map/ppermute | solution.py:267
  32.5 7.1 %collective-permute-start.10 = (bf16[80,1024]{1,0:T(8,128)(2,1)S(1)}, bf16[80,1024]{1,0:T(8,128)(2,1)S(1)}, u32[]{:S(2)}, u32[]{:S(2)}) collective-permute-start(bf16[80,1024]{1,0:T(8,128)(2,1)S(1)} %collective-permute-done.7.arrived_ref.refs_6_), channel_id=1, source_target_pairs={{0,2},{1,3},{2,0},{3,1},{4,6},{5,7},{6,4},{7,5},{8,10},{9,11},{10,... | collective-permute-start | bytes 491528 | tf_op jit(solution)/shard_map/ppermute | solution.py:267
  33.8 8.9 %collective-permute-start.9 = (bf16[80,1024]{1,0:T(8,128)(2,1)S(1)}, bf16[80,1024]{1,0:T(8,128)(2,1)S(1)}, u32[]{:S(2)}, u32[]{:S(2)}) collective-permute-start(bf16[80,1024]{1,0:T(8,128)(2,1)S(1)} %collective-permute-done.6.arrived_ref.refs_5_), channel_id=1, source_target_pairs={{0,2},{1,3},{2,0},{3,1},{4,6},{5,7},{6,4},{7,5},{8,10},{9,11},{10,... | collective-permute-start | bytes 491528 | tf_op jit(solution)/shard_map/ppermute | solution.py:267
  38.8 8.1 %collective-permute-start.13 = (bf16[80,1024]{1,0:T(8,128)(2,1)S(1)}, bf16[80,1024]{1,0:T(8,128)(2,1)S(1)}, u32[]{:S(2)}, u32[]{:S(2)}) collective-permute-start(bf16[80,1024]{1,0:T(8,128)(2,1)S(1)} %collective-permute-done.6.arrived_ref.refs_5_), channel_id=1, source_target_pairs={{0,1},{1,0},{2,3},{3,2},{4,5},{5,4},{6,7},{7,6},{8,9},{9,8},{10,11... | collective-permute-start | bytes 491528 | tf_op jit(solution)/shard_map/ppermute | solution.py:267
  38.8 8.1 %collective-permute-start.16 = (bf16[80,1024]{1,0:T(8,128)(2,1)S(1)}, bf16[80,1024]{1,0:T(8,128)(2,1)S(1)}, u32[]{:S(2)}, u32[]{:S(2)}) collective-permute-start(bf16[80,1024]{1,0:T(8,128)(2,1)S(1)} %collective-permute-done.5.arrived_ref.refs_8_), channel_id=1, source_target_pairs={{0,1},{1,0},{2,3},{3,2},{4,5},{5,4},{6,7},{7,6},{8,9},{9,8},{10,11... | collective-permute-start | bytes 491528 | tf_op jit(solution)/shard_map/ppermute | solution.py:267
  39.3 7.6 %collective-permute-start.19 = (bf16[80,1024]{1,0:T(8,128)(2,1)S(1)}, bf16[80,1024]{1,0:T(8,128)(2,1)S(1)}, u32[]{:S(2)}, u32[]{:S(2)}) collective-permute-start(bf16[80,1024]{1,0:T(8,128)(2,1)S(1)} %collective-permute-done.11.refs_11_), channel_id=1, source_target_pairs={{0,1},{1,0},{2,3},{3,2},{4,5},{5,4},{6,7},{7,6},{8,9},{9,8},{10,11... | collective-permute-start | bytes 491528 | tf_op jit(solution)/shard_map/ppermute | solution.py:267
  39.6 7.3 %collective-permute-start.18 = (bf16[80,1024]{1,0:T(8,128)(2,1)S(1)}, bf16[80,1024]{1,0:T(8,128)(2,1)S(1)}, u32[]{:S(2)}, u32[]{:S(2)}) collective-permute-start(bf16[80,1024]{1,0:T(8,128)(2,1)S(1)} %collective-permute-done.10.refs_10_), channel_id=1, source_target_pairs={{0,1},{1,0},{2,3},{3,2},{4,5},{5,4},{6,7},{7,6},{8,9},{9,8},{10,11... | collective-permute-start | bytes 491528 | tf_op jit(solution)/shard_map/ppermute | solution.py:267
  99.9 14.5 %collective-permute-start.22 = (bf16[1,8,2176]{2,1,0:T(8,128)(2,1)S(1)}, bf16[1,8,2176]{2,1,0:T(8,128)(2,1)S(1)}, u32[]{:S(2)}, u32[]{:S(2)}) collective-permute-start(bf16[1,8,2176]{2,1,0:T(8,128)(2,1)S(1)} %bitcast.9), channel_id=1, source_target_pairs={{0,12},{1,13},{2,14},{3,15},{4,8},{5,9},{6,10},{7,11},{8,4},{9,5},... | collective-permute-start | bytes 104456 | tf_op jit(solution)/shard_map/ppermute | solution.py:267
  112.2 4.8 %collective-permute-start.21 = (bf16[1,8,2176]{2,1,0:T(8,128)(2,1)S(1)}, bf16[1,8,2176]{2,1,0:T(8,128)(2,1)S(1)}, u32[]{:S(2)}, u32[]{:S(2)}) collective-permute-start(bf16[1,8,2176]{2,1,0:T(8,128)(2,1)S(1)} %bitcast.10), channel_id=1, source_target_pairs={{0,8},{1,9},{2,10},{3,11},{4,12},{5,13},{6,14},{7,15},{8,0},{9,1},... | collective-permute-start | bytes 104456 | tf_op jit(solution)/shard_map/ppermute | solution.py:267
  112.2 4.8 %collective-permute-start.20 = (bf16[1,8,2176]{2,1,0:T(8,128)(2,1)S(1)}, bf16[1,8,2176]{2,1,0:T(8,128)(2,1)S(1)}, u32[]{:S(2)}, u32[]{:S(2)}) collective-permute-start(bf16[1,8,2176]{2,1,0:T(8,128)(2,1)S(1)} %bitcast.11), channel_id=1, source_target_pairs={{0,4},{1,5},{2,6},{3,7},{4,0},{5,1},{6,2},{7,3},{8,12},{9,13},{10,... | collective-permute-start | bytes 104456 | tf_op jit(solution)/shard_map/ppermute | solution.py:267
  117.1 5.1 %collective-permute-start.23 = (bf16[4,8,2176]{2,1,0:T(8,128)(2,1)S(1)}, bf16[4,8,2176]{2,1,0:T(8,128)(2,1)S(1)}, u32[]{:S(2)}, u32[]{:S(2)}) collective-permute-start(bf16[4,8,2176]{2,1,0:T(8,128)(2,1)S(1)} %pad_maximum_fusion.1), channel_id=1, source_target_pairs={{0,2},{1,3},{2,0},{3,1},{4,6},{5,7},{6,4},{7,5},{8,10},{9,11},{10,... | collective-permute-start | bytes 417800 | tf_op jit(solution)/shard_map/ppermute | solution.py:267
  133.8 5.9 %collective-permute-start.27 = (f32[8,128]{1,0:T(8,128)S(1)}, f32[8,128]{1,0:T(8,128)S(1)}, u32[]{:S(2)}, u32[]{:S(2)}) collective-permute-start(f32[8,128]{1,0:T(8,128)S(1)} %get-tuple-element.31), channel_id=1, source_target_pairs={{0,12},{1,13},{2,14},{3,15},{4,8},{5,9},{6,10},{7,11},{8,4},{9,5},... | collective-permute-start | bytes 12296 | tf_op jit(solution)/shard_map/ppermute | solution.py:267
  138.2 4.5 %collective-permute-start.26 = (f32[8,128]{1,0:T(8,128)S(1)}, f32[8,128]{1,0:T(8,128)S(1)}, u32[]{:S(2)}, u32[]{:S(2)}) collective-permute-start(f32[8,128]{1,0:T(8,128)S(1)} %get-tuple-element.31), channel_id=1, source_target_pairs={{0,8},{1,9},{2,10},{3,11},{4,12},{5,13},{6,14},{7,15},{8,0},{9,1},... | collective-permute-start | bytes 12296 | tf_op jit(solution)/shard_map/ppermute | solution.py:267
  138.2 4.5 %collective-permute-start.25 = (f32[8,128]{1,0:T(8,128)S(1)}, f32[8,128]{1,0:T(8,128)S(1)}, u32[]{:S(2)}, u32[]{:S(2)}) collective-permute-start(f32[8,128]{1,0:T(8,128)S(1)} %get-tuple-element.31), channel_id=1, source_target_pairs={{0,4},{1,5},{2,6},{3,7},{4,0},{5,1},{6,2},{7,3},{8,12},{9,13},{10,... | collective-permute-start | bytes 12296 | tf_op jit(solution)/shard_map/ppermute | solution.py:267
  (10 other events, 57.9 us)

commit v7 on v6

--- a/solution.py
+++ b/solution.py
@@ -16,6 +16,7 @@
 ROWS = 512
 PARTS = 4
 COLS = 512
+SUB = 64
 FRONT = 3
 HELD = 4
 TAIL = 128
@@ -52,6 +53,17 @@
     return jnp.transpose(jnp.concatenate([feat, feat, feat, norm_rows(norm, 3)], axis=0))
 
 
+def psi_chain(dist):
+    dist = jnp.maximum(dist, 1e-30)
+    radius = dist * lax.rsqrt(dist)
+    u = jnp.maximum(SHRINK - radius, 0.0)
+    two = u * u
+    four = two * two
+    eight = four * four
+    sixteen = eight * eight
+    return (sixteen * two * (u - two)).astype(BF16)
+
+
 def psi_power(dist):
     dist = jnp.maximum(dist, 1e-30)
     radius = dist * lax.rsqrt(dist)
@@ -59,25 +71,14 @@
     return (jnp.exp2(19.0 * lax.log2(u)) * (1.0 - u)).astype(BF16)
 
 
-def tile_rows(left_ref, right_ref, vec_ref, begin, tile_ref, sum_ref, rows_at_once):
-    at = pl.multiple_of(begin, ROWS)
-    left = left_ref[pl.ds(at, ROWS), :]
-    vec = vec_ref[:, pl.ds(at, ROWS)]
-
-    def step(index, carry):
-        cols = pl.ds(pl.multiple_of(index * COLS, COLS), COLS)
-        dist = jnp.dot(left, right_ref[:, cols], preferred_element_type=F32)
-        parts = []
-        for sub in range(0, ROWS, rows_at_once):
-            part = psi_power(dist[sub : sub + rows_at_once])
-            tile_ref[sub : sub + rows_at_once, cols] = part
-            parts.append(part)
-        sum_ref[:, cols] += jnp.dot(
-            vec, jnp.concatenate(parts, axis=0), preferred_element_type=F32
-        )
-        return carry
-
-    lax.fori_loop(0, right_ref.shape[1] // COLS, step, 0)
+def tile_unit(left, right, vec, psis, tile_ref):
+    dist = jnp.dot(left, right, preferred_element_type=F32)
+    parts = []
+    for index, sub in enumerate(range(0, left.shape[0], SUB)):
+        part = psis[index % len(psis)](dist[sub : sub + SUB])
+        tile_ref[sub : sub + SUB, :] = part
+        parts.append(part)
+    return jnp.dot(vec, jnp.concatenate(parts, axis=0), preferred_element_type=F32)
 
 
 def unpack(pay):
@@ -86,22 +87,42 @@
 
 
 def own_kernel(part, pay_ref, right_ref, arrived_ref, tile_ref, sum_ref, left_ref, vec_ref):
-    feat, vec = unpack(pay_ref[...])
-    begin = part * ROWS
-    left_ref[...] = other_factor(feat[:, begin : begin + ROWS])
-    vec_ref[...] = vec[:, begin : begin + ROWS]
-    sum_ref[...] = jnp.zeros_like(sum_ref)
-    tile_rows(left_ref, right_ref, vec_ref, 0, tile_ref, sum_ref, 128)
+    @pl.when(pl.program_id(0) == 0)
+    def _():
+        feat, vec = unpack(pay_ref[...])
+        begin = part * ROWS
+        left_ref[...] = other_factor(feat[:, begin : begin + ROWS])
+        vec_ref[...] = vec[:, begin : begin + ROWS]
+
+    sum_ref[...] = tile_unit(
+        left_ref[...], right_ref[...], vec_ref[...], (psi_power, psi_chain), tile_ref
+    )
 
 
 def factor_kernel(pay_ref, right_ref):
     right_ref[...] = own_factor(unpack(pay_ref[...])[0])
 
 
-def pair_kernel(slots_ref, right_ref, rhs_ref, var_ref, *refs):
+def find_partners(lists_ref, me, slots_ref):
+    count, most = lists_ref.shape
+    for at in range(slots_ref.shape[0]):
+        slots_ref[at] = 0
+    total = jnp.int32(0)
+    for at, place in enumerate(gather_places(count)):
+        if at == 0:
+            continue
+        hit = jnp.bool_(False)
+        for entry in range(most):
+            hit = hit | (lists_ref[at, entry] == me) | (lists_ref[0, entry] == (me ^ place))
+        slots_ref[1 + total] = jnp.where(hit, at, 0)
+        total = total + hit.astype(jnp.int32)
+    slots_ref[0] = total
+
+
+def pair_kernel(lists_ref, me_ref, right_ref, rhs_ref, var_ref, *refs):
     first_refs = refs[:PARTS]
-    block_refs = refs[PARTS:-8]
-    front_ref, back_ref, image_ref, send_ref = refs[-8:-4]
+    block_refs = refs[PARTS:-9]
+    front_ref, back_ref, image_ref, send_ref, slots_ref = refs[-9:-4]
     left_ref, vec_ref, pay_ref, sem_ref = refs[-4:]
     slot, step = pl.program_id(0), pl.program_id(1)
     sum_ref = image_ref
@@ -117,6 +138,7 @@
 
     @pl.when((slot == 0) & (step == 0))
     def _():
+        find_partners(lists_ref, me_ref[0], slots_ref)
         sum_ref[...] = functools.reduce(jnp.add, [first_ref[...] for first_ref in first_refs])
 
         @pl.when(slots_ref[0] > 0)
@@ -142,9 +164,17 @@
         for tile_ref, here in ((front_ref, slot < FRONT), (back_ref, slot >= FRONT)):
             @pl.when(here)
             def _():
-                tile_rows(
-                    left_ref, right_ref, vec_ref, step * ROWS, tile_ref.at[0], sum_ref, 64
-                )
+                rows = pl.ds(pl.multiple_of(step * ROWS, ROWS), ROWS)
+                left, vec = left_ref[rows, :], vec_ref[:, rows]
+
+                def unit(index, carry):
+                    cols = pl.ds(pl.multiple_of(index * COLS, COLS), COLS)
+                    sum_ref[:, cols] += tile_unit(
+                        left, right_ref[:, cols], vec, (psi_power,), tile_ref.at[0, :, cols]
+                    )
+                    return carry
+
+                lax.fori_loop(0, right_ref.shape[1] // COLS, unit, 0)
 
     @pl.when((slot == pl.num_programs(0) - 1) & (step == pl.num_programs(1) - 1))
     def _():
@@ -162,27 +192,23 @@
         send_ref[:, width:] = tail.astype(BF16)
 
 
-def own_again_kernel(*refs):
-    tile_refs, (vec_ref, sum_ref) = refs[:PARTS], refs[PARTS:]
+def own_again_kernel(part, tile_ref, vec_ref, sum_ref):
     step = pl.program_id(0)
-    rows = tile_refs[0].shape[0]
+    rows = tile_ref.shape[0]
 
     @pl.when(step == 0)
     def _():
         sum_ref[...] = jnp.zeros_like(sum_ref)
 
-    for part, tile_ref in enumerate(tile_refs):
-        at = pl.multiple_of(part * ROWS + step * rows, rows)
-        sum_ref[...] += jnp.dot(
-            vec_ref[:, pl.ds(at, rows)], tile_ref[...], preferred_element_type=F32
-        )
+    at = pl.multiple_of(part * ROWS + step * rows, rows)
+    sum_ref[...] += jnp.dot(vec_ref[:, pl.ds(at, rows)], tile_ref[...], preferred_element_type=F32)
 
 
 def again_kernel(
-    slots_ref, front_ref, back_ref, vec_ref, tails_ref, first_ref, rhs_ref, var_ref, image_ref,
-    rows_ref, dots_ref, step_ref,
-    sum_ref, held_ref, sem_ref,
+    slots_ref, front_ref, back_ref, vec_ref, tails_ref, rhs_ref, var_ref, image_ref, *refs
 ):
+    first_refs = refs[:PARTS]
+    rows_ref, dots_ref, step_ref, sum_ref, held_ref, sem_ref = refs[PARTS:]
     slot, step = pl.program_id(0), pl.program_id(1)
     width = rhs_ref.shape[1]
 
@@ -197,7 +223,7 @@
 
     @pl.when((slot == 0) & (step == 0))
     def _():
-        sum_ref[...] = first_ref[...]
+        sum_ref[...] = functools.reduce(jnp.add, [first_ref[...] for first_ref in first_refs])
         for part in range(HELD):
             @pl.when(part < parts)
             def _():
@@ -313,23 +339,6 @@
     return blocks
 
 
-def partners(coupled, count):
-    most = coupled.shape[1]
-    me = lax.axis_index("row")
-    lists = tree_gather(coupled[0], count)
-    number = me ^ jnp.asarray(gather_places(count), jnp.int32)
-    lower = jnp.any(lists == me, axis=1)
-    upper = jnp.any(coupled == number[:, None], axis=1)
-    valid = lower | upper
-    earlier = np.tri(count, k=-1, dtype=bool)
-    before = jnp.sum((valid[None, :] & earlier).astype(jnp.int32), axis=1)
-    total = jnp.sum(valid.astype(jnp.int32))
-    slot = jnp.minimum(jnp.arange(most), jnp.maximum(total - 1, 0))
-    hit = valid[None, :] & (before[None, :] == slot[:, None])
-    where = jnp.sum(jnp.where(hit, jnp.arange(count)[None, :], 0), axis=1)
-    return jnp.concatenate([total[None], where]).astype(jnp.int32)
-
-
 def local(features, right_side, variance, hilbert_order, tile_list):
     width = features.shape[1]
     rhs_count = right_side.shape[0]
@@ -355,14 +364,20 @@
         compiler_params=params,
         name="own_factor",
     )(payload)
-    slots = partners(tile_list[:, :, 1], count)
+    lists = tree_gather(tile_list[0, :, 1], count)
+    me = jnp.full((1,), lax.axis_index("row"), jnp.int32)
     own_parts = [
         pl.pallas_call(
             functools.partial(own_kernel, part),
+            grid=(width // COLS,),
             in_specs=[
-                pl.BlockSpec(payload.shape, lambda: (0, 0)),
-                pl.BlockSpec(right.shape, lambda: (0, 0)),
+                pl.BlockSpec(payload.shape, whole),
+                pl.BlockSpec((KDIM, COLS), lambda i: (0, i)),
                 pl.BlockSpec(memory_space=pl.ANY),
+            ],
+            out_specs=[
+                pl.BlockSpec((ROWS, COLS), lambda i: (0, i)),
+                pl.BlockSpec((rhs_count, COLS), lambda i: (0, i)),
             ],
             out_shape=[pltpu.HBM((ROWS, width), BF16), shape(right_side.shape, F32)],
             scratch_shapes=[pltpu.VMEM((ROWS, KDIM), BF16), pltpu.VMEM((rhs_count, ROWS), BF16)],
@@ -377,18 +392,18 @@
     own_tiles = [part[0] for part in own_parts]
     own_sums = [part[1] for part in own_parts]
 
-    def front_at(k, i, s):
+    def front_at(k, i, *ignored):
         return (jnp.minimum(k, FRONT - 1), jnp.where(k < FRONT, i, steps - 1), 0)
 
-    def back_at(k, i, s):
+    def back_at(k, i, *ignored):
         return (jnp.maximum(k - FRONT, 0), jnp.where(k < FRONT, 0, i), 0)
 
     tile_specs = [pl.BlockSpec((1, ROWS, width), front_at), pl.BlockSpec((1, ROWS, width), back_at)]
     send_shape = (rhs_count, width + TAIL)
-    front_tiles, back_tiles, image, send = pl.pallas_call(
+    front_tiles, back_tiles, image, send, slots = pl.pallas_call(
         pair_kernel,
         grid_spec=pltpu.PrefetchScalarGridSpec(
-            num_scalar_prefetch=1,
+            num_scalar_prefetch=2,
             grid=(most, steps),
             in_specs=[
                 pl.BlockSpec(right.shape, whole),
@@ -401,6 +416,7 @@
             + [
                 row_spec,
                 pl.BlockSpec(send_shape, whole),
+                pl.BlockSpec(memory_space=pltpu.SMEM),
             ],
             scratch_shapes=[pltpu.VMEM((width, KDIM), BF16), pltpu.VMEM((rhs_count, width), BF16)]
             + [pltpu.VMEM((2,) + payload.shape, BF16), pltpu.SemaphoreType.DMA((2,))],
@@ -410,24 +426,33 @@
             pltpu.HBM((most - FRONT, width, width), BF16),
             shape(right_side.shape, F32),
             shape(send_shape, BF16),
+            shape((most + 2,), jnp.int32),
         ],
         compiler_params=params,
         name="pair_tiles",
-    )(slots, right, right_side, var_row, *own_sums, *every)
+    )(lists, me, right, right_side, var_row, *own_sums, *every)
     front_tiles = pltpu.with_memory_space_constraint(front_tiles, pltpu.VMEM)
     back_tiles = pltpu.with_memory_space_constraint(back_tiles, pltpu.HBM)
 
     every_send = tree_gather(send, count)
-    own_again = pl.pallas_call(
-        own_again_kernel,
-        grid=(2,),
-        in_specs=[pl.BlockSpec((ROWS // 2, width), lambda i: (i, 0))] * PARTS
-        + [pl.BlockSpec(send_shape, whole)],
-        out_specs=row_spec,
-        out_shape=shape(right_side.shape, F32),
-        compiler_params=params,
-        name="own_again",
-    )(*[pltpu.with_memory_space_constraint(tile, pltpu.HBM) for tile in own_tiles], send)
+    own_again = [
+        pl.pallas_call(
+            functools.partial(own_again_kernel, part),
+            grid=(2,),
+            in_specs=[
+                pl.BlockSpec((ROWS // 2, width), lambda i: (i, 0)),
+                pl.BlockSpec(send_shape, whole),
+            ],
+            out_specs=row_spec,
+            out_shape=shape(right_side.shape, F32),
+            compiler_params=params,
+            cost_estimate=pl.CostEstimate(
+                flops=3_000_000_000, bytes_accessed=2 * ROWS * width, transcendentals=0
+            ),
+            name=f"own_again_{part}",
+        )(pltpu.with_memory_space_constraint(tile, pltpu.HBM), send)
+        for part, tile in enumerate(own_tiles)
+    ]
     dots_spec = pl.BlockSpec((rhs_count, TAIL), whole)
     rows, dots, steps_one = pl.pallas_call(
         again_kernel,
@@ -440,10 +465,10 @@
                 pl.BlockSpec((1,) + send_shape, lambda k, i, s: (s[1 + k], 0, 0)),
                 pl.BlockSpec((count, rhs_count, TAIL), lambda k, i, s: (0, 0, width // TAIL)),
                 row_spec,
-                row_spec,
                 var_spec,
                 row_spec,
-            ],
+            ]
+            + [row_spec] * PARTS,
             out_specs=[
                 pl.BlockSpec((4 * rhs_count, width), whole),
                 dots_spec,
@@ -462,7 +487,7 @@
         ],
         compiler_params=params,
         name="pair_again",
-    )(slots, front_tiles, back_tiles, every_send, every_send, own_again, right_side, var_row, image)
+    )(slots, front_tiles, back_tiles, every_send, every_send, right_side, var_row, image, *own_again)
 
     dots = tree_sum(dots, count)
     ordered = pl.pallas_call(

time: 148 us -> 147 us (level)
  Pallas kernels: 82.8 us -> 97.7 us
  starting transfers between devices: 37.7 us -> 31.1 us
  waiting for transfers between devices: 18.6 us -> 13.9 us
  other arithmetic: 5.1 us -> 1.89 us
    pallas_call x1, Pallas kernels: 52.9 us -> 63.6 us  [local(): pl.pallas_call(pair_kernel, grid_spec=pltpu.PrefetchScalarGridSpec(num_sc...]
    ppermute x31, starting transfers between devices: 37.7 us -> 31.1 us  [swap(): return lax.ppermute(value, 'row', [(i, i ^ mask) for i in range(count)])]
    ppermute x31, waiting for transfers between devices: 18.6 us -> 13.9 us  [swap(): return lax.ppermute(value, 'row', [(i, i ^ mask) for i in range(count)])]
    pallas_call x1, Pallas kernels: 7.36 us -> 10 us  [local(): pl.pallas_call(again_kernel, grid_spec=pltpu.PrefetchScalarGridSpec(num_s...]
    pallas_call x5 -> x8, Pallas kernels: 20.9 us -> 22.5 us  [the longest x4 15.4 us: local(): pl.pallas_call(functools.partial(own_kernel, part), grid=(width // COLS,)...]
    reduce_sum x3 -> x0, other arithmetic: 1.62 us -> none  [the longest x1 0.8 us: partners(): before = jnp.sum((valid[None, :] & earlier).astype(jnp.int32), axis=1)]
  transfers between devices with their start and end apart: 31 -> 31, of which waited for: 10 -> 9; matrix products, arithmetic and copies ran while one was open for 3% -> 1% of each run, Pallas kernels for 15% -> 16%
where the time goes in v7:
time: 147 us
  Pallas kernels  97.7 us (66%)
  starting transfers between devices  31.1 us (21%)
  waiting for transfers between devices  13.9 us (9%)
  other arithmetic  1.89 us (1%)
  local copies, waits for them, and re-layouts  1.73 us (1%)
    pallas_call x1, Pallas kernels, local(): pl.pallas_call(pair_kernel, grid_spec=pltpu.PrefetchScalarGridSpec(num_sc...  63.6 us
    ppermute x31, starting transfers between devices, swap(): return lax.ppermute(value, 'row', [(i, i ^ mask) for i in range(count)])  31.1 us
    pallas_call x4, Pallas kernels, local(): pl.pallas_call(functools.partial(own_kernel, part), grid=(width // COLS,)...  15.4 us
    ppermute x31, waiting for transfers between devices, swap(): return lax.ppermute(value, 'row', [(i, i ^ mask) for i in range(count)])  13.9 us
    pallas_call x1, Pallas kernels, local(): pl.pallas_call(again_kernel, grid_spec=pltpu.PrefetchScalarGridSpec(num_s...  10 us
    pallas_call x4, Pallas kernels, local(): pl.pallas_call(functools.partial(own_again_kernel, part), grid=(2,), in_s...  7.16 us
  transfers between devices with their start and end apart: 31, of which 9 were waited for; matrix products, arithmetic and copies ran while one was open for 1% of the time, Pallas kernels for 16%

profile of v7, /device:TPU:0, one launch (start us, length us, event | category | flops | bytes accessed | tf_op | source)
XLA Modules:
  0.0 147.1 jit_solution(9269649003753291341)
XLA Ops:
  2.4 5.1 %collective-permute-start.8 = (bf16[80,1024]{1,0:T(8,128)(2,1)S(1)}, bf16[80,1024]{1,0:T(8,128)(2,1)S(1)}, u32[]{:S(2)}, u32[]{:S(2)}) collective-permute-start(bf16[80,1024]{1,0:T(8,128)(2,1)S(1)} %pad_maximum_fusion.pay_ref.refs_4_), channel_id=1, source_target_pairs={{0,12},{1,13},{2,14},{3,15},{4,8},{5,9},{6,10},{7,11},{8,4},{9,5},... | collective-permute-start | bytes 491528 | tf_op jit(solution)/shard_map/ppermute | solution.py:293
  9.2 3.4 %collective-permute-start = (s32[1,5]{1,0:T(1,128)S(1)}, s32[1,5]{1,0:T(1,128)S(1)}, u32[]{:S(2)}, u32[]{:S(2)}) collective-permute-start(s32[1,5]{1,0:T(1,128)S(1)} %slice_bitcast_fusion), channel_id=1, source_target_pairs={{0,4},{1,5},{2,6},{3,7},{4,0},{5,1},{6,2},{7,3},{8,12},{9,13},{10,... | collective-permute-start | bytes 68 | tf_op jit(solution)/shard_map/ppermute | solution.py:293
  13.5 2.5 %collective-permute-start.7 = (bf16[80,1024]{1,0:T(8,128)(2,1)S(1)}, bf16[80,1024]{1,0:T(8,128)(2,1)S(1)}, u32[]{:S(2)}, u32[]{:S(2)}) collective-permute-start(bf16[80,1024]{1,0:T(8,128)(2,1)S(1)} %pad_maximum_fusion.pay_ref.refs_4_), channel_id=1, source_target_pairs={{0,8},{1,9},{2,10},{3,11},{4,12},{5,13},{6,14},{7,15},{8,0},{9,1},... | collective-permute-start | bytes 491528 | tf_op jit(solution)/shard_map/ppermute | solution.py:293
  16.1 1.6 %collective-permute-start.3 = (s32[4,5]{1,0:T(4,128)S(1)}, s32[4,5]{1,0:T(4,128)S(1)}, u32[]{:S(2)}, u32[]{:S(2)}) collective-permute-start(s32[4,5]{1,0:T(4,128)S(1)} %pad_add_fusion), channel_id=1, source_target_pairs={{0,2},{1,3},{2,0},{3,1},{4,6},{5,7},{6,4},{7,5},{8,10},{9,11},{10,... | collective-permute-start | bytes 248 | tf_op jit(solution)/shard_map/ppermute | solution.py:293
  17.8 1.9 %collective-permute-done.3 = s32[4,5]{1,0:T(4,128)S(1)} collective-permute-done((s32[4,5]{1,0:T(4,128)S(1)}, s32[4,5]{1,0:T(4,128)S(1)}, u32[]{:S(2)}, u32[]{:S(2)}) %collective-permute-start.3) | collective-permute-done | bytes 112 | tf_op jit(solution)/shard_map/ppermute | solution.py:293
  21.0 1.5 %collective-permute-start.5 = (bf16[80,1024]{1,0:T(8,128)(2,1)S(1)}, bf16[80,1024]{1,0:T(8,128)(2,1)S(1)}, u32[]{:S(2)}, u32[]{:S(2)}) collective-permute-start(bf16[80,1024]{1,0:T(8,128)(2,1)S(1)} %pad_maximum_fusion.pay_ref.refs_4_), channel_id=1, source_target_pairs={{0,2},{1,3},{2,0},{3,1},{4,6},{5,7},{6,4},{7,5},{8,10},{9,11},{10,... | collective-permute-start | bytes 491528 | tf_op jit(solution)/shard_map/ppermute | solution.py:293
  22.6 3.9 %own_tile_3.1 = (bf16[512,2048]{1,0:T(8,128)(2,1)}, f32[8,2048]{1,0:T(8,128)S(1)}) custom-call(bf16[80,1024]{1,0:T(8,128)(2,1)S(1)} %pad_maximum_fusion.pay_ref.refs_4_, bf16[128,2048]{1,0:T(8,128)(2,1)S(1)} %own_factor.1.right_ref, bf16[80,1024]{1,0:T(8,128)(2,1)S(1)} %collective-permute-done.8.arrived_ref.refs_7_), custom_call_target="tpu_custom_call" | custom-call | flops 4000000000 | bytes 2097152 | tf_op jit(solution)/shard_map/own_tile_3/pallas_call | solution.py:370
  27.0 3.8 %own_tile_2.1 = (bf16[512,2048]{1,0:T(8,128)(2,1)}, f32[8,2048]{1,0:T(8,128)S(1)}) custom-call(bf16[80,1024]{1,0:T(8,128)(2,1)S(1)} %pad_maximum_fusion.pay_ref.refs_4_, bf16[128,2048]{1,0:T(8,128)(2,1)S(1)} %own_factor.1.right_ref, bf16[80,1024]{1,0:T(8,128)(2,1)S(1)} %collective-permute-done.7.arrived_ref.refs_6_), custom_call_target="tpu_custom_call" | custom-call | flops 4000000000 | bytes 2097152 | tf_op jit(solution)/shard_map/own_tile_2/pallas_call | solution.py:370
  31.0 1.5 %collective-permute-start.10 = (bf16[80,1024]{1,0:T(8,128)(2,1)S(1)}, bf16[80,1024]{1,0:T(8,128)(2,1)S(1)}, u32[]{:S(2)}, u32[]{:S(2)}) collective-permute-start(bf16[80,1024]{1,0:T(8,128)(2,1)S(1)} %collective-permute-done.7.arrived_ref.refs_6_), channel_id=1, source_target_pairs={{0,2},{1,3},{2,0},{3,1},{4,6},{5,7},{6,4},{7,5},{8,10},{9,11},{10,... | collective-permute-start | bytes 491528 | tf_op jit(solution)/shard_map/ppermute | solution.py:293
  33.0 3.8 %own_tile_1.1 = (bf16[512,2048]{1,0:T(8,128)(2,1)}, f32[8,2048]{1,0:T(8,128)S(1)}) custom-call(bf16[80,1024]{1,0:T(8,128)(2,1)S(1)} %pad_maximum_fusion.pay_ref.refs_4_, bf16[128,2048]{1,0:T(8,128)(2,1)S(1)} %own_factor.1.right_ref, bf16[80,1024]{1,0:T(8,128)(2,1)S(1)} %collective-permute-done.6.arrived_ref.refs_5_), custom_call_target="tpu_custom_call" | custom-call | flops 4000000000 | bytes 2097152 | tf_op jit(solution)/shard_map/own_tile_1/pallas_call | solution.py:370
  38.0 2.9 %collective-permute-done.9.refs_9_ = bf16[80,1024]{1,0:T(8,128)(2,1)S(1)} collective-permute-done((bf16[80,1024]{1,0:T(8,128)(2,1)S(1)}, bf16[80,1024]{1,0:T(8,128)(2,1)S(1)}, u32[]{:S(2)}, u32[]{:S(2)}) %collective-permute-start.9) | collective-permute-done | bytes 163872 | tf_op jit(solution)/shard_map/ppermute | solution.py:293
  40.9 3.8 %own_tile_0.1 = (bf16[512,2048]{1,0:T(8,128)(2,1)}, f32[8,2048]{1,0:T(8,128)S(1)}) custom-call(bf16[80,1024]{1,0:T(8,128)(2,1)S(1)} %pad_maximum_fusion.pay_ref.refs_4_, bf16[128,2048]{1,0:T(8,128)(2,1)S(1)} %own_factor.1.right_ref, bf16[80,1024]{1,0:T(8,128)(2,1)S(1)} %collective-permute-done.5.arrived_ref.refs_8_), custom_call_target="tpu_custom_call" | custom-call | flops 4000000000 | bytes 2097152 | tf_op jit(solution)/shard_map/own_tile_0/pallas_call | solution.py:370
  44.8 63.6 %pair_tiles.1 = (bf16[3,2048,2048]{2,1,0:T(8,128)(2,1)S(1)}, bf16[2,2048,2048]{2,1,0:T(8,128)(2,1)}, f32[8,2048]{1,0:T(8,128)S(1)}, bf16[8,2176]{1,0:T(8,128)(2,1)S(1)}, s32[7]{0:T(128)S(1)}) custom-call(s32[16,5]{1,0:T(8,128)S(1)} %concatenate.27.lists_ref, s32[1]{0:T(128)} %bitcast.1.me_ref, bf16[128,2048]{1,0:T(8,128)(2,1)S(1)} %own_factor.1.right_ref, ...), custom_call_target="tpu_custom_call" | custom-call | tf_op jit(solution)/shard_map/pair_tiles/pallas_call | solution.py:403
  108.4 3.5 %collective-permute-start.21 = (bf16[1,8,2176]{2,1,0:T(8,128)(2,1)S(1)}, bf16[1,8,2176]{2,1,0:T(8,128)(2,1)S(1)}, u32[]{:S(2)}, u32[]{:S(2)}) collective-permute-start(bf16[1,8,2176]{2,1,0:T(8,128)(2,1)S(1)} %bitcast.8), channel_id=1, source_target_pairs={{0,8},{1,9},{2,10},{3,11},{4,12},{5,13},{6,14},{7,15},{8,0},{9,1},... | collective-permute-start | bytes 104456 | tf_op jit(solution)/shard_map/ppermute | solution.py:293
  112.8 1.8 %own_again_3.1.refs_3_ = f32[8,2048]{1,0:T(8,128)S(1)} custom-call(bf16[512,2048]{1,0:T(8,128)(2,1)} %get-tuple-element.30.tile_ref, bf16[8,2176]{1,0:T(8,128)(2,1)S(1)} %get-tuple-element.25.vec_ref), custom_call_target="tpu_custom_call" | custom-call | flops 3000000000 | bytes 2097152 | tf_op jit(solution)/shard_map/own_again_3/pallas_call | solution.py:439
  114.6 1.8 %own_again_2.1.refs_2_ = f32[8,2048]{1,0:T(8,128)S(1)} custom-call(bf16[512,2048]{1,0:T(8,128)(2,1)} %get-tuple-element.29.tile_ref, bf16[8,2176]{1,0:T(8,128)(2,1)S(1)} %get-tuple-element.25.vec_ref), custom_call_target="tpu_custom_call" | custom-call | flops 3000000000 | bytes 2097152 | tf_op jit(solution)/shard_map/own_again_2/pallas_call | solution.py:439
  116.4 1.8 %own_again_1.1.refs_1_ = f32[8,2048]{1,0:T(8,128)S(1)} custom-call(bf16[512,2048]{1,0:T(8,128)(2,1)} %get-tuple-element.28.tile_ref, bf16[8,2176]{1,0:T(8,128)(2,1)S(1)} %get-tuple-element.25.vec_ref), custom_call_target="tpu_custom_call" | custom-call | flops 3000000000 | bytes 2097152 | tf_op jit(solution)/shard_map/own_again_1/pallas_call | solution.py:439
  118.3 1.6 %collective-permute-start.23 = (bf16[4,8,2176]{2,1,0:T(8,128)(2,1)S(1)}, bf16[4,8,2176]{2,1,0:T(8,128)(2,1)S(1)}, u32[]{:S(2)}, u32[]{:S(2)}) collective-permute-start(bf16[4,8,2176]{2,1,0:T(8,128)(2,1)S(1)} %pad_maximum_fusion.1), channel_id=1, source_target_pairs={{0,2},{1,3},{2,0},{3,1},{4,6},{5,7},{6,4},{7,5},{8,10},{9,11},{10,... | collective-permute-start | bytes 417800 | tf_op jit(solution)/shard_map/ppermute | solution.py:293
  119.9 3.7 %collective-permute-done.23 = bf16[4,8,2176]{2,1,0:T(8,128)(2,1)S(1)} collective-permute-done((bf16[4,8,2176]{2,1,0:T(8,128)(2,1)S(1)}, bf16[4,8,2176]{2,1,0:T(8,128)(2,1)S(1)}, u32[]{:S(2)}, u32[]{:S(2)}) %collective-permute-start.23) | collective-permute-done | bytes 139296 | tf_op jit(solution)/shard_map/ppermute | solution.py:293
  123.7 1.8 %own_again_0.1.refs_0_ = f32[8,2048]{1,0:T(8,128)S(1)} custom-call(bf16[512,2048]{1,0:T(8,128)(2,1)} %get-tuple-element.27.tile_ref, bf16[8,2176]{1,0:T(8,128)(2,1)S(1)} %get-tuple-element.25.vec_ref), custom_call_target="tpu_custom_call" | custom-call | flops 3000000000 | bytes 2097152 | tf_op jit(solution)/shard_map/own_again_0/pallas_call | solution.py:439
  125.6 10.0 %pair_again.1 = (f32[32,2048]{1,0:T(8,128)S(1)}, f32[8,128]{1,0:T(8,128)S(1)}, f32[8,128]{1,0:T(8,128)S(1)}) custom-call(s32[7]{0:T(128)S(1)} %get-tuple-element.22.slots_ref, bf16[3,2048,2048]{2,1,0:T(8,128)(2,1)S(1)} %get-tuple-element.23.front_ref, bf16[2,2048,2048]{2,1,0:T(8,128)(2,1)} %get-tuple-element.24.back_ref, ...), custom_call_target="tpu_custom_call" | custom-call | tf_op jit(solution)/shard_map/pair_again/pallas_call | solution.py:457
  135.7 2.5 %collective-permute-start.26 = (f32[8,128]{1,0:T(8,128)S(1)}, f32[8,128]{1,0:T(8,128)S(1)}, u32[]{:S(2)}, u32[]{:S(2)}) collective-permute-start(f32[8,128]{1,0:T(8,128)S(1)} %get-tuple-element.33), channel_id=1, source_target_pairs={{0,8},{1,9},{2,10},{3,11},{4,12},{5,13},{6,14},{7,15},{8,0},{9,1},... | collective-permute-start | bytes 12296 | tf_op jit(solution)/shard_map/ppermute | solution.py:293
  138.2 1.9 %collective-permute-start.25 = (f32[8,128]{1,0:T(8,128)S(1)}, f32[8,128]{1,0:T(8,128)S(1)}, u32[]{:S(2)}, u32[]{:S(2)}) collective-permute-start(f32[8,128]{1,0:T(8,128)S(1)} %get-tuple-element.33), channel_id=1, source_target_pairs={{0,4},{1,5},{2,6},{3,7},{4,0},{5,1},{6,2},{7,3},{8,12},{9,13},{10,... | collective-permute-start | bytes 12296 | tf_op jit(solution)/shard_map/ppermute | solution.py:293
  143.6 1.5 curve_order.1
  (75 shorter events, 15.2 us)
Async XLA Ops:
  2.4 20.1 %collective-permute-start.8 = (bf16[80,1024]{1,0:T(8,128)(2,1)S(1)}, bf16[80,1024]{1,0:T(8,128)(2,1)S(1)}, u32[]{:S(2)}, u32[]{:S(2)}) collective-permute-start(bf16[80,1024]{1,0:T(8,128)(2,1)S(1)} %pad_maximum_fusion.pay_ref.refs_4_), channel_id=1, source_target_pairs={{0,12},{1,13},{2,14},{3,15},{4,8},{5,9},{6,10},{7,11},{8,4},{9,5},... | collective-permute-start | bytes 491528 | tf_op jit(solution)/shard_map/ppermute | solution.py:293
  8.2 5.3 %collective-permute-start.2 = (s32[1,5]{1,0:T(1,128)S(1)}, s32[1,5]{1,0:T(1,128)S(1)}, u32[]{:S(2)}, u32[]{:S(2)}) collective-permute-start(s32[1,5]{1,0:T(1,128)S(1)} %slice_bitcast_fusion), channel_id=1, source_target_pairs={{0,12},{1,13},{2,14},{3,15},{4,8},{5,9},{6,10},{7,11},{8,4},{9,5},... | collective-permute-start | bytes 68 | tf_op jit(solution)/shard_map/ppermute | solution.py:293
  8.2 7.8 %collective-permute-start.1 = (s32[1,5]{1,0:T(1,128)S(1)}, s32[1,5]{1,0:T(1,128)S(1)}, u32[]{:S(2)}, u32[]{:S(2)}) collective-permute-start(s32[1,5]{1,0:T(1,128)S(1)} %slice_bitcast_fusion), channel_id=1, source_target_pairs={{0,8},{1,9},{2,10},{3,11},{4,12},{5,13},{6,14},{7,15},{8,0},{9,1},... | collective-permute-start | bytes 68 | tf_op jit(solution)/shard_map/ppermute | solution.py:293
  9.2 6.8 %collective-permute-start = (s32[1,5]{1,0:T(1,128)S(1)}, s32[1,5]{1,0:T(1,128)S(1)}, u32[]{:S(2)}, u32[]{:S(2)}) collective-permute-start(s32[1,5]{1,0:T(1,128)S(1)} %slice_bitcast_fusion), channel_id=1, source_target_pairs={{0,4},{1,5},{2,6},{3,7},{4,0},{5,1},{6,2},{7,3},{8,12},{9,13},{10,... | collective-permute-start | bytes 68 | tf_op jit(solution)/shard_map/ppermute | solution.py:293
  12.6 18.2 %collective-permute-start.12 = (bf16[80,1024]{1,0:T(8,128)(2,1)S(1)}, bf16[80,1024]{1,0:T(8,128)(2,1)S(1)}, u32[]{:S(2)}, u32[]{:S(2)}) collective-permute-start(bf16[80,1024]{1,0:T(8,128)(2,1)S(1)} %pad_maximum_fusion.pay_ref.refs_4_), channel_id=1, source_target_pairs={{0,1},{1,0},{2,3},{3,2},{4,5},{5,4},{6,7},{7,6},{8,9},{9,8},{10,11... | collective-permute-start | bytes 491528 | tf_op jit(solution)/shard_map/ppermute | solution.py:293
  13.5 13.0 %collective-permute-start.7 = (bf16[80,1024]{1,0:T(8,128)(2,1)S(1)}, bf16[80,1024]{1,0:T(8,128)(2,1)S(1)}, u32[]{:S(2)}, u32[]{:S(2)}) collective-permute-start(bf16[80,1024]{1,0:T(8,128)(2,1)S(1)} %pad_maximum_fusion.pay_ref.refs_4_), channel_id=1, source_target_pairs={{0,8},{1,9},{2,10},{3,11},{4,12},{5,13},{6,14},{7,15},{8,0},{9,1},... | collective-permute-start | bytes 491528 | tf_op jit(solution)/shard_map/ppermute | solution.py:293
  16.0 15.0 %collective-permute-start.6 = (bf16[80,1024]{1,0:T(8,128)(2,1)S(1)}, bf16[80,1024]{1,0:T(8,128)(2,1)S(1)}, u32[]{:S(2)}, u32[]{:S(2)}) collective-permute-start(bf16[80,1024]{1,0:T(8,128)(2,1)S(1)} %pad_maximum_fusion.pay_ref.refs_4_), channel_id=1, source_target_pairs={{0,4},{1,5},{2,6},{3,7},{4,0},{5,1},{6,2},{7,3},{8,12},{9,13},{10,... | collective-permute-start | bytes 491528 | tf_op jit(solution)/shard_map/ppermute | solution.py:293
  21.0 11.6 %collective-permute-start.5 = (bf16[80,1024]{1,0:T(8,128)(2,1)S(1)}, bf16[80,1024]{1,0:T(8,128)(2,1)S(1)}, u32[]{:S(2)}, u32[]{:S(2)}) collective-permute-start(bf16[80,1024]{1,0:T(8,128)(2,1)S(1)} %pad_maximum_fusion.pay_ref.refs_4_), channel_id=1, source_target_pairs={{0,2},{1,3},{2,0},{3,1},{4,6},{5,7},{6,4},{7,5},{8,10},{9,11},{10,... | collective-permute-start | bytes 491528 | tf_op jit(solution)/shard_map/ppermute | solution.py:293
  22.5 14.4 %collective-permute-start.15 = (bf16[80,1024]{1,0:T(8,128)(2,1)S(1)}, bf16[80,1024]{1,0:T(8,128)(2,1)S(1)}, u32[]{:S(2)}, u32[]{:S(2)}) collective-permute-start(bf16[80,1024]{1,0:T(8,128)(2,1)S(1)} %collective-permute-done.8.arrived_ref.refs_7_), channel_id=1, source_target_pairs={{0,1},{1,0},{2,3},{3,2},{4,5},{5,4},{6,7},{7,6},{8,9},{9,8},{10,11... | collective-permute-start | bytes 491528 | tf_op jit(solution)/shard_map/ppermute | solution.py:293
  26.5 10.5 %collective-permute-start.11 = (bf16[80,1024]{1,0:T(8,128)(2,1)S(1)}, bf16[80,1024]{1,0:T(8,128)(2,1)S(1)}, u32[]{:S(2)}, u32[]{:S(2)}) collective-permute-start(bf16[80,1024]{1,0:T(8,128)(2,1)S(1)} %collective-permute-done.8.arrived_ref.refs_7_), channel_id=1, source_target_pairs={{0,2},{1,3},{2,0},{3,1},{4,6},{5,7},{6,4},{7,5},{8,10},{9,11},{10,... | collective-permute-start | bytes 491528 | tf_op jit(solution)/shard_map/ppermute | solution.py:293
  30.8 6.6 %collective-permute-start.14 = (bf16[80,1024]{1,0:T(8,128)(2,1)S(1)}, bf16[80,1024]{1,0:T(8,128)(2,1)S(1)}, u32[]{:S(2)}, u32[]{:S(2)}) collective-permute-start(bf16[80,1024]{1,0:T(8,128)(2,1)S(1)} %collective-permute-done.7.arrived_ref.refs_6_), channel_id=1, source_target_pairs={{0,1},{1,0},{2,3},{3,2},{4,5},{5,4},{6,7},{7,6},{8,9},{9,8},{10,11... | collective-permute-start | bytes 491528 | tf_op jit(solution)/shard_map/ppermute | solution.py:293
  31.0 7.0 %collective-permute-start.10 = (bf16[80,1024]{1,0:T(8,128)(2,1)S(1)}, bf16[80,1024]{1,0:T(8,128)(2,1)S(1)}, u32[]{:S(2)}, u32[]{:S(2)}) collective-permute-start(bf16[80,1024]{1,0:T(8,128)(2,1)S(1)} %collective-permute-done.7.arrived_ref.refs_6_), channel_id=1, source_target_pairs={{0,2},{1,3},{2,0},{3,1},{4,6},{5,7},{6,4},{7,5},{8,10},{9,11},{10,... | collective-permute-start | bytes 491528 | tf_op jit(solution)/shard_map/ppermute | solution.py:293
  32.5 8.4 %collective-permute-start.9 = (bf16[80,1024]{1,0:T(8,128)(2,1)S(1)}, bf16[80,1024]{1,0:T(8,128)(2,1)S(1)}, u32[]{:S(2)}, u32[]{:S(2)}) collective-permute-start(bf16[80,1024]{1,0:T(8,128)(2,1)S(1)} %collective-permute-done.6.arrived_ref.refs_5_), channel_id=1, source_target_pairs={{0,2},{1,3},{2,0},{3,1},{4,6},{5,7},{6,4},{7,5},{8,10},{9,11},{10,... | collective-permute-start | bytes 491528 | tf_op jit(solution)/shard_map/ppermute | solution.py:293
  36.9 7.9 %collective-permute-start.13 = (bf16[80,1024]{1,0:T(8,128)(2,1)S(1)}, bf16[80,1024]{1,0:T(8,128)(2,1)S(1)}, u32[]{:S(2)}, u32[]{:S(2)}) collective-permute-start(bf16[80,1024]{1,0:T(8,128)(2,1)S(1)} %collective-permute-done.6.arrived_ref.refs_5_), channel_id=1, source_target_pairs={{0,1},{1,0},{2,3},{3,2},{4,5},{5,4},{6,7},{7,6},{8,9},{9,8},{10,11... | collective-permute-start | bytes 491528 | tf_op jit(solution)/shard_map/ppermute | solution.py:293
  37.0 7.8 %collective-permute-start.16 = (bf16[80,1024]{1,0:T(8,128)(2,1)S(1)}, bf16[80,1024]{1,0:T(8,128)(2,1)S(1)}, u32[]{:S(2)}, u32[]{:S(2)}) collective-permute-start(bf16[80,1024]{1,0:T(8,128)(2,1)S(1)} %collective-permute-done.5.arrived_ref.refs_8_), channel_id=1, source_target_pairs={{0,1},{1,0},{2,3},{3,2},{4,5},{5,4},{6,7},{7,6},{8,9},{9,8},{10,11... | collective-permute-start | bytes 491528 | tf_op jit(solution)/shard_map/ppermute | solution.py:293
  37.4 7.3 %collective-permute-start.19 = (bf16[80,1024]{1,0:T(8,128)(2,1)S(1)}, bf16[80,1024]{1,0:T(8,128)(2,1)S(1)}, u32[]{:S(2)}, u32[]{:S(2)}) collective-permute-start(bf16[80,1024]{1,0:T(8,128)(2,1)S(1)} %collective-permute-done.11.refs_11_), channel_id=1, source_target_pairs={{0,1},{1,0},{2,3},{3,2},{4,5},{5,4},{6,7},{7,6},{8,9},{9,8},{10,11... | collective-permute-start | bytes 491528 | tf_op jit(solution)/shard_map/ppermute | solution.py:293
  38.0 6.7 %collective-permute-start.18 = (bf16[80,1024]{1,0:T(8,128)(2,1)S(1)}, bf16[80,1024]{1,0:T(8,128)(2,1)S(1)}, u32[]{:S(2)}, u32[]{:S(2)}) collective-permute-start(bf16[80,1024]{1,0:T(8,128)(2,1)S(1)} %collective-permute-done.10.refs_10_), channel_id=1, source_target_pairs={{0,1},{1,0},{2,3},{3,2},{4,5},{5,4},{6,7},{7,6},{8,9},{9,8},{10,11... | collective-permute-start | bytes 491528 | tf_op jit(solution)/shard_map/ppermute | solution.py:293
  40.9 3.9 %collective-permute-start.17 = (bf16[80,1024]{1,0:T(8,128)(2,1)S(1)}, bf16[80,1024]{1,0:T(8,128)(2,1)S(1)}, u32[]{:S(2)}, u32[]{:S(2)}) collective-permute-start(bf16[80,1024]{1,0:T(8,128)(2,1)S(1)} %collective-permute-done.9.refs_9_), channel_id=1, source_target_pairs={{0,1},{1,0},{2,3},{3,2},{4,5},{5,4},{6,7},{7,6},{8,9},{9,8},{10,11... | collective-permute-start | bytes 491528 | tf_op jit(solution)/shard_map/ppermute | solution.py:293
  108.4 9.8 %collective-permute-start.22 = (bf16[1,8,2176]{2,1,0:T(8,128)(2,1)S(1)}, bf16[1,8,2176]{2,1,0:T(8,128)(2,1)S(1)}, u32[]{:S(2)}, u32[]{:S(2)}) collective-permute-start(bf16[1,8,2176]{2,1,0:T(8,128)(2,1)S(1)} %bitcast.7), channel_id=1, source_target_pairs={{0,12},{1,13},{2,14},{3,15},{4,8},{5,9},{6,10},{7,11},{8,4},{9,5},... | collective-permute-start | bytes 104456 | tf_op jit(solution)/shard_map/ppermute | solution.py:293
  108.4 9.8 %collective-permute-start.21 = (bf16[1,8,2176]{2,1,0:T(8,128)(2,1)S(1)}, bf16[1,8,2176]{2,1,0:T(8,128)(2,1)S(1)}, u32[]{:S(2)}, u32[]{:S(2)}) collective-permute-start(bf16[1,8,2176]{2,1,0:T(8,128)(2,1)S(1)} %bitcast.8), channel_id=1, source_target_pairs={{0,8},{1,9},{2,10},{3,11},{4,12},{5,13},{6,14},{7,15},{8,0},{9,1},... | collective-permute-start | bytes 104456 | tf_op jit(solution)/shard_map/ppermute | solution.py:293
  111.9 6.3 %collective-permute-start.20 = (bf16[1,8,2176]{2,1,0:T(8,128)(2,1)S(1)}, bf16[1,8,2176]{2,1,0:T(8,128)(2,1)S(1)}, u32[]{:S(2)}, u32[]{:S(2)}) collective-permute-start(bf16[1,8,2176]{2,1,0:T(8,128)(2,1)S(1)} %bitcast.9), channel_id=1, source_target_pairs={{0,4},{1,5},{2,6},{3,7},{4,0},{5,1},{6,2},{7,3},{8,12},{9,13},{10,... | collective-permute-start | bytes 104456 | tf_op jit(solution)/shard_map/ppermute | solution.py:293
  118.3 5.3 %collective-permute-start.23 = (bf16[4,8,2176]{2,1,0:T(8,128)(2,1)S(1)}, bf16[4,8,2176]{2,1,0:T(8,128)(2,1)S(1)}, u32[]{:S(2)}, u32[]{:S(2)}) collective-permute-start(bf16[4,8,2176]{2,1,0:T(8,128)(2,1)S(1)} %pad_maximum_fusion.1), channel_id=1, source_target_pairs={{0,2},{1,3},{2,0},{3,1},{4,6},{5,7},{6,4},{7,5},{8,10},{9,11},{10,... | collective-permute-start | bytes 417800 | tf_op jit(solution)/shard_map/ppermute | solution.py:293
  135.6 5.5 %collective-permute-start.27 = (f32[8,128]{1,0:T(8,128)S(1)}, f32[8,128]{1,0:T(8,128)S(1)}, u32[]{:S(2)}, u32[]{:S(2)}) collective-permute-start(f32[8,128]{1,0:T(8,128)S(1)} %get-tuple-element.33), channel_id=1, source_target_pairs={{0,12},{1,13},{2,14},{3,15},{4,8},{5,9},{6,10},{7,11},{8,4},{9,5},... | collective-permute-start | bytes 12296 | tf_op jit(solution)/shard_map/ppermute | solution.py:293
  135.7 5.4 %collective-permute-start.26 = (f32[8,128]{1,0:T(8,128)S(1)}, f32[8,128]{1,0:T(8,128)S(1)}, u32[]{:S(2)}, u32[]{:S(2)}) collective-permute-start(f32[8,128]{1,0:T(8,128)S(1)} %get-tuple-element.33), channel_id=1, source_target_pairs={{0,8},{1,9},{2,10},{3,11},{4,12},{5,13},{6,14},{7,15},{8,0},{9,1},... | collective-permute-start | bytes 12296 | tf_op jit(solution)/shard_map/ppermute | solution.py:293
  (10 other events, 54.0 us)

commit v8 on v7

--- a/solution.py
+++ b/solution.py
@@ -14,7 +14,7 @@
 DIAGONAL = float(1.0 - SCALE * float(np.float32(1.0 / SCALE).astype(jnp.bfloat16)))
 KDIM = 128
 ROWS = 512
-PARTS = 4
+PARTS = 2
 COLS = 512
 SUB = 64
 FRONT = 3
@@ -22,6 +22,7 @@
 TAIL = 128
 BF16 = jnp.bfloat16
 F32 = jnp.float32
+CONTRACT_LANES = (((1,), (1,)), ((), ()))
 
 
 def split_three(value):
@@ -53,17 +54,6 @@
     return jnp.transpose(jnp.concatenate([feat, feat, feat, norm_rows(norm, 3)], axis=0))
 
 
-def psi_chain(dist):
-    dist = jnp.maximum(dist, 1e-30)
-    radius = dist * lax.rsqrt(dist)
-    u = jnp.maximum(SHRINK - radius, 0.0)
-    two = u * u
-    four = two * two
-    eight = four * four
-    sixteen = eight * eight
-    return (sixteen * two * (u - two)).astype(BF16)
-
-
 def psi_power(dist):
     dist = jnp.maximum(dist, 1e-30)
     radius = dist * lax.rsqrt(dist)
@@ -71,36 +61,88 @@
     return (jnp.exp2(19.0 * lax.log2(u)) * (1.0 - u)).astype(BF16)
 
 
-def tile_unit(left, right, vec, psis, tile_ref):
+def tile_unit(left, right, vec, tile_ref):
     dist = jnp.dot(left, right, preferred_element_type=F32)
     parts = []
-    for index, sub in enumerate(range(0, left.shape[0], SUB)):
-        part = psis[index % len(psis)](dist[sub : sub + SUB])
+    for sub in range(0, left.shape[0], SUB):
+        part = psi_power(dist[sub : sub + SUB])
         tile_ref[sub : sub + SUB, :] = part
         parts.append(part)
     return jnp.dot(vec, jnp.concatenate(parts, axis=0), preferred_element_type=F32)
 
 
 def unpack(pay):
-    half = pay.shape[1]
     return jnp.concatenate([pay[:32], pay[32:64]], axis=1), jnp.concatenate([pay[64:72], pay[72:80]], axis=1)
 
 
-def own_kernel(part, pay_ref, right_ref, arrived_ref, tile_ref, sum_ref, left_ref, vec_ref):
-    @pl.when(pl.program_id(0) == 0)
-    def _():
-        feat, vec = unpack(pay_ref[...])
-        begin = part * ROWS
-        left_ref[...] = other_factor(feat[:, begin : begin + ROWS])
-        vec_ref[...] = vec[:, begin : begin + ROWS]
-
-    sum_ref[...] = tile_unit(
-        left_ref[...], right_ref[...], vec_ref[...], (psi_power, psi_chain), tile_ref
+def own_blocks(count):
+    return [(row, col) for row in range(count) for col in range(row, count)]
+
+
+def own_kernel(
+    pay_ref, right_ref, list_ref, out_ref, sum_ref, list_out_ref,
+    left_ref, vec_ref, tile_ref, sem_ref,
+):
+    list_out_ref[...] = list_ref[...]
+    feat, vec = unpack(pay_ref[...])
+    left_ref[...] = other_factor(feat)
+    vec_ref[...] = vec
+    sum_ref[...] = jnp.zeros_like(sum_ref)
+    count = feat.shape[1] // ROWS
+    piece = lambda index: pl.ds(pl.multiple_of(index * ROWS, ROWS), ROWS)
+    save = lambda at: pltpu.make_async_copy(tile_ref.at[at], out_ref.at[at], sem_ref.at[at])
+
+    def row_step(row, at):
+        def col_step(col, at):
+            sum_ref[:, piece(col)] += tile_unit(
+                left_ref[piece(row), :], right_ref[:, piece(col)], vec_ref[:, piece(row)],
+                tile_ref.at[at],
+            )
+            save(at).start()
+
+            @pl.when(row != col)
+            def _():
+                sum_ref[:, piece(row)] += lax.dot_general(
+                    vec_ref[:, piece(col)], tile_ref[at], CONTRACT_LANES,
+                    preferred_element_type=F32,
+                )
+
+            return at + 1
+
+        return lax.fori_loop(row, count, col_step, at)
+
+    lax.fori_loop(0, count, row_step, 0)
+    for at in range(tile_ref.shape[0]):
+        save(at).wait()
+
+
+def own_again_kernel(first, blocks, in_ref, vec_ref, sum_ref, tile_ref, sem_ref):
+    load = lambda index: pltpu.make_async_copy(
+        in_ref.at[first + index], tile_ref.at[index], sem_ref.at[index]
     )
-
-
-def factor_kernel(pay_ref, right_ref):
-    right_ref[...] = own_factor(unpack(pay_ref[...])[0])
+    for index in range(len(blocks)):
+        load(index).start()
+    sum_ref[...] = jnp.zeros_like(sum_ref)
+    piece = lambda index: slice(index * ROWS, (index + 1) * ROWS)
+    for index, (row, col) in enumerate(blocks):
+        load(index).wait()
+        sum_ref[:, piece(col)] += jnp.dot(
+            vec_ref[:, piece(row)], tile_ref[index], preferred_element_type=F32
+        )
+        if row != col:
+            sum_ref[:, piece(row)] += lax.dot_general(
+                vec_ref[:, piece(col)], tile_ref[index], CONTRACT_LANES, preferred_element_type=F32
+            )
+
+
+def payload_kernel(feat_ref, rhs_ref, pay_ref, right_ref):
+    half = feat_ref.shape[1] // 2
+    feat = feat_ref[...]
+    rounded = rhs_ref[...].astype(BF16)
+    pay_ref[:32] = feat[:, :half]
+    pay_ref[32:64] = feat[:, half:]
+    pay_ref[64:80] = jnp.concatenate([rounded[:, :half], rounded[:, half:]], axis=0)
+    right_ref[...] = own_factor(feat)
 
 
 def find_partners(lists_ref, me, slots_ref):
@@ -119,9 +161,8 @@
     slots_ref[0] = total
 
 
-def pair_kernel(lists_ref, me_ref, right_ref, rhs_ref, var_ref, *refs):
-    first_refs = refs[:PARTS]
-    block_refs = refs[PARTS:-9]
+def pair_kernel(block_at, lists_ref, me_ref, right_ref, rhs_ref, var_ref, *refs):
+    first_ref, block_refs = refs[0], refs[1:-9]
     front_ref, back_ref, image_ref, send_ref, slots_ref = refs[-9:-4]
     left_ref, vec_ref, pay_ref, sem_ref = refs[-4:]
     slot, step = pl.program_id(0), pl.program_id(1)
@@ -129,17 +170,19 @@
 
     def fetch(which):
         place = slots_ref[1 + which]
-        for at, block_ref in enumerate(block_refs):
+        for at, (index, row) in enumerate(block_at):
             @pl.when(place == at)
             def _():
                 pltpu.make_async_copy(
-                    block_ref, pay_ref.at[which % 2], sem_ref.at[which % 2]
+                    block_refs[index].at[pl.ds(row, pay_ref.shape[1])],
+                    pay_ref.at[which % 2],
+                    sem_ref.at[which % 2],
                 ).start()
 
     @pl.when((slot == 0) & (step == 0))
     def _():
         find_partners(lists_ref, me_ref[0], slots_ref)
-        sum_ref[...] = functools.reduce(jnp.add, [first_ref[...] for first_ref in first_refs])
+        sum_ref[...] = first_ref[...]
 
         @pl.when(slots_ref[0] > 0)
         def _():
@@ -170,7 +213,7 @@
                 def unit(index, carry):
                     cols = pl.ds(pl.multiple_of(index * COLS, COLS), COLS)
                     sum_ref[:, cols] += tile_unit(
-                        left, right_ref[:, cols], vec, (psi_power,), tile_ref.at[0, :, cols]
+                        left, right_ref[:, cols], vec, tile_ref.at[0, :, cols]
                     )
                     return carry
 
@@ -190,18 +233,6 @@
         for place, piece in enumerate(pieces):
             tail = jnp.where(lane == place, piece, tail)
         send_ref[:, width:] = tail.astype(BF16)
-
-
-def own_again_kernel(part, tile_ref, vec_ref, sum_ref):
-    step = pl.program_id(0)
-    rows = tile_ref.shape[0]
-
-    @pl.when(step == 0)
-    def _():
-        sum_ref[...] = jnp.zeros_like(sum_ref)
-
-    at = pl.multiple_of(part * ROWS + step * rows, rows)
-    sum_ref[...] += jnp.dot(vec_ref[:, pl.ds(at, rows)], tile_ref[...], preferred_element_type=F32)
 
 
 def again_kernel(
@@ -326,17 +357,40 @@
 
 
 def tree_gather(value, count):
-    blocks = value[None]
+    blocks, out = value[None], []
     for masks in gather_levels(count):
         blocks = jnp.concatenate([blocks] + [swap(blocks, mask, count) for mask in masks], axis=0)
-    return blocks
-
-
-def pass_on(value, count):
+        out.append(blocks)
+    return out
+
+
+def gate(block, *behind):
+    return pl.pallas_call(
+        lambda *refs: None,
+        in_specs=[pl.BlockSpec(memory_space=pl.ANY)] * (1 + len(behind)),
+        out_specs=pl.BlockSpec(memory_space=pl.ANY),
+        out_shape=jax.ShapeDtypeStruct(block.shape, block.dtype),
+        input_output_aliases={0: 0},
+        name="gate",
+    )(block, *behind)
+
+
+def pass_on(value, behind, lists, count):
+    rows = value.shape[0]
+    *early, (mask,) = gather_levels(count)
     blocks = [value]
-    for masks in gather_levels(count):
-        blocks = blocks + [swap(block, mask, count) for mask in masks for block in blocks]
-    return blocks
+    for level, masks in enumerate(early):
+        blocks = blocks + [swap(block, other, count) for other in masks for block in blocks]
+        if level == 0:
+            blocks = blocks[:2] + [gate(block, behind) for block in blocks[2:]]
+    blocks[-1] = gate(blocks[-1], lists[-2])
+    places = [(block, 0) for block in blocks] + [None] * len(blocks)
+    for kinds in ((0, 1), (2,), (3,)):
+        group = [index for index in range(len(blocks)) if index % 4 in kinds]
+        arrived = swap(jnp.concatenate([blocks[index] for index in group], axis=0), mask, count)
+        for at, index in enumerate(group):
+            places[len(blocks) + index] = (arrived, at * rows)
+    return places
 
 
 def local(features, right_side, variance, hilbert_order, tile_list):
@@ -349,48 +403,46 @@
     params = pltpu.CompilerParams(vmem_limit_bytes=10 * 1024 * 1024)
     var_row = variance[None, :]
 
-    rounded = right_side.astype(BF16)
-    half = width // 2
-    payload = jnp.concatenate(
-        [features[:, :half], features[:, half:], rounded[:, :half], rounded[:, half:]], axis=0
-    )
-    every = pass_on(payload, count)
     whole = lambda *ignored: (0, 0)
     row_spec = pl.BlockSpec(right_side.shape, whole)
     var_spec = pl.BlockSpec(var_row.shape, whole)
-    right = pl.pallas_call(
-        factor_kernel,
-        out_shape=shape((KDIM, width), BF16),
+    pay_shape = (80, width // 2)
+    payload, right = pl.pallas_call(
+        payload_kernel,
+        out_shape=[shape(pay_shape, BF16), shape((KDIM, width), BF16)],
         compiler_params=params,
-        name="own_factor",
-    )(payload)
-    lists = tree_gather(tile_list[0, :, 1], count)
+        name="payload",
+    )(features, right_side)
+    any_spec = pl.BlockSpec(memory_space=pl.ANY)
+    blocks = own_blocks(width // ROWS)
+    coupled = tile_list[:, :, 1]
+    list_spec = pl.BlockSpec(coupled.shape, whole)
+    own_tiles, own_sum, coupled = pl.pallas_call(
+        own_kernel,
+        in_specs=[pl.BlockSpec(payload.shape, whole), pl.BlockSpec(right.shape, whole), list_spec],
+        out_specs=[any_spec, row_spec, list_spec],
+        out_shape=[
+            pltpu.HBM((len(blocks), ROWS, ROWS), BF16),
+            shape(right_side.shape, F32),
+            shape(coupled.shape, jnp.int32),
+        ],
+        scratch_shapes=[
+            pltpu.VMEM((width, KDIM), BF16),
+            pltpu.VMEM((rhs_count, width), BF16),
+            pltpu.VMEM((len(blocks), ROWS, ROWS), BF16),
+            pltpu.SemaphoreType.DMA((len(blocks),)),
+        ],
+        compiler_params=params,
+        cost_estimate=pl.CostEstimate(
+            flops=9_000_000_000, bytes_accessed=2 * len(blocks) * ROWS * ROWS, transcendentals=0
+        ),
+        name="own_tile",
+    )(payload, right, coupled)
+    lists = tree_gather(coupled[0], count)
+    places = pass_on(payload, own_sum, lists, count)
+    arrays = list({id(array): array for array, _ in places}.values())
+    block_at = [([id(array) for array in arrays].index(id(array)), row) for array, row in places]
     me = jnp.full((1,), lax.axis_index("row"), jnp.int32)
-    own_parts = [
-        pl.pallas_call(
-            functools.partial(own_kernel, part),
-            grid=(width // COLS,),
-            in_specs=[
-                pl.BlockSpec(payload.shape, whole),
-                pl.BlockSpec((KDIM, COLS), lambda i: (0, i)),
-                pl.BlockSpec(memory_space=pl.ANY),
-            ],
-            out_specs=[
-                pl.BlockSpec((ROWS, COLS), lambda i: (0, i)),
-                pl.BlockSpec((rhs_count, COLS), lambda i: (0, i)),
-            ],
-            out_shape=[pltpu.HBM((ROWS, width), BF16), shape(right_side.shape, F32)],
-            scratch_shapes=[pltpu.VMEM((ROWS, KDIM), BF16), pltpu.VMEM((rhs_count, ROWS), BF16)],
-            compiler_params=params,
-            cost_estimate=pl.CostEstimate(
-                flops=4_000_000_000, bytes_accessed=2 * ROWS * width, transcendentals=0
-            ),
-            name=f"own_tile_{part}",
-        )(payload, right, every[part or PARTS])
-        for part in range(PARTS)
-    ]
-    own_tiles = [part[0] for part in own_parts]
-    own_sums = [part[1] for part in own_parts]
 
     def front_at(k, i, *ignored):
         return (jnp.minimum(k, FRONT - 1), jnp.where(k < FRONT, i, steps - 1), 0)
@@ -401,7 +453,7 @@
     tile_specs = [pl.BlockSpec((1, ROWS, width), front_at), pl.BlockSpec((1, ROWS, width), back_at)]
     send_shape = (rhs_count, width + TAIL)
     front_tiles, back_tiles, image, send, slots = pl.pallas_call(
-        pair_kernel,
+        functools.partial(pair_kernel, block_at),
         grid_spec=pltpu.PrefetchScalarGridSpec(
             num_scalar_prefetch=2,
             grid=(most, steps),
@@ -410,8 +462,8 @@
                 row_spec,
                 var_spec,
             ]
-            + [row_spec] * PARTS
-            + [pl.BlockSpec(memory_space=pl.ANY)] * count,
+            + [row_spec]
+            + [any_spec] * len(arrays),
             out_specs=tile_specs
             + [
                 row_spec,
@@ -430,29 +482,32 @@
         ],
         compiler_params=params,
         name="pair_tiles",
-    )(lists, me, right, right_side, var_row, *own_sums, *every)
+    )(lists[-1], me, right, right_side, var_row, own_sum, *arrays)
     front_tiles = pltpu.with_memory_space_constraint(front_tiles, pltpu.VMEM)
     back_tiles = pltpu.with_memory_space_constraint(back_tiles, pltpu.HBM)
 
-    every_send = tree_gather(send, count)
-    own_again = [
-        pl.pallas_call(
-            functools.partial(own_again_kernel, part),
-            grid=(2,),
-            in_specs=[
-                pl.BlockSpec((ROWS // 2, width), lambda i: (i, 0)),
-                pl.BlockSpec(send_shape, whole),
-            ],
-            out_specs=row_spec,
-            out_shape=shape(right_side.shape, F32),
-            compiler_params=params,
-            cost_estimate=pl.CostEstimate(
-                flops=3_000_000_000, bytes_accessed=2 * ROWS * width, transcendentals=0
-            ),
-            name=f"own_again_{part}",
-        )(pltpu.with_memory_space_constraint(tile, pltpu.HBM), send)
-        for part, tile in enumerate(own_tiles)
-    ]
+    every_send = tree_gather(send, count)[-1]
+    own_again = []
+    part = -(-len(blocks) // PARTS)
+    for first in range(0, len(blocks), part):
+        here = blocks[first : first + part]
+        own_again.append(
+            pl.pallas_call(
+                functools.partial(own_again_kernel, first, here),
+                in_specs=[any_spec, pl.BlockSpec(send_shape, whole)],
+                out_specs=row_spec,
+                out_shape=shape(right_side.shape, F32),
+                scratch_shapes=[
+                    pltpu.VMEM((len(here), ROWS, ROWS), BF16),
+                    pltpu.SemaphoreType.DMA((len(here),)),
+                ],
+                compiler_params=params,
+                cost_estimate=pl.CostEstimate(
+                    flops=5_000_000_000, bytes_accessed=2 * len(here) * ROWS * ROWS, transcendentals=0
+                ),
+                name=f"own_again_{first}",
+            )(pltpu.with_memory_space_constraint(own_tiles, pltpu.HBM), send)
+        )
     dots_spec = pl.BlockSpec((rhs_count, TAIL), whole)
     rows, dots, steps_one = pl.pallas_call(
         again_kernel,
@@ -461,7 +516,7 @@
             grid=(most, steps),
             in_specs=[
                 tile_specs[0],
-                pl.BlockSpec(memory_space=pl.ANY),
+                any_spec,
                 pl.BlockSpec((1,) + send_shape, lambda k, i, s: (s[1 + k], 0, 0)),
                 pl.BlockSpec((count, rhs_count, TAIL), lambda k, i, s: (0, 0, width // TAIL)),
                 row_spec,

time: 147 us -> 148 us (level)
  Pallas kernels: 97.7 us -> 51.9 us
  starting transfers between devices: 31.1 us -> 62 us
  waiting for transfers between devices: 13.9 us -> 24.4 us
  local copies, waits for them, and re-layouts: 1.73 us -> 4.62 us
  other arithmetic: 1.89 us -> 4.41 us
    pallas_call x10 -> x8, Pallas kernels: 86.2 us -> 45.9 us  [the longest x1 32.1 us: local(): pl.pallas_call(functools.partial(pair_kernel, block_at), grid_spec=pltpu....]
    ppermute x31 -> x26, starting transfers between devices: 31.1 us -> 62 us  [swap(): return lax.ppermute(value, 'row', [(i, i ^ mask) for i in range(count)])]
    ppermute x31 -> x26, waiting for transfers between devices: 13.9 us -> 24.4 us  [swap(): return lax.ppermute(value, 'row', [(i, i ^ mask) for i in range(count)])]
    pallas_call x1, Pallas kernels: 10 us -> 4.54 us  [local(): pl.pallas_call(again_kernel, grid_spec=pltpu.PrefetchScalarGridSpec(num_s...]
    concatenate x1 -> x3, other arithmetic: 0.01 us -> 3.38 us  [pass_on(): jnp.concatenate([blocks[index] for index in group], axis=0)]
    unnamed x10 -> x32, local copies, waits for them, and re-layouts: 0.05 us -> 3.26 us
  transfers between devices with their start and end apart: 31 -> 26, of which waited for: 9 -> 9; matrix products, arithmetic and copies ran while one was open for 1% -> 3% of each run, Pallas kernels for 16% -> 10%
where the time goes in v8:
time: 148 us
  starting transfers between devices  62 us (42%)
  Pallas kernels  51.9 us (35%)
  waiting for transfers between devices  24.4 us (16%)
  local copies, waits for them, and re-layouts  4.62 us (3%)
  other arithmetic  4.41 us (3%)
    ppermute x26, starting transfers between devices, swap(): return lax.ppermute(value, 'row', [(i, i ^ mask) for i in range(count)])  62 us
    pallas_call x1, Pallas kernels, local(): pl.pallas_call(functools.partial(pair_kernel, block_at), grid_spec=pltpu....  32.1 us
    ppermute x26, waiting for transfers between devices, swap(): return lax.ppermute(value, 'row', [(i, i ^ mask) for i in range(count)])  24.4 us
    pallas_call x1, Pallas kernels, local(): pl.pallas_call(own_kernel, in_specs=[pl.BlockSpec(payload.shape, whole),...  9.36 us
    pallas_call x1, Pallas kernels, local(): pl.pallas_call(again_kernel, grid_spec=pltpu.PrefetchScalarGridSpec(num_s...  4.54 us
    pallas_call x2, Pallas kernels, local(): pl.pallas_call(functools.partial(own_again_kernel, first, here), in_specs...  4.36 us
    concatenate x3, other arithmetic, pass_on(): jnp.concatenate([blocks[index] for index in group], axis=0)  3.38 us
    unnamed x32, local copies, waits for them, and re-layouts  3.26 us
  transfers between devices with their start and end apart: 26, of which 9 were waited for; matrix products, arithmetic and copies ran while one was open for 3% of the time, Pallas kernels for 10%

profile of v8, /device:TPU:0, one launch (start us, length us, event | category | flops | bytes accessed | tf_op | source)
XLA Modules:
  0.0 148.2 jit_solution(10939924715181692893)
XLA Ops:
  1.5 0.9 copy-done.10
  2.5 3.0 %collective-permute-start.8 = (bf16[80,1024]{1,0:T(8,128)(2,1)S(1)}, bf16[80,1024]{1,0:T(8,128)(2,1)S(1)}, u32[]{:S(2)}, u32[]{:S(2)}) collective-permute-start(bf16[80,1024]{1,0:T(8,128)(2,1)S(1)} %get-tuple-element.15.pay_ref.refs_1_), channel_id=1, source_target_pairs={{0,2},{1,3},{2,0},{3,1},{4,6},{5,7},{6,4},{7,5},{8,10},{9,11},{10,... | collective-permute-start | bytes 491528 | tf_op jit(solution)/shard_map/ppermute | solution.py:324
  5.5 3.6 %collective-permute-start.7 = (bf16[80,1024]{1,0:T(8,128)(2,1)S(1)}, bf16[80,1024]{1,0:T(8,128)(2,1)S(1)}, u32[]{:S(2)}, u32[]{:S(2)}) collective-permute-start(bf16[80,1024]{1,0:T(8,128)(2,1)S(1)} %get-tuple-element.15.pay_ref.refs_1_), channel_id=1, source_target_pairs={{0,12},{1,13},{2,14},{3,15},{4,8},{5,9},{6,10},{7,11},{8,4},{9,5},... | collective-permute-start | bytes 491528 | tf_op jit(solution)/shard_map/ppermute | solution.py:324
  10.6 8.8 %collective-permute-done.5.refs_2_ = bf16[80,1024]{1,0:T(8,128)(2,1)S(1)} collective-permute-done((bf16[80,1024]{1,0:T(8,128)(2,1)S(1)}, bf16[80,1024]{1,0:T(8,128)(2,1)S(1)}, u32[]{:S(2)}, u32[]{:S(2)}) %collective-permute-start.5) | collective-permute-done | bytes 163872 | tf_op jit(solution)/shard_map/ppermute | solution.py:324
  19.9 9.4 %own_tile.1 = (bf16[10,512,512]{2,1,0:T(8,128)(2,1)}, f32[8,2048]{1,0:T(8,128)S(1)}, s32[1,5]{1,0:T(1,128)S(1)}) custom-call(bf16[80,1024]{1,0:T(8,128)(2,1)S(1)} %get-tuple-element.15.pay_ref.refs_1_, bf16[128,2048]{1,0:T(8,128)(2,1)S(1)} %get-tuple-element.16.right_ref, s32[1,5]{1,0:T(1,128)S(1)} %slice_bitcast_fusion.list_ref), custom_call_target="tpu_custom_call" | custom-call | flops 8999999488 | bytes 5242880 | tf_op jit(solution)/shard_map/own_tile/pallas_call | solution.py:420
  29.9 1.2 collective-permute-start.2
  31.2 2.7 %collective-permute-start.1 = (s32[1,5]{1,0:T(1,128)S(1)}, s32[1,5]{1,0:T(1,128)S(1)}, u32[]{:S(2)}, u32[]{:S(2)}) collective-permute-start(s32[1,5]{1,0:T(1,128)S(1)} %get-tuple-element.17), channel_id=1, source_target_pairs={{0,8},{1,9},{2,10},{3,11},{4,12},{5,13},{6,14},{7,15},{8,0},{9,1},... | collective-permute-start | bytes 68 | tf_op jit(solution)/shard_map/ppermute | solution.py:324
  34.6 1.6 %collective-permute-start.10 = (bf16[80,1024]{1,0:T(8,128)(2,1)}, bf16[80,1024]{1,0:T(8,128)(2,1)S(1)}, u32[]{:S(2)}, u32[]{:S(2)}) collective-permute-start(bf16[80,1024]{1,0:T(8,128)(2,1)} %gate.3.refs_3_), channel_id=1, source_target_pairs={{0,2},{1,3},{2,0},{3,1},{4,6},{5,7},{6,4},{7,5},{8,10},{9,11},{10,... | collective-permute-start | bytes 491528 | tf_op jit(solution)/shard_map/ppermute | solution.py:324
  37.6 1.6 %collective-permute-start.3 = (s32[4,5]{1,0:T(4,128)S(1)}, s32[4,5]{1,0:T(4,128)S(1)}, u32[]{:S(2)}, u32[]{:S(2)}) collective-permute-start(s32[4,5]{1,0:T(4,128)S(1)} %pad_add_fusion), channel_id=1, source_target_pairs={{0,2},{1,3},{2,0},{3,1},{4,6},{5,7},{6,4},{7,5},{8,10},{9,11},{10,... | collective-permute-start | bytes 248 | tf_op jit(solution)/shard_map/ppermute | solution.py:324
  39.2 3.2 %collective-permute-done.3 = s32[4,5]{1,0:T(4,128)S(1)} collective-permute-done((s32[4,5]{1,0:T(4,128)S(1)}, s32[4,5]{1,0:T(4,128)S(1)}, u32[]{:S(2)}, u32[]{:S(2)}) %collective-permute-start.3) | collective-permute-done | bytes 112 | tf_op jit(solution)/shard_map/ppermute | solution.py:324
  43.7 1.7 %pad_maximum_fusion.2 = bf16[160,1024]{1,0:T(8,128)(2,1)} fusion(bf16[80,1024]{1,0:T(8,128)(2,1)} %gate.5.refs_8_, bf16[80,1024]{1,0:T(8,128)(2,1)S(1)} %copy-done.3), kind=kLoop, calls=%fused_computation.2 | loop fusion | flops 655360 | bytes 655360 | tf_op jit(solution)/shard_map/concatenate | solution.py:390
  46.7 1.6 %collective-permute-done.4 = s32[8,5]{1,0:T(8,128)S(1)} collective-permute-done((s32[8,5]{1,0:T(8,128)S(1)}, s32[8,5]{1,0:T(8,128)S(1)}, u32[]{:S(2)}, u32[]{:S(2)}) %collective-permute-start.4) | collective-permute-done | bytes 192 | tf_op jit(solution)/shard_map/ppermute | solution.py:324
  48.5 32.1 %pair_tiles.1 = (bf16[3,2048,2048]{2,1,0:T(8,128)(2,1)S(1)}, bf16[2,2048,2048]{2,1,0:T(8,128)(2,1)}, f32[8,2048]{1,0:T(8,128)S(1)}, bf16[8,2176]{1,0:T(8,128)(2,1)S(1)}, s32[7]{0:T(128)S(1)}) custom-call(s32[16,5]{1,0:T(8,128)S(1)} %concatenate.33.lists_ref, s32[1]{0:T(128)} %bitcast.1.me_ref, bf16[128,2048]{1,0:T(8,128)(2,1)S(1)} %get-tuple-element.16.right_ref, ...), custom_call_target="tpu_custom_call" | custom-call | tf_op jit(solution)/shard_map/pair_tiles/pallas_call | solution.py:455
  80.6 34.1 %collective-permute-start.17 = (bf16[1,8,2176]{2,1,0:T(8,128)(2,1)S(1)}, bf16[1,8,2176]{2,1,0:T(8,128)(2,1)S(1)}, u32[]{:S(2)}, u32[]{:S(2)}) collective-permute-start(bf16[1,8,2176]{2,1,0:T(8,128)(2,1)S(1)} %bitcast.7), channel_id=1, source_target_pairs={{0,12},{1,13},{2,14},{3,15},{4,8},{5,9},{6,10},{7,11},{8,4},{9,5},... | collective-permute-start | bytes 104456 | tf_op jit(solution)/shard_map/ppermute | solution.py:324
  115.3 2.2 %own_again_5.1.refs_1_ = f32[8,2048]{1,0:T(8,128)S(1)} custom-call(bf16[10,512,512]{2,1,0:T(8,128)(2,1)} %get-tuple-element.24.in_ref, bf16[8,2176]{1,0:T(8,128)(2,1)S(1)} %get-tuple-element.22.vec_ref), custom_call_target="tpu_custom_call" | custom-call | flops 5000000000 | bytes 2621440 | tf_op jit(solution)/shard_map/own_again_5/pallas_call | solution.py:495
  117.5 2.0 %collective-permute-done.16 = bf16[1,8,2176]{2,1,0:T(8,128)(2,1)S(1)} collective-permute-done((bf16[1,8,2176]{2,1,0:T(8,128)(2,1)S(1)}, bf16[1,8,2176]{2,1,0:T(8,128)(2,1)S(1)}, u32[]{:S(2)}, u32[]{:S(2)}) %collective-permute-start.16) | collective-permute-done | bytes 34848 | tf_op jit(solution)/shard_map/ppermute | solution.py:324
  120.2 4.4 %collective-permute-done.18 = bf16[4,8,2176]{2,1,0:T(8,128)(2,1)S(1)} collective-permute-done((bf16[4,8,2176]{2,1,0:T(8,128)(2,1)S(1)}, bf16[4,8,2176]{2,1,0:T(8,128)(2,1)S(1)}, u32[]{:S(2)}, u32[]{:S(2)}) %collective-permute-start.18) | collective-permute-done | bytes 139296 | tf_op jit(solution)/shard_map/ppermute | solution.py:324
  124.8 2.2 %own_again_0.1.refs_0_ = f32[8,2048]{1,0:T(8,128)S(1)} custom-call(bf16[10,512,512]{2,1,0:T(8,128)(2,1)} %get-tuple-element.24.in_ref, bf16[8,2176]{1,0:T(8,128)(2,1)S(1)} %get-tuple-element.22.vec_ref), custom_call_target="tpu_custom_call" | custom-call | flops 5000000000 | bytes 2621440 | tf_op jit(solution)/shard_map/own_again_0/pallas_call | solution.py:495
  127.0 4.5 %pair_again.1 = (f32[32,2048]{1,0:T(8,128)S(1)}, f32[8,128]{1,0:T(8,128)S(1)}, f32[8,128]{1,0:T(8,128)S(1)}) custom-call(s32[7]{0:T(128)S(1)} %get-tuple-element.19.slots_ref, bf16[3,2048,2048]{2,1,0:T(8,128)(2,1)S(1)} %get-tuple-element.20.front_ref, bf16[2,2048,2048]{2,1,0:T(8,128)(2,1)} %get-tuple-element.21.back_ref, ...), custom_call_target="tpu_custom_call" | custom-call | tf_op jit(solution)/shard_map/pair_again/pallas_call | solution.py:512
  131.6 7.3 %collective-permute-start.22 = (f32[8,128]{1,0:T(8,128)S(1)}, f32[8,128]{1,0:T(8,128)S(1)}, u32[]{:S(2)}, u32[]{:S(2)}) collective-permute-start(f32[8,128]{1,0:T(8,128)S(1)} %get-tuple-element.27), channel_id=1, source_target_pairs={{0,12},{1,13},{2,14},{3,15},{4,8},{5,9},{6,10},{7,11},{8,4},{9,5},... | collective-permute-start | bytes 12296 | tf_op jit(solution)/shard_map/ppermute | solution.py:324
  139.5 0.9 collective-permute-done.22
  140.5 2.9 %collective-permute-done.21 = f32[8,128]{1,0:T(8,128)S(1)} collective-permute-done((f32[8,128]{1,0:T(8,128)S(1)}, f32[8,128]{1,0:T(8,128)S(1)}, u32[]{:S(2)}, u32[]{:S(2)}) %collective-permute-start.21) | collective-permute-done | bytes 4128 | tf_op jit(solution)/shard_map/ppermute | solution.py:324
  143.8 1.6 %collective-permute-start.23 = (f32[8,128]{1,0:T(8,128)S(1)}, f32[8,128]{1,0:T(8,128)S(1)}, u32[]{:S(2)}, u32[]{:S(2)}) collective-permute-start(f32[8,128]{1,0:T(8,128)S(1)} %add_add_fusion.1), channel_id=1, source_target_pairs={{0,1},{1,0},{2,3},{3,2},{4,5},{5,4},{6,7},{7,6},{8,9},{9,8},{10,11... | collective-permute-start | bytes 12296 | tf_op jit(solution)/shard_map/ppermute | solution.py:324
  145.4 1.5 curve_order.1
  (84 shorter events, 12.3 us)
Async XLA Ops:
  2.5 32.1 %collective-permute-start.8 = (bf16[80,1024]{1,0:T(8,128)(2,1)S(1)}, bf16[80,1024]{1,0:T(8,128)(2,1)S(1)}, u32[]{:S(2)}, u32[]{:S(2)}) collective-permute-start(bf16[80,1024]{1,0:T(8,128)(2,1)S(1)} %get-tuple-element.15.pay_ref.refs_1_), channel_id=1, source_target_pairs={{0,2},{1,3},{2,0},{3,1},{4,6},{5,7},{6,4},{7,5},{8,10},{9,11},{10,... | collective-permute-start | bytes 491528 | tf_op jit(solution)/shard_map/ppermute | solution.py:324
  5.5 25.6 %collective-permute-start.7 = (bf16[80,1024]{1,0:T(8,128)(2,1)S(1)}, bf16[80,1024]{1,0:T(8,128)(2,1)S(1)}, u32[]{:S(2)}, u32[]{:S(2)}) collective-permute-start(bf16[80,1024]{1,0:T(8,128)(2,1)S(1)} %get-tuple-element.15.pay_ref.refs_1_), channel_id=1, source_target_pairs={{0,12},{1,13},{2,14},{3,15},{4,8},{5,9},{6,10},{7,11},{8,4},{9,5},... | collective-permute-start | bytes 491528 | tf_op jit(solution)/shard_map/ppermute | solution.py:324
  9.1 24.8 %collective-permute-start.6 = (bf16[80,1024]{1,0:T(8,128)(2,1)S(1)}, bf16[80,1024]{1,0:T(8,128)(2,1)S(1)}, u32[]{:S(2)}, u32[]{:S(2)}) collective-permute-start(bf16[80,1024]{1,0:T(8,128)(2,1)S(1)} %get-tuple-element.15.pay_ref.refs_1_), channel_id=1, source_target_pairs={{0,8},{1,9},{2,10},{3,11},{4,12},{5,13},{6,14},{7,15},{8,0},{9,1},... | collective-permute-start | bytes 491528 | tf_op jit(solution)/shard_map/ppermute | solution.py:324
  9.1 10.3 %collective-permute-start.5 = (bf16[80,1024]{1,0:T(8,128)(2,1)S(1)}, bf16[80,1024]{1,0:T(8,128)(2,1)S(1)}, u32[]{:S(2)}, u32[]{:S(2)}) collective-permute-start(bf16[80,1024]{1,0:T(8,128)(2,1)S(1)} %get-tuple-element.15.pay_ref.refs_1_), channel_id=1, source_target_pairs={{0,4},{1,5},{2,6},{3,7},{4,0},{5,1},{6,2},{7,3},{8,12},{9,13},{10,... | collective-permute-start | bytes 491528 | tf_op jit(solution)/shard_map/ppermute | solution.py:324
  19.4 16.8 %collective-permute-start.9 = (bf16[80,1024]{1,0:T(8,128)(2,1)S(1)}, bf16[80,1024]{1,0:T(8,128)(2,1)S(1)}, u32[]{:S(2)}, u32[]{:S(2)}) collective-permute-start(bf16[80,1024]{1,0:T(8,128)(2,1)S(1)} %collective-permute-done.5.refs_2_), channel_id=1, source_target_pairs={{0,2},{1,3},{2,0},{3,1},{4,6},{5,7},{6,4},{7,5},{8,10},{9,11},{10,... | collective-permute-start | bytes 491528 | tf_op jit(solution)/shard_map/ppermute | solution.py:324
  29.9 7.6 %collective-permute-start.2 = (s32[1,5]{1,0:T(1,128)S(1)}, s32[1,5]{1,0:T(1,128)S(1)}, u32[]{:S(2)}, u32[]{:S(2)}) collective-permute-start(s32[1,5]{1,0:T(1,128)S(1)} %get-tuple-element.17), channel_id=1, source_target_pairs={{0,12},{1,13},{2,14},{3,15},{4,8},{5,9},{6,10},{7,11},{8,4},{9,5},... | collective-permute-start | bytes 68 | tf_op jit(solution)/shard_map/ppermute | solution.py:324
  31.2 6.4 %collective-permute-start.1 = (s32[1,5]{1,0:T(1,128)S(1)}, s32[1,5]{1,0:T(1,128)S(1)}, u32[]{:S(2)}, u32[]{:S(2)}) collective-permute-start(s32[1,5]{1,0:T(1,128)S(1)} %get-tuple-element.17), channel_id=1, source_target_pairs={{0,8},{1,9},{2,10},{3,11},{4,12},{5,13},{6,14},{7,15},{8,0},{9,1},... | collective-permute-start | bytes 68 | tf_op jit(solution)/shard_map/ppermute | solution.py:324
  33.9 3.7 %collective-permute-start = (s32[1,5]{1,0:T(1,128)S(1)}, s32[1,5]{1,0:T(1,128)S(1)}, u32[]{:S(2)}, u32[]{:S(2)}) collective-permute-start(s32[1,5]{1,0:T(1,128)S(1)} %get-tuple-element.17), channel_id=1, source_target_pairs={{0,4},{1,5},{2,6},{3,7},{4,0},{5,1},{6,2},{7,3},{8,12},{9,13},{10,... | collective-permute-start | bytes 68 | tf_op jit(solution)/shard_map/ppermute | solution.py:324
  34.6 10.8 %collective-permute-start.10 = (bf16[80,1024]{1,0:T(8,128)(2,1)}, bf16[80,1024]{1,0:T(8,128)(2,1)S(1)}, u32[]{:S(2)}, u32[]{:S(2)}) collective-permute-start(bf16[80,1024]{1,0:T(8,128)(2,1)} %gate.3.refs_3_), channel_id=1, source_target_pairs={{0,2},{1,3},{2,0},{3,1},{4,6},{5,7},{6,4},{7,5},{8,10},{9,11},{10,... | collective-permute-start | bytes 491528 | tf_op jit(solution)/shard_map/ppermute | solution.py:324
  36.2 6.8 %collective-permute-start.11 = (bf16[80,1024]{1,0:T(8,128)(2,1)}, bf16[80,1024]{1,0:T(8,128)(2,1)S(1)}, u32[]{:S(2)}, u32[]{:S(2)}) collective-permute-start(bf16[80,1024]{1,0:T(8,128)(2,1)} %gate.4.refs_4_), channel_id=1, source_target_pairs={{0,2},{1,3},{2,0},{3,1},{4,6},{5,7},{6,4},{7,5},{8,10},{9,11},{10,... | collective-permute-start | bytes 491528 | tf_op jit(solution)/shard_map/ppermute | solution.py:324
  37.6 10.9 %collective-permute-start.12 = (bf16[320,1024]{1,0:T(8,128)(2,1)}, bf16[320,1024]{1,0:T(8,128)(2,1)S(1)}, u32[]{:S(2)}, u32[]{:S(2)}) collective-permute-start(bf16[320,1024]{1,0:T(8,128)(2,1)} %pad_maximum_fusion), channel_id=1, source_target_pairs={{0,1},{1,0},{2,3},{3,2},{4,5},{5,4},{6,7},{7,6},{8,9},{9,8},{10,11... | collective-permute-start | bytes 1966088 | tf_op jit(solution)/shard_map/ppermute | solution.py:324
  37.6 4.8 %collective-permute-start.3 = (s32[4,5]{1,0:T(4,128)S(1)}, s32[4,5]{1,0:T(4,128)S(1)}, u32[]{:S(2)}, u32[]{:S(2)}) collective-permute-start(s32[4,5]{1,0:T(4,128)S(1)} %pad_add_fusion), channel_id=1, source_target_pairs={{0,2},{1,3},{2,0},{3,1},{4,6},{5,7},{6,4},{7,5},{8,10},{9,11},{10,... | collective-permute-start | bytes 248 | tf_op jit(solution)/shard_map/ppermute | solution.py:324
  46.2 2.3 %collective-permute-start.14 = (bf16[160,1024]{1,0:T(8,128)(2,1)}, bf16[160,1024]{1,0:T(8,128)(2,1)S(1)}, u32[]{:S(2)}, u32[]{:S(2)}) collective-permute-start(bf16[160,1024]{1,0:T(8,128)(2,1)} %pad_maximum_fusion.2), channel_id=1, source_target_pairs={{0,1},{1,0},{2,3},{3,2},{4,5},{5,4},{6,7},{7,6},{8,9},{9,8},{10,11... | collective-permute-start | bytes 983048 | tf_op jit(solution)/shard_map/ppermute | solution.py:324
  80.6 36.9 %collective-permute-start.17 = (bf16[1,8,2176]{2,1,0:T(8,128)(2,1)S(1)}, bf16[1,8,2176]{2,1,0:T(8,128)(2,1)S(1)}, u32[]{:S(2)}, u32[]{:S(2)}) collective-permute-start(bf16[1,8,2176]{2,1,0:T(8,128)(2,1)S(1)} %bitcast.7), channel_id=1, source_target_pairs={{0,12},{1,13},{2,14},{3,15},{4,8},{5,9},{6,10},{7,11},{8,4},{9,5},... | collective-permute-start | bytes 104456 | tf_op jit(solution)/shard_map/ppermute | solution.py:324
  114.7 4.8 %collective-permute-start.16 = (bf16[1,8,2176]{2,1,0:T(8,128)(2,1)S(1)}, bf16[1,8,2176]{2,1,0:T(8,128)(2,1)S(1)}, u32[]{:S(2)}, u32[]{:S(2)}) collective-permute-start(bf16[1,8,2176]{2,1,0:T(8,128)(2,1)S(1)} %bitcast.8), channel_id=1, source_target_pairs={{0,8},{1,9},{2,10},{3,11},{4,12},{5,13},{6,14},{7,15},{8,0},{9,1},... | collective-permute-start | bytes 104456 | tf_op jit(solution)/shard_map/ppermute | solution.py:324
  114.7 4.8 %collective-permute-start.15 = (bf16[1,8,2176]{2,1,0:T(8,128)(2,1)S(1)}, bf16[1,8,2176]{2,1,0:T(8,128)(2,1)S(1)}, u32[]{:S(2)}, u32[]{:S(2)}) collective-permute-start(bf16[1,8,2176]{2,1,0:T(8,128)(2,1)S(1)} %bitcast.9), channel_id=1, source_target_pairs={{0,4},{1,5},{2,6},{3,7},{4,0},{5,1},{6,2},{7,3},{8,12},{9,13},{10,... | collective-permute-start | bytes 104456 | tf_op jit(solution)/shard_map/ppermute | solution.py:324
  119.6 5.1 %collective-permute-start.18 = (bf16[4,8,2176]{2,1,0:T(8,128)(2,1)S(1)}, bf16[4,8,2176]{2,1,0:T(8,128)(2,1)S(1)}, u32[]{:S(2)}, u32[]{:S(2)}) collective-permute-start(bf16[4,8,2176]{2,1,0:T(8,128)(2,1)S(1)} %pad_maximum_fusion.3), channel_id=1, source_target_pairs={{0,2},{1,3},{2,0},{3,1},{4,6},{5,7},{6,4},{7,5},{8,10},{9,11},{10,... | collective-permute-start | bytes 417800 | tf_op jit(solution)/shard_map/ppermute | solution.py:324
  124.7 2.3 %collective-permute-start.19 = (bf16[8,8,2176]{2,1,0:T(8,128)(2,1)S(1)}, bf16[8,8,2176]{2,1,0:T(8,128)(2,1)S(1)}, u32[]{:S(2)}, u32[]{:S(2)}) collective-permute-start(bf16[8,8,2176]{2,1,0:T(8,128)(2,1)S(1)} %get-tuple-element.33), channel_id=1, source_target_pairs={{0,1},{1,0},{2,3},{3,2},{4,5},{5,4},{6,7},{7,6},{8,9},{9,8},{10,11... | collective-permute-start | bytes 835592 | tf_op jit(solution)/shard_map/ppermute | solution.py:324
  131.6 8.9 %collective-permute-start.22 = (f32[8,128]{1,0:T(8,128)S(1)}, f32[8,128]{1,0:T(8,128)S(1)}, u32[]{:S(2)}, u32[]{:S(2)}) collective-permute-start(f32[8,128]{1,0:T(8,128)S(1)} %get-tuple-element.27), channel_id=1, source_target_pairs={{0,12},{1,13},{2,14},{3,15},{4,8},{5,9},{6,10},{7,11},{8,4},{9,5},... | collective-permute-start | bytes 12296 | tf_op jit(solution)/shard_map/ppermute | solution.py:324
  138.9 4.5 %collective-permute-start.21 = (f32[8,128]{1,0:T(8,128)S(1)}, f32[8,128]{1,0:T(8,128)S(1)}, u32[]{:S(2)}, u32[]{:S(2)}) collective-permute-start(f32[8,128]{1,0:T(8,128)S(1)} %get-tuple-element.27), channel_id=1, source_target_pairs={{0,8},{1,9},{2,10},{3,11},{4,12},{5,13},{6,14},{7,15},{8,0},{9,1},... | collective-permute-start | bytes 12296 | tf_op jit(solution)/shard_map/ppermute | solution.py:324
  138.9 4.5 %collective-permute-start.20 = (f32[8,128]{1,0:T(8,128)S(1)}, f32[8,128]{1,0:T(8,128)S(1)}, u32[]{:S(2)}, u32[]{:S(2)}) collective-permute-start(f32[8,128]{1,0:T(8,128)S(1)} %get-tuple-element.27), channel_id=1, source_target_pairs={{0,4},{1,5},{2,6},{3,7},{4,0},{5,1},{6,2},{7,3},{8,12},{9,13},{10,... | collective-permute-start | bytes 12296 | tf_op jit(solution)/shard_map/ppermute | solution.py:324
  143.4 3.4 %collective-permute-start.25 = (f32[8,128]{1,0:T(8,128)S(1)}, f32[8,128]{1,0:T(8,128)S(1)}, u32[]{:S(2)}, u32[]{:S(2)}) collective-permute-start(f32[8,128]{1,0:T(8,128)S(1)} %add_add_fusion.1), channel_id=1, source_target_pairs={{0,3},{1,2},{2,1},{3,0},{4,7},{5,6},{6,5},{7,4},{8,11},{9,10},{10,... | collective-permute-start | bytes 12296 | tf_op jit(solution)/shard_map/ppermute | solution.py:324
  143.5 3.7 %collective-permute-start.24 = (f32[8,128]{1,0:T(8,128)S(1)}, f32[8,128]{1,0:T(8,128)S(1)}, u32[]{:S(2)}, u32[]{:S(2)}) collective-permute-start(f32[8,128]{1,0:T(8,128)S(1)} %add_add_fusion.1), channel_id=1, source_target_pairs={{0,2},{1,3},{2,0},{3,1},{4,6},{5,7},{6,4},{7,5},{8,10},{9,11},{10,... | collective-permute-start | bytes 12296 | tf_op jit(solution)/shard_map/ppermute | solution.py:324
  143.8 3.4 %collective-permute-start.23 = (f32[8,128]{1,0:T(8,128)S(1)}, f32[8,128]{1,0:T(8,128)S(1)}, u32[]{:S(2)}, u32[]{:S(2)}) collective-permute-start(f32[8,128]{1,0:T(8,128)S(1)} %add_add_fusion.1), channel_id=1, source_target_pairs={{0,1},{1,0},{2,3},{3,2},{4,5},{5,4},{6,7},{7,6},{8,9},{9,8},{10,11... | collective-permute-start | bytes 12296 | tf_op jit(solution)/shard_map/ppermute | solution.py:324
  (16 other events, 99.4 us)

commit v9 on v8

--- a/solution.py
+++ b/solution.py
@@ -80,13 +80,11 @@
 
 
 def own_kernel(
-    pay_ref, right_ref, list_ref, out_ref, sum_ref, list_out_ref,
-    left_ref, vec_ref, tile_ref, sem_ref,
+    feat_ref, rhs_ref, right_ref, out_ref, sum_ref, left_ref, vec_ref, tile_ref, sem_ref
 ):
-    list_out_ref[...] = list_ref[...]
-    feat, vec = unpack(pay_ref[...])
+    feat = feat_ref[...]
     left_ref[...] = other_factor(feat)
-    vec_ref[...] = vec
+    vec_ref[...] = rhs_ref[...].astype(BF16)
     sum_ref[...] = jnp.zeros_like(sum_ref)
     count = feat.shape[1] // ROWS
     piece = lambda index: pl.ds(pl.multiple_of(index * ROWS, ROWS), ROWS)
@@ -135,13 +133,15 @@
             )
 
 
-def payload_kernel(feat_ref, rhs_ref, pay_ref, right_ref):
-    half = feat_ref.shape[1] // 2
+def payload_kernel(feat_ref, rhs_ref, pay_zero_ref, pay_one_ref, right_ref):
     feat = feat_ref[...]
     rounded = rhs_ref[...].astype(BF16)
-    pay_ref[:32] = feat[:, :half]
-    pay_ref[32:64] = feat[:, half:]
-    pay_ref[64:80] = jnp.concatenate([rounded[:, :half], rounded[:, half:]], axis=0)
+    quarter = feat.shape[1] // 4
+    for half, pay_ref in enumerate((pay_zero_ref, pay_one_ref)):
+        first, second = [slice(at * quarter, (at + 1) * quarter) for at in (2 * half, 2 * half + 1)]
+        pay_ref[:32] = feat[:, first]
+        pay_ref[32:64] = feat[:, second]
+        pay_ref[64:80] = jnp.concatenate([rounded[:, first], rounded[:, second]], axis=0)
     right_ref[...] = own_factor(feat)
 
 
@@ -153,63 +153,48 @@
     for at, place in enumerate(gather_places(count)):
         if at == 0:
             continue
+        number = me ^ place
         hit = jnp.bool_(False)
         for entry in range(most):
-            hit = hit | (lists_ref[at, entry] == me) | (lists_ref[0, entry] == (me ^ place))
+            hit = hit | (lists_ref[at, entry] == me) | (lists_ref[0, entry] == number)
         slots_ref[1 + total] = jnp.where(hit, at, 0)
+        slots_ref[most + 2 + total] = jnp.where(hit, number, 0)
         total = total + hit.astype(jnp.int32)
     slots_ref[0] = total
 
 
-def pair_kernel(block_at, lists_ref, me_ref, right_ref, rhs_ref, var_ref, *refs):
-    first_ref, block_refs = refs[0], refs[1:-9]
-    front_ref, back_ref, image_ref, send_ref, slots_ref = refs[-9:-4]
-    left_ref, vec_ref, pay_ref, sem_ref = refs[-4:]
+def half_tiles(slots_ref, right_ref, every_ref, front_ref, back_ref, sum_ref, left_ref, vec_ref, pay_ref, sem_ref):
     slot, step = pl.program_id(0), pl.program_id(1)
-    sum_ref = image_ref
+    numbers = pl.num_programs(0) + 2
 
     def fetch(which):
-        place = slots_ref[1 + which]
-        for at, (index, row) in enumerate(block_at):
-            @pl.when(place == at)
-            def _():
-                pltpu.make_async_copy(
-                    block_refs[index].at[pl.ds(row, pay_ref.shape[1])],
-                    pay_ref.at[which % 2],
-                    sem_ref.at[which % 2],
-                ).start()
-
-    @pl.when((slot == 0) & (step == 0))
-    def _():
-        find_partners(lists_ref, me_ref[0], slots_ref)
-        sum_ref[...] = first_ref[...]
-
-        @pl.when(slots_ref[0] > 0)
-        def _():
-            fetch(0)
+        return pltpu.make_async_copy(
+            every_ref.at[slots_ref[numbers + which]], pay_ref.at[which % 2], sem_ref.at[which % 2]
+        )
+
+    @pl.when((slot == 0) & (step == 0) & (slots_ref[0] > 0))
+    def _():
+        fetch(0).start()
 
     @pl.when(slot < slots_ref[0])
     def _():
         @pl.when(step == 0)
         def _():
-            pltpu.make_async_copy(
-                block_refs[0], pay_ref.at[slot % 2], sem_ref.at[slot % 2]
-            ).wait()
+            fetch(slot).wait()
 
             @pl.when(slot + 1 < slots_ref[0])
             def _():
-                fetch(slot + 1)
+                fetch(slot + 1).start()
 
             feat, vec = unpack(pay_ref[slot % 2])
             left_ref[...] = other_factor(feat)
             vec_ref[...] = vec
 
+        rows = pl.ds(pl.multiple_of(step * ROWS, ROWS), ROWS)
+        left, vec = left_ref[rows, :], vec_ref[:, rows]
         for tile_ref, here in ((front_ref, slot < FRONT), (back_ref, slot >= FRONT)):
             @pl.when(here)
             def _():
-                rows = pl.ds(pl.multiple_of(step * ROWS, ROWS), ROWS)
-                left, vec = left_ref[rows, :], vec_ref[:, rows]
-
                 def unit(index, carry):
                     cols = pl.ds(pl.multiple_of(index * COLS, COLS), COLS)
                     sum_ref[:, cols] += tile_unit(
@@ -219,11 +204,35 @@
 
                 lax.fori_loop(0, right_ref.shape[1] // COLS, unit, 0)
 
+
+def pair_zero_kernel(
+    lists_ref, me_ref, right_ref, first_ref, every_ref, front_ref, back_ref, sum_ref, slots_ref, *refs
+):
+    @pl.when((pl.program_id(0) == 0) & (pl.program_id(1) == 0))
+    def _():
+        find_partners(lists_ref, me_ref[0], slots_ref)
+        sum_ref[...] = first_ref[...]
+
+    half_tiles(slots_ref, right_ref, every_ref, front_ref, back_ref, sum_ref, *refs)
+
+
+def pair_one_kernel(
+    slots_ref, right_ref, first_ref, every_ref, rhs_ref, var_ref,
+    front_ref, back_ref, image_ref, send_ref, *refs
+):
+    slot, step = pl.program_id(0), pl.program_id(1)
+
+    @pl.when((slot == 0) & (step == 0))
+    def _():
+        image_ref[...] = first_ref[...]
+
+    half_tiles(slots_ref, right_ref, every_ref, front_ref, back_ref, image_ref, *refs)
+
     @pl.when((slot == pl.num_programs(0) - 1) & (step == pl.num_programs(1) - 1))
     def _():
         rhs = rhs_ref[...]
         width = rhs.shape[1]
-        image = (var_ref[...] + DIAGONAL) * rhs + SCALE * sum_ref[...]
+        image = (var_ref[...] + DIAGONAL) * rhs + SCALE * image_ref[...]
         image_ref[...] = image
         send_ref[:, :width] = image.astype(BF16)
         pieces = split_three(jnp.sum(rhs * rhs, axis=1, keepdims=True))
@@ -236,51 +245,56 @@
 
 
 def again_kernel(
-    slots_ref, front_ref, back_ref, vec_ref, tails_ref, rhs_ref, var_ref, image_ref, *refs
+    slots_ref, front_zero_ref, front_one_ref, back_zero_ref, back_one_ref,
+    vec_ref, tails_ref, rhs_ref, var_ref, image_ref, *refs
 ):
     first_refs = refs[:PARTS]
     rows_ref, dots_ref, step_ref, sum_ref, held_ref, sem_ref = refs[PARTS:]
     slot, step = pl.program_id(0), pl.program_id(1)
     width = rhs_ref.shape[1]
-
     steps = width // ROWS
+    half = steps // 2
     parts = (slots_ref[0] - FRONT) * steps
 
-    def fetch(part):
-        at = pl.ds(pl.multiple_of((part % steps) * ROWS, ROWS), ROWS)
+    def fetch(part, back_ref, first):
+        at = pl.ds(pl.multiple_of((part % steps - first) * ROWS, ROWS), ROWS)
         return pltpu.make_async_copy(
             back_ref.at[part // steps, at], held_ref.at[part % HELD], sem_ref.at[part % HELD]
         )
 
+    def start(part):
+        @pl.when((part < parts) & (part % steps < half))
+        def _():
+            fetch(part, back_zero_ref, 0).start()
+
+        @pl.when((part < parts) & (part % steps >= half))
+        def _():
+            fetch(part, back_one_ref, half).start()
+
     @pl.when((slot == 0) & (step == 0))
     def _():
         sum_ref[...] = functools.reduce(jnp.add, [first_ref[...] for first_ref in first_refs])
         for part in range(HELD):
-            @pl.when(part < parts)
+            start(part)
+
+    @pl.when(slot < slots_ref[0])
+    def _():
+        at = pl.multiple_of(step * ROWS, ROWS)
+        for front_ref, here in ((front_zero_ref, step < half), (front_one_ref, step >= half)):
+            @pl.when((slot < FRONT) & here)
             def _():
-                fetch(part).start()
-
-    @pl.when(slot < slots_ref[0])
-    def _():
-        at = pl.multiple_of(step * ROWS, ROWS)
-
-        @pl.when(slot < FRONT)
-        def _():
-            sum_ref[...] += jnp.dot(
-                vec_ref[0, :, pl.ds(at, ROWS)], front_ref[0], preferred_element_type=F32
-            )
+                sum_ref[...] += jnp.dot(
+                    vec_ref[0, :, pl.ds(at, ROWS)], front_ref[0], preferred_element_type=F32
+                )
 
         @pl.when(slot >= FRONT)
         def _():
             part = (slot - FRONT) * steps + step
-            fetch(part).wait()
+            fetch(part % HELD, back_zero_ref, part % HELD // half * half).wait()
             sum_ref[...] += jnp.dot(
                 vec_ref[0, :, pl.ds(at, ROWS)], held_ref[part % HELD], preferred_element_type=F32
             )
-
-            @pl.when(part + HELD < parts)
-            def _():
-                fetch(part + HELD).start()
+            start(part + HELD)
 
     @pl.when((slot == pl.num_programs(0) - 1) & (step == pl.num_programs(1) - 1))
     def _():
@@ -364,35 +378,6 @@
     return out
 
 
-def gate(block, *behind):
-    return pl.pallas_call(
-        lambda *refs: None,
-        in_specs=[pl.BlockSpec(memory_space=pl.ANY)] * (1 + len(behind)),
-        out_specs=pl.BlockSpec(memory_space=pl.ANY),
-        out_shape=jax.ShapeDtypeStruct(block.shape, block.dtype),
-        input_output_aliases={0: 0},
-        name="gate",
-    )(block, *behind)
-
-
-def pass_on(value, behind, lists, count):
-    rows = value.shape[0]
-    *early, (mask,) = gather_levels(count)
-    blocks = [value]
-    for level, masks in enumerate(early):
-        blocks = blocks + [swap(block, other, count) for other in masks for block in blocks]
-        if level == 0:
-            blocks = blocks[:2] + [gate(block, behind) for block in blocks[2:]]
-    blocks[-1] = gate(blocks[-1], lists[-2])
-    places = [(block, 0) for block in blocks] + [None] * len(blocks)
-    for kinds in ((0, 1), (2,), (3,)):
-        group = [index for index in range(len(blocks)) if index % 4 in kinds]
-        arrived = swap(jnp.concatenate([blocks[index] for index in group], axis=0), mask, count)
-        for at, index in enumerate(group):
-            places[len(blocks) + index] = (arrived, at * rows)
-    return places
-
-
 def local(features, right_side, variance, hilbert_order, tile_list):
     width = features.shape[1]
     rhs_count = right_side.shape[0]
@@ -406,26 +391,24 @@
     whole = lambda *ignored: (0, 0)
     row_spec = pl.BlockSpec(right_side.shape, whole)
     var_spec = pl.BlockSpec(var_row.shape, whole)
-    pay_shape = (80, width // 2)
-    payload, right = pl.pallas_call(
+    pay_shape = (80, width // 4)
+    pay_zero, pay_one, right = pl.pallas_call(
         payload_kernel,
-        out_shape=[shape(pay_shape, BF16), shape((KDIM, width), BF16)],
+        out_shape=[shape(pay_shape, BF16), shape(pay_shape, BF16), shape((KDIM, width), BF16)],
         compiler_params=params,
         name="payload",
     )(features, right_side)
+    in_hbm = lambda array: pltpu.with_memory_space_constraint(array, pltpu.HBM)
+    every_zero = in_hbm(lax.all_gather(pay_zero, "row", axis=0))
+    every_one = in_hbm(lax.all_gather(pay_one, "row", axis=0))
+    lists = tree_gather(tile_list[0, :, 1], count)
+    me = jnp.full((1,), lax.axis_index("row"), jnp.int32)
     any_spec = pl.BlockSpec(memory_space=pl.ANY)
     blocks = own_blocks(width // ROWS)
-    coupled = tile_list[:, :, 1]
-    list_spec = pl.BlockSpec(coupled.shape, whole)
-    own_tiles, own_sum, coupled = pl.pallas_call(
+    own_tiles, own_sum = pl.pallas_call(
         own_kernel,
-        in_specs=[pl.BlockSpec(payload.shape, whole), pl.BlockSpec(right.shape, whole), list_spec],
-        out_specs=[any_spec, row_spec, list_spec],
-        out_shape=[
-            pltpu.HBM((len(blocks), ROWS, ROWS), BF16),
-            shape(right_side.shape, F32),
-            shape(coupled.shape, jnp.int32),
-        ],
+        out_specs=[any_spec, pl.BlockSpec(memory_space=pltpu.VMEM)],
+        out_shape=[pltpu.HBM((len(blocks), ROWS, ROWS), BF16), shape(right_side.shape, F32)],
         scratch_shapes=[
             pltpu.VMEM((width, KDIM), BF16),
             pltpu.VMEM((rhs_count, width), BF16),
@@ -437,54 +420,64 @@
             flops=9_000_000_000, bytes_accessed=2 * len(blocks) * ROWS * ROWS, transcendentals=0
         ),
         name="own_tile",
-    )(payload, right, coupled)
-    lists = tree_gather(coupled[0], count)
-    places = pass_on(payload, own_sum, lists, count)
-    arrays = list({id(array): array for array, _ in places}.values())
-    block_at = [([id(array) for array in arrays].index(id(array)), row) for array, row in places]
-    me = jnp.full((1,), lax.axis_index("row"), jnp.int32)
+    )(features, right_side, right)
+
+    half = steps // 2
 
     def front_at(k, i, *ignored):
-        return (jnp.minimum(k, FRONT - 1), jnp.where(k < FRONT, i, steps - 1), 0)
+        return (jnp.minimum(k, FRONT - 1), jnp.where(k < FRONT, i, half - 1), 0)
 
     def back_at(k, i, *ignored):
         return (jnp.maximum(k - FRONT, 0), jnp.where(k < FRONT, 0, i), 0)
 
-    tile_specs = [pl.BlockSpec((1, ROWS, width), front_at), pl.BlockSpec((1, ROWS, width), back_at)]
+    half_specs = [pl.BlockSpec((1, ROWS, width), front_at), pl.BlockSpec((1, ROWS, width), back_at)]
+    half_shapes = [
+        pltpu.VMEM((FRONT, width // 2, width), BF16),
+        pltpu.HBM((most - FRONT, width // 2, width), BF16),
+    ]
+    half_scratch = [
+        pltpu.VMEM((width // 2, KDIM), BF16),
+        pltpu.VMEM((rhs_count, width // 2), BF16),
+        pltpu.VMEM((2,) + pay_shape, BF16),
+        pltpu.SemaphoreType.DMA((2,)),
+    ]
+    right_spec = pl.BlockSpec(right.shape, whole)
     send_shape = (rhs_count, width + TAIL)
-    front_tiles, back_tiles, image, send, slots = pl.pallas_call(
-        functools.partial(pair_kernel, block_at),
+    front_zero, back_zero, half_sum, slots = pl.pallas_call(
+        pair_zero_kernel,
         grid_spec=pltpu.PrefetchScalarGridSpec(
             num_scalar_prefetch=2,
-            grid=(most, steps),
-            in_specs=[
-                pl.BlockSpec(right.shape, whole),
-                row_spec,
-                var_spec,
-            ]
-            + [row_spec]
-            + [any_spec] * len(arrays),
-            out_specs=tile_specs
-            + [
-                row_spec,
-                pl.BlockSpec(send_shape, whole),
-                pl.BlockSpec(memory_space=pltpu.SMEM),
-            ],
-            scratch_shapes=[pltpu.VMEM((width, KDIM), BF16), pltpu.VMEM((rhs_count, width), BF16)]
-            + [pltpu.VMEM((2,) + payload.shape, BF16), pltpu.SemaphoreType.DMA((2,))],
+            grid=(most, half),
+            in_specs=[right_spec, row_spec, any_spec],
+            out_specs=half_specs + [row_spec, pl.BlockSpec(memory_space=pltpu.SMEM)],
+            scratch_shapes=half_scratch,
         ),
-        out_shape=[
-            pltpu.VMEM((FRONT, width, width), BF16),
-            pltpu.HBM((most - FRONT, width, width), BF16),
-            shape(right_side.shape, F32),
-            shape(send_shape, BF16),
-            shape((most + 2,), jnp.int32),
-        ],
+        out_shape=half_shapes
+        + [shape(right_side.shape, F32), shape((2 * (most + 2),), jnp.int32)],
         compiler_params=params,
-        name="pair_tiles",
-    )(lists[-1], me, right, right_side, var_row, own_sum, *arrays)
-    front_tiles = pltpu.with_memory_space_constraint(front_tiles, pltpu.VMEM)
-    back_tiles = pltpu.with_memory_space_constraint(back_tiles, pltpu.HBM)
+        name="pair_zero",
+    )(lists[-1], me, right, own_sum, every_zero)
+    front_one, back_one, image, send = pl.pallas_call(
+        pair_one_kernel,
+        grid_spec=pltpu.PrefetchScalarGridSpec(
+            num_scalar_prefetch=1,
+            grid=(most, half),
+            in_specs=[right_spec, row_spec, any_spec, row_spec, var_spec],
+            out_specs=half_specs + [row_spec, pl.BlockSpec(send_shape, whole)],
+            scratch_shapes=half_scratch,
+        ),
+        out_shape=half_shapes + [shape(right_side.shape, F32), shape(send_shape, BF16)],
+        compiler_params=params,
+        name="pair_one",
+    )(slots, right, half_sum, every_one, right_side, var_row)
+    fronts = [pltpu.with_memory_space_constraint(part, pltpu.VMEM) for part in (front_zero, front_one)]
+    backs = [pltpu.with_memory_space_constraint(part, pltpu.HBM) for part in (back_zero, back_one)]
+
+    def front_zero_at(k, i, *ignored):
+        return (jnp.minimum(k, FRONT - 1), jnp.where(k < FRONT, jnp.minimum(i, half - 1), half - 1), 0)
+
+    def front_one_at(k, i, *ignored):
+        return (jnp.minimum(k, FRONT - 1), jnp.where(k < FRONT, jnp.maximum(i - half, 0), half - 1), 0)
 
     every_send = tree_gather(send, count)[-1]
     own_again = []
@@ -515,7 +508,9 @@
             num_scalar_prefetch=1,
             grid=(most, steps),
             in_specs=[
-                tile_specs[0],
+                pl.BlockSpec((1, ROWS, width), front_zero_at),
+                pl.BlockSpec((1, ROWS, width), front_one_at),
+                any_spec,
                 any_spec,
                 pl.BlockSpec((1,) + send_shape, lambda k, i, s: (s[1 + k], 0, 0)),
                 pl.BlockSpec((count, rhs_count, TAIL), lambda k, i, s: (0, 0, width // TAIL)),
@@ -542,7 +537,7 @@
         ],
         compiler_params=params,
         name="pair_again",
-    )(slots, front_tiles, back_tiles, every_send, every_send, right_side, var_row, image, *own_again)
+    )(slots, *fronts, *backs, every_send, every_send, right_side, var_row, image, *own_again)
 
     dots = tree_sum(dots, count)
     ordered = pl.pallas_call(

time: 148 us -> 168 us (1.14)
  starting transfers between devices: 62 us -> 19.2 us
  Pallas kernels: 51.9 us -> 91.7 us
  between operations: 0.85 us -> 14.3 us
  waiting for transfers between devices: 24.4 us -> 31.5 us
  local copies, waits for them, and re-layouts: 4.62 us -> 9.32 us
  other arithmetic: 4.41 us -> 1.03 us
    ppermute x26 -> x16, starting transfers between devices: 62 us -> 19.1 us  [swap(): return lax.ppermute(value, 'row', [(i, i ^ mask) for i in range(count)])]
    pallas_call x6 -> x4, Pallas kernels: 41.6 us -> 75.5 us  [the longest x1 33.1 us: local(): pl.pallas_call(pair_zero_kernel, grid_spec=pltpu.PrefetchScalarGridSpec(n...]
    all_gather x0 -> x2, waiting for transfers between devices: none -> 21.5 us  [the longest x1 19.1 us: local(): every_zero = in_hbm(lax.all_gather(pay_zero, 'row', axis=0))]
    ppermute x26 -> x16, waiting for transfers between devices: 24.4 us -> 9.23 us  [swap(): return lax.ppermute(value, 'row', [(i, i ^ mask) for i in range(count)])]
    pallas_call x1, Pallas kernels: 4.54 us -> 10.1 us  [local(): pl.pallas_call(again_kernel, grid_spec=pltpu.PrefetchScalarGridSpec(num_s...]
    unnamed x32 -> x26, local copies, waits for them, and re-layouts: 3.26 us -> 8.54 us
    concatenate x3 -> x0, other arithmetic: 3.38 us -> none  [pass_on(): jnp.concatenate([blocks[index] for index in group], axis=0)]
  transfers between devices with their start and end apart: 26 -> 18, of which waited for: 9 -> 8; matrix products, arithmetic and copies ran while one was open for 3% -> 0% of each run, Pallas kernels for 10% -> 29%
where the time goes in v9:
time: 168 us; the launch traced here: 167 us
  Pallas kernels  91.7 us (55%)
  waiting for transfers between devices  31.5 us (19%)
  starting transfers between devices  19.2 us (11%)
  between operations  14.3 us (9%)
  local copies, waits for them, and re-layouts  9.32 us (6%)
    pallas_call x1, Pallas kernels, local(): pl.pallas_call(pair_zero_kernel, grid_spec=pltpu.PrefetchScalarGridSpec(n...  33.1 us
    pallas_call x1, Pallas kernels, local(): pl.pallas_call(pair_one_kernel, grid_spec=pltpu.PrefetchScalarGridSpec(nu...  32.3 us
    all_gather x1, waiting for transfers between devices, local(): every_zero = in_hbm(lax.all_gather(pay_zero, 'row', axis=0))  19.1 us
    ppermute x16, starting transfers between devices, swap(): return lax.ppermute(value, 'row', [(i, i ^ mask) for i in range(count)])  19.1 us
    pallas_call x1, Pallas kernels, local(): pl.pallas_call(again_kernel, grid_spec=pltpu.PrefetchScalarGridSpec(num_s...  10.1 us
    pallas_call x1, Pallas kernels, local(): pl.pallas_call(own_kernel, out_specs=[any_spec, pl.BlockSpec(memory_space...  9.34 us
    ppermute x16, waiting for transfers between devices, swap(): return lax.ppermute(value, 'row', [(i, i ^ mask) for i in range(count)])  9.23 us
    unnamed x26, local copies, waits for them, and re-layouts  8.54 us
  transfers between devices with their start and end apart: 18, of which 8 were waited for; matrix products, arithmetic and copies ran while one was open for 0% of the time, Pallas kernels for 29%

profile of v9, /device:TPU:0, one launch (start us, length us, event | category | flops | bytes accessed | tf_op | source)
XLA Modules:
  0.0 167.0 jit_solution(9509754646094314237)
XLA Ops:
  7.2 0.8 copy-done.1
  8.1 0.9 copy-done.4
  9.0 0.8 payload.1
  11.2 5.0 %collective-permute-start.2 = (s32[1,5]{1,0:T(1,128)S(1)}, s32[1,5]{1,0:T(1,128)S(1)}, u32[]{:S(2)}, u32[]{:S(2)}) collective-permute-start(s32[1,5]{1,0:T(1,128)S(1)} %slice_bitcast_fusion), channel_id=1, source_target_pairs={{0,12},{1,13},{2,14},{3,15},{4,8},{5,9},{6,10},{7,11},{8,4},{9,5},... | collective-permute-start | bytes 68 | tf_op jit(solution)/shard_map/ppermute | solution.py:338
  16.8 0.8 copy-done.2
  17.7 0.9 copy-done.5
  18.6 9.3 %own_tile.1 = (bf16[10,512,512]{2,1,0:T(8,128)(2,1)}, f32[8,2048]{1,0:T(8,128)S(1)}) custom-call(bf16[32,2048]{1,0:T(8,128)(2,1)S(1)} %copy-done.5, f32[8,2048]{1,0:T(8,128)S(1)} %copy-done.2, bf16[128,2048]{1,0:T(8,128)(2,1)S(1)} %get-tuple-element.18.right_ref), custom_call_target="tpu_custom_call" | custom-call | flops 8999999488 | bytes 5242880 | tf_op jit(solution)/shard_map/own_tile/pallas_call | solution.py:408
  28.0 1.8 %collective-permute-start.3 = (s32[4,5]{1,0:T(4,128)S(1)}, s32[4,5]{1,0:T(4,128)S(1)}, u32[]{:S(2)}, u32[]{:S(2)}) collective-permute-start(s32[4,5]{1,0:T(4,128)S(1)} %pad_add_fusion), channel_id=1, source_target_pairs={{0,2},{1,3},{2,0},{3,1},{4,6},{5,7},{6,4},{7,5},{8,10},{9,11},{10,... | collective-permute-start | bytes 248 | tf_op jit(solution)/shard_map/ppermute | solution.py:338
  29.8 1.8 %collective-permute-done.3 = s32[4,5]{1,0:T(4,128)S(1)} collective-permute-done((s32[4,5]{1,0:T(4,128)S(1)}, s32[4,5]{1,0:T(4,128)S(1)}, u32[]{:S(2)}, u32[]{:S(2)}) %collective-permute-start.3) | collective-permute-done | bytes 112 | tf_op jit(solution)/shard_map/ppermute | solution.py:338
  31.7 1.2 collective-permute-done.4
  32.9 19.1 %all-gather.5.cloned.1.call-done = bf16[1280,512]{1,0:T(8,128)(2,1)} async-done(((bf16[80,512]{1,0:T(8,128)(2,1)}), bf16[1280,512]{1,0:T(8,128)(2,1)}) %all-gather.5.cloned.1.call-update) | async-done | bytes 1310736 | tf_op jit(solution)/shard_map/all_gather | solution.py:402
  52.0 33.1 %pair_zero.1 = (bf16[3,1024,2048]{2,1,0:T(8,128)(2,1)S(1)}, bf16[2,1024,2048]{2,1,0:T(8,128)(2,1)}, f32[8,2048]{1,0:T(8,128)S(1)}, s32[14]{0:T(128)S(1)}) custom-call(s32[16,5]{1,0:T(8,128)S(1)} %concatenate.24.lists_ref, s32[1]{0:T(128)} %bitcast.1.me_ref, bf16[128,2048]{1,0:T(8,128)(2,1)S(1)} %get-tuple-element.18.right_ref, ...), custom_call_target="tpu_custom_call" | custom-call | tf_op jit(solution)/shard_map/pair_zero/pallas_call | solution.py:446
  85.1 4.5 %copy-done = bf16[3,1024,2048]{2,1,0:T(8,128)(2,1)} copy-done((bf16[3,1024,2048]{2,1,0:T(8,128)(2,1)}, bf16[3,1024,2048]{2,1,0:T(8,128)(2,1)S(1)}, u32[]{:S(2)}) %copy-start) | copy-done | bytes 12582936
  89.6 2.4 %all-gather.7.cloned.1.call-done = bf16[1280,512]{1,0:T(8,128)(2,1)} async-done(((bf16[80,512]{1,0:T(8,128)(2,1)}), bf16[1280,512]{1,0:T(8,128)(2,1)}) %all-gather.7.cloned.1.call-update) | async-done | bytes 1310736 | tf_op jit(solution)/shard_map/all_gather | solution.py:403
  92.0 32.3 %pair_one.1 = (bf16[3,1024,2048]{2,1,0:T(8,128)(2,1)S(1)}, bf16[2,1024,2048]{2,1,0:T(8,128)(2,1)}, f32[8,2048]{1,0:T(8,128)S(1)}, bf16[8,2176]{1,0:T(8,128)(2,1)S(1)}) custom-call(s32[14]{0:T(128)S(1)} %get-tuple-element.21.slots_ref, bf16[128,2048]{1,0:T(8,128)(2,1)S(1)} %get-tuple-element.18.right_ref, f32[8,2048]{1,0:T(8,128)S(1)} %get-tuple-element.23.first_ref, ...), custom_call_target="tpu_custom_call" | custom-call | tf_op jit(solution)/shard_map/pair_one/pallas_call | solution.py:460
  124.5 4.3 %collective-permute-start.5 = (bf16[1,8,2176]{2,1,0:T(8,128)(2,1)S(1)}, bf16[1,8,2176]{2,1,0:T(8,128)(2,1)S(1)}, u32[]{:S(2)}, u32[]{:S(2)}) collective-permute-start(bf16[1,8,2176]{2,1,0:T(8,128)(2,1)S(1)} %bitcast.13), channel_id=1, source_target_pairs={{0,4},{1,5},{2,6},{3,7},{4,0},{5,1},{6,2},{7,3},{8,12},{9,13},{10,... | collective-permute-start | bytes 104456 | tf_op jit(solution)/shard_map/ppermute | solution.py:338
  128.8 2.3 %own_again_5.1.refs_1_ = f32[8,2048]{1,0:T(8,128)S(1)} custom-call(bf16[10,512,512]{2,1,0:T(8,128)(2,1)} %get-tuple-element.30.in_ref, bf16[8,2176]{1,0:T(8,128)(2,1)S(1)} %get-tuple-element.28.vec_ref), custom_call_target="tpu_custom_call" | custom-call | flops 5000000000 | bytes 2621440 | tf_op jit(solution)/shard_map/own_again_5/pallas_call | solution.py:488
  132.0 4.3 %collective-permute-done.8 = bf16[4,8,2176]{2,1,0:T(8,128)(2,1)S(1)} collective-permute-done((bf16[4,8,2176]{2,1,0:T(8,128)(2,1)S(1)}, bf16[4,8,2176]{2,1,0:T(8,128)(2,1)S(1)}, u32[]{:S(2)}, u32[]{:S(2)}) %collective-permute-start.8) | collective-permute-done | bytes 139296 | tf_op jit(solution)/shard_map/ppermute | solution.py:338
  136.5 2.3 %own_again_0.1.refs_0_ = f32[8,2048]{1,0:T(8,128)S(1)} custom-call(bf16[10,512,512]{2,1,0:T(8,128)(2,1)} %get-tuple-element.30.in_ref, bf16[8,2176]{1,0:T(8,128)(2,1)S(1)} %get-tuple-element.28.vec_ref), custom_call_target="tpu_custom_call" | custom-call | flops 5000000000 | bytes 2621440 | tf_op jit(solution)/shard_map/own_again_0/pallas_call | solution.py:488
  139.3 10.1 %pair_again.1 = (f32[32,2048]{1,0:T(8,128)S(1)}, f32[8,128]{1,0:T(8,128)S(1)}, f32[8,128]{1,0:T(8,128)S(1)}) custom-call(s32[14]{0:T(128)S(1)} %get-tuple-element.21.slots_ref, bf16[3,1024,2048]{2,1,0:T(8,128)(2,1)S(1)} %bitcast.10, bf16[3,1024,2048]{2,1,0:T(8,128)(2,1)S(1)} %get-tuple-element.25.front_one_ref, ...), custom_call_target="tpu_custom_call" | custom-call | tf_op jit(solution)/shard_map/pair_again/pallas_call | solution.py:505
  149.6 4.3 %collective-permute-start.10 = (f32[8,128]{1,0:T(8,128)S(1)}, f32[8,128]{1,0:T(8,128)S(1)}, u32[]{:S(2)}, u32[]{:S(2)}) collective-permute-start(f32[8,128]{1,0:T(8,128)S(1)} %get-tuple-element.33), channel_id=1, source_target_pairs={{0,4},{1,5},{2,6},{3,7},{4,0},{5,1},{6,2},{7,3},{8,12},{9,13},{10,... | collective-permute-start | bytes 12296 | tf_op jit(solution)/shard_map/ppermute | solution.py:338
  153.9 1.0 collective-permute-done.12
  155.5 1.4 collective-permute-start.14
  157.3 1.5 curve_order.1
  (60 shorter events, 6.4 us)
Async XLA Ops:
  7.2 44.8 %all-gather.5.cloned.1.call-start = ((), (), s32[]{:S(2)}) async-start(), calls=%async_computation | async-start | bytes 1392640 | tf_op jit(solution)/shard_map/all_gather | solution.py:402
  9.8 82.2 %all-gather.7.cloned.1.call-start = ((), (), s32[]{:S(2)}) async-start(), calls=%async_computation.1 | async-start | bytes 1392640 | tf_op jit(solution)/shard_map/all_gather | solution.py:403
  11.2 16.7 %collective-permute-start.2 = (s32[1,5]{1,0:T(1,128)S(1)}, s32[1,5]{1,0:T(1,128)S(1)}, u32[]{:S(2)}, u32[]{:S(2)}) collective-permute-start(s32[1,5]{1,0:T(1,128)S(1)} %slice_bitcast_fusion), channel_id=1, source_target_pairs={{0,12},{1,13},{2,14},{3,15},{4,8},{5,9},{6,10},{7,11},{8,4},{9,5},... | collective-permute-start | bytes 68 | tf_op jit(solution)/shard_map/ppermute | solution.py:338
  16.3 11.7 %collective-permute-start.1 = (s32[1,5]{1,0:T(1,128)S(1)}, s32[1,5]{1,0:T(1,128)S(1)}, u32[]{:S(2)}, u32[]{:S(2)}) collective-permute-start(s32[1,5]{1,0:T(1,128)S(1)} %slice_bitcast_fusion), channel_id=1, source_target_pairs={{0,8},{1,9},{2,10},{3,11},{4,12},{5,13},{6,14},{7,15},{8,0},{9,1},... | collective-permute-start | bytes 68 | tf_op jit(solution)/shard_map/ppermute | solution.py:338
  16.3 11.7 %collective-permute-start = (s32[1,5]{1,0:T(1,128)S(1)}, s32[1,5]{1,0:T(1,128)S(1)}, u32[]{:S(2)}, u32[]{:S(2)}) collective-permute-start(s32[1,5]{1,0:T(1,128)S(1)} %slice_bitcast_fusion), channel_id=1, source_target_pairs={{0,4},{1,5},{2,6},{3,7},{4,0},{5,1},{6,2},{7,3},{8,12},{9,13},{10,... | collective-permute-start | bytes 68 | tf_op jit(solution)/shard_map/ppermute | solution.py:338
  18.6 73.4 %copy-start.3 = (f32[8,2048]{1,0:T(8,128)S(1)}, f32[8,2048]{1,0:T(8,128)}, u32[]{:S(2)}) copy-start(f32[8,2048]{1,0:T(8,128)} %rhs_ref.7) | copy-start | bytes 196612
  18.6 73.4 %copy-start.6 = (f32[2048]{0:T(1024)S(1)}, f32[2048]{0:T(1024)}, u32[]{:S(2)}) copy-start(f32[2048]{0:T(1024)} %param.7) | copy-start | bytes 24580
  28.0 3.7 %collective-permute-start.3 = (s32[4,5]{1,0:T(4,128)S(1)}, s32[4,5]{1,0:T(4,128)S(1)}, u32[]{:S(2)}, u32[]{:S(2)}) collective-permute-start(s32[4,5]{1,0:T(4,128)S(1)} %pad_add_fusion), channel_id=1, source_target_pairs={{0,2},{1,3},{2,0},{3,1},{4,6},{5,7},{6,4},{7,5},{8,10},{9,11},{10,... | collective-permute-start | bytes 248 | tf_op jit(solution)/shard_map/ppermute | solution.py:338
  31.6 1.2 collective-permute-start.4
  85.1 4.5 %copy-start = (bf16[3,1024,2048]{2,1,0:T(8,128)(2,1)}, bf16[3,1024,2048]{2,1,0:T(8,128)(2,1)S(1)}, u32[]{:S(2)}) copy-start(bf16[3,1024,2048]{2,1,0:T(8,128)(2,1)S(1)} %get-tuple-element.22.front_zero_ref) | copy-start | bytes 37748740
  124.3 6.8 %collective-permute-start.7 = (bf16[1,8,2176]{2,1,0:T(8,128)(2,1)S(1)}, bf16[1,8,2176]{2,1,0:T(8,128)(2,1)S(1)}, u32[]{:S(2)}, u32[]{:S(2)}) collective-permute-start(bf16[1,8,2176]{2,1,0:T(8,128)(2,1)S(1)} %bitcast.11), channel_id=1, source_target_pairs={{0,12},{1,13},{2,14},{3,15},{4,8},{5,9},{6,10},{7,11},{8,4},{9,5},... | collective-permute-start | bytes 104456 | tf_op jit(solution)/shard_map/ppermute | solution.py:338
  124.4 6.8 %collective-permute-start.6 = (bf16[1,8,2176]{2,1,0:T(8,128)(2,1)S(1)}, bf16[1,8,2176]{2,1,0:T(8,128)(2,1)S(1)}, u32[]{:S(2)}, u32[]{:S(2)}) collective-permute-start(bf16[1,8,2176]{2,1,0:T(8,128)(2,1)S(1)} %bitcast.12), channel_id=1, source_target_pairs={{0,8},{1,9},{2,10},{3,11},{4,12},{5,13},{6,14},{7,15},{8,0},{9,1},... | collective-permute-start | bytes 104456 | tf_op jit(solution)/shard_map/ppermute | solution.py:338
  124.5 6.7 %collective-permute-start.5 = (bf16[1,8,2176]{2,1,0:T(8,128)(2,1)S(1)}, bf16[1,8,2176]{2,1,0:T(8,128)(2,1)S(1)}, u32[]{:S(2)}, u32[]{:S(2)}) collective-permute-start(bf16[1,8,2176]{2,1,0:T(8,128)(2,1)S(1)} %bitcast.13), channel_id=1, source_target_pairs={{0,4},{1,5},{2,6},{3,7},{4,0},{5,1},{6,2},{7,3},{8,12},{9,13},{10,... | collective-permute-start | bytes 104456 | tf_op jit(solution)/shard_map/ppermute | solution.py:338
  128.8 10.0 %slice-start = ((s8[12582912]{0:T(1024)(128)(4,1)}), s8[4194304]{0:T(1024)(128)(4,1)S(1)}, s32[]{:S(2)}) async-start(s8[12582912]{0:T(1024)(128)(4,1)} %bitcast.9), calls=%async_computation.2 | async-start | bytes 8388608
  128.8 10.1 %slice-start.1 = ((s8[12582912]{0:T(1024)(128)(4,1)}), s8[4194304]{0:T(1024)(128)(4,1)S(1)}, s32[]{:S(2)}) async-start(s8[12582912]{0:T(1024)(128)(4,1)} %bitcast.9), calls=%async_computation.3 | async-start | bytes 8388608
  131.2 5.1 %collective-permute-start.8 = (bf16[4,8,2176]{2,1,0:T(8,128)(2,1)S(1)}, bf16[4,8,2176]{2,1,0:T(8,128)(2,1)S(1)}, u32[]{:S(2)}, u32[]{:S(2)}) collective-permute-start(bf16[4,8,2176]{2,1,0:T(8,128)(2,1)S(1)} %pad_maximum_fusion), channel_id=1, source_target_pairs={{0,2},{1,3},{2,0},{3,1},{4,6},{5,7},{6,4},{7,5},{8,10},{9,11},{10,... | collective-permute-start | bytes 417800 | tf_op jit(solution)/shard_map/ppermute | solution.py:338
  136.4 2.4 %collective-permute-start.9 = (bf16[8,8,2176]{2,1,0:T(8,128)(2,1)S(1)}, bf16[8,8,2176]{2,1,0:T(8,128)(2,1)S(1)}, u32[]{:S(2)}, u32[]{:S(2)}) collective-permute-start(bf16[8,8,2176]{2,1,0:T(8,128)(2,1)S(1)} %get-tuple-element.39), channel_id=1, source_target_pairs={{0,1},{1,0},{2,3},{3,2},{4,5},{5,4},{6,7},{7,6},{8,9},{9,8},{10,11... | collective-permute-start | bytes 835592 | tf_op jit(solution)/shard_map/ppermute | solution.py:338
  139.3 18.0 %copy-start.7 = (s32[1,2048]{1,0:T(1,128)S(1)}, s32[1,2048]{1,0:T(1,128)}, u32[]{:S(2)}) copy-start(s32[1,2048]{1,0:T(1,128)} %perm_ref.1) | copy-start | bytes 24580
  149.4 5.5 %collective-permute-start.12 = (f32[8,128]{1,0:T(8,128)S(1)}, f32[8,128]{1,0:T(8,128)S(1)}, u32[]{:S(2)}, u32[]{:S(2)}) collective-permute-start(f32[8,128]{1,0:T(8,128)S(1)} %get-tuple-element.33), channel_id=1, source_target_pairs={{0,12},{1,13},{2,14},{3,15},{4,8},{5,9},{6,10},{7,11},{8,4},{9,5},... | collective-permute-start | bytes 12296 | tf_op jit(solution)/shard_map/ppermute | solution.py:338
  149.5 5.4 %collective-permute-start.11 = (f32[8,128]{1,0:T(8,128)S(1)}, f32[8,128]{1,0:T(8,128)S(1)}, u32[]{:S(2)}, u32[]{:S(2)}) collective-permute-start(f32[8,128]{1,0:T(8,128)S(1)} %get-tuple-element.33), channel_id=1, source_target_pairs={{0,8},{1,9},{2,10},{3,11},{4,12},{5,13},{6,14},{7,15},{8,0},{9,1},... | collective-permute-start | bytes 12296 | tf_op jit(solution)/shard_map/ppermute | solution.py:338
  149.6 5.9 %collective-permute-start.10 = (f32[8,128]{1,0:T(8,128)S(1)}, f32[8,128]{1,0:T(8,128)S(1)}, u32[]{:S(2)}, u32[]{:S(2)}) collective-permute-start(f32[8,128]{1,0:T(8,128)S(1)} %get-tuple-element.33), channel_id=1, source_target_pairs={{0,4},{1,5},{2,6},{3,7},{4,0},{5,1},{6,2},{7,3},{8,12},{9,13},{10,... | collective-permute-start | bytes 12296 | tf_op jit(solution)/shard_map/ppermute | solution.py:338
  155.5 3.3 %collective-permute-start.15 = (f32[8,128]{1,0:T(8,128)S(1)}, f32[8,128]{1,0:T(8,128)S(1)}, u32[]{:S(2)}, u32[]{:S(2)}) collective-permute-start(f32[8,128]{1,0:T(8,128)S(1)} %add_add_fusion.1), channel_id=1, source_target_pairs={{0,3},{1,2},{2,1},{3,0},{4,7},{5,6},{6,5},{7,4},{8,11},{9,10},{10,... | collective-permute-start | bytes 12296 | tf_op jit(solution)/shard_map/ppermute | solution.py:338
  155.5 3.7 %collective-permute-start.14 = (f32[8,128]{1,0:T(8,128)S(1)}, f32[8,128]{1,0:T(8,128)S(1)}, u32[]{:S(2)}, u32[]{:S(2)}) collective-permute-start(f32[8,128]{1,0:T(8,128)S(1)} %add_add_fusion.1), channel_id=1, source_target_pairs={{0,2},{1,3},{2,0},{3,1},{4,6},{5,7},{6,4},{7,5},{8,10},{9,11},{10,... | collective-permute-start | bytes 12296 | tf_op jit(solution)/shard_map/ppermute | solution.py:338
  156.9 2.3 %collective-permute-start.13 = (f32[8,128]{1,0:T(8,128)S(1)}, f32[8,128]{1,0:T(8,128)S(1)}, u32[]{:S(2)}, u32[]{:S(2)}) collective-permute-start(f32[8,128]{1,0:T(8,128)S(1)} %add_add_fusion.1), channel_id=1, source_target_pairs={{0,1},{1,0},{2,3},{3,2},{4,5},{5,4},{6,7},{7,6},{8,9},{9,8},{10,11... | collective-permute-start | bytes 12296 | tf_op jit(solution)/shard_map/ppermute | solution.py:338
  (5 other events, 6.5 us)
Sparse Core Ops, SparseCore 0:
  10.3 41.6 all-gather.4
  54.3 37.7 all-gather.6

commit v10 on v9

--- a/solution.py
+++ b/solution.py
@@ -75,12 +75,13 @@
     return jnp.concatenate([pay[:32], pay[32:64]], axis=1), jnp.concatenate([pay[64:72], pay[72:80]], axis=1)
 
 
-def own_blocks(count):
-    return [(row, col) for row in range(count) for col in range(row, count)]
+def own_blocks(rows, count):
+    return [(row, col) for row in rows for col in range(row, count)]
 
 
 def own_kernel(
-    feat_ref, rhs_ref, right_ref, out_ref, sum_ref, left_ref, vec_ref, tile_ref, sem_ref
+    rows, feat_ref, rhs_ref, right_ref, arrived_ref, out_ref, sum_ref,
+    left_ref, vec_ref, tile_ref, sem_ref,
 ):
     feat = feat_ref[...]
     left_ref[...] = other_factor(feat)
@@ -109,14 +110,14 @@
 
         return lax.fori_loop(row, count, col_step, at)
 
-    lax.fori_loop(0, count, row_step, 0)
+    lax.fori_loop(rows[0], rows[-1] + 1, row_step, 0)
     for at in range(tile_ref.shape[0]):
         save(at).wait()
 
 
-def own_again_kernel(first, blocks, in_ref, vec_ref, sum_ref, tile_ref, sem_ref):
+def own_again_kernel(blocks, in_ref, vec_ref, sum_ref, tile_ref, sem_ref):
     load = lambda index: pltpu.make_async_copy(
-        in_ref.at[first + index], tile_ref.at[index], sem_ref.at[index]
+        in_ref.at[index], tile_ref.at[index], sem_ref.at[index]
     )
     for index in range(len(blocks)):
         load(index).start()
@@ -133,7 +134,7 @@
             )
 
 
-def payload_kernel(feat_ref, rhs_ref, pay_zero_ref, pay_one_ref, right_ref):
+def payload_kernel(list_ref, feat_ref, rhs_ref, pay_zero_ref, pay_one_ref, right_ref):
     feat = feat_ref[...]
     rounded = rhs_ref[...].astype(BF16)
     quarter = feat.shape[1] // 4
@@ -142,11 +143,16 @@
         pay_ref[:32] = feat[:, first]
         pay_ref[32:64] = feat[:, second]
         pay_ref[64:80] = jnp.concatenate([rounded[:, first], rounded[:, second]], axis=0)
+    lane = lax.broadcasted_iota(jnp.int32, (16, quarter), 1)
+    numbers = jnp.full(lane.shape, -1, jnp.int32)
+    for entry in range(list_ref.shape[1]):
+        numbers = jnp.where(lane == entry, list_ref[0, entry, 1], numbers)
+    pay_zero_ref[80:96] = numbers.astype(F32).astype(BF16)
     right_ref[...] = own_factor(feat)
 
 
 def find_partners(lists_ref, me, slots_ref):
-    count, most = lists_ref.shape
+    count, most = lists_ref.shape[0], slots_ref.shape[0] // 2 - 2
     for at in range(slots_ref.shape[0]):
         slots_ref[at] = 0
     total = jnp.int32(0)
@@ -163,28 +169,24 @@
     slots_ref[0] = total
 
 
-def half_tiles(slots_ref, right_ref, every_ref, front_ref, back_ref, sum_ref, left_ref, vec_ref, pay_ref, sem_ref):
+def half_tiles(slots_ref, right_ref, fetch, front_ref, back_ref, sum_ref, left_ref, vec_ref, pay_ref, sem_ref):
     slot, step = pl.program_id(0), pl.program_id(1)
-    numbers = pl.num_programs(0) + 2
-
-    def fetch(which):
-        return pltpu.make_async_copy(
-            every_ref.at[slots_ref[numbers + which]], pay_ref.at[which % 2], sem_ref.at[which % 2]
-        )
 
     @pl.when((slot == 0) & (step == 0) & (slots_ref[0] > 0))
     def _():
-        fetch(0).start()
+        fetch(0)
 
     @pl.when(slot < slots_ref[0])
     def _():
         @pl.when(step == 0)
         def _():
-            fetch(slot).wait()
+            pltpu.make_async_copy(
+                pay_ref.at[(slot + 1) % 2], pay_ref.at[slot % 2], sem_ref.at[slot % 2]
+            ).wait()
 
             @pl.when(slot + 1 < slots_ref[0])
             def _():
-                fetch(slot + 1).start()
+                fetch(slot + 1)
 
             feat, vec = unpack(pay_ref[slot % 2])
             left_ref[...] = other_factor(feat)
@@ -205,20 +207,50 @@
                 lax.fori_loop(0, right_ref.shape[1] // COLS, unit, 0)
 
 
-def pair_zero_kernel(
-    lists_ref, me_ref, right_ref, first_ref, every_ref, front_ref, back_ref, sum_ref, slots_ref, *refs
-):
+def pair_zero_kernel(block_at, me_ref, right_ref, *refs):
+    first_refs, block_refs = refs[:PARTS], refs[PARTS:-12]
+    front_ref, back_ref, sum_ref, slots_ref = refs[-12:-8]
+    left_ref, vec_ref, pay_ref, sem_ref, strip_ref, list_ref, lists_ref, strip_sem_ref = refs[-8:]
+
     @pl.when((pl.program_id(0) == 0) & (pl.program_id(1) == 0))
     def _():
+        strips = [
+            pltpu.make_async_copy(
+                block_refs[index].at[pl.ds(row + 80, 16), pl.ds(0, 128)],
+                strip_ref.at[at],
+                strip_sem_ref.at[at],
+            )
+            for at, (index, row) in enumerate(block_at)
+        ]
+        for strip in strips:
+            strip.start()
+        sum_ref[...] = functools.reduce(jnp.add, [first_ref[...] for first_ref in first_refs])
+        for at, strip in enumerate(strips):
+            strip.wait()
+            list_ref[at : at + 1, :] = strip_ref[at].astype(F32)[:1].astype(jnp.int32)
+        numbers = pltpu.make_async_copy(list_ref, lists_ref, strip_sem_ref.at[0])
+        numbers.start()
+        numbers.wait()
         find_partners(lists_ref, me_ref[0], slots_ref)
-        sum_ref[...] = first_ref[...]
-
-    half_tiles(slots_ref, right_ref, every_ref, front_ref, back_ref, sum_ref, *refs)
+
+    def fetch(which):
+        for at, (index, row) in enumerate(block_at):
+            @pl.when(slots_ref[1 + which] == at)
+            def _():
+                pltpu.make_async_copy(
+                    block_refs[index].at[pl.ds(row, 80)],
+                    pay_ref.at[which % 2],
+                    sem_ref.at[which % 2],
+                ).start()
+
+    half_tiles(
+        slots_ref, right_ref, fetch, front_ref, back_ref, sum_ref, left_ref, vec_ref, pay_ref, sem_ref
+    )
 
 
 def pair_one_kernel(
     slots_ref, right_ref, first_ref, every_ref, rhs_ref, var_ref,
-    front_ref, back_ref, image_ref, send_ref, *refs
+    front_ref, back_ref, image_ref, send_ref, left_ref, vec_ref, pay_ref, sem_ref,
 ):
     slot, step = pl.program_id(0), pl.program_id(1)
 
@@ -226,7 +258,15 @@
     def _():
         image_ref[...] = first_ref[...]
 
-    half_tiles(slots_ref, right_ref, every_ref, front_ref, back_ref, image_ref, *refs)
+    def fetch(which):
+        number = slots_ref[pl.num_programs(0) + 2 + which]
+        pltpu.make_async_copy(
+            every_ref.at[number], pay_ref.at[which % 2], sem_ref.at[which % 2]
+        ).start()
+
+    half_tiles(
+        slots_ref, right_ref, fetch, front_ref, back_ref, image_ref, left_ref, vec_ref, pay_ref, sem_ref
+    )
 
     @pl.when((slot == pl.num_programs(0) - 1) & (step == pl.num_programs(1) - 1))
     def _():
@@ -378,6 +418,17 @@
     return out
 
 
+def gate(block, behind):
+    return pl.pallas_call(
+        lambda *refs: None,
+        in_specs=[pl.BlockSpec(memory_space=pl.ANY)] * 2,
+        out_specs=pl.BlockSpec(memory_space=pl.ANY),
+        out_shape=jax.ShapeDtypeStruct(block.shape, block.dtype),
+        input_output_aliases={0: 0},
+        name="gate",
+    )(block, behind)
+
+
 def local(features, right_side, variance, hilbert_order, tile_list):
     width = features.shape[1]
     rhs_count = right_side.shape[0]
@@ -392,35 +443,56 @@
     row_spec = pl.BlockSpec(right_side.shape, whole)
     var_spec = pl.BlockSpec(var_row.shape, whole)
     pay_shape = (80, width // 4)
+    smem = pl.BlockSpec(memory_space=pltpu.SMEM)
+    vmem = pl.BlockSpec(memory_space=pltpu.VMEM)
     pay_zero, pay_one, right = pl.pallas_call(
         payload_kernel,
-        out_shape=[shape(pay_shape, BF16), shape(pay_shape, BF16), shape((KDIM, width), BF16)],
+        in_specs=[smem, vmem, vmem],
+        out_shape=[
+            shape((96, width // 4), BF16),
+            shape(pay_shape, BF16),
+            shape((KDIM, width), BF16),
+        ],
         compiler_params=params,
         name="payload",
-    )(features, right_side)
+    )(tile_list, features, right_side)
     in_hbm = lambda array: pltpu.with_memory_space_constraint(array, pltpu.HBM)
-    every_zero = in_hbm(lax.all_gather(pay_zero, "row", axis=0))
     every_one = in_hbm(lax.all_gather(pay_one, "row", axis=0))
-    lists = tree_gather(tile_list[0, :, 1], count)
     me = jnp.full((1,), lax.axis_index("row"), jnp.int32)
     any_spec = pl.BlockSpec(memory_space=pl.ANY)
-    blocks = own_blocks(width // ROWS)
-    own_tiles, own_sum = pl.pallas_call(
-        own_kernel,
-        out_specs=[any_spec, pl.BlockSpec(memory_space=pltpu.VMEM)],
-        out_shape=[pltpu.HBM((len(blocks), ROWS, ROWS), BF16), shape(right_side.shape, F32)],
-        scratch_shapes=[
-            pltpu.VMEM((width, KDIM), BF16),
-            pltpu.VMEM((rhs_count, width), BF16),
-            pltpu.VMEM((len(blocks), ROWS, ROWS), BF16),
-            pltpu.SemaphoreType.DMA((len(blocks),)),
-        ],
-        compiler_params=params,
-        cost_estimate=pl.CostEstimate(
-            flops=9_000_000_000, bytes_accessed=2 * len(blocks) * ROWS * ROWS, transcendentals=0
-        ),
-        name="own_tile",
-    )(features, right_side, right)
+
+    def own_part(rows, arrived):
+        blocks = own_blocks(rows, steps)
+        tiles, sums = pl.pallas_call(
+            functools.partial(own_kernel, rows),
+            in_specs=[vmem, vmem, vmem, any_spec],
+            out_specs=[any_spec, vmem],
+            out_shape=[pltpu.HBM((len(blocks), ROWS, ROWS), BF16), shape(right_side.shape, F32)],
+            scratch_shapes=[
+                pltpu.VMEM((width, KDIM), BF16),
+                pltpu.VMEM((rhs_count, width), BF16),
+                pltpu.VMEM((len(blocks), ROWS, ROWS), BF16),
+                pltpu.SemaphoreType.DMA((len(blocks),)),
+            ],
+            compiler_params=params,
+            cost_estimate=pl.CostEstimate(
+                flops=5_000_000_000, bytes_accessed=2 * len(blocks) * ROWS * ROWS, transcendentals=0
+            ),
+            name=f"own_tile_{rows[0]}",
+        )(features, right_side, right, arrived)
+        return blocks, tiles, sums
+
+    first_masks, *later = gather_levels(count)
+    near = jnp.concatenate([pay_zero] + [swap(pay_zero, mask, count) for mask in first_masks], axis=0)
+    own_parts = [own_part(range(1), right)]
+    near = gate(near, own_parts[0][2])
+    own_parts.append(own_part(range(1, steps), near))
+    arrays = [near]
+    for level, masks in enumerate(later):
+        arrays = arrays + [swap(array, mask, count) for mask in masks for array in arrays]
+        if level == 0:
+            arrays[-1] = gate(arrays[-1], own_parts[1][2])
+    block_at = [(at, row * 96) for at in range(len(arrays)) for row in range(len(first_masks) + 1)]
 
     half = steps // 2
 
@@ -444,19 +516,25 @@
     right_spec = pl.BlockSpec(right.shape, whole)
     send_shape = (rhs_count, width + TAIL)
     front_zero, back_zero, half_sum, slots = pl.pallas_call(
-        pair_zero_kernel,
+        functools.partial(pair_zero_kernel, block_at),
         grid_spec=pltpu.PrefetchScalarGridSpec(
-            num_scalar_prefetch=2,
+            num_scalar_prefetch=1,
             grid=(most, half),
-            in_specs=[right_spec, row_spec, any_spec],
-            out_specs=half_specs + [row_spec, pl.BlockSpec(memory_space=pltpu.SMEM)],
-            scratch_shapes=half_scratch,
+            in_specs=[right_spec] + [row_spec] * PARTS + [any_spec] * len(arrays),
+            out_specs=half_specs + [row_spec, smem],
+            scratch_shapes=half_scratch
+            + [
+                pltpu.VMEM((count, 16, 128), BF16),
+                pltpu.VMEM((count, 128), jnp.int32),
+                pltpu.SMEM((count, 128), jnp.int32),
+                pltpu.SemaphoreType.DMA((count,)),
+            ],
         ),
         out_shape=half_shapes
         + [shape(right_side.shape, F32), shape((2 * (most + 2),), jnp.int32)],
         compiler_params=params,
         name="pair_zero",
-    )(lists[-1], me, right, own_sum, every_zero)
+    )(me, right, *[part[2] for part in own_parts], *arrays)
     front_one, back_one, image, send = pl.pallas_call(
         pair_one_kernel,
         grid_spec=pltpu.PrefetchScalarGridSpec(
@@ -480,27 +558,24 @@
         return (jnp.minimum(k, FRONT - 1), jnp.where(k < FRONT, jnp.maximum(i - half, 0), half - 1), 0)
 
     every_send = tree_gather(send, count)[-1]
-    own_again = []
-    part = -(-len(blocks) // PARTS)
-    for first in range(0, len(blocks), part):
-        here = blocks[first : first + part]
-        own_again.append(
-            pl.pallas_call(
-                functools.partial(own_again_kernel, first, here),
-                in_specs=[any_spec, pl.BlockSpec(send_shape, whole)],
-                out_specs=row_spec,
-                out_shape=shape(right_side.shape, F32),
-                scratch_shapes=[
-                    pltpu.VMEM((len(here), ROWS, ROWS), BF16),
-                    pltpu.SemaphoreType.DMA((len(here),)),
-                ],
-                compiler_params=params,
-                cost_estimate=pl.CostEstimate(
-                    flops=5_000_000_000, bytes_accessed=2 * len(here) * ROWS * ROWS, transcendentals=0
-                ),
-                name=f"own_again_{first}",
-            )(pltpu.with_memory_space_constraint(own_tiles, pltpu.HBM), send)
-        )
+    own_again = [
+        pl.pallas_call(
+            functools.partial(own_again_kernel, blocks),
+            in_specs=[any_spec, pl.BlockSpec(send_shape, whole)],
+            out_specs=row_spec,
+            out_shape=shape(right_side.shape, F32),
+            scratch_shapes=[
+                pltpu.VMEM((len(blocks), ROWS, ROWS), BF16),
+                pltpu.SemaphoreType.DMA((len(blocks),)),
+            ],
+            compiler_params=params,
+            cost_estimate=pl.CostEstimate(
+                flops=5_000_000_000, bytes_accessed=2 * len(blocks) * ROWS * ROWS, transcendentals=0
+            ),
+            name=f"own_again_{part}",
+        )(in_hbm(tiles), send)
+        for part, (blocks, tiles, _) in enumerate(own_parts)
+    ]
     dots_spec = pl.BlockSpec((rhs_count, TAIL), whole)
     rows, dots, steps_one = pl.pallas_call(
         again_kernel,

time: 168 us -> 156 us (0.929)
  waiting for transfers between devices: 31.5 us -> 12.9 us
  local copies, waits for them, and re-layouts: 9.32 us -> 13.8 us
  Pallas kernels: 91.7 us -> 93.5 us
    all_gather x1 -> x0, waiting for transfers between devices: 19.1 us -> none  [local(): every_zero = in_hbm(lax.all_gather(pay_zero, 'row', axis=0))]
    unnamed x26 -> x45, local copies, waits for them, and re-layouts: 8.54 us -> 13.7 us
    ppermute x16 -> x17, waiting for transfers between devices: 9.23 us -> 12.9 us  [swap(): return lax.ppermute(value, 'row', [(i, i ^ mask) for i in range(count)])]
    all_gather x1, waiting for transfers between devices: 2.42 us -> 0.01 us  [local(): every_one = in_hbm(lax.all_gather(pay_one, 'row', axis=0))]
    pallas_call x5 -> x8, Pallas kernels: 47.9 us -> 49.6 us  [the longest x1 33.6 us: local(): pl.pallas_call(functools.partial(pair_zero_kernel, block_at), grid_spec=p...]
    ppermute x16 -> x17, starting transfers between devices: 19.1 us -> 19.8 us  [swap(): return lax.ppermute(value, 'row', [(i, i ^ mask) for i in range(count)])]
  transfers between devices with their start and end apart: 18 -> 18, of which waited for: 8 -> 7; matrix products, arithmetic and copies ran while one was open for 0% -> 1% of each run, Pallas kernels for 29% -> 32%
where the time goes in v10:
time: 156 us
  Pallas kernels  93.5 us (60%)
  starting transfers between devices  19.8 us (13%)
  between operations  14.3 us (9%)
  local copies, waits for them, and re-layouts  13.8 us (9%)
  waiting for transfers between devices  12.9 us (8%)
  other arithmetic  1.79 us (1%)
    pallas_call x1, Pallas kernels, local(): pl.pallas_call(functools.partial(pair_zero_kernel, block_at), grid_spec=p...  33.6 us
    pallas_call x1, Pallas kernels, local(): pl.pallas_call(pair_one_kernel, grid_spec=pltpu.PrefetchScalarGridSpec(nu...  32.3 us
    ppermute x17, starting transfers between devices, swap(): return lax.ppermute(value, 'row', [(i, i ^ mask) for i in range(count)])  19.8 us
    unnamed x45, local copies, waits for them, and re-layouts  13.7 us
    ppermute x17, waiting for transfers between devices, swap(): return lax.ppermute(value, 'row', [(i, i ^ mask) for i in range(count)])  12.9 us
    pallas_call x1, Pallas kernels, local(): pl.pallas_call(again_kernel, grid_spec=pltpu.PrefetchScalarGridSpec(num_s...  10.1 us
    pallas_call x2, Pallas kernels, own_part(): pl.pallas_call(functools.partial(own_kernel, rows), in_specs=[vmem, vmem,...  10 us
    pallas_call x2, Pallas kernels, local(): pl.pallas_call(functools.partial(own_again_kernel, blocks), in_specs=[any...  4.63 us
  transfers between devices with their start and end apart: 18, of which 7 were waited for; matrix products, arithmetic and copies ran while one was open for 1% of the time, Pallas kernels for 32%

profile of v10, /device:TPU:0, one launch (start us, length us, event | category | flops | bytes accessed | tf_op | source)
XLA Modules:
  0.0 156.0 jit_solution(1055389693714558896)
XLA Ops:
  9.7 1.4 payload.1
  11.1 5.1 %collective-permute-start.2 = (bf16[96,512]{1,0:T(8,128)(2,1)S(1)}, bf16[96,512]{1,0:T(8,128)(2,1)S(1)}, u32[]{:S(2)}, u32[]{:S(2)}) collective-permute-start(bf16[96,512]{1,0:T(8,128)(2,1)S(1)} %get-tuple-element.22), channel_id=1, source_target_pairs={{0,12},{1,13},{2,14},{3,15},{4,8},{5,9},{6,10},{7,11},{8,4},{9,5},... | collective-permute-start | bytes 294920 | tf_op jit(solution)/shard_map/ppermute | solution.py:378
  18.6 4.2 %own_tile_0.1 = (bf16[4,512,512]{2,1,0:T(8,128)(2,1)}, f32[8,2048]{1,0:T(8,128)S(1)}) custom-call(bf16[32,2048]{1,0:T(8,128)(2,1)S(1)} %copy-done.13, f32[8,2048]{1,0:T(8,128)S(1)} %copy-done.6, bf16[128,2048]{1,0:T(8,128)(2,1)S(1)} %get-tuple-element.20.right_ref.arrived_ref, bf16[128,2048]{1,0:T(8,128)(2,1)S(1)} %get-tuple-element.20.right_ref.arrived_ref), custom_call_target="tpu_custom_call" | custom-call | flops 5000000000 | bytes 2097152 | tf_op jit(solution)/shard_map/own_tile_0/pallas_call | solution.py:466
  22.8 1.7 %collective-permute-done.1 = bf16[96,512]{1,0:T(8,128)(2,1)S(1)} collective-permute-done((bf16[96,512]{1,0:T(8,128)(2,1)S(1)}, bf16[96,512]{1,0:T(8,128)(2,1)S(1)}, u32[]{:S(2)}, u32[]{:S(2)}) %collective-permute-start.1) | collective-permute-done | bytes 98336 | tf_op jit(solution)/shard_map/ppermute | solution.py:378
  25.3 1.6 %collective-permute-start.3 = (bf16[384,512]{1,0:T(8,128)(2,1)}, bf16[384,512]{1,0:T(8,128)(2,1)S(1)}, u32[]{:S(2)}, u32[]{:S(2)}) collective-permute-start(bf16[384,512]{1,0:T(8,128)(2,1)} %gate.2.arrived_ref.refs_2_), channel_id=1, source_target_pairs={{0,2},{1,3},{2,0},{3,1},{4,6},{5,7},{6,4},{7,5},{8,10},{9,11},{10,... | collective-permute-start | bytes 1179656 | tf_op jit(solution)/shard_map/ppermute | solution.py:378
  26.9 1.0 copy-done.1
  27.9 5.8 %own_tile_1.1 = (bf16[6,512,512]{2,1,0:T(8,128)(2,1)}, f32[8,2048]{1,0:T(8,128)S(1)}) custom-call(bf16[32,2048]{1,0:T(8,128)(2,1)S(1)} %copy-done.14, f32[8,2048]{1,0:T(8,128)S(1)} %copy-done.7, bf16[128,2048]{1,0:T(8,128)(2,1)S(1)} %get-tuple-element.20.right_ref.arrived_ref, bf16[384,512]{1,0:T(8,128)(2,1)S(1)} %copy-done.1), custom_call_target="tpu_custom_call" | custom-call | flops 5000000000 | bytes 3145728 | tf_op jit(solution)/shard_map/own_tile_1/pallas_call | solution.py:466
  34.4 2.6 %collective-permute-done.3.refs_0_ = bf16[384,512]{1,0:T(8,128)(2,1)S(1)} collective-permute-done((bf16[384,512]{1,0:T(8,128)(2,1)}, bf16[384,512]{1,0:T(8,128)(2,1)S(1)}, u32[]{:S(2)}, u32[]{:S(2)}) %collective-permute-start.3) | collective-permute-done | bytes 393248 | tf_op jit(solution)/shard_map/ppermute | solution.py:378
  37.8 1.9 %collective-permute-done.5.refs_5_ = bf16[384,512]{1,0:T(8,128)(2,1)S(1)} collective-permute-done((bf16[384,512]{1,0:T(8,128)(2,1)}, bf16[384,512]{1,0:T(8,128)(2,1)S(1)}, u32[]{:S(2)}, u32[]{:S(2)}) %collective-permute-start.5) | collective-permute-done | bytes 393248 | tf_op jit(solution)/shard_map/ppermute | solution.py:378
  41.6 33.6 %pair_zero.1 = (bf16[3,1024,2048]{2,1,0:T(8,128)(2,1)S(1)}, bf16[2,1024,2048]{2,1,0:T(8,128)(2,1)}, f32[8,2048]{1,0:T(8,128)S(1)}, s32[14]{0:T(128)S(1)}) custom-call(s32[1]{0:T(128)} %bitcast.me_ref, bf16[128,2048]{1,0:T(8,128)(2,1)S(1)} %get-tuple-element.20.right_ref.arrived_ref, f32[8,2048]{1,0:T(8,128)S(1)} %copy-done.9, f32[8,2048]{1,0:T(8,128)S(1)} %copy-done.11, ...), custom_call_target="tpu_custom_call" | custom-call | tf_op jit(solution)/shard_map/pair_zero/pallas_call | solution.py:518
  75.2 4.5 %copy-done = bf16[3,1024,2048]{2,1,0:T(8,128)(2,1)} copy-done((bf16[3,1024,2048]{2,1,0:T(8,128)(2,1)}, bf16[3,1024,2048]{2,1,0:T(8,128)(2,1)S(1)}, u32[]{:S(2)}) %copy-start) | copy-done | bytes 12582936
  79.7 32.3 %pair_one.1 = (bf16[3,1024,2048]{2,1,0:T(8,128)(2,1)S(1)}, bf16[2,1024,2048]{2,1,0:T(8,128)(2,1)}, f32[8,2048]{1,0:T(8,128)S(1)}, bf16[8,2176]{1,0:T(8,128)(2,1)S(1)}) custom-call(s32[14]{0:T(128)S(1)} %get-tuple-element.24.slots_ref, bf16[128,2048]{1,0:T(8,128)(2,1)S(1)} %get-tuple-element.20.right_ref.arrived_ref, ...), custom_call_target="tpu_custom_call" | custom-call | tf_op jit(solution)/shard_map/pair_one/pallas_call | solution.py:538
  112.1 2.0 %collective-permute-start.7 = (bf16[1,8,2176]{2,1,0:T(8,128)(2,1)S(1)}, bf16[1,8,2176]{2,1,0:T(8,128)(2,1)S(1)}, u32[]{:S(2)}, u32[]{:S(2)}) collective-permute-start(bf16[1,8,2176]{2,1,0:T(8,128)(2,1)S(1)} %bitcast.9), channel_id=1, source_target_pairs={{0,8},{1,9},{2,10},{3,11},{4,12},{5,13},{6,14},{7,15},{8,0},{9,1},... | collective-permute-start | bytes 104456 | tf_op jit(solution)/shard_map/ppermute | solution.py:378
  114.1 2.3 %collective-permute-start.6 = (bf16[1,8,2176]{2,1,0:T(8,128)(2,1)S(1)}, bf16[1,8,2176]{2,1,0:T(8,128)(2,1)S(1)}, u32[]{:S(2)}, u32[]{:S(2)}) collective-permute-start(bf16[1,8,2176]{2,1,0:T(8,128)(2,1)S(1)} %bitcast.10), channel_id=1, source_target_pairs={{0,4},{1,5},{2,6},{3,7},{4,0},{5,1},{6,2},{7,3},{8,12},{9,13},{10,... | collective-permute-start | bytes 104456 | tf_op jit(solution)/shard_map/ppermute | solution.py:378
  116.5 2.5 %own_again_1.1.refs_1_ = f32[8,2048]{1,0:T(8,128)S(1)} custom-call(bf16[6,512,512]{2,1,0:T(8,128)(2,1)} %get-tuple-element.34.in_ref, bf16[8,2176]{1,0:T(8,128)(2,1)S(1)} %get-tuple-element.31.vec_ref), custom_call_target="tpu_custom_call" | custom-call | flops 5000000000 | bytes 3145728 | tf_op jit(solution)/shard_map/own_again_1/pallas_call | solution.py:562
  119.1 1.6 %collective-permute-start.9 = (bf16[4,8,2176]{2,1,0:T(8,128)(2,1)S(1)}, bf16[4,8,2176]{2,1,0:T(8,128)(2,1)S(1)}, u32[]{:S(2)}, u32[]{:S(2)}) collective-permute-start(bf16[4,8,2176]{2,1,0:T(8,128)(2,1)S(1)} %pad_maximum_fusion.1), channel_id=1, source_target_pairs={{0,2},{1,3},{2,0},{3,1},{4,6},{5,7},{6,4},{7,5},{8,10},{9,11},{10,... | collective-permute-start | bytes 417800 | tf_op jit(solution)/shard_map/ppermute | solution.py:378
  120.7 3.5 %collective-permute-done.9 = bf16[4,8,2176]{2,1,0:T(8,128)(2,1)S(1)} collective-permute-done((bf16[4,8,2176]{2,1,0:T(8,128)(2,1)S(1)}, bf16[4,8,2176]{2,1,0:T(8,128)(2,1)S(1)}, u32[]{:S(2)}, u32[]{:S(2)}) %collective-permute-start.9) | collective-permute-done | bytes 139296 | tf_op jit(solution)/shard_map/ppermute | solution.py:378
  124.3 2.1 %own_again_0.1.refs_0_ = f32[8,2048]{1,0:T(8,128)S(1)} custom-call(bf16[4,512,512]{2,1,0:T(8,128)(2,1)} %get-tuple-element.33.in_ref, bf16[8,2176]{1,0:T(8,128)(2,1)S(1)} %get-tuple-element.31.vec_ref), custom_call_target="tpu_custom_call" | custom-call | flops 5000000000 | bytes 2097152 | tf_op jit(solution)/shard_map/own_again_0/pallas_call | solution.py:562
  127.1 10.1 %pair_again.1 = (f32[32,2048]{1,0:T(8,128)S(1)}, f32[8,128]{1,0:T(8,128)S(1)}, f32[8,128]{1,0:T(8,128)S(1)}) custom-call(s32[14]{0:T(128)S(1)} %get-tuple-element.24.slots_ref, bf16[3,1024,2048]{2,1,0:T(8,128)(2,1)S(1)} %bitcast.7, bf16[3,1024,2048]{2,1,0:T(8,128)(2,1)S(1)} %get-tuple-element.28.front_one_ref, ...), custom_call_target="tpu_custom_call" | custom-call | tf_op jit(solution)/shard_map/pair_again/pallas_call | solution.py:580
  137.3 2.8 %collective-permute-start.12 = (f32[8,128]{1,0:T(8,128)S(1)}, f32[8,128]{1,0:T(8,128)S(1)}, u32[]{:S(2)}, u32[]{:S(2)}) collective-permute-start(f32[8,128]{1,0:T(8,128)S(1)} %get-tuple-element.37), channel_id=1, source_target_pairs={{0,8},{1,9},{2,10},{3,11},{4,12},{5,13},{6,14},{7,15},{8,0},{9,1},... | collective-permute-start | bytes 12296 | tf_op jit(solution)/shard_map/ppermute | solution.py:378
  140.1 1.6 %collective-permute-start.11 = (f32[8,128]{1,0:T(8,128)S(1)}, f32[8,128]{1,0:T(8,128)S(1)}, u32[]{:S(2)}, u32[]{:S(2)}) collective-permute-start(f32[8,128]{1,0:T(8,128)S(1)} %get-tuple-element.37), channel_id=1, source_target_pairs={{0,4},{1,5},{2,6},{3,7},{4,0},{5,1},{6,2},{7,3},{8,12},{9,13},{10,... | collective-permute-start | bytes 12296 | tf_op jit(solution)/shard_map/ppermute | solution.py:378
  142.7 1.0 collective-permute-done.11
  145.6 1.5 curve_order.1
  147.1 1.1 collective-permute-done.15
  (78 shorter events, 13.8 us)
Async XLA Ops:
  7.2 72.5 %all-gather.3.cloned.1.call-start = ((), (), s32[]{:S(2)}) async-start(), calls=%async_computation | async-start | bytes 1392640 | tf_op jit(solution)/shard_map/all_gather | solution.py:460
  11.1 11.7 %collective-permute-start.2 = (bf16[96,512]{1,0:T(8,128)(2,1)S(1)}, bf16[96,512]{1,0:T(8,128)(2,1)S(1)}, u32[]{:S(2)}, u32[]{:S(2)}) collective-permute-start(bf16[96,512]{1,0:T(8,128)(2,1)S(1)} %get-tuple-element.22), channel_id=1, source_target_pairs={{0,12},{1,13},{2,14},{3,15},{4,8},{5,9},{6,10},{7,11},{8,4},{9,5},... | collective-permute-start | bytes 294920 | tf_op jit(solution)/shard_map/ppermute | solution.py:378
  16.2 8.3 %collective-permute-start.1 = (bf16[96,512]{1,0:T(8,128)(2,1)S(1)}, bf16[96,512]{1,0:T(8,128)(2,1)S(1)}, u32[]{:S(2)}, u32[]{:S(2)}) collective-permute-start(bf16[96,512]{1,0:T(8,128)(2,1)S(1)} %get-tuple-element.22), channel_id=1, source_target_pairs={{0,8},{1,9},{2,10},{3,11},{4,12},{5,13},{6,14},{7,15},{8,0},{9,1},... | collective-permute-start | bytes 294920 | tf_op jit(solution)/shard_map/ppermute | solution.py:378
  16.2 8.3 %collective-permute-start = (bf16[96,512]{1,0:T(8,128)(2,1)S(1)}, bf16[96,512]{1,0:T(8,128)(2,1)S(1)}, u32[]{:S(2)}, u32[]{:S(2)}) collective-permute-start(bf16[96,512]{1,0:T(8,128)(2,1)S(1)} %get-tuple-element.22), channel_id=1, source_target_pairs={{0,4},{1,5},{2,6},{3,7},{4,0},{5,1},{6,2},{7,3},{8,12},{9,13},{10,... | collective-permute-start | bytes 294920 | tf_op jit(solution)/shard_map/ppermute | solution.py:378
  25.3 54.4 %copy-start.15 = (f32[2048]{0:T(1024)S(1)}, f32[2048]{0:T(1024)}, u32[]{:S(2)}) copy-start(f32[2048]{0:T(1024)} %param.7) | copy-start | bytes 24580
  25.3 12.5 %collective-permute-start.4 = (bf16[384,512]{1,0:T(8,128)(2,1)}, bf16[384,512]{1,0:T(8,128)(2,1)S(1)}, u32[]{:S(2)}, u32[]{:S(2)}) collective-permute-start(bf16[384,512]{1,0:T(8,128)(2,1)} %gate.2.arrived_ref.refs_2_), channel_id=1, source_target_pairs={{0,1},{1,0},{2,3},{3,2},{4,5},{5,4},{6,7},{7,6},{8,9},{9,8},{10,11... | collective-permute-start | bytes 1179656 | tf_op jit(solution)/shard_map/ppermute | solution.py:378
  25.3 11.7 %collective-permute-start.3 = (bf16[384,512]{1,0:T(8,128)(2,1)}, bf16[384,512]{1,0:T(8,128)(2,1)S(1)}, u32[]{:S(2)}, u32[]{:S(2)}) collective-permute-start(bf16[384,512]{1,0:T(8,128)(2,1)} %gate.2.arrived_ref.refs_2_), channel_id=1, source_target_pairs={{0,2},{1,3},{2,0},{3,1},{4,6},{5,7},{6,4},{7,5},{8,10},{9,11},{10,... | collective-permute-start | bytes 1179656 | tf_op jit(solution)/shard_map/ppermute | solution.py:378
  27.9 11.8 %copy-start.2 = (bf16[384,512]{1,0:T(8,128)(2,1)S(1)}, bf16[384,512]{1,0:T(8,128)(2,1)}, u32[]{:S(2)}) copy-start(bf16[384,512]{1,0:T(8,128)(2,1)} %gate.2.arrived_ref.refs_2_) | copy-start | bytes 1179652
  27.9 11.8 %copy-start.9 = (f32[8,2048]{1,0:T(8,128)S(1)}, f32[8,2048]{1,0:T(8,128)}, u32[]{:S(2)}) copy-start(f32[8,2048]{1,0:T(8,128)} %copy-done.8) | copy-start | bytes 196612
  37.8 1.9 %collective-permute-start.5 = (bf16[384,512]{1,0:T(8,128)(2,1)}, bf16[384,512]{1,0:T(8,128)(2,1)S(1)}, u32[]{:S(2)}, u32[]{:S(2)}) collective-permute-start(bf16[384,512]{1,0:T(8,128)(2,1)} %gate.3.refs_3_), channel_id=1, source_target_pairs={{0,1},{1,0},{2,3},{3,2},{4,5},{5,4},{6,7},{7,6},{8,9},{9,8},{10,11... | collective-permute-start | bytes 1179656 | tf_op jit(solution)/shard_map/ppermute | solution.py:378
  112.0 7.0 %collective-permute-start.8 = (bf16[1,8,2176]{2,1,0:T(8,128)(2,1)S(1)}, bf16[1,8,2176]{2,1,0:T(8,128)(2,1)S(1)}, u32[]{:S(2)}, u32[]{:S(2)}) collective-permute-start(bf16[1,8,2176]{2,1,0:T(8,128)(2,1)S(1)} %bitcast.8), channel_id=1, source_target_pairs={{0,12},{1,13},{2,14},{3,15},{4,8},{5,9},{6,10},{7,11},{8,4},{9,5},... | collective-permute-start | bytes 104456 | tf_op jit(solution)/shard_map/ppermute | solution.py:378
  112.1 6.9 %collective-permute-start.7 = (bf16[1,8,2176]{2,1,0:T(8,128)(2,1)S(1)}, bf16[1,8,2176]{2,1,0:T(8,128)(2,1)S(1)}, u32[]{:S(2)}, u32[]{:S(2)}) collective-permute-start(bf16[1,8,2176]{2,1,0:T(8,128)(2,1)S(1)} %bitcast.9), channel_id=1, source_target_pairs={{0,8},{1,9},{2,10},{3,11},{4,12},{5,13},{6,14},{7,15},{8,0},{9,1},... | collective-permute-start | bytes 104456 | tf_op jit(solution)/shard_map/ppermute | solution.py:378
  114.1 4.9 %collective-permute-start.6 = (bf16[1,8,2176]{2,1,0:T(8,128)(2,1)S(1)}, bf16[1,8,2176]{2,1,0:T(8,128)(2,1)S(1)}, u32[]{:S(2)}, u32[]{:S(2)}) collective-permute-start(bf16[1,8,2176]{2,1,0:T(8,128)(2,1)S(1)} %bitcast.10), channel_id=1, source_target_pairs={{0,4},{1,5},{2,6},{3,7},{4,0},{5,1},{6,2},{7,3},{8,12},{9,13},{10,... | collective-permute-start | bytes 104456 | tf_op jit(solution)/shard_map/ppermute | solution.py:378
  116.5 10.0 %slice-start = ((s8[12582912]{0:T(1024)(128)(4,1)}), s8[4194304]{0:T(1024)(128)(4,1)S(1)}, s32[]{:S(2)}) async-start(s8[12582912]{0:T(1024)(128)(4,1)} %bitcast.6), calls=%async_computation.1 | async-start | bytes 8388608
  116.5 10.0 %slice-start.1 = ((s8[12582912]{0:T(1024)(128)(4,1)}), s8[4194304]{0:T(1024)(128)(4,1)S(1)}, s32[]{:S(2)}) async-start(s8[12582912]{0:T(1024)(128)(4,1)} %bitcast.6), calls=%async_computation.2 | async-start | bytes 8388608
  119.1 5.1 %collective-permute-start.9 = (bf16[4,8,2176]{2,1,0:T(8,128)(2,1)S(1)}, bf16[4,8,2176]{2,1,0:T(8,128)(2,1)S(1)}, u32[]{:S(2)}, u32[]{:S(2)}) collective-permute-start(bf16[4,8,2176]{2,1,0:T(8,128)(2,1)S(1)} %pad_maximum_fusion.1), channel_id=1, source_target_pairs={{0,2},{1,3},{2,0},{3,1},{4,6},{5,7},{6,4},{7,5},{8,10},{9,11},{10,... | collective-permute-start | bytes 417800 | tf_op jit(solution)/shard_map/ppermute | solution.py:378
  124.2 2.2 %collective-permute-start.10 = (bf16[8,8,2176]{2,1,0:T(8,128)(2,1)S(1)}, bf16[8,8,2176]{2,1,0:T(8,128)(2,1)S(1)}, u32[]{:S(2)}, u32[]{:S(2)}) collective-permute-start(bf16[8,8,2176]{2,1,0:T(8,128)(2,1)S(1)} %get-tuple-element.43), channel_id=1, source_target_pairs={{0,1},{1,0},{2,3},{3,2},{4,5},{5,4},{6,7},{7,6},{8,9},{9,8},{10,11... | collective-permute-start | bytes 835592 | tf_op jit(solution)/shard_map/ppermute | solution.py:378
  127.1 18.5 %copy-start.16 = (s32[1,2048]{1,0:T(1,128)S(1)}, s32[1,2048]{1,0:T(1,128)}, u32[]{:S(2)}) copy-start(s32[1,2048]{1,0:T(1,128)} %perm_ref.1) | copy-start | bytes 24580
  137.2 5.5 %collective-permute-start.13 = (f32[8,128]{1,0:T(8,128)S(1)}, f32[8,128]{1,0:T(8,128)S(1)}, u32[]{:S(2)}, u32[]{:S(2)}) collective-permute-start(f32[8,128]{1,0:T(8,128)S(1)} %get-tuple-element.37), channel_id=1, source_target_pairs={{0,12},{1,13},{2,14},{3,15},{4,8},{5,9},{6,10},{7,11},{8,4},{9,5},... | collective-permute-start | bytes 12296 | tf_op jit(solution)/shard_map/ppermute | solution.py:378
  137.3 5.4 %collective-permute-start.12 = (f32[8,128]{1,0:T(8,128)S(1)}, f32[8,128]{1,0:T(8,128)S(1)}, u32[]{:S(2)}, u32[]{:S(2)}) collective-permute-start(f32[8,128]{1,0:T(8,128)S(1)} %get-tuple-element.37), channel_id=1, source_target_pairs={{0,8},{1,9},{2,10},{3,11},{4,12},{5,13},{6,14},{7,15},{8,0},{9,1},... | collective-permute-start | bytes 12296 | tf_op jit(solution)/shard_map/ppermute | solution.py:378
  140.1 3.6 %collective-permute-start.11 = (f32[8,128]{1,0:T(8,128)S(1)}, f32[8,128]{1,0:T(8,128)S(1)}, u32[]{:S(2)}, u32[]{:S(2)}) collective-permute-start(f32[8,128]{1,0:T(8,128)S(1)} %get-tuple-element.37), channel_id=1, source_target_pairs={{0,4},{1,5},{2,6},{3,7},{4,0},{5,1},{6,2},{7,3},{8,12},{9,13},{10,... | collective-permute-start | bytes 12296 | tf_op jit(solution)/shard_map/ppermute | solution.py:378
  143.7 3.3 %collective-permute-start.16 = (f32[8,128]{1,0:T(8,128)S(1)}, f32[8,128]{1,0:T(8,128)S(1)}, u32[]{:S(2)}, u32[]{:S(2)}) collective-permute-start(f32[8,128]{1,0:T(8,128)S(1)} %add_add_fusion.1), channel_id=1, source_target_pairs={{0,3},{1,2},{2,1},{3,0},{4,7},{5,6},{6,5},{7,4},{8,11},{9,10},{10,... | collective-permute-start | bytes 12296 | tf_op jit(solution)/shard_map/ppermute | solution.py:378
  144.6 3.6 %collective-permute-start.15 = (f32[8,128]{1,0:T(8,128)S(1)}, f32[8,128]{1,0:T(8,128)S(1)}, u32[]{:S(2)}, u32[]{:S(2)}) collective-permute-start(f32[8,128]{1,0:T(8,128)S(1)} %add_add_fusion.1), channel_id=1, source_target_pairs={{0,2},{1,3},{2,0},{3,1},{4,6},{5,7},{6,4},{7,5},{8,10},{9,11},{10,... | collective-permute-start | bytes 12296 | tf_op jit(solution)/shard_map/ppermute | solution.py:378
  145.1 3.1 %collective-permute-start.14 = (f32[8,128]{1,0:T(8,128)S(1)}, f32[8,128]{1,0:T(8,128)S(1)}, u32[]{:S(2)}, u32[]{:S(2)}) collective-permute-start(f32[8,128]{1,0:T(8,128)S(1)} %add_add_fusion.1), channel_id=1, source_target_pairs={{0,1},{1,0},{2,3},{3,2},{4,5},{5,4},{6,7},{7,6},{8,9},{9,8},{10,11... | collective-permute-start | bytes 12296 | tf_op jit(solution)/shard_map/ppermute | solution.py:378
  (14 other events, 34.1 us)
Sparse Core Ops, SparseCore 0:
  11.2 41.6 all-gather.2

commit v11 on v10

--- a/solution.py
+++ b/solution.py
@@ -80,14 +80,10 @@
 
 
 def own_kernel(
-    rows, feat_ref, rhs_ref, right_ref, arrived_ref, out_ref, sum_ref,
-    left_ref, vec_ref, tile_ref, sem_ref,
+    rows, left_ref, right_ref, vec_ref, arrived_ref, out_ref, sum_ref, tile_ref, sem_ref
 ):
-    feat = feat_ref[...]
-    left_ref[...] = other_factor(feat)
-    vec_ref[...] = rhs_ref[...].astype(BF16)
     sum_ref[...] = jnp.zeros_like(sum_ref)
-    count = feat.shape[1] // ROWS
+    count = vec_ref.shape[1] // ROWS
     piece = lambda index: pl.ds(pl.multiple_of(index * ROWS, ROWS), ROWS)
     save = lambda at: pltpu.make_async_copy(tile_ref.at[at], out_ref.at[at], sem_ref.at[at])
 
@@ -134,7 +130,9 @@
             )
 
 
-def payload_kernel(list_ref, feat_ref, rhs_ref, pay_zero_ref, pay_one_ref, right_ref):
+def payload_kernel(
+    list_ref, feat_ref, rhs_ref, pay_zero_ref, pay_one_ref, right_ref, left_ref, vec_ref
+):
     feat = feat_ref[...]
     rounded = rhs_ref[...].astype(BF16)
     quarter = feat.shape[1] // 4
@@ -149,10 +147,12 @@
         numbers = jnp.where(lane == entry, list_ref[0, entry, 1], numbers)
     pay_zero_ref[80:96] = numbers.astype(F32).astype(BF16)
     right_ref[...] = own_factor(feat)
+    left_ref[...] = other_factor(feat)
+    vec_ref[...] = rounded
 
 
 def find_partners(lists_ref, me, slots_ref):
-    count, most = lists_ref.shape[0], slots_ref.shape[0] // 2 - 2
+    count, most = lists_ref.shape[0], slots_ref.shape[0] - 2
     for at in range(slots_ref.shape[0]):
         slots_ref[at] = 0
     total = jnp.int32(0)
@@ -164,9 +164,22 @@
         for entry in range(most):
             hit = hit | (lists_ref[at, entry] == me) | (lists_ref[0, entry] == number)
         slots_ref[1 + total] = jnp.where(hit, at, 0)
-        slots_ref[most + 2 + total] = jnp.where(hit, number, 0)
         total = total + hit.astype(jnp.int32)
     slots_ref[0] = total
+
+
+def fetch_from(block_at, block_refs, slots_ref, pay_ref, sem_ref):
+    def fetch(which):
+        for at, (index, row) in enumerate(block_at):
+            @pl.when(slots_ref[1 + which] == at)
+            def _():
+                pltpu.make_async_copy(
+                    block_refs[index].at[pl.ds(row, 80)],
+                    pay_ref.at[which % 2],
+                    sem_ref.at[which % 2],
+                ).start()
+
+    return fetch
 
 
 def half_tiles(slots_ref, right_ref, fetch, front_ref, back_ref, sum_ref, left_ref, vec_ref, pay_ref, sem_ref):
@@ -233,37 +246,22 @@
         numbers.wait()
         find_partners(lists_ref, me_ref[0], slots_ref)
 
-    def fetch(which):
-        for at, (index, row) in enumerate(block_at):
-            @pl.when(slots_ref[1 + which] == at)
-            def _():
-                pltpu.make_async_copy(
-                    block_refs[index].at[pl.ds(row, 80)],
-                    pay_ref.at[which % 2],
-                    sem_ref.at[which % 2],
-                ).start()
-
+    fetch = fetch_from(block_at, block_refs, slots_ref, pay_ref, sem_ref)
     half_tiles(
         slots_ref, right_ref, fetch, front_ref, back_ref, sum_ref, left_ref, vec_ref, pay_ref, sem_ref
     )
 
 
-def pair_one_kernel(
-    slots_ref, right_ref, first_ref, every_ref, rhs_ref, var_ref,
-    front_ref, back_ref, image_ref, send_ref, left_ref, vec_ref, pay_ref, sem_ref,
-):
+def pair_one_kernel(block_at, slots_ref, right_ref, first_ref, rhs_ref, var_ref, *refs):
+    block_refs = refs[:-8]
+    front_ref, back_ref, image_ref, send_ref, left_ref, vec_ref, pay_ref, sem_ref = refs[-8:]
     slot, step = pl.program_id(0), pl.program_id(1)
 
     @pl.when((slot == 0) & (step == 0))
     def _():
         image_ref[...] = first_ref[...]
 
-    def fetch(which):
-        number = slots_ref[pl.num_programs(0) + 2 + which]
-        pltpu.make_async_copy(
-            every_ref.at[number], pay_ref.at[which % 2], sem_ref.at[which % 2]
-        ).start()
-
+    fetch = fetch_from(block_at, block_refs, slots_ref, pay_ref, sem_ref)
     half_tiles(
         slots_ref, right_ref, fetch, front_ref, back_ref, image_ref, left_ref, vec_ref, pay_ref, sem_ref
     )
@@ -445,19 +443,20 @@
     pay_shape = (80, width // 4)
     smem = pl.BlockSpec(memory_space=pltpu.SMEM)
     vmem = pl.BlockSpec(memory_space=pltpu.VMEM)
-    pay_zero, pay_one, right = pl.pallas_call(
+    in_hbm = lambda array: pltpu.with_memory_space_constraint(array, pltpu.HBM)
+    pay_zero, pay_one, right, left, rounded = pl.pallas_call(
         payload_kernel,
         in_specs=[smem, vmem, vmem],
         out_shape=[
             shape((96, width // 4), BF16),
             shape(pay_shape, BF16),
             shape((KDIM, width), BF16),
+            shape((width, KDIM), BF16),
+            shape(right_side.shape, BF16),
         ],
         compiler_params=params,
         name="payload",
-    )(tile_list, features, right_side)
-    in_hbm = lambda array: pltpu.with_memory_space_constraint(array, pltpu.HBM)
-    every_one = in_hbm(lax.all_gather(pay_one, "row", axis=0))
+    )(tile_list, in_hbm(features), in_hbm(right_side))
     me = jnp.full((1,), lax.axis_index("row"), jnp.int32)
     any_spec = pl.BlockSpec(memory_space=pl.ANY)
 
@@ -469,8 +468,6 @@
             out_specs=[any_spec, vmem],
             out_shape=[pltpu.HBM((len(blocks), ROWS, ROWS), BF16), shape(right_side.shape, F32)],
             scratch_shapes=[
-                pltpu.VMEM((width, KDIM), BF16),
-                pltpu.VMEM((rhs_count, width), BF16),
                 pltpu.VMEM((len(blocks), ROWS, ROWS), BF16),
                 pltpu.SemaphoreType.DMA((len(blocks),)),
             ],
@@ -479,20 +476,29 @@
                 flops=5_000_000_000, bytes_accessed=2 * len(blocks) * ROWS * ROWS, transcendentals=0
             ),
             name=f"own_tile_{rows[0]}",
-        )(features, right_side, right, arrived)
+        )(left, right, rounded, arrived)
         return blocks, tiles, sums
 
     first_masks, *later = gather_levels(count)
-    near = jnp.concatenate([pay_zero] + [swap(pay_zero, mask, count) for mask in first_masks], axis=0)
+    first_level = lambda pay: jnp.concatenate(
+        [pay] + [swap(pay, mask, count) for mask in first_masks], axis=0
+    )
+    near_zero = first_level(pay_zero)
     own_parts = [own_part(range(1), right)]
-    near = gate(near, own_parts[0][2])
-    own_parts.append(own_part(range(1, steps), near))
-    arrays = [near]
+    near_zero = gate(near_zero, own_parts[0][2])
+    near_one = first_level(gate(pay_one, own_parts[0][2]))
+    own_parts.append(own_part(range(1, steps), near_zero))
+    near_one = gate(near_one, own_parts[1][2])
+    zero, places = [near_zero], [0]
     for level, masks in enumerate(later):
-        arrays = arrays + [swap(array, mask, count) for mask in masks for array in arrays]
+        zero = zero + [swap(array, mask, count) for mask in masks for array in zero]
+        places = places + [mask ^ place for mask in masks for place in places]
         if level == 0:
-            arrays[-1] = gate(arrays[-1], own_parts[1][2])
-    block_at = [(at, row * 96) for at in range(len(arrays)) for row in range(len(first_masks) + 1)]
+            zero[-1] = gate(zero[-1], own_parts[1][2])
+    one = [near_one] + [swap(near_one, place, count) for place in places[1:]]
+    each = len(first_masks) + 1
+    zero_at = [(at, row * 96) for at in range(len(zero)) for row in range(each)]
+    one_at = [(at, row * 80) for at in range(len(one)) for row in range(each)]
 
     half = steps // 2
 
@@ -516,11 +522,11 @@
     right_spec = pl.BlockSpec(right.shape, whole)
     send_shape = (rhs_count, width + TAIL)
     front_zero, back_zero, half_sum, slots = pl.pallas_call(
-        functools.partial(pair_zero_kernel, block_at),
+        functools.partial(pair_zero_kernel, zero_at),
         grid_spec=pltpu.PrefetchScalarGridSpec(
             num_scalar_prefetch=1,
             grid=(most, half),
-            in_specs=[right_spec] + [row_spec] * PARTS + [any_spec] * len(arrays),
+            in_specs=[right_spec] + [row_spec] * PARTS + [any_spec] * len(zero),
             out_specs=half_specs + [row_spec, smem],
             scratch_shapes=half_scratch
             + [
@@ -531,23 +537,23 @@
             ],
         ),
         out_shape=half_shapes
-        + [shape(right_side.shape, F32), shape((2 * (most + 2),), jnp.int32)],
+        + [shape(right_side.shape, F32), shape((most + 2,), jnp.int32)],
         compiler_params=params,
         name="pair_zero",
-    )(me, right, *[part[2] for part in own_parts], *arrays)
+    )(me, right, *[part[2] for part in own_parts], *zero)
     front_one, back_one, image, send = pl.pallas_call(
-        pair_one_kernel,
+        functools.partial(pair_one_kernel, one_at),
         grid_spec=pltpu.PrefetchScalarGridSpec(
             num_scalar_prefetch=1,
             grid=(most, half),
-            in_specs=[right_spec, row_spec, any_spec, row_spec, var_spec],
+            in_specs=[right_spec, row_spec, row_spec, var_spec] + [any_spec] * len(one),
             out_specs=half_specs + [row_spec, pl.BlockSpec(send_shape, whole)],
             scratch_shapes=half_scratch,
         ),
         out_shape=half_shapes + [shape(right_side.shape, F32), shape(send_shape, BF16)],
         compiler_params=params,
         name="pair_one",
-    )(slots, right, half_sum, every_one, right_side, var_row)
+    )(slots, right, half_sum, right_side, var_row, *one)
     fronts = [pltpu.with_memory_space_constraint(part, pltpu.VMEM) for part in (front_zero, front_one)]
     backs = [pltpu.with_memory_space_constraint(part, pltpu.HBM) for part in (back_zero, back_one)]
 

time: 156 us -> 140 us (0.90)
  between operations: 14.3 us -> 0.94 us
  starting transfers between devices: 19.8 us -> 28.9 us
  local copies, waits for them, and re-layouts: 13.8 us -> 6.71 us
  waiting for transfers between devices: 12.9 us -> 8.26 us
    ppermute x17 -> x23, starting transfers between devices: 19.8 us -> 28.9 us  [swap(): return lax.ppermute(value, 'row', [(i, i ^ mask) for i in range(count)])]
    unnamed x45 -> x33, local copies, waits for them, and re-layouts: 13.7 us -> 6.66 us
    ppermute x17 -> x23, waiting for transfers between devices: 12.9 us -> 8.26 us  [swap(): return lax.ppermute(value, 'row', [(i, i ^ mask) for i in range(count)])]
  transfers between devices with their start and end apart: 18 -> 23, of which waited for: 7 -> 6; matrix products, arithmetic and copies ran while one was open for 1% -> 1% of each run, Pallas kernels for 32% -> 35%
where the time goes in v11:
time: 140 us
  Pallas kernels  92.8 us (66%)
  starting transfers between devices  28.9 us (21%)
  waiting for transfers between devices  8.26 us (6%)
  local copies, waits for them, and re-layouts  6.71 us (5%)
  other arithmetic  2.58 us (2%)
    pallas_call x1, Pallas kernels, local(): pl.pallas_call(functools.partial(pair_zero_kernel, zero_at), grid_spec=pl...  33.7 us
    pallas_call x1, Pallas kernels, local(): pl.pallas_call(functools.partial(pair_one_kernel, one_at), grid_spec=pltp...  32.5 us
    ppermute x23, starting transfers between devices, swap(): return lax.ppermute(value, 'row', [(i, i ^ mask) for i in range(count)])  28.9 us
    pallas_call x1, Pallas kernels, local(): pl.pallas_call(again_kernel, grid_spec=pltpu.PrefetchScalarGridSpec(num_s...  10.1 us
    pallas_call x2, Pallas kernels, own_part(): pl.pallas_call(functools.partial(own_kernel, rows), in_specs=[vmem, vmem,...  9.61 us
    ppermute x23, waiting for transfers between devices, swap(): return lax.ppermute(value, 'row', [(i, i ^ mask) for i in range(count)])  8.26 us
    unnamed x33, local copies, waits for them, and re-layouts  6.66 us
    pallas_call x2, Pallas kernels, local(): pl.pallas_call(functools.partial(own_again_kernel, blocks), in_specs=[any...  4.33 us
  transfers between devices with their start and end apart: 23, of which 6 were waited for; matrix products, arithmetic and copies ran while one was open for 1% of the time, Pallas kernels for 35%

profile of v11, /device:TPU:0, one launch (start us, length us, event | category | flops | bytes accessed | tf_op | source)
XLA Modules:
  0.0 140.2 jit_solution(5331957526178319550)
XLA Ops:
  1.4 1.2 payload.1
  2.6 5.1 %collective-permute-start.2 = (bf16[96,512]{1,0:T(8,128)(2,1)S(1)}, bf16[96,512]{1,0:T(8,128)(2,1)S(1)}, u32[]{:S(2)}, u32[]{:S(2)}) collective-permute-start(bf16[96,512]{1,0:T(8,128)(2,1)S(1)} %get-tuple-element.26), channel_id=1, source_target_pairs={{0,12},{1,13},{2,14},{3,15},{4,8},{5,9},{6,10},{7,11},{8,4},{9,5},... | collective-permute-start | bytes 294920 | tf_op jit(solution)/shard_map/ppermute | solution.py:376
  8.3 4.0 %own_tile_0.1 = (bf16[4,512,512]{2,1,0:T(8,128)(2,1)}, f32[8,2048]{1,0:T(8,128)S(1)}) custom-call(bf16[2048,128]{1,0:T(8,128)(2,1)S(1)} %get-tuple-element.23.left_ref, bf16[128,2048]{1,0:T(8,128)(2,1)S(1)} %get-tuple-element.22.right_ref.arrived_ref, bf16[8,2048]{1,0:T(8,128)(2,1)S(1)} %get-tuple-element.24.vec_ref, ...), custom_call_target="tpu_custom_call" | custom-call | flops 5000000000 | bytes 2097152 | tf_op jit(solution)/shard_map/own_tile_0/pallas_call | solution.py:465
  13.0 3.7 %collective-permute-start.8 = (bf16[80,512]{1,0:T(8,128)(2,1)}, bf16[80,512]{1,0:T(8,128)(2,1)S(1)}, u32[]{:S(2)}, u32[]{:S(2)}) collective-permute-start(bf16[80,512]{1,0:T(8,128)(2,1)} %gate.6), channel_id=1, source_target_pairs={{0,12},{1,13},{2,14},{3,15},{4,8},{5,9},{6,10},{7,11},{8,4},{9,5},... | collective-permute-start | bytes 245768 | tf_op jit(solution)/shard_map/ppermute | solution.py:376
  18.2 1.7 %collective-permute-start.3 = (bf16[384,512]{1,0:T(8,128)(2,1)}, bf16[384,512]{1,0:T(8,128)(2,1)S(1)}, u32[]{:S(2)}, u32[]{:S(2)}) collective-permute-start(bf16[384,512]{1,0:T(8,128)(2,1)} %gate.4.arrived_ref.refs_2_), channel_id=1, source_target_pairs={{0,2},{1,3},{2,0},{3,1},{4,6},{5,7},{6,4},{7,5},{8,10},{9,11},{10,... | collective-permute-start | bytes 1179656 | tf_op jit(solution)/shard_map/ppermute | solution.py:376
  20.0 1.0 copy-done
  21.0 5.6 %own_tile_1.1 = (bf16[6,512,512]{2,1,0:T(8,128)(2,1)}, f32[8,2048]{1,0:T(8,128)S(1)}) custom-call(bf16[2048,128]{1,0:T(8,128)(2,1)S(1)} %get-tuple-element.23.left_ref, bf16[128,2048]{1,0:T(8,128)(2,1)S(1)} %get-tuple-element.22.right_ref.arrived_ref, bf16[8,2048]{1,0:T(8,128)(2,1)S(1)} %get-tuple-element.24.vec_ref, bf16[384,512]{1,0:T(8,128)(2,1)S(1)} %copy-done), custom_call_target="tpu_custom_call" | custom-call | flops 5000000000 | bytes 3145728 | tf_op jit(solution)/shard_map/own_tile_1/pallas_call | solution.py:465
  27.3 2.7 %collective-permute-done.3.refs_0_ = bf16[384,512]{1,0:T(8,128)(2,1)S(1)} collective-permute-done((bf16[384,512]{1,0:T(8,128)(2,1)}, bf16[384,512]{1,0:T(8,128)(2,1)S(1)}, u32[]{:S(2)}, u32[]{:S(2)}) %collective-permute-start.3) | collective-permute-done | bytes 393248 | tf_op jit(solution)/shard_map/ppermute | solution.py:376
  31.6 1.8 %collective-permute-start.11 = (bf16[320,512]{1,0:T(8,128)(2,1)}, bf16[320,512]{1,0:T(8,128)(2,1)S(1)}, u32[]{:S(2)}, u32[]{:S(2)}) collective-permute-start(bf16[320,512]{1,0:T(8,128)(2,1)} %gate.7.refs_0_), channel_id=1, source_target_pairs={{0,3},{1,2},{2,1},{3,0},{4,7},{5,6},{6,5},{7,4},{8,11},{9,10},{10,... | collective-permute-start | bytes 983048 | tf_op jit(solution)/shard_map/ppermute | solution.py:376
  35.6 33.7 %pair_zero.1 = (bf16[3,1024,2048]{2,1,0:T(8,128)(2,1)S(1)}, bf16[2,1024,2048]{2,1,0:T(8,128)(2,1)}, f32[8,2048]{1,0:T(8,128)S(1)}, s32[7]{0:T(128)S(1)}) custom-call(s32[1]{0:T(128)} %bitcast.me_ref, bf16[128,2048]{1,0:T(8,128)(2,1)S(1)} %get-tuple-element.22.right_ref.arrived_ref, f32[8,2048]{1,0:T(8,128)S(1)} %copy-done.7, f32[8,2048]{1,0:T(8,128)S(1)} %copy-done.9, ...), custom_call_target="tpu_custom_call" | custom-call | tf_op jit(solution)/shard_map/pair_zero/pallas_call | solution.py:524
  70.3 32.5 %pair_one.1 = (bf16[3,1024,2048]{2,1,0:T(8,128)(2,1)S(1)}, bf16[2,1024,2048]{2,1,0:T(8,128)(2,1)}, f32[8,2048]{1,0:T(8,128)S(1)}, bf16[8,2176]{1,0:T(8,128)(2,1)S(1)}) custom-call(s32[7]{0:T(128)S(1)} %get-tuple-element.28.slots_ref, bf16[128,2048]{1,0:T(8,128)(2,1)S(1)} %get-tuple-element.22.right_ref.arrived_ref, ...), custom_call_target="tpu_custom_call" | custom-call | tf_op jit(solution)/shard_map/pair_one/pallas_call | solution.py:544
  102.8 2.8 %collective-permute-start.13 = (bf16[1,8,2176]{2,1,0:T(8,128)(2,1)S(1)}, bf16[1,8,2176]{2,1,0:T(8,128)(2,1)S(1)}, u32[]{:S(2)}, u32[]{:S(2)}) collective-permute-start(bf16[1,8,2176]{2,1,0:T(8,128)(2,1)S(1)} %bitcast.6), channel_id=1, source_target_pairs={{0,8},{1,9},{2,10},{3,11},{4,12},{5,13},{6,14},{7,15},{8,0},{9,1},... | collective-permute-start | bytes 104456 | tf_op jit(solution)/shard_map/ppermute | solution.py:376
  105.6 1.6 %collective-permute-start.12 = (bf16[1,8,2176]{2,1,0:T(8,128)(2,1)S(1)}, bf16[1,8,2176]{2,1,0:T(8,128)(2,1)S(1)}, u32[]{:S(2)}, u32[]{:S(2)}) collective-permute-start(bf16[1,8,2176]{2,1,0:T(8,128)(2,1)S(1)} %bitcast.7), channel_id=1, source_target_pairs={{0,4},{1,5},{2,6},{3,7},{4,0},{5,1},{6,2},{7,3},{8,12},{9,13},{10,... | collective-permute-start | bytes 104456 | tf_op jit(solution)/shard_map/ppermute | solution.py:376
  107.2 2.4 %own_again_1.1.refs_1_ = f32[8,2048]{1,0:T(8,128)S(1)} custom-call(bf16[6,512,512]{2,1,0:T(8,128)(2,1)} %get-tuple-element.38.in_ref, bf16[8,2176]{1,0:T(8,128)(2,1)S(1)} %get-tuple-element.35.vec_ref), custom_call_target="tpu_custom_call" | custom-call | flops 5000000000 | bytes 3145728 | tf_op jit(solution)/shard_map/own_again_1/pallas_call | solution.py:568
  109.8 3.1 %collective-permute-start.15 = (bf16[4,8,2176]{2,1,0:T(8,128)(2,1)S(1)}, bf16[4,8,2176]{2,1,0:T(8,128)(2,1)S(1)}, u32[]{:S(2)}, u32[]{:S(2)}) collective-permute-start(bf16[4,8,2176]{2,1,0:T(8,128)(2,1)S(1)} %pad_maximum_fusion.2), channel_id=1, source_target_pairs={{0,2},{1,3},{2,0},{3,1},{4,6},{5,7},{6,4},{7,5},{8,10},{9,11},{10,... | collective-permute-start | bytes 417800 | tf_op jit(solution)/shard_map/ppermute | solution.py:376
  113.0 3.0 %collective-permute-done.15 = bf16[4,8,2176]{2,1,0:T(8,128)(2,1)S(1)} collective-permute-done((bf16[4,8,2176]{2,1,0:T(8,128)(2,1)S(1)}, bf16[4,8,2176]{2,1,0:T(8,128)(2,1)S(1)}, u32[]{:S(2)}, u32[]{:S(2)}) %collective-permute-start.15) | collective-permute-done | bytes 139296 | tf_op jit(solution)/shard_map/ppermute | solution.py:376
  116.1 2.0 %own_again_0.1.refs_0_ = f32[8,2048]{1,0:T(8,128)S(1)} custom-call(bf16[4,512,512]{2,1,0:T(8,128)(2,1)} %get-tuple-element.37.in_ref, bf16[8,2176]{1,0:T(8,128)(2,1)S(1)} %get-tuple-element.35.vec_ref), custom_call_target="tpu_custom_call" | custom-call | flops 5000000000 | bytes 2097152 | tf_op jit(solution)/shard_map/own_again_0/pallas_call | solution.py:568
  118.2 10.1 %pair_again.1 = (f32[32,2048]{1,0:T(8,128)S(1)}, f32[8,128]{1,0:T(8,128)S(1)}, f32[8,128]{1,0:T(8,128)S(1)}) custom-call(s32[7]{0:T(128)S(1)} %get-tuple-element.28.slots_ref, bf16[3,1024,2048]{2,1,0:T(8,128)(2,1)S(1)} %get-tuple-element.29.front_zero_ref, bf16[3,1024,2048]{2,1,0:T(8,128)(2,1)S(1)} %get-tuple-element.32.front_one_ref, ...), custom_call_target="tpu_custom_call" | custom-call | tf_op jit(solution)/shard_map/pair_again/pallas_call | solution.py:586
  128.4 2.1 %collective-permute-start.18 = (f32[8,128]{1,0:T(8,128)S(1)}, f32[8,128]{1,0:T(8,128)S(1)}, u32[]{:S(2)}, u32[]{:S(2)}) collective-permute-start(f32[8,128]{1,0:T(8,128)S(1)} %get-tuple-element.41), channel_id=1, source_target_pairs={{0,8},{1,9},{2,10},{3,11},{4,12},{5,13},{6,14},{7,15},{8,0},{9,1},... | collective-permute-start | bytes 12296 | tf_op jit(solution)/shard_map/ppermute | solution.py:376
  130.4 2.3 %collective-permute-start.17 = (f32[8,128]{1,0:T(8,128)S(1)}, f32[8,128]{1,0:T(8,128)S(1)}, u32[]{:S(2)}, u32[]{:S(2)}) collective-permute-start(f32[8,128]{1,0:T(8,128)S(1)} %get-tuple-element.41), channel_id=1, source_target_pairs={{0,4},{1,5},{2,6},{3,7},{4,0},{5,1},{6,2},{7,3},{8,12},{9,13},{10,... | collective-permute-start | bytes 12296 | tf_op jit(solution)/shard_map/ppermute | solution.py:376
  132.7 1.0 collective-permute-done.19
  134.3 1.2 collective-permute-start.22
  135.6 1.4 %collective-permute-start.21 = (f32[8,128]{1,0:T(8,128)S(1)}, f32[8,128]{1,0:T(8,128)S(1)}, u32[]{:S(2)}, u32[]{:S(2)}) collective-permute-start(f32[8,128]{1,0:T(8,128)S(1)} %add_add_fusion.1), channel_id=1, source_target_pairs={{0,2},{1,3},{2,0},{3,1},{4,6},{5,7},{6,4},{7,5},{8,10},{9,11},{10,... | collective-permute-start | bytes 12296 | tf_op jit(solution)/shard_map/ppermute | solution.py:376
  137.0 1.5 %curve_order.1 = f32[32,2048]{1,0:T(8,128)S(1)} custom-call(f32[32,2048]{1,0:T(8,128)S(1)} %get-tuple-element.40.rows_ref, s32[1,2048]{1,0:T(1,128)S(1)} %copy-done.13), custom_call_target="tpu_custom_call" | custom-call | tf_op jit(solution)/shard_map/curve_order/pallas_call | solution.py:624
  (77 shorter events, 11.8 us)
Async XLA Ops:
  2.6 14.2 %collective-permute-start.2 = (bf16[96,512]{1,0:T(8,128)(2,1)S(1)}, bf16[96,512]{1,0:T(8,128)(2,1)S(1)}, u32[]{:S(2)}, u32[]{:S(2)}) collective-permute-start(bf16[96,512]{1,0:T(8,128)(2,1)S(1)} %get-tuple-element.26), channel_id=1, source_target_pairs={{0,12},{1,13},{2,14},{3,15},{4,8},{5,9},{6,10},{7,11},{8,4},{9,5},... | collective-permute-start | bytes 294920 | tf_op jit(solution)/shard_map/ppermute | solution.py:376
  7.7 9.7 %collective-permute-start.1 = (bf16[96,512]{1,0:T(8,128)(2,1)S(1)}, bf16[96,512]{1,0:T(8,128)(2,1)S(1)}, u32[]{:S(2)}, u32[]{:S(2)}) collective-permute-start(bf16[96,512]{1,0:T(8,128)(2,1)S(1)} %get-tuple-element.26), channel_id=1, source_target_pairs={{0,8},{1,9},{2,10},{3,11},{4,12},{5,13},{6,14},{7,15},{8,0},{9,1},... | collective-permute-start | bytes 294920 | tf_op jit(solution)/shard_map/ppermute | solution.py:376
  7.7 9.7 %collective-permute-start = (bf16[96,512]{1,0:T(8,128)(2,1)S(1)}, bf16[96,512]{1,0:T(8,128)(2,1)S(1)}, u32[]{:S(2)}, u32[]{:S(2)}) collective-permute-start(bf16[96,512]{1,0:T(8,128)(2,1)S(1)} %get-tuple-element.26), channel_id=1, source_target_pairs={{0,4},{1,5},{2,6},{3,7},{4,0},{5,1},{6,2},{7,3},{8,12},{9,13},{10,... | collective-permute-start | bytes 294920 | tf_op jit(solution)/shard_map/ppermute | solution.py:376
  13.0 17.8 %collective-permute-start.8 = (bf16[80,512]{1,0:T(8,128)(2,1)}, bf16[80,512]{1,0:T(8,128)(2,1)S(1)}, u32[]{:S(2)}, u32[]{:S(2)}) collective-permute-start(bf16[80,512]{1,0:T(8,128)(2,1)} %gate.6), channel_id=1, source_target_pairs={{0,12},{1,13},{2,14},{3,15},{4,8},{5,9},{6,10},{7,11},{8,4},{9,5},... | collective-permute-start | bytes 245768 | tf_op jit(solution)/shard_map/ppermute | solution.py:376
  16.7 14.0 %collective-permute-start.7 = (bf16[80,512]{1,0:T(8,128)(2,1)}, bf16[80,512]{1,0:T(8,128)(2,1)S(1)}, u32[]{:S(2)}, u32[]{:S(2)}) collective-permute-start(bf16[80,512]{1,0:T(8,128)(2,1)} %gate.6), channel_id=1, source_target_pairs={{0,8},{1,9},{2,10},{3,11},{4,12},{5,13},{6,14},{7,15},{8,0},{9,1},... | collective-permute-start | bytes 245768 | tf_op jit(solution)/shard_map/ppermute | solution.py:376
  16.7 14.0 %collective-permute-start.6 = (bf16[80,512]{1,0:T(8,128)(2,1)}, bf16[80,512]{1,0:T(8,128)(2,1)S(1)}, u32[]{:S(2)}, u32[]{:S(2)}) collective-permute-start(bf16[80,512]{1,0:T(8,128)(2,1)} %gate.6), channel_id=1, source_target_pairs={{0,4},{1,5},{2,6},{3,7},{4,0},{5,1},{6,2},{7,3},{8,12},{9,13},{10,... | collective-permute-start | bytes 245768 | tf_op jit(solution)/shard_map/ppermute | solution.py:376
  18.1 51.1 %copy-start.12 = (f32[2048]{0:T(1024)S(1)}, f32[2048]{0:T(1024)}, u32[]{:S(2)}) copy-start(f32[2048]{0:T(1024)} %param.7) | copy-start | bytes 24580
  18.2 15.6 %collective-permute-start.4 = (bf16[384,512]{1,0:T(8,128)(2,1)}, bf16[384,512]{1,0:T(8,128)(2,1)S(1)}, u32[]{:S(2)}, u32[]{:S(2)}) collective-permute-start(bf16[384,512]{1,0:T(8,128)(2,1)} %gate.4.arrived_ref.refs_2_), channel_id=1, source_target_pairs={{0,1},{1,0},{2,3},{3,2},{4,5},{5,4},{6,7},{7,6},{8,9},{9,8},{10,11... | collective-permute-start | bytes 1179656 | tf_op jit(solution)/shard_map/ppermute | solution.py:376
  18.2 11.7 %collective-permute-start.3 = (bf16[384,512]{1,0:T(8,128)(2,1)}, bf16[384,512]{1,0:T(8,128)(2,1)S(1)}, u32[]{:S(2)}, u32[]{:S(2)}) collective-permute-start(bf16[384,512]{1,0:T(8,128)(2,1)} %gate.4.arrived_ref.refs_2_), channel_id=1, source_target_pairs={{0,2},{1,3},{2,0},{3,1},{4,6},{5,7},{6,4},{7,5},{8,10},{9,11},{10,... | collective-permute-start | bytes 1179656 | tf_op jit(solution)/shard_map/ppermute | solution.py:376
  30.7 3.0 %collective-permute-start.5 = (bf16[384,512]{1,0:T(8,128)(2,1)}, bf16[384,512]{1,0:T(8,128)(2,1)S(1)}, u32[]{:S(2)}, u32[]{:S(2)}) collective-permute-start(bf16[384,512]{1,0:T(8,128)(2,1)} %gate.5.refs_3_), channel_id=1, source_target_pairs={{0,1},{1,0},{2,3},{3,2},{4,5},{5,4},{6,7},{7,6},{8,9},{9,8},{10,11... | collective-permute-start | bytes 1179656 | tf_op jit(solution)/shard_map/ppermute | solution.py:376
  31.6 37.7 %collective-permute-start.11 = (bf16[320,512]{1,0:T(8,128)(2,1)}, bf16[320,512]{1,0:T(8,128)(2,1)S(1)}, u32[]{:S(2)}, u32[]{:S(2)}) collective-permute-start(bf16[320,512]{1,0:T(8,128)(2,1)} %gate.7.refs_0_), channel_id=1, source_target_pairs={{0,3},{1,2},{2,1},{3,0},{4,7},{5,6},{6,5},{7,4},{8,11},{9,10},{10,... | collective-permute-start | bytes 983048 | tf_op jit(solution)/shard_map/ppermute | solution.py:376
  33.3 35.9 %collective-permute-start.10 = (bf16[320,512]{1,0:T(8,128)(2,1)}, bf16[320,512]{1,0:T(8,128)(2,1)S(1)}, u32[]{:S(2)}, u32[]{:S(2)}) collective-permute-start(bf16[320,512]{1,0:T(8,128)(2,1)} %gate.7.refs_0_), channel_id=1, source_target_pairs={{0,1},{1,0},{2,3},{3,2},{4,5},{5,4},{6,7},{7,6},{8,9},{9,8},{10,11... | collective-permute-start | bytes 983048 | tf_op jit(solution)/shard_map/ppermute | solution.py:376
  33.3 35.9 %collective-permute-start.9 = (bf16[320,512]{1,0:T(8,128)(2,1)}, bf16[320,512]{1,0:T(8,128)(2,1)S(1)}, u32[]{:S(2)}, u32[]{:S(2)}) collective-permute-start(bf16[320,512]{1,0:T(8,128)(2,1)} %gate.7.refs_0_), channel_id=1, source_target_pairs={{0,2},{1,3},{2,0},{3,1},{4,6},{5,7},{6,4},{7,5},{8,10},{9,11},{10,... | collective-permute-start | bytes 983048 | tf_op jit(solution)/shard_map/ppermute | solution.py:376
  102.7 6.8 %collective-permute-start.14 = (bf16[1,8,2176]{2,1,0:T(8,128)(2,1)S(1)}, bf16[1,8,2176]{2,1,0:T(8,128)(2,1)S(1)}, u32[]{:S(2)}, u32[]{:S(2)}) collective-permute-start(bf16[1,8,2176]{2,1,0:T(8,128)(2,1)S(1)} %bitcast.5), channel_id=1, source_target_pairs={{0,12},{1,13},{2,14},{3,15},{4,8},{5,9},{6,10},{7,11},{8,4},{9,5},... | collective-permute-start | bytes 104456 | tf_op jit(solution)/shard_map/ppermute | solution.py:376
  102.8 6.8 %collective-permute-start.13 = (bf16[1,8,2176]{2,1,0:T(8,128)(2,1)S(1)}, bf16[1,8,2176]{2,1,0:T(8,128)(2,1)S(1)}, u32[]{:S(2)}, u32[]{:S(2)}) collective-permute-start(bf16[1,8,2176]{2,1,0:T(8,128)(2,1)S(1)} %bitcast.6), channel_id=1, source_target_pairs={{0,8},{1,9},{2,10},{3,11},{4,12},{5,13},{6,14},{7,15},{8,0},{9,1},... | collective-permute-start | bytes 104456 | tf_op jit(solution)/shard_map/ppermute | solution.py:376
  105.6 4.2 %collective-permute-start.12 = (bf16[1,8,2176]{2,1,0:T(8,128)(2,1)S(1)}, bf16[1,8,2176]{2,1,0:T(8,128)(2,1)S(1)}, u32[]{:S(2)}, u32[]{:S(2)}) collective-permute-start(bf16[1,8,2176]{2,1,0:T(8,128)(2,1)S(1)} %bitcast.7), channel_id=1, source_target_pairs={{0,4},{1,5},{2,6},{3,7},{4,0},{5,1},{6,2},{7,3},{8,12},{9,13},{10,... | collective-permute-start | bytes 104456 | tf_op jit(solution)/shard_map/ppermute | solution.py:376
  109.8 6.2 %collective-permute-start.15 = (bf16[4,8,2176]{2,1,0:T(8,128)(2,1)S(1)}, bf16[4,8,2176]{2,1,0:T(8,128)(2,1)S(1)}, u32[]{:S(2)}, u32[]{:S(2)}) collective-permute-start(bf16[4,8,2176]{2,1,0:T(8,128)(2,1)S(1)} %pad_maximum_fusion.2), channel_id=1, source_target_pairs={{0,2},{1,3},{2,0},{3,1},{4,6},{5,7},{6,4},{7,5},{8,10},{9,11},{10,... | collective-permute-start | bytes 417800 | tf_op jit(solution)/shard_map/ppermute | solution.py:376
  116.0 2.1 %collective-permute-start.16 = (bf16[8,8,2176]{2,1,0:T(8,128)(2,1)S(1)}, bf16[8,8,2176]{2,1,0:T(8,128)(2,1)S(1)}, u32[]{:S(2)}, u32[]{:S(2)}) collective-permute-start(bf16[8,8,2176]{2,1,0:T(8,128)(2,1)S(1)} %get-tuple-element.47), channel_id=1, source_target_pairs={{0,1},{1,0},{2,3},{3,2},{4,5},{5,4},{6,7},{7,6},{8,9},{9,8},{10,11... | collective-permute-start | bytes 835592 | tf_op jit(solution)/shard_map/ppermute | solution.py:376
  128.3 5.5 %collective-permute-start.19 = (f32[8,128]{1,0:T(8,128)S(1)}, f32[8,128]{1,0:T(8,128)S(1)}, u32[]{:S(2)}, u32[]{:S(2)}) collective-permute-start(f32[8,128]{1,0:T(8,128)S(1)} %get-tuple-element.41), channel_id=1, source_target_pairs={{0,12},{1,13},{2,14},{3,15},{4,8},{5,9},{6,10},{7,11},{8,4},{9,5},... | collective-permute-start | bytes 12296 | tf_op jit(solution)/shard_map/ppermute | solution.py:376
  128.4 5.4 %collective-permute-start.18 = (f32[8,128]{1,0:T(8,128)S(1)}, f32[8,128]{1,0:T(8,128)S(1)}, u32[]{:S(2)}, u32[]{:S(2)}) collective-permute-start(f32[8,128]{1,0:T(8,128)S(1)} %get-tuple-element.41), channel_id=1, source_target_pairs={{0,8},{1,9},{2,10},{3,11},{4,12},{5,13},{6,14},{7,15},{8,0},{9,1},... | collective-permute-start | bytes 12296 | tf_op jit(solution)/shard_map/ppermute | solution.py:376
  130.4 3.9 %collective-permute-start.17 = (f32[8,128]{1,0:T(8,128)S(1)}, f32[8,128]{1,0:T(8,128)S(1)}, u32[]{:S(2)}, u32[]{:S(2)}) collective-permute-start(f32[8,128]{1,0:T(8,128)S(1)} %get-tuple-element.41), channel_id=1, source_target_pairs={{0,4},{1,5},{2,6},{3,7},{4,0},{5,1},{6,2},{7,3},{8,12},{9,13},{10,... | collective-permute-start | bytes 12296 | tf_op jit(solution)/shard_map/ppermute | solution.py:376
  134.3 4.2 %collective-permute-start.22 = (f32[8,128]{1,0:T(8,128)S(1)}, f32[8,128]{1,0:T(8,128)S(1)}, u32[]{:S(2)}, u32[]{:S(2)}) collective-permute-start(f32[8,128]{1,0:T(8,128)S(1)} %add_add_fusion.1), channel_id=1, source_target_pairs={{0,3},{1,2},{2,1},{3,0},{4,7},{5,6},{6,5},{7,4},{8,11},{9,10},{10,... | collective-permute-start | bytes 12296 | tf_op jit(solution)/shard_map/ppermute | solution.py:376
  135.6 3.6 %collective-permute-start.21 = (f32[8,128]{1,0:T(8,128)S(1)}, f32[8,128]{1,0:T(8,128)S(1)}, u32[]{:S(2)}, u32[]{:S(2)}) collective-permute-start(f32[8,128]{1,0:T(8,128)S(1)} %add_add_fusion.1), channel_id=1, source_target_pairs={{0,2},{1,3},{2,0},{3,1},{4,6},{5,7},{6,4},{7,5},{8,10},{9,11},{10,... | collective-permute-start | bytes 12296 | tf_op jit(solution)/shard_map/ppermute | solution.py:376
  137.0 2.2 %collective-permute-start.20 = (f32[8,128]{1,0:T(8,128)S(1)}, f32[8,128]{1,0:T(8,128)S(1)}, u32[]{:S(2)}, u32[]{:S(2)}) collective-permute-start(f32[8,128]{1,0:T(8,128)S(1)} %add_add_fusion.1), channel_id=1, source_target_pairs={{0,1},{1,0},{2,3},{3,2},{4,5},{5,4},{6,7},{7,6},{8,9},{9,8},{10,11... | collective-permute-start | bytes 12296 | tf_op jit(solution)/shard_map/ppermute | solution.py:376
  (13 other events, 126.6 us)

commit v12 on v11

--- a/solution.py
+++ b/solution.py
@@ -182,7 +182,7 @@
     return fetch
 
 
-def half_tiles(slots_ref, right_ref, fetch, front_ref, back_ref, sum_ref, left_ref, vec_ref, pay_ref, sem_ref):
+def half_tiles(at_once, slots_ref, right_ref, fetch, front_ref, back_ref, sum_ref, left_ref, vec_ref, pay_ref, sem_ref):
     slot, step = pl.program_id(0), pl.program_id(1)
 
     @pl.when((slot == 0) & (step == 0) & (slots_ref[0] > 0))
@@ -211,13 +211,13 @@
             @pl.when(here)
             def _():
                 def unit(index, carry):
-                    cols = pl.ds(pl.multiple_of(index * COLS, COLS), COLS)
+                    cols = pl.ds(pl.multiple_of(index * at_once, at_once), at_once)
                     sum_ref[:, cols] += tile_unit(
                         left, right_ref[:, cols], vec, tile_ref.at[0, :, cols]
                     )
                     return carry
 
-                lax.fori_loop(0, right_ref.shape[1] // COLS, unit, 0)
+                lax.fori_loop(0, right_ref.shape[1] // at_once, unit, 0)
 
 
 def pair_zero_kernel(block_at, me_ref, right_ref, *refs):
@@ -248,7 +248,7 @@
 
     fetch = fetch_from(block_at, block_refs, slots_ref, pay_ref, sem_ref)
     half_tiles(
-        slots_ref, right_ref, fetch, front_ref, back_ref, sum_ref, left_ref, vec_ref, pay_ref, sem_ref
+        2 * COLS, slots_ref, right_ref, fetch, front_ref, back_ref, sum_ref, left_ref, vec_ref, pay_ref, sem_ref
     )
 
 
@@ -263,7 +263,7 @@
 
     fetch = fetch_from(block_at, block_refs, slots_ref, pay_ref, sem_ref)
     half_tiles(
-        slots_ref, right_ref, fetch, front_ref, back_ref, image_ref, left_ref, vec_ref, pay_ref, sem_ref
+        4 * COLS, slots_ref, right_ref, fetch, front_ref, back_ref, image_ref, left_ref, vec_ref, pay_ref, sem_ref
     )
 
     @pl.when((slot == pl.num_programs(0) - 1) & (step == pl.num_programs(1) - 1))
@@ -423,6 +423,7 @@
         out_specs=pl.BlockSpec(memory_space=pl.ANY),
         out_shape=jax.ShapeDtypeStruct(block.shape, block.dtype),
         input_output_aliases={0: 0},
+        compiler_params=pltpu.CompilerParams(vmem_limit_bytes=1024 * 1024),
         name="gate",
     )(block, behind)
 

time: 140 us -> 126 us (0.900)
  Pallas kernels: 92.8 us -> 83.2 us
  waiting for transfers between devices: 8.26 us -> 14.4 us
  local copies, waits for them, and re-layouts: 6.71 us -> 0.89 us
  starting transfers between devices: 28.9 us -> 24.9 us
  other arithmetic: 2.58 us -> 1.07 us
    ppermute x23, waiting for transfers between devices: 8.26 us -> 14.4 us  [swap(): return lax.ppermute(value, 'row', [(i, i ^ mask) for i in range(count)])]
    unnamed x33 -> x11, local copies, waits for them, and re-layouts: 6.66 us -> 0.83 us
    pallas_call x1, Pallas kernels: 33.7 us -> 28.7 us  [local(): pl.pallas_call(functools.partial(pair_zero_kernel, zero_at), grid_spec=pl...]
    pallas_call x1, Pallas kernels: 32.5 us -> 27.6 us  [local(): pl.pallas_call(functools.partial(pair_one_kernel, one_at), grid_spec=pltp...]
    ppermute x23, starting transfers between devices: 28.9 us -> 24.9 us  [swap(): return lax.ppermute(value, 'row', [(i, i ^ mask) for i in range(count)])]
    concatenate x2, other arithmetic: 1.56 us -> 0.05 us  [local(): jnp.concatenate([pay] + [swap(pay, mask, count) for mask in first_masks],...]
  transfers between devices with their start and end apart: 23 -> 23, of which waited for: 6 -> 6; matrix products, arithmetic and copies ran while one was open for 1% -> 0% of each run, Pallas kernels for 35% -> 35%
where the time goes in v12:
time: 126 us; the launch traced here: 125 us
  Pallas kernels  83.2 us (66%)
  starting transfers between devices  24.9 us (20%)
  waiting for transfers between devices  14.4 us (11%)
    pallas_call x1, Pallas kernels, local(): pl.pallas_call(functools.partial(pair_zero_kernel, zero_at), grid_spec=pl...  28.7 us
    pallas_call x1, Pallas kernels, local(): pl.pallas_call(functools.partial(pair_one_kernel, one_at), grid_spec=pltp...  27.6 us
    ppermute x23, starting transfers between devices, swap(): return lax.ppermute(value, 'row', [(i, i ^ mask) for i in range(count)])  24.9 us
    ppermute x23, waiting for transfers between devices, swap(): return lax.ppermute(value, 'row', [(i, i ^ mask) for i in range(count)])  14.4 us
    pallas_call x1, Pallas kernels, local(): pl.pallas_call(again_kernel, grid_spec=pltpu.PrefetchScalarGridSpec(num_s...  10.3 us
    pallas_call x2, Pallas kernels, own_part(): pl.pallas_call(functools.partial(own_kernel, rows), in_specs=[vmem, vmem,...  9.62 us
    pallas_call x2, Pallas kernels, local(): pl.pallas_call(functools.partial(own_again_kernel, blocks), in_specs=[any...  4.34 us
  transfers between devices with their start and end apart: 23, of which 6 were waited for; matrix products, arithmetic and copies ran while one was open for 0% of the time, Pallas kernels for 35%

profile of v12, /device:TPU:0, one launch (start us, length us, event | category | flops | bytes accessed | tf_op | source)
XLA Modules:
  0.0 125.4 jit_solution(13752911030684206608)
XLA Ops:
  0.6 0.8 copy.12.list_ref
  1.4 1.2 payload.1
  2.6 5.1 %collective-permute-start.2 = (bf16[96,512]{1,0:T(8,128)(2,1)S(1)}, bf16[96,512]{1,0:T(8,128)(2,1)S(1)}, u32[]{:S(2)}, u32[]{:S(2)}) collective-permute-start(bf16[96,512]{1,0:T(8,128)(2,1)S(1)} %get-tuple-element.26), channel_id=1, source_target_pairs={{0,12},{1,13},{2,14},{3,15},{4,8},{5,9},{6,10},{7,11},{8,4},{9,5},... | collective-permute-start | bytes 294920 | tf_op jit(solution)/shard_map/ppermute | solution.py:376
  7.7 0.6 collective-permute-start
  8.3 4.0 %own_tile_0.1 = (bf16[4,512,512]{2,1,0:T(8,128)(2,1)}, f32[8,2048]{1,0:T(8,128)S(1)}) custom-call(bf16[2048,128]{1,0:T(8,128)(2,1)S(1)} %get-tuple-element.23.left_ref, bf16[128,2048]{1,0:T(8,128)(2,1)S(1)} %get-tuple-element.22.right_ref.arrived_ref, bf16[8,2048]{1,0:T(8,128)(2,1)S(1)} %get-tuple-element.24.vec_ref, ...), custom_call_target="tpu_custom_call" | custom-call | flops 5000000000 | bytes 2097152 | tf_op jit(solution)/shard_map/own_tile_0/pallas_call | solution.py:466
  12.3 3.8 %collective-permute-start.8 = (bf16[80,512]{1,0:T(8,128)(2,1)S(1)}, bf16[80,512]{1,0:T(8,128)(2,1)S(1)}, u32[]{:S(2)}, u32[]{:S(2)}) collective-permute-start(bf16[80,512]{1,0:T(8,128)(2,1)S(1)} %gate.6), channel_id=1, source_target_pairs={{0,12},{1,13},{2,14},{3,15},{4,8},{5,9},{6,10},{7,11},{8,4},{9,5},... | collective-permute-start | bytes 245768 | tf_op jit(solution)/shard_map/ppermute | solution.py:376
  16.2 0.6 collective-permute-start.6
  16.8 3.1 %collective-permute-done.1 = bf16[96,512]{1,0:T(8,128)(2,1)S(1)} collective-permute-done((bf16[96,512]{1,0:T(8,128)(2,1)S(1)}, bf16[96,512]{1,0:T(8,128)(2,1)S(1)}, u32[]{:S(2)}, u32[]{:S(2)}) %collective-permute-start.1) | collective-permute-done | bytes 98336 | tf_op jit(solution)/shard_map/ppermute | solution.py:376
  20.0 1.6 %collective-permute-start.3 = (bf16[384,512]{1,0:T(8,128)(2,1)S(1)}, bf16[384,512]{1,0:T(8,128)(2,1)S(1)}, u32[]{:S(2)}, u32[]{:S(2)}) collective-permute-start(bf16[384,512]{1,0:T(8,128)(2,1)S(1)} %gate.4.arrived_ref.refs_2_), channel_id=1, source_target_pairs={{0,2},{1,3},{2,0},{3,1},{4,6},{5,7},{6,4},{7,5},{8,10},{9,11},{10,... | collective-permute-start | bytes 1179656 | tf_op jit(solution)/shard_map/ppermute | solution.py:376
  21.6 5.6 %own_tile_1.1 = (bf16[6,512,512]{2,1,0:T(8,128)(2,1)}, f32[8,2048]{1,0:T(8,128)S(1)}) custom-call(bf16[2048,128]{1,0:T(8,128)(2,1)S(1)} %get-tuple-element.23.left_ref, bf16[128,2048]{1,0:T(8,128)(2,1)S(1)} %get-tuple-element.22.right_ref.arrived_ref, bf16[8,2048]{1,0:T(8,128)(2,1)S(1)} %get-tuple-element.24.vec_ref, ...), custom_call_target="tpu_custom_call" | custom-call | flops 5000000000 | bytes 3145728 | tf_op jit(solution)/shard_map/own_tile_1/pallas_call | solution.py:466
  27.2 4.3 %collective-permute-done.3.refs_0_ = bf16[384,512]{1,0:T(8,128)(2,1)S(1)} collective-permute-done((bf16[384,512]{1,0:T(8,128)(2,1)S(1)}, bf16[384,512]{1,0:T(8,128)(2,1)S(1)}, u32[]{:S(2)}, u32[]{:S(2)}) %collective-permute-start.3) | collective-permute-done | bytes 393248 | tf_op jit(solution)/shard_map/ppermute | solution.py:376
  31.6 1.7 %collective-permute-start.11 = (bf16[320,512]{1,0:T(8,128)(2,1)S(1)}, bf16[320,512]{1,0:T(8,128)(2,1)S(1)}, u32[]{:S(2)}, u32[]{:S(2)}) collective-permute-start(bf16[320,512]{1,0:T(8,128)(2,1)S(1)} %gate.7.refs_0_), channel_id=1, source_target_pairs={{0,3},{1,2},{2,1},{3,0},{4,7},{5,6},{6,5},{7,4},{8,11},{9,10},{10,... | collective-permute-start | bytes 983048 | tf_op jit(solution)/shard_map/ppermute | solution.py:376
  33.9 28.7 %pair_zero.1 = (bf16[3,1024,2048]{2,1,0:T(8,128)(2,1)S(1)}, bf16[2,1024,2048]{2,1,0:T(8,128)(2,1)}, f32[8,2048]{1,0:T(8,128)S(1)}, s32[7]{0:T(128)S(1)}) custom-call(s32[1]{0:T(128)} %bitcast.me_ref, bf16[128,2048]{1,0:T(8,128)(2,1)S(1)} %get-tuple-element.22.right_ref.arrived_ref, f32[8,2048]{1,0:T(8,128)S(1)} %get-tuple-element.25.refs_1_.refs_0_, ...), custom_call_target="tpu_custom_call" | custom-call | tf_op jit(solution)/shard_map/pair_zero/pallas_call | solution.py:525
  62.7 27.6 %pair_one.1 = (bf16[3,1024,2048]{2,1,0:T(8,128)(2,1)S(1)}, bf16[2,1024,2048]{2,1,0:T(8,128)(2,1)}, f32[8,2048]{1,0:T(8,128)S(1)}, bf16[8,2176]{1,0:T(8,128)(2,1)S(1)}) custom-call(s32[7]{0:T(128)S(1)} %get-tuple-element.28.slots_ref, bf16[128,2048]{1,0:T(8,128)(2,1)S(1)} %get-tuple-element.22.right_ref.arrived_ref, ...), custom_call_target="tpu_custom_call" | custom-call | tf_op jit(solution)/shard_map/pair_one/pallas_call | solution.py:545
  90.4 4.3 %collective-permute-start.12 = (bf16[1,8,2176]{2,1,0:T(8,128)(2,1)S(1)}, bf16[1,8,2176]{2,1,0:T(8,128)(2,1)S(1)}, u32[]{:S(2)}, u32[]{:S(2)}) collective-permute-start(bf16[1,8,2176]{2,1,0:T(8,128)(2,1)S(1)} %bitcast.7), channel_id=1, source_target_pairs={{0,4},{1,5},{2,6},{3,7},{4,0},{5,1},{6,2},{7,3},{8,12},{9,13},{10,... | collective-permute-start | bytes 104456 | tf_op jit(solution)/shard_map/ppermute | solution.py:376
  94.7 2.4 %own_again_1.1.refs_1_ = f32[8,2048]{1,0:T(8,128)S(1)} custom-call(bf16[6,512,512]{2,1,0:T(8,128)(2,1)} %get-tuple-element.38.in_ref, bf16[8,2176]{1,0:T(8,128)(2,1)S(1)} %get-tuple-element.35.vec_ref), custom_call_target="tpu_custom_call" | custom-call | flops 5000000000 | bytes 3145728 | tf_op jit(solution)/shard_map/own_again_1/pallas_call | solution.py:569
  97.2 5.0 %collective-permute-done.15 = bf16[4,8,2176]{2,1,0:T(8,128)(2,1)S(1)} collective-permute-done((bf16[4,8,2176]{2,1,0:T(8,128)(2,1)S(1)}, bf16[4,8,2176]{2,1,0:T(8,128)(2,1)S(1)}, u32[]{:S(2)}, u32[]{:S(2)}) %collective-permute-start.15) | collective-permute-done | bytes 139296 | tf_op jit(solution)/shard_map/ppermute | solution.py:376
  102.3 2.0 %own_again_0.1.refs_0_ = f32[8,2048]{1,0:T(8,128)S(1)} custom-call(bf16[4,512,512]{2,1,0:T(8,128)(2,1)} %get-tuple-element.37.in_ref, bf16[8,2176]{1,0:T(8,128)(2,1)S(1)} %get-tuple-element.35.vec_ref), custom_call_target="tpu_custom_call" | custom-call | flops 5000000000 | bytes 2097152 | tf_op jit(solution)/shard_map/own_again_0/pallas_call | solution.py:569
  104.4 10.3 %pair_again.1 = (f32[32,2048]{1,0:T(8,128)S(1)}, f32[8,128]{1,0:T(8,128)S(1)}, f32[8,128]{1,0:T(8,128)S(1)}) custom-call(s32[7]{0:T(128)S(1)} %get-tuple-element.28.slots_ref, bf16[3,1024,2048]{2,1,0:T(8,128)(2,1)S(1)} %get-tuple-element.29.front_zero_ref, bf16[3,1024,2048]{2,1,0:T(8,128)(2,1)S(1)} %get-tuple-element.32.front_one_ref, ...), custom_call_target="tpu_custom_call" | custom-call | tf_op jit(solution)/shard_map/pair_again/pallas_call | solution.py:587
  114.8 4.3 %collective-permute-start.17 = (f32[8,128]{1,0:T(8,128)S(1)}, f32[8,128]{1,0:T(8,128)S(1)}, u32[]{:S(2)}, u32[]{:S(2)}) collective-permute-start(f32[8,128]{1,0:T(8,128)S(1)} %get-tuple-element.41), channel_id=1, source_target_pairs={{0,4},{1,5},{2,6},{3,7},{4,0},{5,1},{6,2},{7,3},{8,12},{9,13},{10,... | collective-permute-start | bytes 12296 | tf_op jit(solution)/shard_map/ppermute | solution.py:376
  119.1 1.0 collective-permute-done.19
  120.7 1.2 collective-permute-start.21
  122.6 1.5 %curve_order.1 = f32[32,2048]{1,0:T(8,128)S(1)} custom-call(f32[32,2048]{1,0:T(8,128)S(1)} %get-tuple-element.40.rows_ref, s32[1,2048]{1,0:T(1,128)S(1)} %copy-done.2), custom_call_target="tpu_custom_call" | custom-call | tf_op jit(solution)/shard_map/curve_order/pallas_call | solution.py:625
  124.6 0.8 fusion.2
  (55 shorter events, 3.0 us)
Async XLA Ops:
  2.6 13.6 %collective-permute-start.2 = (bf16[96,512]{1,0:T(8,128)(2,1)S(1)}, bf16[96,512]{1,0:T(8,128)(2,1)S(1)}, u32[]{:S(2)}, u32[]{:S(2)}) collective-permute-start(bf16[96,512]{1,0:T(8,128)(2,1)S(1)} %get-tuple-element.26), channel_id=1, source_target_pairs={{0,12},{1,13},{2,14},{3,15},{4,8},{5,9},{6,10},{7,11},{8,4},{9,5},... | collective-permute-start | bytes 294920 | tf_op jit(solution)/shard_map/ppermute | solution.py:376
  7.7 12.2 %collective-permute-start.1 = (bf16[96,512]{1,0:T(8,128)(2,1)S(1)}, bf16[96,512]{1,0:T(8,128)(2,1)S(1)}, u32[]{:S(2)}, u32[]{:S(2)}) collective-permute-start(bf16[96,512]{1,0:T(8,128)(2,1)S(1)} %get-tuple-element.26), channel_id=1, source_target_pairs={{0,8},{1,9},{2,10},{3,11},{4,12},{5,13},{6,14},{7,15},{8,0},{9,1},... | collective-permute-start | bytes 294920 | tf_op jit(solution)/shard_map/ppermute | solution.py:376
  7.7 12.2 %collective-permute-start = (bf16[96,512]{1,0:T(8,128)(2,1)S(1)}, bf16[96,512]{1,0:T(8,128)(2,1)S(1)}, u32[]{:S(2)}, u32[]{:S(2)}) collective-permute-start(bf16[96,512]{1,0:T(8,128)(2,1)S(1)} %get-tuple-element.26), channel_id=1, source_target_pairs={{0,4},{1,5},{2,6},{3,7},{4,0},{5,1},{6,2},{7,3},{8,12},{9,13},{10,... | collective-permute-start | bytes 294920 | tf_op jit(solution)/shard_map/ppermute | solution.py:376
  12.3 19.2 %collective-permute-start.8 = (bf16[80,512]{1,0:T(8,128)(2,1)S(1)}, bf16[80,512]{1,0:T(8,128)(2,1)S(1)}, u32[]{:S(2)}, u32[]{:S(2)}) collective-permute-start(bf16[80,512]{1,0:T(8,128)(2,1)S(1)} %gate.6), channel_id=1, source_target_pairs={{0,12},{1,13},{2,14},{3,15},{4,8},{5,9},{6,10},{7,11},{8,4},{9,5},... | collective-permute-start | bytes 245768 | tf_op jit(solution)/shard_map/ppermute | solution.py:376
  16.1 15.4 %collective-permute-start.7 = (bf16[80,512]{1,0:T(8,128)(2,1)S(1)}, bf16[80,512]{1,0:T(8,128)(2,1)S(1)}, u32[]{:S(2)}, u32[]{:S(2)}) collective-permute-start(bf16[80,512]{1,0:T(8,128)(2,1)S(1)} %gate.6), channel_id=1, source_target_pairs={{0,8},{1,9},{2,10},{3,11},{4,12},{5,13},{6,14},{7,15},{8,0},{9,1},... | collective-permute-start | bytes 245768 | tf_op jit(solution)/shard_map/ppermute | solution.py:376
  16.2 15.4 %collective-permute-start.6 = (bf16[80,512]{1,0:T(8,128)(2,1)S(1)}, bf16[80,512]{1,0:T(8,128)(2,1)S(1)}, u32[]{:S(2)}, u32[]{:S(2)}) collective-permute-start(bf16[80,512]{1,0:T(8,128)(2,1)S(1)} %gate.6), channel_id=1, source_target_pairs={{0,4},{1,5},{2,6},{3,7},{4,0},{5,1},{6,2},{7,3},{8,12},{9,13},{10,... | collective-permute-start | bytes 245768 | tf_op jit(solution)/shard_map/ppermute | solution.py:376
  19.9 42.7 %copy-start = (f32[8,2048]{1,0:T(8,128)S(1)}, f32[8,2048]{1,0:T(8,128)}, u32[]{:S(2)}) copy-start(f32[8,2048]{1,0:T(8,128)} %rhs_ref.5) | copy-start | bytes 196612
  20.0 13.9 %collective-permute-start.4 = (bf16[384,512]{1,0:T(8,128)(2,1)S(1)}, bf16[384,512]{1,0:T(8,128)(2,1)S(1)}, u32[]{:S(2)}, u32[]{:S(2)}) collective-permute-start(bf16[384,512]{1,0:T(8,128)(2,1)S(1)} %gate.4.arrived_ref.refs_2_), channel_id=1, source_target_pairs={{0,1},{1,0},{2,3},{3,2},{4,5},{5,4},{6,7},{7,6},{8,9},{9,8},{10,11... | collective-permute-start | bytes 1179656 | tf_op jit(solution)/shard_map/ppermute | solution.py:376
  20.0 11.5 %collective-permute-start.3 = (bf16[384,512]{1,0:T(8,128)(2,1)S(1)}, bf16[384,512]{1,0:T(8,128)(2,1)S(1)}, u32[]{:S(2)}, u32[]{:S(2)}) collective-permute-start(bf16[384,512]{1,0:T(8,128)(2,1)S(1)} %gate.4.arrived_ref.refs_2_), channel_id=1, source_target_pairs={{0,2},{1,3},{2,0},{3,1},{4,6},{5,7},{6,4},{7,5},{8,10},{9,11},{10,... | collective-permute-start | bytes 1179656 | tf_op jit(solution)/shard_map/ppermute | solution.py:376
  31.6 2.3 %collective-permute-start.5 = (bf16[384,512]{1,0:T(8,128)(2,1)S(1)}, bf16[384,512]{1,0:T(8,128)(2,1)S(1)}, u32[]{:S(2)}, u32[]{:S(2)}) collective-permute-start(bf16[384,512]{1,0:T(8,128)(2,1)S(1)} %gate.5.refs_3_), channel_id=1, source_target_pairs={{0,1},{1,0},{2,3},{3,2},{4,5},{5,4},{6,7},{7,6},{8,9},{9,8},{10,11... | collective-permute-start | bytes 1179656 | tf_op jit(solution)/shard_map/ppermute | solution.py:376
  31.6 31.0 %collective-permute-start.11 = (bf16[320,512]{1,0:T(8,128)(2,1)S(1)}, bf16[320,512]{1,0:T(8,128)(2,1)S(1)}, u32[]{:S(2)}, u32[]{:S(2)}) collective-permute-start(bf16[320,512]{1,0:T(8,128)(2,1)S(1)} %gate.7.refs_0_), channel_id=1, source_target_pairs={{0,3},{1,2},{2,1},{3,0},{4,7},{5,6},{6,5},{7,4},{8,11},{9,10},{10,... | collective-permute-start | bytes 983048 | tf_op jit(solution)/shard_map/ppermute | solution.py:376
  33.3 29.3 %collective-permute-start.10 = (bf16[320,512]{1,0:T(8,128)(2,1)S(1)}, bf16[320,512]{1,0:T(8,128)(2,1)S(1)}, u32[]{:S(2)}, u32[]{:S(2)}) collective-permute-start(bf16[320,512]{1,0:T(8,128)(2,1)S(1)} %gate.7.refs_0_), channel_id=1, source_target_pairs={{0,1},{1,0},{2,3},{3,2},{4,5},{5,4},{6,7},{7,6},{8,9},{9,8},{10,11... | collective-permute-start | bytes 983048 | tf_op jit(solution)/shard_map/ppermute | solution.py:376
  33.3 29.3 %collective-permute-start.9 = (bf16[320,512]{1,0:T(8,128)(2,1)S(1)}, bf16[320,512]{1,0:T(8,128)(2,1)}, u32[]{:S(2)}, u32[]{:S(2)}) collective-permute-start(bf16[320,512]{1,0:T(8,128)(2,1)S(1)} %gate.7.refs_0_), channel_id=1, source_target_pairs={{0,2},{1,3},{2,0},{3,1},{4,6},{5,7},{6,4},{7,5},{8,10},{9,11},{10,... | collective-permute-start | bytes 983048 | tf_op jit(solution)/shard_map/ppermute | solution.py:376
  90.2 6.8 %collective-permute-start.14 = (bf16[1,8,2176]{2,1,0:T(8,128)(2,1)S(1)}, bf16[1,8,2176]{2,1,0:T(8,128)(2,1)S(1)}, u32[]{:S(2)}, u32[]{:S(2)}) collective-permute-start(bf16[1,8,2176]{2,1,0:T(8,128)(2,1)S(1)} %bitcast.5), channel_id=1, source_target_pairs={{0,12},{1,13},{2,14},{3,15},{4,8},{5,9},{6,10},{7,11},{8,4},{9,5},... | collective-permute-start | bytes 104456 | tf_op jit(solution)/shard_map/ppermute | solution.py:376
  90.3 6.8 %collective-permute-start.13 = (bf16[1,8,2176]{2,1,0:T(8,128)(2,1)S(1)}, bf16[1,8,2176]{2,1,0:T(8,128)(2,1)S(1)}, u32[]{:S(2)}, u32[]{:S(2)}) collective-permute-start(bf16[1,8,2176]{2,1,0:T(8,128)(2,1)S(1)} %bitcast.6), channel_id=1, source_target_pairs={{0,8},{1,9},{2,10},{3,11},{4,12},{5,13},{6,14},{7,15},{8,0},{9,1},... | collective-permute-start | bytes 104456 | tf_op jit(solution)/shard_map/ppermute | solution.py:376
  90.4 6.7 %collective-permute-start.12 = (bf16[1,8,2176]{2,1,0:T(8,128)(2,1)S(1)}, bf16[1,8,2176]{2,1,0:T(8,128)(2,1)S(1)}, u32[]{:S(2)}, u32[]{:S(2)}) collective-permute-start(bf16[1,8,2176]{2,1,0:T(8,128)(2,1)S(1)} %bitcast.7), channel_id=1, source_target_pairs={{0,4},{1,5},{2,6},{3,7},{4,0},{5,1},{6,2},{7,3},{8,12},{9,13},{10,... | collective-permute-start | bytes 104456 | tf_op jit(solution)/shard_map/ppermute | solution.py:376
  97.1 5.1 %collective-permute-start.15 = (bf16[4,8,2176]{2,1,0:T(8,128)(2,1)S(1)}, bf16[4,8,2176]{2,1,0:T(8,128)(2,1)S(1)}, u32[]{:S(2)}, u32[]{:S(2)}) collective-permute-start(bf16[4,8,2176]{2,1,0:T(8,128)(2,1)S(1)} %pad_maximum_fusion.2), channel_id=1, source_target_pairs={{0,2},{1,3},{2,0},{3,1},{4,6},{5,7},{6,4},{7,5},{8,10},{9,11},{10,... | collective-permute-start | bytes 417800 | tf_op jit(solution)/shard_map/ppermute | solution.py:376
  102.3 2.1 %collective-permute-start.16 = (bf16[8,8,2176]{2,1,0:T(8,128)(2,1)S(1)}, bf16[8,8,2176]{2,1,0:T(8,128)(2,1)S(1)}, u32[]{:S(2)}, u32[]{:S(2)}) collective-permute-start(bf16[8,8,2176]{2,1,0:T(8,128)(2,1)S(1)} %get-tuple-element.47), channel_id=1, source_target_pairs={{0,1},{1,0},{2,3},{3,2},{4,5},{5,4},{6,7},{7,6},{8,9},{9,8},{10,11... | collective-permute-start | bytes 835592 | tf_op jit(solution)/shard_map/ppermute | solution.py:376
  114.7 5.5 %collective-permute-start.19 = (f32[8,128]{1,0:T(8,128)S(1)}, f32[8,128]{1,0:T(8,128)S(1)}, u32[]{:S(2)}, u32[]{:S(2)}) collective-permute-start(f32[8,128]{1,0:T(8,128)S(1)} %get-tuple-element.41), channel_id=1, source_target_pairs={{0,12},{1,13},{2,14},{3,15},{4,8},{5,9},{6,10},{7,11},{8,4},{9,5},... | collective-permute-start | bytes 12296 | tf_op jit(solution)/shard_map/ppermute | solution.py:376
  114.7 5.4 %collective-permute-start.18 = (f32[8,128]{1,0:T(8,128)S(1)}, f32[8,128]{1,0:T(8,128)S(1)}, u32[]{:S(2)}, u32[]{:S(2)}) collective-permute-start(f32[8,128]{1,0:T(8,128)S(1)} %get-tuple-element.41), channel_id=1, source_target_pairs={{0,8},{1,9},{2,10},{3,11},{4,12},{5,13},{6,14},{7,15},{8,0},{9,1},... | collective-permute-start | bytes 12296 | tf_op jit(solution)/shard_map/ppermute | solution.py:376
  114.8 5.9 %collective-permute-start.17 = (f32[8,128]{1,0:T(8,128)S(1)}, f32[8,128]{1,0:T(8,128)S(1)}, u32[]{:S(2)}, u32[]{:S(2)}) collective-permute-start(f32[8,128]{1,0:T(8,128)S(1)} %get-tuple-element.41), channel_id=1, source_target_pairs={{0,4},{1,5},{2,6},{3,7},{4,0},{5,1},{6,2},{7,3},{8,12},{9,13},{10,... | collective-permute-start | bytes 12296 | tf_op jit(solution)/shard_map/ppermute | solution.py:376
  120.7 3.3 %collective-permute-start.22 = (f32[8,128]{1,0:T(8,128)S(1)}, f32[8,128]{1,0:T(8,128)S(1)}, u32[]{:S(2)}, u32[]{:S(2)}) collective-permute-start(f32[8,128]{1,0:T(8,128)S(1)} %add_add_fusion.1), channel_id=1, source_target_pairs={{0,3},{1,2},{2,1},{3,0},{4,7},{5,6},{6,5},{7,4},{8,11},{9,10},{10,... | collective-permute-start | bytes 12296 | tf_op jit(solution)/shard_map/ppermute | solution.py:376
  120.7 3.7 %collective-permute-start.21 = (f32[8,128]{1,0:T(8,128)S(1)}, f32[8,128]{1,0:T(8,128)S(1)}, u32[]{:S(2)}, u32[]{:S(2)}) collective-permute-start(f32[8,128]{1,0:T(8,128)S(1)} %add_add_fusion.1), channel_id=1, source_target_pairs={{0,2},{1,3},{2,0},{3,1},{4,6},{5,7},{6,4},{7,5},{8,10},{9,11},{10,... | collective-permute-start | bytes 12296 | tf_op jit(solution)/shard_map/ppermute | solution.py:376
  122.0 2.4 %collective-permute-start.20 = (f32[8,128]{1,0:T(8,128)S(1)}, f32[8,128]{1,0:T(8,128)S(1)}, u32[]{:S(2)}, u32[]{:S(2)}) collective-permute-start(f32[8,128]{1,0:T(8,128)S(1)} %add_add_fusion.1), channel_id=1, source_target_pairs={{0,1},{1,0},{2,3},{3,2},{4,5},{5,4},{6,7},{7,6},{8,9},{9,8},{10,11... | collective-permute-start | bytes 12296 | tf_op jit(solution)/shard_map/ppermute | solution.py:376
  (2 other events, 60.9 us)

commit v13 on v11

--- a/solution.py
+++ b/solution.py
@@ -15,8 +15,7 @@
 KDIM = 128
 ROWS = 512
 PARTS = 2
-COLS = 512
-SUB = 64
+COLS = 1024
 FRONT = 3
 HELD = 4
 TAIL = 128
@@ -54,6 +53,16 @@
     return jnp.transpose(jnp.concatenate([feat, feat, feat, norm_rows(norm, 3)], axis=0))
 
 
+def psi_chain(dist):
+    dist = jnp.maximum(dist, 1e-30)
+    radius = dist * lax.rsqrt(dist)
+    u = jnp.maximum(SHRINK - radius, 0.0)
+    two = u * u
+    four = two * two
+    eight = four * four
+    return (eight * eight * two * (u - two)).astype(BF16)
+
+
 def psi_power(dist):
     dist = jnp.maximum(dist, 1e-30)
     radius = dist * lax.rsqrt(dist)
@@ -61,12 +70,12 @@
     return (jnp.exp2(19.0 * lax.log2(u)) * (1.0 - u)).astype(BF16)
 
 
-def tile_unit(left, right, vec, tile_ref):
+def tile_unit(left, right, vec, tile_ref, psis, strip):
     dist = jnp.dot(left, right, preferred_element_type=F32)
     parts = []
-    for sub in range(0, left.shape[0], SUB):
-        part = psi_power(dist[sub : sub + SUB])
-        tile_ref[sub : sub + SUB, :] = part
+    for index, sub in enumerate(range(0, left.shape[0], strip)):
+        part = psis[index % len(psis)](dist[sub : sub + strip])
+        tile_ref[sub : sub + strip, :] = part
         parts.append(part)
     return jnp.dot(vec, jnp.concatenate(parts, axis=0), preferred_element_type=F32)
 
@@ -91,7 +100,7 @@
         def col_step(col, at):
             sum_ref[:, piece(col)] += tile_unit(
                 left_ref[piece(row), :], right_ref[:, piece(col)], vec_ref[:, piece(row)],
-                tile_ref.at[at],
+                tile_ref.at[at], (psi_power,), 64,
             )
             save(at).start()
 
@@ -182,7 +191,7 @@
     return fetch
 
 
-def half_tiles(slots_ref, right_ref, fetch, front_ref, back_ref, sum_ref, left_ref, vec_ref, pay_ref, sem_ref):
+def half_tiles(psis, strip, slots_ref, right_ref, fetch, front_ref, back_ref, sum_ref, left_ref, vec_ref, pay_ref, sem_ref):
     slot, step = pl.program_id(0), pl.program_id(1)
 
     @pl.when((slot == 0) & (step == 0) & (slots_ref[0] > 0))
@@ -213,7 +222,7 @@
                 def unit(index, carry):
                     cols = pl.ds(pl.multiple_of(index * COLS, COLS), COLS)
                     sum_ref[:, cols] += tile_unit(
-                        left, right_ref[:, cols], vec, tile_ref.at[0, :, cols]
+                        left, right_ref[:, cols], vec, tile_ref.at[0, :, cols], psis, strip
                     )
                     return carry
 
@@ -248,7 +257,7 @@
 
     fetch = fetch_from(block_at, block_refs, slots_ref, pay_ref, sem_ref)
     half_tiles(
-        slots_ref, right_ref, fetch, front_ref, back_ref, sum_ref, left_ref, vec_ref, pay_ref, sem_ref
+        (psi_power, psi_chain), 64, slots_ref, right_ref, fetch, front_ref, back_ref, sum_ref, left_ref, vec_ref, pay_ref, sem_ref
     )
 
 
@@ -263,7 +272,7 @@
 
     fetch = fetch_from(block_at, block_refs, slots_ref, pay_ref, sem_ref)
     half_tiles(
-        slots_ref, right_ref, fetch, front_ref, back_ref, image_ref, left_ref, vec_ref, pay_ref, sem_ref
+        (psi_power,), 128, slots_ref, right_ref, fetch, front_ref, back_ref, image_ref, left_ref, vec_ref, pay_ref, sem_ref
     )
 
     @pl.when((slot == pl.num_programs(0) - 1) & (step == pl.num_programs(1) - 1))
@@ -423,6 +432,7 @@
         out_specs=pl.BlockSpec(memory_space=pl.ANY),
         out_shape=jax.ShapeDtypeStruct(block.shape, block.dtype),
         input_output_aliases={0: 0},
+        compiler_params=pltpu.CompilerParams(vmem_limit_bytes=1024 * 1024),
         name="gate",
     )(block, behind)
 

time: 140 us -> 126 us (0.900)
  Pallas kernels: 92.8 us -> 40.1 us
  starting transfers between devices: 28.9 us -> 61.1 us
  waiting for transfers between devices: 8.26 us -> 22.6 us
  local copies, waits for them, and re-layouts: 6.71 us -> 0.88 us
  other arithmetic: 2.58 us -> 1.07 us
    ppermute x23, starting transfers between devices: 28.9 us -> 61.1 us  [swap(): return lax.ppermute(value, 'row', [(i, i ^ mask) for i in range(count)])]
    pallas_call x1, Pallas kernels: 33.7 us -> 10.2 us  [local(): pl.pallas_call(functools.partial(pair_zero_kernel, zero_at), grid_spec=pl...]
    pallas_call x1, Pallas kernels: 32.5 us -> 10.1 us  [local(): pl.pallas_call(functools.partial(pair_one_kernel, one_at), grid_spec=pltp...]
    ppermute x23, waiting for transfers between devices: 8.26 us -> 22.6 us  [swap(): return lax.ppermute(value, 'row', [(i, i ^ mask) for i in range(count)])]
    pallas_call x1, Pallas kernels: 10.1 us -> 3.31 us  [local(): pl.pallas_call(again_kernel, grid_spec=pltpu.PrefetchScalarGridSpec(num_s...]
    unnamed x33 -> x11, local copies, waits for them, and re-layouts: 6.66 us -> 0.83 us
    concatenate x2, other arithmetic: 1.56 us -> 0.05 us  [local(): jnp.concatenate([pay] + [swap(pay, mask, count) for mask in first_masks],...]
  transfers between devices with their start and end apart: 23 -> 23, of which waited for: 6 -> 8; matrix products, arithmetic and copies ran while one was open for 1% -> 0% of each run, Pallas kernels for 35% -> 20%
where the time goes in v13:
time: 126 us; the launch traced here: 127 us
  starting transfers between devices  61.1 us (48%)
  Pallas kernels  40.1 us (32%)
  waiting for transfers between devices  22.6 us (18%)
    ppermute x23, starting transfers between devices, swap(): return lax.ppermute(value, 'row', [(i, i ^ mask) for i in range(count)])  61.1 us
    ppermute x23, waiting for transfers between devices, swap(): return lax.ppermute(value, 'row', [(i, i ^ mask) for i in range(count)])  22.6 us
    pallas_call x1, Pallas kernels, local(): pl.pallas_call(functools.partial(pair_zero_kernel, zero_at), grid_spec=pl...  10.2 us
    pallas_call x1, Pallas kernels, local(): pl.pallas_call(functools.partial(pair_one_kernel, one_at), grid_spec=pltp...  10.1 us
    pallas_call x2, Pallas kernels, own_part(): pl.pallas_call(functools.partial(own_kernel, rows), in_specs=[vmem, vmem,...  9.61 us
    pallas_call x2, Pallas kernels, local(): pl.pallas_call(functools.partial(own_again_kernel, blocks), in_specs=[any...  4.34 us
    pallas_call x1, Pallas kernels, local(): pl.pallas_call(again_kernel, grid_spec=pltpu.PrefetchScalarGridSpec(num_s...  3.31 us
  transfers between devices with their start and end apart: 23, of which 8 were waited for; matrix products, arithmetic and copies ran while one was open for 0% of the time, Pallas kernels for 20%

profile of v13, /device:TPU:0, one launch (start us, length us, event | category | flops | bytes accessed | tf_op | source)
XLA Modules:
  0.0 126.7 jit_solution(3273950193260901089)
XLA Ops:
  1.4 1.2 payload.1
  2.6 5.1 %collective-permute-start.2 = (bf16[96,512]{1,0:T(8,128)(2,1)S(1)}, bf16[96,512]{1,0:T(8,128)(2,1)S(1)}, u32[]{:S(2)}, u32[]{:S(2)}) collective-permute-start(bf16[96,512]{1,0:T(8,128)(2,1)S(1)} %get-tuple-element.26), channel_id=1, source_target_pairs={{0,12},{1,13},{2,14},{3,15},{4,8},{5,9},{6,10},{7,11},{8,4},{9,5},... | collective-permute-start | bytes 294920 | tf_op jit(solution)/shard_map/ppermute | solution.py:385
  8.3 4.0 %own_tile_0.1 = (bf16[4,512,512]{2,1,0:T(8,128)(2,1)}, f32[8,2048]{1,0:T(8,128)S(1)}) custom-call(bf16[2048,128]{1,0:T(8,128)(2,1)S(1)} %get-tuple-element.23.left_ref, bf16[128,2048]{1,0:T(8,128)(2,1)S(1)} %get-tuple-element.22.right_ref.arrived_ref, bf16[8,2048]{1,0:T(8,128)(2,1)S(1)} %get-tuple-element.24.vec_ref, ...), custom_call_target="tpu_custom_call" | custom-call | flops 5000000000 | bytes 2097152 | tf_op jit(solution)/shard_map/own_tile_0/pallas_call | solution.py:475
  12.3 3.8 %collective-permute-start.8 = (bf16[80,512]{1,0:T(8,128)(2,1)S(1)}, bf16[80,512]{1,0:T(8,128)(2,1)S(1)}, u32[]{:S(2)}, u32[]{:S(2)}) collective-permute-start(bf16[80,512]{1,0:T(8,128)(2,1)S(1)} %gate.6), channel_id=1, source_target_pairs={{0,12},{1,13},{2,14},{3,15},{4,8},{5,9},{6,10},{7,11},{8,4},{9,5},... | collective-permute-start | bytes 245768 | tf_op jit(solution)/shard_map/ppermute | solution.py:385
  16.8 3.1 %collective-permute-done.1 = bf16[96,512]{1,0:T(8,128)(2,1)S(1)} collective-permute-done((bf16[96,512]{1,0:T(8,128)(2,1)S(1)}, bf16[96,512]{1,0:T(8,128)(2,1)S(1)}, u32[]{:S(2)}, u32[]{:S(2)}) %collective-permute-start.1) | collective-permute-done | bytes 98336 | tf_op jit(solution)/shard_map/ppermute | solution.py:385
  20.0 1.6 %collective-permute-start.3 = (bf16[384,512]{1,0:T(8,128)(2,1)S(1)}, bf16[384,512]{1,0:T(8,128)(2,1)S(1)}, u32[]{:S(2)}, u32[]{:S(2)}) collective-permute-start(bf16[384,512]{1,0:T(8,128)(2,1)S(1)} %gate.4.arrived_ref.refs_2_), channel_id=1, source_target_pairs={{0,2},{1,3},{2,0},{3,1},{4,6},{5,7},{6,4},{7,5},{8,10},{9,11},{10,... | collective-permute-start | bytes 1179656 | tf_op jit(solution)/shard_map/ppermute | solution.py:385
  21.6 5.6 %own_tile_1.1 = (bf16[6,512,512]{2,1,0:T(8,128)(2,1)}, f32[8,2048]{1,0:T(8,128)S(1)}) custom-call(bf16[2048,128]{1,0:T(8,128)(2,1)S(1)} %get-tuple-element.23.left_ref, bf16[128,2048]{1,0:T(8,128)(2,1)S(1)} %get-tuple-element.22.right_ref.arrived_ref, bf16[8,2048]{1,0:T(8,128)(2,1)S(1)} %get-tuple-element.24.vec_ref, ...), custom_call_target="tpu_custom_call" | custom-call | flops 5000000000 | bytes 3145728 | tf_op jit(solution)/shard_map/own_tile_1/pallas_call | solution.py:475
  27.2 4.3 %collective-permute-done.3.refs_0_ = bf16[384,512]{1,0:T(8,128)(2,1)S(1)} collective-permute-done((bf16[384,512]{1,0:T(8,128)(2,1)S(1)}, bf16[384,512]{1,0:T(8,128)(2,1)S(1)}, u32[]{:S(2)}, u32[]{:S(2)}) %collective-permute-start.3) | collective-permute-done | bytes 393248 | tf_op jit(solution)/shard_map/ppermute | solution.py:385
  31.6 1.7 %collective-permute-start.11 = (bf16[320,512]{1,0:T(8,128)(2,1)S(1)}, bf16[320,512]{1,0:T(8,128)(2,1)S(1)}, u32[]{:S(2)}, u32[]{:S(2)}) collective-permute-start(bf16[320,512]{1,0:T(8,128)(2,1)S(1)} %gate.7.refs_0_), channel_id=1, source_target_pairs={{0,3},{1,2},{2,1},{3,0},{4,7},{5,6},{6,5},{7,4},{8,11},{9,10},{10,... | collective-permute-start | bytes 983048 | tf_op jit(solution)/shard_map/ppermute | solution.py:385
  33.8 10.2 %pair_zero.1 = (bf16[3,1024,2048]{2,1,0:T(8,128)(2,1)S(1)}, bf16[2,1024,2048]{2,1,0:T(8,128)(2,1)}, f32[8,2048]{1,0:T(8,128)S(1)}, s32[7]{0:T(128)S(1)}) custom-call(s32[1]{0:T(128)} %bitcast.me_ref, bf16[128,2048]{1,0:T(8,128)(2,1)S(1)} %get-tuple-element.22.right_ref.arrived_ref, f32[8,2048]{1,0:T(8,128)S(1)} %get-tuple-element.25.refs_1_.refs_0_, ...), custom_call_target="tpu_custom_call" | custom-call | tf_op jit(solution)/shard_map/pair_zero/pallas_call | solution.py:534
  44.0 4.8 %collective-permute-done.9.refs_1_ = bf16[320,512]{1,0:T(8,128)(2,1)} collective-permute-done((bf16[320,512]{1,0:T(8,128)(2,1)S(1)}, bf16[320,512]{1,0:T(8,128)(2,1)}, u32[]{:S(2)}, u32[]{:S(2)}) %collective-permute-start.9) | collective-permute-done | bytes 327712 | tf_op jit(solution)/shard_map/ppermute | solution.py:385
  48.8 10.1 %pair_one.1 = (bf16[3,1024,2048]{2,1,0:T(8,128)(2,1)S(1)}, bf16[2,1024,2048]{2,1,0:T(8,128)(2,1)}, f32[8,2048]{1,0:T(8,128)S(1)}, bf16[8,2176]{1,0:T(8,128)(2,1)S(1)}) custom-call(s32[7]{0:T(128)S(1)} %get-tuple-element.28.slots_ref, bf16[128,2048]{1,0:T(8,128)(2,1)S(1)} %get-tuple-element.22.right_ref.arrived_ref, ...), custom_call_target="tpu_custom_call" | custom-call | tf_op jit(solution)/shard_map/pair_one/pallas_call | solution.py:554
  58.9 32.3 %collective-permute-start.14 = (bf16[1,8,2176]{2,1,0:T(8,128)(2,1)S(1)}, bf16[1,8,2176]{2,1,0:T(8,128)(2,1)S(1)}, u32[]{:S(2)}, u32[]{:S(2)}) collective-permute-start(bf16[1,8,2176]{2,1,0:T(8,128)(2,1)S(1)} %bitcast.5), channel_id=1, source_target_pairs={{0,12},{1,13},{2,14},{3,15},{4,8},{5,9},{6,10},{7,11},{8,4},{9,5},... | collective-permute-start | bytes 104456 | tf_op jit(solution)/shard_map/ppermute | solution.py:385
  91.9 2.4 %own_again_1.1.refs_1_ = f32[8,2048]{1,0:T(8,128)S(1)} custom-call(bf16[6,512,512]{2,1,0:T(8,128)(2,1)} %get-tuple-element.38.in_ref, bf16[8,2176]{1,0:T(8,128)(2,1)S(1)} %get-tuple-element.35.vec_ref), custom_call_target="tpu_custom_call" | custom-call | flops 5000000000 | bytes 3145728 | tf_op jit(solution)/shard_map/own_again_1/pallas_call | solution.py:578
  94.2 2.0 %collective-permute-done.13 = bf16[1,8,2176]{2,1,0:T(8,128)(2,1)S(1)} collective-permute-done((bf16[1,8,2176]{2,1,0:T(8,128)(2,1)S(1)}, bf16[1,8,2176]{2,1,0:T(8,128)(2,1)S(1)}, u32[]{:S(2)}, u32[]{:S(2)}) %collective-permute-start.13) | collective-permute-done | bytes 34848 | tf_op jit(solution)/shard_map/ppermute | solution.py:385
  96.2 2.9 %collective-permute-start.15 = (bf16[4,8,2176]{2,1,0:T(8,128)(2,1)S(1)}, bf16[4,8,2176]{2,1,0:T(8,128)(2,1)S(1)}, u32[]{:S(2)}, u32[]{:S(2)}) collective-permute-start(bf16[4,8,2176]{2,1,0:T(8,128)(2,1)S(1)} %pad_maximum_fusion.2), channel_id=1, source_target_pairs={{0,2},{1,3},{2,0},{3,1},{4,6},{5,7},{6,4},{7,5},{8,10},{9,11},{10,... | collective-permute-start | bytes 417800 | tf_op jit(solution)/shard_map/ppermute | solution.py:385
  99.2 3.9 %collective-permute-done.15 = bf16[4,8,2176]{2,1,0:T(8,128)(2,1)S(1)} collective-permute-done((bf16[4,8,2176]{2,1,0:T(8,128)(2,1)S(1)}, bf16[4,8,2176]{2,1,0:T(8,128)(2,1)S(1)}, u32[]{:S(2)}, u32[]{:S(2)}) %collective-permute-start.15) | collective-permute-done | bytes 139296 | tf_op jit(solution)/shard_map/ppermute | solution.py:385
  103.2 2.0 %own_again_0.1.refs_0_ = f32[8,2048]{1,0:T(8,128)S(1)} custom-call(bf16[4,512,512]{2,1,0:T(8,128)(2,1)} %get-tuple-element.37.in_ref, bf16[8,2176]{1,0:T(8,128)(2,1)S(1)} %get-tuple-element.35.vec_ref), custom_call_target="tpu_custom_call" | custom-call | flops 5000000000 | bytes 2097152 | tf_op jit(solution)/shard_map/own_again_0/pallas_call | solution.py:578
  105.2 3.3 %pair_again.1 = (f32[32,2048]{1,0:T(8,128)S(1)}, f32[8,128]{1,0:T(8,128)S(1)}, f32[8,128]{1,0:T(8,128)S(1)}) custom-call(s32[7]{0:T(128)S(1)} %get-tuple-element.28.slots_ref, bf16[3,1024,2048]{2,1,0:T(8,128)(2,1)S(1)} %get-tuple-element.29.front_zero_ref, bf16[3,1024,2048]{2,1,0:T(8,128)(2,1)S(1)} %get-tuple-element.32.front_one_ref, ...), custom_call_target="tpu_custom_call" | custom-call | tf_op jit(solution)/shard_map/pair_again/pallas_call | solution.py:596
  108.5 8.5 %collective-permute-start.19 = (f32[8,128]{1,0:T(8,128)S(1)}, f32[8,128]{1,0:T(8,128)S(1)}, u32[]{:S(2)}, u32[]{:S(2)}) collective-permute-start(f32[8,128]{1,0:T(8,128)S(1)} %get-tuple-element.41), channel_id=1, source_target_pairs={{0,12},{1,13},{2,14},{3,15},{4,8},{5,9},{6,10},{7,11},{8,4},{9,5},... | collective-permute-start | bytes 12296 | tf_op jit(solution)/shard_map/ppermute | solution.py:385
  117.7 0.9 collective-permute-done.19
  118.6 2.9 %collective-permute-done.18 = f32[8,128]{1,0:T(8,128)S(1)} collective-permute-done((f32[8,128]{1,0:T(8,128)S(1)}, f32[8,128]{1,0:T(8,128)S(1)}, u32[]{:S(2)}, u32[]{:S(2)}) %collective-permute-start.18) | collective-permute-done | bytes 4128 | tf_op jit(solution)/shard_map/ppermute | solution.py:385
  122.1 1.4 %collective-permute-start.21 = (f32[8,128]{1,0:T(8,128)S(1)}, f32[8,128]{1,0:T(8,128)S(1)}, u32[]{:S(2)}, u32[]{:S(2)}) collective-permute-start(f32[8,128]{1,0:T(8,128)S(1)} %add_add_fusion.1), channel_id=1, source_target_pairs={{0,2},{1,3},{2,0},{3,1},{4,6},{5,7},{6,4},{7,5},{8,10},{9,11},{10,... | collective-permute-start | bytes 12296 | tf_op jit(solution)/shard_map/ppermute | solution.py:385
  123.5 1.5 %curve_order.1 = f32[32,2048]{1,0:T(8,128)S(1)} custom-call(f32[32,2048]{1,0:T(8,128)S(1)} %get-tuple-element.40.rows_ref, s32[1,2048]{1,0:T(1,128)S(1)} %copy-done.2), custom_call_target="tpu_custom_call" | custom-call | tf_op jit(solution)/shard_map/curve_order/pallas_call | solution.py:634
  (55 shorter events, 6.5 us)
Async XLA Ops:
  2.6 13.6 %collective-permute-start.2 = (bf16[96,512]{1,0:T(8,128)(2,1)S(1)}, bf16[96,512]{1,0:T(8,128)(2,1)S(1)}, u32[]{:S(2)}, u32[]{:S(2)}) collective-permute-start(bf16[96,512]{1,0:T(8,128)(2,1)S(1)} %get-tuple-element.26), channel_id=1, source_target_pairs={{0,12},{1,13},{2,14},{3,15},{4,8},{5,9},{6,10},{7,11},{8,4},{9,5},... | collective-permute-start | bytes 294920 | tf_op jit(solution)/shard_map/ppermute | solution.py:385
  7.7 12.2 %collective-permute-start.1 = (bf16[96,512]{1,0:T(8,128)(2,1)S(1)}, bf16[96,512]{1,0:T(8,128)(2,1)S(1)}, u32[]{:S(2)}, u32[]{:S(2)}) collective-permute-start(bf16[96,512]{1,0:T(8,128)(2,1)S(1)} %get-tuple-element.26), channel_id=1, source_target_pairs={{0,8},{1,9},{2,10},{3,11},{4,12},{5,13},{6,14},{7,15},{8,0},{9,1},... | collective-permute-start | bytes 294920 | tf_op jit(solution)/shard_map/ppermute | solution.py:385
  7.7 12.2 %collective-permute-start = (bf16[96,512]{1,0:T(8,128)(2,1)S(1)}, bf16[96,512]{1,0:T(8,128)(2,1)S(1)}, u32[]{:S(2)}, u32[]{:S(2)}) collective-permute-start(bf16[96,512]{1,0:T(8,128)(2,1)S(1)} %get-tuple-element.26), channel_id=1, source_target_pairs={{0,4},{1,5},{2,6},{3,7},{4,0},{5,1},{6,2},{7,3},{8,12},{9,13},{10,... | collective-permute-start | bytes 294920 | tf_op jit(solution)/shard_map/ppermute | solution.py:385
  12.3 19.2 %collective-permute-start.8 = (bf16[80,512]{1,0:T(8,128)(2,1)S(1)}, bf16[80,512]{1,0:T(8,128)(2,1)S(1)}, u32[]{:S(2)}, u32[]{:S(2)}) collective-permute-start(bf16[80,512]{1,0:T(8,128)(2,1)S(1)} %gate.6), channel_id=1, source_target_pairs={{0,12},{1,13},{2,14},{3,15},{4,8},{5,9},{6,10},{7,11},{8,4},{9,5},... | collective-permute-start | bytes 245768 | tf_op jit(solution)/shard_map/ppermute | solution.py:385
  16.2 15.4 %collective-permute-start.7 = (bf16[80,512]{1,0:T(8,128)(2,1)S(1)}, bf16[80,512]{1,0:T(8,128)(2,1)S(1)}, u32[]{:S(2)}, u32[]{:S(2)}) collective-permute-start(bf16[80,512]{1,0:T(8,128)(2,1)S(1)} %gate.6), channel_id=1, source_target_pairs={{0,8},{1,9},{2,10},{3,11},{4,12},{5,13},{6,14},{7,15},{8,0},{9,1},... | collective-permute-start | bytes 245768 | tf_op jit(solution)/shard_map/ppermute | solution.py:385
  16.2 15.4 %collective-permute-start.6 = (bf16[80,512]{1,0:T(8,128)(2,1)S(1)}, bf16[80,512]{1,0:T(8,128)(2,1)S(1)}, u32[]{:S(2)}, u32[]{:S(2)}) collective-permute-start(bf16[80,512]{1,0:T(8,128)(2,1)S(1)} %gate.6), channel_id=1, source_target_pairs={{0,4},{1,5},{2,6},{3,7},{4,0},{5,1},{6,2},{7,3},{8,12},{9,13},{10,... | collective-permute-start | bytes 245768 | tf_op jit(solution)/shard_map/ppermute | solution.py:385
  19.9 28.9 %copy-start = (f32[8,2048]{1,0:T(8,128)S(1)}, f32[8,2048]{1,0:T(8,128)}, u32[]{:S(2)}) copy-start(f32[8,2048]{1,0:T(8,128)} %rhs_ref.5) | copy-start | bytes 196612
  19.9 13.9 %collective-permute-start.4 = (bf16[384,512]{1,0:T(8,128)(2,1)S(1)}, bf16[384,512]{1,0:T(8,128)(2,1)S(1)}, u32[]{:S(2)}, u32[]{:S(2)}) collective-permute-start(bf16[384,512]{1,0:T(8,128)(2,1)S(1)} %gate.4.arrived_ref.refs_2_), channel_id=1, source_target_pairs={{0,1},{1,0},{2,3},{3,2},{4,5},{5,4},{6,7},{7,6},{8,9},{9,8},{10,11... | collective-permute-start | bytes 1179656 | tf_op jit(solution)/shard_map/ppermute | solution.py:385
  20.0 11.5 %collective-permute-start.3 = (bf16[384,512]{1,0:T(8,128)(2,1)S(1)}, bf16[384,512]{1,0:T(8,128)(2,1)S(1)}, u32[]{:S(2)}, u32[]{:S(2)}) collective-permute-start(bf16[384,512]{1,0:T(8,128)(2,1)S(1)} %gate.4.arrived_ref.refs_2_), channel_id=1, source_target_pairs={{0,2},{1,3},{2,0},{3,1},{4,6},{5,7},{6,4},{7,5},{8,10},{9,11},{10,... | collective-permute-start | bytes 1179656 | tf_op jit(solution)/shard_map/ppermute | solution.py:385
  31.6 2.3 %collective-permute-start.5 = (bf16[384,512]{1,0:T(8,128)(2,1)S(1)}, bf16[384,512]{1,0:T(8,128)(2,1)S(1)}, u32[]{:S(2)}, u32[]{:S(2)}) collective-permute-start(bf16[384,512]{1,0:T(8,128)(2,1)S(1)} %gate.5.refs_3_), channel_id=1, source_target_pairs={{0,1},{1,0},{2,3},{3,2},{4,5},{5,4},{6,7},{7,6},{8,9},{9,8},{10,11... | collective-permute-start | bytes 1179656 | tf_op jit(solution)/shard_map/ppermute | solution.py:385
  31.6 12.4 %collective-permute-start.11 = (bf16[320,512]{1,0:T(8,128)(2,1)S(1)}, bf16[320,512]{1,0:T(8,128)(2,1)S(1)}, u32[]{:S(2)}, u32[]{:S(2)}) collective-permute-start(bf16[320,512]{1,0:T(8,128)(2,1)S(1)} %gate.7.refs_0_), channel_id=1, source_target_pairs={{0,3},{1,2},{2,1},{3,0},{4,7},{5,6},{6,5},{7,4},{8,11},{9,10},{10,... | collective-permute-start | bytes 983048 | tf_op jit(solution)/shard_map/ppermute | solution.py:385
  33.3 10.7 %collective-permute-start.10 = (bf16[320,512]{1,0:T(8,128)(2,1)S(1)}, bf16[320,512]{1,0:T(8,128)(2,1)S(1)}, u32[]{:S(2)}, u32[]{:S(2)}) collective-permute-start(bf16[320,512]{1,0:T(8,128)(2,1)S(1)} %gate.7.refs_0_), channel_id=1, source_target_pairs={{0,1},{1,0},{2,3},{3,2},{4,5},{5,4},{6,7},{7,6},{8,9},{9,8},{10,11... | collective-permute-start | bytes 983048 | tf_op jit(solution)/shard_map/ppermute | solution.py:385
  33.3 15.5 %collective-permute-start.9 = (bf16[320,512]{1,0:T(8,128)(2,1)S(1)}, bf16[320,512]{1,0:T(8,128)(2,1)}, u32[]{:S(2)}, u32[]{:S(2)}) collective-permute-start(bf16[320,512]{1,0:T(8,128)(2,1)S(1)} %gate.7.refs_0_), channel_id=1, source_target_pairs={{0,2},{1,3},{2,0},{3,1},{4,6},{5,7},{6,4},{7,5},{8,10},{9,11},{10,... | collective-permute-start | bytes 983048 | tf_op jit(solution)/shard_map/ppermute | solution.py:385
  58.9 35.3 %collective-permute-start.14 = (bf16[1,8,2176]{2,1,0:T(8,128)(2,1)S(1)}, bf16[1,8,2176]{2,1,0:T(8,128)(2,1)S(1)}, u32[]{:S(2)}, u32[]{:S(2)}) collective-permute-start(bf16[1,8,2176]{2,1,0:T(8,128)(2,1)S(1)} %bitcast.5), channel_id=1, source_target_pairs={{0,12},{1,13},{2,14},{3,15},{4,8},{5,9},{6,10},{7,11},{8,4},{9,5},... | collective-permute-start | bytes 104456 | tf_op jit(solution)/shard_map/ppermute | solution.py:385
  91.2 5.0 %collective-permute-start.13 = (bf16[1,8,2176]{2,1,0:T(8,128)(2,1)S(1)}, bf16[1,8,2176]{2,1,0:T(8,128)(2,1)S(1)}, u32[]{:S(2)}, u32[]{:S(2)}) collective-permute-start(bf16[1,8,2176]{2,1,0:T(8,128)(2,1)S(1)} %bitcast.6), channel_id=1, source_target_pairs={{0,8},{1,9},{2,10},{3,11},{4,12},{5,13},{6,14},{7,15},{8,0},{9,1},... | collective-permute-start | bytes 104456 | tf_op jit(solution)/shard_map/ppermute | solution.py:385
  91.2 5.0 %collective-permute-start.12 = (bf16[1,8,2176]{2,1,0:T(8,128)(2,1)S(1)}, bf16[1,8,2176]{2,1,0:T(8,128)(2,1)S(1)}, u32[]{:S(2)}, u32[]{:S(2)}) collective-permute-start(bf16[1,8,2176]{2,1,0:T(8,128)(2,1)S(1)} %bitcast.7), channel_id=1, source_target_pairs={{0,4},{1,5},{2,6},{3,7},{4,0},{5,1},{6,2},{7,3},{8,12},{9,13},{10,... | collective-permute-start | bytes 104456 | tf_op jit(solution)/shard_map/ppermute | solution.py:385
  96.2 6.8 %collective-permute-start.15 = (bf16[4,8,2176]{2,1,0:T(8,128)(2,1)S(1)}, bf16[4,8,2176]{2,1,0:T(8,128)(2,1)S(1)}, u32[]{:S(2)}, u32[]{:S(2)}) collective-permute-start(bf16[4,8,2176]{2,1,0:T(8,128)(2,1)S(1)} %pad_maximum_fusion.2), channel_id=1, source_target_pairs={{0,2},{1,3},{2,0},{3,1},{4,6},{5,7},{6,4},{7,5},{8,10},{9,11},{10,... | collective-permute-start | bytes 417800 | tf_op jit(solution)/shard_map/ppermute | solution.py:385
  103.1 2.1 %collective-permute-start.16 = (bf16[8,8,2176]{2,1,0:T(8,128)(2,1)S(1)}, bf16[8,8,2176]{2,1,0:T(8,128)(2,1)S(1)}, u32[]{:S(2)}, u32[]{:S(2)}) collective-permute-start(bf16[8,8,2176]{2,1,0:T(8,128)(2,1)S(1)} %get-tuple-element.47), channel_id=1, source_target_pairs={{0,1},{1,0},{2,3},{3,2},{4,5},{5,4},{6,7},{7,6},{8,9},{9,8},{10,11... | collective-permute-start | bytes 835592 | tf_op jit(solution)/shard_map/ppermute | solution.py:385
  108.5 10.1 %collective-permute-start.19 = (f32[8,128]{1,0:T(8,128)S(1)}, f32[8,128]{1,0:T(8,128)S(1)}, u32[]{:S(2)}, u32[]{:S(2)}) collective-permute-start(f32[8,128]{1,0:T(8,128)S(1)} %get-tuple-element.41), channel_id=1, source_target_pairs={{0,12},{1,13},{2,14},{3,15},{4,8},{5,9},{6,10},{7,11},{8,4},{9,5},... | collective-permute-start | bytes 12296 | tf_op jit(solution)/shard_map/ppermute | solution.py:385
  117.0 4.5 %collective-permute-start.18 = (f32[8,128]{1,0:T(8,128)S(1)}, f32[8,128]{1,0:T(8,128)S(1)}, u32[]{:S(2)}, u32[]{:S(2)}) collective-permute-start(f32[8,128]{1,0:T(8,128)S(1)} %get-tuple-element.41), channel_id=1, source_target_pairs={{0,8},{1,9},{2,10},{3,11},{4,12},{5,13},{6,14},{7,15},{8,0},{9,1},... | collective-permute-start | bytes 12296 | tf_op jit(solution)/shard_map/ppermute | solution.py:385
  117.4 4.1 %collective-permute-start.17 = (f32[8,128]{1,0:T(8,128)S(1)}, f32[8,128]{1,0:T(8,128)S(1)}, u32[]{:S(2)}, u32[]{:S(2)}) collective-permute-start(f32[8,128]{1,0:T(8,128)S(1)} %get-tuple-element.41), channel_id=1, source_target_pairs={{0,4},{1,5},{2,6},{3,7},{4,0},{5,1},{6,2},{7,3},{8,12},{9,13},{10,... | collective-permute-start | bytes 12296 | tf_op jit(solution)/shard_map/ppermute | solution.py:385
  121.6 3.4 %collective-permute-start.22 = (f32[8,128]{1,0:T(8,128)S(1)}, f32[8,128]{1,0:T(8,128)S(1)}, u32[]{:S(2)}, u32[]{:S(2)}) collective-permute-start(f32[8,128]{1,0:T(8,128)S(1)} %add_add_fusion.1), channel_id=1, source_target_pairs={{0,3},{1,2},{2,1},{3,0},{4,7},{5,6},{6,5},{7,4},{8,11},{9,10},{10,... | collective-permute-start | bytes 12296 | tf_op jit(solution)/shard_map/ppermute | solution.py:385
  122.1 3.6 %collective-permute-start.21 = (f32[8,128]{1,0:T(8,128)S(1)}, f32[8,128]{1,0:T(8,128)S(1)}, u32[]{:S(2)}, u32[]{:S(2)}) collective-permute-start(f32[8,128]{1,0:T(8,128)S(1)} %add_add_fusion.1), channel_id=1, source_target_pairs={{0,2},{1,3},{2,0},{3,1},{4,6},{5,7},{6,4},{7,5},{8,10},{9,11},{10,... | collective-permute-start | bytes 12296 | tf_op jit(solution)/shard_map/ppermute | solution.py:385
  123.4 2.2 %collective-permute-start.20 = (f32[8,128]{1,0:T(8,128)S(1)}, f32[8,128]{1,0:T(8,128)S(1)}, u32[]{:S(2)}, u32[]{:S(2)}) collective-permute-start(f32[8,128]{1,0:T(8,128)S(1)} %add_add_fusion.1), channel_id=1, source_target_pairs={{0,1},{1,0},{2,3},{3,2},{4,5},{5,4},{6,7},{7,6},{8,9},{9,8},{10,11... | collective-permute-start | bytes 12296 | tf_op jit(solution)/shard_map/ppermute | solution.py:385
  (2 other events, 47.2 us)

commit v14 on v12

--- a/solution.py
+++ b/solution.py
@@ -15,8 +15,8 @@
 KDIM = 128
 ROWS = 512
 PARTS = 2
-COLS = 512
-SUB = 64
+PIECE = 256
+STRIP = 64
 FRONT = 3
 HELD = 4
 TAIL = 128
@@ -61,14 +61,25 @@
     return (jnp.exp2(19.0 * lax.log2(u)) * (1.0 - u)).astype(BF16)
 
 
-def tile_unit(left, right, vec, tile_ref):
-    dist = jnp.dot(left, right, preferred_element_type=F32)
-    parts = []
-    for sub in range(0, left.shape[0], SUB):
-        part = psi_power(dist[sub : sub + SUB])
-        tile_ref[sub : sub + SUB, :] = part
-        parts.append(part)
-    return jnp.dot(vec, jnp.concatenate(parts, axis=0), preferred_element_type=F32)
+def tile_unit(left, right, vec, tile_ref, ahead):
+    pieces = [slice(at, at + PIECE) for at in range(0, right.shape[1], PIECE)]
+    gram = lambda piece: jnp.dot(left, right[:, piece], preferred_element_type=F32)
+    product = lambda part: jnp.dot(vec, part, preferred_element_type=F32)
+    dists = [gram(piece) for piece in pieces[:ahead]]
+    parts, terms = [], []
+    for index, piece in enumerate(pieces):
+        if index + ahead < len(pieces):
+            dists.append(gram(pieces[index + ahead]))
+        dist = dists[index]
+        strips = []
+        for sub in range(0, left.shape[0], STRIP):
+            strips.append(psi_power(dist[sub : sub + STRIP]))
+            tile_ref[sub : sub + STRIP, piece] = strips[-1]
+        parts.append(jnp.concatenate(strips, axis=0))
+        if index >= ahead:
+            terms.append(product(parts[index - ahead]))
+    terms += [product(part) for part in parts[len(terms) :]]
+    return jnp.concatenate(terms, axis=1)
 
 
 def unpack(pay):
@@ -91,7 +102,7 @@
         def col_step(col, at):
             sum_ref[:, piece(col)] += tile_unit(
                 left_ref[piece(row), :], right_ref[:, piece(col)], vec_ref[:, piece(row)],
-                tile_ref.at[at],
+                tile_ref.at[at], 1,
             )
             save(at).start()
 
@@ -182,7 +193,7 @@
     return fetch
 
 
-def half_tiles(at_once, slots_ref, right_ref, fetch, front_ref, back_ref, sum_ref, left_ref, vec_ref, pay_ref, sem_ref):
+def half_tiles(ahead, slots_ref, right_ref, fetch, front_ref, back_ref, sum_ref, left_ref, vec_ref, pay_ref, sem_ref):
     slot, step = pl.program_id(0), pl.program_id(1)
 
     @pl.when((slot == 0) & (step == 0) & (slots_ref[0] > 0))
@@ -210,14 +221,7 @@
         for tile_ref, here in ((front_ref, slot < FRONT), (back_ref, slot >= FRONT)):
             @pl.when(here)
             def _():
-                def unit(index, carry):
-                    cols = pl.ds(pl.multiple_of(index * at_once, at_once), at_once)
-                    sum_ref[:, cols] += tile_unit(
-                        left, right_ref[:, cols], vec, tile_ref.at[0, :, cols]
-                    )
-                    return carry
-
-                lax.fori_loop(0, right_ref.shape[1] // at_once, unit, 0)
+                sum_ref[...] += tile_unit(left, right_ref[...], vec, tile_ref.at[0], ahead)
 
 
 def pair_zero_kernel(block_at, me_ref, right_ref, *refs):
@@ -248,7 +252,7 @@
 
     fetch = fetch_from(block_at, block_refs, slots_ref, pay_ref, sem_ref)
     half_tiles(
-        2 * COLS, slots_ref, right_ref, fetch, front_ref, back_ref, sum_ref, left_ref, vec_ref, pay_ref, sem_ref
+        1, slots_ref, right_ref, fetch, front_ref, back_ref, sum_ref, left_ref, vec_ref, pay_ref, sem_ref
     )
 
 
@@ -263,7 +267,7 @@
 
     fetch = fetch_from(block_at, block_refs, slots_ref, pay_ref, sem_ref)
     half_tiles(
-        4 * COLS, slots_ref, right_ref, fetch, front_ref, back_ref, image_ref, left_ref, vec_ref, pay_ref, sem_ref
+        0, slots_ref, right_ref, fetch, front_ref, back_ref, image_ref, left_ref, vec_ref, pay_ref, sem_ref
     )
 
     @pl.when((slot == pl.num_programs(0) - 1) & (step == pl.num_programs(1) - 1))

time: 126 us -> 128 us (1.016)
  Pallas kernels: 83.2 us -> 27.9 us
  starting transfers between devices: 24.9 us -> 71.6 us
  waiting for transfers between devices: 14.4 us -> 25.8 us
    ppermute x23, starting transfers between devices: 24.9 us -> 71.6 us  [swap(): return lax.ppermute(value, 'row', [(i, i ^ mask) for i in range(count)])]
    pallas_call x1, Pallas kernels: 28.7 us -> 4.94 us  [local(): pl.pallas_call(functools.partial(pair_zero_kernel, zero_at), grid_spec=pl...]
    pallas_call x1, Pallas kernels: 27.6 us -> 4.45 us  [local(): pl.pallas_call(functools.partial(pair_one_kernel, one_at), grid_spec=pltp...]
    ppermute x23, waiting for transfers between devices: 14.4 us -> 25.8 us  [swap(): return lax.ppermute(value, 'row', [(i, i ^ mask) for i in range(count)])]
    pallas_call x1, Pallas kernels: 10.3 us -> 1.91 us  [local(): pl.pallas_call(again_kernel, grid_spec=pltpu.PrefetchScalarGridSpec(num_s...]
  transfers between devices with their start and end apart: 23 -> 23, of which waited for: 6 -> 9; matrix products, arithmetic and copies ran while one was open for 0% -> 0% of each run, Pallas kernels for 35% -> 16%
where the time goes in v14:
time: 128 us
  starting transfers between devices  71.6 us (56%)
  Pallas kernels  27.9 us (22%)
  waiting for transfers between devices  25.8 us (20%)
    ppermute x23, starting transfers between devices, swap(): return lax.ppermute(value, 'row', [(i, i ^ mask) for i in range(count)])  71.6 us
    ppermute x23, waiting for transfers between devices, swap(): return lax.ppermute(value, 'row', [(i, i ^ mask) for i in range(count)])  25.8 us
    pallas_call x2, Pallas kernels, own_part(): pl.pallas_call(functools.partial(own_kernel, rows), in_specs=[vmem, vmem,...  9.62 us
    pallas_call x1, Pallas kernels, local(): pl.pallas_call(functools.partial(pair_zero_kernel, zero_at), grid_spec=pl...  4.94 us
    pallas_call x1, Pallas kernels, local(): pl.pallas_call(functools.partial(pair_one_kernel, one_at), grid_spec=pltp...  4.45 us
    pallas_call x2, Pallas kernels, local(): pl.pallas_call(functools.partial(own_again_kernel, blocks), in_specs=[any...  4.34 us
  transfers between devices with their start and end apart: 23, of which 9 were waited for; matrix products, arithmetic and copies ran while one was open for 0% of the time, Pallas kernels for 16%

profile of v14, /device:TPU:0, one launch (start us, length us, event | category | flops | bytes accessed | tf_op | source)
XLA Modules:
  0.0 128.1 jit_solution(8280682252362015200)
XLA Ops:
  2.6 5.1 %collective-permute-start.2 = (bf16[96,512]{1,0:T(8,128)(2,1)S(1)}, bf16[96,512]{1,0:T(8,128)(2,1)S(1)}, u32[]{:S(2)}, u32[]{:S(2)}) collective-permute-start(bf16[96,512]{1,0:T(8,128)(2,1)S(1)} %get-tuple-element.26), channel_id=1, source_target_pairs={{0,12},{1,13},{2,14},{3,15},{4,8},{5,9},{6,10},{7,11},{8,4},{9,5},... | collective-permute-start | bytes 294920 | tf_op jit(solution)/shard_map/ppermute | solution.py:380
  8.3 4.0 %own_tile_0.1 = (bf16[4,512,512]{2,1,0:T(8,128)(2,1)}, f32[8,2048]{1,0:T(8,128)S(1)}) custom-call(bf16[2048,128]{1,0:T(8,128)(2,1)S(1)} %get-tuple-element.23.left_ref, bf16[128,2048]{1,0:T(8,128)(2,1)S(1)} %get-tuple-element.22.right_ref.arrived_ref, bf16[8,2048]{1,0:T(8,128)(2,1)S(1)} %get-tuple-element.24.vec_ref, ...), custom_call_target="tpu_custom_call" | custom-call | flops 5000000000 | bytes 2097152 | tf_op jit(solution)/shard_map/own_tile_0/pallas_call | solution.py:470
  12.3 3.8 %collective-permute-start.8 = (bf16[80,512]{1,0:T(8,128)(2,1)S(1)}, bf16[80,512]{1,0:T(8,128)(2,1)S(1)}, u32[]{:S(2)}, u32[]{:S(2)}) collective-permute-start(bf16[80,512]{1,0:T(8,128)(2,1)S(1)} %gate.6), channel_id=1, source_target_pairs={{0,12},{1,13},{2,14},{3,15},{4,8},{5,9},{6,10},{7,11},{8,4},{9,5},... | collective-permute-start | bytes 245768 | tf_op jit(solution)/shard_map/ppermute | solution.py:380
  16.8 3.1 %collective-permute-done.1 = bf16[96,512]{1,0:T(8,128)(2,1)S(1)} collective-permute-done((bf16[96,512]{1,0:T(8,128)(2,1)S(1)}, bf16[96,512]{1,0:T(8,128)(2,1)S(1)}, u32[]{:S(2)}, u32[]{:S(2)}) %collective-permute-start.1) | collective-permute-done | bytes 98336 | tf_op jit(solution)/shard_map/ppermute | solution.py:380
  20.0 1.6 %collective-permute-start.3 = (bf16[384,512]{1,0:T(8,128)(2,1)S(1)}, bf16[384,512]{1,0:T(8,128)(2,1)S(1)}, u32[]{:S(2)}, u32[]{:S(2)}) collective-permute-start(bf16[384,512]{1,0:T(8,128)(2,1)S(1)} %gate.4.arrived_ref.refs_2_), channel_id=1, source_target_pairs={{0,2},{1,3},{2,0},{3,1},{4,6},{5,7},{6,4},{7,5},{8,10},{9,11},{10,... | collective-permute-start | bytes 1179656 | tf_op jit(solution)/shard_map/ppermute | solution.py:380
  21.6 5.6 %own_tile_1.1 = (bf16[6,512,512]{2,1,0:T(8,128)(2,1)}, f32[8,2048]{1,0:T(8,128)S(1)}) custom-call(bf16[2048,128]{1,0:T(8,128)(2,1)S(1)} %get-tuple-element.23.left_ref, bf16[128,2048]{1,0:T(8,128)(2,1)S(1)} %get-tuple-element.22.right_ref.arrived_ref, bf16[8,2048]{1,0:T(8,128)(2,1)S(1)} %get-tuple-element.24.vec_ref, ...), custom_call_target="tpu_custom_call" | custom-call | flops 5000000000 | bytes 3145728 | tf_op jit(solution)/shard_map/own_tile_1/pallas_call | solution.py:470
  27.2 4.3 %collective-permute-done.3.refs_0_ = bf16[384,512]{1,0:T(8,128)(2,1)S(1)} collective-permute-done((bf16[384,512]{1,0:T(8,128)(2,1)S(1)}, bf16[384,512]{1,0:T(8,128)(2,1)S(1)}, u32[]{:S(2)}, u32[]{:S(2)}) %collective-permute-start.3) | collective-permute-done | bytes 393248 | tf_op jit(solution)/shard_map/ppermute | solution.py:380
  31.6 1.7 %collective-permute-start.11 = (bf16[320,512]{1,0:T(8,128)(2,1)S(1)}, bf16[320,512]{1,0:T(8,128)(2,1)S(1)}, u32[]{:S(2)}, u32[]{:S(2)}) collective-permute-start(bf16[320,512]{1,0:T(8,128)(2,1)S(1)} %gate.7.refs_0_), channel_id=1, source_target_pairs={{0,3},{1,2},{2,1},{3,0},{4,7},{5,6},{6,5},{7,4},{8,11},{9,10},{10,... | collective-permute-start | bytes 983048 | tf_op jit(solution)/shard_map/ppermute | solution.py:380
  33.9 4.9 %pair_zero.1 = (bf16[3,1024,2048]{2,1,0:T(8,128)(2,1)S(1)}, bf16[2,1024,2048]{2,1,0:T(8,128)(2,1)}, f32[8,2048]{1,0:T(8,128)S(1)}, s32[7]{0:T(128)S(1)}) custom-call(s32[1]{0:T(128)} %bitcast.me_ref, bf16[128,2048]{1,0:T(8,128)(2,1)S(1)} %get-tuple-element.22.right_ref.arrived_ref, f32[8,2048]{1,0:T(8,128)S(1)} %get-tuple-element.25.refs_1_.refs_0_, ...), custom_call_target="tpu_custom_call" | custom-call | tf_op jit(solution)/shard_map/pair_zero/pallas_call | solution.py:529
  38.8 2.6 %collective-permute-done.11.refs_3_ = bf16[320,512]{1,0:T(8,128)(2,1)S(1)} collective-permute-done((bf16[320,512]{1,0:T(8,128)(2,1)S(1)}, bf16[320,512]{1,0:T(8,128)(2,1)S(1)}, u32[]{:S(2)}, u32[]{:S(2)}) %collective-permute-start.11) | collective-permute-done | bytes 327712 | tf_op jit(solution)/shard_map/ppermute | solution.py:380
  41.4 7.5 %collective-permute-done.9.refs_1_ = bf16[320,512]{1,0:T(8,128)(2,1)} collective-permute-done((bf16[320,512]{1,0:T(8,128)(2,1)S(1)}, bf16[320,512]{1,0:T(8,128)(2,1)}, u32[]{:S(2)}, u32[]{:S(2)}) %collective-permute-start.9) | collective-permute-done | bytes 327712 | tf_op jit(solution)/shard_map/ppermute | solution.py:380
  48.9 4.4 %pair_one.1 = (bf16[3,1024,2048]{2,1,0:T(8,128)(2,1)S(1)}, bf16[2,1024,2048]{2,1,0:T(8,128)(2,1)}, f32[8,2048]{1,0:T(8,128)S(1)}, bf16[8,2176]{1,0:T(8,128)(2,1)S(1)}) custom-call(s32[7]{0:T(128)S(1)} %get-tuple-element.28.slots_ref, bf16[128,2048]{1,0:T(8,128)(2,1)S(1)} %get-tuple-element.22.right_ref.arrived_ref, ...), custom_call_target="tpu_custom_call" | custom-call | tf_op jit(solution)/shard_map/pair_one/pallas_call | solution.py:549
  54.0 39.0 %collective-permute-start.13 = (bf16[1,8,2176]{2,1,0:T(8,128)(2,1)S(1)}, bf16[1,8,2176]{2,1,0:T(8,128)(2,1)S(1)}, u32[]{:S(2)}, u32[]{:S(2)}) collective-permute-start(bf16[1,8,2176]{2,1,0:T(8,128)(2,1)S(1)} %bitcast.6), channel_id=1, source_target_pairs={{0,8},{1,9},{2,10},{3,11},{4,12},{5,13},{6,14},{7,15},{8,0},{9,1},... | collective-permute-start | bytes 104456 | tf_op jit(solution)/shard_map/ppermute | solution.py:380
  93.0 2.4 %own_again_1.1.refs_1_ = f32[8,2048]{1,0:T(8,128)S(1)} custom-call(bf16[6,512,512]{2,1,0:T(8,128)(2,1)} %get-tuple-element.38.in_ref, bf16[8,2176]{1,0:T(8,128)(2,1)S(1)} %get-tuple-element.35.vec_ref), custom_call_target="tpu_custom_call" | custom-call | flops 5000000000 | bytes 3145728 | tf_op jit(solution)/shard_map/own_again_1/pallas_call | solution.py:573
  95.4 1.5 %collective-permute-done.12 = bf16[1,8,2176]{2,1,0:T(8,128)(2,1)S(1)} collective-permute-done((bf16[1,8,2176]{2,1,0:T(8,128)(2,1)S(1)}, bf16[1,8,2176]{2,1,0:T(8,128)(2,1)S(1)}, u32[]{:S(2)}, u32[]{:S(2)}) %collective-permute-start.12) | collective-permute-done | bytes 34848 | tf_op jit(solution)/shard_map/ppermute | solution.py:380
  97.0 3.9 %collective-permute-start.15 = (bf16[4,8,2176]{2,1,0:T(8,128)(2,1)S(1)}, bf16[4,8,2176]{2,1,0:T(8,128)(2,1)S(1)}, u32[]{:S(2)}, u32[]{:S(2)}) collective-permute-start(bf16[4,8,2176]{2,1,0:T(8,128)(2,1)S(1)} %pad_maximum_fusion.2), channel_id=1, source_target_pairs={{0,2},{1,3},{2,0},{3,1},{4,6},{5,7},{6,4},{7,5},{8,10},{9,11},{10,... | collective-permute-start | bytes 417800 | tf_op jit(solution)/shard_map/ppermute | solution.py:380
  100.9 3.0 %collective-permute-done.15 = bf16[4,8,2176]{2,1,0:T(8,128)(2,1)S(1)} collective-permute-done((bf16[4,8,2176]{2,1,0:T(8,128)(2,1)S(1)}, bf16[4,8,2176]{2,1,0:T(8,128)(2,1)S(1)}, u32[]{:S(2)}, u32[]{:S(2)}) %collective-permute-start.15) | collective-permute-done | bytes 139296 | tf_op jit(solution)/shard_map/ppermute | solution.py:380
  104.0 2.0 %own_again_0.1.refs_0_ = f32[8,2048]{1,0:T(8,128)S(1)} custom-call(bf16[4,512,512]{2,1,0:T(8,128)(2,1)} %get-tuple-element.37.in_ref, bf16[8,2176]{1,0:T(8,128)(2,1)S(1)} %get-tuple-element.35.vec_ref), custom_call_target="tpu_custom_call" | custom-call | flops 5000000000 | bytes 2097152 | tf_op jit(solution)/shard_map/own_again_0/pallas_call | solution.py:573
  106.1 1.9 %pair_again.1 = (f32[32,2048]{1,0:T(8,128)S(1)}, f32[8,128]{1,0:T(8,128)S(1)}, f32[8,128]{1,0:T(8,128)S(1)}) custom-call(s32[7]{0:T(128)S(1)} %get-tuple-element.28.slots_ref, bf16[3,1024,2048]{2,1,0:T(8,128)(2,1)S(1)} %get-tuple-element.29.front_zero_ref, bf16[3,1024,2048]{2,1,0:T(8,128)(2,1)S(1)} %get-tuple-element.32.front_one_ref, ...), custom_call_target="tpu_custom_call" | custom-call | tf_op jit(solution)/shard_map/pair_again/pallas_call | solution.py:591
  108.0 2.0 %collective-permute-start.19 = (f32[8,128]{1,0:T(8,128)S(1)}, f32[8,128]{1,0:T(8,128)S(1)}, u32[]{:S(2)}, u32[]{:S(2)}) collective-permute-start(f32[8,128]{1,0:T(8,128)S(1)} %get-tuple-element.41), channel_id=1, source_target_pairs={{0,12},{1,13},{2,14},{3,15},{4,8},{5,9},{6,10},{7,11},{8,4},{9,5},... | collective-permute-start | bytes 12296 | tf_op jit(solution)/shard_map/ppermute | solution.py:380
  110.0 8.3 %collective-permute-start.18 = (f32[8,128]{1,0:T(8,128)S(1)}, f32[8,128]{1,0:T(8,128)S(1)}, u32[]{:S(2)}, u32[]{:S(2)}) collective-permute-start(f32[8,128]{1,0:T(8,128)S(1)} %get-tuple-element.41), channel_id=1, source_target_pairs={{0,8},{1,9},{2,10},{3,11},{4,12},{5,13},{6,14},{7,15},{8,0},{9,1},... | collective-permute-start | bytes 12296 | tf_op jit(solution)/shard_map/ppermute | solution.py:380
  119.9 2.0 %collective-permute-done.17 = f32[8,128]{1,0:T(8,128)S(1)} collective-permute-done((f32[8,128]{1,0:T(8,128)S(1)}, f32[8,128]{1,0:T(8,128)S(1)}, u32[]{:S(2)}, u32[]{:S(2)}) %collective-permute-start.17) | collective-permute-done | bytes 4128 | tf_op jit(solution)/shard_map/ppermute | solution.py:380
  122.0 1.5 %collective-permute-start.22 = (f32[8,128]{1,0:T(8,128)S(1)}, f32[8,128]{1,0:T(8,128)S(1)}, u32[]{:S(2)}, u32[]{:S(2)}) collective-permute-start(f32[8,128]{1,0:T(8,128)S(1)} %add_add_fusion.1), channel_id=1, source_target_pairs={{0,3},{1,2},{2,1},{3,0},{4,7},{5,6},{6,5},{7,4},{8,11},{9,10},{10,... | collective-permute-start | bytes 12296 | tf_op jit(solution)/shard_map/ppermute | solution.py:380
  124.9 1.5 %curve_order.1 = f32[32,2048]{1,0:T(8,128)S(1)} custom-call(f32[32,2048]{1,0:T(8,128)S(1)} %get-tuple-element.40.rows_ref, s32[1,2048]{1,0:T(1,128)S(1)} %copy-done.2), custom_call_target="tpu_custom_call" | custom-call | tf_op jit(solution)/shard_map/curve_order/pallas_call | solution.py:629
  (55 shorter events, 9.5 us)
Async XLA Ops:
  2.6 13.6 %collective-permute-start.2 = (bf16[96,512]{1,0:T(8,128)(2,1)S(1)}, bf16[96,512]{1,0:T(8,128)(2,1)S(1)}, u32[]{:S(2)}, u32[]{:S(2)}) collective-permute-start(bf16[96,512]{1,0:T(8,128)(2,1)S(1)} %get-tuple-element.26), channel_id=1, source_target_pairs={{0,12},{1,13},{2,14},{3,15},{4,8},{5,9},{6,10},{7,11},{8,4},{9,5},... | collective-permute-start | bytes 294920 | tf_op jit(solution)/shard_map/ppermute | solution.py:380
  7.7 12.2 %collective-permute-start.1 = (bf16[96,512]{1,0:T(8,128)(2,1)S(1)}, bf16[96,512]{1,0:T(8,128)(2,1)S(1)}, u32[]{:S(2)}, u32[]{:S(2)}) collective-permute-start(bf16[96,512]{1,0:T(8,128)(2,1)S(1)} %get-tuple-element.26), channel_id=1, source_target_pairs={{0,8},{1,9},{2,10},{3,11},{4,12},{5,13},{6,14},{7,15},{8,0},{9,1},... | collective-permute-start | bytes 294920 | tf_op jit(solution)/shard_map/ppermute | solution.py:380
  7.7 12.2 %collective-permute-start = (bf16[96,512]{1,0:T(8,128)(2,1)S(1)}, bf16[96,512]{1,0:T(8,128)(2,1)S(1)}, u32[]{:S(2)}, u32[]{:S(2)}) collective-permute-start(bf16[96,512]{1,0:T(8,128)(2,1)S(1)} %get-tuple-element.26), channel_id=1, source_target_pairs={{0,4},{1,5},{2,6},{3,7},{4,0},{5,1},{6,2},{7,3},{8,12},{9,13},{10,... | collective-permute-start | bytes 294920 | tf_op jit(solution)/shard_map/ppermute | solution.py:380
  12.3 19.2 %collective-permute-start.8 = (bf16[80,512]{1,0:T(8,128)(2,1)S(1)}, bf16[80,512]{1,0:T(8,128)(2,1)S(1)}, u32[]{:S(2)}, u32[]{:S(2)}) collective-permute-start(bf16[80,512]{1,0:T(8,128)(2,1)S(1)} %gate.6), channel_id=1, source_target_pairs={{0,12},{1,13},{2,14},{3,15},{4,8},{5,9},{6,10},{7,11},{8,4},{9,5},... | collective-permute-start | bytes 245768 | tf_op jit(solution)/shard_map/ppermute | solution.py:380
  16.1 15.4 %collective-permute-start.7 = (bf16[80,512]{1,0:T(8,128)(2,1)S(1)}, bf16[80,512]{1,0:T(8,128)(2,1)S(1)}, u32[]{:S(2)}, u32[]{:S(2)}) collective-permute-start(bf16[80,512]{1,0:T(8,128)(2,1)S(1)} %gate.6), channel_id=1, source_target_pairs={{0,8},{1,9},{2,10},{3,11},{4,12},{5,13},{6,14},{7,15},{8,0},{9,1},... | collective-permute-start | bytes 245768 | tf_op jit(solution)/shard_map/ppermute | solution.py:380
  16.2 15.4 %collective-permute-start.6 = (bf16[80,512]{1,0:T(8,128)(2,1)S(1)}, bf16[80,512]{1,0:T(8,128)(2,1)S(1)}, u32[]{:S(2)}, u32[]{:S(2)}) collective-permute-start(bf16[80,512]{1,0:T(8,128)(2,1)S(1)} %gate.6), channel_id=1, source_target_pairs={{0,4},{1,5},{2,6},{3,7},{4,0},{5,1},{6,2},{7,3},{8,12},{9,13},{10,... | collective-permute-start | bytes 245768 | tf_op jit(solution)/shard_map/ppermute | solution.py:380
  19.9 28.9 %copy-start = (f32[8,2048]{1,0:T(8,128)S(1)}, f32[8,2048]{1,0:T(8,128)}, u32[]{:S(2)}) copy-start(f32[8,2048]{1,0:T(8,128)} %rhs_ref.5) | copy-start | bytes 196612
  20.0 13.9 %collective-permute-start.4 = (bf16[384,512]{1,0:T(8,128)(2,1)S(1)}, bf16[384,512]{1,0:T(8,128)(2,1)S(1)}, u32[]{:S(2)}, u32[]{:S(2)}) collective-permute-start(bf16[384,512]{1,0:T(8,128)(2,1)S(1)} %gate.4.arrived_ref.refs_2_), channel_id=1, source_target_pairs={{0,1},{1,0},{2,3},{3,2},{4,5},{5,4},{6,7},{7,6},{8,9},{9,8},{10,11... | collective-permute-start | bytes 1179656 | tf_op jit(solution)/shard_map/ppermute | solution.py:380
  20.0 11.5 %collective-permute-start.3 = (bf16[384,512]{1,0:T(8,128)(2,1)S(1)}, bf16[384,512]{1,0:T(8,128)(2,1)S(1)}, u32[]{:S(2)}, u32[]{:S(2)}) collective-permute-start(bf16[384,512]{1,0:T(8,128)(2,1)S(1)} %gate.4.arrived_ref.refs_2_), channel_id=1, source_target_pairs={{0,2},{1,3},{2,0},{3,1},{4,6},{5,7},{6,4},{7,5},{8,10},{9,11},{10,... | collective-permute-start | bytes 1179656 | tf_op jit(solution)/shard_map/ppermute | solution.py:380
  31.6 2.3 %collective-permute-start.5 = (bf16[384,512]{1,0:T(8,128)(2,1)S(1)}, bf16[384,512]{1,0:T(8,128)(2,1)S(1)}, u32[]{:S(2)}, u32[]{:S(2)}) collective-permute-start(bf16[384,512]{1,0:T(8,128)(2,1)S(1)} %gate.5.refs_3_), channel_id=1, source_target_pairs={{0,1},{1,0},{2,3},{3,2},{4,5},{5,4},{6,7},{7,6},{8,9},{9,8},{10,11... | collective-permute-start | bytes 1179656 | tf_op jit(solution)/shard_map/ppermute | solution.py:380
  31.6 9.7 %collective-permute-start.11 = (bf16[320,512]{1,0:T(8,128)(2,1)S(1)}, bf16[320,512]{1,0:T(8,128)(2,1)S(1)}, u32[]{:S(2)}, u32[]{:S(2)}) collective-permute-start(bf16[320,512]{1,0:T(8,128)(2,1)S(1)} %gate.7.refs_0_), channel_id=1, source_target_pairs={{0,3},{1,2},{2,1},{3,0},{4,7},{5,6},{6,5},{7,4},{8,11},{9,10},{10,... | collective-permute-start | bytes 983048 | tf_op jit(solution)/shard_map/ppermute | solution.py:380
  33.3 8.1 %collective-permute-start.10 = (bf16[320,512]{1,0:T(8,128)(2,1)S(1)}, bf16[320,512]{1,0:T(8,128)(2,1)S(1)}, u32[]{:S(2)}, u32[]{:S(2)}) collective-permute-start(bf16[320,512]{1,0:T(8,128)(2,1)S(1)} %gate.7.refs_0_), channel_id=1, source_target_pairs={{0,1},{1,0},{2,3},{3,2},{4,5},{5,4},{6,7},{7,6},{8,9},{9,8},{10,11... | collective-permute-start | bytes 983048 | tf_op jit(solution)/shard_map/ppermute | solution.py:380
  33.3 15.5 %collective-permute-start.9 = (bf16[320,512]{1,0:T(8,128)(2,1)S(1)}, bf16[320,512]{1,0:T(8,128)(2,1)}, u32[]{:S(2)}, u32[]{:S(2)}) collective-permute-start(bf16[320,512]{1,0:T(8,128)(2,1)S(1)} %gate.7.refs_0_), channel_id=1, source_target_pairs={{0,2},{1,3},{2,0},{3,1},{4,6},{5,7},{6,4},{7,5},{8,10},{9,11},{10,... | collective-permute-start | bytes 983048 | tf_op jit(solution)/shard_map/ppermute | solution.py:380
  53.3 42.1 %collective-permute-start.14 = (bf16[1,8,2176]{2,1,0:T(8,128)(2,1)S(1)}, bf16[1,8,2176]{2,1,0:T(8,128)(2,1)S(1)}, u32[]{:S(2)}, u32[]{:S(2)}) collective-permute-start(bf16[1,8,2176]{2,1,0:T(8,128)(2,1)S(1)} %bitcast.5), channel_id=1, source_target_pairs={{0,12},{1,13},{2,14},{3,15},{4,8},{5,9},{6,10},{7,11},{8,4},{9,5},... | collective-permute-start | bytes 104456 | tf_op jit(solution)/shard_map/ppermute | solution.py:380
  54.0 41.4 %collective-permute-start.13 = (bf16[1,8,2176]{2,1,0:T(8,128)(2,1)S(1)}, bf16[1,8,2176]{2,1,0:T(8,128)(2,1)S(1)}, u32[]{:S(2)}, u32[]{:S(2)}) collective-permute-start(bf16[1,8,2176]{2,1,0:T(8,128)(2,1)S(1)} %bitcast.6), channel_id=1, source_target_pairs={{0,8},{1,9},{2,10},{3,11},{4,12},{5,13},{6,14},{7,15},{8,0},{9,1},... | collective-permute-start | bytes 104456 | tf_op jit(solution)/shard_map/ppermute | solution.py:380
  93.0 3.9 %collective-permute-start.12 = (bf16[1,8,2176]{2,1,0:T(8,128)(2,1)S(1)}, bf16[1,8,2176]{2,1,0:T(8,128)(2,1)S(1)}, u32[]{:S(2)}, u32[]{:S(2)}) collective-permute-start(bf16[1,8,2176]{2,1,0:T(8,128)(2,1)S(1)} %bitcast.7), channel_id=1, source_target_pairs={{0,4},{1,5},{2,6},{3,7},{4,0},{5,1},{6,2},{7,3},{8,12},{9,13},{10,... | collective-permute-start | bytes 104456 | tf_op jit(solution)/shard_map/ppermute | solution.py:380
  97.0 7.0 %collective-permute-start.15 = (bf16[4,8,2176]{2,1,0:T(8,128)(2,1)S(1)}, bf16[4,8,2176]{2,1,0:T(8,128)(2,1)S(1)}, u32[]{:S(2)}, u32[]{:S(2)}) collective-permute-start(bf16[4,8,2176]{2,1,0:T(8,128)(2,1)S(1)} %pad_maximum_fusion.2), channel_id=1, source_target_pairs={{0,2},{1,3},{2,0},{3,1},{4,6},{5,7},{6,4},{7,5},{8,10},{9,11},{10,... | collective-permute-start | bytes 417800 | tf_op jit(solution)/shard_map/ppermute | solution.py:380
  104.0 2.1 %collective-permute-start.16 = (bf16[8,8,2176]{2,1,0:T(8,128)(2,1)S(1)}, bf16[8,8,2176]{2,1,0:T(8,128)(2,1)S(1)}, u32[]{:S(2)}, u32[]{:S(2)}) collective-permute-start(bf16[8,8,2176]{2,1,0:T(8,128)(2,1)S(1)} %get-tuple-element.47), channel_id=1, source_target_pairs={{0,1},{1,0},{2,3},{3,2},{4,5},{5,4},{6,7},{7,6},{8,9},{9,8},{10,11... | collective-permute-start | bytes 835592 | tf_op jit(solution)/shard_map/ppermute | solution.py:380
  108.0 10.8 %collective-permute-start.19 = (f32[8,128]{1,0:T(8,128)S(1)}, f32[8,128]{1,0:T(8,128)S(1)}, u32[]{:S(2)}, u32[]{:S(2)}) collective-permute-start(f32[8,128]{1,0:T(8,128)S(1)} %get-tuple-element.41), channel_id=1, source_target_pairs={{0,12},{1,13},{2,14},{3,15},{4,8},{5,9},{6,10},{7,11},{8,4},{9,5},... | collective-permute-start | bytes 12296 | tf_op jit(solution)/shard_map/ppermute | solution.py:380
  110.0 9.9 %collective-permute-start.18 = (f32[8,128]{1,0:T(8,128)S(1)}, f32[8,128]{1,0:T(8,128)S(1)}, u32[]{:S(2)}, u32[]{:S(2)}) collective-permute-start(f32[8,128]{1,0:T(8,128)S(1)} %get-tuple-element.41), channel_id=1, source_target_pairs={{0,8},{1,9},{2,10},{3,11},{4,12},{5,13},{6,14},{7,15},{8,0},{9,1},... | collective-permute-start | bytes 12296 | tf_op jit(solution)/shard_map/ppermute | solution.py:380
  118.3 3.6 %collective-permute-start.17 = (f32[8,128]{1,0:T(8,128)S(1)}, f32[8,128]{1,0:T(8,128)S(1)}, u32[]{:S(2)}, u32[]{:S(2)}) collective-permute-start(f32[8,128]{1,0:T(8,128)S(1)} %get-tuple-element.41), channel_id=1, source_target_pairs={{0,4},{1,5},{2,6},{3,7},{4,0},{5,1},{6,2},{7,3},{8,12},{9,13},{10,... | collective-permute-start | bytes 12296 | tf_op jit(solution)/shard_map/ppermute | solution.py:380
  122.0 4.4 %collective-permute-start.22 = (f32[8,128]{1,0:T(8,128)S(1)}, f32[8,128]{1,0:T(8,128)S(1)}, u32[]{:S(2)}, u32[]{:S(2)}) collective-permute-start(f32[8,128]{1,0:T(8,128)S(1)} %add_add_fusion.1), channel_id=1, source_target_pairs={{0,3},{1,2},{2,1},{3,0},{4,7},{5,6},{6,5},{7,4},{8,11},{9,10},{10,... | collective-permute-start | bytes 12296 | tf_op jit(solution)/shard_map/ppermute | solution.py:380
  123.5 3.6 %collective-permute-start.21 = (f32[8,128]{1,0:T(8,128)S(1)}, f32[8,128]{1,0:T(8,128)S(1)}, u32[]{:S(2)}, u32[]{:S(2)}) collective-permute-start(f32[8,128]{1,0:T(8,128)S(1)} %add_add_fusion.1), channel_id=1, source_target_pairs={{0,2},{1,3},{2,0},{3,1},{4,6},{5,7},{6,4},{7,5},{8,10},{9,11},{10,... | collective-permute-start | bytes 12296 | tf_op jit(solution)/shard_map/ppermute | solution.py:380
  124.9 2.2 %collective-permute-start.20 = (f32[8,128]{1,0:T(8,128)S(1)}, f32[8,128]{1,0:T(8,128)S(1)}, u32[]{:S(2)}, u32[]{:S(2)}) collective-permute-start(f32[8,128]{1,0:T(8,128)S(1)} %add_add_fusion.1), channel_id=1, source_target_pairs={{0,1},{1,0},{2,3},{3,2},{4,5},{5,4},{6,7},{7,6},{8,9},{9,8},{10,11... | collective-permute-start | bytes 12296 | tf_op jit(solution)/shard_map/ppermute | solution.py:380
  (2 other events, 47.8 us)

commit v15 on v14

--- a/solution.py
+++ b/solution.py
@@ -61,24 +61,41 @@
     return (jnp.exp2(19.0 * lax.log2(u)) * (1.0 - u)).astype(BF16)
 
 
-def tile_unit(left, right, vec, tile_ref, ahead):
+def tile_unit(left, right, vec, tile_ref, cuts):
+    rows = left.shape[0]
     pieces = [slice(at, at + PIECE) for at in range(0, right.shape[1], PIECE)]
-    gram = lambda piece: jnp.dot(left, right[:, piece], preferred_element_type=F32)
-    product = lambda part: jnp.dot(vec, part, preferred_element_type=F32)
-    dists = [gram(piece) for piece in pieces[:ahead]]
-    parts, terms = [], []
+    part = rows // cuts
+    strips = part // STRIP
+
+    def gram(piece, cut):
+        at = slice(cut * part, (cut + 1) * part)
+        return jnp.dot(left[at], right[:, piece], preferred_element_type=F32)
+
+    def product(done, cut):
+        at = slice(cut * part, (cut + 1) * part)
+        return jnp.dot(
+            vec[:, at], jnp.concatenate(done[cut], axis=0), preferred_element_type=F32
+        )
+
+    dists = [gram(pieces[0], cut) for cut in range(cuts)]
+    before, terms = None, []
     for index, piece in enumerate(pieces):
-        if index + ahead < len(pieces):
-            dists.append(gram(pieces[index + ahead]))
-        dist = dists[index]
-        strips = []
-        for sub in range(0, left.shape[0], STRIP):
-            strips.append(psi_power(dist[sub : sub + STRIP]))
-            tile_ref[sub : sub + STRIP, piece] = strips[-1]
-        parts.append(jnp.concatenate(strips, axis=0))
-        if index >= ahead:
-            terms.append(product(parts[index - ahead]))
-    terms += [product(part) for part in parts[len(terms) :]]
+        following, done, term = [], [], 0.0
+        for cut in range(cuts):
+            if index + 1 < len(pieces):
+                following.append(gram(pieces[index + 1], cut))
+            done.append([])
+            for strip in range(strips):
+                at = strip * STRIP
+                values = psi_power(dists[cut][at : at + STRIP])
+                tile_ref[cut * part + at : cut * part + at + STRIP, piece] = values
+                done[cut].append(values)
+                if before is not None and strip == strips // 2:
+                    term = term + product(before, cut)
+        if before is not None:
+            terms.append(term)
+        dists, before = following, done
+    terms.append(sum(product(before, cut) for cut in range(cuts)))
     return jnp.concatenate(terms, axis=1)
 
 
@@ -193,7 +210,7 @@
     return fetch
 
 
-def half_tiles(ahead, slots_ref, right_ref, fetch, front_ref, back_ref, sum_ref, left_ref, vec_ref, pay_ref, sem_ref):
+def half_tiles(cuts, slots_ref, right_ref, fetch, front_ref, back_ref, sum_ref, left_ref, vec_ref, pay_ref, sem_ref):
     slot, step = pl.program_id(0), pl.program_id(1)
 
     @pl.when((slot == 0) & (step == 0) & (slots_ref[0] > 0))
@@ -221,7 +238,7 @@
         for tile_ref, here in ((front_ref, slot < FRONT), (back_ref, slot >= FRONT)):
             @pl.when(here)
             def _():
-                sum_ref[...] += tile_unit(left, right_ref[...], vec, tile_ref.at[0], ahead)
+                sum_ref[...] += tile_unit(left, right_ref[...], vec, tile_ref.at[0], cuts)
 
 
 def pair_zero_kernel(block_at, me_ref, right_ref, *refs):
@@ -252,7 +269,7 @@
 
     fetch = fetch_from(block_at, block_refs, slots_ref, pay_ref, sem_ref)
     half_tiles(
-        1, slots_ref, right_ref, fetch, front_ref, back_ref, sum_ref, left_ref, vec_ref, pay_ref, sem_ref
+        2, slots_ref, right_ref, fetch, front_ref, back_ref, sum_ref, left_ref, vec_ref, pay_ref, sem_ref
     )
 
 
@@ -267,7 +284,7 @@
 
     fetch = fetch_from(block_at, block_refs, slots_ref, pay_ref, sem_ref)
     half_tiles(
-        0, slots_ref, right_ref, fetch, front_ref, back_ref, image_ref, left_ref, vec_ref, pay_ref, sem_ref
+        1, slots_ref, right_ref, fetch, front_ref, back_ref, image_ref, left_ref, vec_ref, pay_ref, sem_ref
     )
 
     @pl.when((slot == pl.num_programs(0) - 1) & (step == pl.num_programs(1) - 1))

time: 128 us -> 120 us (0.938)
  Pallas kernels: 27.9 us -> 77.9 us
  starting transfers between devices: 71.6 us -> 26.2 us
  waiting for transfers between devices: 25.8 us -> 13.6 us
    ppermute x23, starting transfers between devices: 71.6 us -> 26.2 us  [swap(): return lax.ppermute(value, 'row', [(i, i ^ mask) for i in range(count)])]
    pallas_call x1, Pallas kernels: 4.94 us -> 26.8 us  [local(): pl.pallas_call(functools.partial(pair_zero_kernel, zero_at), grid_spec=pl...]
    pallas_call x1, Pallas kernels: 4.45 us -> 24.4 us  [local(): pl.pallas_call(functools.partial(pair_one_kernel, one_at), grid_spec=pltp...]
    ppermute x23, waiting for transfers between devices: 25.8 us -> 13.6 us  [swap(): return lax.ppermute(value, 'row', [(i, i ^ mask) for i in range(count)])]
    pallas_call x1, Pallas kernels: 1.91 us -> 10.1 us  [local(): pl.pallas_call(again_kernel, grid_spec=pltpu.PrefetchScalarGridSpec(num_s...]
  transfers between devices with their start and end apart: 23 -> 23, of which waited for: 9 -> 6; matrix products, arithmetic and copies ran while one was open for 0% -> 0% of each run, Pallas kernels for 16% -> 35%
where the time goes in v15:
time: 120 us; the launch traced here: 121 us
  Pallas kernels  77.9 us (65%)
  starting transfers between devices  26.2 us (22%)
  waiting for transfers between devices  13.6 us (11%)
    pallas_call x1, Pallas kernels, local(): pl.pallas_call(functools.partial(pair_zero_kernel, zero_at), grid_spec=pl...  26.8 us
    ppermute x23, starting transfers between devices, swap(): return lax.ppermute(value, 'row', [(i, i ^ mask) for i in range(count)])  26.2 us
    pallas_call x1, Pallas kernels, local(): pl.pallas_call(functools.partial(pair_one_kernel, one_at), grid_spec=pltp...  24.4 us
    ppermute x23, waiting for transfers between devices, swap(): return lax.ppermute(value, 'row', [(i, i ^ mask) for i in range(count)])  13.6 us
    pallas_call x1, Pallas kernels, local(): pl.pallas_call(again_kernel, grid_spec=pltpu.PrefetchScalarGridSpec(num_s...  10.1 us
    pallas_call x2, Pallas kernels, own_part(): pl.pallas_call(functools.partial(own_kernel, rows), in_specs=[vmem, vmem,...  9.62 us
    pallas_call x2, Pallas kernels, local(): pl.pallas_call(functools.partial(own_again_kernel, blocks), in_specs=[any...  4.34 us
  transfers between devices with their start and end apart: 23, of which 6 were waited for; matrix products, arithmetic and copies ran while one was open for 0% of the time, Pallas kernels for 35%

profile of v15, /device:TPU:0, one launch (start us, length us, event | category | flops | bytes accessed | tf_op | source)
XLA Modules:
  0.0 120.6 jit_solution(12472955161709734532)
XLA Ops:
  1.4 1.2 payload.1
  2.6 5.1 %collective-permute-start.2 = (bf16[96,512]{1,0:T(8,128)(2,1)S(1)}, bf16[96,512]{1,0:T(8,128)(2,1)S(1)}, u32[]{:S(2)}, u32[]{:S(2)}) collective-permute-start(bf16[96,512]{1,0:T(8,128)(2,1)S(1)} %get-tuple-element.26), channel_id=1, source_target_pairs={{0,12},{1,13},{2,14},{3,15},{4,8},{5,9},{6,10},{7,11},{8,4},{9,5},... | collective-permute-start | bytes 294920 | tf_op jit(solution)/shard_map/ppermute | solution.py:397
  8.3 4.0 %own_tile_0.1 = (bf16[4,512,512]{2,1,0:T(8,128)(2,1)}, f32[8,2048]{1,0:T(8,128)S(1)}) custom-call(bf16[2048,128]{1,0:T(8,128)(2,1)S(1)} %get-tuple-element.23.left_ref, bf16[128,2048]{1,0:T(8,128)(2,1)S(1)} %get-tuple-element.22.right_ref.arrived_ref, bf16[8,2048]{1,0:T(8,128)(2,1)S(1)} %get-tuple-element.24.vec_ref, ...), custom_call_target="tpu_custom_call" | custom-call | flops 5000000000 | bytes 2097152 | tf_op jit(solution)/shard_map/own_tile_0/pallas_call | solution.py:487
  12.3 3.8 %collective-permute-start.8 = (bf16[80,512]{1,0:T(8,128)(2,1)S(1)}, bf16[80,512]{1,0:T(8,128)(2,1)S(1)}, u32[]{:S(2)}, u32[]{:S(2)}) collective-permute-start(bf16[80,512]{1,0:T(8,128)(2,1)S(1)} %gate.6), channel_id=1, source_target_pairs={{0,12},{1,13},{2,14},{3,15},{4,8},{5,9},{6,10},{7,11},{8,4},{9,5},... | collective-permute-start | bytes 245768 | tf_op jit(solution)/shard_map/ppermute | solution.py:397
  16.8 3.1 %collective-permute-done.1 = bf16[96,512]{1,0:T(8,128)(2,1)S(1)} collective-permute-done((bf16[96,512]{1,0:T(8,128)(2,1)S(1)}, bf16[96,512]{1,0:T(8,128)(2,1)S(1)}, u32[]{:S(2)}, u32[]{:S(2)}) %collective-permute-start.1) | collective-permute-done | bytes 98336 | tf_op jit(solution)/shard_map/ppermute | solution.py:397
  20.0 1.6 %collective-permute-start.3 = (bf16[384,512]{1,0:T(8,128)(2,1)S(1)}, bf16[384,512]{1,0:T(8,128)(2,1)S(1)}, u32[]{:S(2)}, u32[]{:S(2)}) collective-permute-start(bf16[384,512]{1,0:T(8,128)(2,1)S(1)} %gate.4.arrived_ref.refs_2_), channel_id=1, source_target_pairs={{0,2},{1,3},{2,0},{3,1},{4,6},{5,7},{6,4},{7,5},{8,10},{9,11},{10,... | collective-permute-start | bytes 1179656 | tf_op jit(solution)/shard_map/ppermute | solution.py:397
  21.6 5.6 %own_tile_1.1 = (bf16[6,512,512]{2,1,0:T(8,128)(2,1)}, f32[8,2048]{1,0:T(8,128)S(1)}) custom-call(bf16[2048,128]{1,0:T(8,128)(2,1)S(1)} %get-tuple-element.23.left_ref, bf16[128,2048]{1,0:T(8,128)(2,1)S(1)} %get-tuple-element.22.right_ref.arrived_ref, bf16[8,2048]{1,0:T(8,128)(2,1)S(1)} %get-tuple-element.24.vec_ref, ...), custom_call_target="tpu_custom_call" | custom-call | flops 5000000000 | bytes 3145728 | tf_op jit(solution)/shard_map/own_tile_1/pallas_call | solution.py:487
  27.2 4.3 %collective-permute-done.3.refs_0_ = bf16[384,512]{1,0:T(8,128)(2,1)S(1)} collective-permute-done((bf16[384,512]{1,0:T(8,128)(2,1)S(1)}, bf16[384,512]{1,0:T(8,128)(2,1)S(1)}, u32[]{:S(2)}, u32[]{:S(2)}) %collective-permute-start.3) | collective-permute-done | bytes 393248 | tf_op jit(solution)/shard_map/ppermute | solution.py:397
  31.6 1.7 %collective-permute-start.11 = (bf16[320,512]{1,0:T(8,128)(2,1)S(1)}, bf16[320,512]{1,0:T(8,128)(2,1)S(1)}, u32[]{:S(2)}, u32[]{:S(2)}) collective-permute-start(bf16[320,512]{1,0:T(8,128)(2,1)S(1)} %gate.7.refs_0_), channel_id=1, source_target_pairs={{0,3},{1,2},{2,1},{3,0},{4,7},{5,6},{6,5},{7,4},{8,11},{9,10},{10,... | collective-permute-start | bytes 983048 | tf_op jit(solution)/shard_map/ppermute | solution.py:397
  33.9 26.8 %pair_zero.1 = (bf16[3,1024,2048]{2,1,0:T(8,128)(2,1)S(1)}, bf16[2,1024,2048]{2,1,0:T(8,128)(2,1)}, f32[8,2048]{1,0:T(8,128)S(1)}, s32[7]{0:T(128)S(1)}) custom-call(s32[1]{0:T(128)} %bitcast.me_ref, bf16[128,2048]{1,0:T(8,128)(2,1)S(1)} %get-tuple-element.22.right_ref.arrived_ref, f32[8,2048]{1,0:T(8,128)S(1)} %get-tuple-element.25.refs_1_.refs_0_, ...), custom_call_target="tpu_custom_call" | custom-call | tf_op jit(solution)/shard_map/pair_zero/pallas_call | solution.py:546
  60.7 24.4 %pair_one.1 = (bf16[3,1024,2048]{2,1,0:T(8,128)(2,1)S(1)}, bf16[2,1024,2048]{2,1,0:T(8,128)(2,1)}, f32[8,2048]{1,0:T(8,128)S(1)}, bf16[8,2176]{1,0:T(8,128)(2,1)S(1)}) custom-call(s32[7]{0:T(128)S(1)} %get-tuple-element.28.slots_ref, bf16[128,2048]{1,0:T(8,128)(2,1)S(1)} %get-tuple-element.22.right_ref.arrived_ref, ...), custom_call_target="tpu_custom_call" | custom-call | tf_op jit(solution)/shard_map/pair_one/pallas_call | solution.py:566
  85.2 0.9 collective-permute-start.14
  86.1 3.5 %collective-permute-start.12 = (bf16[1,8,2176]{2,1,0:T(8,128)(2,1)S(1)}, bf16[1,8,2176]{2,1,0:T(8,128)(2,1)S(1)}, u32[]{:S(2)}, u32[]{:S(2)}) collective-permute-start(bf16[1,8,2176]{2,1,0:T(8,128)(2,1)S(1)} %bitcast.7), channel_id=1, source_target_pairs={{0,4},{1,5},{2,6},{3,7},{4,0},{5,1},{6,2},{7,3},{8,12},{9,13},{10,... | collective-permute-start | bytes 104456 | tf_op jit(solution)/shard_map/ppermute | solution.py:397
  89.6 2.4 %own_again_1.1.refs_1_ = f32[8,2048]{1,0:T(8,128)S(1)} custom-call(bf16[6,512,512]{2,1,0:T(8,128)(2,1)} %get-tuple-element.38.in_ref, bf16[8,2176]{1,0:T(8,128)(2,1)S(1)} %get-tuple-element.35.vec_ref), custom_call_target="tpu_custom_call" | custom-call | flops 5000000000 | bytes 3145728 | tf_op jit(solution)/shard_map/own_again_1/pallas_call | solution.py:590
  92.1 1.3 %collective-permute-start.15 = (bf16[4,8,2176]{2,1,0:T(8,128)(2,1)S(1)}, bf16[4,8,2176]{2,1,0:T(8,128)(2,1)S(1)}, u32[]{:S(2)}, u32[]{:S(2)}) collective-permute-start(bf16[4,8,2176]{2,1,0:T(8,128)(2,1)S(1)} %pad_maximum_fusion.2), channel_id=1, source_target_pairs={{0,2},{1,3},{2,0},{3,1},{4,6},{5,7},{6,4},{7,5},{8,10},{9,11},{10,... | collective-permute-start | bytes 417800 | tf_op jit(solution)/shard_map/ppermute | solution.py:397
  93.4 3.8 %collective-permute-done.15 = bf16[4,8,2176]{2,1,0:T(8,128)(2,1)S(1)} collective-permute-done((bf16[4,8,2176]{2,1,0:T(8,128)(2,1)S(1)}, bf16[4,8,2176]{2,1,0:T(8,128)(2,1)S(1)}, u32[]{:S(2)}, u32[]{:S(2)}) %collective-permute-start.15) | collective-permute-done | bytes 139296 | tf_op jit(solution)/shard_map/ppermute | solution.py:397
  97.3 2.0 %own_again_0.1.refs_0_ = f32[8,2048]{1,0:T(8,128)S(1)} custom-call(bf16[4,512,512]{2,1,0:T(8,128)(2,1)} %get-tuple-element.37.in_ref, bf16[8,2176]{1,0:T(8,128)(2,1)S(1)} %get-tuple-element.35.vec_ref), custom_call_target="tpu_custom_call" | custom-call | flops 5000000000 | bytes 2097152 | tf_op jit(solution)/shard_map/own_again_0/pallas_call | solution.py:590
  99.3 10.1 %pair_again.1 = (f32[32,2048]{1,0:T(8,128)S(1)}, f32[8,128]{1,0:T(8,128)S(1)}, f32[8,128]{1,0:T(8,128)S(1)}) custom-call(s32[7]{0:T(128)S(1)} %get-tuple-element.28.slots_ref, bf16[3,1024,2048]{2,1,0:T(8,128)(2,1)S(1)} %get-tuple-element.29.front_zero_ref, bf16[3,1024,2048]{2,1,0:T(8,128)(2,1)S(1)} %get-tuple-element.32.front_one_ref, ...), custom_call_target="tpu_custom_call" | custom-call | tf_op jit(solution)/shard_map/pair_again/pallas_call | solution.py:608
  109.5 1.9 %collective-permute-start.19 = (f32[8,128]{1,0:T(8,128)S(1)}, f32[8,128]{1,0:T(8,128)S(1)}, u32[]{:S(2)}, u32[]{:S(2)}) collective-permute-start(f32[8,128]{1,0:T(8,128)S(1)} %get-tuple-element.41), channel_id=1, source_target_pairs={{0,12},{1,13},{2,14},{3,15},{4,8},{5,9},{6,10},{7,11},{8,4},{9,5},... | collective-permute-start | bytes 12296 | tf_op jit(solution)/shard_map/ppermute | solution.py:397
  111.4 2.5 %collective-permute-start.17 = (f32[8,128]{1,0:T(8,128)S(1)}, f32[8,128]{1,0:T(8,128)S(1)}, u32[]{:S(2)}, u32[]{:S(2)}) collective-permute-start(f32[8,128]{1,0:T(8,128)S(1)} %get-tuple-element.41), channel_id=1, source_target_pairs={{0,4},{1,5},{2,6},{3,7},{4,0},{5,1},{6,2},{7,3},{8,12},{9,13},{10,... | collective-permute-start | bytes 12296 | tf_op jit(solution)/shard_map/ppermute | solution.py:397
  113.9 1.0 collective-permute-done.19
  114.9 1.0 collective-permute-done.18
  116.0 1.2 %collective-permute-start.21 = (f32[8,128]{1,0:T(8,128)S(1)}, f32[8,128]{1,0:T(8,128)S(1)}, u32[]{:S(2)}, u32[]{:S(2)}) collective-permute-start(f32[8,128]{1,0:T(8,128)S(1)} %add_add_fusion.1), channel_id=1, source_target_pairs={{0,2},{1,3},{2,0},{3,1},{4,6},{5,7},{6,4},{7,5},{8,10},{9,11},{10,... | collective-permute-start | bytes 12296 | tf_op jit(solution)/shard_map/ppermute | solution.py:397
  117.8 1.5 %curve_order.1 = f32[32,2048]{1,0:T(8,128)S(1)} custom-call(f32[32,2048]{1,0:T(8,128)S(1)} %get-tuple-element.40.rows_ref, s32[1,2048]{1,0:T(1,128)S(1)} %copy-done.2), custom_call_target="tpu_custom_call" | custom-call | tf_op jit(solution)/shard_map/curve_order/pallas_call | solution.py:646
  (55 shorter events, 5.0 us)
Async XLA Ops:
  2.6 13.6 %collective-permute-start.2 = (bf16[96,512]{1,0:T(8,128)(2,1)S(1)}, bf16[96,512]{1,0:T(8,128)(2,1)S(1)}, u32[]{:S(2)}, u32[]{:S(2)}) collective-permute-start(bf16[96,512]{1,0:T(8,128)(2,1)S(1)} %get-tuple-element.26), channel_id=1, source_target_pairs={{0,12},{1,13},{2,14},{3,15},{4,8},{5,9},{6,10},{7,11},{8,4},{9,5},... | collective-permute-start | bytes 294920 | tf_op jit(solution)/shard_map/ppermute | solution.py:397
  7.7 12.2 %collective-permute-start.1 = (bf16[96,512]{1,0:T(8,128)(2,1)S(1)}, bf16[96,512]{1,0:T(8,128)(2,1)S(1)}, u32[]{:S(2)}, u32[]{:S(2)}) collective-permute-start(bf16[96,512]{1,0:T(8,128)(2,1)S(1)} %get-tuple-element.26), channel_id=1, source_target_pairs={{0,8},{1,9},{2,10},{3,11},{4,12},{5,13},{6,14},{7,15},{8,0},{9,1},... | collective-permute-start | bytes 294920 | tf_op jit(solution)/shard_map/ppermute | solution.py:397
  7.7 12.2 %collective-permute-start = (bf16[96,512]{1,0:T(8,128)(2,1)S(1)}, bf16[96,512]{1,0:T(8,128)(2,1)S(1)}, u32[]{:S(2)}, u32[]{:S(2)}) collective-permute-start(bf16[96,512]{1,0:T(8,128)(2,1)S(1)} %get-tuple-element.26), channel_id=1, source_target_pairs={{0,4},{1,5},{2,6},{3,7},{4,0},{5,1},{6,2},{7,3},{8,12},{9,13},{10,... | collective-permute-start | bytes 294920 | tf_op jit(solution)/shard_map/ppermute | solution.py:397
  12.3 19.2 %collective-permute-start.8 = (bf16[80,512]{1,0:T(8,128)(2,1)S(1)}, bf16[80,512]{1,0:T(8,128)(2,1)S(1)}, u32[]{:S(2)}, u32[]{:S(2)}) collective-permute-start(bf16[80,512]{1,0:T(8,128)(2,1)S(1)} %gate.6), channel_id=1, source_target_pairs={{0,12},{1,13},{2,14},{3,15},{4,8},{5,9},{6,10},{7,11},{8,4},{9,5},... | collective-permute-start | bytes 245768 | tf_op jit(solution)/shard_map/ppermute | solution.py:397
  16.1 15.4 %collective-permute-start.7 = (bf16[80,512]{1,0:T(8,128)(2,1)S(1)}, bf16[80,512]{1,0:T(8,128)(2,1)S(1)}, u32[]{:S(2)}, u32[]{:S(2)}) collective-permute-start(bf16[80,512]{1,0:T(8,128)(2,1)S(1)} %gate.6), channel_id=1, source_target_pairs={{0,8},{1,9},{2,10},{3,11},{4,12},{5,13},{6,14},{7,15},{8,0},{9,1},... | collective-permute-start | bytes 245768 | tf_op jit(solution)/shard_map/ppermute | solution.py:397
  16.2 15.4 %collective-permute-start.6 = (bf16[80,512]{1,0:T(8,128)(2,1)S(1)}, bf16[80,512]{1,0:T(8,128)(2,1)S(1)}, u32[]{:S(2)}, u32[]{:S(2)}) collective-permute-start(bf16[80,512]{1,0:T(8,128)(2,1)S(1)} %gate.6), channel_id=1, source_target_pairs={{0,4},{1,5},{2,6},{3,7},{4,0},{5,1},{6,2},{7,3},{8,12},{9,13},{10,... | collective-permute-start | bytes 245768 | tf_op jit(solution)/shard_map/ppermute | solution.py:397
  19.9 40.8 %copy-start = (f32[8,2048]{1,0:T(8,128)S(1)}, f32[8,2048]{1,0:T(8,128)}, u32[]{:S(2)}) copy-start(f32[8,2048]{1,0:T(8,128)} %rhs_ref.5) | copy-start | bytes 196612
  20.0 13.9 %collective-permute-start.4 = (bf16[384,512]{1,0:T(8,128)(2,1)S(1)}, bf16[384,512]{1,0:T(8,128)(2,1)S(1)}, u32[]{:S(2)}, u32[]{:S(2)}) collective-permute-start(bf16[384,512]{1,0:T(8,128)(2,1)S(1)} %gate.4.arrived_ref.refs_2_), channel_id=1, source_target_pairs={{0,1},{1,0},{2,3},{3,2},{4,5},{5,4},{6,7},{7,6},{8,9},{9,8},{10,11... | collective-permute-start | bytes 1179656 | tf_op jit(solution)/shard_map/ppermute | solution.py:397
  20.0 11.5 %collective-permute-start.3 = (bf16[384,512]{1,0:T(8,128)(2,1)S(1)}, bf16[384,512]{1,0:T(8,128)(2,1)S(1)}, u32[]{:S(2)}, u32[]{:S(2)}) collective-permute-start(bf16[384,512]{1,0:T(8,128)(2,1)S(1)} %gate.4.arrived_ref.refs_2_), channel_id=1, source_target_pairs={{0,2},{1,3},{2,0},{3,1},{4,6},{5,7},{6,4},{7,5},{8,10},{9,11},{10,... | collective-permute-start | bytes 1179656 | tf_op jit(solution)/shard_map/ppermute | solution.py:397
  31.6 2.3 %collective-permute-start.5 = (bf16[384,512]{1,0:T(8,128)(2,1)S(1)}, bf16[384,512]{1,0:T(8,128)(2,1)S(1)}, u32[]{:S(2)}, u32[]{:S(2)}) collective-permute-start(bf16[384,512]{1,0:T(8,128)(2,1)S(1)} %gate.5.refs_3_), channel_id=1, source_target_pairs={{0,1},{1,0},{2,3},{3,2},{4,5},{5,4},{6,7},{7,6},{8,9},{9,8},{10,11... | collective-permute-start | bytes 1179656 | tf_op jit(solution)/shard_map/ppermute | solution.py:397
  31.6 29.0 %collective-permute-start.11 = (bf16[320,512]{1,0:T(8,128)(2,1)S(1)}, bf16[320,512]{1,0:T(8,128)(2,1)S(1)}, u32[]{:S(2)}, u32[]{:S(2)}) collective-permute-start(bf16[320,512]{1,0:T(8,128)(2,1)S(1)} %gate.7.refs_0_), channel_id=1, source_target_pairs={{0,3},{1,2},{2,1},{3,0},{4,7},{5,6},{6,5},{7,4},{8,11},{9,10},{10,... | collective-permute-start | bytes 983048 | tf_op jit(solution)/shard_map/ppermute | solution.py:397
  33.3 27.4 %collective-permute-start.10 = (bf16[320,512]{1,0:T(8,128)(2,1)S(1)}, bf16[320,512]{1,0:T(8,128)(2,1)S(1)}, u32[]{:S(2)}, u32[]{:S(2)}) collective-permute-start(bf16[320,512]{1,0:T(8,128)(2,1)S(1)} %gate.7.refs_0_), channel_id=1, source_target_pairs={{0,1},{1,0},{2,3},{3,2},{4,5},{5,4},{6,7},{7,6},{8,9},{9,8},{10,11... | collective-permute-start | bytes 983048 | tf_op jit(solution)/shard_map/ppermute | solution.py:397
  33.3 27.4 %collective-permute-start.9 = (bf16[320,512]{1,0:T(8,128)(2,1)S(1)}, bf16[320,512]{1,0:T(8,128)(2,1)}, u32[]{:S(2)}, u32[]{:S(2)}) collective-permute-start(bf16[320,512]{1,0:T(8,128)(2,1)S(1)} %gate.7.refs_0_), channel_id=1, source_target_pairs={{0,2},{1,3},{2,0},{3,1},{4,6},{5,7},{6,4},{7,5},{8,10},{9,11},{10,... | collective-permute-start | bytes 983048 | tf_op jit(solution)/shard_map/ppermute | solution.py:397
  85.2 6.8 %collective-permute-start.14 = (bf16[1,8,2176]{2,1,0:T(8,128)(2,1)S(1)}, bf16[1,8,2176]{2,1,0:T(8,128)(2,1)S(1)}, u32[]{:S(2)}, u32[]{:S(2)}) collective-permute-start(bf16[1,8,2176]{2,1,0:T(8,128)(2,1)S(1)} %bitcast.5), channel_id=1, source_target_pairs={{0,12},{1,13},{2,14},{3,15},{4,8},{5,9},{6,10},{7,11},{8,4},{9,5},... | collective-permute-start | bytes 104456 | tf_op jit(solution)/shard_map/ppermute | solution.py:397
  86.1 5.9 %collective-permute-start.13 = (bf16[1,8,2176]{2,1,0:T(8,128)(2,1)S(1)}, bf16[1,8,2176]{2,1,0:T(8,128)(2,1)S(1)}, u32[]{:S(2)}, u32[]{:S(2)}) collective-permute-start(bf16[1,8,2176]{2,1,0:T(8,128)(2,1)S(1)} %bitcast.6), channel_id=1, source_target_pairs={{0,8},{1,9},{2,10},{3,11},{4,12},{5,13},{6,14},{7,15},{8,0},{9,1},... | collective-permute-start | bytes 104456 | tf_op jit(solution)/shard_map/ppermute | solution.py:397
  86.1 5.9 %collective-permute-start.12 = (bf16[1,8,2176]{2,1,0:T(8,128)(2,1)S(1)}, bf16[1,8,2176]{2,1,0:T(8,128)(2,1)S(1)}, u32[]{:S(2)}, u32[]{:S(2)}) collective-permute-start(bf16[1,8,2176]{2,1,0:T(8,128)(2,1)S(1)} %bitcast.7), channel_id=1, source_target_pairs={{0,4},{1,5},{2,6},{3,7},{4,0},{5,1},{6,2},{7,3},{8,12},{9,13},{10,... | collective-permute-start | bytes 104456 | tf_op jit(solution)/shard_map/ppermute | solution.py:397
  92.1 5.1 %collective-permute-start.15 = (bf16[4,8,2176]{2,1,0:T(8,128)(2,1)S(1)}, bf16[4,8,2176]{2,1,0:T(8,128)(2,1)S(1)}, u32[]{:S(2)}, u32[]{:S(2)}) collective-permute-start(bf16[4,8,2176]{2,1,0:T(8,128)(2,1)S(1)} %pad_maximum_fusion.2), channel_id=1, source_target_pairs={{0,2},{1,3},{2,0},{3,1},{4,6},{5,7},{6,4},{7,5},{8,10},{9,11},{10,... | collective-permute-start | bytes 417800 | tf_op jit(solution)/shard_map/ppermute | solution.py:397
  97.2 2.1 %collective-permute-start.16 = (bf16[8,8,2176]{2,1,0:T(8,128)(2,1)S(1)}, bf16[8,8,2176]{2,1,0:T(8,128)(2,1)S(1)}, u32[]{:S(2)}, u32[]{:S(2)}) collective-permute-start(bf16[8,8,2176]{2,1,0:T(8,128)(2,1)S(1)} %get-tuple-element.47), channel_id=1, source_target_pairs={{0,1},{1,0},{2,3},{3,2},{4,5},{5,4},{6,7},{7,6},{8,9},{9,8},{10,11... | collective-permute-start | bytes 835592 | tf_op jit(solution)/shard_map/ppermute | solution.py:397
  109.5 5.5 %collective-permute-start.19 = (f32[8,128]{1,0:T(8,128)S(1)}, f32[8,128]{1,0:T(8,128)S(1)}, u32[]{:S(2)}, u32[]{:S(2)}) collective-permute-start(f32[8,128]{1,0:T(8,128)S(1)} %get-tuple-element.41), channel_id=1, source_target_pairs={{0,12},{1,13},{2,14},{3,15},{4,8},{5,9},{6,10},{7,11},{8,4},{9,5},... | collective-permute-start | bytes 12296 | tf_op jit(solution)/shard_map/ppermute | solution.py:397
  111.4 4.5 %collective-permute-start.18 = (f32[8,128]{1,0:T(8,128)S(1)}, f32[8,128]{1,0:T(8,128)S(1)}, u32[]{:S(2)}, u32[]{:S(2)}) collective-permute-start(f32[8,128]{1,0:T(8,128)S(1)} %get-tuple-element.41), channel_id=1, source_target_pairs={{0,8},{1,9},{2,10},{3,11},{4,12},{5,13},{6,14},{7,15},{8,0},{9,1},... | collective-permute-start | bytes 12296 | tf_op jit(solution)/shard_map/ppermute | solution.py:397
  111.4 4.5 %collective-permute-start.17 = (f32[8,128]{1,0:T(8,128)S(1)}, f32[8,128]{1,0:T(8,128)S(1)}, u32[]{:S(2)}, u32[]{:S(2)}) collective-permute-start(f32[8,128]{1,0:T(8,128)S(1)} %get-tuple-element.41), channel_id=1, source_target_pairs={{0,4},{1,5},{2,6},{3,7},{4,0},{5,1},{6,2},{7,3},{8,12},{9,13},{10,... | collective-permute-start | bytes 12296 | tf_op jit(solution)/shard_map/ppermute | solution.py:397
  115.9 3.4 %collective-permute-start.22 = (f32[8,128]{1,0:T(8,128)S(1)}, f32[8,128]{1,0:T(8,128)S(1)}, u32[]{:S(2)}, u32[]{:S(2)}) collective-permute-start(f32[8,128]{1,0:T(8,128)S(1)} %add_add_fusion.1), channel_id=1, source_target_pairs={{0,3},{1,2},{2,1},{3,0},{4,7},{5,6},{6,5},{7,4},{8,11},{9,10},{10,... | collective-permute-start | bytes 12296 | tf_op jit(solution)/shard_map/ppermute | solution.py:397
  116.0 3.7 %collective-permute-start.21 = (f32[8,128]{1,0:T(8,128)S(1)}, f32[8,128]{1,0:T(8,128)S(1)}, u32[]{:S(2)}, u32[]{:S(2)}) collective-permute-start(f32[8,128]{1,0:T(8,128)S(1)} %add_add_fusion.1), channel_id=1, source_target_pairs={{0,2},{1,3},{2,0},{3,1},{4,6},{5,7},{6,4},{7,5},{8,10},{9,11},{10,... | collective-permute-start | bytes 12296 | tf_op jit(solution)/shard_map/ppermute | solution.py:397
  117.2 2.4 %collective-permute-start.20 = (f32[8,128]{1,0:T(8,128)S(1)}, f32[8,128]{1,0:T(8,128)S(1)}, u32[]{:S(2)}, u32[]{:S(2)}) collective-permute-start(f32[8,128]{1,0:T(8,128)S(1)} %add_add_fusion.1), channel_id=1, source_target_pairs={{0,1},{1,0},{2,3},{3,2},{4,5},{5,4},{6,7},{7,6},{8,9},{9,8},{10,11... | collective-permute-start | bytes 12296 | tf_op jit(solution)/shard_map/ppermute | solution.py:397
  (2 other events, 59.3 us)

commit v16 on v14

--- a/solution.py
+++ b/solution.py
@@ -15,8 +15,6 @@
 KDIM = 128
 ROWS = 512
 PARTS = 2
-PIECE = 256
-STRIP = 64
 FRONT = 3
 HELD = 4
 TAIL = 128
@@ -61,25 +59,21 @@
     return (jnp.exp2(19.0 * lax.log2(u)) * (1.0 - u)).astype(BF16)
 
 
-def tile_unit(left, right, vec, tile_ref, ahead):
-    pieces = [slice(at, at + PIECE) for at in range(0, right.shape[1], PIECE)]
+def tile_unit(left, right, vec, tile_ref, width, strip):
+    pieces = [slice(at, at + width) for at in range(0, right.shape[1], width)]
     gram = lambda piece: jnp.dot(left, right[:, piece], preferred_element_type=F32)
     product = lambda part: jnp.dot(vec, part, preferred_element_type=F32)
-    dists = [gram(piece) for piece in pieces[:ahead]]
-    parts, terms = [], []
+    dist, part, terms = gram(pieces[0]), None, []
     for index, piece in enumerate(pieces):
-        if index + ahead < len(pieces):
-            dists.append(gram(pieces[index + ahead]))
-        dist = dists[index]
+        following = gram(pieces[index + 1]) if index + 1 < len(pieces) else None
         strips = []
-        for sub in range(0, left.shape[0], STRIP):
-            strips.append(psi_power(dist[sub : sub + STRIP]))
-            tile_ref[sub : sub + STRIP, piece] = strips[-1]
-        parts.append(jnp.concatenate(strips, axis=0))
-        if index >= ahead:
-            terms.append(product(parts[index - ahead]))
-    terms += [product(part) for part in parts[len(terms) :]]
-    return jnp.concatenate(terms, axis=1)
+        for at in range(0, left.shape[0], strip):
+            strips.append(psi_power(dist[at : at + strip]))
+            tile_ref[at : at + strip, piece] = strips[-1]
+        if part is not None:
+            terms.append(product(part))
+        dist, part = following, jnp.concatenate(strips, axis=0)
+    return jnp.concatenate(terms + [product(part)], axis=1)
 
 
 def unpack(pay):
@@ -102,7 +96,7 @@
         def col_step(col, at):
             sum_ref[:, piece(col)] += tile_unit(
                 left_ref[piece(row), :], right_ref[:, piece(col)], vec_ref[:, piece(row)],
-                tile_ref.at[at], 1,
+                tile_ref.at[at], 256, 64,
             )
             save(at).start()
 
@@ -193,7 +187,7 @@
     return fetch
 
 
-def half_tiles(ahead, slots_ref, right_ref, fetch, front_ref, back_ref, sum_ref, left_ref, vec_ref, pay_ref, sem_ref):
+def half_tiles(piece, strip, slots_ref, right_ref, fetch, front_ref, back_ref, sum_ref, left_ref, vec_ref, pay_ref, sem_ref):
     slot, step = pl.program_id(0), pl.program_id(1)
 
     @pl.when((slot == 0) & (step == 0) & (slots_ref[0] > 0))
@@ -221,7 +215,7 @@
         for tile_ref, here in ((front_ref, slot < FRONT), (back_ref, slot >= FRONT)):
             @pl.when(here)
             def _():
-                sum_ref[...] += tile_unit(left, right_ref[...], vec, tile_ref.at[0], ahead)
+                sum_ref[...] += tile_unit(left, right_ref[...], vec, tile_ref.at[0], piece, strip)
 
 
 def pair_zero_kernel(block_at, me_ref, right_ref, *refs):
@@ -252,7 +246,7 @@
 
     fetch = fetch_from(block_at, block_refs, slots_ref, pay_ref, sem_ref)
     half_tiles(
-        1, slots_ref, right_ref, fetch, front_ref, back_ref, sum_ref, left_ref, vec_ref, pay_ref, sem_ref
+        256, 128, slots_ref, right_ref, fetch, front_ref, back_ref, sum_ref, left_ref, vec_ref, pay_ref, sem_ref
     )
 
 
@@ -267,7 +261,7 @@
 
     fetch = fetch_from(block_at, block_refs, slots_ref, pay_ref, sem_ref)
     half_tiles(
-        0, slots_ref, right_ref, fetch, front_ref, back_ref, image_ref, left_ref, vec_ref, pay_ref, sem_ref
+        512, 64, slots_ref, right_ref, fetch, front_ref, back_ref, image_ref, left_ref, vec_ref, pay_ref, sem_ref
     )
 
     @pl.when((slot == pl.num_programs(0) - 1) & (step == pl.num_programs(1) - 1))
@@ -292,10 +286,10 @@
 ):
     first_refs = refs[:PARTS]
     rows_ref, dots_ref, step_ref, sum_ref, held_ref, sem_ref = refs[PARTS:]
-    slot, step = pl.program_id(0), pl.program_id(1)
+    slot = pl.program_id(0)
     width = rhs_ref.shape[1]
     steps = width // ROWS
-    half = steps // 2
+    half = width // 2
     parts = (slots_ref[0] - FRONT) * steps
 
     def fetch(part, back_ref, first):
@@ -305,40 +299,40 @@
         )
 
     def start(part):
-        @pl.when((part < parts) & (part % steps < half))
+        @pl.when((part < parts) & (part % steps < steps // 2))
         def _():
             fetch(part, back_zero_ref, 0).start()
 
-        @pl.when((part < parts) & (part % steps >= half))
+        @pl.when((part < parts) & (part % steps >= steps // 2))
         def _():
-            fetch(part, back_one_ref, half).start()
-
-    @pl.when((slot == 0) & (step == 0))
+            fetch(part, back_one_ref, steps // 2).start()
+
+    @pl.when(slot == 0)
     def _():
         sum_ref[...] = functools.reduce(jnp.add, [first_ref[...] for first_ref in first_refs])
         for part in range(HELD):
             start(part)
 
-    @pl.when(slot < slots_ref[0])
-    def _():
-        at = pl.multiple_of(step * ROWS, ROWS)
-        for front_ref, here in ((front_zero_ref, step < half), (front_one_ref, step >= half)):
-            @pl.when((slot < FRONT) & here)
-            def _():
-                sum_ref[...] += jnp.dot(
-                    vec_ref[0, :, pl.ds(at, ROWS)], front_ref[0], preferred_element_type=F32
-                )
-
-        @pl.when(slot >= FRONT)
-        def _():
+    @pl.when((slot < slots_ref[0]) & (slot < FRONT))
+    def _():
+        for index, front_ref in enumerate((front_zero_ref, front_one_ref)):
+            sum_ref[...] += jnp.dot(
+                vec_ref[0, :, index * half : (index + 1) * half], front_ref[0],
+                preferred_element_type=F32,
+            )
+
+    @pl.when((slot < slots_ref[0]) & (slot >= FRONT))
+    def _():
+        for step in range(steps):
             part = (slot - FRONT) * steps + step
-            fetch(part % HELD, back_zero_ref, part % HELD // half * half).wait()
+            fetch(part % HELD, back_zero_ref, part % HELD // (steps // 2) * (steps // 2)).wait()
             sum_ref[...] += jnp.dot(
-                vec_ref[0, :, pl.ds(at, ROWS)], held_ref[part % HELD], preferred_element_type=F32
+                vec_ref[0, :, step * ROWS : (step + 1) * ROWS], held_ref[part % HELD],
+                preferred_element_type=F32,
             )
             start(part + HELD)
 
-    @pl.when((slot == pl.num_programs(0) - 1) & (step == pl.num_programs(1) - 1))
+    @pl.when(slot == pl.num_programs(0) - 1)
     def _():
         rhs = rhs_ref[...]
         image = image_ref[...]
@@ -562,12 +556,6 @@
     fronts = [pltpu.with_memory_space_constraint(part, pltpu.VMEM) for part in (front_zero, front_one)]
     backs = [pltpu.with_memory_space_constraint(part, pltpu.HBM) for part in (back_zero, back_one)]
 
-    def front_zero_at(k, i, *ignored):
-        return (jnp.minimum(k, FRONT - 1), jnp.where(k < FRONT, jnp.minimum(i, half - 1), half - 1), 0)
-
-    def front_one_at(k, i, *ignored):
-        return (jnp.minimum(k, FRONT - 1), jnp.where(k < FRONT, jnp.maximum(i - half, 0), half - 1), 0)
-
     every_send = tree_gather(send, count)[-1]
     own_again = [
         pl.pallas_call(
@@ -592,14 +580,14 @@
         again_kernel,
         grid_spec=pltpu.PrefetchScalarGridSpec(
             num_scalar_prefetch=1,
-            grid=(most, steps),
+            grid=(most,),
             in_specs=[
-                pl.BlockSpec((1, ROWS, width), front_zero_at),
-                pl.BlockSpec((1, ROWS, width), front_one_at),
+                pl.BlockSpec((1, width // 2, width), lambda k, s: (jnp.minimum(k, FRONT - 1), 0, 0)),
+                pl.BlockSpec((1, width // 2, width), lambda k, s: (jnp.minimum(k, FRONT - 1), 0, 0)),
                 any_spec,
                 any_spec,
-                pl.BlockSpec((1,) + send_shape, lambda k, i, s: (s[1 + k], 0, 0)),
-                pl.BlockSpec((count, rhs_count, TAIL), lambda k, i, s: (0, 0, width // TAIL)),
+                pl.BlockSpec((1,) + send_shape, lambda k, s: (s[1 + k], 0, 0)),
+                pl.BlockSpec((count, rhs_count, TAIL), lambda k, s: (0, 0, width // TAIL)),
                 row_spec,
                 var_spec,
                 row_spec,

time: 128 us -> 121 us (0.945)
  Pallas kernels: 27.9 us -> 47.9 us
  starting transfers between devices: 71.6 us -> 53.3 us
  waiting for transfers between devices: 25.8 us -> 16.5 us
    ppermute x23, starting transfers between devices: 71.6 us -> 53.3 us  [swap(): return lax.ppermute(value, 'row', [(i, i ^ mask) for i in range(count)])]
    pallas_call x1, Pallas kernels: 4.45 us -> 14 us  [local(): pl.pallas_call(functools.partial(pair_one_kernel, one_at), grid_spec=pltp...]
    ppermute x23, waiting for transfers between devices: 25.8 us -> 16.5 us  [swap(): return lax.ppermute(value, 'row', [(i, i ^ mask) for i in range(count)])]
    pallas_call x1, Pallas kernels: 4.94 us -> 13.8 us  [local(): pl.pallas_call(functools.partial(pair_zero_kernel, zero_at), grid_spec=pl...]
    pallas_call x1, Pallas kernels: 1.91 us -> 3.4 us  [local(): pl.pallas_call(again_kernel, grid_spec=pltpu.PrefetchScalarGridSpec(num_s...]
  transfers between devices with their start and end apart: 23 -> 23, of which waited for: 9 -> 8; matrix products, arithmetic and copies ran while one was open for 0% -> 0% of each run, Pallas kernels for 16% -> 24%
where the time goes in v16:
time: 121 us; the launch traced here: 120 us
  starting transfers between devices  53.3 us (44%)
  Pallas kernels  47.9 us (40%)
  waiting for transfers between devices  16.5 us (14%)
    ppermute x23, starting transfers between devices, swap(): return lax.ppermute(value, 'row', [(i, i ^ mask) for i in range(count)])  53.3 us
    ppermute x23, waiting for transfers between devices, swap(): return lax.ppermute(value, 'row', [(i, i ^ mask) for i in range(count)])  16.5 us
    pallas_call x1, Pallas kernels, local(): pl.pallas_call(functools.partial(pair_one_kernel, one_at), grid_spec=pltp...  14 us
    pallas_call x1, Pallas kernels, local(): pl.pallas_call(functools.partial(pair_zero_kernel, zero_at), grid_spec=pl...  13.8 us
    pallas_call x2, Pallas kernels, own_part(): pl.pallas_call(functools.partial(own_kernel, rows), in_specs=[vmem, vmem,...  9.62 us
    pallas_call x2, Pallas kernels, local(): pl.pallas_call(functools.partial(own_again_kernel, blocks), in_specs=[any...  4.34 us
    pallas_call x1, Pallas kernels, local(): pl.pallas_call(again_kernel, grid_spec=pltpu.PrefetchScalarGridSpec(num_s...  3.4 us
  transfers between devices with their start and end apart: 23, of which 8 were waited for; matrix products, arithmetic and copies ran while one was open for 0% of the time, Pallas kernels for 24%

profile of v16, /device:TPU:0, one launch (start us, length us, event | category | flops | bytes accessed | tf_op | source)
XLA Modules:
  0.0 120.5 jit_solution(1212342877830299235)
XLA Ops:
  1.4 1.2 payload.1
  2.6 5.1 %collective-permute-start.2 = (bf16[96,512]{1,0:T(8,128)(2,1)S(1)}, bf16[96,512]{1,0:T(8,128)(2,1)S(1)}, u32[]{:S(2)}, u32[]{:S(2)}) collective-permute-start(bf16[96,512]{1,0:T(8,128)(2,1)S(1)} %get-tuple-element.26), channel_id=1, source_target_pairs={{0,12},{1,13},{2,14},{3,15},{4,8},{5,9},{6,10},{7,11},{8,4},{9,5},... | collective-permute-start | bytes 294920 | tf_op jit(solution)/shard_map/ppermute | solution.py:374
  8.3 4.0 %own_tile_0.1 = (bf16[4,512,512]{2,1,0:T(8,128)(2,1)}, f32[8,2048]{1,0:T(8,128)S(1)}) custom-call(bf16[2048,128]{1,0:T(8,128)(2,1)S(1)} %get-tuple-element.23.left_ref, bf16[128,2048]{1,0:T(8,128)(2,1)S(1)} %get-tuple-element.22.right_ref.arrived_ref, bf16[8,2048]{1,0:T(8,128)(2,1)S(1)} %get-tuple-element.24.vec_ref, ...), custom_call_target="tpu_custom_call" | custom-call | flops 5000000000 | bytes 2097152 | tf_op jit(solution)/shard_map/own_tile_0/pallas_call | solution.py:464
  12.3 3.8 %collective-permute-start.8 = (bf16[80,512]{1,0:T(8,128)(2,1)S(1)}, bf16[80,512]{1,0:T(8,128)(2,1)S(1)}, u32[]{:S(2)}, u32[]{:S(2)}) collective-permute-start(bf16[80,512]{1,0:T(8,128)(2,1)S(1)} %gate.6), channel_id=1, source_target_pairs={{0,12},{1,13},{2,14},{3,15},{4,8},{5,9},{6,10},{7,11},{8,4},{9,5},... | collective-permute-start | bytes 245768 | tf_op jit(solution)/shard_map/ppermute | solution.py:374
  16.8 3.1 %collective-permute-done.1 = bf16[96,512]{1,0:T(8,128)(2,1)S(1)} collective-permute-done((bf16[96,512]{1,0:T(8,128)(2,1)S(1)}, bf16[96,512]{1,0:T(8,128)(2,1)S(1)}, u32[]{:S(2)}, u32[]{:S(2)}) %collective-permute-start.1) | collective-permute-done | bytes 98336 | tf_op jit(solution)/shard_map/ppermute | solution.py:374
  20.0 1.6 %collective-permute-start.3 = (bf16[384,512]{1,0:T(8,128)(2,1)S(1)}, bf16[384,512]{1,0:T(8,128)(2,1)S(1)}, u32[]{:S(2)}, u32[]{:S(2)}) collective-permute-start(bf16[384,512]{1,0:T(8,128)(2,1)S(1)} %gate.4.arrived_ref.refs_2_), channel_id=1, source_target_pairs={{0,2},{1,3},{2,0},{3,1},{4,6},{5,7},{6,4},{7,5},{8,10},{9,11},{10,... | collective-permute-start | bytes 1179656 | tf_op jit(solution)/shard_map/ppermute | solution.py:374
  21.6 5.6 %own_tile_1.1 = (bf16[6,512,512]{2,1,0:T(8,128)(2,1)}, f32[8,2048]{1,0:T(8,128)S(1)}) custom-call(bf16[2048,128]{1,0:T(8,128)(2,1)S(1)} %get-tuple-element.23.left_ref, bf16[128,2048]{1,0:T(8,128)(2,1)S(1)} %get-tuple-element.22.right_ref.arrived_ref, bf16[8,2048]{1,0:T(8,128)(2,1)S(1)} %get-tuple-element.24.vec_ref, ...), custom_call_target="tpu_custom_call" | custom-call | flops 5000000000 | bytes 3145728 | tf_op jit(solution)/shard_map/own_tile_1/pallas_call | solution.py:464
  27.2 4.3 %collective-permute-done.3.refs_0_ = bf16[384,512]{1,0:T(8,128)(2,1)S(1)} collective-permute-done((bf16[384,512]{1,0:T(8,128)(2,1)S(1)}, bf16[384,512]{1,0:T(8,128)(2,1)S(1)}, u32[]{:S(2)}, u32[]{:S(2)}) %collective-permute-start.3) | collective-permute-done | bytes 393248 | tf_op jit(solution)/shard_map/ppermute | solution.py:374
  31.6 1.7 %collective-permute-start.11 = (bf16[320,512]{1,0:T(8,128)(2,1)S(1)}, bf16[320,512]{1,0:T(8,128)(2,1)S(1)}, u32[]{:S(2)}, u32[]{:S(2)}) collective-permute-start(bf16[320,512]{1,0:T(8,128)(2,1)S(1)} %gate.7.refs_0_), channel_id=1, source_target_pairs={{0,3},{1,2},{2,1},{3,0},{4,7},{5,6},{6,5},{7,4},{8,11},{9,10},{10,... | collective-permute-start | bytes 983048 | tf_op jit(solution)/shard_map/ppermute | solution.py:374
  33.9 13.8 %pair_zero.1 = (bf16[3,1024,2048]{2,1,0:T(8,128)(2,1)S(1)}, bf16[2,1024,2048]{2,1,0:T(8,128)(2,1)}, f32[8,2048]{1,0:T(8,128)S(1)}, s32[7]{0:T(128)S(1)}) custom-call(s32[1]{0:T(128)} %bitcast.me_ref, bf16[128,2048]{1,0:T(8,128)(2,1)S(1)} %get-tuple-element.22.right_ref.arrived_ref, f32[8,2048]{1,0:T(8,128)S(1)} %get-tuple-element.25.refs_1_.refs_0_, ...), custom_call_target="tpu_custom_call" | custom-call | tf_op jit(solution)/shard_map/pair_zero/pallas_call | solution.py:523
  47.7 1.1 collective-permute-done.9.refs_1_
  48.9 14.0 %pair_one.1 = (bf16[3,1024,2048]{2,1,0:T(8,128)(2,1)S(1)}, bf16[2,1024,2048]{2,1,0:T(8,128)(2,1)}, f32[8,2048]{1,0:T(8,128)S(1)}, bf16[8,2176]{1,0:T(8,128)(2,1)S(1)}) custom-call(s32[7]{0:T(128)S(1)} %get-tuple-element.28.slots_ref, bf16[128,2048]{1,0:T(8,128)(2,1)S(1)} %get-tuple-element.22.right_ref.arrived_ref, ...), custom_call_target="tpu_custom_call" | custom-call | tf_op jit(solution)/shard_map/pair_one/pallas_call | solution.py:543
  63.0 23.0 %collective-permute-start.13 = (bf16[1,8,2176]{2,1,0:T(8,128)(2,1)S(1)}, bf16[1,8,2176]{2,1,0:T(8,128)(2,1)S(1)}, u32[]{:S(2)}, u32[]{:S(2)}) collective-permute-start(bf16[1,8,2176]{2,1,0:T(8,128)(2,1)S(1)} %bitcast.6), channel_id=1, source_target_pairs={{0,8},{1,9},{2,10},{3,11},{4,12},{5,13},{6,14},{7,15},{8,0},{9,1},... | collective-permute-start | bytes 104456 | tf_op jit(solution)/shard_map/ppermute | solution.py:374
  86.5 2.4 %own_again_1.1.refs_1_ = f32[8,2048]{1,0:T(8,128)S(1)} custom-call(bf16[6,512,512]{2,1,0:T(8,128)(2,1)} %get-tuple-element.38.in_ref, bf16[8,2176]{1,0:T(8,128)(2,1)S(1)} %get-tuple-element.35.vec_ref), custom_call_target="tpu_custom_call" | custom-call | flops 5000000000 | bytes 3145728 | tf_op jit(solution)/shard_map/own_again_1/pallas_call | solution.py:561
  90.0 4.6 %collective-permute-start.15 = (bf16[4,8,2176]{2,1,0:T(8,128)(2,1)S(1)}, bf16[4,8,2176]{2,1,0:T(8,128)(2,1)S(1)}, u32[]{:S(2)}, u32[]{:S(2)}) collective-permute-start(bf16[4,8,2176]{2,1,0:T(8,128)(2,1)S(1)} %pad_maximum_fusion.2), channel_id=1, source_target_pairs={{0,2},{1,3},{2,0},{3,1},{4,6},{5,7},{6,4},{7,5},{8,10},{9,11},{10,... | collective-permute-start | bytes 417800 | tf_op jit(solution)/shard_map/ppermute | solution.py:374
  94.6 3.2 %collective-permute-done.15 = bf16[4,8,2176]{2,1,0:T(8,128)(2,1)S(1)} collective-permute-done((bf16[4,8,2176]{2,1,0:T(8,128)(2,1)S(1)}, bf16[4,8,2176]{2,1,0:T(8,128)(2,1)S(1)}, u32[]{:S(2)}, u32[]{:S(2)}) %collective-permute-start.15) | collective-permute-done | bytes 139296 | tf_op jit(solution)/shard_map/ppermute | solution.py:374
  97.9 2.0 %own_again_0.1.refs_0_ = f32[8,2048]{1,0:T(8,128)S(1)} custom-call(bf16[4,512,512]{2,1,0:T(8,128)(2,1)} %get-tuple-element.37.in_ref, bf16[8,2176]{1,0:T(8,128)(2,1)S(1)} %get-tuple-element.35.vec_ref), custom_call_target="tpu_custom_call" | custom-call | flops 5000000000 | bytes 2097152 | tf_op jit(solution)/shard_map/own_again_0/pallas_call | solution.py:561
  99.9 3.4 %pair_again.1 = (f32[32,2048]{1,0:T(8,128)S(1)}, f32[8,128]{1,0:T(8,128)S(1)}, f32[8,128]{1,0:T(8,128)S(1)}) custom-call(s32[7]{0:T(128)S(1)} %get-tuple-element.28.slots_ref, bf16[3,1024,2048]{2,1,0:T(8,128)(2,1)S(1)} %get-tuple-element.29.front_zero_ref, bf16[3,1024,2048]{2,1,0:T(8,128)(2,1)S(1)} %get-tuple-element.32.front_one_ref, ...), custom_call_target="tpu_custom_call" | custom-call | tf_op jit(solution)/shard_map/pair_again/pallas_call | solution.py:579
  103.4 6.1 %collective-permute-start.18 = (f32[8,128]{1,0:T(8,128)S(1)}, f32[8,128]{1,0:T(8,128)S(1)}, u32[]{:S(2)}, u32[]{:S(2)}) collective-permute-start(f32[8,128]{1,0:T(8,128)S(1)} %get-tuple-element.41), channel_id=1, source_target_pairs={{0,8},{1,9},{2,10},{3,11},{4,12},{5,13},{6,14},{7,15},{8,0},{9,1},... | collective-permute-start | bytes 12296 | tf_op jit(solution)/shard_map/ppermute | solution.py:374
  110.0 1.1 collective-permute-done.18
  111.1 2.0 %collective-permute-done.17 = f32[8,128]{1,0:T(8,128)S(1)} collective-permute-done((f32[8,128]{1,0:T(8,128)S(1)}, f32[8,128]{1,0:T(8,128)S(1)}, u32[]{:S(2)}, u32[]{:S(2)}) %collective-permute-start.17) | collective-permute-done | bytes 4128 | tf_op jit(solution)/shard_map/ppermute | solution.py:374
  113.1 2.8 %collective-permute-start.22 = (f32[8,128]{1,0:T(8,128)S(1)}, f32[8,128]{1,0:T(8,128)S(1)}, u32[]{:S(2)}, u32[]{:S(2)}) collective-permute-start(f32[8,128]{1,0:T(8,128)S(1)} %add_add_fusion.1), channel_id=1, source_target_pairs={{0,3},{1,2},{2,1},{3,0},{4,7},{5,6},{6,5},{7,4},{8,11},{9,10},{10,... | collective-permute-start | bytes 12296 | tf_op jit(solution)/shard_map/ppermute | solution.py:374
  115.9 1.5 %collective-permute-start.21 = (f32[8,128]{1,0:T(8,128)S(1)}, f32[8,128]{1,0:T(8,128)S(1)}, u32[]{:S(2)}, u32[]{:S(2)}) collective-permute-start(f32[8,128]{1,0:T(8,128)S(1)} %add_add_fusion.1), channel_id=1, source_target_pairs={{0,2},{1,3},{2,0},{3,1},{4,6},{5,7},{6,4},{7,5},{8,10},{9,11},{10,... | collective-permute-start | bytes 12296 | tf_op jit(solution)/shard_map/ppermute | solution.py:374
  117.4 1.5 %curve_order.1 = f32[32,2048]{1,0:T(8,128)S(1)} custom-call(f32[32,2048]{1,0:T(8,128)S(1)} %get-tuple-element.40.rows_ref, s32[1,2048]{1,0:T(1,128)S(1)} %copy-done.2), custom_call_target="tpu_custom_call" | custom-call | tf_op jit(solution)/shard_map/curve_order/pallas_call | solution.py:617
  (55 shorter events, 6.8 us)
Async XLA Ops:
  2.6 13.6 %collective-permute-start.2 = (bf16[96,512]{1,0:T(8,128)(2,1)S(1)}, bf16[96,512]{1,0:T(8,128)(2,1)S(1)}, u32[]{:S(2)}, u32[]{:S(2)}) collective-permute-start(bf16[96,512]{1,0:T(8,128)(2,1)S(1)} %get-tuple-element.26), channel_id=1, source_target_pairs={{0,12},{1,13},{2,14},{3,15},{4,8},{5,9},{6,10},{7,11},{8,4},{9,5},... | collective-permute-start | bytes 294920 | tf_op jit(solution)/shard_map/ppermute | solution.py:374
  7.7 12.2 %collective-permute-start.1 = (bf16[96,512]{1,0:T(8,128)(2,1)S(1)}, bf16[96,512]{1,0:T(8,128)(2,1)S(1)}, u32[]{:S(2)}, u32[]{:S(2)}) collective-permute-start(bf16[96,512]{1,0:T(8,128)(2,1)S(1)} %get-tuple-element.26), channel_id=1, source_target_pairs={{0,8},{1,9},{2,10},{3,11},{4,12},{5,13},{6,14},{7,15},{8,0},{9,1},... | collective-permute-start | bytes 294920 | tf_op jit(solution)/shard_map/ppermute | solution.py:374
  7.7 12.2 %collective-permute-start = (bf16[96,512]{1,0:T(8,128)(2,1)S(1)}, bf16[96,512]{1,0:T(8,128)(2,1)S(1)}, u32[]{:S(2)}, u32[]{:S(2)}) collective-permute-start(bf16[96,512]{1,0:T(8,128)(2,1)S(1)} %get-tuple-element.26), channel_id=1, source_target_pairs={{0,4},{1,5},{2,6},{3,7},{4,0},{5,1},{6,2},{7,3},{8,12},{9,13},{10,... | collective-permute-start | bytes 294920 | tf_op jit(solution)/shard_map/ppermute | solution.py:374
  12.3 19.2 %collective-permute-start.8 = (bf16[80,512]{1,0:T(8,128)(2,1)S(1)}, bf16[80,512]{1,0:T(8,128)(2,1)S(1)}, u32[]{:S(2)}, u32[]{:S(2)}) collective-permute-start(bf16[80,512]{1,0:T(8,128)(2,1)S(1)} %gate.6), channel_id=1, source_target_pairs={{0,12},{1,13},{2,14},{3,15},{4,8},{5,9},{6,10},{7,11},{8,4},{9,5},... | collective-permute-start | bytes 245768 | tf_op jit(solution)/shard_map/ppermute | solution.py:374
  16.1 15.4 %collective-permute-start.7 = (bf16[80,512]{1,0:T(8,128)(2,1)S(1)}, bf16[80,512]{1,0:T(8,128)(2,1)S(1)}, u32[]{:S(2)}, u32[]{:S(2)}) collective-permute-start(bf16[80,512]{1,0:T(8,128)(2,1)S(1)} %gate.6), channel_id=1, source_target_pairs={{0,8},{1,9},{2,10},{3,11},{4,12},{5,13},{6,14},{7,15},{8,0},{9,1},... | collective-permute-start | bytes 245768 | tf_op jit(solution)/shard_map/ppermute | solution.py:374
  16.2 15.4 %collective-permute-start.6 = (bf16[80,512]{1,0:T(8,128)(2,1)S(1)}, bf16[80,512]{1,0:T(8,128)(2,1)S(1)}, u32[]{:S(2)}, u32[]{:S(2)}) collective-permute-start(bf16[80,512]{1,0:T(8,128)(2,1)S(1)} %gate.6), channel_id=1, source_target_pairs={{0,4},{1,5},{2,6},{3,7},{4,0},{5,1},{6,2},{7,3},{8,12},{9,13},{10,... | collective-permute-start | bytes 245768 | tf_op jit(solution)/shard_map/ppermute | solution.py:374
  19.9 28.9 %copy-start = (f32[8,2048]{1,0:T(8,128)S(1)}, f32[8,2048]{1,0:T(8,128)}, u32[]{:S(2)}) copy-start(f32[8,2048]{1,0:T(8,128)} %rhs_ref.5) | copy-start | bytes 196612
  20.0 13.9 %collective-permute-start.4 = (bf16[384,512]{1,0:T(8,128)(2,1)S(1)}, bf16[384,512]{1,0:T(8,128)(2,1)S(1)}, u32[]{:S(2)}, u32[]{:S(2)}) collective-permute-start(bf16[384,512]{1,0:T(8,128)(2,1)S(1)} %gate.4.arrived_ref.refs_2_), channel_id=1, source_target_pairs={{0,1},{1,0},{2,3},{3,2},{4,5},{5,4},{6,7},{7,6},{8,9},{9,8},{10,11... | collective-permute-start | bytes 1179656 | tf_op jit(solution)/shard_map/ppermute | solution.py:374
  20.0 11.5 %collective-permute-start.3 = (bf16[384,512]{1,0:T(8,128)(2,1)S(1)}, bf16[384,512]{1,0:T(8,128)(2,1)S(1)}, u32[]{:S(2)}, u32[]{:S(2)}) collective-permute-start(bf16[384,512]{1,0:T(8,128)(2,1)S(1)} %gate.4.arrived_ref.refs_2_), channel_id=1, source_target_pairs={{0,2},{1,3},{2,0},{3,1},{4,6},{5,7},{6,4},{7,5},{8,10},{9,11},{10,... | collective-permute-start | bytes 1179656 | tf_op jit(solution)/shard_map/ppermute | solution.py:374
  31.6 2.3 %collective-permute-start.5 = (bf16[384,512]{1,0:T(8,128)(2,1)S(1)}, bf16[384,512]{1,0:T(8,128)(2,1)S(1)}, u32[]{:S(2)}, u32[]{:S(2)}) collective-permute-start(bf16[384,512]{1,0:T(8,128)(2,1)S(1)} %gate.5.refs_3_), channel_id=1, source_target_pairs={{0,1},{1,0},{2,3},{3,2},{4,5},{5,4},{6,7},{7,6},{8,9},{9,8},{10,11... | collective-permute-start | bytes 1179656 | tf_op jit(solution)/shard_map/ppermute | solution.py:374
  31.6 16.1 %collective-permute-start.11 = (bf16[320,512]{1,0:T(8,128)(2,1)S(1)}, bf16[320,512]{1,0:T(8,128)(2,1)S(1)}, u32[]{:S(2)}, u32[]{:S(2)}) collective-permute-start(bf16[320,512]{1,0:T(8,128)(2,1)S(1)} %gate.7.refs_0_), channel_id=1, source_target_pairs={{0,3},{1,2},{2,1},{3,0},{4,7},{5,6},{6,5},{7,4},{8,11},{9,10},{10,... | collective-permute-start | bytes 983048 | tf_op jit(solution)/shard_map/ppermute | solution.py:374
  33.3 14.4 %collective-permute-start.10 = (bf16[320,512]{1,0:T(8,128)(2,1)S(1)}, bf16[320,512]{1,0:T(8,128)(2,1)S(1)}, u32[]{:S(2)}, u32[]{:S(2)}) collective-permute-start(bf16[320,512]{1,0:T(8,128)(2,1)S(1)} %gate.7.refs_0_), channel_id=1, source_target_pairs={{0,1},{1,0},{2,3},{3,2},{4,5},{5,4},{6,7},{7,6},{8,9},{9,8},{10,11... | collective-permute-start | bytes 983048 | tf_op jit(solution)/shard_map/ppermute | solution.py:374
  33.3 15.5 %collective-permute-start.9 = (bf16[320,512]{1,0:T(8,128)(2,1)S(1)}, bf16[320,512]{1,0:T(8,128)(2,1)}, u32[]{:S(2)}, u32[]{:S(2)}) collective-permute-start(bf16[320,512]{1,0:T(8,128)(2,1)S(1)} %gate.7.refs_0_), channel_id=1, source_target_pairs={{0,2},{1,3},{2,0},{3,1},{4,6},{5,7},{6,4},{7,5},{8,10},{9,11},{10,... | collective-permute-start | bytes 983048 | tf_op jit(solution)/shard_map/ppermute | solution.py:374
  62.9 26.0 %collective-permute-start.14 = (bf16[1,8,2176]{2,1,0:T(8,128)(2,1)S(1)}, bf16[1,8,2176]{2,1,0:T(8,128)(2,1)S(1)}, u32[]{:S(2)}, u32[]{:S(2)}) collective-permute-start(bf16[1,8,2176]{2,1,0:T(8,128)(2,1)S(1)} %bitcast.5), channel_id=1, source_target_pairs={{0,12},{1,13},{2,14},{3,15},{4,8},{5,9},{6,10},{7,11},{8,4},{9,5},... | collective-permute-start | bytes 104456 | tf_op jit(solution)/shard_map/ppermute | solution.py:374
  63.0 25.9 %collective-permute-start.13 = (bf16[1,8,2176]{2,1,0:T(8,128)(2,1)S(1)}, bf16[1,8,2176]{2,1,0:T(8,128)(2,1)S(1)}, u32[]{:S(2)}, u32[]{:S(2)}) collective-permute-start(bf16[1,8,2176]{2,1,0:T(8,128)(2,1)S(1)} %bitcast.6), channel_id=1, source_target_pairs={{0,8},{1,9},{2,10},{3,11},{4,12},{5,13},{6,14},{7,15},{8,0},{9,1},... | collective-permute-start | bytes 104456 | tf_op jit(solution)/shard_map/ppermute | solution.py:374
  86.0 3.9 %collective-permute-start.12 = (bf16[1,8,2176]{2,1,0:T(8,128)(2,1)S(1)}, bf16[1,8,2176]{2,1,0:T(8,128)(2,1)S(1)}, u32[]{:S(2)}, u32[]{:S(2)}) collective-permute-start(bf16[1,8,2176]{2,1,0:T(8,128)(2,1)S(1)} %bitcast.7), channel_id=1, source_target_pairs={{0,4},{1,5},{2,6},{3,7},{4,0},{5,1},{6,2},{7,3},{8,12},{9,13},{10,... | collective-permute-start | bytes 104456 | tf_op jit(solution)/shard_map/ppermute | solution.py:374
  90.0 7.8 %collective-permute-start.15 = (bf16[4,8,2176]{2,1,0:T(8,128)(2,1)S(1)}, bf16[4,8,2176]{2,1,0:T(8,128)(2,1)S(1)}, u32[]{:S(2)}, u32[]{:S(2)}) collective-permute-start(bf16[4,8,2176]{2,1,0:T(8,128)(2,1)S(1)} %pad_maximum_fusion.2), channel_id=1, source_target_pairs={{0,2},{1,3},{2,0},{3,1},{4,6},{5,7},{6,4},{7,5},{8,10},{9,11},{10,... | collective-permute-start | bytes 417800 | tf_op jit(solution)/shard_map/ppermute | solution.py:374
  97.8 2.1 %collective-permute-start.16 = (bf16[8,8,2176]{2,1,0:T(8,128)(2,1)S(1)}, bf16[8,8,2176]{2,1,0:T(8,128)(2,1)S(1)}, u32[]{:S(2)}, u32[]{:S(2)}) collective-permute-start(bf16[8,8,2176]{2,1,0:T(8,128)(2,1)S(1)} %get-tuple-element.47), channel_id=1, source_target_pairs={{0,1},{1,0},{2,3},{3,2},{4,5},{5,4},{6,7},{7,6},{8,9},{9,8},{10,11... | collective-permute-start | bytes 835592 | tf_op jit(solution)/shard_map/ppermute | solution.py:374
  103.3 6.6 %collective-permute-start.19 = (f32[8,128]{1,0:T(8,128)S(1)}, f32[8,128]{1,0:T(8,128)S(1)}, u32[]{:S(2)}, u32[]{:S(2)}) collective-permute-start(f32[8,128]{1,0:T(8,128)S(1)} %get-tuple-element.41), channel_id=1, source_target_pairs={{0,12},{1,13},{2,14},{3,15},{4,8},{5,9},{6,10},{7,11},{8,4},{9,5},... | collective-permute-start | bytes 12296 | tf_op jit(solution)/shard_map/ppermute | solution.py:374
  103.4 7.7 %collective-permute-start.18 = (f32[8,128]{1,0:T(8,128)S(1)}, f32[8,128]{1,0:T(8,128)S(1)}, u32[]{:S(2)}, u32[]{:S(2)}) collective-permute-start(f32[8,128]{1,0:T(8,128)S(1)} %get-tuple-element.41), channel_id=1, source_target_pairs={{0,8},{1,9},{2,10},{3,11},{4,12},{5,13},{6,14},{7,15},{8,0},{9,1},... | collective-permute-start | bytes 12296 | tf_op jit(solution)/shard_map/ppermute | solution.py:374
  109.5 3.6 %collective-permute-start.17 = (f32[8,128]{1,0:T(8,128)S(1)}, f32[8,128]{1,0:T(8,128)S(1)}, u32[]{:S(2)}, u32[]{:S(2)}) collective-permute-start(f32[8,128]{1,0:T(8,128)S(1)} %get-tuple-element.41), channel_id=1, source_target_pairs={{0,4},{1,5},{2,6},{3,7},{4,0},{5,1},{6,2},{7,3},{8,12},{9,13},{10,... | collective-permute-start | bytes 12296 | tf_op jit(solution)/shard_map/ppermute | solution.py:374
  113.1 5.8 %collective-permute-start.22 = (f32[8,128]{1,0:T(8,128)S(1)}, f32[8,128]{1,0:T(8,128)S(1)}, u32[]{:S(2)}, u32[]{:S(2)}) collective-permute-start(f32[8,128]{1,0:T(8,128)S(1)} %add_add_fusion.1), channel_id=1, source_target_pairs={{0,3},{1,2},{2,1},{3,0},{4,7},{5,6},{6,5},{7,4},{8,11},{9,10},{10,... | collective-permute-start | bytes 12296 | tf_op jit(solution)/shard_map/ppermute | solution.py:374
  115.9 3.6 %collective-permute-start.21 = (f32[8,128]{1,0:T(8,128)S(1)}, f32[8,128]{1,0:T(8,128)S(1)}, u32[]{:S(2)}, u32[]{:S(2)}) collective-permute-start(f32[8,128]{1,0:T(8,128)S(1)} %add_add_fusion.1), channel_id=1, source_target_pairs={{0,2},{1,3},{2,0},{3,1},{4,6},{5,7},{6,4},{7,5},{8,10},{9,11},{10,... | collective-permute-start | bytes 12296 | tf_op jit(solution)/shard_map/ppermute | solution.py:374
  117.4 2.1 %collective-permute-start.20 = (f32[8,128]{1,0:T(8,128)S(1)}, f32[8,128]{1,0:T(8,128)S(1)}, u32[]{:S(2)}, u32[]{:S(2)}) collective-permute-start(f32[8,128]{1,0:T(8,128)S(1)} %add_add_fusion.1), channel_id=1, source_target_pairs={{0,1},{1,0},{2,3},{3,2},{4,5},{5,4},{6,7},{7,6},{8,9},{9,8},{10,11... | collective-permute-start | bytes 12296 | tf_op jit(solution)/shard_map/ppermute | solution.py:374
  (2 other events, 46.4 us)

commit v17 on v16

--- a/solution.py
+++ b/solution.py
@@ -15,6 +15,8 @@
 KDIM = 128
 ROWS = 512
 PARTS = 2
+PIECE = 256
+STRIP = 64
 FRONT = 3
 HELD = 4
 TAIL = 128
@@ -59,20 +61,22 @@
     return (jnp.exp2(19.0 * lax.log2(u)) * (1.0 - u)).astype(BF16)
 
 
-def tile_unit(left, right, vec, tile_ref, width, strip):
-    pieces = [slice(at, at + width) for at in range(0, right.shape[1], width)]
+def tile_unit(left, right, vec, tile_ref, edge, ahead):
+    width = right.shape[1]
+    begins = [0] + list(range(edge, width, PIECE)) + [width]
+    pieces = [slice(begin, end) for begin, end in zip(begins, begins[1:])]
     gram = lambda piece: jnp.dot(left, right[:, piece], preferred_element_type=F32)
     product = lambda part: jnp.dot(vec, part, preferred_element_type=F32)
-    dist, part, terms = gram(pieces[0]), None, []
+    dists, part, terms = [gram(piece) for piece in pieces[:ahead]], None, []
     for index, piece in enumerate(pieces):
-        following = gram(pieces[index + 1]) if index + 1 < len(pieces) else None
+        dists += [gram(later) for later in pieces[index + ahead : index + ahead + 1]]
         strips = []
-        for at in range(0, left.shape[0], strip):
-            strips.append(psi_power(dist[at : at + strip]))
-            tile_ref[at : at + strip, piece] = strips[-1]
+        for at in range(0, left.shape[0], STRIP):
+            strips.append(psi_power(dists[index][at : at + STRIP]))
+            tile_ref[at : at + STRIP, piece] = strips[-1]
         if part is not None:
             terms.append(product(part))
-        dist, part = following, jnp.concatenate(strips, axis=0)
+        part = jnp.concatenate(strips, axis=0)
     return jnp.concatenate(terms + [product(part)], axis=1)
 
 
@@ -96,7 +100,7 @@
         def col_step(col, at):
             sum_ref[:, piece(col)] += tile_unit(
                 left_ref[piece(row), :], right_ref[:, piece(col)], vec_ref[:, piece(row)],
-                tile_ref.at[at], 256, 64,
+                tile_ref.at[at], PIECE, 1,
             )
             save(at).start()
 
@@ -187,7 +191,7 @@
     return fetch
 
 
-def half_tiles(piece, strip, slots_ref, right_ref, fetch, front_ref, back_ref, sum_ref, left_ref, vec_ref, pay_ref, sem_ref):
+def half_tiles(edge, ahead, slots_ref, right_ref, fetch, front_ref, back_ref, sum_ref, left_ref, vec_ref, pay_ref, sem_ref):
     slot, step = pl.program_id(0), pl.program_id(1)
 
     @pl.when((slot == 0) & (step == 0) & (slots_ref[0] > 0))
@@ -215,7 +219,7 @@
         for tile_ref, here in ((front_ref, slot < FRONT), (back_ref, slot >= FRONT)):
             @pl.when(here)
             def _():
-                sum_ref[...] += tile_unit(left, right_ref[...], vec, tile_ref.at[0], piece, strip)
+                sum_ref[...] += tile_unit(left, right_ref[...], vec, tile_ref.at[0], edge, ahead)
 
 
 def pair_zero_kernel(block_at, me_ref, right_ref, *refs):
@@ -246,7 +250,7 @@
 
     fetch = fetch_from(block_at, block_refs, slots_ref, pay_ref, sem_ref)
     half_tiles(
-        256, 128, slots_ref, right_ref, fetch, front_ref, back_ref, sum_ref, left_ref, vec_ref, pay_ref, sem_ref
+        PIECE // 2, 1, slots_ref, right_ref, fetch, front_ref, back_ref, sum_ref, left_ref, vec_ref, pay_ref, sem_ref
     )
 
 
@@ -261,7 +265,7 @@
 
     fetch = fetch_from(block_at, block_refs, slots_ref, pay_ref, sem_ref)
     half_tiles(
-        512, 64, slots_ref, right_ref, fetch, front_ref, back_ref, image_ref, left_ref, vec_ref, pay_ref, sem_ref
+        PIECE, 2, slots_ref, right_ref, fetch, front_ref, back_ref, image_ref, left_ref, vec_ref, pay_ref, sem_ref
     )
 
     @pl.when((slot == pl.num_programs(0) - 1) & (step == pl.num_programs(1) - 1))

time: 121 us -> 119 us (0.983)
  the two profiles are of different devices: /device:TPU:0 before, /device:TPU:11 now
where the time goes in v17:
time: 119 us; the launch traced here: 118 us
  starting transfers between devices  62.3 us (52%)
  Pallas kernels  37.8 us (32%)
  waiting for transfers between devices  15.3 us (13%)
    ppermute x23, starting transfers between devices, swap(): return lax.ppermute(value, 'row', [(i, i ^ mask) for i in range(count)])  62.3 us
    ppermute x23, waiting for transfers between devices, swap(): return lax.ppermute(value, 'row', [(i, i ^ mask) for i in range(count)])  15.3 us
    pallas_call x2, Pallas kernels, own_part(): pl.pallas_call(functools.partial(own_kernel, rows), in_specs=[vmem, vmem,...  9.61 us
    pallas_call x1, Pallas kernels, local(): pl.pallas_call(functools.partial(pair_one_kernel, one_at), grid_spec=pltp...  9.51 us
    pallas_call x1, Pallas kernels, local(): pl.pallas_call(functools.partial(pair_zero_kernel, zero_at), grid_spec=pl...  9.48 us
    pallas_call x2, Pallas kernels, local(): pl.pallas_call(functools.partial(own_again_kernel, blocks), in_specs=[any...  4.34 us
  transfers between devices with their start and end apart: 23, of which 7 were waited for; matrix products, arithmetic and copies ran while one was open for 0% of the time, Pallas kernels for 21%

profile of v17, /device:TPU:11, one launch (start us, length us, event | category | flops | bytes accessed | tf_op | source)
XLA Modules:
  0.0 118.2 jit_solution(6518433015691153408)
XLA Ops:
  2.6 1.4 %collective-permute-start.2 = (bf16[96,512]{1,0:T(8,128)(2,1)S(1)}, bf16[96,512]{1,0:T(8,128)(2,1)S(1)}, u32[]{:S(2)}, u32[]{:S(2)}) collective-permute-start(bf16[96,512]{1,0:T(8,128)(2,1)S(1)} %get-tuple-element.26), channel_id=1, source_target_pairs={{0,12},{1,13},{2,14},{3,15},{4,8},{5,9},{6,10},{7,11},{8,4},{9,5},... | collective-permute-start | bytes 294920 | tf_op jit(solution)/shard_map/ppermute | solution.py:378
  6.1 4.0 %own_tile_0.1 = (bf16[4,512,512]{2,1,0:T(8,128)(2,1)}, f32[8,2048]{1,0:T(8,128)S(1)}) custom-call(bf16[2048,128]{1,0:T(8,128)(2,1)S(1)} %get-tuple-element.23.left_ref, bf16[128,2048]{1,0:T(8,128)(2,1)S(1)} %get-tuple-element.22.right_ref.arrived_ref, bf16[8,2048]{1,0:T(8,128)(2,1)S(1)} %get-tuple-element.24.vec_ref, ...), custom_call_target="tpu_custom_call" | custom-call | flops 5000000000 | bytes 2097152 | tf_op jit(solution)/shard_map/own_tile_0/pallas_call | solution.py:468
  10.1 1.3 %collective-permute-start.8 = (bf16[80,512]{1,0:T(8,128)(2,1)S(1)}, bf16[80,512]{1,0:T(8,128)(2,1)S(1)}, u32[]{:S(2)}, u32[]{:S(2)}) collective-permute-start(bf16[80,512]{1,0:T(8,128)(2,1)S(1)} %gate.6), channel_id=1, source_target_pairs={{0,12},{1,13},{2,14},{3,15},{4,8},{5,9},{6,10},{7,11},{8,4},{9,5},... | collective-permute-start | bytes 245768 | tf_op jit(solution)/shard_map/ppermute | solution.py:378
  11.4 1.3 %collective-permute-start.7 = (bf16[80,512]{1,0:T(8,128)(2,1)S(1)}, bf16[80,512]{1,0:T(8,128)(2,1)S(1)}, u32[]{:S(2)}, u32[]{:S(2)}) collective-permute-start(bf16[80,512]{1,0:T(8,128)(2,1)S(1)} %gate.6), channel_id=1, source_target_pairs={{0,8},{1,9},{2,10},{3,11},{4,12},{5,13},{6,14},{7,15},{8,0},{9,1},... | collective-permute-start | bytes 245768 | tf_op jit(solution)/shard_map/ppermute | solution.py:378
  13.8 2.1 %collective-permute-start.4 = (bf16[384,512]{1,0:T(8,128)(2,1)S(1)}, bf16[384,512]{1,0:T(8,128)(2,1)S(1)}, u32[]{:S(2)}, u32[]{:S(2)}) collective-permute-start(bf16[384,512]{1,0:T(8,128)(2,1)S(1)} %gate.4.arrived_ref.refs_2_), channel_id=1, source_target_pairs={{0,1},{1,0},{2,3},{3,2},{4,5},{5,4},{6,7},{7,6},{8,9},{9,8},{10,11... | collective-permute-start | bytes 1179656 | tf_op jit(solution)/shard_map/ppermute | solution.py:378
  16.0 1.3 %collective-permute-start.3 = (bf16[384,512]{1,0:T(8,128)(2,1)S(1)}, bf16[384,512]{1,0:T(8,128)(2,1)S(1)}, u32[]{:S(2)}, u32[]{:S(2)}) collective-permute-start(bf16[384,512]{1,0:T(8,128)(2,1)S(1)} %gate.4.arrived_ref.refs_2_), channel_id=1, source_target_pairs={{0,2},{1,3},{2,0},{3,1},{4,6},{5,7},{6,4},{7,5},{8,10},{9,11},{10,... | collective-permute-start | bytes 1179656 | tf_op jit(solution)/shard_map/ppermute | solution.py:378
  17.2 5.6 %own_tile_1.1 = (bf16[6,512,512]{2,1,0:T(8,128)(2,1)}, f32[8,2048]{1,0:T(8,128)S(1)}) custom-call(bf16[2048,128]{1,0:T(8,128)(2,1)S(1)} %get-tuple-element.23.left_ref, bf16[128,2048]{1,0:T(8,128)(2,1)S(1)} %get-tuple-element.22.right_ref.arrived_ref, bf16[8,2048]{1,0:T(8,128)(2,1)S(1)} %get-tuple-element.24.vec_ref, ...), custom_call_target="tpu_custom_call" | custom-call | flops 5000000000 | bytes 3145728 | tf_op jit(solution)/shard_map/own_tile_1/pallas_call | solution.py:468
  22.8 3.8 %collective-permute-done.3.refs_0_ = bf16[384,512]{1,0:T(8,128)(2,1)S(1)} collective-permute-done((bf16[384,512]{1,0:T(8,128)(2,1)S(1)}, bf16[384,512]{1,0:T(8,128)(2,1)S(1)}, u32[]{:S(2)}, u32[]{:S(2)}) %collective-permute-start.3) | collective-permute-done | bytes 393248 | tf_op jit(solution)/shard_map/ppermute | solution.py:378
  29.5 9.5 %pair_zero.1 = (bf16[3,1024,2048]{2,1,0:T(8,128)(2,1)S(1)}, bf16[2,1024,2048]{2,1,0:T(8,128)(2,1)}, f32[8,2048]{1,0:T(8,128)S(1)}, s32[7]{0:T(128)S(1)}) custom-call(s32[1]{0:T(128)} %bitcast.me_ref, bf16[128,2048]{1,0:T(8,128)(2,1)S(1)} %get-tuple-element.22.right_ref.arrived_ref, f32[8,2048]{1,0:T(8,128)S(1)} %get-tuple-element.25.refs_1_.refs_0_, ...), custom_call_target="tpu_custom_call" | custom-call | tf_op jit(solution)/shard_map/pair_zero/pallas_call | solution.py:527
  39.0 4.7 %collective-permute-done.9.refs_1_ = bf16[320,512]{1,0:T(8,128)(2,1)} collective-permute-done((bf16[320,512]{1,0:T(8,128)(2,1)S(1)}, bf16[320,512]{1,0:T(8,128)(2,1)}, u32[]{:S(2)}, u32[]{:S(2)}) %collective-permute-start.9) | collective-permute-done | bytes 327712 | tf_op jit(solution)/shard_map/ppermute | solution.py:378
  43.8 9.5 %pair_one.1 = (bf16[3,1024,2048]{2,1,0:T(8,128)(2,1)S(1)}, bf16[2,1024,2048]{2,1,0:T(8,128)(2,1)}, f32[8,2048]{1,0:T(8,128)S(1)}, bf16[8,2176]{1,0:T(8,128)(2,1)S(1)}) custom-call(s32[7]{0:T(128)S(1)} %get-tuple-element.28.slots_ref, bf16[128,2048]{1,0:T(8,128)(2,1)S(1)} %get-tuple-element.22.right_ref.arrived_ref, ...), custom_call_target="tpu_custom_call" | custom-call | tf_op jit(solution)/shard_map/pair_one/pallas_call | solution.py:547
  53.3 28.0 %collective-permute-start.14 = (bf16[1,8,2176]{2,1,0:T(8,128)(2,1)S(1)}, bf16[1,8,2176]{2,1,0:T(8,128)(2,1)S(1)}, u32[]{:S(2)}, u32[]{:S(2)}) collective-permute-start(bf16[1,8,2176]{2,1,0:T(8,128)(2,1)S(1)} %bitcast.5), channel_id=1, source_target_pairs={{0,12},{1,13},{2,14},{3,15},{4,8},{5,9},{6,10},{7,11},{8,4},{9,5},... | collective-permute-start | bytes 104456 | tf_op jit(solution)/shard_map/ppermute | solution.py:378
  81.2 5.0 %collective-permute-start.13 = (bf16[1,8,2176]{2,1,0:T(8,128)(2,1)S(1)}, bf16[1,8,2176]{2,1,0:T(8,128)(2,1)S(1)}, u32[]{:S(2)}, u32[]{:S(2)}) collective-permute-start(bf16[1,8,2176]{2,1,0:T(8,128)(2,1)S(1)} %bitcast.6), channel_id=1, source_target_pairs={{0,8},{1,9},{2,10},{3,11},{4,12},{5,13},{6,14},{7,15},{8,0},{9,1},... | collective-permute-start | bytes 104456 | tf_op jit(solution)/shard_map/ppermute | solution.py:378
  86.3 2.4 %own_again_1.1.refs_1_ = f32[8,2048]{1,0:T(8,128)S(1)} custom-call(bf16[6,512,512]{2,1,0:T(8,128)(2,1)} %get-tuple-element.38.in_ref, bf16[8,2176]{1,0:T(8,128)(2,1)S(1)} %get-tuple-element.35.vec_ref), custom_call_target="tpu_custom_call" | custom-call | flops 5000000000 | bytes 3145728 | tf_op jit(solution)/shard_map/own_again_1/pallas_call | solution.py:565
  89.1 1.2 %collective-permute-start.15 = (bf16[4,8,2176]{2,1,0:T(8,128)(2,1)S(1)}, bf16[4,8,2176]{2,1,0:T(8,128)(2,1)S(1)}, u32[]{:S(2)}, u32[]{:S(2)}) collective-permute-start(bf16[4,8,2176]{2,1,0:T(8,128)(2,1)S(1)} %pad_maximum_fusion.2), channel_id=1, source_target_pairs={{0,2},{1,3},{2,0},{3,1},{4,6},{5,7},{6,4},{7,5},{8,10},{9,11},{10,... | collective-permute-start | bytes 417800 | tf_op jit(solution)/shard_map/ppermute | solution.py:378
  90.3 3.3 %collective-permute-done.15 = bf16[4,8,2176]{2,1,0:T(8,128)(2,1)S(1)} collective-permute-done((bf16[4,8,2176]{2,1,0:T(8,128)(2,1)S(1)}, bf16[4,8,2176]{2,1,0:T(8,128)(2,1)S(1)}, u32[]{:S(2)}, u32[]{:S(2)}) %collective-permute-start.15) | collective-permute-done | bytes 139296 | tf_op jit(solution)/shard_map/ppermute | solution.py:378
  93.7 1.6 %collective-permute-start.16 = (bf16[8,8,2176]{2,1,0:T(8,128)(2,1)S(1)}, bf16[8,8,2176]{2,1,0:T(8,128)(2,1)S(1)}, u32[]{:S(2)}, u32[]{:S(2)}) collective-permute-start(bf16[8,8,2176]{2,1,0:T(8,128)(2,1)S(1)} %get-tuple-element.47), channel_id=1, source_target_pairs={{0,1},{1,0},{2,3},{3,2},{4,5},{5,4},{6,7},{7,6},{8,9},{9,8},{10,11... | collective-permute-start | bytes 835592 | tf_op jit(solution)/shard_map/ppermute | solution.py:378
  95.3 2.0 %own_again_0.1.refs_0_ = f32[8,2048]{1,0:T(8,128)S(1)} custom-call(bf16[4,512,512]{2,1,0:T(8,128)(2,1)} %get-tuple-element.37.in_ref, bf16[8,2176]{1,0:T(8,128)(2,1)S(1)} %get-tuple-element.35.vec_ref), custom_call_target="tpu_custom_call" | custom-call | flops 5000000000 | bytes 2097152 | tf_op jit(solution)/shard_map/own_again_0/pallas_call | solution.py:565
  97.4 2.2 %pair_again.1 = (f32[32,2048]{1,0:T(8,128)S(1)}, f32[8,128]{1,0:T(8,128)S(1)}, f32[8,128]{1,0:T(8,128)S(1)}) custom-call(s32[7]{0:T(128)S(1)} %get-tuple-element.28.slots_ref, bf16[3,1024,2048]{2,1,0:T(8,128)(2,1)S(1)} %get-tuple-element.29.front_zero_ref, bf16[3,1024,2048]{2,1,0:T(8,128)(2,1)S(1)} %get-tuple-element.32.front_one_ref, ...), custom_call_target="tpu_custom_call" | custom-call | tf_op jit(solution)/shard_map/pair_again/pallas_call | solution.py:583
  99.6 7.2 %collective-permute-start.19 = (f32[8,128]{1,0:T(8,128)S(1)}, f32[8,128]{1,0:T(8,128)S(1)}, u32[]{:S(2)}, u32[]{:S(2)}) collective-permute-start(f32[8,128]{1,0:T(8,128)S(1)} %get-tuple-element.41), channel_id=1, source_target_pairs={{0,12},{1,13},{2,14},{3,15},{4,8},{5,9},{6,10},{7,11},{8,4},{9,5},... | collective-permute-start | bytes 12296 | tf_op jit(solution)/shard_map/ppermute | solution.py:378
  106.9 2.6 %collective-permute-start.18 = (f32[8,128]{1,0:T(8,128)S(1)}, f32[8,128]{1,0:T(8,128)S(1)}, u32[]{:S(2)}, u32[]{:S(2)}) collective-permute-start(f32[8,128]{1,0:T(8,128)S(1)} %get-tuple-element.41), channel_id=1, source_target_pairs={{0,8},{1,9},{2,10},{3,11},{4,12},{5,13},{6,14},{7,15},{8,0},{9,1},... | collective-permute-start | bytes 12296 | tf_op jit(solution)/shard_map/ppermute | solution.py:378
  110.5 1.4 %collective-permute-done.17 = f32[8,128]{1,0:T(8,128)S(1)} collective-permute-done((f32[8,128]{1,0:T(8,128)S(1)}, f32[8,128]{1,0:T(8,128)S(1)}, u32[]{:S(2)}, u32[]{:S(2)}) %collective-permute-start.17) | collective-permute-done | bytes 4128 | tf_op jit(solution)/shard_map/ppermute | solution.py:378
  111.9 2.8 %collective-permute-start.22 = (f32[8,128]{1,0:T(8,128)S(1)}, f32[8,128]{1,0:T(8,128)S(1)}, u32[]{:S(2)}, u32[]{:S(2)}) collective-permute-start(f32[8,128]{1,0:T(8,128)S(1)} %add_add_fusion.1), channel_id=1, source_target_pairs={{0,3},{1,2},{2,1},{3,0},{4,7},{5,6},{6,5},{7,4},{8,11},{9,10},{10,... | collective-permute-start | bytes 12296 | tf_op jit(solution)/shard_map/ppermute | solution.py:378
  115.2 1.5 %curve_order.1 = f32[32,2048]{1,0:T(8,128)S(1)} custom-call(f32[32,2048]{1,0:T(8,128)S(1)} %get-tuple-element.40.rows_ref, s32[1,2048]{1,0:T(1,128)S(1)} %copy-done.2), custom_call_target="tpu_custom_call" | custom-call | tf_op jit(solution)/shard_map/curve_order/pallas_call | solution.py:621
  (55 shorter events, 11.6 us)
Async XLA Ops:
  2.6 10.1 %collective-permute-start.2 = (bf16[96,512]{1,0:T(8,128)(2,1)S(1)}, bf16[96,512]{1,0:T(8,128)(2,1)S(1)}, u32[]{:S(2)}, u32[]{:S(2)}) collective-permute-start(bf16[96,512]{1,0:T(8,128)(2,1)S(1)} %get-tuple-element.26), channel_id=1, source_target_pairs={{0,12},{1,13},{2,14},{3,15},{4,8},{5,9},{6,10},{7,11},{8,4},{9,5},... | collective-permute-start | bytes 294920 | tf_op jit(solution)/shard_map/ppermute | solution.py:378
  3.9 9.8 %collective-permute-start.1 = (bf16[96,512]{1,0:T(8,128)(2,1)S(1)}, bf16[96,512]{1,0:T(8,128)(2,1)S(1)}, u32[]{:S(2)}, u32[]{:S(2)}) collective-permute-start(bf16[96,512]{1,0:T(8,128)(2,1)S(1)} %get-tuple-element.26), channel_id=1, source_target_pairs={{0,8},{1,9},{2,10},{3,11},{4,12},{5,13},{6,14},{7,15},{8,0},{9,1},... | collective-permute-start | bytes 294920 | tf_op jit(solution)/shard_map/ppermute | solution.py:378
  5.0 8.7 %collective-permute-start = (bf16[96,512]{1,0:T(8,128)(2,1)S(1)}, bf16[96,512]{1,0:T(8,128)(2,1)S(1)}, u32[]{:S(2)}, u32[]{:S(2)}) collective-permute-start(bf16[96,512]{1,0:T(8,128)(2,1)S(1)} %get-tuple-element.26), channel_id=1, source_target_pairs={{0,4},{1,5},{2,6},{3,7},{4,0},{5,1},{6,2},{7,3},{8,12},{9,13},{10,... | collective-permute-start | bytes 294920 | tf_op jit(solution)/shard_map/ppermute | solution.py:378
  10.1 17.4 %collective-permute-start.8 = (bf16[80,512]{1,0:T(8,128)(2,1)S(1)}, bf16[80,512]{1,0:T(8,128)(2,1)S(1)}, u32[]{:S(2)}, u32[]{:S(2)}) collective-permute-start(bf16[80,512]{1,0:T(8,128)(2,1)S(1)} %gate.6), channel_id=1, source_target_pairs={{0,12},{1,13},{2,14},{3,15},{4,8},{5,9},{6,10},{7,11},{8,4},{9,5},... | collective-permute-start | bytes 245768 | tf_op jit(solution)/shard_map/ppermute | solution.py:378
  11.4 16.1 %collective-permute-start.7 = (bf16[80,512]{1,0:T(8,128)(2,1)S(1)}, bf16[80,512]{1,0:T(8,128)(2,1)S(1)}, u32[]{:S(2)}, u32[]{:S(2)}) collective-permute-start(bf16[80,512]{1,0:T(8,128)(2,1)S(1)} %gate.6), channel_id=1, source_target_pairs={{0,8},{1,9},{2,10},{3,11},{4,12},{5,13},{6,14},{7,15},{8,0},{9,1},... | collective-permute-start | bytes 245768 | tf_op jit(solution)/shard_map/ppermute | solution.py:378
  12.6 14.9 %collective-permute-start.6 = (bf16[80,512]{1,0:T(8,128)(2,1)S(1)}, bf16[80,512]{1,0:T(8,128)(2,1)S(1)}, u32[]{:S(2)}, u32[]{:S(2)}) collective-permute-start(bf16[80,512]{1,0:T(8,128)(2,1)S(1)} %gate.6), channel_id=1, source_target_pairs={{0,4},{1,5},{2,6},{3,7},{4,0},{5,1},{6,2},{7,3},{8,12},{9,13},{10,... | collective-permute-start | bytes 245768 | tf_op jit(solution)/shard_map/ppermute | solution.py:378
  13.8 29.9 %copy-start = (f32[8,2048]{1,0:T(8,128)S(1)}, f32[8,2048]{1,0:T(8,128)}, u32[]{:S(2)}) copy-start(f32[8,2048]{1,0:T(8,128)} %rhs_ref.5) | copy-start | bytes 196612
  13.8 15.7 %collective-permute-start.4 = (bf16[384,512]{1,0:T(8,128)(2,1)S(1)}, bf16[384,512]{1,0:T(8,128)(2,1)S(1)}, u32[]{:S(2)}, u32[]{:S(2)}) collective-permute-start(bf16[384,512]{1,0:T(8,128)(2,1)S(1)} %gate.4.arrived_ref.refs_2_), channel_id=1, source_target_pairs={{0,1},{1,0},{2,3},{3,2},{4,5},{5,4},{6,7},{7,6},{8,9},{9,8},{10,11... | collective-permute-start | bytes 1179656 | tf_op jit(solution)/shard_map/ppermute | solution.py:378
  16.0 10.7 %collective-permute-start.3 = (bf16[384,512]{1,0:T(8,128)(2,1)S(1)}, bf16[384,512]{1,0:T(8,128)(2,1)S(1)}, u32[]{:S(2)}, u32[]{:S(2)}) collective-permute-start(bf16[384,512]{1,0:T(8,128)(2,1)S(1)} %gate.4.arrived_ref.refs_2_), channel_id=1, source_target_pairs={{0,2},{1,3},{2,0},{3,1},{4,6},{5,7},{6,4},{7,5},{8,10},{9,11},{10,... | collective-permute-start | bytes 1179656 | tf_op jit(solution)/shard_map/ppermute | solution.py:378
  26.7 2.8 %collective-permute-start.5 = (bf16[384,512]{1,0:T(8,128)(2,1)S(1)}, bf16[384,512]{1,0:T(8,128)(2,1)S(1)}, u32[]{:S(2)}, u32[]{:S(2)}) collective-permute-start(bf16[384,512]{1,0:T(8,128)(2,1)S(1)} %gate.5.refs_3_), channel_id=1, source_target_pairs={{0,1},{1,0},{2,3},{3,2},{4,5},{5,4},{6,7},{7,6},{8,9},{9,8},{10,11... | collective-permute-start | bytes 1179656 | tf_op jit(solution)/shard_map/ppermute | solution.py:378
  27.6 11.4 %collective-permute-start.11 = (bf16[320,512]{1,0:T(8,128)(2,1)S(1)}, bf16[320,512]{1,0:T(8,128)(2,1)S(1)}, u32[]{:S(2)}, u32[]{:S(2)}) collective-permute-start(bf16[320,512]{1,0:T(8,128)(2,1)S(1)} %gate.7.refs_0_), channel_id=1, source_target_pairs={{0,3},{1,2},{2,1},{3,0},{4,7},{5,6},{6,5},{7,4},{8,11},{9,10},{10,... | collective-permute-start | bytes 983048 | tf_op jit(solution)/shard_map/ppermute | solution.py:378
  28.8 10.2 %collective-permute-start.10 = (bf16[320,512]{1,0:T(8,128)(2,1)S(1)}, bf16[320,512]{1,0:T(8,128)(2,1)S(1)}, u32[]{:S(2)}, u32[]{:S(2)}) collective-permute-start(bf16[320,512]{1,0:T(8,128)(2,1)S(1)} %gate.7.refs_0_), channel_id=1, source_target_pairs={{0,1},{1,0},{2,3},{3,2},{4,5},{5,4},{6,7},{7,6},{8,9},{9,8},{10,11... | collective-permute-start | bytes 983048 | tf_op jit(solution)/shard_map/ppermute | solution.py:378
  29.3 14.5 %collective-permute-start.9 = (bf16[320,512]{1,0:T(8,128)(2,1)S(1)}, bf16[320,512]{1,0:T(8,128)(2,1)}, u32[]{:S(2)}, u32[]{:S(2)}) collective-permute-start(bf16[320,512]{1,0:T(8,128)(2,1)S(1)} %gate.7.refs_0_), channel_id=1, source_target_pairs={{0,2},{1,3},{2,0},{3,1},{4,6},{5,7},{6,4},{7,5},{8,10},{9,11},{10,... | collective-permute-start | bytes 983048 | tf_op jit(solution)/shard_map/ppermute | solution.py:378
  53.3 35.4 %collective-permute-start.14 = (bf16[1,8,2176]{2,1,0:T(8,128)(2,1)S(1)}, bf16[1,8,2176]{2,1,0:T(8,128)(2,1)S(1)}, u32[]{:S(2)}, u32[]{:S(2)}) collective-permute-start(bf16[1,8,2176]{2,1,0:T(8,128)(2,1)S(1)} %bitcast.5), channel_id=1, source_target_pairs={{0,12},{1,13},{2,14},{3,15},{4,8},{5,9},{6,10},{7,11},{8,4},{9,5},... | collective-permute-start | bytes 104456 | tf_op jit(solution)/shard_map/ppermute | solution.py:378
  81.2 7.4 %collective-permute-start.13 = (bf16[1,8,2176]{2,1,0:T(8,128)(2,1)S(1)}, bf16[1,8,2176]{2,1,0:T(8,128)(2,1)S(1)}, u32[]{:S(2)}, u32[]{:S(2)}) collective-permute-start(bf16[1,8,2176]{2,1,0:T(8,128)(2,1)S(1)} %bitcast.6), channel_id=1, source_target_pairs={{0,8},{1,9},{2,10},{3,11},{4,12},{5,13},{6,14},{7,15},{8,0},{9,1},... | collective-permute-start | bytes 104456 | tf_op jit(solution)/shard_map/ppermute | solution.py:378
  86.3 2.8 %collective-permute-start.12 = (bf16[1,8,2176]{2,1,0:T(8,128)(2,1)S(1)}, bf16[1,8,2176]{2,1,0:T(8,128)(2,1)S(1)}, u32[]{:S(2)}, u32[]{:S(2)}) collective-permute-start(bf16[1,8,2176]{2,1,0:T(8,128)(2,1)S(1)} %bitcast.7), channel_id=1, source_target_pairs={{0,4},{1,5},{2,6},{3,7},{4,0},{5,1},{6,2},{7,3},{8,12},{9,13},{10,... | collective-permute-start | bytes 104456 | tf_op jit(solution)/shard_map/ppermute | solution.py:378
  89.1 4.6 %collective-permute-start.15 = (bf16[4,8,2176]{2,1,0:T(8,128)(2,1)S(1)}, bf16[4,8,2176]{2,1,0:T(8,128)(2,1)S(1)}, u32[]{:S(2)}, u32[]{:S(2)}) collective-permute-start(bf16[4,8,2176]{2,1,0:T(8,128)(2,1)S(1)} %pad_maximum_fusion.2), channel_id=1, source_target_pairs={{0,2},{1,3},{2,0},{3,1},{4,6},{5,7},{6,4},{7,5},{8,10},{9,11},{10,... | collective-permute-start | bytes 417800 | tf_op jit(solution)/shard_map/ppermute | solution.py:378
  93.7 3.6 %collective-permute-start.16 = (bf16[8,8,2176]{2,1,0:T(8,128)(2,1)S(1)}, bf16[8,8,2176]{2,1,0:T(8,128)(2,1)S(1)}, u32[]{:S(2)}, u32[]{:S(2)}) collective-permute-start(bf16[8,8,2176]{2,1,0:T(8,128)(2,1)S(1)} %get-tuple-element.47), channel_id=1, source_target_pairs={{0,1},{1,0},{2,3},{3,2},{4,5},{5,4},{6,7},{7,6},{8,9},{9,8},{10,11... | collective-permute-start | bytes 835592 | tf_op jit(solution)/shard_map/ppermute | solution.py:378
  99.6 9.8 %collective-permute-start.19 = (f32[8,128]{1,0:T(8,128)S(1)}, f32[8,128]{1,0:T(8,128)S(1)}, u32[]{:S(2)}, u32[]{:S(2)}) collective-permute-start(f32[8,128]{1,0:T(8,128)S(1)} %get-tuple-element.41), channel_id=1, source_target_pairs={{0,12},{1,13},{2,14},{3,15},{4,8},{5,9},{6,10},{7,11},{8,4},{9,5},... | collective-permute-start | bytes 12296 | tf_op jit(solution)/shard_map/ppermute | solution.py:378
  106.9 3.6 %collective-permute-start.18 = (f32[8,128]{1,0:T(8,128)S(1)}, f32[8,128]{1,0:T(8,128)S(1)}, u32[]{:S(2)}, u32[]{:S(2)}) collective-permute-start(f32[8,128]{1,0:T(8,128)S(1)} %get-tuple-element.41), channel_id=1, source_target_pairs={{0,8},{1,9},{2,10},{3,11},{4,12},{5,13},{6,14},{7,15},{8,0},{9,1},... | collective-permute-start | bytes 12296 | tf_op jit(solution)/shard_map/ppermute | solution.py:378
  109.5 2.5 %collective-permute-start.17 = (f32[8,128]{1,0:T(8,128)S(1)}, f32[8,128]{1,0:T(8,128)S(1)}, u32[]{:S(2)}, u32[]{:S(2)}) collective-permute-start(f32[8,128]{1,0:T(8,128)S(1)} %get-tuple-element.41), channel_id=1, source_target_pairs={{0,4},{1,5},{2,6},{3,7},{4,0},{5,1},{6,2},{7,3},{8,12},{9,13},{10,... | collective-permute-start | bytes 12296 | tf_op jit(solution)/shard_map/ppermute | solution.py:378
  111.9 4.7 %collective-permute-start.22 = (f32[8,128]{1,0:T(8,128)S(1)}, f32[8,128]{1,0:T(8,128)S(1)}, u32[]{:S(2)}, u32[]{:S(2)}) collective-permute-start(f32[8,128]{1,0:T(8,128)S(1)} %add_add_fusion.1), channel_id=1, source_target_pairs={{0,3},{1,2},{2,1},{3,0},{4,7},{5,6},{6,5},{7,4},{8,11},{9,10},{10,... | collective-permute-start | bytes 12296 | tf_op jit(solution)/shard_map/ppermute | solution.py:378
  114.7 2.5 %collective-permute-start.21 = (f32[8,128]{1,0:T(8,128)S(1)}, f32[8,128]{1,0:T(8,128)S(1)}, u32[]{:S(2)}, u32[]{:S(2)}) collective-permute-start(f32[8,128]{1,0:T(8,128)S(1)} %add_add_fusion.1), channel_id=1, source_target_pairs={{0,2},{1,3},{2,0},{3,1},{4,6},{5,7},{6,4},{7,5},{8,10},{9,11},{10,... | collective-permute-start | bytes 12296 | tf_op jit(solution)/shard_map/ppermute | solution.py:378
  114.7 2.5 %collective-permute-start.20 = (f32[8,128]{1,0:T(8,128)S(1)}, f32[8,128]{1,0:T(8,128)S(1)}, u32[]{:S(2)}, u32[]{:S(2)}) collective-permute-start(f32[8,128]{1,0:T(8,128)S(1)} %add_add_fusion.1), channel_id=1, source_target_pairs={{0,1},{1,0},{2,3},{3,2},{4,5},{5,4},{6,7},{7,6},{8,9},{9,8},{10,11... | collective-permute-start | bytes 12296 | tf_op jit(solution)/shard_map/ppermute | solution.py:378
  (2 other events, 47.8 us)

commit v18 on v16

--- a/solution.py
+++ b/solution.py
@@ -15,6 +15,8 @@
 KDIM = 128
 ROWS = 512
 PARTS = 2
+PIECE = 256
+STRIP = 64
 FRONT = 3
 HELD = 4
 TAIL = 128
@@ -52,6 +54,16 @@
     return jnp.transpose(jnp.concatenate([feat, feat, feat, norm_rows(norm, 3)], axis=0))
 
 
+def psi_chain(dist):
+    dist = jnp.maximum(dist, 1e-30)
+    radius = dist * lax.rsqrt(dist)
+    u = jnp.maximum(SHRINK - radius, 0.0)
+    two = u * u
+    four = two * two
+    eight = four * four
+    return (eight * eight * (two * (u - two))).astype(BF16)
+
+
 def psi_power(dist):
     dist = jnp.maximum(dist, 1e-30)
     radius = dist * lax.rsqrt(dist)
@@ -59,17 +71,18 @@
     return (jnp.exp2(19.0 * lax.log2(u)) * (1.0 - u)).astype(BF16)
 
 
-def tile_unit(left, right, vec, tile_ref, width, strip):
-    pieces = [slice(at, at + width) for at in range(0, right.shape[1], width)]
+def tile_unit(left, right, vec, tile_ref, psis):
+    pieces = [slice(at, at + PIECE) for at in range(0, right.shape[1], PIECE)]
     gram = lambda piece: jnp.dot(left, right[:, piece], preferred_element_type=F32)
     product = lambda part: jnp.dot(vec, part, preferred_element_type=F32)
     dist, part, terms = gram(pieces[0]), None, []
     for index, piece in enumerate(pieces):
         following = gram(pieces[index + 1]) if index + 1 < len(pieces) else None
         strips = []
-        for at in range(0, left.shape[0], strip):
-            strips.append(psi_power(dist[at : at + strip]))
-            tile_ref[at : at + strip, piece] = strips[-1]
+        for at in range(0, left.shape[0], STRIP):
+            psi = psis[len(strips) % len(psis)]
+            strips.append(psi(dist[at : at + STRIP]))
+            tile_ref[at : at + STRIP, piece] = strips[-1]
         if part is not None:
             terms.append(product(part))
         dist, part = following, jnp.concatenate(strips, axis=0)
@@ -96,7 +109,7 @@
         def col_step(col, at):
             sum_ref[:, piece(col)] += tile_unit(
                 left_ref[piece(row), :], right_ref[:, piece(col)], vec_ref[:, piece(row)],
-                tile_ref.at[at], 256, 64,
+                tile_ref.at[at], (psi_power,),
             )
             save(at).start()
 
@@ -187,7 +200,7 @@
     return fetch
 
 
-def half_tiles(piece, strip, slots_ref, right_ref, fetch, front_ref, back_ref, sum_ref, left_ref, vec_ref, pay_ref, sem_ref):
+def half_tiles(psis, slots_ref, right_ref, fetch, front_ref, back_ref, sum_ref, left_ref, vec_ref, pay_ref, sem_ref):
     slot, step = pl.program_id(0), pl.program_id(1)
 
     @pl.when((slot == 0) & (step == 0) & (slots_ref[0] > 0))
@@ -215,7 +228,7 @@
         for tile_ref, here in ((front_ref, slot < FRONT), (back_ref, slot >= FRONT)):
             @pl.when(here)
             def _():
-                sum_ref[...] += tile_unit(left, right_ref[...], vec, tile_ref.at[0], piece, strip)
+                sum_ref[...] += tile_unit(left, right_ref[...], vec, tile_ref.at[0], psis)
 
 
 def pair_zero_kernel(block_at, me_ref, right_ref, *refs):
@@ -246,7 +259,7 @@
 
     fetch = fetch_from(block_at, block_refs, slots_ref, pay_ref, sem_ref)
     half_tiles(
-        256, 128, slots_ref, right_ref, fetch, front_ref, back_ref, sum_ref, left_ref, vec_ref, pay_ref, sem_ref
+        (psi_power, psi_chain), slots_ref, right_ref, fetch, front_ref, back_ref, sum_ref, left_ref, vec_ref, pay_ref, sem_ref
     )
 
 
@@ -261,7 +274,7 @@
 
     fetch = fetch_from(block_at, block_refs, slots_ref, pay_ref, sem_ref)
     half_tiles(
-        512, 64, slots_ref, right_ref, fetch, front_ref, back_ref, image_ref, left_ref, vec_ref, pay_ref, sem_ref
+        (psi_chain,), slots_ref, right_ref, fetch, front_ref, back_ref, image_ref, left_ref, vec_ref, pay_ref, sem_ref
     )
 
     @pl.when((slot == pl.num_programs(0) - 1) & (step == pl.num_programs(1) - 1))

time: 121 us -> 121 us (level)
  Pallas kernels: 47.9 us -> 27.1 us
  waiting for transfers between devices: 16.5 us -> 29.6 us
  starting transfers between devices: 53.3 us -> 60.2 us
    ppermute x23, waiting for transfers between devices: 16.5 us -> 29.6 us  [swap(): return lax.ppermute(value, 'row', [(i, i ^ mask) for i in range(count)])]
    pallas_call x1, Pallas kernels: 14 us -> 4.45 us  [local(): pl.pallas_call(functools.partial(pair_one_kernel, one_at), grid_spec=pltp...]
    pallas_call x1, Pallas kernels: 13.8 us -> 4.94 us  [local(): pl.pallas_call(functools.partial(pair_zero_kernel, zero_at), grid_spec=pl...]
    ppermute x23, starting transfers between devices: 53.3 us -> 60.2 us  [swap(): return lax.ppermute(value, 'row', [(i, i ^ mask) for i in range(count)])]
    pallas_call x1, Pallas kernels: 3.4 us -> 1.17 us  [local(): pl.pallas_call(again_kernel, grid_spec=pltpu.PrefetchScalarGridSpec(num_s...]
  transfers between devices with their start and end apart: 23 -> 23, of which waited for: 8 -> 10; matrix products, arithmetic and copies ran while one was open for 0% -> 0% of each run, Pallas kernels for 24% -> 17%
where the time goes in v18:
time: 121 us; the launch traced here: 120 us
  starting transfers between devices  60.2 us (50%)
  waiting for transfers between devices  29.6 us (24%)
  Pallas kernels  27.1 us (22%)
    ppermute x23, starting transfers between devices, swap(): return lax.ppermute(value, 'row', [(i, i ^ mask) for i in range(count)])  60.2 us
    ppermute x23, waiting for transfers between devices, swap(): return lax.ppermute(value, 'row', [(i, i ^ mask) for i in range(count)])  29.6 us
    pallas_call x2, Pallas kernels, own_part(): pl.pallas_call(functools.partial(own_kernel, rows), in_specs=[vmem, vmem,...  9.62 us
    pallas_call x1, Pallas kernels, local(): pl.pallas_call(functools.partial(pair_zero_kernel, zero_at), grid_spec=pl...  4.94 us
    pallas_call x1, Pallas kernels, local(): pl.pallas_call(functools.partial(pair_one_kernel, one_at), grid_spec=pltp...  4.45 us
    pallas_call x2, Pallas kernels, local(): pl.pallas_call(functools.partial(own_again_kernel, blocks), in_specs=[any...  4.34 us
  transfers between devices with their start and end apart: 23, of which 10 were waited for; matrix products, arithmetic and copies ran while one was open for 0% of the time, Pallas kernels for 17%

profile of v18, /device:TPU:0, one launch (start us, length us, event | category | flops | bytes accessed | tf_op | source)
XLA Modules:
  0.0 119.8 jit_solution(17385589628808826482)
XLA Ops:
  1.4 1.2 payload.1
  2.6 5.1 %collective-permute-start.2 = (bf16[96,512]{1,0:T(8,128)(2,1)S(1)}, bf16[96,512]{1,0:T(8,128)(2,1)S(1)}, u32[]{:S(2)}, u32[]{:S(2)}) collective-permute-start(bf16[96,512]{1,0:T(8,128)(2,1)S(1)} %get-tuple-element.26), channel_id=1, source_target_pairs={{0,12},{1,13},{2,14},{3,15},{4,8},{5,9},{6,10},{7,11},{8,4},{9,5},... | collective-permute-start | bytes 294920 | tf_op jit(solution)/shard_map/ppermute | solution.py:387
  8.3 4.0 %own_tile_0.1 = (bf16[4,512,512]{2,1,0:T(8,128)(2,1)}, f32[8,2048]{1,0:T(8,128)S(1)}) custom-call(bf16[2048,128]{1,0:T(8,128)(2,1)S(1)} %get-tuple-element.23.left_ref, bf16[128,2048]{1,0:T(8,128)(2,1)S(1)} %get-tuple-element.22.right_ref.arrived_ref, bf16[8,2048]{1,0:T(8,128)(2,1)S(1)} %get-tuple-element.24.vec_ref, ...), custom_call_target="tpu_custom_call" | custom-call | flops 5000000000 | bytes 2097152 | tf_op jit(solution)/shard_map/own_tile_0/pallas_call | solution.py:477
  12.3 3.8 %collective-permute-start.8 = (bf16[80,512]{1,0:T(8,128)(2,1)S(1)}, bf16[80,512]{1,0:T(8,128)(2,1)S(1)}, u32[]{:S(2)}, u32[]{:S(2)}) collective-permute-start(bf16[80,512]{1,0:T(8,128)(2,1)S(1)} %gate.6), channel_id=1, source_target_pairs={{0,12},{1,13},{2,14},{3,15},{4,8},{5,9},{6,10},{7,11},{8,4},{9,5},... | collective-permute-start | bytes 245768 | tf_op jit(solution)/shard_map/ppermute | solution.py:387
  16.8 3.1 %collective-permute-done.1 = bf16[96,512]{1,0:T(8,128)(2,1)S(1)} collective-permute-done((bf16[96,512]{1,0:T(8,128)(2,1)S(1)}, bf16[96,512]{1,0:T(8,128)(2,1)S(1)}, u32[]{:S(2)}, u32[]{:S(2)}) %collective-permute-start.1) | collective-permute-done | bytes 98336 | tf_op jit(solution)/shard_map/ppermute | solution.py:387
  20.0 1.6 %collective-permute-start.3 = (bf16[384,512]{1,0:T(8,128)(2,1)S(1)}, bf16[384,512]{1,0:T(8,128)(2,1)S(1)}, u32[]{:S(2)}, u32[]{:S(2)}) collective-permute-start(bf16[384,512]{1,0:T(8,128)(2,1)S(1)} %gate.4.arrived_ref.refs_2_), channel_id=1, source_target_pairs={{0,2},{1,3},{2,0},{3,1},{4,6},{5,7},{6,4},{7,5},{8,10},{9,11},{10,... | collective-permute-start | bytes 1179656 | tf_op jit(solution)/shard_map/ppermute | solution.py:387
  21.6 5.6 %own_tile_1.1 = (bf16[6,512,512]{2,1,0:T(8,128)(2,1)}, f32[8,2048]{1,0:T(8,128)S(1)}) custom-call(bf16[2048,128]{1,0:T(8,128)(2,1)S(1)} %get-tuple-element.23.left_ref, bf16[128,2048]{1,0:T(8,128)(2,1)S(1)} %get-tuple-element.22.right_ref.arrived_ref, bf16[8,2048]{1,0:T(8,128)(2,1)S(1)} %get-tuple-element.24.vec_ref, ...), custom_call_target="tpu_custom_call" | custom-call | flops 5000000000 | bytes 3145728 | tf_op jit(solution)/shard_map/own_tile_1/pallas_call | solution.py:477
  27.2 4.3 %collective-permute-done.3.refs_0_ = bf16[384,512]{1,0:T(8,128)(2,1)S(1)} collective-permute-done((bf16[384,512]{1,0:T(8,128)(2,1)S(1)}, bf16[384,512]{1,0:T(8,128)(2,1)S(1)}, u32[]{:S(2)}, u32[]{:S(2)}) %collective-permute-start.3) | collective-permute-done | bytes 393248 | tf_op jit(solution)/shard_map/ppermute | solution.py:387
  31.6 1.7 %collective-permute-start.11 = (bf16[320,512]{1,0:T(8,128)(2,1)S(1)}, bf16[320,512]{1,0:T(8,128)(2,1)S(1)}, u32[]{:S(2)}, u32[]{:S(2)}) collective-permute-start(bf16[320,512]{1,0:T(8,128)(2,1)S(1)} %gate.7.refs_0_), channel_id=1, source_target_pairs={{0,3},{1,2},{2,1},{3,0},{4,7},{5,6},{6,5},{7,4},{8,11},{9,10},{10,... | collective-permute-start | bytes 983048 | tf_op jit(solution)/shard_map/ppermute | solution.py:387
  33.9 4.9 %pair_zero.1 = (bf16[3,1024,2048]{2,1,0:T(8,128)(2,1)S(1)}, bf16[2,1024,2048]{2,1,0:T(8,128)(2,1)}, f32[8,2048]{1,0:T(8,128)S(1)}, s32[7]{0:T(128)S(1)}) custom-call(s32[1]{0:T(128)} %bitcast.me_ref, bf16[128,2048]{1,0:T(8,128)(2,1)S(1)} %get-tuple-element.22.right_ref.arrived_ref, f32[8,2048]{1,0:T(8,128)S(1)} %get-tuple-element.25.refs_1_.refs_0_, ...), custom_call_target="tpu_custom_call" | custom-call | tf_op jit(solution)/shard_map/pair_zero/pallas_call | solution.py:536
  38.8 2.6 %collective-permute-done.11.refs_3_ = bf16[320,512]{1,0:T(8,128)(2,1)S(1)} collective-permute-done((bf16[320,512]{1,0:T(8,128)(2,1)S(1)}, bf16[320,512]{1,0:T(8,128)(2,1)S(1)}, u32[]{:S(2)}, u32[]{:S(2)}) %collective-permute-start.11) | collective-permute-done | bytes 327712 | tf_op jit(solution)/shard_map/ppermute | solution.py:387
  41.4 7.5 %collective-permute-done.9.refs_1_ = bf16[320,512]{1,0:T(8,128)(2,1)} collective-permute-done((bf16[320,512]{1,0:T(8,128)(2,1)S(1)}, bf16[320,512]{1,0:T(8,128)(2,1)}, u32[]{:S(2)}, u32[]{:S(2)}) %collective-permute-start.9) | collective-permute-done | bytes 327712 | tf_op jit(solution)/shard_map/ppermute | solution.py:387
  48.9 4.4 %pair_one.1 = (bf16[3,1024,2048]{2,1,0:T(8,128)(2,1)S(1)}, bf16[2,1024,2048]{2,1,0:T(8,128)(2,1)}, f32[8,2048]{1,0:T(8,128)S(1)}, bf16[8,2176]{1,0:T(8,128)(2,1)S(1)}) custom-call(s32[7]{0:T(128)S(1)} %get-tuple-element.28.slots_ref, bf16[128,2048]{1,0:T(8,128)(2,1)S(1)} %get-tuple-element.22.right_ref.arrived_ref, ...), custom_call_target="tpu_custom_call" | custom-call | tf_op jit(solution)/shard_map/pair_one/pallas_call | solution.py:556
  53.3 33.8 %collective-permute-start.14 = (bf16[1,8,2176]{2,1,0:T(8,128)(2,1)S(1)}, bf16[1,8,2176]{2,1,0:T(8,128)(2,1)S(1)}, u32[]{:S(2)}, u32[]{:S(2)}) collective-permute-start(bf16[1,8,2176]{2,1,0:T(8,128)(2,1)S(1)} %bitcast.5), channel_id=1, source_target_pairs={{0,12},{1,13},{2,14},{3,15},{4,8},{5,9},{6,10},{7,11},{8,4},{9,5},... | collective-permute-start | bytes 104456 | tf_op jit(solution)/shard_map/ppermute | solution.py:387
  87.8 2.4 %own_again_1.1.refs_1_ = f32[8,2048]{1,0:T(8,128)S(1)} custom-call(bf16[6,512,512]{2,1,0:T(8,128)(2,1)} %get-tuple-element.38.in_ref, bf16[8,2176]{1,0:T(8,128)(2,1)S(1)} %get-tuple-element.35.vec_ref), custom_call_target="tpu_custom_call" | custom-call | flops 5000000000 | bytes 3145728 | tf_op jit(solution)/shard_map/own_again_1/pallas_call | solution.py:574
  90.1 2.0 %collective-permute-done.13 = bf16[1,8,2176]{2,1,0:T(8,128)(2,1)S(1)} collective-permute-done((bf16[1,8,2176]{2,1,0:T(8,128)(2,1)S(1)}, bf16[1,8,2176]{2,1,0:T(8,128)(2,1)S(1)}, u32[]{:S(2)}, u32[]{:S(2)}) %collective-permute-start.13) | collective-permute-done | bytes 34848 | tf_op jit(solution)/shard_map/ppermute | solution.py:387
  92.4 5.8 %collective-permute-done.15 = bf16[4,8,2176]{2,1,0:T(8,128)(2,1)S(1)} collective-permute-done((bf16[4,8,2176]{2,1,0:T(8,128)(2,1)S(1)}, bf16[4,8,2176]{2,1,0:T(8,128)(2,1)S(1)}, u32[]{:S(2)}, u32[]{:S(2)}) %collective-permute-start.15) | collective-permute-done | bytes 139296 | tf_op jit(solution)/shard_map/ppermute | solution.py:387
  98.3 2.0 %own_again_0.1.refs_0_ = f32[8,2048]{1,0:T(8,128)S(1)} custom-call(bf16[4,512,512]{2,1,0:T(8,128)(2,1)} %get-tuple-element.37.in_ref, bf16[8,2176]{1,0:T(8,128)(2,1)S(1)} %get-tuple-element.35.vec_ref), custom_call_target="tpu_custom_call" | custom-call | flops 5000000000 | bytes 2097152 | tf_op jit(solution)/shard_map/own_again_0/pallas_call | solution.py:574
  100.3 1.2 pair_again.1
  101.5 9.0 %collective-permute-start.19 = (f32[8,128]{1,0:T(8,128)S(1)}, f32[8,128]{1,0:T(8,128)S(1)}, u32[]{:S(2)}, u32[]{:S(2)}) collective-permute-start(f32[8,128]{1,0:T(8,128)S(1)} %get-tuple-element.41), channel_id=1, source_target_pairs={{0,12},{1,13},{2,14},{3,15},{4,8},{5,9},{6,10},{7,11},{8,4},{9,5},... | collective-permute-start | bytes 12296 | tf_op jit(solution)/shard_map/ppermute | solution.py:387
  111.2 0.9 collective-permute-done.19
  112.1 2.9 %collective-permute-done.18 = f32[8,128]{1,0:T(8,128)S(1)} collective-permute-done((f32[8,128]{1,0:T(8,128)S(1)}, f32[8,128]{1,0:T(8,128)S(1)}, u32[]{:S(2)}, u32[]{:S(2)}) %collective-permute-start.18) | collective-permute-done | bytes 4128 | tf_op jit(solution)/shard_map/ppermute | solution.py:387
  115.1 1.0 collective-permute-start.21
  117.0 1.5 %curve_order.1 = f32[32,2048]{1,0:T(8,128)S(1)} custom-call(f32[32,2048]{1,0:T(8,128)S(1)} %get-tuple-element.40.rows_ref, s32[1,2048]{1,0:T(1,128)S(1)} %copy-done.2), custom_call_target="tpu_custom_call" | custom-call | tf_op jit(solution)/shard_map/curve_order/pallas_call | solution.py:630
  (55 shorter events, 6.7 us)
Async XLA Ops:
  2.6 13.6 %collective-permute-start.2 = (bf16[96,512]{1,0:T(8,128)(2,1)S(1)}, bf16[96,512]{1,0:T(8,128)(2,1)S(1)}, u32[]{:S(2)}, u32[]{:S(2)}) collective-permute-start(bf16[96,512]{1,0:T(8,128)(2,1)S(1)} %get-tuple-element.26), channel_id=1, source_target_pairs={{0,12},{1,13},{2,14},{3,15},{4,8},{5,9},{6,10},{7,11},{8,4},{9,5},... | collective-permute-start | bytes 294920 | tf_op jit(solution)/shard_map/ppermute | solution.py:387
  7.7 12.2 %collective-permute-start.1 = (bf16[96,512]{1,0:T(8,128)(2,1)S(1)}, bf16[96,512]{1,0:T(8,128)(2,1)S(1)}, u32[]{:S(2)}, u32[]{:S(2)}) collective-permute-start(bf16[96,512]{1,0:T(8,128)(2,1)S(1)} %get-tuple-element.26), channel_id=1, source_target_pairs={{0,8},{1,9},{2,10},{3,11},{4,12},{5,13},{6,14},{7,15},{8,0},{9,1},... | collective-permute-start | bytes 294920 | tf_op jit(solution)/shard_map/ppermute | solution.py:387
  7.7 12.2 %collective-permute-start = (bf16[96,512]{1,0:T(8,128)(2,1)S(1)}, bf16[96,512]{1,0:T(8,128)(2,1)S(1)}, u32[]{:S(2)}, u32[]{:S(2)}) collective-permute-start(bf16[96,512]{1,0:T(8,128)(2,1)S(1)} %get-tuple-element.26), channel_id=1, source_target_pairs={{0,4},{1,5},{2,6},{3,7},{4,0},{5,1},{6,2},{7,3},{8,12},{9,13},{10,... | collective-permute-start | bytes 294920 | tf_op jit(solution)/shard_map/ppermute | solution.py:387
  12.3 19.2 %collective-permute-start.8 = (bf16[80,512]{1,0:T(8,128)(2,1)S(1)}, bf16[80,512]{1,0:T(8,128)(2,1)S(1)}, u32[]{:S(2)}, u32[]{:S(2)}) collective-permute-start(bf16[80,512]{1,0:T(8,128)(2,1)S(1)} %gate.6), channel_id=1, source_target_pairs={{0,12},{1,13},{2,14},{3,15},{4,8},{5,9},{6,10},{7,11},{8,4},{9,5},... | collective-permute-start | bytes 245768 | tf_op jit(solution)/shard_map/ppermute | solution.py:387
  16.1 15.4 %collective-permute-start.7 = (bf16[80,512]{1,0:T(8,128)(2,1)S(1)}, bf16[80,512]{1,0:T(8,128)(2,1)S(1)}, u32[]{:S(2)}, u32[]{:S(2)}) collective-permute-start(bf16[80,512]{1,0:T(8,128)(2,1)S(1)} %gate.6), channel_id=1, source_target_pairs={{0,8},{1,9},{2,10},{3,11},{4,12},{5,13},{6,14},{7,15},{8,0},{9,1},... | collective-permute-start | bytes 245768 | tf_op jit(solution)/shard_map/ppermute | solution.py:387
  16.2 15.4 %collective-permute-start.6 = (bf16[80,512]{1,0:T(8,128)(2,1)S(1)}, bf16[80,512]{1,0:T(8,128)(2,1)S(1)}, u32[]{:S(2)}, u32[]{:S(2)}) collective-permute-start(bf16[80,512]{1,0:T(8,128)(2,1)S(1)} %gate.6), channel_id=1, source_target_pairs={{0,4},{1,5},{2,6},{3,7},{4,0},{5,1},{6,2},{7,3},{8,12},{9,13},{10,... | collective-permute-start | bytes 245768 | tf_op jit(solution)/shard_map/ppermute | solution.py:387
  19.9 28.9 %copy-start = (f32[8,2048]{1,0:T(8,128)S(1)}, f32[8,2048]{1,0:T(8,128)}, u32[]{:S(2)}) copy-start(f32[8,2048]{1,0:T(8,128)} %rhs_ref.5) | copy-start | bytes 196612
  20.0 13.9 %collective-permute-start.4 = (bf16[384,512]{1,0:T(8,128)(2,1)S(1)}, bf16[384,512]{1,0:T(8,128)(2,1)S(1)}, u32[]{:S(2)}, u32[]{:S(2)}) collective-permute-start(bf16[384,512]{1,0:T(8,128)(2,1)S(1)} %gate.4.arrived_ref.refs_2_), channel_id=1, source_target_pairs={{0,1},{1,0},{2,3},{3,2},{4,5},{5,4},{6,7},{7,6},{8,9},{9,8},{10,11... | collective-permute-start | bytes 1179656 | tf_op jit(solution)/shard_map/ppermute | solution.py:387
  20.0 11.5 %collective-permute-start.3 = (bf16[384,512]{1,0:T(8,128)(2,1)S(1)}, bf16[384,512]{1,0:T(8,128)(2,1)S(1)}, u32[]{:S(2)}, u32[]{:S(2)}) collective-permute-start(bf16[384,512]{1,0:T(8,128)(2,1)S(1)} %gate.4.arrived_ref.refs_2_), channel_id=1, source_target_pairs={{0,2},{1,3},{2,0},{3,1},{4,6},{5,7},{6,4},{7,5},{8,10},{9,11},{10,... | collective-permute-start | bytes 1179656 | tf_op jit(solution)/shard_map/ppermute | solution.py:387
  31.6 2.3 %collective-permute-start.5 = (bf16[384,512]{1,0:T(8,128)(2,1)S(1)}, bf16[384,512]{1,0:T(8,128)(2,1)S(1)}, u32[]{:S(2)}, u32[]{:S(2)}) collective-permute-start(bf16[384,512]{1,0:T(8,128)(2,1)S(1)} %gate.5.refs_3_), channel_id=1, source_target_pairs={{0,1},{1,0},{2,3},{3,2},{4,5},{5,4},{6,7},{7,6},{8,9},{9,8},{10,11... | collective-permute-start | bytes 1179656 | tf_op jit(solution)/shard_map/ppermute | solution.py:387
  31.6 9.7 %collective-permute-start.11 = (bf16[320,512]{1,0:T(8,128)(2,1)S(1)}, bf16[320,512]{1,0:T(8,128)(2,1)S(1)}, u32[]{:S(2)}, u32[]{:S(2)}) collective-permute-start(bf16[320,512]{1,0:T(8,128)(2,1)S(1)} %gate.7.refs_0_), channel_id=1, source_target_pairs={{0,3},{1,2},{2,1},{3,0},{4,7},{5,6},{6,5},{7,4},{8,11},{9,10},{10,... | collective-permute-start | bytes 983048 | tf_op jit(solution)/shard_map/ppermute | solution.py:387
  33.3 8.1 %collective-permute-start.10 = (bf16[320,512]{1,0:T(8,128)(2,1)S(1)}, bf16[320,512]{1,0:T(8,128)(2,1)S(1)}, u32[]{:S(2)}, u32[]{:S(2)}) collective-permute-start(bf16[320,512]{1,0:T(8,128)(2,1)S(1)} %gate.7.refs_0_), channel_id=1, source_target_pairs={{0,1},{1,0},{2,3},{3,2},{4,5},{5,4},{6,7},{7,6},{8,9},{9,8},{10,11... | collective-permute-start | bytes 983048 | tf_op jit(solution)/shard_map/ppermute | solution.py:387
  33.3 15.5 %collective-permute-start.9 = (bf16[320,512]{1,0:T(8,128)(2,1)S(1)}, bf16[320,512]{1,0:T(8,128)(2,1)}, u32[]{:S(2)}, u32[]{:S(2)}) collective-permute-start(bf16[320,512]{1,0:T(8,128)(2,1)S(1)} %gate.7.refs_0_), channel_id=1, source_target_pairs={{0,2},{1,3},{2,0},{3,1},{4,6},{5,7},{6,4},{7,5},{8,10},{9,11},{10,... | collective-permute-start | bytes 983048 | tf_op jit(solution)/shard_map/ppermute | solution.py:387
  53.3 36.8 %collective-permute-start.14 = (bf16[1,8,2176]{2,1,0:T(8,128)(2,1)S(1)}, bf16[1,8,2176]{2,1,0:T(8,128)(2,1)S(1)}, u32[]{:S(2)}, u32[]{:S(2)}) collective-permute-start(bf16[1,8,2176]{2,1,0:T(8,128)(2,1)S(1)} %bitcast.5), channel_id=1, source_target_pairs={{0,12},{1,13},{2,14},{3,15},{4,8},{5,9},{6,10},{7,11},{8,4},{9,5},... | collective-permute-start | bytes 104456 | tf_op jit(solution)/shard_map/ppermute | solution.py:387
  87.1 5.0 %collective-permute-start.13 = (bf16[1,8,2176]{2,1,0:T(8,128)(2,1)S(1)}, bf16[1,8,2176]{2,1,0:T(8,128)(2,1)S(1)}, u32[]{:S(2)}, u32[]{:S(2)}) collective-permute-start(bf16[1,8,2176]{2,1,0:T(8,128)(2,1)S(1)} %bitcast.6), channel_id=1, source_target_pairs={{0,8},{1,9},{2,10},{3,11},{4,12},{5,13},{6,14},{7,15},{8,0},{9,1},... | collective-permute-start | bytes 104456 | tf_op jit(solution)/shard_map/ppermute | solution.py:387
  87.1 5.1 %collective-permute-start.12 = (bf16[1,8,2176]{2,1,0:T(8,128)(2,1)S(1)}, bf16[1,8,2176]{2,1,0:T(8,128)(2,1)S(1)}, u32[]{:S(2)}, u32[]{:S(2)}) collective-permute-start(bf16[1,8,2176]{2,1,0:T(8,128)(2,1)S(1)} %bitcast.7), channel_id=1, source_target_pairs={{0,4},{1,5},{2,6},{3,7},{4,0},{5,1},{6,2},{7,3},{8,12},{9,13},{10,... | collective-permute-start | bytes 104456 | tf_op jit(solution)/shard_map/ppermute | solution.py:387
  92.3 5.9 %collective-permute-start.15 = (bf16[4,8,2176]{2,1,0:T(8,128)(2,1)S(1)}, bf16[4,8,2176]{2,1,0:T(8,128)(2,1)S(1)}, u32[]{:S(2)}, u32[]{:S(2)}) collective-permute-start(bf16[4,8,2176]{2,1,0:T(8,128)(2,1)S(1)} %pad_maximum_fusion.2), channel_id=1, source_target_pairs={{0,2},{1,3},{2,0},{3,1},{4,6},{5,7},{6,4},{7,5},{8,10},{9,11},{10,... | collective-permute-start | bytes 417800 | tf_op jit(solution)/shard_map/ppermute | solution.py:387
  98.2 2.1 %collective-permute-start.16 = (bf16[8,8,2176]{2,1,0:T(8,128)(2,1)S(1)}, bf16[8,8,2176]{2,1,0:T(8,128)(2,1)S(1)}, u32[]{:S(2)}, u32[]{:S(2)}) collective-permute-start(bf16[8,8,2176]{2,1,0:T(8,128)(2,1)S(1)} %get-tuple-element.47), channel_id=1, source_target_pairs={{0,1},{1,0},{2,3},{3,2},{4,5},{5,4},{6,7},{7,6},{8,9},{9,8},{10,11... | collective-permute-start | bytes 835592 | tf_op jit(solution)/shard_map/ppermute | solution.py:387
  101.5 10.6 %collective-permute-start.19 = (f32[8,128]{1,0:T(8,128)S(1)}, f32[8,128]{1,0:T(8,128)S(1)}, u32[]{:S(2)}, u32[]{:S(2)}) collective-permute-start(f32[8,128]{1,0:T(8,128)S(1)} %get-tuple-element.41), channel_id=1, source_target_pairs={{0,12},{1,13},{2,14},{3,15},{4,8},{5,9},{6,10},{7,11},{8,4},{9,5},... | collective-permute-start | bytes 12296 | tf_op jit(solution)/shard_map/ppermute | solution.py:387
  110.5 4.5 %collective-permute-start.18 = (f32[8,128]{1,0:T(8,128)S(1)}, f32[8,128]{1,0:T(8,128)S(1)}, u32[]{:S(2)}, u32[]{:S(2)}) collective-permute-start(f32[8,128]{1,0:T(8,128)S(1)} %get-tuple-element.41), channel_id=1, source_target_pairs={{0,8},{1,9},{2,10},{3,11},{4,12},{5,13},{6,14},{7,15},{8,0},{9,1},... | collective-permute-start | bytes 12296 | tf_op jit(solution)/shard_map/ppermute | solution.py:387
  110.8 4.3 %collective-permute-start.17 = (f32[8,128]{1,0:T(8,128)S(1)}, f32[8,128]{1,0:T(8,128)S(1)}, u32[]{:S(2)}, u32[]{:S(2)}) collective-permute-start(f32[8,128]{1,0:T(8,128)S(1)} %get-tuple-element.41), channel_id=1, source_target_pairs={{0,4},{1,5},{2,6},{3,7},{4,0},{5,1},{6,2},{7,3},{8,12},{9,13},{10,... | collective-permute-start | bytes 12296 | tf_op jit(solution)/shard_map/ppermute | solution.py:387
  115.1 3.4 %collective-permute-start.22 = (f32[8,128]{1,0:T(8,128)S(1)}, f32[8,128]{1,0:T(8,128)S(1)}, u32[]{:S(2)}, u32[]{:S(2)}) collective-permute-start(f32[8,128]{1,0:T(8,128)S(1)} %add_add_fusion.1), channel_id=1, source_target_pairs={{0,3},{1,2},{2,1},{3,0},{4,7},{5,6},{6,5},{7,4},{8,11},{9,10},{10,... | collective-permute-start | bytes 12296 | tf_op jit(solution)/shard_map/ppermute | solution.py:387
  115.1 3.7 %collective-permute-start.21 = (f32[8,128]{1,0:T(8,128)S(1)}, f32[8,128]{1,0:T(8,128)S(1)}, u32[]{:S(2)}, u32[]{:S(2)}) collective-permute-start(f32[8,128]{1,0:T(8,128)S(1)} %add_add_fusion.1), channel_id=1, source_target_pairs={{0,2},{1,3},{2,0},{3,1},{4,6},{5,7},{6,4},{7,5},{8,10},{9,11},{10,... | collective-permute-start | bytes 12296 | tf_op jit(solution)/shard_map/ppermute | solution.py:387
  116.1 2.7 %collective-permute-start.20 = (f32[8,128]{1,0:T(8,128)S(1)}, f32[8,128]{1,0:T(8,128)S(1)}, u32[]{:S(2)}, u32[]{:S(2)}) collective-permute-start(f32[8,128]{1,0:T(8,128)S(1)} %add_add_fusion.1), channel_id=1, source_target_pairs={{0,1},{1,0},{2,3},{3,2},{4,5},{5,4},{6,7},{7,6},{8,9},{9,8},{10,11... | collective-permute-start | bytes 12296 | tf_op jit(solution)/shard_map/ppermute | solution.py:387
  (2 other events, 45.6 us)

commit v19 on v16

--- a/solution.py
+++ b/solution.py
@@ -15,6 +15,8 @@
 KDIM = 128
 ROWS = 512
 PARTS = 2
+PIECE = 256
+STRIP = 64
 FRONT = 3
 HELD = 4
 TAIL = 128
@@ -59,19 +61,21 @@
     return (jnp.exp2(19.0 * lax.log2(u)) * (1.0 - u)).astype(BF16)
 
 
-def tile_unit(left, right, vec, tile_ref, width, strip):
-    pieces = [slice(at, at + width) for at in range(0, right.shape[1], width)]
+def tile_unit(left, right, vec, tile_ref, aside=None):
+    pieces = [slice(at, at + PIECE) for at in range(0, right.shape[1], PIECE)]
     gram = lambda piece: jnp.dot(left, right[:, piece], preferred_element_type=F32)
     product = lambda part: jnp.dot(vec, part, preferred_element_type=F32)
     dist, part, terms = gram(pieces[0]), None, []
     for index, piece in enumerate(pieces):
         following = gram(pieces[index + 1]) if index + 1 < len(pieces) else None
         strips = []
-        for at in range(0, left.shape[0], strip):
-            strips.append(psi_power(dist[at : at + strip]))
-            tile_ref[at : at + strip, piece] = strips[-1]
+        for at in range(0, left.shape[0], STRIP):
+            strips.append(psi_power(dist[at : at + STRIP]))
+            tile_ref[at : at + STRIP, piece] = strips[-1]
         if part is not None:
             terms.append(product(part))
+        if index == 1 and aside is not None:
+            aside()
         dist, part = following, jnp.concatenate(strips, axis=0)
     return jnp.concatenate(terms + [product(part)], axis=1)
 
@@ -96,7 +100,7 @@
         def col_step(col, at):
             sum_ref[:, piece(col)] += tile_unit(
                 left_ref[piece(row), :], right_ref[:, piece(col)], vec_ref[:, piece(row)],
-                tile_ref.at[at], 256, 64,
+                tile_ref.at[at],
             )
             save(at).start()
 
@@ -187,8 +191,19 @@
     return fetch
 
 
-def half_tiles(piece, strip, slots_ref, right_ref, fetch, front_ref, back_ref, sum_ref, left_ref, vec_ref, pay_ref, sem_ref):
+def half_tiles(early, slots_ref, right_ref, fetch, front_ref, back_ref, sum_ref, left_ref, vec_ref, pay_ref, sem_ref):
     slot, step = pl.program_id(0), pl.program_id(1)
+    last = pl.num_programs(1) - 1
+
+    def arrive(which):
+        pltpu.make_async_copy(
+            pay_ref.at[(which + 1) % 2], pay_ref.at[which % 2], sem_ref.at[which % 2]
+        ).wait()
+
+    def factor(which):
+        feat, vec = unpack(pay_ref[which % 2])
+        left_ref[which % 2] = other_factor(feat)
+        vec_ref[which % 2] = vec
 
     @pl.when((slot == 0) & (step == 0) & (slots_ref[0] > 0))
     def _():
@@ -196,26 +211,29 @@
 
     @pl.when(slot < slots_ref[0])
     def _():
-        @pl.when(step == 0)
+        @pl.when((step == 0) & ((slot == 0) | (not early)))
         def _():
-            pltpu.make_async_copy(
-                pay_ref.at[(slot + 1) % 2], pay_ref.at[slot % 2], sem_ref.at[slot % 2]
-            ).wait()
-
-            @pl.when(slot + 1 < slots_ref[0])
+            arrive(slot)
+            factor(slot)
+
+        @pl.when((step == 0) & (slot + 1 < slots_ref[0]))
+        def _():
+            fetch(slot + 1)
+
+        if early:
+            @pl.when((step == last) & (slot + 1 < slots_ref[0]))
             def _():
-                fetch(slot + 1)
-
-            feat, vec = unpack(pay_ref[slot % 2])
-            left_ref[...] = other_factor(feat)
-            vec_ref[...] = vec
+                arrive(slot + 1)
 
         rows = pl.ds(pl.multiple_of(step * ROWS, ROWS), ROWS)
-        left, vec = left_ref[rows, :], vec_ref[:, rows]
+        place = slot % 2
+        left, vec = left_ref[place, rows, :], vec_ref[place, :, rows]
         for tile_ref, here in ((front_ref, slot < FRONT), (back_ref, slot >= FRONT)):
-            @pl.when(here)
-            def _():
-                sum_ref[...] += tile_unit(left, right_ref[...], vec, tile_ref.at[0], piece, strip)
+            for ends in (False, True) if early else (None,):
+                @pl.when(here if ends is None else here & ((step == last) == ends))
+                def _():
+                    aside = (lambda: factor(slot + 1)) if ends else None
+                    sum_ref[...] += tile_unit(left, right_ref[...], vec, tile_ref.at[0], aside)
 
 
 def pair_zero_kernel(block_at, me_ref, right_ref, *refs):
@@ -246,7 +264,7 @@
 
     fetch = fetch_from(block_at, block_refs, slots_ref, pay_ref, sem_ref)
     half_tiles(
-        256, 128, slots_ref, right_ref, fetch, front_ref, back_ref, sum_ref, left_ref, vec_ref, pay_ref, sem_ref
+        True, slots_ref, right_ref, fetch, front_ref, back_ref, sum_ref, left_ref, vec_ref, pay_ref, sem_ref
     )
 
 
@@ -261,7 +279,7 @@
 
     fetch = fetch_from(block_at, block_refs, slots_ref, pay_ref, sem_ref)
     half_tiles(
-        512, 64, slots_ref, right_ref, fetch, front_ref, back_ref, image_ref, left_ref, vec_ref, pay_ref, sem_ref
+        False, slots_ref, right_ref, fetch, front_ref, back_ref, image_ref, left_ref, vec_ref, pay_ref, sem_ref
     )
 
     @pl.when((slot == pl.num_programs(0) - 1) & (step == pl.num_programs(1) - 1))
@@ -513,8 +531,8 @@
         pltpu.HBM((most - FRONT, width // 2, width), BF16),
     ]
     half_scratch = [
-        pltpu.VMEM((width // 2, KDIM), BF16),
-        pltpu.VMEM((rhs_count, width // 2), BF16),
+        pltpu.VMEM((2, width // 2, KDIM), BF16),
+        pltpu.VMEM((2, rhs_count, width // 2), BF16),
         pltpu.VMEM((2,) + pay_shape, BF16),
         pltpu.SemaphoreType.DMA((2,)),
     ]

time: 121 us -> 118 us (0.975); the launches traced: 120 us -> 116 us
  starting transfers between devices: 53.3 us -> 39.9 us
  Pallas kernels: 47.9 us -> 56.7 us
    ppermute x23, starting transfers between devices: 53.3 us -> 39.9 us  [swap(): return lax.ppermute(value, 'row', [(i, i ^ mask) for i in range(count)])]
    pallas_call x1, Pallas kernels: 13.8 us -> 18.2 us  [local(): pl.pallas_call(functools.partial(pair_zero_kernel, zero_at), grid_spec=pl...]
    pallas_call x1, Pallas kernels: 14 us -> 17.4 us  [local(): pl.pallas_call(functools.partial(pair_one_kernel, one_at), grid_spec=pltp...]
  transfers between devices with their start and end apart: 23 -> 23, of which waited for: 8 -> 7; matrix products, arithmetic and copies ran while one was open for 0% -> 0% of each run, Pallas kernels for 24% -> 29%
where the time goes in v19:
time: 118 us; the launch traced here: 116 us
  Pallas kernels  56.7 us (48%)
  starting transfers between devices  39.9 us (34%)
  waiting for transfers between devices  16.6 us (14%)
    ppermute x23, starting transfers between devices, swap(): return lax.ppermute(value, 'row', [(i, i ^ mask) for i in range(count)])  39.9 us
    pallas_call x1, Pallas kernels, local(): pl.pallas_call(functools.partial(pair_zero_kernel, zero_at), grid_spec=pl...  18.2 us
    pallas_call x1, Pallas kernels, local(): pl.pallas_call(functools.partial(pair_one_kernel, one_at), grid_spec=pltp...  17.4 us
    ppermute x23, waiting for transfers between devices, swap(): return lax.ppermute(value, 'row', [(i, i ^ mask) for i in range(count)])  16.6 us
    pallas_call x2, Pallas kernels, own_part(): pl.pallas_call(functools.partial(own_kernel, rows), in_specs=[vmem, vmem,...  9.62 us
    pallas_call x1, Pallas kernels, local(): pl.pallas_call(again_kernel, grid_spec=pltpu.PrefetchScalarGridSpec(num_s...  4.58 us
    pallas_call x2, Pallas kernels, local(): pl.pallas_call(functools.partial(own_again_kernel, blocks), in_specs=[any...  4.34 us
  transfers between devices with their start and end apart: 23, of which 7 were waited for; matrix products, arithmetic and copies ran while one was open for 0% of the time, Pallas kernels for 29%

profile of v19, /device:TPU:0, one launch (start us, length us, event | category | flops | bytes accessed | tf_op | source)
XLA Modules:
  0.0 116.0 jit_solution(15059119877073971484)
XLA Ops:
  1.4 1.2 %payload.1 = (bf16[96,512]{1,0:T(8,128)(2,1)S(1)}, bf16[80,512]{1,0:T(8,128)(2,1)S(1)}, bf16[128,2048]{1,0:T(8,128)(2,1)S(1)}, bf16[2048,128]{1,0:T(8,128)(2,1)S(1)}, bf16[8,2048]{1,0:T(8,128)(2,1)S(1)}) custom-call(s32[1,5,2]{2,1,0:T(8,128)S(1)} %copy.12.list_ref, bf16[32,2048]{1,0:T(8,128)(2,1)} %feat_ref.1, f32[8,2048]{1,0:T(8,128)} %rhs_ref.5), custom_call_target="tpu_custom_call" | custom-call | tf_op jit(solution)/shard_map/payload/pallas_call | solution.py:464
  2.6 5.1 %collective-permute-start.2 = (bf16[96,512]{1,0:T(8,128)(2,1)S(1)}, bf16[96,512]{1,0:T(8,128)(2,1)S(1)}, u32[]{:S(2)}, u32[]{:S(2)}) collective-permute-start(bf16[96,512]{1,0:T(8,128)(2,1)S(1)} %get-tuple-element.26), channel_id=1, source_target_pairs={{0,12},{1,13},{2,14},{3,15},{4,8},{5,9},{6,10},{7,11},{8,4},{9,5},... | collective-permute-start | bytes 294920 | tf_op jit(solution)/shard_map/ppermute | solution.py:392
  8.3 4.0 %own_tile_0.1 = (bf16[4,512,512]{2,1,0:T(8,128)(2,1)}, f32[8,2048]{1,0:T(8,128)S(1)}) custom-call(bf16[2048,128]{1,0:T(8,128)(2,1)S(1)} %get-tuple-element.23.left_ref, bf16[128,2048]{1,0:T(8,128)(2,1)S(1)} %get-tuple-element.22.right_ref.arrived_ref, bf16[8,2048]{1,0:T(8,128)(2,1)S(1)} %get-tuple-element.24.vec_ref, ...), custom_call_target="tpu_custom_call" | custom-call | flops 5000000000 | bytes 2097152 | tf_op jit(solution)/shard_map/own_tile_0/pallas_call | solution.py:482
  12.3 3.8 %collective-permute-start.8 = (bf16[80,512]{1,0:T(8,128)(2,1)S(1)}, bf16[80,512]{1,0:T(8,128)(2,1)S(1)}, u32[]{:S(2)}, u32[]{:S(2)}) collective-permute-start(bf16[80,512]{1,0:T(8,128)(2,1)S(1)} %gate.6), channel_id=1, source_target_pairs={{0,12},{1,13},{2,14},{3,15},{4,8},{5,9},{6,10},{7,11},{8,4},{9,5},... | collective-permute-start | bytes 245768 | tf_op jit(solution)/shard_map/ppermute | solution.py:392
  16.8 3.1 %collective-permute-done.1 = bf16[96,512]{1,0:T(8,128)(2,1)S(1)} collective-permute-done((bf16[96,512]{1,0:T(8,128)(2,1)S(1)}, bf16[96,512]{1,0:T(8,128)(2,1)S(1)}, u32[]{:S(2)}, u32[]{:S(2)}) %collective-permute-start.1) | collective-permute-done | bytes 98336 | tf_op jit(solution)/shard_map/ppermute | solution.py:392
  20.0 1.6 %collective-permute-start.3 = (bf16[384,512]{1,0:T(8,128)(2,1)S(1)}, bf16[384,512]{1,0:T(8,128)(2,1)S(1)}, u32[]{:S(2)}, u32[]{:S(2)}) collective-permute-start(bf16[384,512]{1,0:T(8,128)(2,1)S(1)} %gate.4.arrived_ref.refs_2_), channel_id=1, source_target_pairs={{0,2},{1,3},{2,0},{3,1},{4,6},{5,7},{6,4},{7,5},{8,10},{9,11},{10,... | collective-permute-start | bytes 1179656 | tf_op jit(solution)/shard_map/ppermute | solution.py:392
  21.6 5.6 %own_tile_1.1 = (bf16[6,512,512]{2,1,0:T(8,128)(2,1)}, f32[8,2048]{1,0:T(8,128)S(1)}) custom-call(bf16[2048,128]{1,0:T(8,128)(2,1)S(1)} %get-tuple-element.23.left_ref, bf16[128,2048]{1,0:T(8,128)(2,1)S(1)} %get-tuple-element.22.right_ref.arrived_ref, bf16[8,2048]{1,0:T(8,128)(2,1)S(1)} %get-tuple-element.24.vec_ref, ...), custom_call_target="tpu_custom_call" | custom-call | flops 5000000000 | bytes 3145728 | tf_op jit(solution)/shard_map/own_tile_1/pallas_call | solution.py:482
  27.2 4.3 %collective-permute-done.3.refs_0_ = bf16[384,512]{1,0:T(8,128)(2,1)S(1)} collective-permute-done((bf16[384,512]{1,0:T(8,128)(2,1)S(1)}, bf16[384,512]{1,0:T(8,128)(2,1)S(1)}, u32[]{:S(2)}, u32[]{:S(2)}) %collective-permute-start.3) | collective-permute-done | bytes 393248 | tf_op jit(solution)/shard_map/ppermute | solution.py:392
  31.6 1.7 %collective-permute-start.11 = (bf16[320,512]{1,0:T(8,128)(2,1)S(1)}, bf16[320,512]{1,0:T(8,128)(2,1)S(1)}, u32[]{:S(2)}, u32[]{:S(2)}) collective-permute-start(bf16[320,512]{1,0:T(8,128)(2,1)S(1)} %gate.7.refs_0_), channel_id=1, source_target_pairs={{0,3},{1,2},{2,1},{3,0},{4,7},{5,6},{6,5},{7,4},{8,11},{9,10},{10,... | collective-permute-start | bytes 983048 | tf_op jit(solution)/shard_map/ppermute | solution.py:392
  33.9 18.2 %pair_zero.1 = (bf16[3,1024,2048]{2,1,0:T(8,128)(2,1)S(1)}, bf16[2,1024,2048]{2,1,0:T(8,128)(2,1)}, f32[8,2048]{1,0:T(8,128)S(1)}, s32[7]{0:T(128)S(1)}) custom-call(s32[1]{0:T(128)} %bitcast.me_ref, bf16[128,2048]{1,0:T(8,128)(2,1)S(1)} %get-tuple-element.22.right_ref.arrived_ref, f32[8,2048]{1,0:T(8,128)S(1)} %get-tuple-element.25.refs_1_.refs_0_, ...), custom_call_target="tpu_custom_call" | custom-call | tf_op jit(solution)/shard_map/pair_zero/pallas_call | solution.py:541
  52.1 17.4 %pair_one.1 = (bf16[3,1024,2048]{2,1,0:T(8,128)(2,1)S(1)}, bf16[2,1024,2048]{2,1,0:T(8,128)(2,1)}, f32[8,2048]{1,0:T(8,128)S(1)}, bf16[8,2176]{1,0:T(8,128)(2,1)S(1)}) custom-call(s32[7]{0:T(128)S(1)} %get-tuple-element.28.slots_ref, bf16[128,2048]{1,0:T(8,128)(2,1)S(1)} %get-tuple-element.22.right_ref.arrived_ref, ...), custom_call_target="tpu_custom_call" | custom-call | tf_op jit(solution)/shard_map/pair_one/pallas_call | solution.py:561
  69.4 8.4 %collective-permute-start.14 = (bf16[1,8,2176]{2,1,0:T(8,128)(2,1)S(1)}, bf16[1,8,2176]{2,1,0:T(8,128)(2,1)S(1)}, u32[]{:S(2)}, u32[]{:S(2)}) collective-permute-start(bf16[1,8,2176]{2,1,0:T(8,128)(2,1)S(1)} %bitcast.5), channel_id=1, source_target_pairs={{0,12},{1,13},{2,14},{3,15},{4,8},{5,9},{6,10},{7,11},{8,4},{9,5},... | collective-permute-start | bytes 104456 | tf_op jit(solution)/shard_map/ppermute | solution.py:392
  78.5 2.4 %own_again_1.1.refs_1_ = f32[8,2048]{1,0:T(8,128)S(1)} custom-call(bf16[6,512,512]{2,1,0:T(8,128)(2,1)} %get-tuple-element.38.in_ref, bf16[8,2176]{1,0:T(8,128)(2,1)S(1)} %get-tuple-element.35.vec_ref), custom_call_target="tpu_custom_call" | custom-call | flops 5000000000 | bytes 3145728 | tf_op jit(solution)/shard_map/own_again_1/pallas_call | solution.py:579
  80.8 1.8 %collective-permute-done.13 = bf16[1,8,2176]{2,1,0:T(8,128)(2,1)S(1)} collective-permute-done((bf16[1,8,2176]{2,1,0:T(8,128)(2,1)S(1)}, bf16[1,8,2176]{2,1,0:T(8,128)(2,1)S(1)}, u32[]{:S(2)}, u32[]{:S(2)}) %collective-permute-start.13) | collective-permute-done | bytes 34848 | tf_op jit(solution)/shard_map/ppermute | solution.py:392
  82.7 7.9 %collective-permute-start.15 = (bf16[4,8,2176]{2,1,0:T(8,128)(2,1)S(1)}, bf16[4,8,2176]{2,1,0:T(8,128)(2,1)S(1)}, u32[]{:S(2)}, u32[]{:S(2)}) collective-permute-start(bf16[4,8,2176]{2,1,0:T(8,128)(2,1)S(1)} %pad_maximum_fusion.2), channel_id=1, source_target_pairs={{0,2},{1,3},{2,0},{3,1},{4,6},{5,7},{6,4},{7,5},{8,10},{9,11},{10,... | collective-permute-start | bytes 417800 | tf_op jit(solution)/shard_map/ppermute | solution.py:392
  90.7 4.3 %collective-permute-done.15 = bf16[4,8,2176]{2,1,0:T(8,128)(2,1)S(1)} collective-permute-done((bf16[4,8,2176]{2,1,0:T(8,128)(2,1)S(1)}, bf16[4,8,2176]{2,1,0:T(8,128)(2,1)S(1)}, u32[]{:S(2)}, u32[]{:S(2)}) %collective-permute-start.15) | collective-permute-done | bytes 139296 | tf_op jit(solution)/shard_map/ppermute | solution.py:392
  95.1 2.0 %own_again_0.1.refs_0_ = f32[8,2048]{1,0:T(8,128)S(1)} custom-call(bf16[4,512,512]{2,1,0:T(8,128)(2,1)} %get-tuple-element.37.in_ref, bf16[8,2176]{1,0:T(8,128)(2,1)S(1)} %get-tuple-element.35.vec_ref), custom_call_target="tpu_custom_call" | custom-call | flops 5000000000 | bytes 2097152 | tf_op jit(solution)/shard_map/own_again_0/pallas_call | solution.py:579
  97.2 4.6 %pair_again.1 = (f32[32,2048]{1,0:T(8,128)S(1)}, f32[8,128]{1,0:T(8,128)S(1)}, f32[8,128]{1,0:T(8,128)S(1)}) custom-call(s32[7]{0:T(128)S(1)} %get-tuple-element.28.slots_ref, bf16[3,1024,2048]{2,1,0:T(8,128)(2,1)S(1)} %get-tuple-element.29.front_zero_ref, bf16[3,1024,2048]{2,1,0:T(8,128)(2,1)S(1)} %get-tuple-element.32.front_one_ref, ...), custom_call_target="tpu_custom_call" | custom-call | tf_op jit(solution)/shard_map/pair_again/pallas_call | solution.py:597
  101.8 2.9 %collective-permute-start.19 = (f32[8,128]{1,0:T(8,128)S(1)}, f32[8,128]{1,0:T(8,128)S(1)}, u32[]{:S(2)}, u32[]{:S(2)}) collective-permute-start(f32[8,128]{1,0:T(8,128)S(1)} %get-tuple-element.41), channel_id=1, source_target_pairs={{0,12},{1,13},{2,14},{3,15},{4,8},{5,9},{6,10},{7,11},{8,4},{9,5},... | collective-permute-start | bytes 12296 | tf_op jit(solution)/shard_map/ppermute | solution.py:392
  104.7 1.6 %collective-permute-start.17 = (f32[8,128]{1,0:T(8,128)S(1)}, f32[8,128]{1,0:T(8,128)S(1)}, u32[]{:S(2)}, u32[]{:S(2)}) collective-permute-start(f32[8,128]{1,0:T(8,128)S(1)} %get-tuple-element.41), channel_id=1, source_target_pairs={{0,4},{1,5},{2,6},{3,7},{4,0},{5,1},{6,2},{7,3},{8,12},{9,13},{10,... | collective-permute-start | bytes 12296 | tf_op jit(solution)/shard_map/ppermute | solution.py:392
  107.2 1.9 %collective-permute-done.18 = f32[8,128]{1,0:T(8,128)S(1)} collective-permute-done((f32[8,128]{1,0:T(8,128)S(1)}, f32[8,128]{1,0:T(8,128)S(1)}, u32[]{:S(2)}, u32[]{:S(2)}) %collective-permute-start.18) | collective-permute-done | bytes 4128 | tf_op jit(solution)/shard_map/ppermute | solution.py:392
  109.2 1.7 %collective-permute-start.22 = (f32[8,128]{1,0:T(8,128)S(1)}, f32[8,128]{1,0:T(8,128)S(1)}, u32[]{:S(2)}, u32[]{:S(2)}) collective-permute-start(f32[8,128]{1,0:T(8,128)S(1)} %add_add_fusion.1), channel_id=1, source_target_pairs={{0,3},{1,2},{2,1},{3,0},{4,7},{5,6},{6,5},{7,4},{8,11},{9,10},{10,... | collective-permute-start | bytes 12296 | tf_op jit(solution)/shard_map/ppermute | solution.py:392
  110.9 2.5 %collective-permute-start.21 = (f32[8,128]{1,0:T(8,128)S(1)}, f32[8,128]{1,0:T(8,128)S(1)}, u32[]{:S(2)}, u32[]{:S(2)}) collective-permute-start(f32[8,128]{1,0:T(8,128)S(1)} %add_add_fusion.1), channel_id=1, source_target_pairs={{0,2},{1,3},{2,0},{3,1},{4,6},{5,7},{6,4},{7,5},{8,10},{9,11},{10,... | collective-permute-start | bytes 12296 | tf_op jit(solution)/shard_map/ppermute | solution.py:392
  113.4 1.5 %curve_order.1 = f32[32,2048]{1,0:T(8,128)S(1)} custom-call(f32[32,2048]{1,0:T(8,128)S(1)} %get-tuple-element.40.rows_ref, s32[1,2048]{1,0:T(1,128)S(1)} %copy-done.2), custom_call_target="tpu_custom_call" | custom-call | tf_op jit(solution)/shard_map/curve_order/pallas_call | solution.py:635
  (55 shorter events, 5.8 us)
Async XLA Ops:
  2.6 13.6 %collective-permute-start.2 = (bf16[96,512]{1,0:T(8,128)(2,1)S(1)}, bf16[96,512]{1,0:T(8,128)(2,1)S(1)}, u32[]{:S(2)}, u32[]{:S(2)}) collective-permute-start(bf16[96,512]{1,0:T(8,128)(2,1)S(1)} %get-tuple-element.26), channel_id=1, source_target_pairs={{0,12},{1,13},{2,14},{3,15},{4,8},{5,9},{6,10},{7,11},{8,4},{9,5},... | collective-permute-start | bytes 294920 | tf_op jit(solution)/shard_map/ppermute | solution.py:392
  7.7 12.2 %collective-permute-start.1 = (bf16[96,512]{1,0:T(8,128)(2,1)S(1)}, bf16[96,512]{1,0:T(8,128)(2,1)S(1)}, u32[]{:S(2)}, u32[]{:S(2)}) collective-permute-start(bf16[96,512]{1,0:T(8,128)(2,1)S(1)} %get-tuple-element.26), channel_id=1, source_target_pairs={{0,8},{1,9},{2,10},{3,11},{4,12},{5,13},{6,14},{7,15},{8,0},{9,1},... | collective-permute-start | bytes 294920 | tf_op jit(solution)/shard_map/ppermute | solution.py:392
  7.7 12.2 %collective-permute-start = (bf16[96,512]{1,0:T(8,128)(2,1)S(1)}, bf16[96,512]{1,0:T(8,128)(2,1)S(1)}, u32[]{:S(2)}, u32[]{:S(2)}) collective-permute-start(bf16[96,512]{1,0:T(8,128)(2,1)S(1)} %get-tuple-element.26), channel_id=1, source_target_pairs={{0,4},{1,5},{2,6},{3,7},{4,0},{5,1},{6,2},{7,3},{8,12},{9,13},{10,... | collective-permute-start | bytes 294920 | tf_op jit(solution)/shard_map/ppermute | solution.py:392
  12.3 19.2 %collective-permute-start.8 = (bf16[80,512]{1,0:T(8,128)(2,1)S(1)}, bf16[80,512]{1,0:T(8,128)(2,1)S(1)}, u32[]{:S(2)}, u32[]{:S(2)}) collective-permute-start(bf16[80,512]{1,0:T(8,128)(2,1)S(1)} %gate.6), channel_id=1, source_target_pairs={{0,12},{1,13},{2,14},{3,15},{4,8},{5,9},{6,10},{7,11},{8,4},{9,5},... | collective-permute-start | bytes 245768 | tf_op jit(solution)/shard_map/ppermute | solution.py:392
  16.1 15.4 %collective-permute-start.7 = (bf16[80,512]{1,0:T(8,128)(2,1)S(1)}, bf16[80,512]{1,0:T(8,128)(2,1)S(1)}, u32[]{:S(2)}, u32[]{:S(2)}) collective-permute-start(bf16[80,512]{1,0:T(8,128)(2,1)S(1)} %gate.6), channel_id=1, source_target_pairs={{0,8},{1,9},{2,10},{3,11},{4,12},{5,13},{6,14},{7,15},{8,0},{9,1},... | collective-permute-start | bytes 245768 | tf_op jit(solution)/shard_map/ppermute | solution.py:392
  16.2 15.4 %collective-permute-start.6 = (bf16[80,512]{1,0:T(8,128)(2,1)S(1)}, bf16[80,512]{1,0:T(8,128)(2,1)S(1)}, u32[]{:S(2)}, u32[]{:S(2)}) collective-permute-start(bf16[80,512]{1,0:T(8,128)(2,1)S(1)} %gate.6), channel_id=1, source_target_pairs={{0,4},{1,5},{2,6},{3,7},{4,0},{5,1},{6,2},{7,3},{8,12},{9,13},{10,... | collective-permute-start | bytes 245768 | tf_op jit(solution)/shard_map/ppermute | solution.py:392
  19.9 32.1 %copy-start = (f32[8,2048]{1,0:T(8,128)S(1)}, f32[8,2048]{1,0:T(8,128)}, u32[]{:S(2)}) copy-start(f32[8,2048]{1,0:T(8,128)} %rhs_ref.5) | copy-start | bytes 196612
  20.0 13.9 %collective-permute-start.4 = (bf16[384,512]{1,0:T(8,128)(2,1)S(1)}, bf16[384,512]{1,0:T(8,128)(2,1)S(1)}, u32[]{:S(2)}, u32[]{:S(2)}) collective-permute-start(bf16[384,512]{1,0:T(8,128)(2,1)S(1)} %gate.4.arrived_ref.refs_2_), channel_id=1, source_target_pairs={{0,1},{1,0},{2,3},{3,2},{4,5},{5,4},{6,7},{7,6},{8,9},{9,8},{10,11... | collective-permute-start | bytes 1179656 | tf_op jit(solution)/shard_map/ppermute | solution.py:392
  20.0 11.5 %collective-permute-start.3 = (bf16[384,512]{1,0:T(8,128)(2,1)S(1)}, bf16[384,512]{1,0:T(8,128)(2,1)S(1)}, u32[]{:S(2)}, u32[]{:S(2)}) collective-permute-start(bf16[384,512]{1,0:T(8,128)(2,1)S(1)} %gate.4.arrived_ref.refs_2_), channel_id=1, source_target_pairs={{0,2},{1,3},{2,0},{3,1},{4,6},{5,7},{6,4},{7,5},{8,10},{9,11},{10,... | collective-permute-start | bytes 1179656 | tf_op jit(solution)/shard_map/ppermute | solution.py:392
  31.6 2.3 %collective-permute-start.5 = (bf16[384,512]{1,0:T(8,128)(2,1)S(1)}, bf16[384,512]{1,0:T(8,128)(2,1)S(1)}, u32[]{:S(2)}, u32[]{:S(2)}) collective-permute-start(bf16[384,512]{1,0:T(8,128)(2,1)S(1)} %gate.5.refs_3_), channel_id=1, source_target_pairs={{0,1},{1,0},{2,3},{3,2},{4,5},{5,4},{6,7},{7,6},{8,9},{9,8},{10,11... | collective-permute-start | bytes 1179656 | tf_op jit(solution)/shard_map/ppermute | solution.py:392
  31.6 20.4 %collective-permute-start.11 = (bf16[320,512]{1,0:T(8,128)(2,1)S(1)}, bf16[320,512]{1,0:T(8,128)(2,1)S(1)}, u32[]{:S(2)}, u32[]{:S(2)}) collective-permute-start(bf16[320,512]{1,0:T(8,128)(2,1)S(1)} %gate.7.refs_0_), channel_id=1, source_target_pairs={{0,3},{1,2},{2,1},{3,0},{4,7},{5,6},{6,5},{7,4},{8,11},{9,10},{10,... | collective-permute-start | bytes 983048 | tf_op jit(solution)/shard_map/ppermute | solution.py:392
  33.3 18.7 %collective-permute-start.10 = (bf16[320,512]{1,0:T(8,128)(2,1)S(1)}, bf16[320,512]{1,0:T(8,128)(2,1)S(1)}, u32[]{:S(2)}, u32[]{:S(2)}) collective-permute-start(bf16[320,512]{1,0:T(8,128)(2,1)S(1)} %gate.7.refs_0_), channel_id=1, source_target_pairs={{0,1},{1,0},{2,3},{3,2},{4,5},{5,4},{6,7},{7,6},{8,9},{9,8},{10,11... | collective-permute-start | bytes 983048 | tf_op jit(solution)/shard_map/ppermute | solution.py:392
  33.3 18.7 %collective-permute-start.9 = (bf16[320,512]{1,0:T(8,128)(2,1)S(1)}, bf16[320,512]{1,0:T(8,128)(2,1)}, u32[]{:S(2)}, u32[]{:S(2)}) collective-permute-start(bf16[320,512]{1,0:T(8,128)(2,1)S(1)} %gate.7.refs_0_), channel_id=1, source_target_pairs={{0,2},{1,3},{2,0},{3,1},{4,6},{5,7},{6,4},{7,5},{8,10},{9,11},{10,... | collective-permute-start | bytes 983048 | tf_op jit(solution)/shard_map/ppermute | solution.py:392
  69.4 11.4 %collective-permute-start.14 = (bf16[1,8,2176]{2,1,0:T(8,128)(2,1)S(1)}, bf16[1,8,2176]{2,1,0:T(8,128)(2,1)S(1)}, u32[]{:S(2)}, u32[]{:S(2)}) collective-permute-start(bf16[1,8,2176]{2,1,0:T(8,128)(2,1)S(1)} %bitcast.5), channel_id=1, source_target_pairs={{0,12},{1,13},{2,14},{3,15},{4,8},{5,9},{6,10},{7,11},{8,4},{9,5},... | collective-permute-start | bytes 104456 | tf_op jit(solution)/shard_map/ppermute | solution.py:392
  77.8 4.8 %collective-permute-start.13 = (bf16[1,8,2176]{2,1,0:T(8,128)(2,1)S(1)}, bf16[1,8,2176]{2,1,0:T(8,128)(2,1)S(1)}, u32[]{:S(2)}, u32[]{:S(2)}) collective-permute-start(bf16[1,8,2176]{2,1,0:T(8,128)(2,1)S(1)} %bitcast.6), channel_id=1, source_target_pairs={{0,8},{1,9},{2,10},{3,11},{4,12},{5,13},{6,14},{7,15},{8,0},{9,1},... | collective-permute-start | bytes 104456 | tf_op jit(solution)/shard_map/ppermute | solution.py:392
  77.8 4.8 %collective-permute-start.12 = (bf16[1,8,2176]{2,1,0:T(8,128)(2,1)S(1)}, bf16[1,8,2176]{2,1,0:T(8,128)(2,1)S(1)}, u32[]{:S(2)}, u32[]{:S(2)}) collective-permute-start(bf16[1,8,2176]{2,1,0:T(8,128)(2,1)S(1)} %bitcast.7), channel_id=1, source_target_pairs={{0,4},{1,5},{2,6},{3,7},{4,0},{5,1},{6,2},{7,3},{8,12},{9,13},{10,... | collective-permute-start | bytes 104456 | tf_op jit(solution)/shard_map/ppermute | solution.py:392
  82.7 12.3 %collective-permute-start.15 = (bf16[4,8,2176]{2,1,0:T(8,128)(2,1)S(1)}, bf16[4,8,2176]{2,1,0:T(8,128)(2,1)S(1)}, u32[]{:S(2)}, u32[]{:S(2)}) collective-permute-start(bf16[4,8,2176]{2,1,0:T(8,128)(2,1)S(1)} %pad_maximum_fusion.2), channel_id=1, source_target_pairs={{0,2},{1,3},{2,0},{3,1},{4,6},{5,7},{6,4},{7,5},{8,10},{9,11},{10,... | collective-permute-start | bytes 417800 | tf_op jit(solution)/shard_map/ppermute | solution.py:392
  95.0 2.2 %collective-permute-start.16 = (bf16[8,8,2176]{2,1,0:T(8,128)(2,1)S(1)}, bf16[8,8,2176]{2,1,0:T(8,128)(2,1)S(1)}, u32[]{:S(2)}, u32[]{:S(2)}) collective-permute-start(bf16[8,8,2176]{2,1,0:T(8,128)(2,1)S(1)} %get-tuple-element.47), channel_id=1, source_target_pairs={{0,1},{1,0},{2,3},{3,2},{4,5},{5,4},{6,7},{7,6},{8,9},{9,8},{10,11... | collective-permute-start | bytes 835592 | tf_op jit(solution)/shard_map/ppermute | solution.py:392
  101.8 5.5 %collective-permute-start.19 = (f32[8,128]{1,0:T(8,128)S(1)}, f32[8,128]{1,0:T(8,128)S(1)}, u32[]{:S(2)}, u32[]{:S(2)}) collective-permute-start(f32[8,128]{1,0:T(8,128)S(1)} %get-tuple-element.41), channel_id=1, source_target_pairs={{0,12},{1,13},{2,14},{3,15},{4,8},{5,9},{6,10},{7,11},{8,4},{9,5},... | collective-permute-start | bytes 12296 | tf_op jit(solution)/shard_map/ppermute | solution.py:392
  104.7 4.5 %collective-permute-start.18 = (f32[8,128]{1,0:T(8,128)S(1)}, f32[8,128]{1,0:T(8,128)S(1)}, u32[]{:S(2)}, u32[]{:S(2)}) collective-permute-start(f32[8,128]{1,0:T(8,128)S(1)} %get-tuple-element.41), channel_id=1, source_target_pairs={{0,8},{1,9},{2,10},{3,11},{4,12},{5,13},{6,14},{7,15},{8,0},{9,1},... | collective-permute-start | bytes 12296 | tf_op jit(solution)/shard_map/ppermute | solution.py:392
  104.7 4.5 %collective-permute-start.17 = (f32[8,128]{1,0:T(8,128)S(1)}, f32[8,128]{1,0:T(8,128)S(1)}, u32[]{:S(2)}, u32[]{:S(2)}) collective-permute-start(f32[8,128]{1,0:T(8,128)S(1)} %get-tuple-element.41), channel_id=1, source_target_pairs={{0,4},{1,5},{2,6},{3,7},{4,0},{5,1},{6,2},{7,3},{8,12},{9,13},{10,... | collective-permute-start | bytes 12296 | tf_op jit(solution)/shard_map/ppermute | solution.py:392
  109.2 5.7 %collective-permute-start.22 = (f32[8,128]{1,0:T(8,128)S(1)}, f32[8,128]{1,0:T(8,128)S(1)}, u32[]{:S(2)}, u32[]{:S(2)}) collective-permute-start(f32[8,128]{1,0:T(8,128)S(1)} %add_add_fusion.1), channel_id=1, source_target_pairs={{0,3},{1,2},{2,1},{3,0},{4,7},{5,6},{6,5},{7,4},{8,11},{9,10},{10,... | collective-permute-start | bytes 12296 | tf_op jit(solution)/shard_map/ppermute | solution.py:392
  110.9 4.1 %collective-permute-start.21 = (f32[8,128]{1,0:T(8,128)S(1)}, f32[8,128]{1,0:T(8,128)S(1)}, u32[]{:S(2)}, u32[]{:S(2)}) collective-permute-start(f32[8,128]{1,0:T(8,128)S(1)} %add_add_fusion.1), channel_id=1, source_target_pairs={{0,2},{1,3},{2,0},{3,1},{4,6},{5,7},{6,4},{7,5},{8,10},{9,11},{10,... | collective-permute-start | bytes 12296 | tf_op jit(solution)/shard_map/ppermute | solution.py:392
  113.4 1.6 %collective-permute-start.20 = (f32[8,128]{1,0:T(8,128)S(1)}, f32[8,128]{1,0:T(8,128)S(1)}, u32[]{:S(2)}, u32[]{:S(2)}) collective-permute-start(f32[8,128]{1,0:T(8,128)S(1)} %add_add_fusion.1), channel_id=1, source_target_pairs={{0,1},{1,0},{2,3},{3,2},{4,5},{5,4},{6,7},{7,6},{8,9},{9,8},{10,11... | collective-permute-start | bytes 12296 | tf_op jit(solution)/shard_map/ppermute | solution.py:392
  (2 other events, 48.4 us)

commit v20 on v19

--- a/solution.py
+++ b/solution.py
@@ -62,22 +62,32 @@
 
 
 def tile_unit(left, right, vec, tile_ref, aside=None):
-    pieces = [slice(at, at + PIECE) for at in range(0, right.shape[1], PIECE)]
-    gram = lambda piece: jnp.dot(left, right[:, piece], preferred_element_type=F32)
-    product = lambda part: jnp.dot(vec, part, preferred_element_type=F32)
-    dist, part, terms = gram(pieces[0]), None, []
-    for index, piece in enumerate(pieces):
-        following = gram(pieces[index + 1]) if index + 1 < len(pieces) else None
+    cols = [slice(at, at + PIECE) for at in range(0, right.shape[1], PIECE)]
+    pieces = [(row, col) for row in range(0, left.shape[0], ROWS) for col in range(len(cols))]
+    gram = lambda row, col: jnp.dot(
+        left[row : row + ROWS], right[:, cols[col]], preferred_element_type=F32
+    )
+    terms = [0.0] * len(cols)
+
+    def product(row, col, part):
+        terms[col] = terms[col] + jnp.dot(
+            vec[:, row : row + ROWS], part, preferred_element_type=F32
+        )
+
+    dist, before = gram(*pieces[0]), None
+    for index, (row, col) in enumerate(pieces):
+        following = gram(*pieces[index + 1]) if index + 1 < len(pieces) else None
         strips = []
-        for at in range(0, left.shape[0], STRIP):
+        for at in range(0, ROWS, STRIP):
             strips.append(psi_power(dist[at : at + STRIP]))
-            tile_ref[at : at + STRIP, piece] = strips[-1]
-        if part is not None:
-            terms.append(product(part))
+            tile_ref[row + at : row + at + STRIP, cols[col]] = strips[-1]
+        if before is not None:
+            product(*before)
         if index == 1 and aside is not None:
             aside()
-        dist, part = following, jnp.concatenate(strips, axis=0)
-    return jnp.concatenate(terms + [product(part)], axis=1)
+        dist, before = following, (row, col, jnp.concatenate(strips, axis=0))
+    product(*before)
+    return jnp.concatenate(terms, axis=1)
 
 
 def unpack(pay):
@@ -191,9 +201,9 @@
     return fetch
 
 
-def half_tiles(early, slots_ref, right_ref, fetch, front_ref, back_ref, sum_ref, left_ref, vec_ref, pay_ref, sem_ref):
-    slot, step = pl.program_id(0), pl.program_id(1)
-    last = pl.num_programs(1) - 1
+def half_tiles(slots_ref, right_ref, fetch, front_ref, back_ref, sum_ref, left_ref, vec_ref, pay_ref, sem_ref):
+    slot = pl.program_id(0)
+    total = slots_ref[0]
 
     def arrive(which):
         pltpu.make_async_copy(
@@ -205,35 +215,32 @@
         left_ref[which % 2] = other_factor(feat)
         vec_ref[which % 2] = vec
 
-    @pl.when((slot == 0) & (step == 0) & (slots_ref[0] > 0))
+    @pl.when((slot == 0) & (total > 0))
     def _():
         fetch(0)
 
-    @pl.when(slot < slots_ref[0])
-    def _():
-        @pl.when((step == 0) & ((slot == 0) | (not early)))
+        @pl.when(total > 1)
         def _():
-            arrive(slot)
-            factor(slot)
-
-        @pl.when((step == 0) & (slot + 1 < slots_ref[0]))
+            fetch(1)
+
+        arrive(0)
+        factor(0)
+
+    @pl.when(slot + 1 < total)
+    def _():
+        arrive(slot + 1)
+
+    left, vec = left_ref.at[slot % 2], vec_ref.at[slot % 2]
+    for tile_ref, here in ((front_ref, slot < FRONT), (back_ref, slot >= FRONT)):
+        @pl.when((slot < total) & here)
         def _():
-            fetch(slot + 1)
-
-        if early:
-            @pl.when((step == last) & (slot + 1 < slots_ref[0]))
-            def _():
-                arrive(slot + 1)
-
-        rows = pl.ds(pl.multiple_of(step * ROWS, ROWS), ROWS)
-        place = slot % 2
-        left, vec = left_ref[place, rows, :], vec_ref[place, :, rows]
-        for tile_ref, here in ((front_ref, slot < FRONT), (back_ref, slot >= FRONT)):
-            for ends in (False, True) if early else (None,):
-                @pl.when(here if ends is None else here & ((step == last) == ends))
-                def _():
-                    aside = (lambda: factor(slot + 1)) if ends else None
-                    sum_ref[...] += tile_unit(left, right_ref[...], vec, tile_ref.at[0], aside)
+            sum_ref[...] += tile_unit(
+                left[...], right_ref[...], vec[...], tile_ref.at[0], lambda: factor(slot + 1)
+            )
+
+    @pl.when(slot + 2 < total)
+    def _():
+        fetch(slot + 2)
 
 
 def pair_zero_kernel(block_at, me_ref, right_ref, *refs):
@@ -241,7 +248,7 @@
     front_ref, back_ref, sum_ref, slots_ref = refs[-12:-8]
     left_ref, vec_ref, pay_ref, sem_ref, strip_ref, list_ref, lists_ref, strip_sem_ref = refs[-8:]
 
-    @pl.when((pl.program_id(0) == 0) & (pl.program_id(1) == 0))
+    @pl.when(pl.program_id(0) == 0)
     def _():
         strips = [
             pltpu.make_async_copy(
@@ -264,25 +271,25 @@
 
     fetch = fetch_from(block_at, block_refs, slots_ref, pay_ref, sem_ref)
     half_tiles(
-        True, slots_ref, right_ref, fetch, front_ref, back_ref, sum_ref, left_ref, vec_ref, pay_ref, sem_ref
+        slots_ref, right_ref, fetch, front_ref, back_ref, sum_ref, left_ref, vec_ref, pay_ref, sem_ref
     )
 
 
 def pair_one_kernel(block_at, slots_ref, right_ref, first_ref, rhs_ref, var_ref, *refs):
     block_refs = refs[:-8]
     front_ref, back_ref, image_ref, send_ref, left_ref, vec_ref, pay_ref, sem_ref = refs[-8:]
-    slot, step = pl.program_id(0), pl.program_id(1)
-
-    @pl.when((slot == 0) & (step == 0))
+    slot = pl.program_id(0)
+
+    @pl.when(slot == 0)
     def _():
         image_ref[...] = first_ref[...]
 
     fetch = fetch_from(block_at, block_refs, slots_ref, pay_ref, sem_ref)
     half_tiles(
-        False, slots_ref, right_ref, fetch, front_ref, back_ref, image_ref, left_ref, vec_ref, pay_ref, sem_ref
+        slots_ref, right_ref, fetch, front_ref, back_ref, image_ref, left_ref, vec_ref, pay_ref, sem_ref
     )
 
-    @pl.when((slot == pl.num_programs(0) - 1) & (step == pl.num_programs(1) - 1))
+    @pl.when(slot == pl.num_programs(0) - 1)
     def _():
         rhs = rhs_ref[...]
         width = rhs.shape[1]
@@ -517,15 +524,12 @@
     zero_at = [(at, row * 96) for at in range(len(zero)) for row in range(each)]
     one_at = [(at, row * 80) for at in range(len(one)) for row in range(each)]
 
-    half = steps // 2
-
-    def front_at(k, i, *ignored):
-        return (jnp.minimum(k, FRONT - 1), jnp.where(k < FRONT, i, half - 1), 0)
-
-    def back_at(k, i, *ignored):
-        return (jnp.maximum(k - FRONT, 0), jnp.where(k < FRONT, 0, i), 0)
-
-    half_specs = [pl.BlockSpec((1, ROWS, width), front_at), pl.BlockSpec((1, ROWS, width), back_at)]
+    half_block = (1, width // 2, width)
+    half_specs = [
+        pl.BlockSpec(half_block, lambda k, *ignored: (jnp.minimum(k, FRONT - 1), 0, 0)),
+        pl.BlockSpec(half_block, lambda k, *ignored: (jnp.maximum(k - FRONT, 0), 0, 0)),
+    ]
+    half_params = pltpu.CompilerParams(vmem_limit_bytes=18 * 1024 * 1024)
     half_shapes = [
         pltpu.VMEM((FRONT, width // 2, width), BF16),
         pltpu.HBM((most - FRONT, width // 2, width), BF16),
@@ -542,7 +546,7 @@
         functools.partial(pair_zero_kernel, zero_at),
         grid_spec=pltpu.PrefetchScalarGridSpec(
             num_scalar_prefetch=1,
-            grid=(most, half),
+            grid=(most,),
             in_specs=[right_spec] + [row_spec] * PARTS + [any_spec] * len(zero),
             out_specs=half_specs + [row_spec, smem],
             scratch_shapes=half_scratch
@@ -555,20 +559,20 @@
         ),
         out_shape=half_shapes
         + [shape(right_side.shape, F32), shape((most + 2,), jnp.int32)],
-        compiler_params=params,
+        compiler_params=half_params,
         name="pair_zero",
     )(me, right, *[part[2] for part in own_parts], *zero)
     front_one, back_one, image, send = pl.pallas_call(
         functools.partial(pair_one_kernel, one_at),
         grid_spec=pltpu.PrefetchScalarGridSpec(
             num_scalar_prefetch=1,
-            grid=(most, half),
+            grid=(most,),
             in_specs=[right_spec, row_spec, row_spec, var_spec] + [any_spec] * len(one),
             out_specs=half_specs + [row_spec, pl.BlockSpec(send_shape, whole)],
             scratch_shapes=half_scratch,
         ),
         out_shape=half_shapes + [shape(right_side.shape, F32), shape(send_shape, BF16)],
-        compiler_params=params,
+        compiler_params=half_params,
         name="pair_one",
     )(slots, right, half_sum, right_side, var_row, *one)
     fronts = [pltpu.with_memory_space_constraint(part, pltpu.VMEM) for part in (front_zero, front_one)]

time: 118 us -> 121 us (1.025); the launches traced: 116 us -> 121 us
  Pallas kernels: 56.7 us -> 76.7 us
  starting transfers between devices: 39.9 us -> 27.2 us
  waiting for transfers between devices: 16.6 us -> 13.9 us
    ppermute x23, starting transfers between devices: 39.9 us -> 27.2 us  [swap(): return lax.ppermute(value, 'row', [(i, i ^ mask) for i in range(count)])]
    pallas_call x1, Pallas kernels: 17.4 us -> 25.3 us  [local(): pl.pallas_call(functools.partial(pair_one_kernel, one_at), grid_spec=pltp...]
    pallas_call x1, Pallas kernels: 18.2 us -> 25.8 us  [local(): pl.pallas_call(functools.partial(pair_zero_kernel, zero_at), grid_spec=pl...]
    pallas_call x1, Pallas kernels: 4.58 us -> 9.07 us  [local(): pl.pallas_call(again_kernel, grid_spec=pltpu.PrefetchScalarGridSpec(num_s...]
    ppermute x23, waiting for transfers between devices: 16.6 us -> 13.9 us  [swap(): return lax.ppermute(value, 'row', [(i, i ^ mask) for i in range(count)])]
  transfers between devices with their start and end apart: 23 -> 23, of which waited for: 7 -> 6; matrix products, arithmetic and copies ran while one was open for 0% -> 0% of each run, Pallas kernels for 29% -> 34%
where the time goes in v20:
time: 121 us
  Pallas kernels  76.7 us (63%)
  starting transfers between devices  27.2 us (22%)
  waiting for transfers between devices  13.9 us (11%)
    ppermute x23, starting transfers between devices, swap(): return lax.ppermute(value, 'row', [(i, i ^ mask) for i in range(count)])  27.2 us
    pallas_call x1, Pallas kernels, local(): pl.pallas_call(functools.partial(pair_zero_kernel, zero_at), grid_spec=pl...  25.8 us
    pallas_call x1, Pallas kernels, local(): pl.pallas_call(functools.partial(pair_one_kernel, one_at), grid_spec=pltp...  25.3 us
    ppermute x23, waiting for transfers between devices, swap(): return lax.ppermute(value, 'row', [(i, i ^ mask) for i in range(count)])  13.9 us
    pallas_call x2, Pallas kernels, own_part(): pl.pallas_call(functools.partial(own_kernel, rows), in_specs=[vmem, vmem,...  9.62 us
    pallas_call x1, Pallas kernels, local(): pl.pallas_call(again_kernel, grid_spec=pltpu.PrefetchScalarGridSpec(num_s...  9.07 us
    pallas_call x2, Pallas kernels, local(): pl.pallas_call(functools.partial(own_again_kernel, blocks), in_specs=[any...  4.34 us
  transfers between devices with their start and end apart: 23, of which 6 were waited for; matrix products, arithmetic and copies ran while one was open for 0% of the time, Pallas kernels for 34%

profile of v20, /device:TPU:0, one launch (start us, length us, event | category | flops | bytes accessed | tf_op | source)
XLA Modules:
  0.0 120.7 jit_solution(16674925025540260489)
XLA Ops:
  1.4 1.2 payload.1
  2.6 5.1 %collective-permute-start.2 = (bf16[96,512]{1,0:T(8,128)(2,1)S(1)}, bf16[96,512]{1,0:T(8,128)(2,1)S(1)}, u32[]{:S(2)}, u32[]{:S(2)}) collective-permute-start(bf16[96,512]{1,0:T(8,128)(2,1)S(1)} %get-tuple-element.26), channel_id=1, source_target_pairs={{0,12},{1,13},{2,14},{3,15},{4,8},{5,9},{6,10},{7,11},{8,4},{9,5},... | collective-permute-start | bytes 294920 | tf_op jit(solution)/shard_map/ppermute | solution.py:399
  8.3 4.0 %own_tile_0.1 = (bf16[4,512,512]{2,1,0:T(8,128)(2,1)}, f32[8,2048]{1,0:T(8,128)S(1)}) custom-call(bf16[2048,128]{1,0:T(8,128)(2,1)S(1)} %get-tuple-element.23.left_ref, bf16[128,2048]{1,0:T(8,128)(2,1)S(1)} %get-tuple-element.22.right_ref.arrived_ref, bf16[8,2048]{1,0:T(8,128)(2,1)S(1)} %get-tuple-element.24.vec_ref, ...), custom_call_target="tpu_custom_call" | custom-call | flops 5000000000 | bytes 2097152 | tf_op jit(solution)/shard_map/own_tile_0/pallas_call | solution.py:489
  12.3 3.8 %collective-permute-start.8 = (bf16[80,512]{1,0:T(8,128)(2,1)S(1)}, bf16[80,512]{1,0:T(8,128)(2,1)S(1)}, u32[]{:S(2)}, u32[]{:S(2)}) collective-permute-start(bf16[80,512]{1,0:T(8,128)(2,1)S(1)} %gate.6), channel_id=1, source_target_pairs={{0,12},{1,13},{2,14},{3,15},{4,8},{5,9},{6,10},{7,11},{8,4},{9,5},... | collective-permute-start | bytes 245768 | tf_op jit(solution)/shard_map/ppermute | solution.py:399
  16.8 3.1 %collective-permute-done.1 = bf16[96,512]{1,0:T(8,128)(2,1)S(1)} collective-permute-done((bf16[96,512]{1,0:T(8,128)(2,1)S(1)}, bf16[96,512]{1,0:T(8,128)(2,1)S(1)}, u32[]{:S(2)}, u32[]{:S(2)}) %collective-permute-start.1) | collective-permute-done | bytes 98336 | tf_op jit(solution)/shard_map/ppermute | solution.py:399
  20.0 1.6 %collective-permute-start.3 = (bf16[384,512]{1,0:T(8,128)(2,1)S(1)}, bf16[384,512]{1,0:T(8,128)(2,1)S(1)}, u32[]{:S(2)}, u32[]{:S(2)}) collective-permute-start(bf16[384,512]{1,0:T(8,128)(2,1)S(1)} %gate.4.arrived_ref.refs_2_), channel_id=1, source_target_pairs={{0,2},{1,3},{2,0},{3,1},{4,6},{5,7},{6,4},{7,5},{8,10},{9,11},{10,... | collective-permute-start | bytes 1179656 | tf_op jit(solution)/shard_map/ppermute | solution.py:399
  21.6 5.6 %own_tile_1.1 = (bf16[6,512,512]{2,1,0:T(8,128)(2,1)}, f32[8,2048]{1,0:T(8,128)S(1)}) custom-call(bf16[2048,128]{1,0:T(8,128)(2,1)S(1)} %get-tuple-element.23.left_ref, bf16[128,2048]{1,0:T(8,128)(2,1)S(1)} %get-tuple-element.22.right_ref.arrived_ref, bf16[8,2048]{1,0:T(8,128)(2,1)S(1)} %get-tuple-element.24.vec_ref, ...), custom_call_target="tpu_custom_call" | custom-call | flops 5000000000 | bytes 3145728 | tf_op jit(solution)/shard_map/own_tile_1/pallas_call | solution.py:489
  27.2 4.3 %collective-permute-done.3.refs_0_ = bf16[384,512]{1,0:T(8,128)(2,1)S(1)} collective-permute-done((bf16[384,512]{1,0:T(8,128)(2,1)S(1)}, bf16[384,512]{1,0:T(8,128)(2,1)S(1)}, u32[]{:S(2)}, u32[]{:S(2)}) %collective-permute-start.3) | collective-permute-done | bytes 393248 | tf_op jit(solution)/shard_map/ppermute | solution.py:399
  31.6 1.7 %collective-permute-start.11 = (bf16[320,512]{1,0:T(8,128)(2,1)S(1)}, bf16[320,512]{1,0:T(8,128)(2,1)S(1)}, u32[]{:S(2)}, u32[]{:S(2)}) collective-permute-start(bf16[320,512]{1,0:T(8,128)(2,1)S(1)} %gate.7.refs_0_), channel_id=1, source_target_pairs={{0,3},{1,2},{2,1},{3,0},{4,7},{5,6},{6,5},{7,4},{8,11},{9,10},{10,... | collective-permute-start | bytes 983048 | tf_op jit(solution)/shard_map/ppermute | solution.py:399
  33.9 25.8 %pair_zero.1 = (bf16[3,1024,2048]{2,1,0:T(8,128)(2,1)S(1)}, bf16[2,1024,2048]{2,1,0:T(8,128)(2,1)}, f32[8,2048]{1,0:T(8,128)S(1)}, s32[7]{0:T(128)S(1)}) custom-call(s32[1]{0:T(128)} %bitcast.me_ref, bf16[128,2048]{1,0:T(8,128)(2,1)S(1)} %get-tuple-element.22.right_ref.arrived_ref, f32[8,2048]{1,0:T(8,128)S(1)} %get-tuple-element.25.refs_1_.refs_0_, ...), custom_call_target="tpu_custom_call" | custom-call | tf_op jit(solution)/shard_map/pair_zero/pallas_call | solution.py:545
  59.7 25.3 %pair_one.1 = (bf16[3,1024,2048]{2,1,0:T(8,128)(2,1)S(1)}, bf16[2,1024,2048]{2,1,0:T(8,128)(2,1)}, f32[8,2048]{1,0:T(8,128)S(1)}, bf16[8,2176]{1,0:T(8,128)(2,1)S(1)}) custom-call(s32[7]{0:T(128)S(1)} %get-tuple-element.28.slots_ref, bf16[128,2048]{1,0:T(8,128)(2,1)S(1)} %get-tuple-element.22.right_ref.arrived_ref, ...), custom_call_target="tpu_custom_call" | custom-call | tf_op jit(solution)/shard_map/pair_one/pallas_call | solution.py:565
  85.2 4.3 %collective-permute-start.12 = (bf16[1,8,2176]{2,1,0:T(8,128)(2,1)S(1)}, bf16[1,8,2176]{2,1,0:T(8,128)(2,1)S(1)}, u32[]{:S(2)}, u32[]{:S(2)}) collective-permute-start(bf16[1,8,2176]{2,1,0:T(8,128)(2,1)S(1)} %bitcast.7), channel_id=1, source_target_pairs={{0,4},{1,5},{2,6},{3,7},{4,0},{5,1},{6,2},{7,3},{8,12},{9,13},{10,... | collective-permute-start | bytes 104456 | tf_op jit(solution)/shard_map/ppermute | solution.py:399
  89.5 2.4 %own_again_1.1.refs_1_ = f32[8,2048]{1,0:T(8,128)S(1)} custom-call(bf16[6,512,512]{2,1,0:T(8,128)(2,1)} %get-tuple-element.38.in_ref, bf16[8,2176]{1,0:T(8,128)(2,1)S(1)} %get-tuple-element.35.vec_ref), custom_call_target="tpu_custom_call" | custom-call | flops 5000000000 | bytes 3145728 | tf_op jit(solution)/shard_map/own_again_1/pallas_call | solution.py:583
  91.9 1.9 %collective-permute-start.15 = (bf16[4,8,2176]{2,1,0:T(8,128)(2,1)S(1)}, bf16[4,8,2176]{2,1,0:T(8,128)(2,1)S(1)}, u32[]{:S(2)}, u32[]{:S(2)}) collective-permute-start(bf16[4,8,2176]{2,1,0:T(8,128)(2,1)S(1)} %pad_maximum_fusion.2), channel_id=1, source_target_pairs={{0,2},{1,3},{2,0},{3,1},{4,6},{5,7},{6,4},{7,5},{8,10},{9,11},{10,... | collective-permute-start | bytes 417800 | tf_op jit(solution)/shard_map/ppermute | solution.py:399
  93.9 4.0 %collective-permute-done.15 = bf16[4,8,2176]{2,1,0:T(8,128)(2,1)S(1)} collective-permute-done((bf16[4,8,2176]{2,1,0:T(8,128)(2,1)S(1)}, bf16[4,8,2176]{2,1,0:T(8,128)(2,1)S(1)}, u32[]{:S(2)}, u32[]{:S(2)}) %collective-permute-start.15) | collective-permute-done | bytes 139296 | tf_op jit(solution)/shard_map/ppermute | solution.py:399
  98.0 2.0 %own_again_0.1.refs_0_ = f32[8,2048]{1,0:T(8,128)S(1)} custom-call(bf16[4,512,512]{2,1,0:T(8,128)(2,1)} %get-tuple-element.37.in_ref, bf16[8,2176]{1,0:T(8,128)(2,1)S(1)} %get-tuple-element.35.vec_ref), custom_call_target="tpu_custom_call" | custom-call | flops 5000000000 | bytes 2097152 | tf_op jit(solution)/shard_map/own_again_0/pallas_call | solution.py:583
  100.0 9.1 %pair_again.1 = (f32[32,2048]{1,0:T(8,128)S(1)}, f32[8,128]{1,0:T(8,128)S(1)}, f32[8,128]{1,0:T(8,128)S(1)}) custom-call(s32[7]{0:T(128)S(1)} %get-tuple-element.28.slots_ref, bf16[3,1024,2048]{2,1,0:T(8,128)(2,1)S(1)} %get-tuple-element.29.front_zero_ref, bf16[3,1024,2048]{2,1,0:T(8,128)(2,1)S(1)} %get-tuple-element.32.front_one_ref, ...), custom_call_target="tpu_custom_call" | custom-call | tf_op jit(solution)/shard_map/pair_again/pallas_call | solution.py:601
  109.2 1.1 collective-permute-start.18
  110.2 3.3 %collective-permute-start.17 = (f32[8,128]{1,0:T(8,128)S(1)}, f32[8,128]{1,0:T(8,128)S(1)}, u32[]{:S(2)}, u32[]{:S(2)}) collective-permute-start(f32[8,128]{1,0:T(8,128)S(1)} %get-tuple-element.41), channel_id=1, source_target_pairs={{0,4},{1,5},{2,6},{3,7},{4,0},{5,1},{6,2},{7,3},{8,12},{9,13},{10,... | collective-permute-start | bytes 12296 | tf_op jit(solution)/shard_map/ppermute | solution.py:399
  113.5 1.0 collective-permute-done.19
  115.1 1.0 collective-permute-start.22
  116.1 1.2 %collective-permute-start.21 = (f32[8,128]{1,0:T(8,128)S(1)}, f32[8,128]{1,0:T(8,128)S(1)}, u32[]{:S(2)}, u32[]{:S(2)}) collective-permute-start(f32[8,128]{1,0:T(8,128)S(1)} %add_add_fusion.1), channel_id=1, source_target_pairs={{0,2},{1,3},{2,0},{3,1},{4,6},{5,7},{6,4},{7,5},{8,10},{9,11},{10,... | collective-permute-start | bytes 12296 | tf_op jit(solution)/shard_map/ppermute | solution.py:399
  117.3 1.5 %curve_order.1 = f32[32,2048]{1,0:T(8,128)S(1)} custom-call(f32[32,2048]{1,0:T(8,128)S(1)} %get-tuple-element.40.rows_ref, s32[1,2048]{1,0:T(1,128)S(1)} %copy-done.2), custom_call_target="tpu_custom_call" | custom-call | tf_op jit(solution)/shard_map/curve_order/pallas_call | solution.py:639
  118.8 0.9 collective-permute-done.21
  (55 shorter events, 4.8 us)
Async XLA Ops:
  2.6 13.6 %collective-permute-start.2 = (bf16[96,512]{1,0:T(8,128)(2,1)S(1)}, bf16[96,512]{1,0:T(8,128)(2,1)S(1)}, u32[]{:S(2)}, u32[]{:S(2)}) collective-permute-start(bf16[96,512]{1,0:T(8,128)(2,1)S(1)} %get-tuple-element.26), channel_id=1, source_target_pairs={{0,12},{1,13},{2,14},{3,15},{4,8},{5,9},{6,10},{7,11},{8,4},{9,5},... | collective-permute-start | bytes 294920 | tf_op jit(solution)/shard_map/ppermute | solution.py:399
  7.7 12.2 %collective-permute-start.1 = (bf16[96,512]{1,0:T(8,128)(2,1)S(1)}, bf16[96,512]{1,0:T(8,128)(2,1)S(1)}, u32[]{:S(2)}, u32[]{:S(2)}) collective-permute-start(bf16[96,512]{1,0:T(8,128)(2,1)S(1)} %get-tuple-element.26), channel_id=1, source_target_pairs={{0,8},{1,9},{2,10},{3,11},{4,12},{5,13},{6,14},{7,15},{8,0},{9,1},... | collective-permute-start | bytes 294920 | tf_op jit(solution)/shard_map/ppermute | solution.py:399
  7.7 12.2 %collective-permute-start = (bf16[96,512]{1,0:T(8,128)(2,1)S(1)}, bf16[96,512]{1,0:T(8,128)(2,1)S(1)}, u32[]{:S(2)}, u32[]{:S(2)}) collective-permute-start(bf16[96,512]{1,0:T(8,128)(2,1)S(1)} %get-tuple-element.26), channel_id=1, source_target_pairs={{0,4},{1,5},{2,6},{3,7},{4,0},{5,1},{6,2},{7,3},{8,12},{9,13},{10,... | collective-permute-start | bytes 294920 | tf_op jit(solution)/shard_map/ppermute | solution.py:399
  12.3 19.2 %collective-permute-start.8 = (bf16[80,512]{1,0:T(8,128)(2,1)S(1)}, bf16[80,512]{1,0:T(8,128)(2,1)S(1)}, u32[]{:S(2)}, u32[]{:S(2)}) collective-permute-start(bf16[80,512]{1,0:T(8,128)(2,1)S(1)} %gate.6), channel_id=1, source_target_pairs={{0,12},{1,13},{2,14},{3,15},{4,8},{5,9},{6,10},{7,11},{8,4},{9,5},... | collective-permute-start | bytes 245768 | tf_op jit(solution)/shard_map/ppermute | solution.py:399
  16.1 15.4 %collective-permute-start.7 = (bf16[80,512]{1,0:T(8,128)(2,1)S(1)}, bf16[80,512]{1,0:T(8,128)(2,1)S(1)}, u32[]{:S(2)}, u32[]{:S(2)}) collective-permute-start(bf16[80,512]{1,0:T(8,128)(2,1)S(1)} %gate.6), channel_id=1, source_target_pairs={{0,8},{1,9},{2,10},{3,11},{4,12},{5,13},{6,14},{7,15},{8,0},{9,1},... | collective-permute-start | bytes 245768 | tf_op jit(solution)/shard_map/ppermute | solution.py:399
  16.2 15.4 %collective-permute-start.6 = (bf16[80,512]{1,0:T(8,128)(2,1)S(1)}, bf16[80,512]{1,0:T(8,128)(2,1)S(1)}, u32[]{:S(2)}, u32[]{:S(2)}) collective-permute-start(bf16[80,512]{1,0:T(8,128)(2,1)S(1)} %gate.6), channel_id=1, source_target_pairs={{0,4},{1,5},{2,6},{3,7},{4,0},{5,1},{6,2},{7,3},{8,12},{9,13},{10,... | collective-permute-start | bytes 245768 | tf_op jit(solution)/shard_map/ppermute | solution.py:399
  19.9 39.7 %copy-start = (f32[8,2048]{1,0:T(8,128)S(1)}, f32[8,2048]{1,0:T(8,128)}, u32[]{:S(2)}) copy-start(f32[8,2048]{1,0:T(8,128)} %rhs_ref.5) | copy-start | bytes 196612
  20.0 13.9 %collective-permute-start.4 = (bf16[384,512]{1,0:T(8,128)(2,1)S(1)}, bf16[384,512]{1,0:T(8,128)(2,1)S(1)}, u32[]{:S(2)}, u32[]{:S(2)}) collective-permute-start(bf16[384,512]{1,0:T(8,128)(2,1)S(1)} %gate.4.arrived_ref.refs_2_), channel_id=1, source_target_pairs={{0,1},{1,0},{2,3},{3,2},{4,5},{5,4},{6,7},{7,6},{8,9},{9,8},{10,11... | collective-permute-start | bytes 1179656 | tf_op jit(solution)/shard_map/ppermute | solution.py:399
  20.0 11.5 %collective-permute-start.3 = (bf16[384,512]{1,0:T(8,128)(2,1)S(1)}, bf16[384,512]{1,0:T(8,128)(2,1)S(1)}, u32[]{:S(2)}, u32[]{:S(2)}) collective-permute-start(bf16[384,512]{1,0:T(8,128)(2,1)S(1)} %gate.4.arrived_ref.refs_2_), channel_id=1, source_target_pairs={{0,2},{1,3},{2,0},{3,1},{4,6},{5,7},{6,4},{7,5},{8,10},{9,11},{10,... | collective-permute-start | bytes 1179656 | tf_op jit(solution)/shard_map/ppermute | solution.py:399
  31.6 2.3 %collective-permute-start.5 = (bf16[384,512]{1,0:T(8,128)(2,1)S(1)}, bf16[384,512]{1,0:T(8,128)(2,1)S(1)}, u32[]{:S(2)}, u32[]{:S(2)}) collective-permute-start(bf16[384,512]{1,0:T(8,128)(2,1)S(1)} %gate.5.refs_3_), channel_id=1, source_target_pairs={{0,1},{1,0},{2,3},{3,2},{4,5},{5,4},{6,7},{7,6},{8,9},{9,8},{10,11... | collective-permute-start | bytes 1179656 | tf_op jit(solution)/shard_map/ppermute | solution.py:399
  31.6 28.0 %collective-permute-start.11 = (bf16[320,512]{1,0:T(8,128)(2,1)S(1)}, bf16[320,512]{1,0:T(8,128)(2,1)S(1)}, u32[]{:S(2)}, u32[]{:S(2)}) collective-permute-start(bf16[320,512]{1,0:T(8,128)(2,1)S(1)} %gate.7.refs_0_), channel_id=1, source_target_pairs={{0,3},{1,2},{2,1},{3,0},{4,7},{5,6},{6,5},{7,4},{8,11},{9,10},{10,... | collective-permute-start | bytes 983048 | tf_op jit(solution)/shard_map/ppermute | solution.py:399
  33.3 26.3 %collective-permute-start.10 = (bf16[320,512]{1,0:T(8,128)(2,1)S(1)}, bf16[320,512]{1,0:T(8,128)(2,1)S(1)}, u32[]{:S(2)}, u32[]{:S(2)}) collective-permute-start(bf16[320,512]{1,0:T(8,128)(2,1)S(1)} %gate.7.refs_0_), channel_id=1, source_target_pairs={{0,1},{1,0},{2,3},{3,2},{4,5},{5,4},{6,7},{7,6},{8,9},{9,8},{10,11... | collective-permute-start | bytes 983048 | tf_op jit(solution)/shard_map/ppermute | solution.py:399
  33.3 26.3 %collective-permute-start.9 = (bf16[320,512]{1,0:T(8,128)(2,1)S(1)}, bf16[320,512]{1,0:T(8,128)(2,1)}, u32[]{:S(2)}, u32[]{:S(2)}) collective-permute-start(bf16[320,512]{1,0:T(8,128)(2,1)S(1)} %gate.7.refs_0_), channel_id=1, source_target_pairs={{0,2},{1,3},{2,0},{3,1},{4,6},{5,7},{6,4},{7,5},{8,10},{9,11},{10,... | collective-permute-start | bytes 983048 | tf_op jit(solution)/shard_map/ppermute | solution.py:399
  85.0 6.8 %collective-permute-start.14 = (bf16[1,8,2176]{2,1,0:T(8,128)(2,1)S(1)}, bf16[1,8,2176]{2,1,0:T(8,128)(2,1)S(1)}, u32[]{:S(2)}, u32[]{:S(2)}) collective-permute-start(bf16[1,8,2176]{2,1,0:T(8,128)(2,1)S(1)} %bitcast.5), channel_id=1, source_target_pairs={{0,12},{1,13},{2,14},{3,15},{4,8},{5,9},{6,10},{7,11},{8,4},{9,5},... | collective-permute-start | bytes 104456 | tf_op jit(solution)/shard_map/ppermute | solution.py:399
  85.1 6.8 %collective-permute-start.13 = (bf16[1,8,2176]{2,1,0:T(8,128)(2,1)S(1)}, bf16[1,8,2176]{2,1,0:T(8,128)(2,1)S(1)}, u32[]{:S(2)}, u32[]{:S(2)}) collective-permute-start(bf16[1,8,2176]{2,1,0:T(8,128)(2,1)S(1)} %bitcast.6), channel_id=1, source_target_pairs={{0,8},{1,9},{2,10},{3,11},{4,12},{5,13},{6,14},{7,15},{8,0},{9,1},... | collective-permute-start | bytes 104456 | tf_op jit(solution)/shard_map/ppermute | solution.py:399
  85.2 6.7 %collective-permute-start.12 = (bf16[1,8,2176]{2,1,0:T(8,128)(2,1)S(1)}, bf16[1,8,2176]{2,1,0:T(8,128)(2,1)S(1)}, u32[]{:S(2)}, u32[]{:S(2)}) collective-permute-start(bf16[1,8,2176]{2,1,0:T(8,128)(2,1)S(1)} %bitcast.7), channel_id=1, source_target_pairs={{0,4},{1,5},{2,6},{3,7},{4,0},{5,1},{6,2},{7,3},{8,12},{9,13},{10,... | collective-permute-start | bytes 104456 | tf_op jit(solution)/shard_map/ppermute | solution.py:399
  91.9 5.9 %collective-permute-start.15 = (bf16[4,8,2176]{2,1,0:T(8,128)(2,1)S(1)}, bf16[4,8,2176]{2,1,0:T(8,128)(2,1)S(1)}, u32[]{:S(2)}, u32[]{:S(2)}) collective-permute-start(bf16[4,8,2176]{2,1,0:T(8,128)(2,1)S(1)} %pad_maximum_fusion.2), channel_id=1, source_target_pairs={{0,2},{1,3},{2,0},{3,1},{4,6},{5,7},{6,4},{7,5},{8,10},{9,11},{10,... | collective-permute-start | bytes 417800 | tf_op jit(solution)/shard_map/ppermute | solution.py:399
  97.9 2.1 %collective-permute-start.16 = (bf16[8,8,2176]{2,1,0:T(8,128)(2,1)S(1)}, bf16[8,8,2176]{2,1,0:T(8,128)(2,1)S(1)}, u32[]{:S(2)}, u32[]{:S(2)}) collective-permute-start(bf16[8,8,2176]{2,1,0:T(8,128)(2,1)S(1)} %get-tuple-element.47), channel_id=1, source_target_pairs={{0,1},{1,0},{2,3},{3,2},{4,5},{5,4},{6,7},{7,6},{8,9},{9,8},{10,11... | collective-permute-start | bytes 835592 | tf_op jit(solution)/shard_map/ppermute | solution.py:399
  109.1 5.5 %collective-permute-start.19 = (f32[8,128]{1,0:T(8,128)S(1)}, f32[8,128]{1,0:T(8,128)S(1)}, u32[]{:S(2)}, u32[]{:S(2)}) collective-permute-start(f32[8,128]{1,0:T(8,128)S(1)} %get-tuple-element.41), channel_id=1, source_target_pairs={{0,12},{1,13},{2,14},{3,15},{4,8},{5,9},{6,10},{7,11},{8,4},{9,5},... | collective-permute-start | bytes 12296 | tf_op jit(solution)/shard_map/ppermute | solution.py:399
  109.2 5.4 %collective-permute-start.18 = (f32[8,128]{1,0:T(8,128)S(1)}, f32[8,128]{1,0:T(8,128)S(1)}, u32[]{:S(2)}, u32[]{:S(2)}) collective-permute-start(f32[8,128]{1,0:T(8,128)S(1)} %get-tuple-element.41), channel_id=1, source_target_pairs={{0,8},{1,9},{2,10},{3,11},{4,12},{5,13},{6,14},{7,15},{8,0},{9,1},... | collective-permute-start | bytes 12296 | tf_op jit(solution)/shard_map/ppermute | solution.py:399
  110.2 4.9 %collective-permute-start.17 = (f32[8,128]{1,0:T(8,128)S(1)}, f32[8,128]{1,0:T(8,128)S(1)}, u32[]{:S(2)}, u32[]{:S(2)}) collective-permute-start(f32[8,128]{1,0:T(8,128)S(1)} %get-tuple-element.41), channel_id=1, source_target_pairs={{0,4},{1,5},{2,6},{3,7},{4,0},{5,1},{6,2},{7,3},{8,12},{9,13},{10,... | collective-permute-start | bytes 12296 | tf_op jit(solution)/shard_map/ppermute | solution.py:399
  115.1 3.7 %collective-permute-start.22 = (f32[8,128]{1,0:T(8,128)S(1)}, f32[8,128]{1,0:T(8,128)S(1)}, u32[]{:S(2)}, u32[]{:S(2)}) collective-permute-start(f32[8,128]{1,0:T(8,128)S(1)} %add_add_fusion.1), channel_id=1, source_target_pairs={{0,3},{1,2},{2,1},{3,0},{4,7},{5,6},{6,5},{7,4},{8,11},{9,10},{10,... | collective-permute-start | bytes 12296 | tf_op jit(solution)/shard_map/ppermute | solution.py:399
  116.1 3.6 %collective-permute-start.21 = (f32[8,128]{1,0:T(8,128)S(1)}, f32[8,128]{1,0:T(8,128)S(1)}, u32[]{:S(2)}, u32[]{:S(2)}) collective-permute-start(f32[8,128]{1,0:T(8,128)S(1)} %add_add_fusion.1), channel_id=1, source_target_pairs={{0,2},{1,3},{2,0},{3,1},{4,6},{5,7},{6,4},{7,5},{8,10},{9,11},{10,... | collective-permute-start | bytes 12296 | tf_op jit(solution)/shard_map/ppermute | solution.py:399
  117.3 2.4 %collective-permute-start.20 = (f32[8,128]{1,0:T(8,128)S(1)}, f32[8,128]{1,0:T(8,128)S(1)}, u32[]{:S(2)}, u32[]{:S(2)}) collective-permute-start(f32[8,128]{1,0:T(8,128)S(1)} %add_add_fusion.1), channel_id=1, source_target_pairs={{0,1},{1,0},{2,3},{3,2},{4,5},{5,4},{6,7},{7,6},{8,9},{9,8},{10,11... | collective-permute-start | bytes 12296 | tf_op jit(solution)/shard_map/ppermute | solution.py:399
  (2 other events, 57.1 us)

commit v21 on v19

--- a/solution.py
+++ b/solution.py
@@ -61,7 +61,14 @@
     return (jnp.exp2(19.0 * lax.log2(u)) * (1.0 - u)).astype(BF16)
 
 
-def tile_unit(left, right, vec, tile_ref, aside=None):
+def psi_natural(dist):
+    dist = jnp.maximum(dist, 1e-30)
+    radius = dist * lax.rsqrt(dist)
+    u = jnp.maximum(SHRINK - radius, 1e-30)
+    return (jnp.exp(19.0 * jnp.log(u)) * (1.0 - u)).astype(BF16)
+
+
+def tile_unit(left, right, vec, tile_ref, aside=None, psi=psi_power):
     pieces = [slice(at, at + PIECE) for at in range(0, right.shape[1], PIECE)]
     gram = lambda piece: jnp.dot(left, right[:, piece], preferred_element_type=F32)
     product = lambda part: jnp.dot(vec, part, preferred_element_type=F32)
@@ -70,7 +77,7 @@
         following = gram(pieces[index + 1]) if index + 1 < len(pieces) else None
         strips = []
         for at in range(0, left.shape[0], STRIP):
-            strips.append(psi_power(dist[at : at + STRIP]))
+            strips.append(psi(dist[at : at + STRIP]))
             tile_ref[at : at + STRIP, piece] = strips[-1]
         if part is not None:
             terms.append(product(part))
@@ -191,7 +198,7 @@
     return fetch
 
 
-def half_tiles(early, slots_ref, right_ref, fetch, front_ref, back_ref, sum_ref, left_ref, vec_ref, pay_ref, sem_ref):
+def half_tiles(early, psi, slots_ref, right_ref, fetch, front_ref, back_ref, sum_ref, left_ref, vec_ref, pay_ref, sem_ref):
     slot, step = pl.program_id(0), pl.program_id(1)
     last = pl.num_programs(1) - 1
 
@@ -233,7 +240,7 @@
                 @pl.when(here if ends is None else here & ((step == last) == ends))
                 def _():
                     aside = (lambda: factor(slot + 1)) if ends else None
-                    sum_ref[...] += tile_unit(left, right_ref[...], vec, tile_ref.at[0], aside)
+                    sum_ref[...] += tile_unit(left, right_ref[...], vec, tile_ref.at[0], aside, psi)
 
 
 def pair_zero_kernel(block_at, me_ref, right_ref, *refs):
@@ -264,7 +271,7 @@
 
     fetch = fetch_from(block_at, block_refs, slots_ref, pay_ref, sem_ref)
     half_tiles(
-        True, slots_ref, right_ref, fetch, front_ref, back_ref, sum_ref, left_ref, vec_ref, pay_ref, sem_ref
+        True, psi_natural, slots_ref, right_ref, fetch, front_ref, back_ref, sum_ref, left_ref, vec_ref, pay_ref, sem_ref
     )
 
 
@@ -279,7 +286,7 @@
 
     fetch = fetch_from(block_at, block_refs, slots_ref, pay_ref, sem_ref)
     half_tiles(
-        False, slots_ref, right_ref, fetch, front_ref, back_ref, image_ref, left_ref, vec_ref, pay_ref, sem_ref
+        True, psi_power, slots_ref, right_ref, fetch, front_ref, back_ref, image_ref, left_ref, vec_ref, pay_ref, sem_ref
     )
 
     @pl.when((slot == pl.num_programs(0) - 1) & (step == pl.num_programs(1) - 1))

time: 118 us -> 121 us (1.025); the launches traced: 116 us -> 121 us
  Pallas kernels: 56.7 us -> 77.7 us
  starting transfers between devices: 39.9 us -> 26.3 us
  waiting for transfers between devices: 16.6 us -> 13.8 us
    ppermute x23, starting transfers between devices: 39.9 us -> 26.3 us  [swap(): return lax.ppermute(value, 'row', [(i, i ^ mask) for i in range(count)])]
    pallas_call x1, Pallas kernels: 18.2 us -> 28.2 us  [local(): pl.pallas_call(functools.partial(pair_zero_kernel, zero_at), grid_spec=pl...]
    pallas_call x1, Pallas kernels: 17.4 us -> 24.1 us  [local(): pl.pallas_call(functools.partial(pair_one_kernel, one_at), grid_spec=pltp...]
    pallas_call x1, Pallas kernels: 4.58 us -> 8.85 us  [local(): pl.pallas_call(again_kernel, grid_spec=pltpu.PrefetchScalarGridSpec(num_s...]
    ppermute x23, waiting for transfers between devices: 16.6 us -> 13.8 us  [swap(): return lax.ppermute(value, 'row', [(i, i ^ mask) for i in range(count)])]
  transfers between devices with their start and end apart: 23 -> 23, of which waited for: 7 -> 6; matrix products, arithmetic and copies ran while one was open for 0% -> 0% of each run, Pallas kernels for 29% -> 36%
where the time goes in v21:
time: 121 us
  Pallas kernels  77.7 us (64%)
  starting transfers between devices  26.3 us (22%)
  waiting for transfers between devices  13.8 us (11%)
    pallas_call x1, Pallas kernels, local(): pl.pallas_call(functools.partial(pair_zero_kernel, zero_at), grid_spec=pl...  28.2 us
    ppermute x23, starting transfers between devices, swap(): return lax.ppermute(value, 'row', [(i, i ^ mask) for i in range(count)])  26.3 us
    pallas_call x1, Pallas kernels, local(): pl.pallas_call(functools.partial(pair_one_kernel, one_at), grid_spec=pltp...  24.1 us
    ppermute x23, waiting for transfers between devices, swap(): return lax.ppermute(value, 'row', [(i, i ^ mask) for i in range(count)])  13.8 us
    pallas_call x2, Pallas kernels, own_part(): pl.pallas_call(functools.partial(own_kernel, rows), in_specs=[vmem, vmem,...  9.62 us
    pallas_call x1, Pallas kernels, local(): pl.pallas_call(again_kernel, grid_spec=pltpu.PrefetchScalarGridSpec(num_s...  8.85 us
    pallas_call x2, Pallas kernels, local(): pl.pallas_call(functools.partial(own_again_kernel, blocks), in_specs=[any...  4.34 us
  transfers between devices with their start and end apart: 23, of which 6 were waited for; matrix products, arithmetic and copies ran while one was open for 0% of the time, Pallas kernels for 36%

profile of v21, /device:TPU:0, one launch (start us, length us, event | category | flops | bytes accessed | tf_op | source)
XLA Modules:
  0.0 120.7 jit_solution(14383031636650420086)
XLA Ops:
  0.6 0.8 copy.12.list_ref
  1.4 1.2 payload.1
  2.6 5.1 %collective-permute-start.2 = (bf16[96,512]{1,0:T(8,128)(2,1)S(1)}, bf16[96,512]{1,0:T(8,128)(2,1)S(1)}, u32[]{:S(2)}, u32[]{:S(2)}) collective-permute-start(bf16[96,512]{1,0:T(8,128)(2,1)S(1)} %get-tuple-element.26), channel_id=1, source_target_pairs={{0,12},{1,13},{2,14},{3,15},{4,8},{5,9},{6,10},{7,11},{8,4},{9,5},... | collective-permute-start | bytes 294920 | tf_op jit(solution)/shard_map/ppermute | solution.py:399
  8.3 4.0 %own_tile_0.1 = (bf16[4,512,512]{2,1,0:T(8,128)(2,1)}, f32[8,2048]{1,0:T(8,128)S(1)}) custom-call(bf16[2048,128]{1,0:T(8,128)(2,1)S(1)} %get-tuple-element.23.left_ref, bf16[128,2048]{1,0:T(8,128)(2,1)S(1)} %get-tuple-element.22.right_ref.arrived_ref, bf16[8,2048]{1,0:T(8,128)(2,1)S(1)} %get-tuple-element.24.vec_ref, ...), custom_call_target="tpu_custom_call" | custom-call | flops 5000000000 | bytes 2097152 | tf_op jit(solution)/shard_map/own_tile_0/pallas_call | solution.py:489
  12.3 3.8 %collective-permute-start.8 = (bf16[80,512]{1,0:T(8,128)(2,1)S(1)}, bf16[80,512]{1,0:T(8,128)(2,1)S(1)}, u32[]{:S(2)}, u32[]{:S(2)}) collective-permute-start(bf16[80,512]{1,0:T(8,128)(2,1)S(1)} %gate.6), channel_id=1, source_target_pairs={{0,12},{1,13},{2,14},{3,15},{4,8},{5,9},{6,10},{7,11},{8,4},{9,5},... | collective-permute-start | bytes 245768 | tf_op jit(solution)/shard_map/ppermute | solution.py:399
  16.8 3.1 %collective-permute-done.1 = bf16[96,512]{1,0:T(8,128)(2,1)S(1)} collective-permute-done((bf16[96,512]{1,0:T(8,128)(2,1)S(1)}, bf16[96,512]{1,0:T(8,128)(2,1)S(1)}, u32[]{:S(2)}, u32[]{:S(2)}) %collective-permute-start.1) | collective-permute-done | bytes 98336 | tf_op jit(solution)/shard_map/ppermute | solution.py:399
  20.0 1.6 %collective-permute-start.3 = (bf16[384,512]{1,0:T(8,128)(2,1)S(1)}, bf16[384,512]{1,0:T(8,128)(2,1)S(1)}, u32[]{:S(2)}, u32[]{:S(2)}) collective-permute-start(bf16[384,512]{1,0:T(8,128)(2,1)S(1)} %gate.4.arrived_ref.refs_2_), channel_id=1, source_target_pairs={{0,2},{1,3},{2,0},{3,1},{4,6},{5,7},{6,4},{7,5},{8,10},{9,11},{10,... | collective-permute-start | bytes 1179656 | tf_op jit(solution)/shard_map/ppermute | solution.py:399
  21.6 5.6 %own_tile_1.1 = (bf16[6,512,512]{2,1,0:T(8,128)(2,1)}, f32[8,2048]{1,0:T(8,128)S(1)}) custom-call(bf16[2048,128]{1,0:T(8,128)(2,1)S(1)} %get-tuple-element.23.left_ref, bf16[128,2048]{1,0:T(8,128)(2,1)S(1)} %get-tuple-element.22.right_ref.arrived_ref, bf16[8,2048]{1,0:T(8,128)(2,1)S(1)} %get-tuple-element.24.vec_ref, ...), custom_call_target="tpu_custom_call" | custom-call | flops 5000000000 | bytes 3145728 | tf_op jit(solution)/shard_map/own_tile_1/pallas_call | solution.py:489
  27.2 4.3 %collective-permute-done.3.refs_0_ = bf16[384,512]{1,0:T(8,128)(2,1)S(1)} collective-permute-done((bf16[384,512]{1,0:T(8,128)(2,1)S(1)}, bf16[384,512]{1,0:T(8,128)(2,1)S(1)}, u32[]{:S(2)}, u32[]{:S(2)}) %collective-permute-start.3) | collective-permute-done | bytes 393248 | tf_op jit(solution)/shard_map/ppermute | solution.py:399
  31.6 1.7 %collective-permute-start.11 = (bf16[320,512]{1,0:T(8,128)(2,1)S(1)}, bf16[320,512]{1,0:T(8,128)(2,1)S(1)}, u32[]{:S(2)}, u32[]{:S(2)}) collective-permute-start(bf16[320,512]{1,0:T(8,128)(2,1)S(1)} %gate.7.refs_0_), channel_id=1, source_target_pairs={{0,3},{1,2},{2,1},{3,0},{4,7},{5,6},{6,5},{7,4},{8,11},{9,10},{10,... | collective-permute-start | bytes 983048 | tf_op jit(solution)/shard_map/ppermute | solution.py:399
  33.9 28.2 %pair_zero.1 = (bf16[3,1024,2048]{2,1,0:T(8,128)(2,1)S(1)}, bf16[2,1024,2048]{2,1,0:T(8,128)(2,1)}, f32[8,2048]{1,0:T(8,128)S(1)}, s32[7]{0:T(128)S(1)}) custom-call(s32[1]{0:T(128)} %bitcast.me_ref, bf16[128,2048]{1,0:T(8,128)(2,1)S(1)} %get-tuple-element.22.right_ref.arrived_ref, f32[8,2048]{1,0:T(8,128)S(1)} %get-tuple-element.25.refs_1_.refs_0_, ...), custom_call_target="tpu_custom_call" | custom-call | tf_op jit(solution)/shard_map/pair_zero/pallas_call | solution.py:548
  62.1 24.1 %pair_one.1 = (bf16[3,1024,2048]{2,1,0:T(8,128)(2,1)S(1)}, bf16[2,1024,2048]{2,1,0:T(8,128)(2,1)}, f32[8,2048]{1,0:T(8,128)S(1)}, bf16[8,2176]{1,0:T(8,128)(2,1)S(1)}) custom-call(s32[7]{0:T(128)S(1)} %get-tuple-element.28.slots_ref, bf16[128,2048]{1,0:T(8,128)(2,1)S(1)} %get-tuple-element.22.right_ref.arrived_ref, ...), custom_call_target="tpu_custom_call" | custom-call | tf_op jit(solution)/shard_map/pair_one/pallas_call | solution.py:568
  86.9 3.7 %collective-permute-start.12 = (bf16[1,8,2176]{2,1,0:T(8,128)(2,1)S(1)}, bf16[1,8,2176]{2,1,0:T(8,128)(2,1)S(1)}, u32[]{:S(2)}, u32[]{:S(2)}) collective-permute-start(bf16[1,8,2176]{2,1,0:T(8,128)(2,1)S(1)} %bitcast.7), channel_id=1, source_target_pairs={{0,4},{1,5},{2,6},{3,7},{4,0},{5,1},{6,2},{7,3},{8,12},{9,13},{10,... | collective-permute-start | bytes 104456 | tf_op jit(solution)/shard_map/ppermute | solution.py:399
  90.7 2.4 %own_again_1.1.refs_1_ = f32[8,2048]{1,0:T(8,128)S(1)} custom-call(bf16[6,512,512]{2,1,0:T(8,128)(2,1)} %get-tuple-element.38.in_ref, bf16[8,2176]{1,0:T(8,128)(2,1)S(1)} %get-tuple-element.35.vec_ref), custom_call_target="tpu_custom_call" | custom-call | flops 5000000000 | bytes 3145728 | tf_op jit(solution)/shard_map/own_again_1/pallas_call | solution.py:586
  93.1 1.3 %collective-permute-start.15 = (bf16[4,8,2176]{2,1,0:T(8,128)(2,1)S(1)}, bf16[4,8,2176]{2,1,0:T(8,128)(2,1)S(1)}, u32[]{:S(2)}, u32[]{:S(2)}) collective-permute-start(bf16[4,8,2176]{2,1,0:T(8,128)(2,1)S(1)} %pad_maximum_fusion.2), channel_id=1, source_target_pairs={{0,2},{1,3},{2,0},{3,1},{4,6},{5,7},{6,4},{7,5},{8,10},{9,11},{10,... | collective-permute-start | bytes 417800 | tf_op jit(solution)/shard_map/ppermute | solution.py:399
  94.5 4.1 %collective-permute-done.15 = bf16[4,8,2176]{2,1,0:T(8,128)(2,1)S(1)} collective-permute-done((bf16[4,8,2176]{2,1,0:T(8,128)(2,1)S(1)}, bf16[4,8,2176]{2,1,0:T(8,128)(2,1)S(1)}, u32[]{:S(2)}, u32[]{:S(2)}) %collective-permute-start.15) | collective-permute-done | bytes 139296 | tf_op jit(solution)/shard_map/ppermute | solution.py:399
  98.7 2.0 %own_again_0.1.refs_0_ = f32[8,2048]{1,0:T(8,128)S(1)} custom-call(bf16[4,512,512]{2,1,0:T(8,128)(2,1)} %get-tuple-element.37.in_ref, bf16[8,2176]{1,0:T(8,128)(2,1)S(1)} %get-tuple-element.35.vec_ref), custom_call_target="tpu_custom_call" | custom-call | flops 5000000000 | bytes 2097152 | tf_op jit(solution)/shard_map/own_again_0/pallas_call | solution.py:586
  100.8 8.8 %pair_again.1 = (f32[32,2048]{1,0:T(8,128)S(1)}, f32[8,128]{1,0:T(8,128)S(1)}, f32[8,128]{1,0:T(8,128)S(1)}) custom-call(s32[7]{0:T(128)S(1)} %get-tuple-element.28.slots_ref, bf16[3,1024,2048]{2,1,0:T(8,128)(2,1)S(1)} %get-tuple-element.29.front_zero_ref, bf16[3,1024,2048]{2,1,0:T(8,128)(2,1)S(1)} %get-tuple-element.32.front_one_ref, ...), custom_call_target="tpu_custom_call" | custom-call | tf_op jit(solution)/shard_map/pair_again/pallas_call | solution.py:604
  109.6 1.6 %collective-permute-start.19 = (f32[8,128]{1,0:T(8,128)S(1)}, f32[8,128]{1,0:T(8,128)S(1)}, u32[]{:S(2)}, u32[]{:S(2)}) collective-permute-start(f32[8,128]{1,0:T(8,128)S(1)} %get-tuple-element.41), channel_id=1, source_target_pairs={{0,12},{1,13},{2,14},{3,15},{4,8},{5,9},{6,10},{7,11},{8,4},{9,5},... | collective-permute-start | bytes 12296 | tf_op jit(solution)/shard_map/ppermute | solution.py:399
  111.2 2.9 %collective-permute-start.17 = (f32[8,128]{1,0:T(8,128)S(1)}, f32[8,128]{1,0:T(8,128)S(1)}, u32[]{:S(2)}, u32[]{:S(2)}) collective-permute-start(f32[8,128]{1,0:T(8,128)S(1)} %get-tuple-element.41), channel_id=1, source_target_pairs={{0,4},{1,5},{2,6},{3,7},{4,0},{5,1},{6,2},{7,3},{8,12},{9,13},{10,... | collective-permute-start | bytes 12296 | tf_op jit(solution)/shard_map/ppermute | solution.py:399
  114.1 1.0 collective-permute-done.19
  116.1 1.3 %collective-permute-start.21 = (f32[8,128]{1,0:T(8,128)S(1)}, f32[8,128]{1,0:T(8,128)S(1)}, u32[]{:S(2)}, u32[]{:S(2)}) collective-permute-start(f32[8,128]{1,0:T(8,128)S(1)} %add_add_fusion.1), channel_id=1, source_target_pairs={{0,2},{1,3},{2,0},{3,1},{4,6},{5,7},{6,4},{7,5},{8,10},{9,11},{10,... | collective-permute-start | bytes 12296 | tf_op jit(solution)/shard_map/ppermute | solution.py:399
  117.6 1.5 %curve_order.1 = f32[32,2048]{1,0:T(8,128)S(1)} custom-call(f32[32,2048]{1,0:T(8,128)S(1)} %get-tuple-element.40.rows_ref, s32[1,2048]{1,0:T(1,128)S(1)} %copy-done.2), custom_call_target="tpu_custom_call" | custom-call | tf_op jit(solution)/shard_map/curve_order/pallas_call | solution.py:642
  119.9 0.8 fusion.2
  (55 shorter events, 5.0 us)
Async XLA Ops:
  2.6 13.6 %collective-permute-start.2 = (bf16[96,512]{1,0:T(8,128)(2,1)S(1)}, bf16[96,512]{1,0:T(8,128)(2,1)S(1)}, u32[]{:S(2)}, u32[]{:S(2)}) collective-permute-start(bf16[96,512]{1,0:T(8,128)(2,1)S(1)} %get-tuple-element.26), channel_id=1, source_target_pairs={{0,12},{1,13},{2,14},{3,15},{4,8},{5,9},{6,10},{7,11},{8,4},{9,5},... | collective-permute-start | bytes 294920 | tf_op jit(solution)/shard_map/ppermute | solution.py:399
  7.7 12.2 %collective-permute-start.1 = (bf16[96,512]{1,0:T(8,128)(2,1)S(1)}, bf16[96,512]{1,0:T(8,128)(2,1)S(1)}, u32[]{:S(2)}, u32[]{:S(2)}) collective-permute-start(bf16[96,512]{1,0:T(8,128)(2,1)S(1)} %get-tuple-element.26), channel_id=1, source_target_pairs={{0,8},{1,9},{2,10},{3,11},{4,12},{5,13},{6,14},{7,15},{8,0},{9,1},... | collective-permute-start | bytes 294920 | tf_op jit(solution)/shard_map/ppermute | solution.py:399
  7.7 12.2 %collective-permute-start = (bf16[96,512]{1,0:T(8,128)(2,1)S(1)}, bf16[96,512]{1,0:T(8,128)(2,1)S(1)}, u32[]{:S(2)}, u32[]{:S(2)}) collective-permute-start(bf16[96,512]{1,0:T(8,128)(2,1)S(1)} %get-tuple-element.26), channel_id=1, source_target_pairs={{0,4},{1,5},{2,6},{3,7},{4,0},{5,1},{6,2},{7,3},{8,12},{9,13},{10,... | collective-permute-start | bytes 294920 | tf_op jit(solution)/shard_map/ppermute | solution.py:399
  12.3 19.2 %collective-permute-start.8 = (bf16[80,512]{1,0:T(8,128)(2,1)S(1)}, bf16[80,512]{1,0:T(8,128)(2,1)S(1)}, u32[]{:S(2)}, u32[]{:S(2)}) collective-permute-start(bf16[80,512]{1,0:T(8,128)(2,1)S(1)} %gate.6), channel_id=1, source_target_pairs={{0,12},{1,13},{2,14},{3,15},{4,8},{5,9},{6,10},{7,11},{8,4},{9,5},... | collective-permute-start | bytes 245768 | tf_op jit(solution)/shard_map/ppermute | solution.py:399
  16.1 15.4 %collective-permute-start.7 = (bf16[80,512]{1,0:T(8,128)(2,1)S(1)}, bf16[80,512]{1,0:T(8,128)(2,1)S(1)}, u32[]{:S(2)}, u32[]{:S(2)}) collective-permute-start(bf16[80,512]{1,0:T(8,128)(2,1)S(1)} %gate.6), channel_id=1, source_target_pairs={{0,8},{1,9},{2,10},{3,11},{4,12},{5,13},{6,14},{7,15},{8,0},{9,1},... | collective-permute-start | bytes 245768 | tf_op jit(solution)/shard_map/ppermute | solution.py:399
  16.2 15.4 %collective-permute-start.6 = (bf16[80,512]{1,0:T(8,128)(2,1)S(1)}, bf16[80,512]{1,0:T(8,128)(2,1)S(1)}, u32[]{:S(2)}, u32[]{:S(2)}) collective-permute-start(bf16[80,512]{1,0:T(8,128)(2,1)S(1)} %gate.6), channel_id=1, source_target_pairs={{0,4},{1,5},{2,6},{3,7},{4,0},{5,1},{6,2},{7,3},{8,12},{9,13},{10,... | collective-permute-start | bytes 245768 | tf_op jit(solution)/shard_map/ppermute | solution.py:399
  19.9 42.1 %copy-start = (f32[8,2048]{1,0:T(8,128)S(1)}, f32[8,2048]{1,0:T(8,128)}, u32[]{:S(2)}) copy-start(f32[8,2048]{1,0:T(8,128)} %rhs_ref.5) | copy-start | bytes 196612
  20.0 13.9 %collective-permute-start.4 = (bf16[384,512]{1,0:T(8,128)(2,1)S(1)}, bf16[384,512]{1,0:T(8,128)(2,1)S(1)}, u32[]{:S(2)}, u32[]{:S(2)}) collective-permute-start(bf16[384,512]{1,0:T(8,128)(2,1)S(1)} %gate.4.arrived_ref.refs_2_), channel_id=1, source_target_pairs={{0,1},{1,0},{2,3},{3,2},{4,5},{5,4},{6,7},{7,6},{8,9},{9,8},{10,11... | collective-permute-start | bytes 1179656 | tf_op jit(solution)/shard_map/ppermute | solution.py:399
  20.0 11.5 %collective-permute-start.3 = (bf16[384,512]{1,0:T(8,128)(2,1)S(1)}, bf16[384,512]{1,0:T(8,128)(2,1)S(1)}, u32[]{:S(2)}, u32[]{:S(2)}) collective-permute-start(bf16[384,512]{1,0:T(8,128)(2,1)S(1)} %gate.4.arrived_ref.refs_2_), channel_id=1, source_target_pairs={{0,2},{1,3},{2,0},{3,1},{4,6},{5,7},{6,4},{7,5},{8,10},{9,11},{10,... | collective-permute-start | bytes 1179656 | tf_op jit(solution)/shard_map/ppermute | solution.py:399
  31.6 2.3 %collective-permute-start.5 = (bf16[384,512]{1,0:T(8,128)(2,1)S(1)}, bf16[384,512]{1,0:T(8,128)(2,1)S(1)}, u32[]{:S(2)}, u32[]{:S(2)}) collective-permute-start(bf16[384,512]{1,0:T(8,128)(2,1)S(1)} %gate.5.refs_3_), channel_id=1, source_target_pairs={{0,1},{1,0},{2,3},{3,2},{4,5},{5,4},{6,7},{7,6},{8,9},{9,8},{10,11... | collective-permute-start | bytes 1179656 | tf_op jit(solution)/shard_map/ppermute | solution.py:399
  31.6 30.4 %collective-permute-start.11 = (bf16[320,512]{1,0:T(8,128)(2,1)S(1)}, bf16[320,512]{1,0:T(8,128)(2,1)S(1)}, u32[]{:S(2)}, u32[]{:S(2)}) collective-permute-start(bf16[320,512]{1,0:T(8,128)(2,1)S(1)} %gate.7.refs_0_), channel_id=1, source_target_pairs={{0,3},{1,2},{2,1},{3,0},{4,7},{5,6},{6,5},{7,4},{8,11},{9,10},{10,... | collective-permute-start | bytes 983048 | tf_op jit(solution)/shard_map/ppermute | solution.py:399
  33.3 28.7 %collective-permute-start.10 = (bf16[320,512]{1,0:T(8,128)(2,1)S(1)}, bf16[320,512]{1,0:T(8,128)(2,1)S(1)}, u32[]{:S(2)}, u32[]{:S(2)}) collective-permute-start(bf16[320,512]{1,0:T(8,128)(2,1)S(1)} %gate.7.refs_0_), channel_id=1, source_target_pairs={{0,1},{1,0},{2,3},{3,2},{4,5},{5,4},{6,7},{7,6},{8,9},{9,8},{10,11... | collective-permute-start | bytes 983048 | tf_op jit(solution)/shard_map/ppermute | solution.py:399
  33.3 28.7 %collective-permute-start.9 = (bf16[320,512]{1,0:T(8,128)(2,1)S(1)}, bf16[320,512]{1,0:T(8,128)(2,1)}, u32[]{:S(2)}, u32[]{:S(2)}) collective-permute-start(bf16[320,512]{1,0:T(8,128)(2,1)S(1)} %gate.7.refs_0_), channel_id=1, source_target_pairs={{0,2},{1,3},{2,0},{3,1},{4,6},{5,7},{6,4},{7,5},{8,10},{9,11},{10,... | collective-permute-start | bytes 983048 | tf_op jit(solution)/shard_map/ppermute | solution.py:399
  86.2 6.8 %collective-permute-start.14 = (bf16[1,8,2176]{2,1,0:T(8,128)(2,1)S(1)}, bf16[1,8,2176]{2,1,0:T(8,128)(2,1)S(1)}, u32[]{:S(2)}, u32[]{:S(2)}) collective-permute-start(bf16[1,8,2176]{2,1,0:T(8,128)(2,1)S(1)} %bitcast.5), channel_id=1, source_target_pairs={{0,12},{1,13},{2,14},{3,15},{4,8},{5,9},{6,10},{7,11},{8,4},{9,5},... | collective-permute-start | bytes 104456 | tf_op jit(solution)/shard_map/ppermute | solution.py:399
  86.9 6.1 %collective-permute-start.13 = (bf16[1,8,2176]{2,1,0:T(8,128)(2,1)S(1)}, bf16[1,8,2176]{2,1,0:T(8,128)(2,1)S(1)}, u32[]{:S(2)}, u32[]{:S(2)}) collective-permute-start(bf16[1,8,2176]{2,1,0:T(8,128)(2,1)S(1)} %bitcast.6), channel_id=1, source_target_pairs={{0,8},{1,9},{2,10},{3,11},{4,12},{5,13},{6,14},{7,15},{8,0},{9,1},... | collective-permute-start | bytes 104456 | tf_op jit(solution)/shard_map/ppermute | solution.py:399
  86.9 6.1 %collective-permute-start.12 = (bf16[1,8,2176]{2,1,0:T(8,128)(2,1)S(1)}, bf16[1,8,2176]{2,1,0:T(8,128)(2,1)S(1)}, u32[]{:S(2)}, u32[]{:S(2)}) collective-permute-start(bf16[1,8,2176]{2,1,0:T(8,128)(2,1)S(1)} %bitcast.7), channel_id=1, source_target_pairs={{0,4},{1,5},{2,6},{3,7},{4,0},{5,1},{6,2},{7,3},{8,12},{9,13},{10,... | collective-permute-start | bytes 104456 | tf_op jit(solution)/shard_map/ppermute | solution.py:399
  93.1 5.5 %collective-permute-start.15 = (bf16[4,8,2176]{2,1,0:T(8,128)(2,1)S(1)}, bf16[4,8,2176]{2,1,0:T(8,128)(2,1)S(1)}, u32[]{:S(2)}, u32[]{:S(2)}) collective-permute-start(bf16[4,8,2176]{2,1,0:T(8,128)(2,1)S(1)} %pad_maximum_fusion.2), channel_id=1, source_target_pairs={{0,2},{1,3},{2,0},{3,1},{4,6},{5,7},{6,4},{7,5},{8,10},{9,11},{10,... | collective-permute-start | bytes 417800 | tf_op jit(solution)/shard_map/ppermute | solution.py:399
  98.6 2.1 %collective-permute-start.16 = (bf16[8,8,2176]{2,1,0:T(8,128)(2,1)S(1)}, bf16[8,8,2176]{2,1,0:T(8,128)(2,1)S(1)}, u32[]{:S(2)}, u32[]{:S(2)}) collective-permute-start(bf16[8,8,2176]{2,1,0:T(8,128)(2,1)S(1)} %get-tuple-element.47), channel_id=1, source_target_pairs={{0,1},{1,0},{2,3},{3,2},{4,5},{5,4},{6,7},{7,6},{8,9},{9,8},{10,11... | collective-permute-start | bytes 835592 | tf_op jit(solution)/shard_map/ppermute | solution.py:399
  109.6 5.5 %collective-permute-start.19 = (f32[8,128]{1,0:T(8,128)S(1)}, f32[8,128]{1,0:T(8,128)S(1)}, u32[]{:S(2)}, u32[]{:S(2)}) collective-permute-start(f32[8,128]{1,0:T(8,128)S(1)} %get-tuple-element.41), channel_id=1, source_target_pairs={{0,12},{1,13},{2,14},{3,15},{4,8},{5,9},{6,10},{7,11},{8,4},{9,5},... | collective-permute-start | bytes 12296 | tf_op jit(solution)/shard_map/ppermute | solution.py:399
  111.2 4.5 %collective-permute-start.18 = (f32[8,128]{1,0:T(8,128)S(1)}, f32[8,128]{1,0:T(8,128)S(1)}, u32[]{:S(2)}, u32[]{:S(2)}) collective-permute-start(f32[8,128]{1,0:T(8,128)S(1)} %get-tuple-element.41), channel_id=1, source_target_pairs={{0,8},{1,9},{2,10},{3,11},{4,12},{5,13},{6,14},{7,15},{8,0},{9,1},... | collective-permute-start | bytes 12296 | tf_op jit(solution)/shard_map/ppermute | solution.py:399
  111.2 4.5 %collective-permute-start.17 = (f32[8,128]{1,0:T(8,128)S(1)}, f32[8,128]{1,0:T(8,128)S(1)}, u32[]{:S(2)}, u32[]{:S(2)}) collective-permute-start(f32[8,128]{1,0:T(8,128)S(1)} %get-tuple-element.41), channel_id=1, source_target_pairs={{0,4},{1,5},{2,6},{3,7},{4,0},{5,1},{6,2},{7,3},{8,12},{9,13},{10,... | collective-permute-start | bytes 12296 | tf_op jit(solution)/shard_map/ppermute | solution.py:399
  115.7 3.4 %collective-permute-start.22 = (f32[8,128]{1,0:T(8,128)S(1)}, f32[8,128]{1,0:T(8,128)S(1)}, u32[]{:S(2)}, u32[]{:S(2)}) collective-permute-start(f32[8,128]{1,0:T(8,128)S(1)} %add_add_fusion.1), channel_id=1, source_target_pairs={{0,3},{1,2},{2,1},{3,0},{4,7},{5,6},{6,5},{7,4},{8,11},{9,10},{10,... | collective-permute-start | bytes 12296 | tf_op jit(solution)/shard_map/ppermute | solution.py:399
  116.1 3.6 %collective-permute-start.21 = (f32[8,128]{1,0:T(8,128)S(1)}, f32[8,128]{1,0:T(8,128)S(1)}, u32[]{:S(2)}, u32[]{:S(2)}) collective-permute-start(f32[8,128]{1,0:T(8,128)S(1)} %add_add_fusion.1), channel_id=1, source_target_pairs={{0,2},{1,3},{2,0},{3,1},{4,6},{5,7},{6,4},{7,5},{8,10},{9,11},{10,... | collective-permute-start | bytes 12296 | tf_op jit(solution)/shard_map/ppermute | solution.py:399
  117.4 2.3 %collective-permute-start.20 = (f32[8,128]{1,0:T(8,128)S(1)}, f32[8,128]{1,0:T(8,128)S(1)}, u32[]{:S(2)}, u32[]{:S(2)}) collective-permute-start(f32[8,128]{1,0:T(8,128)S(1)} %add_add_fusion.1), channel_id=1, source_target_pairs={{0,1},{1,0},{2,3},{3,2},{4,5},{5,4},{6,7},{7,6},{8,9},{9,8},{10,11... | collective-permute-start | bytes 12296 | tf_op jit(solution)/shard_map/ppermute | solution.py:399
  (2 other events, 59.0 us)

commit v22 on v21

--- a/solution.py
+++ b/solution.py
@@ -61,11 +61,10 @@
     return (jnp.exp2(19.0 * lax.log2(u)) * (1.0 - u)).astype(BF16)
 
 
-def psi_natural(dist):
-    dist = jnp.maximum(dist, 1e-30)
-    radius = dist * lax.rsqrt(dist)
+def psi_root(dist):
+    radius = jnp.sqrt(jnp.maximum(dist, 0.0))
     u = jnp.maximum(SHRINK - radius, 1e-30)
-    return (jnp.exp(19.0 * jnp.log(u)) * (1.0 - u)).astype(BF16)
+    return (jnp.exp2(19.0 * lax.log2(u)) * (1.0 - u)).astype(BF16)
 
 
 def tile_unit(left, right, vec, tile_ref, aside=None, psi=psi_power):
@@ -271,7 +270,7 @@
 
     fetch = fetch_from(block_at, block_refs, slots_ref, pay_ref, sem_ref)
     half_tiles(
-        True, psi_natural, slots_ref, right_ref, fetch, front_ref, back_ref, sum_ref, left_ref, vec_ref, pay_ref, sem_ref
+        True, psi_root, slots_ref, right_ref, fetch, front_ref, back_ref, sum_ref, left_ref, vec_ref, pay_ref, sem_ref
     )
 
 

time: 121 us -> 122 us (level)
  Pallas kernels: 77.7 us -> 27.5 us
  starting transfers between devices: 26.3 us -> 63 us
  waiting for transfers between devices: 13.8 us -> 28.5 us
    ppermute x23, starting transfers between devices: 26.3 us -> 63 us  [swap(): return lax.ppermute(value, 'row', [(i, i ^ mask) for i in range(count)])]
    pallas_call x1, Pallas kernels: 28.2 us -> 5.12 us  [local(): pl.pallas_call(functools.partial(pair_zero_kernel, zero_at), grid_spec=pl...]
    pallas_call x1, Pallas kernels: 24.1 us -> 4.67 us  [local(): pl.pallas_call(functools.partial(pair_one_kernel, one_at), grid_spec=pltp...]
    ppermute x23, waiting for transfers between devices: 13.8 us -> 28.5 us  [swap(): return lax.ppermute(value, 'row', [(i, i ^ mask) for i in range(count)])]
    pallas_call x1, Pallas kernels: 8.85 us -> 1.17 us  [local(): pl.pallas_call(again_kernel, grid_spec=pltpu.PrefetchScalarGridSpec(num_s...]
  transfers between devices with their start and end apart: 23 -> 23, of which waited for: 6 -> 9; matrix products, arithmetic and copies ran while one was open for 0% -> 0% of each run, Pallas kernels for 36% -> 17%
where the time goes in v22:
time: 122 us
  starting transfers between devices  63 us (52%)
  waiting for transfers between devices  28.5 us (23%)
  Pallas kernels  27.5 us (23%)
    ppermute x23, starting transfers between devices, swap(): return lax.ppermute(value, 'row', [(i, i ^ mask) for i in range(count)])  63 us
    ppermute x23, waiting for transfers between devices, swap(): return lax.ppermute(value, 'row', [(i, i ^ mask) for i in range(count)])  28.5 us
    pallas_call x2, Pallas kernels, own_part(): pl.pallas_call(functools.partial(own_kernel, rows), in_specs=[vmem, vmem,...  9.62 us
    pallas_call x1, Pallas kernels, local(): pl.pallas_call(functools.partial(pair_zero_kernel, zero_at), grid_spec=pl...  5.12 us
    pallas_call x1, Pallas kernels, local(): pl.pallas_call(functools.partial(pair_one_kernel, one_at), grid_spec=pltp...  4.67 us
    pallas_call x2, Pallas kernels, local(): pl.pallas_call(functools.partial(own_again_kernel, blocks), in_specs=[any...  4.34 us
  transfers between devices with their start and end apart: 23, of which 9 were waited for; matrix products, arithmetic and copies ran while one was open for 0% of the time, Pallas kernels for 17%

profile of v22, /device:TPU:0, one launch (start us, length us, event | category | flops | bytes accessed | tf_op | source)
XLA Modules:
  0.0 121.8 jit_solution(10581999764337261715)
XLA Ops:
  2.6 5.1 %collective-permute-start.2 = (bf16[96,512]{1,0:T(8,128)(2,1)S(1)}, bf16[96,512]{1,0:T(8,128)(2,1)S(1)}, u32[]{:S(2)}, u32[]{:S(2)}) collective-permute-start(bf16[96,512]{1,0:T(8,128)(2,1)S(1)} %get-tuple-element.26), channel_id=1, source_target_pairs={{0,12},{1,13},{2,14},{3,15},{4,8},{5,9},{6,10},{7,11},{8,4},{9,5},... | collective-permute-start | bytes 294920 | tf_op jit(solution)/shard_map/ppermute | solution.py:398
  8.3 4.0 %own_tile_0.1 = (bf16[4,512,512]{2,1,0:T(8,128)(2,1)}, f32[8,2048]{1,0:T(8,128)S(1)}) custom-call(bf16[2048,128]{1,0:T(8,128)(2,1)S(1)} %get-tuple-element.23.left_ref, bf16[128,2048]{1,0:T(8,128)(2,1)S(1)} %get-tuple-element.22.right_ref.arrived_ref, bf16[8,2048]{1,0:T(8,128)(2,1)S(1)} %get-tuple-element.24.vec_ref, ...), custom_call_target="tpu_custom_call" | custom-call | flops 5000000000 | bytes 2097152 | tf_op jit(solution)/shard_map/own_tile_0/pallas_call | solution.py:488
  12.3 3.8 %collective-permute-start.8 = (bf16[80,512]{1,0:T(8,128)(2,1)S(1)}, bf16[80,512]{1,0:T(8,128)(2,1)S(1)}, u32[]{:S(2)}, u32[]{:S(2)}) collective-permute-start(bf16[80,512]{1,0:T(8,128)(2,1)S(1)} %gate.6), channel_id=1, source_target_pairs={{0,12},{1,13},{2,14},{3,15},{4,8},{5,9},{6,10},{7,11},{8,4},{9,5},... | collective-permute-start | bytes 245768 | tf_op jit(solution)/shard_map/ppermute | solution.py:398
  16.8 3.1 %collective-permute-done.1 = bf16[96,512]{1,0:T(8,128)(2,1)S(1)} collective-permute-done((bf16[96,512]{1,0:T(8,128)(2,1)S(1)}, bf16[96,512]{1,0:T(8,128)(2,1)S(1)}, u32[]{:S(2)}, u32[]{:S(2)}) %collective-permute-start.1) | collective-permute-done | bytes 98336 | tf_op jit(solution)/shard_map/ppermute | solution.py:398
  20.0 1.6 %collective-permute-start.3 = (bf16[384,512]{1,0:T(8,128)(2,1)S(1)}, bf16[384,512]{1,0:T(8,128)(2,1)S(1)}, u32[]{:S(2)}, u32[]{:S(2)}) collective-permute-start(bf16[384,512]{1,0:T(8,128)(2,1)S(1)} %gate.4.arrived_ref.refs_2_), channel_id=1, source_target_pairs={{0,2},{1,3},{2,0},{3,1},{4,6},{5,7},{6,4},{7,5},{8,10},{9,11},{10,... | collective-permute-start | bytes 1179656 | tf_op jit(solution)/shard_map/ppermute | solution.py:398
  21.6 5.6 %own_tile_1.1 = (bf16[6,512,512]{2,1,0:T(8,128)(2,1)}, f32[8,2048]{1,0:T(8,128)S(1)}) custom-call(bf16[2048,128]{1,0:T(8,128)(2,1)S(1)} %get-tuple-element.23.left_ref, bf16[128,2048]{1,0:T(8,128)(2,1)S(1)} %get-tuple-element.22.right_ref.arrived_ref, bf16[8,2048]{1,0:T(8,128)(2,1)S(1)} %get-tuple-element.24.vec_ref, ...), custom_call_target="tpu_custom_call" | custom-call | flops 5000000000 | bytes 3145728 | tf_op jit(solution)/shard_map/own_tile_1/pallas_call | solution.py:488
  27.2 4.3 %collective-permute-done.3.refs_0_ = bf16[384,512]{1,0:T(8,128)(2,1)S(1)} collective-permute-done((bf16[384,512]{1,0:T(8,128)(2,1)S(1)}, bf16[384,512]{1,0:T(8,128)(2,1)S(1)}, u32[]{:S(2)}, u32[]{:S(2)}) %collective-permute-start.3) | collective-permute-done | bytes 393248 | tf_op jit(solution)/shard_map/ppermute | solution.py:398
  31.6 1.7 %collective-permute-start.11 = (bf16[320,512]{1,0:T(8,128)(2,1)S(1)}, bf16[320,512]{1,0:T(8,128)(2,1)S(1)}, u32[]{:S(2)}, u32[]{:S(2)}) collective-permute-start(bf16[320,512]{1,0:T(8,128)(2,1)S(1)} %gate.7.refs_0_), channel_id=1, source_target_pairs={{0,3},{1,2},{2,1},{3,0},{4,7},{5,6},{6,5},{7,4},{8,11},{9,10},{10,... | collective-permute-start | bytes 983048 | tf_op jit(solution)/shard_map/ppermute | solution.py:398
  33.9 5.1 %pair_zero.1 = (bf16[3,1024,2048]{2,1,0:T(8,128)(2,1)S(1)}, bf16[2,1024,2048]{2,1,0:T(8,128)(2,1)}, f32[8,2048]{1,0:T(8,128)S(1)}, s32[7]{0:T(128)S(1)}) custom-call(s32[1]{0:T(128)} %bitcast.me_ref, bf16[128,2048]{1,0:T(8,128)(2,1)S(1)} %get-tuple-element.22.right_ref.arrived_ref, f32[8,2048]{1,0:T(8,128)S(1)} %get-tuple-element.25.refs_1_.refs_0_, ...), custom_call_target="tpu_custom_call" | custom-call | tf_op jit(solution)/shard_map/pair_zero/pallas_call | solution.py:547
  39.0 2.4 %collective-permute-done.11.refs_3_ = bf16[320,512]{1,0:T(8,128)(2,1)S(1)} collective-permute-done((bf16[320,512]{1,0:T(8,128)(2,1)S(1)}, bf16[320,512]{1,0:T(8,128)(2,1)S(1)}, u32[]{:S(2)}, u32[]{:S(2)}) %collective-permute-start.11) | collective-permute-done | bytes 327712 | tf_op jit(solution)/shard_map/ppermute | solution.py:398
  41.4 7.5 %collective-permute-done.9.refs_1_ = bf16[320,512]{1,0:T(8,128)(2,1)} collective-permute-done((bf16[320,512]{1,0:T(8,128)(2,1)S(1)}, bf16[320,512]{1,0:T(8,128)(2,1)}, u32[]{:S(2)}, u32[]{:S(2)}) %collective-permute-start.9) | collective-permute-done | bytes 327712 | tf_op jit(solution)/shard_map/ppermute | solution.py:398
  48.9 4.7 %pair_one.1 = (bf16[3,1024,2048]{2,1,0:T(8,128)(2,1)S(1)}, bf16[2,1024,2048]{2,1,0:T(8,128)(2,1)}, f32[8,2048]{1,0:T(8,128)S(1)}, bf16[8,2176]{1,0:T(8,128)(2,1)S(1)}) custom-call(s32[7]{0:T(128)S(1)} %get-tuple-element.28.slots_ref, bf16[128,2048]{1,0:T(8,128)(2,1)S(1)} %get-tuple-element.22.right_ref.arrived_ref, ...), custom_call_target="tpu_custom_call" | custom-call | tf_op jit(solution)/shard_map/pair_one/pallas_call | solution.py:567
  54.2 34.2 %collective-permute-start.13 = (bf16[1,8,2176]{2,1,0:T(8,128)(2,1)S(1)}, bf16[1,8,2176]{2,1,0:T(8,128)(2,1)S(1)}, u32[]{:S(2)}, u32[]{:S(2)}) collective-permute-start(bf16[1,8,2176]{2,1,0:T(8,128)(2,1)S(1)} %bitcast.6), channel_id=1, source_target_pairs={{0,8},{1,9},{2,10},{3,11},{4,12},{5,13},{6,14},{7,15},{8,0},{9,1},... | collective-permute-start | bytes 104456 | tf_op jit(solution)/shard_map/ppermute | solution.py:398
  88.9 2.4 %own_again_1.1.refs_1_ = f32[8,2048]{1,0:T(8,128)S(1)} custom-call(bf16[6,512,512]{2,1,0:T(8,128)(2,1)} %get-tuple-element.38.in_ref, bf16[8,2176]{1,0:T(8,128)(2,1)S(1)} %get-tuple-element.35.vec_ref), custom_call_target="tpu_custom_call" | custom-call | flops 5000000000 | bytes 3145728 | tf_op jit(solution)/shard_map/own_again_1/pallas_call | solution.py:585
  91.3 1.4 %collective-permute-done.12 = bf16[1,8,2176]{2,1,0:T(8,128)(2,1)S(1)} collective-permute-done((bf16[1,8,2176]{2,1,0:T(8,128)(2,1)S(1)}, bf16[1,8,2176]{2,1,0:T(8,128)(2,1)S(1)}, u32[]{:S(2)}, u32[]{:S(2)}) %collective-permute-start.12) | collective-permute-done | bytes 34848 | tf_op jit(solution)/shard_map/ppermute | solution.py:398
  92.7 1.2 collective-permute-start.15
  94.0 4.7 %collective-permute-done.15 = bf16[4,8,2176]{2,1,0:T(8,128)(2,1)S(1)} collective-permute-done((bf16[4,8,2176]{2,1,0:T(8,128)(2,1)S(1)}, bf16[4,8,2176]{2,1,0:T(8,128)(2,1)S(1)}, u32[]{:S(2)}, u32[]{:S(2)}) %collective-permute-start.15) | collective-permute-done | bytes 139296 | tf_op jit(solution)/shard_map/ppermute | solution.py:398
  99.3 2.0 %own_again_0.1.refs_0_ = f32[8,2048]{1,0:T(8,128)S(1)} custom-call(bf16[4,512,512]{2,1,0:T(8,128)(2,1)} %get-tuple-element.37.in_ref, bf16[8,2176]{1,0:T(8,128)(2,1)S(1)} %get-tuple-element.35.vec_ref), custom_call_target="tpu_custom_call" | custom-call | flops 5000000000 | bytes 2097152 | tf_op jit(solution)/shard_map/own_again_0/pallas_call | solution.py:585
  102.5 2.3 %collective-permute-start.19 = (f32[8,128]{1,0:T(8,128)S(1)}, f32[8,128]{1,0:T(8,128)S(1)}, u32[]{:S(2)}, u32[]{:S(2)}) collective-permute-start(f32[8,128]{1,0:T(8,128)S(1)} %get-tuple-element.41), channel_id=1, source_target_pairs={{0,12},{1,13},{2,14},{3,15},{4,8},{5,9},{6,10},{7,11},{8,4},{9,5},... | collective-permute-start | bytes 12296 | tf_op jit(solution)/shard_map/ppermute | solution.py:398
  104.8 7.1 %collective-permute-start.18 = (f32[8,128]{1,0:T(8,128)S(1)}, f32[8,128]{1,0:T(8,128)S(1)}, u32[]{:S(2)}, u32[]{:S(2)}) collective-permute-start(f32[8,128]{1,0:T(8,128)S(1)} %get-tuple-element.41), channel_id=1, source_target_pairs={{0,8},{1,9},{2,10},{3,11},{4,12},{5,13},{6,14},{7,15},{8,0},{9,1},... | collective-permute-start | bytes 12296 | tf_op jit(solution)/shard_map/ppermute | solution.py:398
  113.4 2.0 %collective-permute-done.17 = f32[8,128]{1,0:T(8,128)S(1)} collective-permute-done((f32[8,128]{1,0:T(8,128)S(1)}, f32[8,128]{1,0:T(8,128)S(1)}, u32[]{:S(2)}, u32[]{:S(2)}) %collective-permute-start.17) | collective-permute-done | bytes 4128 | tf_op jit(solution)/shard_map/ppermute | solution.py:398
  115.5 1.7 %collective-permute-start.22 = (f32[8,128]{1,0:T(8,128)S(1)}, f32[8,128]{1,0:T(8,128)S(1)}, u32[]{:S(2)}, u32[]{:S(2)}) collective-permute-start(f32[8,128]{1,0:T(8,128)S(1)} %add_add_fusion.1), channel_id=1, source_target_pairs={{0,3},{1,2},{2,1},{3,0},{4,7},{5,6},{6,5},{7,4},{8,11},{9,10},{10,... | collective-permute-start | bytes 12296 | tf_op jit(solution)/shard_map/ppermute | solution.py:398
  117.4 1.5 %curve_order.1 = f32[32,2048]{1,0:T(8,128)S(1)} custom-call(f32[32,2048]{1,0:T(8,128)S(1)} %get-tuple-element.40.rows_ref, s32[1,2048]{1,0:T(1,128)S(1)} %copy-done.2), custom_call_target="tpu_custom_call" | custom-call | tf_op jit(solution)/shard_map/curve_order/pallas_call | solution.py:641
  118.9 1.9 %collective-permute-done.21 = f32[8,128]{1,0:T(8,128)S(1)} collective-permute-done((f32[8,128]{1,0:T(8,128)S(1)}, f32[8,128]{1,0:T(8,128)S(1)}, u32[]{:S(2)}, u32[]{:S(2)}) %collective-permute-start.21) | collective-permute-done | bytes 4128 | tf_op jit(solution)/shard_map/ppermute | solution.py:398
  (55 shorter events, 9.8 us)
Async XLA Ops:
  2.6 13.6 %collective-permute-start.2 = (bf16[96,512]{1,0:T(8,128)(2,1)S(1)}, bf16[96,512]{1,0:T(8,128)(2,1)S(1)}, u32[]{:S(2)}, u32[]{:S(2)}) collective-permute-start(bf16[96,512]{1,0:T(8,128)(2,1)S(1)} %get-tuple-element.26), channel_id=1, source_target_pairs={{0,12},{1,13},{2,14},{3,15},{4,8},{5,9},{6,10},{7,11},{8,4},{9,5},... | collective-permute-start | bytes 294920 | tf_op jit(solution)/shard_map/ppermute | solution.py:398
  7.7 12.2 %collective-permute-start.1 = (bf16[96,512]{1,0:T(8,128)(2,1)S(1)}, bf16[96,512]{1,0:T(8,128)(2,1)S(1)}, u32[]{:S(2)}, u32[]{:S(2)}) collective-permute-start(bf16[96,512]{1,0:T(8,128)(2,1)S(1)} %get-tuple-element.26), channel_id=1, source_target_pairs={{0,8},{1,9},{2,10},{3,11},{4,12},{5,13},{6,14},{7,15},{8,0},{9,1},... | collective-permute-start | bytes 294920 | tf_op jit(solution)/shard_map/ppermute | solution.py:398
  7.7 12.2 %collective-permute-start = (bf16[96,512]{1,0:T(8,128)(2,1)S(1)}, bf16[96,512]{1,0:T(8,128)(2,1)S(1)}, u32[]{:S(2)}, u32[]{:S(2)}) collective-permute-start(bf16[96,512]{1,0:T(8,128)(2,1)S(1)} %get-tuple-element.26), channel_id=1, source_target_pairs={{0,4},{1,5},{2,6},{3,7},{4,0},{5,1},{6,2},{7,3},{8,12},{9,13},{10,... | collective-permute-start | bytes 294920 | tf_op jit(solution)/shard_map/ppermute | solution.py:398
  12.3 19.2 %collective-permute-start.8 = (bf16[80,512]{1,0:T(8,128)(2,1)S(1)}, bf16[80,512]{1,0:T(8,128)(2,1)S(1)}, u32[]{:S(2)}, u32[]{:S(2)}) collective-permute-start(bf16[80,512]{1,0:T(8,128)(2,1)S(1)} %gate.6), channel_id=1, source_target_pairs={{0,12},{1,13},{2,14},{3,15},{4,8},{5,9},{6,10},{7,11},{8,4},{9,5},... | collective-permute-start | bytes 245768 | tf_op jit(solution)/shard_map/ppermute | solution.py:398
  16.1 15.4 %collective-permute-start.7 = (bf16[80,512]{1,0:T(8,128)(2,1)S(1)}, bf16[80,512]{1,0:T(8,128)(2,1)S(1)}, u32[]{:S(2)}, u32[]{:S(2)}) collective-permute-start(bf16[80,512]{1,0:T(8,128)(2,1)S(1)} %gate.6), channel_id=1, source_target_pairs={{0,8},{1,9},{2,10},{3,11},{4,12},{5,13},{6,14},{7,15},{8,0},{9,1},... | collective-permute-start | bytes 245768 | tf_op jit(solution)/shard_map/ppermute | solution.py:398
  16.2 15.4 %collective-permute-start.6 = (bf16[80,512]{1,0:T(8,128)(2,1)S(1)}, bf16[80,512]{1,0:T(8,128)(2,1)S(1)}, u32[]{:S(2)}, u32[]{:S(2)}) collective-permute-start(bf16[80,512]{1,0:T(8,128)(2,1)S(1)} %gate.6), channel_id=1, source_target_pairs={{0,4},{1,5},{2,6},{3,7},{4,0},{5,1},{6,2},{7,3},{8,12},{9,13},{10,... | collective-permute-start | bytes 245768 | tf_op jit(solution)/shard_map/ppermute | solution.py:398
  19.9 28.9 %copy-start = (f32[8,2048]{1,0:T(8,128)S(1)}, f32[8,2048]{1,0:T(8,128)}, u32[]{:S(2)}) copy-start(f32[8,2048]{1,0:T(8,128)} %rhs_ref.5) | copy-start | bytes 196612
  20.0 13.9 %collective-permute-start.4 = (bf16[384,512]{1,0:T(8,128)(2,1)S(1)}, bf16[384,512]{1,0:T(8,128)(2,1)S(1)}, u32[]{:S(2)}, u32[]{:S(2)}) collective-permute-start(bf16[384,512]{1,0:T(8,128)(2,1)S(1)} %gate.4.arrived_ref.refs_2_), channel_id=1, source_target_pairs={{0,1},{1,0},{2,3},{3,2},{4,5},{5,4},{6,7},{7,6},{8,9},{9,8},{10,11... | collective-permute-start | bytes 1179656 | tf_op jit(solution)/shard_map/ppermute | solution.py:398
  20.0 11.5 %collective-permute-start.3 = (bf16[384,512]{1,0:T(8,128)(2,1)S(1)}, bf16[384,512]{1,0:T(8,128)(2,1)S(1)}, u32[]{:S(2)}, u32[]{:S(2)}) collective-permute-start(bf16[384,512]{1,0:T(8,128)(2,1)S(1)} %gate.4.arrived_ref.refs_2_), channel_id=1, source_target_pairs={{0,2},{1,3},{2,0},{3,1},{4,6},{5,7},{6,4},{7,5},{8,10},{9,11},{10,... | collective-permute-start | bytes 1179656 | tf_op jit(solution)/shard_map/ppermute | solution.py:398
  31.6 2.3 %collective-permute-start.5 = (bf16[384,512]{1,0:T(8,128)(2,1)S(1)}, bf16[384,512]{1,0:T(8,128)(2,1)S(1)}, u32[]{:S(2)}, u32[]{:S(2)}) collective-permute-start(bf16[384,512]{1,0:T(8,128)(2,1)S(1)} %gate.5.refs_3_), channel_id=1, source_target_pairs={{0,1},{1,0},{2,3},{3,2},{4,5},{5,4},{6,7},{7,6},{8,9},{9,8},{10,11... | collective-permute-start | bytes 1179656 | tf_op jit(solution)/shard_map/ppermute | solution.py:398
  31.6 9.7 %collective-permute-start.11 = (bf16[320,512]{1,0:T(8,128)(2,1)S(1)}, bf16[320,512]{1,0:T(8,128)(2,1)S(1)}, u32[]{:S(2)}, u32[]{:S(2)}) collective-permute-start(bf16[320,512]{1,0:T(8,128)(2,1)S(1)} %gate.7.refs_0_), channel_id=1, source_target_pairs={{0,3},{1,2},{2,1},{3,0},{4,7},{5,6},{6,5},{7,4},{8,11},{9,10},{10,... | collective-permute-start | bytes 983048 | tf_op jit(solution)/shard_map/ppermute | solution.py:398
  33.3 8.1 %collective-permute-start.10 = (bf16[320,512]{1,0:T(8,128)(2,1)S(1)}, bf16[320,512]{1,0:T(8,128)(2,1)S(1)}, u32[]{:S(2)}, u32[]{:S(2)}) collective-permute-start(bf16[320,512]{1,0:T(8,128)(2,1)S(1)} %gate.7.refs_0_), channel_id=1, source_target_pairs={{0,1},{1,0},{2,3},{3,2},{4,5},{5,4},{6,7},{7,6},{8,9},{9,8},{10,11... | collective-permute-start | bytes 983048 | tf_op jit(solution)/shard_map/ppermute | solution.py:398
  33.3 15.5 %collective-permute-start.9 = (bf16[320,512]{1,0:T(8,128)(2,1)S(1)}, bf16[320,512]{1,0:T(8,128)(2,1)}, u32[]{:S(2)}, u32[]{:S(2)}) collective-permute-start(bf16[320,512]{1,0:T(8,128)(2,1)S(1)} %gate.7.refs_0_), channel_id=1, source_target_pairs={{0,2},{1,3},{2,0},{3,1},{4,6},{5,7},{6,4},{7,5},{8,10},{9,11},{10,... | collective-permute-start | bytes 983048 | tf_op jit(solution)/shard_map/ppermute | solution.py:398
  53.5 37.7 %collective-permute-start.14 = (bf16[1,8,2176]{2,1,0:T(8,128)(2,1)S(1)}, bf16[1,8,2176]{2,1,0:T(8,128)(2,1)S(1)}, u32[]{:S(2)}, u32[]{:S(2)}) collective-permute-start(bf16[1,8,2176]{2,1,0:T(8,128)(2,1)S(1)} %bitcast.5), channel_id=1, source_target_pairs={{0,12},{1,13},{2,14},{3,15},{4,8},{5,9},{6,10},{7,11},{8,4},{9,5},... | collective-permute-start | bytes 104456 | tf_op jit(solution)/shard_map/ppermute | solution.py:398
  54.2 37.0 %collective-permute-start.13 = (bf16[1,8,2176]{2,1,0:T(8,128)(2,1)S(1)}, bf16[1,8,2176]{2,1,0:T(8,128)(2,1)S(1)}, u32[]{:S(2)}, u32[]{:S(2)}) collective-permute-start(bf16[1,8,2176]{2,1,0:T(8,128)(2,1)S(1)} %bitcast.6), channel_id=1, source_target_pairs={{0,8},{1,9},{2,10},{3,11},{4,12},{5,13},{6,14},{7,15},{8,0},{9,1},... | collective-permute-start | bytes 104456 | tf_op jit(solution)/shard_map/ppermute | solution.py:398
  88.4 4.3 %collective-permute-start.12 = (bf16[1,8,2176]{2,1,0:T(8,128)(2,1)S(1)}, bf16[1,8,2176]{2,1,0:T(8,128)(2,1)S(1)}, u32[]{:S(2)}, u32[]{:S(2)}) collective-permute-start(bf16[1,8,2176]{2,1,0:T(8,128)(2,1)S(1)} %bitcast.7), channel_id=1, source_target_pairs={{0,4},{1,5},{2,6},{3,7},{4,0},{5,1},{6,2},{7,3},{8,12},{9,13},{10,... | collective-permute-start | bytes 104456 | tf_op jit(solution)/shard_map/ppermute | solution.py:398
  92.7 5.9 %collective-permute-start.15 = (bf16[4,8,2176]{2,1,0:T(8,128)(2,1)S(1)}, bf16[4,8,2176]{2,1,0:T(8,128)(2,1)S(1)}, u32[]{:S(2)}, u32[]{:S(2)}) collective-permute-start(bf16[4,8,2176]{2,1,0:T(8,128)(2,1)S(1)} %pad_maximum_fusion.2), channel_id=1, source_target_pairs={{0,2},{1,3},{2,0},{3,1},{4,6},{5,7},{6,4},{7,5},{8,10},{9,11},{10,... | collective-permute-start | bytes 417800 | tf_op jit(solution)/shard_map/ppermute | solution.py:398
  98.7 2.6 %collective-permute-start.16 = (bf16[8,8,2176]{2,1,0:T(8,128)(2,1)S(1)}, bf16[8,8,2176]{2,1,0:T(8,128)(2,1)S(1)}, u32[]{:S(2)}, u32[]{:S(2)}) collective-permute-start(bf16[8,8,2176]{2,1,0:T(8,128)(2,1)S(1)} %get-tuple-element.47), channel_id=1, source_target_pairs={{0,1},{1,0},{2,3},{3,2},{4,5},{5,4},{6,7},{7,6},{8,9},{9,8},{10,11... | collective-permute-start | bytes 835592 | tf_op jit(solution)/shard_map/ppermute | solution.py:398
  102.5 9.9 %collective-permute-start.19 = (f32[8,128]{1,0:T(8,128)S(1)}, f32[8,128]{1,0:T(8,128)S(1)}, u32[]{:S(2)}, u32[]{:S(2)}) collective-permute-start(f32[8,128]{1,0:T(8,128)S(1)} %get-tuple-element.41), channel_id=1, source_target_pairs={{0,12},{1,13},{2,14},{3,15},{4,8},{5,9},{6,10},{7,11},{8,4},{9,5},... | collective-permute-start | bytes 12296 | tf_op jit(solution)/shard_map/ppermute | solution.py:398
  104.8 8.7 %collective-permute-start.18 = (f32[8,128]{1,0:T(8,128)S(1)}, f32[8,128]{1,0:T(8,128)S(1)}, u32[]{:S(2)}, u32[]{:S(2)}) collective-permute-start(f32[8,128]{1,0:T(8,128)S(1)} %get-tuple-element.41), channel_id=1, source_target_pairs={{0,8},{1,9},{2,10},{3,11},{4,12},{5,13},{6,14},{7,15},{8,0},{9,1},... | collective-permute-start | bytes 12296 | tf_op jit(solution)/shard_map/ppermute | solution.py:398
  111.8 3.6 %collective-permute-start.17 = (f32[8,128]{1,0:T(8,128)S(1)}, f32[8,128]{1,0:T(8,128)S(1)}, u32[]{:S(2)}, u32[]{:S(2)}) collective-permute-start(f32[8,128]{1,0:T(8,128)S(1)} %get-tuple-element.41), channel_id=1, source_target_pairs={{0,4},{1,5},{2,6},{3,7},{4,0},{5,1},{6,2},{7,3},{8,12},{9,13},{10,... | collective-permute-start | bytes 12296 | tf_op jit(solution)/shard_map/ppermute | solution.py:398
  115.5 3.4 %collective-permute-start.22 = (f32[8,128]{1,0:T(8,128)S(1)}, f32[8,128]{1,0:T(8,128)S(1)}, u32[]{:S(2)}, u32[]{:S(2)}) collective-permute-start(f32[8,128]{1,0:T(8,128)S(1)} %add_add_fusion.1), channel_id=1, source_target_pairs={{0,3},{1,2},{2,1},{3,0},{4,7},{5,6},{6,5},{7,4},{8,11},{9,10},{10,... | collective-permute-start | bytes 12296 | tf_op jit(solution)/shard_map/ppermute | solution.py:398
  117.2 3.6 %collective-permute-start.21 = (f32[8,128]{1,0:T(8,128)S(1)}, f32[8,128]{1,0:T(8,128)S(1)}, u32[]{:S(2)}, u32[]{:S(2)}) collective-permute-start(f32[8,128]{1,0:T(8,128)S(1)} %add_add_fusion.1), channel_id=1, source_target_pairs={{0,2},{1,3},{2,0},{3,1},{4,6},{5,7},{6,4},{7,5},{8,10},{9,11},{10,... | collective-permute-start | bytes 12296 | tf_op jit(solution)/shard_map/ppermute | solution.py:398
  117.2 3.6 %collective-permute-start.20 = (f32[8,128]{1,0:T(8,128)S(1)}, f32[8,128]{1,0:T(8,128)S(1)}, u32[]{:S(2)}, u32[]{:S(2)}) collective-permute-start(f32[8,128]{1,0:T(8,128)S(1)} %add_add_fusion.1), channel_id=1, source_target_pairs={{0,1},{1,0},{2,3},{3,2},{4,5},{5,4},{6,7},{7,6},{8,9},{9,8},{10,11... | collective-permute-start | bytes 12296 | tf_op jit(solution)/shard_map/ppermute | solution.py:398
  (2 other events, 45.0 us)

commit v23 on v19

--- a/solution.py
+++ b/solution.py
@@ -279,7 +279,7 @@
 
     fetch = fetch_from(block_at, block_refs, slots_ref, pay_ref, sem_ref)
     half_tiles(
-        False, slots_ref, right_ref, fetch, front_ref, back_ref, image_ref, left_ref, vec_ref, pay_ref, sem_ref
+        True, slots_ref, right_ref, fetch, front_ref, back_ref, image_ref, left_ref, vec_ref, pay_ref, sem_ref
     )
 
     @pl.when((slot == pl.num_programs(0) - 1) & (step == pl.num_programs(1) - 1))
@@ -501,10 +501,10 @@
         [pay] + [swap(pay, mask, count) for mask in first_masks], axis=0
     )
     near_zero = first_level(pay_zero)
-    own_parts = [own_part(range(1), right)]
+    own_parts = [own_part(range(steps - 1, steps), right)]
     near_zero = gate(near_zero, own_parts[0][2])
     near_one = first_level(gate(pay_one, own_parts[0][2]))
-    own_parts.append(own_part(range(1, steps), near_zero))
+    own_parts.append(own_part(range(steps - 1), near_zero))
     near_one = gate(near_one, own_parts[1][2])
     zero, places = [near_zero], [0]
     for level, masks in enumerate(later):

time: 118 us -> 119 us (level); the launches traced: 116 us -> 119 us
  Pallas kernels: 56.7 us -> 75.4 us
  starting transfers between devices: 39.9 us -> 31.1 us
  waiting for transfers between devices: 16.6 us -> 9.74 us
    ppermute x23, starting transfers between devices: 39.9 us -> 31.1 us  [swap(): return lax.ppermute(value, 'row', [(i, i ^ mask) for i in range(count)])]
    pallas_call x1, Pallas kernels: 17.4 us -> 24.9 us  [local(): pl.pallas_call(functools.partial(pair_one_kernel, one_at), grid_spec=pltp...]
    pallas_call x1, Pallas kernels: 18.2 us -> 25.1 us  [local(): pl.pallas_call(functools.partial(pair_zero_kernel, zero_at), grid_spec=pl...]
    ppermute x23, waiting for transfers between devices: 16.6 us -> 9.74 us  [swap(): return lax.ppermute(value, 'row', [(i, i ^ mask) for i in range(count)])]
    pallas_call x1, Pallas kernels: 4.58 us -> 8.85 us  [local(): pl.pallas_call(again_kernel, grid_spec=pltpu.PrefetchScalarGridSpec(num_s...]
  transfers between devices with their start and end apart: 23 -> 23, of which waited for: 7 -> 7; matrix products, arithmetic and copies ran while one was open for 0% -> 0% of each run, Pallas kernels for 29% -> 34%
where the time goes in v23:
time: 119 us
  Pallas kernels  75.4 us (63%)
  starting transfers between devices  31.1 us (26%)
  waiting for transfers between devices  9.74 us (8%)
    ppermute x23, starting transfers between devices, swap(): return lax.ppermute(value, 'row', [(i, i ^ mask) for i in range(count)])  31.1 us
    pallas_call x1, Pallas kernels, local(): pl.pallas_call(functools.partial(pair_zero_kernel, zero_at), grid_spec=pl...  25.1 us
    pallas_call x1, Pallas kernels, local(): pl.pallas_call(functools.partial(pair_one_kernel, one_at), grid_spec=pltp...  24.9 us
    ppermute x23, waiting for transfers between devices, swap(): return lax.ppermute(value, 'row', [(i, i ^ mask) for i in range(count)])  9.74 us
    pallas_call x2, Pallas kernels, own_part(): pl.pallas_call(functools.partial(own_kernel, rows), in_specs=[vmem, vmem,...  9.65 us
    pallas_call x1, Pallas kernels, local(): pl.pallas_call(again_kernel, grid_spec=pltpu.PrefetchScalarGridSpec(num_s...  8.85 us
    pallas_call x2, Pallas kernels, local(): pl.pallas_call(functools.partial(own_again_kernel, blocks), in_specs=[any...  4.25 us
  transfers between devices with their start and end apart: 23, of which 7 were waited for; matrix products, arithmetic and copies ran while one was open for 0% of the time, Pallas kernels for 34%

profile of v23, /device:TPU:0, one launch (start us, length us, event | category | flops | bytes accessed | tf_op | source)
XLA Modules:
  0.0 119.1 jit_solution(14632676510404958479)
XLA Ops:
  0.6 0.8 copy.12.list_ref
  1.4 1.2 payload.1
  2.6 5.1 %collective-permute-start.2 = (bf16[96,512]{1,0:T(8,128)(2,1)S(1)}, bf16[96,512]{1,0:T(8,128)(2,1)S(1)}, u32[]{:S(2)}, u32[]{:S(2)}) collective-permute-start(bf16[96,512]{1,0:T(8,128)(2,1)S(1)} %get-tuple-element.26), channel_id=1, source_target_pairs={{0,12},{1,13},{2,14},{3,15},{4,8},{5,9},{6,10},{7,11},{8,4},{9,5},... | collective-permute-start | bytes 294920 | tf_op jit(solution)/shard_map/ppermute | solution.py:392
  8.3 1.4 %own_tile_3.1 = (bf16[1,512,512]{2,1,0:T(8,128)(2,1)}, f32[8,2048]{1,0:T(8,128)S(1)}) custom-call(bf16[2048,128]{1,0:T(8,128)(2,1)S(1)} %get-tuple-element.23.left_ref, bf16[128,2048]{1,0:T(8,128)(2,1)S(1)} %get-tuple-element.22.right_ref.arrived_ref, bf16[8,2048]{1,0:T(8,128)(2,1)S(1)} %get-tuple-element.24.vec_ref, ...), custom_call_target="tpu_custom_call" | custom-call | flops 5000000000 | bytes 524288 | tf_op jit(solution)/shard_map/own_tile_3/pallas_call | solution.py:482
  9.8 3.8 %collective-permute-start.8 = (bf16[80,512]{1,0:T(8,128)(2,1)S(1)}, bf16[80,512]{1,0:T(8,128)(2,1)S(1)}, u32[]{:S(2)}, u32[]{:S(2)}) collective-permute-start(bf16[80,512]{1,0:T(8,128)(2,1)S(1)} %gate.6), channel_id=1, source_target_pairs={{0,12},{1,13},{2,14},{3,15},{4,8},{5,9},{6,10},{7,11},{8,4},{9,5},... | collective-permute-start | bytes 245768 | tf_op jit(solution)/shard_map/ppermute | solution.py:392
  13.6 4.3 %collective-permute-start.6 = (bf16[80,512]{1,0:T(8,128)(2,1)S(1)}, bf16[80,512]{1,0:T(8,128)(2,1)S(1)}, u32[]{:S(2)}, u32[]{:S(2)}) collective-permute-start(bf16[80,512]{1,0:T(8,128)(2,1)S(1)} %gate.6), channel_id=1, source_target_pairs={{0,4},{1,5},{2,6},{3,7},{4,0},{5,1},{6,2},{7,3},{8,12},{9,13},{10,... | collective-permute-start | bytes 245768 | tf_op jit(solution)/shard_map/ppermute | solution.py:392
  17.9 2.5 %collective-permute-done.1 = bf16[96,512]{1,0:T(8,128)(2,1)S(1)} collective-permute-done((bf16[96,512]{1,0:T(8,128)(2,1)S(1)}, bf16[96,512]{1,0:T(8,128)(2,1)S(1)}, u32[]{:S(2)}, u32[]{:S(2)}) %collective-permute-start.1) | collective-permute-done | bytes 98336 | tf_op jit(solution)/shard_map/ppermute | solution.py:392
  20.6 1.6 %collective-permute-start.3 = (bf16[384,512]{1,0:T(8,128)(2,1)S(1)}, bf16[384,512]{1,0:T(8,128)(2,1)S(1)}, u32[]{:S(2)}, u32[]{:S(2)}) collective-permute-start(bf16[384,512]{1,0:T(8,128)(2,1)S(1)} %gate.4.arrived_ref.refs_2_), channel_id=1, source_target_pairs={{0,2},{1,3},{2,0},{3,1},{4,6},{5,7},{6,4},{7,5},{8,10},{9,11},{10,... | collective-permute-start | bytes 1179656 | tf_op jit(solution)/shard_map/ppermute | solution.py:392
  22.2 8.2 %own_tile_0.1 = (bf16[9,512,512]{2,1,0:T(8,128)(2,1)}, f32[8,2048]{1,0:T(8,128)S(1)}) custom-call(bf16[2048,128]{1,0:T(8,128)(2,1)S(1)} %get-tuple-element.23.left_ref, bf16[128,2048]{1,0:T(8,128)(2,1)S(1)} %get-tuple-element.22.right_ref.arrived_ref, bf16[8,2048]{1,0:T(8,128)(2,1)S(1)} %get-tuple-element.24.vec_ref, ...), custom_call_target="tpu_custom_call" | custom-call | flops 5000000000 | bytes 4718592 | tf_op jit(solution)/shard_map/own_tile_0/pallas_call | solution.py:482
  30.4 1.7 %collective-permute-done.3.refs_0_ = bf16[384,512]{1,0:T(8,128)(2,1)S(1)} collective-permute-done((bf16[384,512]{1,0:T(8,128)(2,1)S(1)}, bf16[384,512]{1,0:T(8,128)(2,1)S(1)}, u32[]{:S(2)}, u32[]{:S(2)}) %collective-permute-start.3) | collective-permute-done | bytes 393248 | tf_op jit(solution)/shard_map/ppermute | solution.py:392
  32.2 1.7 %collective-permute-start.11 = (bf16[320,512]{1,0:T(8,128)(2,1)S(1)}, bf16[320,512]{1,0:T(8,128)(2,1)S(1)}, u32[]{:S(2)}, u32[]{:S(2)}) collective-permute-start(bf16[320,512]{1,0:T(8,128)(2,1)S(1)} %gate.7.refs_0_), channel_id=1, source_target_pairs={{0,3},{1,2},{2,1},{3,0},{4,7},{5,6},{6,5},{7,4},{8,11},{9,10},{10,... | collective-permute-start | bytes 983048 | tf_op jit(solution)/shard_map/ppermute | solution.py:392
  34.4 25.1 %pair_zero.1 = (bf16[3,1024,2048]{2,1,0:T(8,128)(2,1)S(1)}, bf16[2,1024,2048]{2,1,0:T(8,128)(2,1)}, f32[8,2048]{1,0:T(8,128)S(1)}, s32[7]{0:T(128)S(1)}) custom-call(s32[1]{0:T(128)} %bitcast.me_ref, bf16[128,2048]{1,0:T(8,128)(2,1)S(1)} %get-tuple-element.22.right_ref.arrived_ref, f32[8,2048]{1,0:T(8,128)S(1)} %get-tuple-element.25.refs_1_.refs_0_, ...), custom_call_target="tpu_custom_call" | custom-call | tf_op jit(solution)/shard_map/pair_zero/pallas_call | solution.py:541
  59.6 24.9 %pair_one.1 = (bf16[3,1024,2048]{2,1,0:T(8,128)(2,1)S(1)}, bf16[2,1024,2048]{2,1,0:T(8,128)(2,1)}, f32[8,2048]{1,0:T(8,128)S(1)}, bf16[8,2176]{1,0:T(8,128)(2,1)S(1)}) custom-call(s32[7]{0:T(128)S(1)} %get-tuple-element.28.slots_ref, bf16[128,2048]{1,0:T(8,128)(2,1)S(1)} %get-tuple-element.22.right_ref.arrived_ref, ...), custom_call_target="tpu_custom_call" | custom-call | tf_op jit(solution)/shard_map/pair_one/pallas_call | solution.py:561
  84.9 4.0 %collective-permute-start.12 = (bf16[1,8,2176]{2,1,0:T(8,128)(2,1)S(1)}, bf16[1,8,2176]{2,1,0:T(8,128)(2,1)S(1)}, u32[]{:S(2)}, u32[]{:S(2)}) collective-permute-start(bf16[1,8,2176]{2,1,0:T(8,128)(2,1)S(1)} %bitcast.7), channel_id=1, source_target_pairs={{0,4},{1,5},{2,6},{3,7},{4,0},{5,1},{6,2},{7,3},{8,12},{9,13},{10,... | collective-permute-start | bytes 104456 | tf_op jit(solution)/shard_map/ppermute | solution.py:392
  89.0 3.0 %own_again_1.1.refs_1_ = f32[8,2048]{1,0:T(8,128)S(1)} custom-call(bf16[9,512,512]{2,1,0:T(8,128)(2,1)} %get-tuple-element.38.in_ref, bf16[8,2176]{1,0:T(8,128)(2,1)S(1)} %get-tuple-element.35.vec_ref), custom_call_target="tpu_custom_call" | custom-call | flops 5000000000 | bytes 4718592 | tf_op jit(solution)/shard_map/own_again_1/pallas_call | solution.py:579
  92.1 1.6 %collective-permute-start.15 = (bf16[4,8,2176]{2,1,0:T(8,128)(2,1)S(1)}, bf16[4,8,2176]{2,1,0:T(8,128)(2,1)S(1)}, u32[]{:S(2)}, u32[]{:S(2)}) collective-permute-start(bf16[4,8,2176]{2,1,0:T(8,128)(2,1)S(1)} %pad_maximum_fusion.2), channel_id=1, source_target_pairs={{0,2},{1,3},{2,0},{3,1},{4,6},{5,7},{6,4},{7,5},{8,10},{9,11},{10,... | collective-permute-start | bytes 417800 | tf_op jit(solution)/shard_map/ppermute | solution.py:392
  93.7 3.5 %collective-permute-done.15 = bf16[4,8,2176]{2,1,0:T(8,128)(2,1)S(1)} collective-permute-done((bf16[4,8,2176]{2,1,0:T(8,128)(2,1)S(1)}, bf16[4,8,2176]{2,1,0:T(8,128)(2,1)S(1)}, u32[]{:S(2)}, u32[]{:S(2)}) %collective-permute-start.15) | collective-permute-done | bytes 139296 | tf_op jit(solution)/shard_map/ppermute | solution.py:392
  97.3 1.2 %own_again_0.1.refs_0_ = f32[8,2048]{1,0:T(8,128)S(1)} custom-call(bf16[1,512,512]{2,1,0:T(8,128)(2,1)} %get-tuple-element.37.in_ref, bf16[8,2176]{1,0:T(8,128)(2,1)S(1)} %get-tuple-element.35.vec_ref), custom_call_target="tpu_custom_call" | custom-call | flops 5000000000 | bytes 524288 | tf_op jit(solution)/shard_map/own_again_0/pallas_call | solution.py:579
  98.9 8.8 %pair_again.1 = (f32[32,2048]{1,0:T(8,128)S(1)}, f32[8,128]{1,0:T(8,128)S(1)}, f32[8,128]{1,0:T(8,128)S(1)}) custom-call(s32[7]{0:T(128)S(1)} %get-tuple-element.28.slots_ref, bf16[3,1024,2048]{2,1,0:T(8,128)(2,1)S(1)} %get-tuple-element.29.front_zero_ref, bf16[3,1024,2048]{2,1,0:T(8,128)(2,1)S(1)} %get-tuple-element.32.front_one_ref, ...), custom_call_target="tpu_custom_call" | custom-call | tf_op jit(solution)/shard_map/pair_again/pallas_call | solution.py:597
  107.8 2.3 %collective-permute-start.18 = (f32[8,128]{1,0:T(8,128)S(1)}, f32[8,128]{1,0:T(8,128)S(1)}, u32[]{:S(2)}, u32[]{:S(2)}) collective-permute-start(f32[8,128]{1,0:T(8,128)S(1)} %get-tuple-element.41), channel_id=1, source_target_pairs={{0,8},{1,9},{2,10},{3,11},{4,12},{5,13},{6,14},{7,15},{8,0},{9,1},... | collective-permute-start | bytes 12296 | tf_op jit(solution)/shard_map/ppermute | solution.py:392
  110.1 2.0 %collective-permute-start.17 = (f32[8,128]{1,0:T(8,128)S(1)}, f32[8,128]{1,0:T(8,128)S(1)}, u32[]{:S(2)}, u32[]{:S(2)}) collective-permute-start(f32[8,128]{1,0:T(8,128)S(1)} %get-tuple-element.41), channel_id=1, source_target_pairs={{0,4},{1,5},{2,6},{3,7},{4,0},{5,1},{6,2},{7,3},{8,12},{9,13},{10,... | collective-permute-start | bytes 12296 | tf_op jit(solution)/shard_map/ppermute | solution.py:392
  112.2 1.0 collective-permute-done.19
  114.0 2.5 %collective-permute-start.21 = (f32[8,128]{1,0:T(8,128)S(1)}, f32[8,128]{1,0:T(8,128)S(1)}, u32[]{:S(2)}, u32[]{:S(2)}) collective-permute-start(f32[8,128]{1,0:T(8,128)S(1)} %add_add_fusion.1), channel_id=1, source_target_pairs={{0,2},{1,3},{2,0},{3,1},{4,6},{5,7},{6,4},{7,5},{8,10},{9,11},{10,... | collective-permute-start | bytes 12296 | tf_op jit(solution)/shard_map/ppermute | solution.py:392
  116.5 1.5 %curve_order.1 = f32[32,2048]{1,0:T(8,128)S(1)} custom-call(f32[32,2048]{1,0:T(8,128)S(1)} %get-tuple-element.40.rows_ref, s32[1,2048]{1,0:T(1,128)S(1)} %copy-done.2), custom_call_target="tpu_custom_call" | custom-call | tf_op jit(solution)/shard_map/curve_order/pallas_call | solution.py:635
  (55 shorter events, 4.2 us)
Async XLA Ops:
  2.6 11.0 %collective-permute-start.2 = (bf16[96,512]{1,0:T(8,128)(2,1)S(1)}, bf16[96,512]{1,0:T(8,128)(2,1)S(1)}, u32[]{:S(2)}, u32[]{:S(2)}) collective-permute-start(bf16[96,512]{1,0:T(8,128)(2,1)S(1)} %get-tuple-element.26), channel_id=1, source_target_pairs={{0,12},{1,13},{2,14},{3,15},{4,8},{5,9},{6,10},{7,11},{8,4},{9,5},... | collective-permute-start | bytes 294920 | tf_op jit(solution)/shard_map/ppermute | solution.py:392
  7.7 12.8 %collective-permute-start.1 = (bf16[96,512]{1,0:T(8,128)(2,1)S(1)}, bf16[96,512]{1,0:T(8,128)(2,1)S(1)}, u32[]{:S(2)}, u32[]{:S(2)}) collective-permute-start(bf16[96,512]{1,0:T(8,128)(2,1)S(1)} %get-tuple-element.26), channel_id=1, source_target_pairs={{0,8},{1,9},{2,10},{3,11},{4,12},{5,13},{6,14},{7,15},{8,0},{9,1},... | collective-permute-start | bytes 294920 | tf_op jit(solution)/shard_map/ppermute | solution.py:392
  7.7 12.8 %collective-permute-start = (bf16[96,512]{1,0:T(8,128)(2,1)S(1)}, bf16[96,512]{1,0:T(8,128)(2,1)S(1)}, u32[]{:S(2)}, u32[]{:S(2)}) collective-permute-start(bf16[96,512]{1,0:T(8,128)(2,1)S(1)} %get-tuple-element.26), channel_id=1, source_target_pairs={{0,4},{1,5},{2,6},{3,7},{4,0},{5,1},{6,2},{7,3},{8,12},{9,13},{10,... | collective-permute-start | bytes 294920 | tf_op jit(solution)/shard_map/ppermute | solution.py:392
  9.8 22.4 %collective-permute-start.8 = (bf16[80,512]{1,0:T(8,128)(2,1)S(1)}, bf16[80,512]{1,0:T(8,128)(2,1)S(1)}, u32[]{:S(2)}, u32[]{:S(2)}) collective-permute-start(bf16[80,512]{1,0:T(8,128)(2,1)S(1)} %gate.6), channel_id=1, source_target_pairs={{0,12},{1,13},{2,14},{3,15},{4,8},{5,9},{6,10},{7,11},{8,4},{9,5},... | collective-permute-start | bytes 245768 | tf_op jit(solution)/shard_map/ppermute | solution.py:392
  13.6 18.6 %collective-permute-start.7 = (bf16[80,512]{1,0:T(8,128)(2,1)S(1)}, bf16[80,512]{1,0:T(8,128)(2,1)S(1)}, u32[]{:S(2)}, u32[]{:S(2)}) collective-permute-start(bf16[80,512]{1,0:T(8,128)(2,1)S(1)} %gate.6), channel_id=1, source_target_pairs={{0,8},{1,9},{2,10},{3,11},{4,12},{5,13},{6,14},{7,15},{8,0},{9,1},... | collective-permute-start | bytes 245768 | tf_op jit(solution)/shard_map/ppermute | solution.py:392
  13.6 18.6 %collective-permute-start.6 = (bf16[80,512]{1,0:T(8,128)(2,1)S(1)}, bf16[80,512]{1,0:T(8,128)(2,1)S(1)}, u32[]{:S(2)}, u32[]{:S(2)}) collective-permute-start(bf16[80,512]{1,0:T(8,128)(2,1)S(1)} %gate.6), channel_id=1, source_target_pairs={{0,4},{1,5},{2,6},{3,7},{4,0},{5,1},{6,2},{7,3},{8,12},{9,13},{10,... | collective-permute-start | bytes 245768 | tf_op jit(solution)/shard_map/ppermute | solution.py:392
  20.5 39.1 %copy-start = (f32[8,2048]{1,0:T(8,128)S(1)}, f32[8,2048]{1,0:T(8,128)}, u32[]{:S(2)}) copy-start(f32[8,2048]{1,0:T(8,128)} %rhs_ref.5) | copy-start | bytes 196612
  20.5 13.9 %collective-permute-start.4 = (bf16[384,512]{1,0:T(8,128)(2,1)S(1)}, bf16[384,512]{1,0:T(8,128)(2,1)S(1)}, u32[]{:S(2)}, u32[]{:S(2)}) collective-permute-start(bf16[384,512]{1,0:T(8,128)(2,1)S(1)} %gate.4.arrived_ref.refs_2_), channel_id=1, source_target_pairs={{0,1},{1,0},{2,3},{3,2},{4,5},{5,4},{6,7},{7,6},{8,9},{9,8},{10,11... | collective-permute-start | bytes 1179656 | tf_op jit(solution)/shard_map/ppermute | solution.py:392
  20.6 11.5 %collective-permute-start.3 = (bf16[384,512]{1,0:T(8,128)(2,1)S(1)}, bf16[384,512]{1,0:T(8,128)(2,1)S(1)}, u32[]{:S(2)}, u32[]{:S(2)}) collective-permute-start(bf16[384,512]{1,0:T(8,128)(2,1)S(1)} %gate.4.arrived_ref.refs_2_), channel_id=1, source_target_pairs={{0,2},{1,3},{2,0},{3,1},{4,6},{5,7},{6,4},{7,5},{8,10},{9,11},{10,... | collective-permute-start | bytes 1179656 | tf_op jit(solution)/shard_map/ppermute | solution.py:392
  32.1 2.3 %collective-permute-start.5 = (bf16[384,512]{1,0:T(8,128)(2,1)S(1)}, bf16[384,512]{1,0:T(8,128)(2,1)S(1)}, u32[]{:S(2)}, u32[]{:S(2)}) collective-permute-start(bf16[384,512]{1,0:T(8,128)(2,1)S(1)} %gate.5.refs_3_), channel_id=1, source_target_pairs={{0,1},{1,0},{2,3},{3,2},{4,5},{5,4},{6,7},{7,6},{8,9},{9,8},{10,11... | collective-permute-start | bytes 1179656 | tf_op jit(solution)/shard_map/ppermute | solution.py:392
  32.2 27.4 %collective-permute-start.11 = (bf16[320,512]{1,0:T(8,128)(2,1)S(1)}, bf16[320,512]{1,0:T(8,128)(2,1)S(1)}, u32[]{:S(2)}, u32[]{:S(2)}) collective-permute-start(bf16[320,512]{1,0:T(8,128)(2,1)S(1)} %gate.7.refs_0_), channel_id=1, source_target_pairs={{0,3},{1,2},{2,1},{3,0},{4,7},{5,6},{6,5},{7,4},{8,11},{9,10},{10,... | collective-permute-start | bytes 983048 | tf_op jit(solution)/shard_map/ppermute | solution.py:392
  33.9 25.7 %collective-permute-start.10 = (bf16[320,512]{1,0:T(8,128)(2,1)S(1)}, bf16[320,512]{1,0:T(8,128)(2,1)S(1)}, u32[]{:S(2)}, u32[]{:S(2)}) collective-permute-start(bf16[320,512]{1,0:T(8,128)(2,1)S(1)} %gate.7.refs_0_), channel_id=1, source_target_pairs={{0,1},{1,0},{2,3},{3,2},{4,5},{5,4},{6,7},{7,6},{8,9},{9,8},{10,11... | collective-permute-start | bytes 983048 | tf_op jit(solution)/shard_map/ppermute | solution.py:392
  33.9 25.7 %collective-permute-start.9 = (bf16[320,512]{1,0:T(8,128)(2,1)S(1)}, bf16[320,512]{1,0:T(8,128)(2,1)}, u32[]{:S(2)}, u32[]{:S(2)}) collective-permute-start(bf16[320,512]{1,0:T(8,128)(2,1)S(1)} %gate.7.refs_0_), channel_id=1, source_target_pairs={{0,2},{1,3},{2,0},{3,1},{4,6},{5,7},{6,4},{7,5},{8,10},{9,11},{10,... | collective-permute-start | bytes 983048 | tf_op jit(solution)/shard_map/ppermute | solution.py:392
  84.5 7.5 %collective-permute-start.14 = (bf16[1,8,2176]{2,1,0:T(8,128)(2,1)S(1)}, bf16[1,8,2176]{2,1,0:T(8,128)(2,1)S(1)}, u32[]{:S(2)}, u32[]{:S(2)}) collective-permute-start(bf16[1,8,2176]{2,1,0:T(8,128)(2,1)S(1)} %bitcast.5), channel_id=1, source_target_pairs={{0,12},{1,13},{2,14},{3,15},{4,8},{5,9},{6,10},{7,11},{8,4},{9,5},... | collective-permute-start | bytes 104456 | tf_op jit(solution)/shard_map/ppermute | solution.py:392
  84.6 7.4 %collective-permute-start.13 = (bf16[1,8,2176]{2,1,0:T(8,128)(2,1)S(1)}, bf16[1,8,2176]{2,1,0:T(8,128)(2,1)S(1)}, u32[]{:S(2)}, u32[]{:S(2)}) collective-permute-start(bf16[1,8,2176]{2,1,0:T(8,128)(2,1)S(1)} %bitcast.6), channel_id=1, source_target_pairs={{0,8},{1,9},{2,10},{3,11},{4,12},{5,13},{6,14},{7,15},{8,0},{9,1},... | collective-permute-start | bytes 104456 | tf_op jit(solution)/shard_map/ppermute | solution.py:392
  84.9 7.1 %collective-permute-start.12 = (bf16[1,8,2176]{2,1,0:T(8,128)(2,1)S(1)}, bf16[1,8,2176]{2,1,0:T(8,128)(2,1)S(1)}, u32[]{:S(2)}, u32[]{:S(2)}) collective-permute-start(bf16[1,8,2176]{2,1,0:T(8,128)(2,1)S(1)} %bitcast.7), channel_id=1, source_target_pairs={{0,4},{1,5},{2,6},{3,7},{4,0},{5,1},{6,2},{7,3},{8,12},{9,13},{10,... | collective-permute-start | bytes 104456 | tf_op jit(solution)/shard_map/ppermute | solution.py:392
  92.1 5.1 %collective-permute-start.15 = (bf16[4,8,2176]{2,1,0:T(8,128)(2,1)S(1)}, bf16[4,8,2176]{2,1,0:T(8,128)(2,1)S(1)}, u32[]{:S(2)}, u32[]{:S(2)}) collective-permute-start(bf16[4,8,2176]{2,1,0:T(8,128)(2,1)S(1)} %pad_maximum_fusion.2), channel_id=1, source_target_pairs={{0,2},{1,3},{2,0},{3,1},{4,6},{5,7},{6,4},{7,5},{8,10},{9,11},{10,... | collective-permute-start | bytes 417800 | tf_op jit(solution)/shard_map/ppermute | solution.py:392
  97.2 1.6 %collective-permute-start.16 = (bf16[8,8,2176]{2,1,0:T(8,128)(2,1)S(1)}, bf16[8,8,2176]{2,1,0:T(8,128)(2,1)S(1)}, u32[]{:S(2)}, u32[]{:S(2)}) collective-permute-start(bf16[8,8,2176]{2,1,0:T(8,128)(2,1)S(1)} %get-tuple-element.47), channel_id=1, source_target_pairs={{0,1},{1,0},{2,3},{3,2},{4,5},{5,4},{6,7},{7,6},{8,9},{9,8},{10,11... | collective-permute-start | bytes 835592 | tf_op jit(solution)/shard_map/ppermute | solution.py:392
  107.7 5.5 %collective-permute-start.19 = (f32[8,128]{1,0:T(8,128)S(1)}, f32[8,128]{1,0:T(8,128)S(1)}, u32[]{:S(2)}, u32[]{:S(2)}) collective-permute-start(f32[8,128]{1,0:T(8,128)S(1)} %get-tuple-element.41), channel_id=1, source_target_pairs={{0,12},{1,13},{2,14},{3,15},{4,8},{5,9},{6,10},{7,11},{8,4},{9,5},... | collective-permute-start | bytes 12296 | tf_op jit(solution)/shard_map/ppermute | solution.py:392
  107.8 5.4 %collective-permute-start.18 = (f32[8,128]{1,0:T(8,128)S(1)}, f32[8,128]{1,0:T(8,128)S(1)}, u32[]{:S(2)}, u32[]{:S(2)}) collective-permute-start(f32[8,128]{1,0:T(8,128)S(1)} %get-tuple-element.41), channel_id=1, source_target_pairs={{0,8},{1,9},{2,10},{3,11},{4,12},{5,13},{6,14},{7,15},{8,0},{9,1},... | collective-permute-start | bytes 12296 | tf_op jit(solution)/shard_map/ppermute | solution.py:392
  110.1 3.6 %collective-permute-start.17 = (f32[8,128]{1,0:T(8,128)S(1)}, f32[8,128]{1,0:T(8,128)S(1)}, u32[]{:S(2)}, u32[]{:S(2)}) collective-permute-start(f32[8,128]{1,0:T(8,128)S(1)} %get-tuple-element.41), channel_id=1, source_target_pairs={{0,4},{1,5},{2,6},{3,7},{4,0},{5,1},{6,2},{7,3},{8,12},{9,13},{10,... | collective-permute-start | bytes 12296 | tf_op jit(solution)/shard_map/ppermute | solution.py:392
  113.8 4.2 %collective-permute-start.22 = (f32[8,128]{1,0:T(8,128)S(1)}, f32[8,128]{1,0:T(8,128)S(1)}, u32[]{:S(2)}, u32[]{:S(2)}) collective-permute-start(f32[8,128]{1,0:T(8,128)S(1)} %add_add_fusion.1), channel_id=1, source_target_pairs={{0,3},{1,2},{2,1},{3,0},{4,7},{5,6},{6,5},{7,4},{8,11},{9,10},{10,... | collective-permute-start | bytes 12296 | tf_op jit(solution)/shard_map/ppermute | solution.py:392
  114.0 4.1 %collective-permute-start.21 = (f32[8,128]{1,0:T(8,128)S(1)}, f32[8,128]{1,0:T(8,128)S(1)}, u32[]{:S(2)}, u32[]{:S(2)}) collective-permute-start(f32[8,128]{1,0:T(8,128)S(1)} %add_add_fusion.1), channel_id=1, source_target_pairs={{0,2},{1,3},{2,0},{3,1},{4,6},{5,7},{6,4},{7,5},{8,10},{9,11},{10,... | collective-permute-start | bytes 12296 | tf_op jit(solution)/shard_map/ppermute | solution.py:392
  116.5 1.6 %collective-permute-start.20 = (f32[8,128]{1,0:T(8,128)S(1)}, f32[8,128]{1,0:T(8,128)S(1)}, u32[]{:S(2)}, u32[]{:S(2)}) collective-permute-start(f32[8,128]{1,0:T(8,128)S(1)} %add_add_fusion.1), channel_id=1, source_target_pairs={{0,1},{1,0},{2,3},{3,2},{4,5},{5,4},{6,7},{7,6},{8,9},{9,8},{10,11... | collective-permute-start | bytes 12296 | tf_op jit(solution)/shard_map/ppermute | solution.py:392
  (2 other events, 56.8 us)

commit v24 on v19

--- a/solution.py
+++ b/solution.py
@@ -279,7 +279,7 @@
 
     fetch = fetch_from(block_at, block_refs, slots_ref, pay_ref, sem_ref)
     half_tiles(
-        False, slots_ref, right_ref, fetch, front_ref, back_ref, image_ref, left_ref, vec_ref, pay_ref, sem_ref
+        True, slots_ref, right_ref, fetch, front_ref, back_ref, image_ref, left_ref, vec_ref, pay_ref, sem_ref
     )
 
     @pl.when((slot == pl.num_programs(0) - 1) & (step == pl.num_programs(1) - 1))

time: 118 us -> 118 us (level)
  Pallas kernels: 56.7 us -> 38 us
  starting transfers between devices: 39.9 us -> 50.8 us
  waiting for transfers between devices: 16.6 us -> 24.8 us
    ppermute x23, starting transfers between devices: 39.9 us -> 50.8 us  [swap(): return lax.ppermute(value, 'row', [(i, i ^ mask) for i in range(count)])]
    pallas_call x1, Pallas kernels: 18.2 us -> 9.43 us  [local(): pl.pallas_call(functools.partial(pair_zero_kernel, zero_at), grid_spec=pl...]
    ppermute x23, waiting for transfers between devices: 16.6 us -> 24.8 us  [swap(): return lax.ppermute(value, 'row', [(i, i ^ mask) for i in range(count)])]
    pallas_call x1, Pallas kernels: 17.4 us -> 9.71 us  [local(): pl.pallas_call(functools.partial(pair_one_kernel, one_at), grid_spec=pltp...]
    pallas_call x1, Pallas kernels: 4.58 us -> 2.24 us  [local(): pl.pallas_call(again_kernel, grid_spec=pltpu.PrefetchScalarGridSpec(num_s...]
  transfers between devices with their start and end apart: 23 -> 23, of which waited for: 7 -> 8; matrix products, arithmetic and copies ran while one was open for 0% -> 0% of each run, Pallas kernels for 29% -> 21%
where the time goes in v24:
time: 118 us; the launch traced here: 116 us
  starting transfers between devices  50.8 us (43%)
  Pallas kernels  38 us (32%)
  waiting for transfers between devices  24.8 us (21%)
    ppermute x23, starting transfers between devices, swap(): return lax.ppermute(value, 'row', [(i, i ^ mask) for i in range(count)])  50.8 us
    ppermute x23, waiting for transfers between devices, swap(): return lax.ppermute(value, 'row', [(i, i ^ mask) for i in range(count)])  24.8 us
    pallas_call x1, Pallas kernels, local(): pl.pallas_call(functools.partial(pair_one_kernel, one_at), grid_spec=pltp...  9.71 us
    pallas_call x2, Pallas kernels, own_part(): pl.pallas_call(functools.partial(own_kernel, rows), in_specs=[vmem, vmem,...  9.62 us
    pallas_call x1, Pallas kernels, local(): pl.pallas_call(functools.partial(pair_zero_kernel, zero_at), grid_spec=pl...  9.43 us
    pallas_call x2, Pallas kernels, local(): pl.pallas_call(functools.partial(own_again_kernel, blocks), in_specs=[any...  4.34 us
  transfers between devices with their start and end apart: 23, of which 8 were waited for; matrix products, arithmetic and copies ran while one was open for 0% of the time, Pallas kernels for 21%

profile of v24, /device:TPU:0, one launch (start us, length us, event | category | flops | bytes accessed | tf_op | source)
XLA Modules:
  0.0 116.4 jit_solution(9857617319844334711)
XLA Ops:
  0.6 0.8 copy.12.list_ref
  1.4 1.2 payload.1
  2.6 5.1 %collective-permute-start.2 = (bf16[96,512]{1,0:T(8,128)(2,1)S(1)}, bf16[96,512]{1,0:T(8,128)(2,1)S(1)}, u32[]{:S(2)}, u32[]{:S(2)}) collective-permute-start(bf16[96,512]{1,0:T(8,128)(2,1)S(1)} %get-tuple-element.26), channel_id=1, source_target_pairs={{0,12},{1,13},{2,14},{3,15},{4,8},{5,9},{6,10},{7,11},{8,4},{9,5},... | collective-permute-start | bytes 294920 | tf_op jit(solution)/shard_map/ppermute | solution.py:392
  8.3 4.0 %own_tile_0.1 = (bf16[4,512,512]{2,1,0:T(8,128)(2,1)}, f32[8,2048]{1,0:T(8,128)S(1)}) custom-call(bf16[2048,128]{1,0:T(8,128)(2,1)S(1)} %get-tuple-element.23.left_ref, bf16[128,2048]{1,0:T(8,128)(2,1)S(1)} %get-tuple-element.22.right_ref.arrived_ref, bf16[8,2048]{1,0:T(8,128)(2,1)S(1)} %get-tuple-element.24.vec_ref, ...), custom_call_target="tpu_custom_call" | custom-call | flops 5000000000 | bytes 2097152 | tf_op jit(solution)/shard_map/own_tile_0/pallas_call | solution.py:482
  12.3 3.8 %collective-permute-start.8 = (bf16[80,512]{1,0:T(8,128)(2,1)S(1)}, bf16[80,512]{1,0:T(8,128)(2,1)S(1)}, u32[]{:S(2)}, u32[]{:S(2)}) collective-permute-start(bf16[80,512]{1,0:T(8,128)(2,1)S(1)} %gate.6), channel_id=1, source_target_pairs={{0,12},{1,13},{2,14},{3,15},{4,8},{5,9},{6,10},{7,11},{8,4},{9,5},... | collective-permute-start | bytes 245768 | tf_op jit(solution)/shard_map/ppermute | solution.py:392
  16.8 3.1 %collective-permute-done.1 = bf16[96,512]{1,0:T(8,128)(2,1)S(1)} collective-permute-done((bf16[96,512]{1,0:T(8,128)(2,1)S(1)}, bf16[96,512]{1,0:T(8,128)(2,1)S(1)}, u32[]{:S(2)}, u32[]{:S(2)}) %collective-permute-start.1) | collective-permute-done | bytes 98336 | tf_op jit(solution)/shard_map/ppermute | solution.py:392
  20.0 1.6 %collective-permute-start.3 = (bf16[384,512]{1,0:T(8,128)(2,1)S(1)}, bf16[384,512]{1,0:T(8,128)(2,1)S(1)}, u32[]{:S(2)}, u32[]{:S(2)}) collective-permute-start(bf16[384,512]{1,0:T(8,128)(2,1)S(1)} %gate.4.arrived_ref.refs_2_), channel_id=1, source_target_pairs={{0,2},{1,3},{2,0},{3,1},{4,6},{5,7},{6,4},{7,5},{8,10},{9,11},{10,... | collective-permute-start | bytes 1179656 | tf_op jit(solution)/shard_map/ppermute | solution.py:392
  21.6 5.6 %own_tile_1.1 = (bf16[6,512,512]{2,1,0:T(8,128)(2,1)}, f32[8,2048]{1,0:T(8,128)S(1)}) custom-call(bf16[2048,128]{1,0:T(8,128)(2,1)S(1)} %get-tuple-element.23.left_ref, bf16[128,2048]{1,0:T(8,128)(2,1)S(1)} %get-tuple-element.22.right_ref.arrived_ref, bf16[8,2048]{1,0:T(8,128)(2,1)S(1)} %get-tuple-element.24.vec_ref, ...), custom_call_target="tpu_custom_call" | custom-call | flops 5000000000 | bytes 3145728 | tf_op jit(solution)/shard_map/own_tile_1/pallas_call | solution.py:482
  27.2 4.3 %collective-permute-done.3.refs_0_ = bf16[384,512]{1,0:T(8,128)(2,1)S(1)} collective-permute-done((bf16[384,512]{1,0:T(8,128)(2,1)S(1)}, bf16[384,512]{1,0:T(8,128)(2,1)S(1)}, u32[]{:S(2)}, u32[]{:S(2)}) %collective-permute-start.3) | collective-permute-done | bytes 393248 | tf_op jit(solution)/shard_map/ppermute | solution.py:392
  31.6 1.7 %collective-permute-start.11 = (bf16[320,512]{1,0:T(8,128)(2,1)S(1)}, bf16[320,512]{1,0:T(8,128)(2,1)S(1)}, u32[]{:S(2)}, u32[]{:S(2)}) collective-permute-start(bf16[320,512]{1,0:T(8,128)(2,1)S(1)} %gate.7.refs_0_), channel_id=1, source_target_pairs={{0,3},{1,2},{2,1},{3,0},{4,7},{5,6},{6,5},{7,4},{8,11},{9,10},{10,... | collective-permute-start | bytes 983048 | tf_op jit(solution)/shard_map/ppermute | solution.py:392
  33.9 9.4 %pair_zero.1 = (bf16[3,1024,2048]{2,1,0:T(8,128)(2,1)S(1)}, bf16[2,1024,2048]{2,1,0:T(8,128)(2,1)}, f32[8,2048]{1,0:T(8,128)S(1)}, s32[7]{0:T(128)S(1)}) custom-call(s32[1]{0:T(128)} %bitcast.me_ref, bf16[128,2048]{1,0:T(8,128)(2,1)S(1)} %get-tuple-element.22.right_ref.arrived_ref, f32[8,2048]{1,0:T(8,128)S(1)} %get-tuple-element.25.refs_1_.refs_0_, ...), custom_call_target="tpu_custom_call" | custom-call | tf_op jit(solution)/shard_map/pair_zero/pallas_call | solution.py:541
  43.3 5.5 %collective-permute-done.9.refs_1_ = bf16[320,512]{1,0:T(8,128)(2,1)} collective-permute-done((bf16[320,512]{1,0:T(8,128)(2,1)S(1)}, bf16[320,512]{1,0:T(8,128)(2,1)}, u32[]{:S(2)}, u32[]{:S(2)}) %collective-permute-start.9) | collective-permute-done | bytes 327712 | tf_op jit(solution)/shard_map/ppermute | solution.py:392
  48.9 9.7 %pair_one.1 = (bf16[3,1024,2048]{2,1,0:T(8,128)(2,1)S(1)}, bf16[2,1024,2048]{2,1,0:T(8,128)(2,1)}, f32[8,2048]{1,0:T(8,128)S(1)}, bf16[8,2176]{1,0:T(8,128)(2,1)S(1)}) custom-call(s32[7]{0:T(128)S(1)} %get-tuple-element.28.slots_ref, bf16[128,2048]{1,0:T(8,128)(2,1)S(1)} %get-tuple-element.22.right_ref.arrived_ref, ...), custom_call_target="tpu_custom_call" | custom-call | tf_op jit(solution)/shard_map/pair_one/pallas_call | solution.py:561
  58.6 25.4 %collective-permute-start.14 = (bf16[1,8,2176]{2,1,0:T(8,128)(2,1)S(1)}, bf16[1,8,2176]{2,1,0:T(8,128)(2,1)S(1)}, u32[]{:S(2)}, u32[]{:S(2)}) collective-permute-start(bf16[1,8,2176]{2,1,0:T(8,128)(2,1)S(1)} %bitcast.5), channel_id=1, source_target_pairs={{0,12},{1,13},{2,14},{3,15},{4,8},{5,9},{6,10},{7,11},{8,4},{9,5},... | collective-permute-start | bytes 104456 | tf_op jit(solution)/shard_map/ppermute | solution.py:392
  84.6 2.4 %own_again_1.1.refs_1_ = f32[8,2048]{1,0:T(8,128)S(1)} custom-call(bf16[6,512,512]{2,1,0:T(8,128)(2,1)} %get-tuple-element.38.in_ref, bf16[8,2176]{1,0:T(8,128)(2,1)S(1)} %get-tuple-element.35.vec_ref), custom_call_target="tpu_custom_call" | custom-call | flops 5000000000 | bytes 3145728 | tf_op jit(solution)/shard_map/own_again_1/pallas_call | solution.py:579
  87.0 1.8 %collective-permute-done.13 = bf16[1,8,2176]{2,1,0:T(8,128)(2,1)S(1)} collective-permute-done((bf16[1,8,2176]{2,1,0:T(8,128)(2,1)S(1)}, bf16[1,8,2176]{2,1,0:T(8,128)(2,1)S(1)}, u32[]{:S(2)}, u32[]{:S(2)}) %collective-permute-start.13) | collective-permute-done | bytes 34848 | tf_op jit(solution)/shard_map/ppermute | solution.py:392
  89.0 5.8 %collective-permute-done.15 = bf16[4,8,2176]{2,1,0:T(8,128)(2,1)S(1)} collective-permute-done((bf16[4,8,2176]{2,1,0:T(8,128)(2,1)S(1)}, bf16[4,8,2176]{2,1,0:T(8,128)(2,1)S(1)}, u32[]{:S(2)}, u32[]{:S(2)}) %collective-permute-start.15) | collective-permute-done | bytes 139296 | tf_op jit(solution)/shard_map/ppermute | solution.py:392
  94.9 2.0 %own_again_0.1.refs_0_ = f32[8,2048]{1,0:T(8,128)S(1)} custom-call(bf16[4,512,512]{2,1,0:T(8,128)(2,1)} %get-tuple-element.37.in_ref, bf16[8,2176]{1,0:T(8,128)(2,1)S(1)} %get-tuple-element.35.vec_ref), custom_call_target="tpu_custom_call" | custom-call | flops 5000000000 | bytes 2097152 | tf_op jit(solution)/shard_map/own_again_0/pallas_call | solution.py:579
  97.0 2.2 %pair_again.1 = (f32[32,2048]{1,0:T(8,128)S(1)}, f32[8,128]{1,0:T(8,128)S(1)}, f32[8,128]{1,0:T(8,128)S(1)}) custom-call(s32[7]{0:T(128)S(1)} %get-tuple-element.28.slots_ref, bf16[3,1024,2048]{2,1,0:T(8,128)(2,1)S(1)} %get-tuple-element.29.front_zero_ref, bf16[3,1024,2048]{2,1,0:T(8,128)(2,1)S(1)} %get-tuple-element.32.front_one_ref, ...), custom_call_target="tpu_custom_call" | custom-call | tf_op jit(solution)/shard_map/pair_again/pallas_call | solution.py:597
  99.2 7.9 %collective-permute-start.19 = (f32[8,128]{1,0:T(8,128)S(1)}, f32[8,128]{1,0:T(8,128)S(1)}, u32[]{:S(2)}, u32[]{:S(2)}) collective-permute-start(f32[8,128]{1,0:T(8,128)S(1)} %get-tuple-element.41), channel_id=1, source_target_pairs={{0,12},{1,13},{2,14},{3,15},{4,8},{5,9},{6,10},{7,11},{8,4},{9,5},... | collective-permute-start | bytes 12296 | tf_op jit(solution)/shard_map/ppermute | solution.py:392
  107.8 0.9 collective-permute-done.19
  108.8 2.9 %collective-permute-done.18 = f32[8,128]{1,0:T(8,128)S(1)} collective-permute-done((f32[8,128]{1,0:T(8,128)S(1)}, f32[8,128]{1,0:T(8,128)S(1)}, u32[]{:S(2)}, u32[]{:S(2)}) %collective-permute-start.18) | collective-permute-done | bytes 4128 | tf_op jit(solution)/shard_map/ppermute | solution.py:392
  111.8 1.8 %collective-permute-start.20 = (f32[8,128]{1,0:T(8,128)S(1)}, f32[8,128]{1,0:T(8,128)S(1)}, u32[]{:S(2)}, u32[]{:S(2)}) collective-permute-start(f32[8,128]{1,0:T(8,128)S(1)} %add_add_fusion.1), channel_id=1, source_target_pairs={{0,1},{1,0},{2,3},{3,2},{4,5},{5,4},{6,7},{7,6},{8,9},{9,8},{10,11... | collective-permute-start | bytes 12296 | tf_op jit(solution)/shard_map/ppermute | solution.py:392
  113.6 1.5 %curve_order.1 = f32[32,2048]{1,0:T(8,128)S(1)} custom-call(f32[32,2048]{1,0:T(8,128)S(1)} %get-tuple-element.40.rows_ref, s32[1,2048]{1,0:T(1,128)S(1)} %copy-done.2), custom_call_target="tpu_custom_call" | custom-call | tf_op jit(solution)/shard_map/curve_order/pallas_call | solution.py:635
  (55 shorter events, 5.0 us)
Async XLA Ops:
  2.6 13.6 %collective-permute-start.2 = (bf16[96,512]{1,0:T(8,128)(2,1)S(1)}, bf16[96,512]{1,0:T(8,128)(2,1)S(1)}, u32[]{:S(2)}, u32[]{:S(2)}) collective-permute-start(bf16[96,512]{1,0:T(8,128)(2,1)S(1)} %get-tuple-element.26), channel_id=1, source_target_pairs={{0,12},{1,13},{2,14},{3,15},{4,8},{5,9},{6,10},{7,11},{8,4},{9,5},... | collective-permute-start | bytes 294920 | tf_op jit(solution)/shard_map/ppermute | solution.py:392
  7.7 12.2 %collective-permute-start.1 = (bf16[96,512]{1,0:T(8,128)(2,1)S(1)}, bf16[96,512]{1,0:T(8,128)(2,1)S(1)}, u32[]{:S(2)}, u32[]{:S(2)}) collective-permute-start(bf16[96,512]{1,0:T(8,128)(2,1)S(1)} %get-tuple-element.26), channel_id=1, source_target_pairs={{0,8},{1,9},{2,10},{3,11},{4,12},{5,13},{6,14},{7,15},{8,0},{9,1},... | collective-permute-start | bytes 294920 | tf_op jit(solution)/shard_map/ppermute | solution.py:392
  7.7 12.2 %collective-permute-start = (bf16[96,512]{1,0:T(8,128)(2,1)S(1)}, bf16[96,512]{1,0:T(8,128)(2,1)S(1)}, u32[]{:S(2)}, u32[]{:S(2)}) collective-permute-start(bf16[96,512]{1,0:T(8,128)(2,1)S(1)} %get-tuple-element.26), channel_id=1, source_target_pairs={{0,4},{1,5},{2,6},{3,7},{4,0},{5,1},{6,2},{7,3},{8,12},{9,13},{10,... | collective-permute-start | bytes 294920 | tf_op jit(solution)/shard_map/ppermute | solution.py:392
  12.3 19.2 %collective-permute-start.8 = (bf16[80,512]{1,0:T(8,128)(2,1)S(1)}, bf16[80,512]{1,0:T(8,128)(2,1)S(1)}, u32[]{:S(2)}, u32[]{:S(2)}) collective-permute-start(bf16[80,512]{1,0:T(8,128)(2,1)S(1)} %gate.6), channel_id=1, source_target_pairs={{0,12},{1,13},{2,14},{3,15},{4,8},{5,9},{6,10},{7,11},{8,4},{9,5},... | collective-permute-start | bytes 245768 | tf_op jit(solution)/shard_map/ppermute | solution.py:392
  16.1 15.4 %collective-permute-start.7 = (bf16[80,512]{1,0:T(8,128)(2,1)S(1)}, bf16[80,512]{1,0:T(8,128)(2,1)S(1)}, u32[]{:S(2)}, u32[]{:S(2)}) collective-permute-start(bf16[80,512]{1,0:T(8,128)(2,1)S(1)} %gate.6), channel_id=1, source_target_pairs={{0,8},{1,9},{2,10},{3,11},{4,12},{5,13},{6,14},{7,15},{8,0},{9,1},... | collective-permute-start | bytes 245768 | tf_op jit(solution)/shard_map/ppermute | solution.py:392
  16.2 15.4 %collective-permute-start.6 = (bf16[80,512]{1,0:T(8,128)(2,1)S(1)}, bf16[80,512]{1,0:T(8,128)(2,1)S(1)}, u32[]{:S(2)}, u32[]{:S(2)}) collective-permute-start(bf16[80,512]{1,0:T(8,128)(2,1)S(1)} %gate.6), channel_id=1, source_target_pairs={{0,4},{1,5},{2,6},{3,7},{4,0},{5,1},{6,2},{7,3},{8,12},{9,13},{10,... | collective-permute-start | bytes 245768 | tf_op jit(solution)/shard_map/ppermute | solution.py:392
  19.9 28.9 %copy-start = (f32[8,2048]{1,0:T(8,128)S(1)}, f32[8,2048]{1,0:T(8,128)}, u32[]{:S(2)}) copy-start(f32[8,2048]{1,0:T(8,128)} %rhs_ref.5) | copy-start | bytes 196612
  20.0 13.9 %collective-permute-start.4 = (bf16[384,512]{1,0:T(8,128)(2,1)S(1)}, bf16[384,512]{1,0:T(8,128)(2,1)S(1)}, u32[]{:S(2)}, u32[]{:S(2)}) collective-permute-start(bf16[384,512]{1,0:T(8,128)(2,1)S(1)} %gate.4.arrived_ref.refs_2_), channel_id=1, source_target_pairs={{0,1},{1,0},{2,3},{3,2},{4,5},{5,4},{6,7},{7,6},{8,9},{9,8},{10,11... | collective-permute-start | bytes 1179656 | tf_op jit(solution)/shard_map/ppermute | solution.py:392
  20.0 11.5 %collective-permute-start.3 = (bf16[384,512]{1,0:T(8,128)(2,1)S(1)}, bf16[384,512]{1,0:T(8,128)(2,1)S(1)}, u32[]{:S(2)}, u32[]{:S(2)}) collective-permute-start(bf16[384,512]{1,0:T(8,128)(2,1)S(1)} %gate.4.arrived_ref.refs_2_), channel_id=1, source_target_pairs={{0,2},{1,3},{2,0},{3,1},{4,6},{5,7},{6,4},{7,5},{8,10},{9,11},{10,... | collective-permute-start | bytes 1179656 | tf_op jit(solution)/shard_map/ppermute | solution.py:392
  31.6 2.3 %collective-permute-start.5 = (bf16[384,512]{1,0:T(8,128)(2,1)S(1)}, bf16[384,512]{1,0:T(8,128)(2,1)S(1)}, u32[]{:S(2)}, u32[]{:S(2)}) collective-permute-start(bf16[384,512]{1,0:T(8,128)(2,1)S(1)} %gate.5.refs_3_), channel_id=1, source_target_pairs={{0,1},{1,0},{2,3},{3,2},{4,5},{5,4},{6,7},{7,6},{8,9},{9,8},{10,11... | collective-permute-start | bytes 1179656 | tf_op jit(solution)/shard_map/ppermute | solution.py:392
  31.6 11.7 %collective-permute-start.11 = (bf16[320,512]{1,0:T(8,128)(2,1)S(1)}, bf16[320,512]{1,0:T(8,128)(2,1)S(1)}, u32[]{:S(2)}, u32[]{:S(2)}) collective-permute-start(bf16[320,512]{1,0:T(8,128)(2,1)S(1)} %gate.7.refs_0_), channel_id=1, source_target_pairs={{0,3},{1,2},{2,1},{3,0},{4,7},{5,6},{6,5},{7,4},{8,11},{9,10},{10,... | collective-permute-start | bytes 983048 | tf_op jit(solution)/shard_map/ppermute | solution.py:392
  33.3 10.0 %collective-permute-start.10 = (bf16[320,512]{1,0:T(8,128)(2,1)S(1)}, bf16[320,512]{1,0:T(8,128)(2,1)S(1)}, u32[]{:S(2)}, u32[]{:S(2)}) collective-permute-start(bf16[320,512]{1,0:T(8,128)(2,1)S(1)} %gate.7.refs_0_), channel_id=1, source_target_pairs={{0,1},{1,0},{2,3},{3,2},{4,5},{5,4},{6,7},{7,6},{8,9},{9,8},{10,11... | collective-permute-start | bytes 983048 | tf_op jit(solution)/shard_map/ppermute | solution.py:392
  33.3 15.5 %collective-permute-start.9 = (bf16[320,512]{1,0:T(8,128)(2,1)S(1)}, bf16[320,512]{1,0:T(8,128)(2,1)}, u32[]{:S(2)}, u32[]{:S(2)}) collective-permute-start(bf16[320,512]{1,0:T(8,128)(2,1)S(1)} %gate.7.refs_0_), channel_id=1, source_target_pairs={{0,2},{1,3},{2,0},{3,1},{4,6},{5,7},{6,4},{7,5},{8,10},{9,11},{10,... | collective-permute-start | bytes 983048 | tf_op jit(solution)/shard_map/ppermute | solution.py:392
  58.6 28.4 %collective-permute-start.14 = (bf16[1,8,2176]{2,1,0:T(8,128)(2,1)S(1)}, bf16[1,8,2176]{2,1,0:T(8,128)(2,1)S(1)}, u32[]{:S(2)}, u32[]{:S(2)}) collective-permute-start(bf16[1,8,2176]{2,1,0:T(8,128)(2,1)S(1)} %bitcast.5), channel_id=1, source_target_pairs={{0,12},{1,13},{2,14},{3,15},{4,8},{5,9},{6,10},{7,11},{8,4},{9,5},... | collective-permute-start | bytes 104456 | tf_op jit(solution)/shard_map/ppermute | solution.py:392
  84.0 4.8 %collective-permute-start.13 = (bf16[1,8,2176]{2,1,0:T(8,128)(2,1)S(1)}, bf16[1,8,2176]{2,1,0:T(8,128)(2,1)S(1)}, u32[]{:S(2)}, u32[]{:S(2)}) collective-permute-start(bf16[1,8,2176]{2,1,0:T(8,128)(2,1)S(1)} %bitcast.6), channel_id=1, source_target_pairs={{0,8},{1,9},{2,10},{3,11},{4,12},{5,13},{6,14},{7,15},{8,0},{9,1},... | collective-permute-start | bytes 104456 | tf_op jit(solution)/shard_map/ppermute | solution.py:392
  84.0 4.8 %collective-permute-start.12 = (bf16[1,8,2176]{2,1,0:T(8,128)(2,1)S(1)}, bf16[1,8,2176]{2,1,0:T(8,128)(2,1)S(1)}, u32[]{:S(2)}, u32[]{:S(2)}) collective-permute-start(bf16[1,8,2176]{2,1,0:T(8,128)(2,1)S(1)} %bitcast.7), channel_id=1, source_target_pairs={{0,4},{1,5},{2,6},{3,7},{4,0},{5,1},{6,2},{7,3},{8,12},{9,13},{10,... | collective-permute-start | bytes 104456 | tf_op jit(solution)/shard_map/ppermute | solution.py:392
  88.9 6.0 %collective-permute-start.15 = (bf16[4,8,2176]{2,1,0:T(8,128)(2,1)S(1)}, bf16[4,8,2176]{2,1,0:T(8,128)(2,1)S(1)}, u32[]{:S(2)}, u32[]{:S(2)}) collective-permute-start(bf16[4,8,2176]{2,1,0:T(8,128)(2,1)S(1)} %pad_maximum_fusion.2), channel_id=1, source_target_pairs={{0,2},{1,3},{2,0},{3,1},{4,6},{5,7},{6,4},{7,5},{8,10},{9,11},{10,... | collective-permute-start | bytes 417800 | tf_op jit(solution)/shard_map/ppermute | solution.py:392
  94.8 2.1 %collective-permute-start.16 = (bf16[8,8,2176]{2,1,0:T(8,128)(2,1)S(1)}, bf16[8,8,2176]{2,1,0:T(8,128)(2,1)S(1)}, u32[]{:S(2)}, u32[]{:S(2)}) collective-permute-start(bf16[8,8,2176]{2,1,0:T(8,128)(2,1)S(1)} %get-tuple-element.47), channel_id=1, source_target_pairs={{0,1},{1,0},{2,3},{3,2},{4,5},{5,4},{6,7},{7,6},{8,9},{9,8},{10,11... | collective-permute-start | bytes 835592 | tf_op jit(solution)/shard_map/ppermute | solution.py:392
  99.2 9.5 %collective-permute-start.19 = (f32[8,128]{1,0:T(8,128)S(1)}, f32[8,128]{1,0:T(8,128)S(1)}, u32[]{:S(2)}, u32[]{:S(2)}) collective-permute-start(f32[8,128]{1,0:T(8,128)S(1)} %get-tuple-element.41), channel_id=1, source_target_pairs={{0,12},{1,13},{2,14},{3,15},{4,8},{5,9},{6,10},{7,11},{8,4},{9,5},... | collective-permute-start | bytes 12296 | tf_op jit(solution)/shard_map/ppermute | solution.py:392
  107.2 4.5 %collective-permute-start.18 = (f32[8,128]{1,0:T(8,128)S(1)}, f32[8,128]{1,0:T(8,128)S(1)}, u32[]{:S(2)}, u32[]{:S(2)}) collective-permute-start(f32[8,128]{1,0:T(8,128)S(1)} %get-tuple-element.41), channel_id=1, source_target_pairs={{0,8},{1,9},{2,10},{3,11},{4,12},{5,13},{6,14},{7,15},{8,0},{9,1},... | collective-permute-start | bytes 12296 | tf_op jit(solution)/shard_map/ppermute | solution.py:392
  107.2 4.5 %collective-permute-start.17 = (f32[8,128]{1,0:T(8,128)S(1)}, f32[8,128]{1,0:T(8,128)S(1)}, u32[]{:S(2)}, u32[]{:S(2)}) collective-permute-start(f32[8,128]{1,0:T(8,128)S(1)} %get-tuple-element.41), channel_id=1, source_target_pairs={{0,4},{1,5},{2,6},{3,7},{4,0},{5,1},{6,2},{7,3},{8,12},{9,13},{10,... | collective-permute-start | bytes 12296 | tf_op jit(solution)/shard_map/ppermute | solution.py:392
  111.7 3.4 %collective-permute-start.22 = (f32[8,128]{1,0:T(8,128)S(1)}, f32[8,128]{1,0:T(8,128)S(1)}, u32[]{:S(2)}, u32[]{:S(2)}) collective-permute-start(f32[8,128]{1,0:T(8,128)S(1)} %add_add_fusion.1), channel_id=1, source_target_pairs={{0,3},{1,2},{2,1},{3,0},{4,7},{5,6},{6,5},{7,4},{8,11},{9,10},{10,... | collective-permute-start | bytes 12296 | tf_op jit(solution)/shard_map/ppermute | solution.py:392
  111.8 3.7 %collective-permute-start.21 = (f32[8,128]{1,0:T(8,128)S(1)}, f32[8,128]{1,0:T(8,128)S(1)}, u32[]{:S(2)}, u32[]{:S(2)}) collective-permute-start(f32[8,128]{1,0:T(8,128)S(1)} %add_add_fusion.1), channel_id=1, source_target_pairs={{0,2},{1,3},{2,0},{3,1},{4,6},{5,7},{6,4},{7,5},{8,10},{9,11},{10,... | collective-permute-start | bytes 12296 | tf_op jit(solution)/shard_map/ppermute | solution.py:392
  111.8 3.6 %collective-permute-start.20 = (f32[8,128]{1,0:T(8,128)S(1)}, f32[8,128]{1,0:T(8,128)S(1)}, u32[]{:S(2)}, u32[]{:S(2)}) collective-permute-start(f32[8,128]{1,0:T(8,128)S(1)} %add_add_fusion.1), channel_id=1, source_target_pairs={{0,1},{1,0},{2,3},{3,2},{4,5},{5,4},{6,7},{7,6},{8,9},{9,8},{10,11... | collective-permute-start | bytes 12296 | tf_op jit(solution)/shard_map/ppermute | solution.py:392
  (2 other events, 45.6 us)
